TPU v7x, 32 devices: a whole 2x2x4 slice. The times are simulated.
32 devices in a mesh: net: 8 (over z, x), scen: 4 (over y, core).
Axes of the slice: x: 2, y: 2, z: 4, core: 2. Of those that a mesh axis runs over, the one named last changes fastest.
Arguments:
- arc_flows: float32 [128, 65536], P('scen', 'net'), may hold values from 0 to 1
- node_duals: float32 [128, 16384], P('scen', 'net'), may hold values from -6 to 6
- demand: float32 [128, 16384], P('scen', 'net'), may hold values from -6 to 6
- excess: float32 [128], P('scen'), may hold values from 0 to 0.5
- risk_duals: float32 [128], P('scen'), may hold values from 0.2 to 6
- threshold: float32 [1], replicated, may hold values from -2.5 to -1.5
- arc_costs: float32 [65536], P('net'), may hold values from 0.05 to 0.75
- local_blocks: bfloat16 [512, 4, 128, 128], P('net'), may hold values from -0.125 to 0.125
- head_blocks: bfloat16 [512, 128, 128], P('net'), may hold values from -0.125 to 0.125
- local_index: int32 [512, 4], P('net'), may hold values from 0 to 15
- head_index: int32 [512], P('net'), may hold values from 0 to 127, as said below
Outputs:
- flows_next: float32 [128, 65536], P('scen', 'net')
- duals_next: float32 [128, 16384], P('scen', 'net')
- excess_next: float32 [128], P('scen')
- risk_next: float32 [128], P('scen')
- threshold_next: float32 [1], replicated
Inputs may be any that keep to these rules, and one draw needn't show every extreme that they name: Among the arc blocks of one device, at most 16 have their head node block on any one device of net (head_index // 16 names the device), and in every device's arc blocks some device of net is named exactly 16 times.
All inputs are finite; a program needn't handle non-finite values.
Results may differ from a plain program's by a relative error of at most 0.0021.
Values may be sent and summed in bfloat16 or wider, within the bound.
No kernel may reach another device: no remote copies, remote signals or barrier semaphores. Data moves between devices by JAX's collectives and lax.ppermute only.
A program may use at most 128 MiB of HBM per device.

v0:
```python
import functools

import jax
import jax.numpy as jnp
from jax import lax
from jax.experimental import pallas as pl
from jax.experimental.pallas import tpu as pltpu
from jax.sharding import PartitionSpec as P

ROUNDS = 3

primal_step = 0.5
dual_step = 0.5
risk_step = 1.0
tail_weight = 2.0

VMEM_LIMIT = 50 * 1024 * 1024
GROUP = 8


def contract_last(left, right):
    return lax.dot_general(
        left, right, (((1,), (1,)), ((), ())), preferred_element_type=jnp.float32
    )


def local_adjoint_kernel(touches, group, index_ref, panel_ref, blocks_ref, out_ref):
    rows = blocks_ref.shape[-1]
    first = pl.program_id(0) * group
    for member in range(group):
        total = None
        left = jnp.concatenate(
            [panel_ref[index_ref[(first + member) * touches + k]] for k in range(touches)], axis=1
        )
        right = jnp.concatenate([blocks_ref[member, k] for k in range(touches)], axis=1)
        out_ref[:, member * rows : (member + 1) * rows] = contract_last(left, right)


def head_kernel(
    group,
    steps,
    node_blks,
    has_losses,
    arc_total,
    index_ref,
    panel_ref,
    heads_ref,
    pulled_ref,
    flows_ref,
    costs_ref,
    risk_ref,
    flows_out,
    bar_out,
    terms_out,
    loss_out,
    risk_out,
    terms,
    loss,
):
    rows = heads_ref.shape[-1]
    step = pl.program_id(0)
    first = step * group
    chunk = node_blks + 1

    @pl.when(step == 0)
    def _():
        terms[...] = jnp.zeros_like(terms)
        loss[...] = jnp.zeros_like(loss)
        risk_start = risk_ref[...]
        if has_losses:
            arrived = jnp.zeros_like(risk_start)
            for source in range(panel_ref.shape[0] // chunk):
                arrived += panel_ref[source * chunk + node_blks].astype(jnp.float32)
            losses = jnp.sum(arrived, axis=1, keepdims=True) / arc_total
            risk_start = jnp.maximum(risk_start + risk_step * losses, 0.0)
        risk_out[...] = risk_start

    risk = risk_out[...]
    loss_sum = jnp.zeros_like(risk)
    for member in range(group):
        head = index_ref[first + member]
        place = head + lax.div(head, node_blks)
        columns = slice(member * rows, (member + 1) * rows)
        pulled = pulled_ref[:, columns] + contract_last(panel_ref[place], heads_ref[member])
        flows = flows_ref[:, columns]
        cost = costs_ref[:, columns]
        flows_new = jnp.maximum(flows - primal_step * (risk * cost - pulled), 0.0)
        bar = 2.0 * flows_new - flows
        flows_out[:, columns] = flows_new
        loss_sum += cost * bar
        half = bar.astype(jnp.bfloat16)
        bar_out[:, columns] = half
        terms[head] += jnp.dot(half, heads_ref[member], preferred_element_type=jnp.float32)
    loss[...] += loss_sum

    @pl.when(step == steps - 1)
    def _():
        terms_out[...] = terms[...].astype(jnp.bfloat16)
        total = jnp.sum(loss[...], axis=1, keepdims=True)
        high = total.astype(jnp.bfloat16).astype(jnp.float32)
        rest = total - high
        middle = rest.astype(jnp.bfloat16).astype(jnp.float32)
        low = rest - middle
        lane = lax.broadcasted_iota(jnp.int32, loss.shape, 1)
        packed = jnp.where(
            lane == 0, high, jnp.where(lane == 1, middle, jnp.where(lane == 2, low, 0.0))
        )
        loss_out[...] = packed.astype(jnp.bfloat16)


def local_forward_kernel(
    touches, group, steps, index_ref, bar_ref, blocks_ref, duals_ref, demand_ref, out_ref, total
):
    rows = blocks_ref.shape[-1]
    step = pl.program_id(0)
    first = step * group

    @pl.when(step == 0)
    def _():
        total[...] = jnp.zeros_like(total)

    for member in range(group):
        right = jnp.concatenate([blocks_ref[member, k] for k in range(touches)], axis=1)
        products = jnp.dot(
            bar_ref[:, member * rows : (member + 1) * rows],
            right,
            preferred_element_type=jnp.float32,
        )
        for k in range(touches):
            place = index_ref[(first + member) * touches + k]
            total[place] += products[:, k * rows : (k + 1) * rows]

    @pl.when(step == steps - 1)
    def _():
        out_ref[...] = duals_ref[...] + dual_step * (demand_ref[...] - total[...])


def whole(*shape):
    return pl.BlockSpec(shape, lambda i, *_: (0,) * len(shape))


def params():
    return pltpu.CompilerParams(
        dimension_semantics=("arbitrary",), vmem_limit_bytes=VMEM_LIMIT
    )


def local_adjoint(index, panel, blocks):
    arc_blks, touches, rows, _ = blocks.shape
    scen_rows = panel.shape[1]
    group = GROUP
    return pl.pallas_call(
        functools.partial(local_adjoint_kernel, touches, group),
        out_shape=jax.ShapeDtypeStruct((scen_rows, arc_blks * rows), jnp.float32),
        grid_spec=pltpu.PrefetchScalarGridSpec(
            num_scalar_prefetch=1,
            grid=(arc_blks // group,),
            in_specs=[
                whole(*panel.shape),
                pl.BlockSpec((group, touches, rows, rows), lambda i, *_: (i, 0, 0, 0)),
            ],
            out_specs=pl.BlockSpec((scen_rows, group * rows), lambda i, *_: (0, i)),
        ),
        compiler_params=params(),
        cost_estimate=pl.CostEstimate(
            flops=2 * scen_rows * blocks.size, bytes_accessed=2 * blocks.size, transcendentals=0
        ),
        name="local_adjoint",
    )(index, panel, blocks)


def head_step(index, panel, heads, pulled, flows, costs, risk, node_blks, has_losses, arc_total):
    arc_blks, rows, _ = heads.shape
    scen_rows = flows.shape[0]
    group = GROUP
    steps = arc_blks // group
    node_total = panel.shape[0] // (node_blks + 1) * node_blks
    arcs = pl.BlockSpec((scen_rows, group * rows), lambda i, *_: (0, i))
    return pl.pallas_call(
        functools.partial(head_kernel, group, steps, node_blks, has_losses, arc_total),
        out_shape=(
            jax.ShapeDtypeStruct(flows.shape, jnp.float32),
            jax.ShapeDtypeStruct(flows.shape, jnp.bfloat16),
            jax.ShapeDtypeStruct((node_total, scen_rows, rows), jnp.bfloat16),
            jax.ShapeDtypeStruct((scen_rows, rows), jnp.bfloat16),
            jax.ShapeDtypeStruct((scen_rows, rows), jnp.float32),
        ),
        grid_spec=pltpu.PrefetchScalarGridSpec(
            num_scalar_prefetch=1,
            grid=(steps,),
            in_specs=[
                whole(*panel.shape),
                pl.BlockSpec((group, rows, rows), lambda i, *_: (i, 0, 0)),
                arcs,
                arcs,
                pl.BlockSpec((1, group * rows), lambda i, *_: (0, i)),
                whole(scen_rows, rows),
            ],
            out_specs=[
                arcs,
                arcs,
                whole(node_total, scen_rows, rows),
                whole(scen_rows, rows),
                whole(scen_rows, rows),
            ],
            scratch_shapes=[
                pltpu.VMEM((node_total, scen_rows, rows), jnp.float32),
                pltpu.VMEM((scen_rows, rows), jnp.float32),
            ],
        ),
        compiler_params=params(),
        cost_estimate=pl.CostEstimate(
            flops=4 * scen_rows * heads.size,
            bytes_accessed=2 * heads.size + 14 * flows.size + 4 * panel.size,
            transcendentals=0,
        ),
        name="head_step",
    )(index, panel, heads, pulled, flows, costs, risk)


def local_forward(index, bar, blocks, duals, demand):
    arc_blks, touches, rows, _ = blocks.shape
    scen_rows = bar.shape[0]
    group = GROUP
    steps = arc_blks // group
    return pl.pallas_call(
        functools.partial(local_forward_kernel, touches, group, steps),
        out_shape=jax.ShapeDtypeStruct(duals.shape, jnp.float32),
        grid_spec=pltpu.PrefetchScalarGridSpec(
            num_scalar_prefetch=1,
            grid=(steps,),
            in_specs=[
                pl.BlockSpec((scen_rows, group * rows), lambda i, *_: (0, i)),
                pl.BlockSpec((group, touches, rows, rows), lambda i, *_: (i, 0, 0, 0)),
                whole(*duals.shape),
                whole(*duals.shape),
            ],
            out_specs=whole(*duals.shape),
            scratch_shapes=[pltpu.VMEM(duals.shape, jnp.float32)],
        ),
        compiler_params=params(),
        cost_estimate=pl.CostEstimate(
            flops=2 * scen_rows * blocks.size, bytes_accessed=2 * blocks.size, transcendentals=0
        ),
        name="local_forward",
    )(index, bar, blocks, duals, demand)


def sum_over(value, axis):
    size = lax.axis_size(axis)
    if size & (size - 1):
        return lax.psum(value, axis)
    stride = 1
    while stride < size:
        value = value + lax.ppermute(value, axis, [(i, i ^ stride) for i in range(size)])
        stride *= 2
    return value


def per_device(
    arc_flows,
    node_duals,
    demand,
    excess,
    risk_duals,
    threshold,
    arc_costs,
    local_blocks,
    head_blocks,
    local_index,
    head_index,
):
    rows = local_blocks.shape[-1]
    scen_rows = arc_flows.shape[0]
    node_blks = node_duals.shape[1] // rows
    net_size = lax.axis_size("net")
    arc_total = arc_flows.shape[1] * net_size
    scen_total = scen_rows * lax.axis_size("scen")
    local_ids = local_index.reshape(-1)
    costs = arc_costs.reshape(1, -1)

    def to_blocks(panel):
        return panel.reshape(scen_rows, node_blks, rows).transpose(1, 0, 2)

    duals = to_blocks(node_duals)
    wanted = to_blocks(demand)
    flows = arc_flows
    excess_now = jnp.broadcast_to(excess[:, None], (scen_rows, rows))
    risk = jnp.broadcast_to(risk_duals[:, None], (scen_rows, rows))
    level = threshold
    loss_half = jnp.zeros((scen_rows, rows), jnp.bfloat16)
    for iteration in range(ROUNDS):
        half = duals.astype(jnp.bfloat16)
        sent = jnp.concatenate([half, loss_half[None]], axis=0)
        panel = lax.all_gather(sent, "net", axis=0, tiled=True)
        pulled = local_adjoint(local_ids, half, local_blocks)
        flows, bar, terms, loss_half, risk = head_step(
            head_index,
            panel,
            head_blocks,
            pulled,
            flows,
            costs,
            risk,
            node_blks,
            iteration > 0,
            arc_total,
        )
        summed = lax.psum_scatter(terms, "net", scatter_dimension=0, tiled=True)
        base = local_forward(local_ids, bar, local_blocks, duals, wanted)
        mean_risk = sum_over(jnp.sum(risk[:, :1]).reshape(1), "scen") / scen_total
        level_new = level - primal_step * (1.0 - mean_risk)
        level_bar = 2.0 * level_new - level
        excess_new = jnp.maximum(excess_now - primal_step * (tail_weight - risk), 0.0)
        excess_bar = 2.0 * excess_new - excess_now
        risk = risk - risk_step * (excess_bar + level_bar)
        excess_now = excess_new
        level = level_new
        duals = base - dual_step * summed.astype(jnp.float32)
    last = lax.all_gather(loss_half, "net", axis=0, tiled=False).astype(jnp.float32)
    losses = jnp.sum(last, axis=(0, 2)) / arc_total
    risk_last = jnp.maximum(risk[:, 0] + risk_step * losses, 0.0)
    duals_last = duals.transpose(1, 0, 2).reshape(node_duals.shape)
    return (flows, duals_last, excess_now[:, 0], risk_last, level)


def solution(mesh):
    placed = (
        P("scen", "net"),
        P("scen", "net"),
        P("scen", "net"),
        P("scen"),
        P("scen"),
        P(),
        P("net"),
        P("net", None, None, None),
        P("net", None, None),
        P("net", None),
        P("net"),
    )
    return jax.shard_map(
        per_device,
        mesh=mesh,
        in_specs=placed,
        out_specs=(P("scen", "net"), P("scen", "net"), P("scen"), P("scen"), P()),
        check_vma=False,
    )
```

profile of v0, /device:TPU:0, one launch (start us, length us, event | category | flops | bytes accessed | tf_op | source)
XLA Modules:
  0.0 384.6 jit_solution(920454785275563723)
XLA Ops:
  7.2 0.0 copy-start
  7.2 0.0 all-gather.5.cloned.1.call-start
  7.2 0.9 copy-done
  8.1 0.7 concatenate.9
  8.8 0.0 all-gather.5.cloned.1.call-update
  8.8 0.0 reduce-scatter.4.cloned.1.call-start
  8.9 0.8 copy.24
  9.7 0.1 reshape.39.index_ref
  9.8 0.0 copy-start.2
  9.8 8.0 %local_adjoint.3.pulled_ref = f32[32,8192]{1,0:T(8,128)S(1)} custom-call(s32[256]{0:T(256)S(1)} %reshape.39.index_ref, bf16[16,32,128]{2,1,0:T(8,128)(2,1)S(1)} %fusion.3.panel_ref, bf16[64,4,128,128]{3,2,1,0:T(8,128)(2,1)} %blocks_ref.11), custom_call_target="tpu_custom_call" | custom-call | flops 268435456 | bytes 8388608 | tf_op jit(solution)/shard_map/local_adjoint/pallas_call | solution.py:152
  17.8 36.3 %all-gather.5.cloned.1.call-done.panel_ref = bf16[136,32,128]{2,1,0:T(8,128)(2,1)} async-done(((bf16[17,32,128]{2,1,0:T(8,128)(2,1)}), bf16[136,32,128]{2,1,0:T(8,128)(2,1)}) %all-gather.5.cloned.1.call-update) | async-done | bytes 1114128 | tf_op jit(solution)/shard_map/all_gather | solution.py:295
  54.1 0.1 broadcast_in_dim.8.risk_ref
  54.2 14.6 %head_step.3 = (f32[32,8192]{1,0:T(8,128)S(1)}, bf16[32,8192]{1,0:T(8,128)(2,1)S(1)}, bf16[128,32,128]{2,1,0:T(8,128)(2,1)}, bf16[32,128]{1,0:T(8,128)(2,1)S(1)}, f32[32,128]{1,0:T(8,128)S(1)}) custom-call(s32[64]{0:T(128)S(1)} %copy-done.14, bf16[136,32,128]{2,1,0:T(8,128)(2,1)} %all-gather.5.cloned.1.call-done.panel_ref, bf16[64,128,128]{2,1,0:T(8,128)(2,1)} %heads_ref.5, ...), custom_call_target="tpu_custom_call" | custom-call | flops 134217728 | bytes 7995392 | tf_op jit(solution)/shard_map/head_step/pallas_call | solution.py:179
  68.8 1.0 copy-done.1
  69.8 0.0 reduce-scatter.4.cloned.1.call-update
  69.8 0.0 all-gather.7.cloned.1.call-start
  69.8 0.9 copy-done.17
  70.7 7.4 %local_forward.3 = f32[16,32,128]{2,1,0:T(8,128)S(1)} custom-call(s32[256]{0:T(256)S(1)} %reshape.39.index_ref, bf16[32,8192]{1,0:T(8,128)(2,1)S(1)} %get-tuple-element.20.bar_ref, bf16[64,4,128,128]{3,2,1,0:T(8,128)(2,1)} %blocks_ref.11, f32[16,32,128]{2,1,0:T(8,128)S(1)} %get-tuple-element.44.duals_ref, f32[16,32,128]{2,1,0:T(8,128)S(1)} %get-tuple-element.43.demand_ref), custom_call_target="tpu_custom_call" | custom-call | flops 268435456 | bytes 8388608 | tf_op jit(solution)/shard_map/local_forward/pallas_call | solution.py:226
  78.2 54.1 %reduce-scatter.4.cloned.1.call-done = bf16[16,32,128]{2,1,0:T(8,128)(2,1)} async-done(((bf16[128,32,128]{2,1,0:T(8,128)(2,1)}), bf16[16,32,128]{2,1,0:T(8,128)(2,1)}) %reduce-scatter.4.cloned.1.call-update) | async-done | bytes 131088 | tf_op jit(solution)/shard_map/reduce_scatter | solution.py:309
  132.3 0.9 fusion.5
  133.2 0.7 pad_maximum_fusion
  133.9 0.0 all-gather.7.cloned.1.call-update
  133.9 0.0 reduce-scatter.6.cloned.1.call-start
  134.6 0.6 slice_reduce_fusion.1
  135.2 1.4 collective-permute-done
  137.9 2.8 collective-permute-start.1
  140.7 0.9 collective-permute-done.1
  142.3 0.7 add_subtract_fusion.1.risk_ref
  142.9 8.0 %local_adjoint.4.pulled_ref = f32[32,8192]{1,0:T(8,128)S(1)} custom-call(s32[256]{0:T(256)S(1)} %reshape.39.index_ref, bf16[16,32,128]{2,1,0:T(8,128)(2,1)S(1)} %get-tuple-element.41.panel_ref, bf16[64,4,128,128]{3,2,1,0:T(8,128)(2,1)} %blocks_ref.11), custom_call_target="tpu_custom_call" | custom-call | flops 268435456 | bytes 8388608 | tf_op jit(solution)/shard_map/local_adjoint/pallas_call | solution.py:152
  150.9 24.0 %all-gather.7.cloned.1.call-done.panel_ref = bf16[136,32,128]{2,1,0:T(8,128)(2,1)} async-done(((bf16[17,32,128]{2,1,0:T(8,128)(2,1)}), bf16[136,32,128]{2,1,0:T(8,128)(2,1)}) %all-gather.7.cloned.1.call-update) | async-done | bytes 1114128 | tf_op jit(solution)/shard_map/all_gather | solution.py:295
  175.0 0.8 copy-done.3
  175.7 0.7 copy-done.5
  176.4 0.7 copy-done.15
  177.1 14.6 %head_step.4 = (f32[32,8192]{1,0:T(8,128)S(1)}, bf16[32,8192]{1,0:T(8,128)(2,1)S(1)}, bf16[128,32,128]{2,1,0:T(8,128)(2,1)}, bf16[32,128]{1,0:T(8,128)(2,1)S(1)}, f32[32,128]{1,0:T(8,128)S(1)}) custom-call(s32[64]{0:T(128)S(1)} %copy-done.15, bf16[136,32,128]{2,1,0:T(8,128)(2,1)} %all-gather.7.cloned.1.call-done.panel_ref, bf16[64,128,128]{2,1,0:T(8,128)(2,1)} %heads_ref.5, ...), custom_call_target="tpu_custom_call" | custom-call | flops 134217728 | bytes 7995392 | tf_op jit(solution)/shard_map/head_step/pallas_call | solution.py:179
  191.7 0.0 reduce-scatter.6.cloned.1.call-update
  191.7 0.0 all-gather.9.cloned.1.call-start
  191.8 7.4 %local_forward.4 = f32[16,32,128]{2,1,0:T(8,128)S(1)} custom-call(s32[256]{0:T(256)S(1)} %copy-done.10, bf16[32,8192]{1,0:T(8,128)(2,1)S(1)} %get-tuple-element.25.bar_ref, bf16[64,4,128,128]{3,2,1,0:T(8,128)(2,1)} %blocks_ref.11, f32[16,32,128]{2,1,0:T(8,128)S(1)} %get-tuple-element.42.duals_ref, f32[16,32,128]{2,1,0:T(8,128)S(1)} %get-tuple-element.43.demand_ref), custom_call_target="tpu_custom_call" | custom-call | flops 268435456 | bytes 8388608 | tf_op jit(solution)/shard_map/local_forward/pallas_call | solution.py:226
  199.2 55.0 %reduce-scatter.6.cloned.1.call-done = bf16[16,32,128]{2,1,0:T(8,128)(2,1)} async-done(((bf16[128,32,128]{2,1,0:T(8,128)(2,1)}), bf16[16,32,128]{2,1,0:T(8,128)(2,1)}) %reduce-scatter.6.cloned.1.call-update) | async-done | bytes 131088 | tf_op jit(solution)/shard_map/reduce_scatter | solution.py:309
  254.2 1.0 fusion.4
  255.2 1.4 pad_maximum_fusion.1
  256.6 0.0 all-gather.9.cloned.1.call-update
  256.6 0.0 reduce-scatter.8.cloned.1.call-start
  256.6 0.6 slice_reduce_fusion
  257.3 1.4 collective-permute-done.2
  259.9 2.8 collective-permute-start.3
  262.8 0.9 collective-permute-done.3
  264.3 0.7 add_subtract_fusion
  265.0 8.0 %local_adjoint.5.pulled_ref = f32[32,8192]{1,0:T(8,128)S(1)} custom-call(s32[256]{0:T(256)S(1)} %copy-done.11, bf16[16,32,128]{2,1,0:T(8,128)(2,1)S(1)} %get-tuple-element.39.panel_ref, bf16[64,4,128,128]{3,2,1,0:T(8,128)(2,1)} %blocks_ref.11), custom_call_target="tpu_custom_call" | custom-call | flops 268435456 | bytes 8388608 | tf_op jit(solution)/shard_map/local_adjoint/pallas_call | solution.py:152
  273.0 23.5 %all-gather.9.cloned.1.call-done.panel_ref = bf16[136,32,128]{2,1,0:T(8,128)(2,1)} async-done(((bf16[17,32,128]{2,1,0:T(8,128)(2,1)}), bf16[136,32,128]{2,1,0:T(8,128)(2,1)}) %all-gather.9.cloned.1.call-update) | async-done | bytes 1114128 | tf_op jit(solution)/shard_map/all_gather | solution.py:295
  296.4 0.8 copy-done.4
  297.2 0.7 copy-done.16
  297.9 14.6 %head_step.5 = (f32[32,8192]{1,0:T(8,128)}, bf16[32,8192]{1,0:T(8,128)(2,1)S(1)}, bf16[128,32,128]{2,1,0:T(8,128)(2,1)}, bf16[32,128]{1,0:T(8,128)(2,1)S(1)}, f32[32,128]{1,0:T(8,128)S(1)}) custom-call(s32[64]{0:T(128)S(1)} %copy-done.16, bf16[136,32,128]{2,1,0:T(8,128)(2,1)} %all-gather.9.cloned.1.call-done.panel_ref, bf16[64,128,128]{2,1,0:T(8,128)(2,1)} %heads_ref.5, ...), custom_call_target="tpu_custom_call" | custom-call | flops 134217728 | bytes 7995392 | tf_op jit(solution)/shard_map/head_step/pallas_call | solution.py:179
  312.5 0.0 reduce-scatter.8.cloned.1.call-update
  312.5 0.6 slice_reduce_fusion.2
  313.1 30.5 %all-gather = bf16[256,128]{1,0:T(8,128)(2,1)S(1)} all-gather(bf16[32,128]{1,0:T(8,128)(2,1)S(1)} %get-tuple-element.34), channel_id=2, replica_groups=mesh['net'=8,'scen'=4] {'net'}, dimensions={0}, use_global_device_ids=true | all-gather | bytes 73728 | tf_op jit(solution)/shard_map/all_gather | solution.py:320
  343.6 0.1 convert_reduce_fusion
  343.7 0.1 reshape.49
  343.8 7.4 %local_forward.5 = f32[16,32,128]{2,1,0:T(8,128)S(1)} custom-call(s32[256]{0:T(256)S(1)} %copy-done.12, bf16[32,8192]{1,0:T(8,128)(2,1)S(1)} %get-tuple-element.31.bar_ref, bf16[64,4,128,128]{3,2,1,0:T(8,128)(2,1)} %blocks_ref.11, f32[16,32,128]{2,1,0:T(8,128)S(1)} %get-tuple-element.40.duals_ref, f32[16,32,128]{2,1,0:T(8,128)S(1)} %get-tuple-element.43.demand_ref), custom_call_target="tpu_custom_call" | custom-call | flops 268435456 | bytes 8388608 | tf_op jit(solution)/shard_map/local_forward/pallas_call | solution.py:226
  352.5 2.8 collective-permute-start.5
  355.3 0.9 collective-permute-done.5
  356.8 0.6 fusion.2
  357.4 0.5 add_maximum_fusion
  357.9 17.0 %reduce-scatter.8.cloned.1.call-done = bf16[16,32,128]{2,1,0:T(8,128)(2,1)} async-done(((bf16[128,32,128]{2,1,0:T(8,128)(2,1)}), bf16[16,32,128]{2,1,0:T(8,128)(2,1)}) %reduce-scatter.8.cloned.1.call-update) | async-done | bytes 131088 | tf_op jit(solution)/shard_map/reduce_scatter | solution.py:309
  375.0 1.6 copy_bitcast_fusion
  (42 shorter events, 0.2 us)
Async XLA Ops:
  7.2 1.0 copy-start
  7.2 46.9 %all-gather.5.cloned.1.call-start = ((), (), s32[]{:S(2)}) async-start(), calls=%async_computation.3 | async-start | bytes 1253376 | tf_op jit(solution)/shard_map/all_gather | solution.py:295
  8.8 123.4 %reduce-scatter.4.cloned.1.call-start = ((), (), s32[]{:S(2)}) async-start(), calls=%async_computation.4 | async-start | bytes 1179648 | tf_op jit(solution)/shard_map/reduce_scatter | solution.py:309
  9.8 133.2 %copy-start.9 = (s32[256]{0:T(256)}, s32[256]{0:T(256)S(1)}, u32[]{:S(2)}) copy-start(s32[256]{0:T(256)S(1)} %reshape.39.index_ref) | copy-start | bytes 3076
  9.8 44.3 %copy-start.21 = (f32[32]{0:T(128)S(1)}, f32[32]{0:T(128)}, u32[]{:S(2)}) copy-start(f32[32]{0:T(128)} %param.15) | copy-start | bytes 388
  9.8 44.4 %copy-start.2 = (f32[8192]{0:T(1024)S(1)}, f32[8192]{0:T(1024)}, u32[]{:S(2)}) copy-start(f32[8192]{0:T(1024)} %param.17) | copy-start | bytes 98308
  9.8 44.4 %copy-start.14 = (s32[64]{0:T(128)S(1)}, s32[64]{0:T(128)}, u32[]{:S(2)}) copy-start(s32[64]{0:T(128)} %index_ref.5) | copy-start | bytes 772
  68.8 1.0 copy-start.1
  69.7 0.9 copy-start.17
  69.8 105.2 %all-gather.7.cloned.1.call-start = ((), (), s32[]{:S(2)}) async-start(), calls=%async_computation.5 | async-start | bytes 1253376 | tf_op jit(solution)/shard_map/all_gather | solution.py:295
  78.2 64.1 %copy-start.19 = (f32[32]{0:T(128)S(1)}, f32[32]{0:T(128)}, u32[]{:S(2)}) copy-start(f32[32]{0:T(128)} %param.14) | copy-start | bytes 388
  133.9 120.3 %reduce-scatter.6.cloned.1.call-start = ((), (), s32[]{:S(2)}) async-start(), calls=%async_computation.6 | async-start | bytes 1179648 | tf_op jit(solution)/shard_map/reduce_scatter | solution.py:309
  135.2 1.4 collective-permute-start
  137.9 3.7 collective-permute-start.1
  175.0 0.8 copy-start.3
  175.7 0.7 copy-start.5
  176.4 0.7 copy-start.15
  177.1 14.7 %copy-start.10 = (s32[256]{0:T(256)S(1)}, s32[256]{0:T(256)}, u32[]{:S(2)}) copy-start(s32[256]{0:T(256)} %copy-done.9) | copy-start | bytes 3076
  191.7 7.5 %copy-start.7 = (f32[32,128]{1,0:T(8,128)}, f32[32,128]{1,0:T(8,128)S(1)}, u32[]{:S(2)}) copy-start(f32[32,128]{1,0:T(8,128)S(1)} %get-tuple-element.29) | copy-start | bytes 49156
  191.7 7.5 %copy-start.13 = (bf16[32,128]{1,0:T(8,128)(2,1)}, bf16[32,128]{1,0:T(8,128)(2,1)S(1)}, u32[]{:S(2)}) copy-start(bf16[32,128]{1,0:T(8,128)(2,1)S(1)} %get-tuple-element.27) | copy-start | bytes 24580
  191.7 104.7 %all-gather.9.cloned.1.call-start = ((), (), s32[]{:S(2)}) async-start(), calls=%async_computation.7 | async-start | bytes 1253376 | tf_op jit(solution)/shard_map/all_gather | solution.py:295
  199.2 65.1 %copy-start.20 = (f32[32]{0:T(128)S(1)}, f32[32]{0:T(128)}, u32[]{:S(2)}) copy-start(f32[32]{0:T(128)} %param.14) | copy-start | bytes 388
  199.2 65.8 %copy-start.11 = (s32[256]{0:T(256)S(1)}, s32[256]{0:T(256)}, u32[]{:S(2)}) copy-start(s32[256]{0:T(256)} %copy-done.9) | copy-start | bytes 3076
  254.2 2.4 copy-start.8
  256.6 118.4 %reduce-scatter.8.cloned.1.call-start = ((), (), s32[]{:S(2)}) async-start(), calls=%async_computation.8 | async-start | bytes 1179648 | tf_op jit(solution)/shard_map/reduce_scatter | solution.py:309
  257.2 1.4 collective-permute-start.2
  259.9 3.7 collective-permute-start.3
  265.0 31.5 %copy-start.6 = (f32[32,128]{1,0:T(8,128)S(1)}, f32[32,128]{1,0:T(8,128)}, u32[]{:S(2)}) copy-start(f32[32,128]{1,0:T(8,128)} %get-tuple-element.37.risk_ref) | copy-start | bytes 49156
  296.4 0.8 copy-start.4
  297.2 0.7 copy-start.16
  312.5 31.3 %copy-start.12 = (s32[256]{0:T(256)S(1)}, s32[256]{0:T(256)}, u32[]{:S(2)}) copy-start(s32[256]{0:T(256)} %copy-done.9) | copy-start | bytes 3076
  313.1 38.2 %collective-permute-start.4 = (f32[1]{0:T(128)}, f32[1]{0:T(128)}, u32[]{:S(2)}, u32[]{:S(2)}) collective-permute-start(f32[1]{0:T(128)} %bitcast.10), channel_id=1, source_target_pairs={{0,1},{1,0},{2,3},{3,2},{4,5},{5,4},{6,7},{7,6},{8,9},{9,8},{10,11... | collective-permute-start | bytes 20 | tf_op jit(solution)/shard_map/ppermute | solution.py:255
  343.8 7.4 %copy-start.18 = (f32[32,128]{1,0:T(8,128)S(1)}, f32[32,128]{1,0:T(8,128)}, u32[]{:S(2)}) copy-start(f32[32,128]{1,0:T(8,128)} %get-tuple-element.38) | copy-start | bytes 49156
  352.5 3.7 collective-permute-start.5
Sparse Core Ops, SparseCore 0:
  10.8 43.2 all-gather.4
  69.9 62.3 reduce-scatter.3
  135.3 39.6 all-gather.6
  191.8 62.3 reduce-scatter.5
  256.8 39.5 all-gather.8
  312.6 62.2 reduce-scatter.7
where the time goes:
time: 386 us; the launch traced here: 385 us
  waiting for transfers between devices  215 us (56%)
  Pallas kernels  90 us (23%)
  blocking collectives  30.5 us (8%)
  between operations  21.8 us (6%)
  other arithmetic  10 us (3%)
  starting transfers between devices  8.76 us (2%)
  local copies, waits for them, and re-layouts  8.09 us (2%)
    reduce_scatter x3, waiting for transfers between devices, per_device(): summed = lax.psum_scatter(terms, 'net', scatter_dimension=0, tiled=True)  126 us
    all_gather x3, waiting for transfers between devices, per_device(): panel = lax.all_gather(sent, 'net', axis=0, tiled=True)  83.8 us
    pallas_call x3, Pallas kernels, head_step(): pl.pallas_call(functools.partial(head_kernel, group, steps, node_blks, ha...  43.8 us
    all_gather x1, blocking collectives, per_device(): lax.all_gather(loss_half, 'net', axis=0, tiled=False).astype(jnp.float32)  30.5 us
    pallas_call x3, Pallas kernels, local_adjoint(): pl.pallas_call(functools.partial(local_adjoint_kernel, touches, group), o...  24 us
    pallas_call x3, Pallas kernels, local_forward(): pl.pallas_call(functools.partial(local_forward_kernel, touches, group, st...  22.2 us
    ppermute x6, starting transfers between devices, sum_over(): lax.ppermute(value, axis, [(i, i ^ stride) for i in range(size)])  8.51 us
  transfers between devices with their start and end apart: 12, of which 11 were waited for; matrix products, arithmetic and copies ran while one was open for 1% of the time, Pallas kernels for 12%

commit v1 on v0

--- a/solution.py
+++ b/solution.py
@@ -14,8 +14,9 @@
 risk_step = 1.0
 tail_weight = 2.0
 
-VMEM_LIMIT = 50 * 1024 * 1024
+MIB = 1024 * 1024
 GROUP = 8
+HEAD_GROUP = 16
 
 
 def contract_last(left, right):
@@ -36,66 +37,48 @@
         out_ref[:, member * rows : (member + 1) * rows] = contract_last(left, right)
 
 
-def head_kernel(
-    group,
-    steps,
-    node_blks,
-    has_losses,
-    arc_total,
-    index_ref,
-    panel_ref,
-    heads_ref,
-    pulled_ref,
-    flows_ref,
-    costs_ref,
-    risk_ref,
-    flows_out,
-    bar_out,
-    terms_out,
-    loss_out,
-    risk_out,
-    terms,
-    loss,
-):
+def head_kernel(group, steps, peers, index_ref, *refs):
+    panels, refs = refs[:peers], refs[peers:]
+    heads_ref, pulled_ref, flows_ref, costs_ref, risk_ref = refs[:5]
+    flows_out, bar_out, refs = refs[5], refs[6], refs[7:]
+    sends, (panel, terms, pulled, loss) = refs[:peers], refs[peers:]
     rows = heads_ref.shape[-1]
+    node_blks = panels[0].shape[0]
     step = pl.program_id(0)
     first = step * group
-    chunk = node_blks + 1
 
     @pl.when(step == 0)
     def _():
         terms[...] = jnp.zeros_like(terms)
         loss[...] = jnp.zeros_like(loss)
-        risk_start = risk_ref[...]
-        if has_losses:
-            arrived = jnp.zeros_like(risk_start)
-            for source in range(panel_ref.shape[0] // chunk):
-                arrived += panel_ref[source * chunk + node_blks].astype(jnp.float32)
-            losses = jnp.sum(arrived, axis=1, keepdims=True) / arc_total
-            risk_start = jnp.maximum(risk_start + risk_step * losses, 0.0)
-        risk_out[...] = risk_start
-
-    risk = risk_out[...]
+        for peer in range(peers):
+            panel[peer * node_blks : (peer + 1) * node_blks] = panels[peer][...]
+
+    places = [index_ref[first + member] for member in range(group)]
+    spans = [slice(member * rows, (member + 1) * rows) for member in range(group)]
+    for member in range(group):
+        pulled[:, spans[member]] = contract_last(panel[places[member]], heads_ref[member])
+    risk = risk_ref[...]
     loss_sum = jnp.zeros_like(risk)
-    for member in range(group):
-        head = index_ref[first + member]
-        place = head + lax.div(head, node_blks)
-        columns = slice(member * rows, (member + 1) * rows)
-        pulled = pulled_ref[:, columns] + contract_last(panel_ref[place], heads_ref[member])
+    for columns in spans:
         flows = flows_ref[:, columns]
         cost = costs_ref[:, columns]
-        flows_new = jnp.maximum(flows - primal_step * (risk * cost - pulled), 0.0)
+        gradient = risk * cost - (pulled[:, columns] + pulled_ref[:, columns])
+        flows_new = jnp.maximum(flows - primal_step * gradient, 0.0)
         bar = 2.0 * flows_new - flows
         flows_out[:, columns] = flows_new
         loss_sum += cost * bar
-        half = bar.astype(jnp.bfloat16)
-        bar_out[:, columns] = half
-        terms[head] += jnp.dot(half, heads_ref[member], preferred_element_type=jnp.float32)
+        bar_out[:, columns] = bar.astype(jnp.bfloat16)
     loss[...] += loss_sum
+    products = [
+        jnp.dot(bar_out[:, spans[m]], heads_ref[m], preferred_element_type=jnp.float32)
+        for m in range(group)
+    ]
+    for member in range(group):
+        terms[places[member]] += products[member]
 
     @pl.when(step == steps - 1)
     def _():
-        terms_out[...] = terms[...].astype(jnp.bfloat16)
         total = jnp.sum(loss[...], axis=1, keepdims=True)
         high = total.astype(jnp.bfloat16).astype(jnp.float32)
         rest = total - high
@@ -104,8 +87,33 @@
         lane = lax.broadcasted_iota(jnp.int32, loss.shape, 1)
         packed = jnp.where(
             lane == 0, high, jnp.where(lane == 1, middle, jnp.where(lane == 2, low, 0.0))
-        )
-        loss_out[...] = packed.astype(jnp.bfloat16)
+        ).astype(jnp.bfloat16)
+        for peer in range(peers):
+            sends[peer][:node_blks] = terms[peer * node_blks : (peer + 1) * node_blks].astype(
+                jnp.bfloat16
+            )
+            sends[peer][node_blks] = packed
+
+
+def pair_sum(values):
+    while len(values) > 1:
+        values = [a + b for a, b in zip(values[::2], values[1::2])]
+    return values[0]
+
+
+def settle_kernel(peers, arc_total, *refs):
+    arrived, (base_ref, risk_ref, duals_out, half_out, risk_out) = refs[:peers], refs[peers:]
+    node_blks = base_ref.shape[0]
+    for block in range(node_blks):
+        total = pair_sum([ref[block].astype(jnp.float32) for ref in arrived])
+        duals = base_ref[block] - dual_step * total
+        duals_out[block] = duals
+        half_out[block] = duals.astype(jnp.bfloat16)
+    parts = [
+        jnp.sum(ref[node_blks].astype(jnp.float32), axis=1, keepdims=True) for ref in arrived
+    ]
+    losses = pair_sum(parts) / arc_total
+    risk_out[...] = jnp.maximum(risk_ref[...] + risk_step * losses, 0.0)
 
 
 def local_forward_kernel(
@@ -139,9 +147,13 @@
     return pl.BlockSpec(shape, lambda i, *_: (0,) * len(shape))
 
 
-def params():
+def vmem_limit(peers):
+    return (8 + peers + peers // 4) * MIB
+
+
+def params(peers=8):
     return pltpu.CompilerParams(
-        dimension_semantics=("arbitrary",), vmem_limit_bytes=VMEM_LIMIT
+        dimension_semantics=("arbitrary",), vmem_limit_bytes=vmem_limit(peers)
     )
 
 
@@ -169,53 +181,64 @@
     )(index, panel, blocks)
 
 
-def head_step(index, panel, heads, pulled, flows, costs, risk, node_blks, has_losses, arc_total):
+def head_step(places, panels, heads, pulled, flows, costs, risk):
     arc_blks, rows, _ = heads.shape
     scen_rows = flows.shape[0]
-    group = GROUP
+    peers = len(panels)
+    node_blks = panels[0].shape[0]
+    group = HEAD_GROUP
     steps = arc_blks // group
-    node_total = panel.shape[0] // (node_blks + 1) * node_blks
+    sent = (node_blks + 1, scen_rows, rows)
     arcs = pl.BlockSpec((scen_rows, group * rows), lambda i, *_: (0, i))
-    return pl.pallas_call(
-        functools.partial(head_kernel, group, steps, node_blks, has_losses, arc_total),
-        out_shape=(
+    results = pl.pallas_call(
+        functools.partial(head_kernel, group, steps, peers),
+        out_shape=[
             jax.ShapeDtypeStruct(flows.shape, jnp.float32),
             jax.ShapeDtypeStruct(flows.shape, jnp.bfloat16),
-            jax.ShapeDtypeStruct((node_total, scen_rows, rows), jnp.bfloat16),
-            jax.ShapeDtypeStruct((scen_rows, rows), jnp.bfloat16),
-            jax.ShapeDtypeStruct((scen_rows, rows), jnp.float32),
-        ),
+        ]
+        + [jax.ShapeDtypeStruct(sent, jnp.bfloat16)] * peers,
         grid_spec=pltpu.PrefetchScalarGridSpec(
             num_scalar_prefetch=1,
             grid=(steps,),
-            in_specs=[
-                whole(*panel.shape),
+            in_specs=[whole(*panels[0].shape)] * peers
+            + [
                 pl.BlockSpec((group, rows, rows), lambda i, *_: (i, 0, 0)),
                 arcs,
                 arcs,
                 pl.BlockSpec((1, group * rows), lambda i, *_: (0, i)),
                 whole(scen_rows, rows),
             ],
-            out_specs=[
-                arcs,
-                arcs,
-                whole(node_total, scen_rows, rows),
-                whole(scen_rows, rows),
-                whole(scen_rows, rows),
-            ],
+            out_specs=[arcs, arcs] + [whole(*sent)] * peers,
             scratch_shapes=[
-                pltpu.VMEM((node_total, scen_rows, rows), jnp.float32),
+                pltpu.VMEM((peers * node_blks, scen_rows, rows), jnp.bfloat16),
+                pltpu.VMEM((peers * node_blks, scen_rows, rows), jnp.float32),
+                pltpu.VMEM((scen_rows, group * rows), jnp.float32),
                 pltpu.VMEM((scen_rows, rows), jnp.float32),
             ],
         ),
-        compiler_params=params(),
+        compiler_params=params(peers),
         cost_estimate=pl.CostEstimate(
             flops=4 * scen_rows * heads.size,
-            bytes_accessed=2 * heads.size + 14 * flows.size + 4 * panel.size,
+            bytes_accessed=2 * heads.size + 14 * flows.size + 4 * peers * panels[0].size,
             transcendentals=0,
         ),
         name="head_step",
-    )(index, panel, heads, pulled, flows, costs, risk)
+    )(places, *panels, heads, pulled, flows, costs, risk)
+    return results[0], results[1], results[2:]
+
+
+def settle(arrived, base, risk, arc_total):
+    peers = len(arrived)
+    return pl.pallas_call(
+        functools.partial(settle_kernel, peers, arc_total),
+        out_shape=(
+            jax.ShapeDtypeStruct(base.shape, jnp.float32),
+            jax.ShapeDtypeStruct(base.shape, jnp.bfloat16),
+            jax.ShapeDtypeStruct(risk.shape, jnp.float32),
+        ),
+        compiler_params=pltpu.CompilerParams(vmem_limit_bytes=vmem_limit(peers)),
+        name="settle",
+    )(*arrived, base, risk)
 
 
 def local_forward(index, bar, blocks, duals, demand):
@@ -246,15 +269,31 @@
     )(index, bar, blocks, duals, demand)
 
 
+def swap(value, axis, distance):
+    size = lax.axis_size(axis)
+    return lax.ppermute(value, axis, [(i, i ^ distance) for i in range(size)])
+
+
 def sum_over(value, axis):
-    size = lax.axis_size(axis)
-    if size & (size - 1):
-        return lax.psum(value, axis)
     stride = 1
-    while stride < size:
-        value = value + lax.ppermute(value, axis, [(i, i ^ stride) for i in range(size)])
+    while stride < lax.axis_size(axis):
+        value = value + swap(value, axis, stride)
         stride *= 2
     return value
+
+
+def gather_panels(own):
+    size = lax.axis_size("net")
+    panels = [own] + [None] * (size - 1)
+    for distance in range(2, size, 2):
+        panels[distance] = swap(own, "net", distance)
+    for distance in range(0, size, 2):
+        panels[distance + 1] = swap(panels[distance], "net", 1)
+    return panels
+
+
+def exchange(sends):
+    return [sends[0]] + [swap(sends[k], "net", k) for k in range(1, len(sends))]
 
 
 def per_device(
@@ -278,50 +317,36 @@
     scen_total = scen_rows * lax.axis_size("scen")
     local_ids = local_index.reshape(-1)
     costs = arc_costs.reshape(1, -1)
+    distance = jnp.bitwise_xor(head_index // node_blks, lax.axis_index("net"))
+    places = distance * node_blks + head_index % node_blks
 
     def to_blocks(panel):
         return panel.reshape(scen_rows, node_blks, rows).transpose(1, 0, 2)
 
     duals = to_blocks(node_duals)
+    half = duals.astype(jnp.bfloat16)
     wanted = to_blocks(demand)
     flows = arc_flows
     excess_now = jnp.broadcast_to(excess[:, None], (scen_rows, rows))
     risk = jnp.broadcast_to(risk_duals[:, None], (scen_rows, rows))
     level = threshold
-    loss_half = jnp.zeros((scen_rows, rows), jnp.bfloat16)
     for iteration in range(ROUNDS):
-        half = duals.astype(jnp.bfloat16)
-        sent = jnp.concatenate([half, loss_half[None]], axis=0)
-        panel = lax.all_gather(sent, "net", axis=0, tiled=True)
+        panels = gather_panels(half)
         pulled = local_adjoint(local_ids, half, local_blocks)
-        flows, bar, terms, loss_half, risk = head_step(
-            head_index,
-            panel,
-            head_blocks,
-            pulled,
-            flows,
-            costs,
-            risk,
-            node_blks,
-            iteration > 0,
-            arc_total,
-        )
-        summed = lax.psum_scatter(terms, "net", scatter_dimension=0, tiled=True)
-        base = local_forward(local_ids, bar, local_blocks, duals, wanted)
         mean_risk = sum_over(jnp.sum(risk[:, :1]).reshape(1), "scen") / scen_total
         level_new = level - primal_step * (1.0 - mean_risk)
         level_bar = 2.0 * level_new - level
         excess_new = jnp.maximum(excess_now - primal_step * (tail_weight - risk), 0.0)
         excess_bar = 2.0 * excess_new - excess_now
-        risk = risk - risk_step * (excess_bar + level_bar)
+        flows, bar, sends = head_step(places, panels, head_blocks, pulled, flows, costs, risk)
+        arrived = exchange(sends)
+        base = local_forward(local_ids, bar, local_blocks, duals, wanted)
+        shifted = risk - risk_step * (excess_bar + level_bar)
+        duals, half, risk = settle(arrived, base, shifted, arc_total)
         excess_now = excess_new
         level = level_new
-        duals = base - dual_step * summed.astype(jnp.float32)
-    last = lax.all_gather(loss_half, "net", axis=0, tiled=False).astype(jnp.float32)
-    losses = jnp.sum(last, axis=(0, 2)) / arc_total
-    risk_last = jnp.maximum(risk[:, 0] + risk_step * losses, 0.0)
     duals_last = duals.transpose(1, 0, 2).reshape(node_duals.shape)
-    return (flows, duals_last, excess_now[:, 0], risk_last, level)
+    return (flows, duals_last, excess_now[:, 0], risk[:, 0], level)
 
 
 def solution(mesh):

time: 386 us -> 193 us (0.50)
  waiting for transfers between devices: 215 us -> 57.2 us
  starting transfers between devices: 8.76 us -> 78.2 us
  Pallas kernels: 90 us -> 35.4 us
  blocking collectives: 30.5 us -> 0 us
  between operations: 21.8 us -> 8.02 us
  other arithmetic: 10 us -> 2.65 us
    reduce_scatter x3 -> x0, waiting for transfers between devices: 126 us -> none  [per_device(): summed = lax.psum_scatter(terms, 'net', scatter_dimension=0, tiled=True)]
    all_gather x3 -> x0, waiting for transfers between devices: 83.8 us -> none  [per_device(): panel = lax.all_gather(sent, 'net', axis=0, tiled=True)]
    ppermute x6 -> x48, starting transfers between devices: 8.51 us -> 78.2 us  [swap(): return lax.ppermute(value, axis, [(i, i ^ distance) for i in range(size)])]
    ppermute x6 -> x48, waiting for transfers between devices: 5.39 us -> 57.2 us  [swap(): return lax.ppermute(value, axis, [(i, i ^ distance) for i in range(size)])]
    pallas_call x3 -> x6, Pallas kernels: 43.8 us -> 12.6 us  [the longest x3 11.1 us: head_step(): pl.pallas_call(functools.partial(head_kernel, group, steps, peers), out_s...]
    all_gather x1 -> x0, blocking collectives: 30.5 us -> none  [per_device(): lax.all_gather(loss_half, 'net', axis=0, tiled=False).astype(jnp.float32)]
    pallas_call x3, Pallas kernels: 22.2 us -> 9.98 us  [local_forward(): pl.pallas_call(functools.partial(local_forward_kernel, touches, group, st...]
    pallas_call x3, Pallas kernels: 24 us -> 12.8 us  [local_adjoint(): pl.pallas_call(functools.partial(local_adjoint_kernel, touches, group), o...]
  transfers between devices with their start and end apart: 12 -> 48, of which waited for: 11 -> 16; matrix products, arithmetic and copies ran while one was open for 1% -> 2% of each run, Pallas kernels for 12% -> 14%
where the time goes in v1:
time: 193 us; the launch traced here: 190 us
  starting transfers between devices  78.2 us (41%)
  waiting for transfers between devices  57.2 us (30%)
  Pallas kernels  35.4 us (18%)
  local copies, waits for them, and re-layouts  8.97 us (5%)
  between operations  8.02 us (4%)
  other arithmetic  2.65 us (1%)
    ppermute x48, starting transfers between devices, swap(): return lax.ppermute(value, axis, [(i, i ^ distance) for i in range(size)])  78.2 us
    ppermute x48, waiting for transfers between devices, swap(): return lax.ppermute(value, axis, [(i, i ^ distance) for i in range(size)])  57.2 us
    pallas_call x3, Pallas kernels, local_adjoint(): pl.pallas_call(functools.partial(local_adjoint_kernel, touches, group), o...  12.8 us
    pallas_call x3, Pallas kernels, head_step(): pl.pallas_call(functools.partial(head_kernel, group, steps, peers), out_s...  11.1 us
    pallas_call x3, Pallas kernels, local_forward(): pl.pallas_call(functools.partial(local_forward_kernel, touches, group, st...  9.98 us
    unnamed x23, local copies, waits for them, and re-layouts  6.7 us
  transfers between devices with their start and end apart: 48, of which 16 were waited for; matrix products, arithmetic and copies ran while one was open for 2% of the time, Pallas kernels for 14%

profile of v1, /device:TPU:0, one launch (start us, length us, event | category | flops | bytes accessed | tf_op | source)
XLA Modules:
  0.0 190.4 jit_solution(15424003557785051363)
XLA Ops:
  0.7 0.9 copy-done
  1.6 5.1 %collective-permute-start.5 = (bf16[16,32,128]{2,1,0:T(8,128)(2,1)S(1)}, bf16[16,32,128]{2,1,0:T(8,128)(2,1)S(1)}, u32[]{:S(2)}, u32[]{:S(2)}) collective-permute-start(bf16[16,32,128]{2,1,0:T(8,128)(2,1)S(1)} %fusion.1.panel_ref.refs_0_), channel_id=1, source_target_pairs={{0,24},{4,28},{8,16},{12,20},{16,8},{20,12},{24,0},{28,4},{1,25},{... | collective-permute-start | bytes 393224 | tf_op jit(solution)/shard_map/ppermute | solution.py:274
  6.7 0.6 collective-permute-start.1
  7.4 1.6 collective-permute-start
  9.0 1.3 reduce_sum.27
  10.9 0.8 copy.17
  11.8 3.4 %copy-done.1 = bf16[64,4,128,128]{3,2,1,0:T(8,128)(2,1)S(1)} copy-done((bf16[64,4,128,128]{3,2,1,0:T(8,128)(2,1)S(1)}, bf16[64,4,128,128]{3,2,1,0:T(8,128)(2,1)}, u32[]{:S(2)}) %copy-start.1) | copy-done | bytes 8388632
  15.2 4.3 %local_adjoint.3.refs_9_ = f32[32,8192]{1,0:T(8,128)S(1)} custom-call(s32[256]{0:T(256)S(1)} %reshape.41.index_ref, bf16[16,32,128]{2,1,0:T(8,128)(2,1)S(1)} %fusion.1.panel_ref.refs_0_, bf16[64,4,128,128]{3,2,1,0:T(8,128)(2,1)S(1)} %copy-done.1), custom_call_target="tpu_custom_call" | custom-call | flops 268435456 | bytes 8388608 | tf_op jit(solution)/shard_map/local_adjoint/pallas_call | solution.py:164
  20.0 1.6 collective-permute-start.4
  22.0 3.8 %collective-permute-done.6.refs_7_ = bf16[16,32,128]{2,1,0:T(8,128)(2,1)S(1)} collective-permute-done((bf16[16,32,128]{2,1,0:T(8,128)(2,1)S(1)}, bf16[16,32,128]{2,1,0:T(8,128)(2,1)S(1)}, u32[]{:S(2)}, u32[]{:S(2)}) %collective-permute-start.6) | collective-permute-done | bytes 131104 | tf_op jit(solution)/shard_map/ppermute | solution.py:274
  25.9 2.8 %collective-permute-done.4.refs_5_ = bf16[16,32,128]{2,1,0:T(8,128)(2,1)S(1)} collective-permute-done((bf16[16,32,128]{2,1,0:T(8,128)(2,1)S(1)}, bf16[16,32,128]{2,1,0:T(8,128)(2,1)S(1)}, u32[]{:S(2)}, u32[]{:S(2)}) %collective-permute-start.4) | collective-permute-done | bytes 131104 | tf_op jit(solution)/shard_map/ppermute | solution.py:274
  28.7 2.4 %collective-permute-done.2.refs_3_ = bf16[16,32,128]{2,1,0:T(8,128)(2,1)S(1)} collective-permute-done((bf16[16,32,128]{2,1,0:T(8,128)(2,1)S(1)}, bf16[16,32,128]{2,1,0:T(8,128)(2,1)S(1)}, u32[]{:S(2)}, u32[]{:S(2)}) %collective-permute-start.2) | collective-permute-done | bytes 131104 | tf_op jit(solution)/shard_map/ppermute | solution.py:274
  31.2 1.6 copy-done.3
  32.8 3.5 %head_step.3 = (f32[32,8192]{1,0:T(8,128)S(1)}, bf16[32,8192]{1,0:T(8,128)(2,1)S(1)}, bf16[17,32,128]{2,1,0:T(8,128)(2,1)S(1)}, bf16[17,32,128]{2,1,0:T(8,128)(2...) custom-call(s32[64]{0:T(128)S(1)} %fusion.index_ref, ...), custom_call_target="tpu_custom_call" | custom-call | flops 134217728 | bytes 7864320 | tf_op jit(solution)/shard_map/head_step/pallas_call | solution.py:193
  36.7 1.4 collective-permute-start.8
  39.4 2.9 %collective-permute-start.15 = (f32[1]{0:T(128)}, f32[1]{0:T(128)}, u32[]{:S(2)}, u32[]{:S(2)}) collective-permute-start(f32[1]{0:T(128)} %add.61), channel_id=1, source_target_pairs={{0,2},{1,3},{2,0},{3,1},{4,6},{5,7},{6,4},{7,5},{8,10},{9,11},{10,... | collective-permute-start | bytes 20 | tf_op jit(solution)/shard_map/ppermute | solution.py:274
  42.2 0.8 collective-permute-done.15
  43.7 1.8 collective-permute-start.9
  45.4 2.1 %collective-permute-start.10 = (bf16[17,32,128]{2,1,0:T(8,128)(2,1)S(1)}, bf16[17,32,128]{2,1,0:T(8,128)(2,1)S(1)}, u32[]{:S(2)}, u32[]{:S(2)}) collective-permute-start(bf16[17,32,128]{2,1,0:T(8,128)(2,1)S(1)} %get-tuple-element.47), channel_id=1, source_target_pairs={{0,16},{4,20},{8,24},{12,28},{16,0},{20,4},{24,8},{28,12},{1,17},{... | collective-permute-start | bytes 417800 | tf_op jit(solution)/shard_map/ppermute | solution.py:274
  48.2 3.7 %collective-permute-start.12 = (bf16[17,32,128]{2,1,0:T(8,128)(2,1)S(1)}, bf16[17,32,128]{2,1,0:T(8,128)(2,1)S(1)}, u32[]{:S(2)}, u32[]{:S(2)}) collective-permute-start(bf16[17,32,128]{2,1,0:T(8,128)(2,1)S(1)} %get-tuple-element.49), channel_id=1, source_target_pairs={{0,24},{4,28},{8,16},{12,20},{16,8},{20,12},{24,0},{28,4},{1,25},{... | collective-permute-start | bytes 417800 | tf_op jit(solution)/shard_map/ppermute | solution.py:274
  51.9 1.2 collective-permute-start.13
  53.1 3.3 %local_forward.3.refs_8_ = f32[16,32,128]{2,1,0:T(8,128)S(1)} custom-call(s32[256]{0:T(256)S(1)} %reshape.41.index_ref, bf16[32,8192]{1,0:T(8,128)(2,1)S(1)} %get-tuple-element.51.bar_ref, bf16[64,4,128,128]{3,2,1,0:T(8,128)(2,1)S(1)} %copy-done.2, f32[16,32,128]{2,1,0:T(8,128)S(1)} %get-tuple-element.86.duals_ref, ...), custom_call_target="tpu_custom_call" | custom-call | flops 268435456 | bytes 8388608 | tf_op jit(solution)/shard_map/local_forward/pallas_call | solution.py:249
  56.5 7.8 %collective-permute-done.10.refs_4_ = bf16[17,32,128]{2,1,0:T(8,128)(2,1)S(1)} collective-permute-done((bf16[17,32,128]{2,1,0:T(8,128)(2,1)S(1)}, bf16[17,32,128]{2,1,0:T(8,128)(2,1)S(1)}, u32[]{:S(2)}, u32[]{:S(2)}) %collective-permute-start.10) | collective-permute-done | bytes 139296 | tf_op jit(solution)/shard_map/ppermute | solution.py:274
  64.3 2.8 %collective-permute-done.11.refs_5_ = bf16[17,32,128]{2,1,0:T(8,128)(2,1)S(1)} collective-permute-done((bf16[17,32,128]{2,1,0:T(8,128)(2,1)S(1)}, bf16[17,32,128]{2,1,0:T(8,128)(2,1)S(1)}, u32[]{:S(2)}, u32[]{:S(2)}) %collective-permute-start.11) | collective-permute-done | bytes 139296 | tf_op jit(solution)/shard_map/ppermute | solution.py:274
  67.5 2.6 %collective-permute-start.21 = (bf16[16,32,128]{2,1,0:T(8,128)(2,1)S(1)}, bf16[16,32,128]{2,1,0:T(8,128)(2,1)S(1)}, u32[]{:S(2)}, u32[]{:S(2)}) collective-permute-start(bf16[16,32,128]{2,1,0:T(8,128)(2,1)S(1)} %get-tuple-element.52.panel_ref.refs_0_), channel_id=1, source_target_pairs={{0,24},{4,28},{8,16},{12,20},{16,8},{20,12},{24,0},{28,4},{1,25},{... | collective-permute-start | bytes 393224 | tf_op jit(solution)/shard_map/ppermute | solution.py:274
  70.1 5.4 %collective-permute-start.19 = (bf16[16,32,128]{2,1,0:T(8,128)(2,1)S(1)}, bf16[16,32,128]{2,1,0:T(8,128)(2,1)S(1)}, u32[]{:S(2)}, u32[]{:S(2)}) collective-permute-start(bf16[16,32,128]{2,1,0:T(8,128)(2,1)S(1)} %get-tuple-element.52.panel_ref.refs_0_), channel_id=1, source_target_pairs={{0,16},{4,20},{8,24},{12,28},{16,0},{20,4},{24,8},{28,12},{1,17},{... | collective-permute-start | bytes 393224 | tf_op jit(solution)/shard_map/ppermute | solution.py:274
  75.6 1.4 collective-permute-start.16
  77.6 5.5 %collective-permute-done.19.refs_4_ = bf16[16,32,128]{2,1,0:T(8,128)(2,1)S(1)} collective-permute-done((bf16[16,32,128]{2,1,0:T(8,128)(2,1)S(1)}, bf16[16,32,128]{2,1,0:T(8,128)(2,1)S(1)}, u32[]{:S(2)}, u32[]{:S(2)}) %collective-permute-start.19) | collective-permute-done | bytes 131104 | tf_op jit(solution)/shard_map/ppermute | solution.py:274
  83.1 1.3 collective-permute-start.20
  84.4 0.8 collective-permute-start.18
  85.1 4.3 %local_adjoint.4.refs_9_ = f32[32,8192]{1,0:T(8,128)S(1)} custom-call(s32[256]{0:T(256)S(1)} %reshape.41.index_ref, bf16[16,32,128]{2,1,0:T(8,128)(2,1)S(1)} %get-tuple-element.52.panel_ref.refs_0_, bf16[64,4,128,128]{3,2,1,0:T(8,128)(2,1)S(1)} %copy-done.2), custom_call_target="tpu_custom_call" | custom-call | flops 268435456 | bytes 8388608 | tf_op jit(solution)/shard_map/local_adjoint/pallas_call | solution.py:164
  89.5 3.5 %head_step.4 = (f32[32,8192]{1,0:T(8,128)S(1)}, bf16[32,8192]{1,0:T(8,128)(2,1)S(1)}, bf16[17,32,128]{2,1,0:T(8,128)(2,1)S(1)}, bf16[17,32,128]{2,1,0:T(8,128)(2...) custom-call(s32[64]{0:T(128)S(1)} %fusion.index_ref, ...), custom_call_target="tpu_custom_call" | custom-call | flops 134217728 | bytes 7864320 | tf_op jit(solution)/shard_map/head_step/pallas_call | solution.py:193
  93.0 1.3 collective-permute-start.23
  94.3 2.0 %collective-permute-start.24 = (bf16[17,32,128]{2,1,0:T(8,128)(2,1)S(1)}, bf16[17,32,128]{2,1,0:T(8,128)(2,1)S(1)}, u32[]{:S(2)}, u32[]{:S(2)}) collective-permute-start(bf16[17,32,128]{2,1,0:T(8,128)(2,1)S(1)} %get-tuple-element.57), channel_id=1, source_target_pairs={{0,8},{4,12},{8,0},{12,4},{16,24},{20,28},{24,16},{28,20},{1,9},{5... | collective-permute-start | bytes 417800 | tf_op jit(solution)/shard_map/ppermute | solution.py:274
  97.0 1.4 collective-permute-done.30
  99.5 2.9 %collective-permute-start.31 = (f32[1]{0:T(128)}, f32[1]{0:T(128)}, u32[]{:S(2)}, u32[]{:S(2)}) collective-permute-start(f32[1]{0:T(128)} %add.66), channel_id=1, source_target_pairs={{0,2},{1,3},{2,0},{3,1},{4,6},{5,7},{6,4},{7,5},{8,10},{9,11},{10,... | collective-permute-start | bytes 20 | tf_op jit(solution)/shard_map/ppermute | solution.py:274
  102.4 0.8 collective-permute-done.31
  104.1 2.1 %collective-permute-start.26 = (bf16[17,32,128]{2,1,0:T(8,128)(2,1)S(1)}, bf16[17,32,128]{2,1,0:T(8,128)(2,1)S(1)}, u32[]{:S(2)}, u32[]{:S(2)}) collective-permute-start(bf16[17,32,128]{2,1,0:T(8,128)(2,1)S(1)} %get-tuple-element.59), channel_id=1, source_target_pairs={{0,16},{4,20},{8,24},{12,28},{16,0},{20,4},{24,8},{28,12},{1,17},{... | collective-permute-start | bytes 417800 | tf_op jit(solution)/shard_map/ppermute | solution.py:274
  106.2 1.6 collective-permute-start.27
  107.7 3.4 %collective-permute-start.28 = (bf16[17,32,128]{2,1,0:T(8,128)(2,1)S(1)}, bf16[17,32,128]{2,1,0:T(8,128)(2,1)S(1)}, u32[]{:S(2)}, u32[]{:S(2)}) collective-permute-start(bf16[17,32,128]{2,1,0:T(8,128)(2,1)S(1)} %get-tuple-element.61), channel_id=1, source_target_pairs={{0,24},{4,28},{8,16},{12,20},{16,8},{20,12},{24,0},{28,4},{1,25},{... | collective-permute-start | bytes 417800 | tf_op jit(solution)/shard_map/ppermute | solution.py:274
  111.8 3.3 %local_forward.4.refs_8_ = f32[16,32,128]{2,1,0:T(8,128)S(1)} custom-call(s32[256]{0:T(256)S(1)} %reshape.41.index_ref, bf16[32,8192]{1,0:T(8,128)(2,1)S(1)} %get-tuple-element.63.bar_ref, bf16[64,4,128,128]{3,2,1,0:T(8,128)(2,1)S(1)} %copy-done.2, f32[16,32,128]{2,1,0:T(8,128)S(1)} %get-tuple-element.64.duals_ref, ...), custom_call_target="tpu_custom_call" | custom-call | flops 268435456 | bytes 8388608 | tf_op jit(solution)/shard_map/local_forward/pallas_call | solution.py:249
  115.2 7.7 %collective-permute-done.26.refs_4_ = bf16[17,32,128]{2,1,0:T(8,128)(2,1)S(1)} collective-permute-done((bf16[17,32,128]{2,1,0:T(8,128)(2,1)S(1)}, bf16[17,32,128]{2,1,0:T(8,128)(2,1)S(1)}, u32[]{:S(2)}, u32[]{:S(2)}) %collective-permute-start.26) | collective-permute-done | bytes 139296 | tf_op jit(solution)/shard_map/ppermute | solution.py:274
  122.8 4.3 %collective-permute-done.27.refs_5_ = bf16[17,32,128]{2,1,0:T(8,128)(2,1)S(1)} collective-permute-done((bf16[17,32,128]{2,1,0:T(8,128)(2,1)S(1)}, bf16[17,32,128]{2,1,0:T(8,128)(2,1)S(1)}, u32[]{:S(2)}, u32[]{:S(2)}) %collective-permute-start.27) | collective-permute-done | bytes 139296 | tf_op jit(solution)/shard_map/ppermute | solution.py:274
  127.4 2.4 %collective-permute-start.37 = (bf16[16,32,128]{2,1,0:T(8,128)(2,1)S(1)}, bf16[16,32,128]{2,1,0:T(8,128)(2,1)S(1)}, u32[]{:S(2)}, u32[]{:S(2)}) collective-permute-start(bf16[16,32,128]{2,1,0:T(8,128)(2,1)S(1)} %get-tuple-element.65.panel_ref.refs_0_), channel_id=1, source_target_pairs={{0,24},{4,28},{8,16},{12,20},{16,8},{20,12},{24,0},{28,4},{1,25},{... | collective-permute-start | bytes 393224 | tf_op jit(solution)/shard_map/ppermute | solution.py:274
  129.8 6.7 %collective-permute-start.35 = (bf16[16,32,128]{2,1,0:T(8,128)(2,1)S(1)}, bf16[16,32,128]{2,1,0:T(8,128)(2,1)S(1)}, u32[]{:S(2)}, u32[]{:S(2)}) collective-permute-start(bf16[16,32,128]{2,1,0:T(8,128)(2,1)S(1)} %get-tuple-element.65.panel_ref.refs_0_), channel_id=1, source_target_pairs={{0,16},{4,20},{8,24},{12,28},{16,0},{20,4},{24,8},{28,12},{1,17},{... | collective-permute-start | bytes 393224 | tf_op jit(solution)/shard_map/ppermute | solution.py:274
  137.0 2.0 %collective-permute-start.38 = (bf16[16,32,128]{2,1,0:T(8,128)(2,1)S(1)}, bf16[16,32,128]{2,1,0:T(8,128)(2,1)S(1)}, u32[]{:S(2)}, u32[]{:S(2)}) collective-permute-start(bf16[16,32,128]{2,1,0:T(8,128)(2,1)S(1)} %collective-permute-done.37.refs_6_), channel_id=1, source_target_pairs={{0,4},{4,0},{8,12},{12,8},{16,20},{20,16},{24,28},{28,24},{1,5},{5... | collective-permute-start | bytes 393224 | tf_op jit(solution)/shard_map/ppermute | solution.py:274
  139.1 4.2 %collective-permute-done.35.refs_4_ = bf16[16,32,128]{2,1,0:T(8,128)(2,1)S(1)} collective-permute-done((bf16[16,32,128]{2,1,0:T(8,128)(2,1)S(1)}, bf16[16,32,128]{2,1,0:T(8,128)(2,1)S(1)}, u32[]{:S(2)}, u32[]{:S(2)}) %collective-permute-start.35) | collective-permute-done | bytes 131104 | tf_op jit(solution)/shard_map/ppermute | solution.py:274
  143.7 1.5 collective-permute-start.34
  145.3 4.3 %local_adjoint.5.refs_9_ = f32[32,8192]{1,0:T(8,128)S(1)} custom-call(s32[256]{0:T(256)S(1)} %reshape.41.index_ref, bf16[16,32,128]{2,1,0:T(8,128)(2,1)S(1)} %get-tuple-element.65.panel_ref.refs_0_, bf16[64,4,128,128]{3,2,1,0:T(8,128)(2,1)S(1)} %copy-done.2), custom_call_target="tpu_custom_call" | custom-call | flops 268435456 | bytes 8388608 | tf_op jit(solution)/shard_map/local_adjoint/pallas_call | solution.py:164
  149.6 4.1 %head_step.5 = (f32[32,8192]{1,0:T(8,128)}, bf16[32,8192]{1,0:T(8,128)(2,1)S(1)}, bf16[17,32,128]{2,1,0:T(8,128)(2,1)S(1)}, bf16[17,32,128]{2,1,0:T(8,128)(2,1)S...) custom-call(s32[64]{0:T(128)S(1)} %fusion.index_ref, ...), custom_call_target="tpu_custom_call" | custom-call | flops 134217728 | bytes 7864320 | tf_op jit(solution)/shard_map/head_step/pallas_call | solution.py:193
  154.4 1.9 %collective-permute-start.40 = (bf16[17,32,128]{2,1,0:T(8,128)(2,1)S(1)}, bf16[17,32,128]{2,1,0:T(8,128)(2,1)S(1)}, u32[]{:S(2)}, u32[]{:S(2)}) collective-permute-start(bf16[17,32,128]{2,1,0:T(8,128)(2,1)S(1)} %get-tuple-element.71), channel_id=1, source_target_pairs={{0,8},{4,12},{8,0},{12,4},{16,24},{20,28},{24,16},{28,20},{1,9},{5... | collective-permute-start | bytes 417800 | tf_op jit(solution)/shard_map/ppermute | solution.py:274
  156.9 1.4 collective-permute-done.46
  159.5 3.0 %collective-permute-start.47 = (f32[1]{0:T(128)}, f32[1]{0:T(128)}, u32[]{:S(2)}, u32[]{:S(2)}) collective-permute-start(f32[1]{0:T(128)} %add.71), channel_id=1, source_target_pairs={{0,2},{1,3},{2,0},{3,1},{4,6},{5,7},{6,4},{7,5},{8,10},{9,11},{10,... | collective-permute-start | bytes 20 | tf_op jit(solution)/shard_map/ppermute | solution.py:274
  162.5 0.7 collective-permute-done.47
  163.8 1.0 collective-permute-start.41
  164.8 2.0 %collective-permute-start.42 = (bf16[17,32,128]{2,1,0:T(8,128)(2,1)S(1)}, bf16[17,32,128]{2,1,0:T(8,128)(2,1)S(1)}, u32[]{:S(2)}, u32[]{:S(2)}) collective-permute-start(bf16[17,32,128]{2,1,0:T(8,128)(2,1)S(1)} %get-tuple-element.73), channel_id=1, source_target_pairs={{0,16},{4,20},{8,24},{12,28},{16,0},{20,4},{24,8},{28,12},{1,17},{... | collective-permute-start | bytes 417800 | tf_op jit(solution)/shard_map/ppermute | solution.py:274
  166.8 1.0 collective-permute-start.43
  167.8 3.3 %collective-permute-start.44 = (bf16[17,32,128]{2,1,0:T(8,128)(2,1)S(1)}, bf16[17,32,128]{2,1,0:T(8,128)(2,1)S(1)}, u32[]{:S(2)}, u32[]{:S(2)}) collective-permute-start(bf16[17,32,128]{2,1,0:T(8,128)(2,1)S(1)} %get-tuple-element.75), channel_id=1, source_target_pairs={{0,24},{4,28},{8,16},{12,20},{16,8},{20,12},{24,0},{28,4},{1,25},{... | collective-permute-start | bytes 417800 | tf_op jit(solution)/shard_map/ppermute | solution.py:274
  171.1 1.3 collective-permute-start.45
  173.1 3.3 %local_forward.5.refs_8_ = f32[16,32,128]{2,1,0:T(8,128)S(1)} custom-call(s32[256]{0:T(256)S(1)} %reshape.41.index_ref, bf16[32,8192]{1,0:T(8,128)(2,1)S(1)} %get-tuple-element.77.bar_ref, bf16[64,4,128,128]{3,2,1,0:T(8,128)(2,1)S(1)} %copy-done.2, f32[16,32,128]{2,1,0:T(8,128)S(1)} %get-tuple-element.78.duals_ref, ...), custom_call_target="tpu_custom_call" | custom-call | flops 268435456 | bytes 8388608 | tf_op jit(solution)/shard_map/local_forward/pallas_call | solution.py:249
  176.5 6.9 %collective-permute-done.42.refs_4_ = bf16[17,32,128]{2,1,0:T(8,128)(2,1)S(1)} collective-permute-done((bf16[17,32,128]{2,1,0:T(8,128)(2,1)S(1)}, bf16[17,32,128]{2,1,0:T(8,128)(2,1)S(1)}, u32[]{:S(2)}, u32[]{:S(2)}) %collective-permute-start.42) | collective-permute-done | bytes 139296 | tf_op jit(solution)/shard_map/ppermute | solution.py:274
  183.4 3.6 %collective-permute-done.43.refs_5_ = bf16[17,32,128]{2,1,0:T(8,128)(2,1)S(1)} collective-permute-done((bf16[17,32,128]{2,1,0:T(8,128)(2,1)S(1)}, bf16[17,32,128]{2,1,0:T(8,128)(2,1)S(1)}, u32[]{:S(2)}, u32[]{:S(2)}) %collective-permute-start.43) | collective-permute-done | bytes 139296 | tf_op jit(solution)/shard_map/ppermute | solution.py:274
  187.0 0.9 settle.5
  187.9 0.7 copy_bitcast_fusion
  (82 shorter events, 8.8 us)
Async XLA Ops:
  0.6 1.0 copy-start
  0.6 30.4 %copy-start.8 = (f32[32]{0:T(128)S(1)}, f32[32]{0:T(128)}, u32[]{:S(2)}) copy-start(f32[32]{0:T(128)} %param.15) | copy-start | bytes 388
  0.7 21.3 %copy-start.10 = (s32[64]{0:T(128)S(1)}, s32[64]{0:T(128)}, u32[]{:S(2)}) copy-start(s32[64]{0:T(128)} %param.21) | copy-start | bytes 772
  0.7 30.5 %copy-start.6 = (f32[8192]{0:T(1024)S(1)}, f32[8192]{0:T(1024)}, u32[]{:S(2)}) copy-start(f32[8192]{0:T(1024)} %param.17) | copy-start | bytes 98308
  0.7 37.4 %copy-start.7 = (f32[32,2048]{1,0:T(8,128)S(1)}, f32[32,2048]{1,0:T(8,128)}, u32[]{:S(2)}) copy-start(f32[32,2048]{1,0:T(8,128)} %param.13) | copy-start | bytes 786436
  1.6 51.5 %copy-start.9 = (f32[32]{0:T(128)S(1)}, f32[32]{0:T(128)}, u32[]{:S(2)}) copy-start(f32[32]{0:T(128)} %param.14) | copy-start | bytes 388
  1.6 17.9 %collective-permute-start.5 = (bf16[16,32,128]{2,1,0:T(8,128)(2,1)S(1)}, bf16[16,32,128]{2,1,0:T(8,128)(2,1)S(1)}, u32[]{:S(2)}, u32[]{:S(2)}) collective-permute-start(bf16[16,32,128]{2,1,0:T(8,128)(2,1)S(1)} %fusion.1.panel_ref.refs_0_), channel_id=1, source_target_pairs={{0,24},{4,28},{8,16},{12,20},{16,8},{20,12},{24,0},{28,4},{1,25},{... | collective-permute-start | bytes 393224 | tf_op jit(solution)/shard_map/ppermute | solution.py:274
  6.7 13.2 %collective-permute-start.3 = (bf16[16,32,128]{2,1,0:T(8,128)(2,1)S(1)}, bf16[16,32,128]{2,1,0:T(8,128)(2,1)S(1)}, u32[]{:S(2)}, u32[]{:S(2)}) collective-permute-start(bf16[16,32,128]{2,1,0:T(8,128)(2,1)S(1)} %fusion.1.panel_ref.refs_0_), channel_id=1, source_target_pairs={{0,16},{4,20},{8,24},{12,28},{16,0},{20,4},{24,8},{28,12},{1,17},{... | collective-permute-start | bytes 393224 | tf_op jit(solution)/shard_map/ppermute | solution.py:274
  6.7 14.8 %collective-permute-start.1 = (bf16[16,32,128]{2,1,0:T(8,128)(2,1)S(1)}, bf16[16,32,128]{2,1,0:T(8,128)(2,1)S(1)}, u32[]{:S(2)}, u32[]{:S(2)}) collective-permute-start(bf16[16,32,128]{2,1,0:T(8,128)(2,1)S(1)} %fusion.1.panel_ref.refs_0_), channel_id=1, source_target_pairs={{0,8},{4,12},{8,0},{12,4},{16,24},{20,28},{24,16},{28,20},{1,9},{5... | collective-permute-start | bytes 393224 | tf_op jit(solution)/shard_map/ppermute | solution.py:274
  7.4 14.6 %collective-permute-start = (bf16[16,32,128]{2,1,0:T(8,128)(2,1)S(1)}, bf16[16,32,128]{2,1,0:T(8,128)(2,1)S(1)}, u32[]{:S(2)}, u32[]{:S(2)}) collective-permute-start(bf16[16,32,128]{2,1,0:T(8,128)(2,1)S(1)} %fusion.1.panel_ref.refs_0_), channel_id=1, source_target_pairs={{0,4},{4,0},{8,12},{12,8},{16,20},{20,16},{24,28},{28,24},{1,5},{5... | collective-permute-start | bytes 393224 | tf_op jit(solution)/shard_map/ppermute | solution.py:274
  10.3 27.9 %collective-permute-start.14 = (f32[1]{0:T(128)}, f32[1]{0:T(128)}, u32[]{:S(2)}, u32[]{:S(2)}) collective-permute-start(f32[1]{0:T(128)} %bitcast.3), channel_id=1, source_target_pairs={{0,1},{1,0},{2,3},{3,2},{4,5},{5,4},{6,7},{7,6},{8,9},{9,8},{10,11... | collective-permute-start | bytes 20 | tf_op jit(solution)/shard_map/ppermute | solution.py:274
  11.8 3.4 %copy-start.1 = (bf16[64,4,128,128]{3,2,1,0:T(8,128)(2,1)S(1)}, bf16[64,4,128,128]{3,2,1,0:T(8,128)(2,1)}, u32[]{:S(2)}) copy-start(bf16[64,4,128,128]{3,2,1,0:T(8,128)(2,1)} %blocks_ref.11) | copy-start | bytes 25165828
  15.2 16.0 %copy-start.5 = (f32[32,8192]{1,0:T(8,128)S(1)}, f32[32,8192]{1,0:T(8,128)}, u32[]{:S(2)}) copy-start(f32[32,8192]{1,0:T(8,128)} %refs_10_.1) | copy-start | bytes 3145732
  15.2 37.9 %copy-start.2 = (bf16[64,4,128,128]{3,2,1,0:T(8,128)(2,1)S(1)}, bf16[64,4,128,128]{3,2,1,0:T(8,128)(2,1)}, u32[]{:S(2)}) copy-start(bf16[64,4,128,128]{3,2,1,0:T(8,128)(2,1)} %blocks_ref.11) | copy-start | bytes 25165828
  19.5 6.4 %collective-permute-start.6 = (bf16[16,32,128]{2,1,0:T(8,128)(2,1)S(1)}, bf16[16,32,128]{2,1,0:T(8,128)(2,1)S(1)}, u32[]{:S(2)}, u32[]{:S(2)}) collective-permute-start(bf16[16,32,128]{2,1,0:T(8,128)(2,1)S(1)} %collective-permute-done.5.refs_6_), channel_id=1, source_target_pairs={{0,4},{4,0},{8,12},{12,8},{16,20},{20,16},{24,28},{28,24},{1,5},{5... | collective-permute-start | bytes 393224 | tf_op jit(solution)/shard_map/ppermute | solution.py:274
  20.0 8.7 %collective-permute-start.4 = (bf16[16,32,128]{2,1,0:T(8,128)(2,1)S(1)}, bf16[16,32,128]{2,1,0:T(8,128)(2,1)S(1)}, u32[]{:S(2)}, u32[]{:S(2)}) collective-permute-start(bf16[16,32,128]{2,1,0:T(8,128)(2,1)S(1)} %collective-permute-done.3.refs_4_), channel_id=1, source_target_pairs={{0,4},{4,0},{8,12},{12,8},{16,20},{20,16},{24,28},{28,24},{1,5},{5... | collective-permute-start | bytes 393224 | tf_op jit(solution)/shard_map/ppermute | solution.py:274
  21.6 9.5 %collective-permute-start.2 = (bf16[16,32,128]{2,1,0:T(8,128)(2,1)S(1)}, bf16[16,32,128]{2,1,0:T(8,128)(2,1)S(1)}, u32[]{:S(2)}, u32[]{:S(2)}) collective-permute-start(bf16[16,32,128]{2,1,0:T(8,128)(2,1)S(1)} %collective-permute-done.1.refs_2_), channel_id=1, source_target_pairs={{0,4},{4,0},{8,12},{12,8},{16,20},{20,16},{24,28},{28,24},{1,5},{5... | collective-permute-start | bytes 393224 | tf_op jit(solution)/shard_map/ppermute | solution.py:274
  31.2 1.6 copy-start.3
  36.3 11.9 %collective-permute-start.7 = (bf16[17,32,128]{2,1,0:T(8,128)(2,1)S(1)}, bf16[17,32,128]{2,1,0:T(8,128)(2,1)S(1)}, u32[]{:S(2)}, u32[]{:S(2)}) collective-permute-start(bf16[17,32,128]{2,1,0:T(8,128)(2,1)S(1)} %get-tuple-element.44), channel_id=1, source_target_pairs={{0,4},{4,0},{8,12},{12,8},{16,20},{20,16},{24,28},{28,24},{1,5},{5... | collective-permute-start | bytes 417800 | tf_op jit(solution)/shard_map/ppermute | solution.py:274
  36.7 15.2 %collective-permute-start.8 = (bf16[17,32,128]{2,1,0:T(8,128)(2,1)S(1)}, bf16[17,32,128]{2,1,0:T(8,128)(2,1)S(1)}, u32[]{:S(2)}, u32[]{:S(2)}) collective-permute-start(bf16[17,32,128]{2,1,0:T(8,128)(2,1)S(1)} %get-tuple-element.45), channel_id=1, source_target_pairs={{0,8},{4,12},{8,0},{12,4},{16,24},{20,28},{24,16},{28,20},{1,9},{5... | collective-permute-start | bytes 417800 | tf_op jit(solution)/shard_map/ppermute | solution.py:274
  39.4 3.7 %collective-permute-start.15 = (f32[1]{0:T(128)}, f32[1]{0:T(128)}, u32[]{:S(2)}, u32[]{:S(2)}) collective-permute-start(f32[1]{0:T(128)} %add.61), channel_id=1, source_target_pairs={{0,2},{1,3},{2,0},{3,1},{4,6},{5,7},{6,4},{7,5},{8,10},{9,11},{10,... | collective-permute-start | bytes 20 | tf_op jit(solution)/shard_map/ppermute | solution.py:274
  43.7 12.8 %collective-permute-start.9 = (bf16[17,32,128]{2,1,0:T(8,128)(2,1)S(1)}, bf16[17,32,128]{2,1,0:T(8,128)(2,1)S(1)}, u32[]{:S(2)}, u32[]{:S(2)}) collective-permute-start(bf16[17,32,128]{2,1,0:T(8,128)(2,1)S(1)} %get-tuple-element.46), channel_id=1, source_target_pairs={{0,12},{4,8},{8,4},{12,0},{16,28},{20,24},{24,20},{28,16},{1,13},{... | collective-permute-start | bytes 417800 | tf_op jit(solution)/shard_map/ppermute | solution.py:274
  45.4 18.9 %collective-permute-start.10 = (bf16[17,32,128]{2,1,0:T(8,128)(2,1)S(1)}, bf16[17,32,128]{2,1,0:T(8,128)(2,1)S(1)}, u32[]{:S(2)}, u32[]{:S(2)}) collective-permute-start(bf16[17,32,128]{2,1,0:T(8,128)(2,1)S(1)} %get-tuple-element.47), channel_id=1, source_target_pairs={{0,16},{4,20},{8,24},{12,28},{16,0},{20,4},{24,8},{28,12},{1,17},{... | collective-permute-start | bytes 417800 | tf_op jit(solution)/shard_map/ppermute | solution.py:274
  47.6 19.6 %collective-permute-start.11 = (bf16[17,32,128]{2,1,0:T(8,128)(2,1)S(1)}, bf16[17,32,128]{2,1,0:T(8,128)(2,1)S(1)}, u32[]{:S(2)}, u32[]{:S(2)}) collective-permute-start(bf16[17,32,128]{2,1,0:T(8,128)(2,1)S(1)} %get-tuple-element.48), channel_id=1, source_target_pairs={{0,20},{4,16},{8,28},{12,24},{16,4},{20,0},{24,12},{28,8},{1,21},{... | collective-permute-start | bytes 417800 | tf_op jit(solution)/shard_map/ppermute | solution.py:274
  48.2 19.0 %collective-permute-start.12 = (bf16[17,32,128]{2,1,0:T(8,128)(2,1)S(1)}, bf16[17,32,128]{2,1,0:T(8,128)(2,1)S(1)}, u32[]{:S(2)}, u32[]{:S(2)}) collective-permute-start(bf16[17,32,128]{2,1,0:T(8,128)(2,1)S(1)} %get-tuple-element.49), channel_id=1, source_target_pairs={{0,24},{4,28},{8,16},{12,20},{16,8},{20,12},{24,0},{28,4},{1,25},{... | collective-permute-start | bytes 417800 | tf_op jit(solution)/shard_map/ppermute | solution.py:274
  51.9 15.2 %collective-permute-start.13 = (bf16[17,32,128]{2,1,0:T(8,128)(2,1)S(1)}, bf16[17,32,128]{2,1,0:T(8,128)(2,1)S(1)}, u32[]{:S(2)}, u32[]{:S(2)}) collective-permute-start(bf16[17,32,128]{2,1,0:T(8,128)(2,1)S(1)} %get-tuple-element.50), channel_id=1, source_target_pairs={{0,28},{4,24},{8,20},{12,16},{16,12},{20,8},{24,4},{28,0},{1,29},{... | collective-permute-start | bytes 417800 | tf_op jit(solution)/shard_map/ppermute | solution.py:274
  53.1 36.4 %copy-start.4 = (bf16[64,128,128]{2,1,0:T(8,128)(2,1)S(1)}, bf16[64,128,128]{2,1,0:T(8,128)(2,1)}, u32[]{:S(2)}) copy-start(bf16[64,128,128]{2,1,0:T(8,128)(2,1)} %refs_8_.5) | copy-start | bytes 6291460
  67.5 9.5 %collective-permute-start.21 = (bf16[16,32,128]{2,1,0:T(8,128)(2,1)S(1)}, bf16[16,32,128]{2,1,0:T(8,128)(2,1)S(1)}, u32[]{:S(2)}, u32[]{:S(2)}) collective-permute-start(bf16[16,32,128]{2,1,0:T(8,128)(2,1)S(1)} %get-tuple-element.52.panel_ref.refs_0_), channel_id=1, source_target_pairs={{0,24},{4,28},{8,16},{12,20},{16,8},{20,12},{24,0},{28,4},{1,25},{... | collective-permute-start | bytes 393224 | tf_op jit(solution)/shard_map/ppermute | solution.py:274
  70.1 13.0 %collective-permute-start.19 = (bf16[16,32,128]{2,1,0:T(8,128)(2,1)S(1)}, bf16[16,32,128]{2,1,0:T(8,128)(2,1)S(1)}, u32[]{:S(2)}, u32[]{:S(2)}) collective-permute-start(bf16[16,32,128]{2,1,0:T(8,128)(2,1)S(1)} %get-tuple-element.52.panel_ref.refs_0_), channel_id=1, source_target_pairs={{0,16},{4,20},{8,24},{12,28},{16,0},{20,4},{24,8},{28,12},{1,17},{... | collective-permute-start | bytes 393224 | tf_op jit(solution)/shard_map/ppermute | solution.py:274
  75.5 8.9 %collective-permute-start.17 = (bf16[16,32,128]{2,1,0:T(8,128)(2,1)S(1)}, bf16[16,32,128]{2,1,0:T(8,128)(2,1)S(1)}, u32[]{:S(2)}, u32[]{:S(2)}) collective-permute-start(bf16[16,32,128]{2,1,0:T(8,128)(2,1)S(1)} %get-tuple-element.52.panel_ref.refs_0_), channel_id=1, source_target_pairs={{0,8},{4,12},{8,0},{12,4},{16,24},{20,28},{24,16},{28,20},{1,9},{5... | collective-permute-start | bytes 393224 | tf_op jit(solution)/shard_map/ppermute | solution.py:274
  75.6 13.8 %collective-permute-start.16 = (bf16[16,32,128]{2,1,0:T(8,128)(2,1)S(1)}, bf16[16,32,128]{2,1,0:T(8,128)(2,1)S(1)}, u32[]{:S(2)}, u32[]{:S(2)}) collective-permute-start(bf16[16,32,128]{2,1,0:T(8,128)(2,1)S(1)} %get-tuple-element.52.panel_ref.refs_0_), channel_id=1, source_target_pairs={{0,4},{4,0},{8,12},{12,8},{16,20},{20,16},{24,28},{28,24},{1,5},{5... | collective-permute-start | bytes 393224 | tf_op jit(solution)/shard_map/ppermute | solution.py:274
  77.0 12.4 %collective-permute-start.22 = (bf16[16,32,128]{2,1,0:T(8,128)(2,1)S(1)}, bf16[16,32,128]{2,1,0:T(8,128)(2,1)S(1)}, u32[]{:S(2)}, u32[]{:S(2)}) collective-permute-start(bf16[16,32,128]{2,1,0:T(8,128)(2,1)S(1)} %collective-permute-done.21.refs_6_), channel_id=1, source_target_pairs={{0,4},{4,0},{8,12},{12,8},{16,20},{20,16},{24,28},{28,24},{1,5},{5... | collective-permute-start | bytes 393224 | tf_op jit(solution)/shard_map/ppermute | solution.py:274
  83.1 6.3 %collective-permute-start.20 = (bf16[16,32,128]{2,1,0:T(8,128)(2,1)S(1)}, bf16[16,32,128]{2,1,0:T(8,128)(2,1)S(1)}, u32[]{:S(2)}, u32[]{:S(2)}) collective-permute-start(bf16[16,32,128]{2,1,0:T(8,128)(2,1)S(1)} %collective-permute-done.19.refs_4_), channel_id=1, source_target_pairs={{0,4},{4,0},{8,12},{12,8},{16,20},{20,16},{24,28},{28,24},{1,5},{5... | collective-permute-start | bytes 393224 | tf_op jit(solution)/shard_map/ppermute | solution.py:274
  84.4 5.1 %collective-permute-start.18 = (bf16[16,32,128]{2,1,0:T(8,128)(2,1)S(1)}, bf16[16,32,128]{2,1,0:T(8,128)(2,1)S(1)}, u32[]{:S(2)}, u32[]{:S(2)}) collective-permute-start(bf16[16,32,128]{2,1,0:T(8,128)(2,1)S(1)} %collective-permute-done.17.refs_2_), channel_id=1, source_target_pairs={{0,4},{4,0},{8,12},{12,8},{16,20},{20,16},{24,28},{28,24},{1,5},{5... | collective-permute-start | bytes 393224 | tf_op jit(solution)/shard_map/ppermute | solution.py:274
  93.0 14.7 %collective-permute-start.23 = (bf16[17,32,128]{2,1,0:T(8,128)(2,1)S(1)}, bf16[17,32,128]{2,1,0:T(8,128)(2,1)S(1)}, u32[]{:S(2)}, u32[]{:S(2)}) collective-permute-start(bf16[17,32,128]{2,1,0:T(8,128)(2,1)S(1)} %get-tuple-element.56), channel_id=1, source_target_pairs={{0,4},{4,0},{8,12},{12,8},{16,20},{20,16},{24,28},{28,24},{1,5},{5... | collective-permute-start | bytes 417800 | tf_op jit(solution)/shard_map/ppermute | solution.py:274
  94.3 16.9 %collective-permute-start.24 = (bf16[17,32,128]{2,1,0:T(8,128)(2,1)S(1)}, bf16[17,32,128]{2,1,0:T(8,128)(2,1)S(1)}, u32[]{:S(2)}, u32[]{:S(2)}) collective-permute-start(bf16[17,32,128]{2,1,0:T(8,128)(2,1)S(1)} %get-tuple-element.57), channel_id=1, source_target_pairs={{0,8},{4,12},{8,0},{12,4},{16,24},{20,28},{24,16},{28,20},{1,9},{5... | collective-permute-start | bytes 417800 | tf_op jit(solution)/shard_map/ppermute | solution.py:274
  97.0 1.4 collective-permute-start.30
  99.5 3.7 %collective-permute-start.31 = (f32[1]{0:T(128)}, f32[1]{0:T(128)}, u32[]{:S(2)}, u32[]{:S(2)}) collective-permute-start(f32[1]{0:T(128)} %add.66), channel_id=1, source_target_pairs={{0,2},{1,3},{2,0},{3,1},{4,6},{5,7},{6,4},{7,5},{8,10},{9,11},{10,... | collective-permute-start | bytes 20 | tf_op jit(solution)/shard_map/ppermute | solution.py:274
  103.8 11.3 %collective-permute-start.25 = (bf16[17,32,128]{2,1,0:T(8,128)(2,1)S(1)}, bf16[17,32,128]{2,1,0:T(8,128)(2,1)S(1)}, u32[]{:S(2)}, u32[]{:S(2)}) collective-permute-start(bf16[17,32,128]{2,1,0:T(8,128)(2,1)S(1)} %get-tuple-element.58), channel_id=1, source_target_pairs={{0,12},{4,8},{8,4},{12,0},{16,28},{20,24},{24,20},{28,16},{1,13},{... | collective-permute-start | bytes 417800 | tf_op jit(solution)/shard_map/ppermute | solution.py:274
  104.1 18.8 %collective-permute-start.26 = (bf16[17,32,128]{2,1,0:T(8,128)(2,1)S(1)}, bf16[17,32,128]{2,1,0:T(8,128)(2,1)S(1)}, u32[]{:S(2)}, u32[]{:S(2)}) collective-permute-start(bf16[17,32,128]{2,1,0:T(8,128)(2,1)S(1)} %get-tuple-element.59), channel_id=1, source_target_pairs={{0,16},{4,20},{8,24},{12,28},{16,0},{20,4},{24,8},{28,12},{1,17},{... | collective-permute-start | bytes 417800 | tf_op jit(solution)/shard_map/ppermute | solution.py:274
  106.2 21.0 %collective-permute-start.27 = (bf16[17,32,128]{2,1,0:T(8,128)(2,1)S(1)}, bf16[17,32,128]{2,1,0:T(8,128)(2,1)S(1)}, u32[]{:S(2)}, u32[]{:S(2)}) collective-permute-start(bf16[17,32,128]{2,1,0:T(8,128)(2,1)S(1)} %get-tuple-element.60), channel_id=1, source_target_pairs={{0,20},{4,16},{8,28},{12,24},{16,4},{20,0},{24,12},{28,8},{1,21},{... | collective-permute-start | bytes 417800 | tf_op jit(solution)/shard_map/ppermute | solution.py:274
  107.7 19.4 %collective-permute-start.28 = (bf16[17,32,128]{2,1,0:T(8,128)(2,1)S(1)}, bf16[17,32,128]{2,1,0:T(8,128)(2,1)S(1)}, u32[]{:S(2)}, u32[]{:S(2)}) collective-permute-start(bf16[17,32,128]{2,1,0:T(8,128)(2,1)S(1)} %get-tuple-element.61), channel_id=1, source_target_pairs={{0,24},{4,28},{8,16},{12,20},{16,8},{20,12},{24,0},{28,4},{1,25},{... | collective-permute-start | bytes 417800 | tf_op jit(solution)/shard_map/ppermute | solution.py:274
  111.2 16.0 %collective-permute-start.29 = (bf16[17,32,128]{2,1,0:T(8,128)(2,1)S(1)}, bf16[17,32,128]{2,1,0:T(8,128)(2,1)S(1)}, u32[]{:S(2)}, u32[]{:S(2)}) collective-permute-start(bf16[17,32,128]{2,1,0:T(8,128)(2,1)S(1)} %get-tuple-element.62), channel_id=1, source_target_pairs={{0,28},{4,24},{8,20},{12,16},{16,12},{20,8},{24,4},{28,0},{1,29},{... | collective-permute-start | bytes 417800 | tf_op jit(solution)/shard_map/ppermute | solution.py:274
  127.4 9.6 %collective-permute-start.37 = (bf16[16,32,128]{2,1,0:T(8,128)(2,1)S(1)}, bf16[16,32,128]{2,1,0:T(8,128)(2,1)S(1)}, u32[]{:S(2)}, u32[]{:S(2)}) collective-permute-start(bf16[16,32,128]{2,1,0:T(8,128)(2,1)S(1)} %get-tuple-element.65.panel_ref.refs_0_), channel_id=1, source_target_pairs={{0,24},{4,28},{8,16},{12,20},{16,8},{20,12},{24,0},{28,4},{1,25},{... | collective-permute-start | bytes 393224 | tf_op jit(solution)/shard_map/ppermute | solution.py:274
  129.8 13.4 %collective-permute-start.35 = (bf16[16,32,128]{2,1,0:T(8,128)(2,1)S(1)}, bf16[16,32,128]{2,1,0:T(8,128)(2,1)S(1)}, u32[]{:S(2)}, u32[]{:S(2)}) collective-permute-start(bf16[16,32,128]{2,1,0:T(8,128)(2,1)S(1)} %get-tuple-element.65.panel_ref.refs_0_), channel_id=1, source_target_pairs={{0,16},{4,20},{8,24},{12,28},{16,0},{20,4},{24,8},{28,12},{1,17},{... | collective-permute-start | bytes 393224 | tf_op jit(solution)/shard_map/ppermute | solution.py:274
  136.6 7.2 %collective-permute-start.33 = (bf16[16,32,128]{2,1,0:T(8,128)(2,1)S(1)}, bf16[16,32,128]{2,1,0:T(8,128)(2,1)S(1)}, u32[]{:S(2)}, u32[]{:S(2)}) collective-permute-start(bf16[16,32,128]{2,1,0:T(8,128)(2,1)S(1)} %get-tuple-element.65.panel_ref.refs_0_), channel_id=1, source_target_pairs={{0,8},{4,12},{8,0},{12,4},{16,24},{20,28},{24,16},{28,20},{1,9},{5... | collective-permute-start | bytes 393224 | tf_op jit(solution)/shard_map/ppermute | solution.py:274
  137.0 12.5 %collective-permute-start.32 = (bf16[16,32,128]{2,1,0:T(8,128)(2,1)S(1)}, bf16[16,32,128]{2,1,0:T(8,128)(2,1)S(1)}, u32[]{:S(2)}, u32[]{:S(2)}) collective-permute-start(bf16[16,32,128]{2,1,0:T(8,128)(2,1)S(1)} %get-tuple-element.65.panel_ref.refs_0_), channel_id=1, source_target_pairs={{0,4},{4,0},{8,12},{12,8},{16,20},{20,16},{24,28},{28,24},{1,5},{5... | collective-permute-start | bytes 393224 | tf_op jit(solution)/shard_map/ppermute | solution.py:274
  137.0 12.5 %collective-permute-start.38 = (bf16[16,32,128]{2,1,0:T(8,128)(2,1)S(1)}, bf16[16,32,128]{2,1,0:T(8,128)(2,1)S(1)}, u32[]{:S(2)}, u32[]{:S(2)}) collective-permute-start(bf16[16,32,128]{2,1,0:T(8,128)(2,1)S(1)} %collective-permute-done.37.refs_6_), channel_id=1, source_target_pairs={{0,4},{4,0},{8,12},{12,8},{16,20},{20,16},{24,28},{28,24},{1,5},{5... | collective-permute-start | bytes 393224 | tf_op jit(solution)/shard_map/ppermute | solution.py:274
  143.2 6.3 %collective-permute-start.36 = (bf16[16,32,128]{2,1,0:T(8,128)(2,1)S(1)}, bf16[16,32,128]{2,1,0:T(8,128)(2,1)S(1)}, u32[]{:S(2)}, u32[]{:S(2)}) collective-permute-start(bf16[16,32,128]{2,1,0:T(8,128)(2,1)S(1)} %collective-permute-done.35.refs_4_), channel_id=1, source_target_pairs={{0,4},{4,0},{8,12},{12,8},{16,20},{20,16},{24,28},{28,24},{1,5},{5... | collective-permute-start | bytes 393224 | tf_op jit(solution)/shard_map/ppermute | solution.py:274
  143.7 5.9 %collective-permute-start.34 = (bf16[16,32,128]{2,1,0:T(8,128)(2,1)S(1)}, bf16[16,32,128]{2,1,0:T(8,128)(2,1)S(1)}, u32[]{:S(2)}, u32[]{:S(2)}) collective-permute-start(bf16[16,32,128]{2,1,0:T(8,128)(2,1)S(1)} %collective-permute-done.33.refs_2_), channel_id=1, source_target_pairs={{0,4},{4,0},{8,12},{12,8},{16,20},{20,16},{24,28},{28,24},{1,5},{5... | collective-permute-start | bytes 393224 | tf_op jit(solution)/shard_map/ppermute | solution.py:274
  153.7 14.0 %collective-permute-start.39 = (bf16[17,32,128]{2,1,0:T(8,128)(2,1)S(1)}, bf16[17,32,128]{2,1,0:T(8,128)(2,1)S(1)}, u32[]{:S(2)}, u32[]{:S(2)}) collective-permute-start(bf16[17,32,128]{2,1,0:T(8,128)(2,1)S(1)} %get-tuple-element.70), channel_id=1, source_target_pairs={{0,4},{4,0},{8,12},{12,8},{16,20},{20,16},{24,28},{28,24},{1,5},{5... | collective-permute-start | bytes 417800 | tf_op jit(solution)/shard_map/ppermute | solution.py:274
  154.4 16.7 %collective-permute-start.40 = (bf16[17,32,128]{2,1,0:T(8,128)(2,1)S(1)}, bf16[17,32,128]{2,1,0:T(8,128)(2,1)S(1)}, u32[]{:S(2)}, u32[]{:S(2)}) collective-permute-start(bf16[17,32,128]{2,1,0:T(8,128)(2,1)S(1)} %get-tuple-element.71), channel_id=1, source_target_pairs={{0,8},{4,12},{8,0},{12,4},{16,24},{20,28},{24,16},{28,20},{1,9},{5... | collective-permute-start | bytes 417800 | tf_op jit(solution)/shard_map/ppermute | solution.py:274
  156.9 1.4 collective-permute-start.46
  159.5 3.7 %collective-permute-start.47 = (f32[1]{0:T(128)}, f32[1]{0:T(128)}, u32[]{:S(2)}, u32[]{:S(2)}) collective-permute-start(f32[1]{0:T(128)} %add.71), channel_id=1, source_target_pairs={{0,2},{1,3},{2,0},{3,1},{4,6},{5,7},{6,4},{7,5},{8,10},{9,11},{10,... | collective-permute-start | bytes 20 | tf_op jit(solution)/shard_map/ppermute | solution.py:274
  163.8 12.7 %collective-permute-start.41 = (bf16[17,32,128]{2,1,0:T(8,128)(2,1)S(1)}, bf16[17,32,128]{2,1,0:T(8,128)(2,1)S(1)}, u32[]{:S(2)}, u32[]{:S(2)}) collective-permute-start(bf16[17,32,128]{2,1,0:T(8,128)(2,1)S(1)} %get-tuple-element.72), channel_id=1, source_target_pairs={{0,12},{4,8},{8,4},{12,0},{16,28},{20,24},{24,20},{28,16},{1,13},{... | collective-permute-start | bytes 417800 | tf_op jit(solution)/shard_map/ppermute | solution.py:274
  164.8 18.7 %collective-permute-start.42 = (bf16[17,32,128]{2,1,0:T(8,128)(2,1)S(1)}, bf16[17,32,128]{2,1,0:T(8,128)(2,1)S(1)}, u32[]{:S(2)}, u32[]{:S(2)}) collective-permute-start(bf16[17,32,128]{2,1,0:T(8,128)(2,1)S(1)} %get-tuple-element.73), channel_id=1, source_target_pairs={{0,16},{4,20},{8,24},{12,28},{16,0},{20,4},{24,8},{28,12},{1,17},{... | collective-permute-start | bytes 417800 | tf_op jit(solution)/shard_map/ppermute | solution.py:274
  166.8 20.3 %collective-permute-start.43 = (bf16[17,32,128]{2,1,0:T(8,128)(2,1)S(1)}, bf16[17,32,128]{2,1,0:T(8,128)(2,1)S(1)}, u32[]{:S(2)}, u32[]{:S(2)}) collective-permute-start(bf16[17,32,128]{2,1,0:T(8,128)(2,1)S(1)} %get-tuple-element.74), channel_id=1, source_target_pairs={{0,20},{4,16},{8,28},{12,24},{16,4},{20,0},{24,12},{28,8},{1,21},{... | collective-permute-start | bytes 417800 | tf_op jit(solution)/shard_map/ppermute | solution.py:274
  167.8 19.3 %collective-permute-start.44 = (bf16[17,32,128]{2,1,0:T(8,128)(2,1)S(1)}, bf16[17,32,128]{2,1,0:T(8,128)(2,1)S(1)}, u32[]{:S(2)}, u32[]{:S(2)}) collective-permute-start(bf16[17,32,128]{2,1,0:T(8,128)(2,1)S(1)} %get-tuple-element.75), channel_id=1, source_target_pairs={{0,24},{4,28},{8,16},{12,20},{16,8},{20,12},{24,0},{28,4},{1,25},{... | collective-permute-start | bytes 417800 | tf_op jit(solution)/shard_map/ppermute | solution.py:274
  171.1 15.9 %collective-permute-start.45 = (bf16[17,32,128]{2,1,0:T(8,128)(2,1)S(1)}, bf16[17,32,128]{2,1,0:T(8,128)(2,1)S(1)}, u32[]{:S(2)}, u32[]{:S(2)}) collective-permute-start(bf16[17,32,128]{2,1,0:T(8,128)(2,1)S(1)} %get-tuple-element.76), channel_id=1, source_target_pairs={{0,28},{4,24},{8,20},{12,16},{16,12},{20,8},{24,4},{28,0},{1,29},{... | collective-permute-start | bytes 417800 | tf_op jit(solution)/shard_map/ppermute | solution.py:274

commit v2 on v1

v2 whole, which is shorter than its diff:
```python
import functools

import jax
import jax.numpy as jnp
from jax import lax
from jax.experimental import pallas as pl
from jax.experimental.pallas import tpu as pltpu
from jax.sharding import PartitionSpec as P

ROUNDS = 3

primal_step = 0.5
dual_step = 0.5
risk_step = 1.0
tail_weight = 2.0

MIB = 1024 * 1024
GROUP = 8
HEAD_GROUP = 16


def contract_last(left, right):
    return lax.dot_general(
        left, right, (((1,), (1,)), ((), ())), preferred_element_type=jnp.float32
    )


def local_adjoint_kernel(
    touches, group, index_ref, panel_ref, blocks_ref, sum_ref, *refs
):
    out_ref, sum_out = refs[-2:]
    rows = blocks_ref.shape[-1]
    first = pl.program_id(0) * group
    sum_out[...] = sum_ref[...]
    for member in range(group):
        left = jnp.concatenate(
            [panel_ref[index_ref[(first + member) * touches + k]] for k in range(touches)], axis=1
        )
        right = jnp.concatenate([blocks_ref[member, k] for k in range(touches)], axis=1)
        out_ref[:, member * rows : (member + 1) * rows] = contract_last(left, right)


def to_parts(column, shape):
    high = column.astype(jnp.bfloat16).astype(jnp.float32)
    rest = column - high
    middle = rest.astype(jnp.bfloat16).astype(jnp.float32)
    low = rest - middle
    lane = lax.broadcasted_iota(jnp.int32, shape, 1)
    packed = jnp.where(
        lane == 0, high, jnp.where(lane == 1, middle, jnp.where(lane == 2, low, 0.0))
    )
    return packed.astype(jnp.bfloat16)


def from_parts(parts):
    return jnp.sum(parts.astype(jnp.float32), axis=1, keepdims=True)


def head_kernel(group, steps, peers, index_ref, *refs):
    panels, refs = refs[:peers], refs[peers:]
    heads_ref, pulled_ref, flows_ref, costs_ref, risk_ref, sum_ref, other_ref = refs[:7]
    flows_out, bar_out, loss_out, sum_out, refs = *refs[7:11], refs[11:]
    kept, refs = refs[: peers // 2], refs[peers // 2 :]
    sends, (panel, terms, pulled, loss) = refs[:-4], refs[-4:]
    rows = heads_ref.shape[-1]
    node_blks = panels[0].shape[0]
    step = pl.program_id(0)
    first = step * group

    @pl.when(step == 0)
    def _():
        terms[...] = jnp.zeros_like(terms)
        loss[...] = jnp.zeros_like(loss)
        sum_out[...] = sum_ref[...] + other_ref[...]
        for peer in range(peers):
            panel[peer * node_blks : (peer + 1) * node_blks] = panels[peer][...]

    places = [index_ref[first + member] for member in range(group)]
    spans = [slice(member * rows, (member + 1) * rows) for member in range(group)]
    for member in range(group):
        pulled[:, spans[member]] = contract_last(panel[places[member]], heads_ref[member])
    risk = risk_ref[...]
    loss_sum = jnp.zeros_like(risk)
    for columns in spans:
        flows = flows_ref[:, columns]
        cost = costs_ref[:, columns]
        gradient = risk * cost - (pulled[:, columns] + pulled_ref[:, columns])
        flows_new = jnp.maximum(flows - primal_step * gradient, 0.0)
        bar = 2.0 * flows_new - flows
        flows_out[:, columns] = flows_new
        loss_sum += cost * bar
        bar_out[:, columns] = bar.astype(jnp.bfloat16)
    loss[...] += loss_sum
    products = [
        jnp.dot(bar_out[:, spans[m]], heads_ref[m], preferred_element_type=jnp.float32)
        for m in range(group)
    ]
    for member in range(group):
        terms[places[member]] += products[member]

    @pl.when(step == steps - 1)
    def _():
        loss_parts = to_parts(jnp.sum(loss[...], axis=1, keepdims=True), loss.shape)
        loss_out[...] = loss_parts
        for half in range(peers // 2):
            begin = 2 * half * node_blks
            kept[half][...] = terms[begin : begin + node_blks]
        for send, distances in zip(sends, near_pieces(peers)):
            for place, distance in enumerate(distances):
                send[place * node_blks : (place + 1) * node_blks] = terms[
                    distance * node_blks : (distance + 1) * node_blks
                ].astype(jnp.bfloat16)
        sends[0][2 * node_blks] = loss_parts


def near_pieces(peers):
    return [(k, k - 2) for k in range(peers - 1, 2, -4)]


def pair_sum(values):
    while len(values) > 1:
        values = [a + b for a, b in zip(values[::2], values[1::2])]
    return values[0]


def fold_kernel(count, first, last, *refs):
    kept, (arrived_ref, loss_ref, extra_ref), refs = refs[:count], refs[count : count + 3], refs[count + 3 :]
    outs, refs = refs[:count], refs[count:]
    node_blks = kept[0].shape[0]
    for place in range(count):
        for block in range(node_blks):
            term = arrived_ref[place * node_blks + block].astype(jnp.float32)
            outs[place][block] = (kept[place][block] + term).astype(jnp.bfloat16)
    parts = loss_ref[...]
    if first:
        both = from_parts(parts) + from_parts(arrived_ref[2 * node_blks])
        parts = to_parts(both, loss_ref.shape)
        refs[0][...] = parts
    for out in outs:
        out[node_blks] = parts
    if not last:
        refs[-1][...] = extra_ref[...]


def settle_kernel(peers, arc_total, scen_total, last, *refs):
    kept_ref, near_ref, refs = refs[0], refs[1], refs[2:]
    arrived, refs = refs[: peers // 2 - 1], refs[peers // 2 - 1 :]
    pair_ref, base_ref, risk_ref, excess_ref, level_ref, sum_ref, other_ref = refs[:7]
    duals_out, half_out, risk_out, excess_out, level_out, sum_out = refs[7:]
    node_blks, _, rows = base_ref.shape
    for block in range(node_blks):
        parts = [near_ref[node_blks + block]] + [ref[block] for ref in arrived]
        total = kept_ref[block] + pair_sum([part.astype(jnp.float32) for part in parts])
        duals = base_ref[block] - dual_step * total
        if last:
            duals_out[:, block * rows : (block + 1) * rows] = duals
        else:
            duals_out[block] = duals
        half_out[block] = duals.astype(jnp.bfloat16)
    losses = [from_parts(pair_ref[...])] + [from_parts(ref[node_blks]) for ref in arrived]
    losses = pair_sum(losses) / arc_total
    mean_risk = (sum_ref[...] + other_ref[...]) / scen_total
    level = level_ref[...]
    level_new = level - primal_step * (1.0 - mean_risk)
    level_bar = 2.0 * level_new - level
    level_out[...] = level_new
    risk = risk_ref[...]
    excess = excess_ref[...]
    excess_new = jnp.maximum(excess - primal_step * (tail_weight - risk), 0.0)
    excess_bar = 2.0 * excess_new - excess
    excess_out[...] = excess_new
    risk_new = jnp.maximum(risk + risk_step * (losses - excess_bar - level_bar[:1]), 0.0)
    risk_out[...] = risk_new
    sum_out[...] = jnp.broadcast_to(jnp.sum(risk_new, axis=0, keepdims=True), sum_out.shape)


def local_forward_kernel(
    touches,
    group,
    steps,
    index_ref,
    bar_ref,
    blocks_ref,
    duals_ref,
    demand_ref,
    sum_ref,
    after_ref,
    out_ref,
    sum_out,
    total,
):
    rows = blocks_ref.shape[-1]
    step = pl.program_id(0)
    first = step * group

    @pl.when(step == 0)
    def _():
        total[...] = jnp.zeros_like(total)
        sum_out[...] = sum_ref[...]

    for member in range(group):
        right = jnp.concatenate([blocks_ref[member, k] for k in range(touches)], axis=1)
        products = jnp.dot(
            bar_ref[:, member * rows : (member + 1) * rows],
            right,
            preferred_element_type=jnp.float32,
        )
        for k in range(touches):
            place = index_ref[(first + member) * touches + k]
            total[place] += products[:, k * rows : (k + 1) * rows]

    @pl.when(step == steps - 1)
    def _():
        out_ref[...] = duals_ref[...] + dual_step * (demand_ref[...] - total[...])


def whole(*shape):
    return pl.BlockSpec(shape, lambda i, *_: (0,) * len(shape))


def vmem_limit(peers):
    return (8 + peers + peers // 4) * MIB


def params(peers=8):
    return pltpu.CompilerParams(
        dimension_semantics=("arbitrary",), vmem_limit_bytes=vmem_limit(peers)
    )


def local_adjoint(index, panel, blocks, risk_sum, after):
    arc_blks, touches, rows, _ = blocks.shape
    scen_rows = panel.shape[1]
    group = GROUP
    return pl.pallas_call(
        functools.partial(local_adjoint_kernel, touches, group),
        out_shape=(
            jax.ShapeDtypeStruct((scen_rows, arc_blks * rows), jnp.float32),
            jax.ShapeDtypeStruct(risk_sum.shape, jnp.float32),
        ),
        grid_spec=pltpu.PrefetchScalarGridSpec(
            num_scalar_prefetch=1,
            grid=(arc_blks // group,),
            in_specs=[
                whole(*panel.shape),
                pl.BlockSpec((group, touches, rows, rows), lambda i, *_: (i, 0, 0, 0)),
                whole(*risk_sum.shape),
            ]
            + [pl.BlockSpec(memory_space=pl.ANY)] * len(after),
            out_specs=[
                pl.BlockSpec((scen_rows, group * rows), lambda i, *_: (0, i)),
                whole(*risk_sum.shape),
            ],
        ),
        compiler_params=params(),
        cost_estimate=pl.CostEstimate(
            flops=2 * scen_rows * blocks.size, bytes_accessed=2 * blocks.size, transcendentals=0
        ),
        name="local_adjoint",
    )(index, panel, blocks, risk_sum, *after)


def head_step(places, panels, heads, pulled, flows, costs, risk, sums):
    arc_blks, rows, _ = heads.shape
    scen_rows = flows.shape[0]
    peers = len(panels)
    node_blks = panels[0].shape[0]
    group = HEAD_GROUP
    steps = arc_blks // group
    kept = (node_blks, scen_rows, rows)
    pieces = near_pieces(peers)
    sent = [(len(piece) * node_blks, scen_rows, rows) for piece in pieces]
    sent[0] = (2 * node_blks + 1, scen_rows, rows)
    arcs = pl.BlockSpec((scen_rows, group * rows), lambda i, *_: (0, i))
    results = pl.pallas_call(
        functools.partial(head_kernel, group, steps, peers),
        out_shape=[
            jax.ShapeDtypeStruct(flows.shape, jnp.float32),
            jax.ShapeDtypeStruct(flows.shape, jnp.bfloat16),
            jax.ShapeDtypeStruct((scen_rows, rows), jnp.bfloat16),
            jax.ShapeDtypeStruct(sums[0].shape, jnp.float32),
        ]
        + [jax.ShapeDtypeStruct(kept, jnp.float32)] * (peers // 2)
        + [jax.ShapeDtypeStruct(shape, jnp.bfloat16) for shape in sent],
        grid_spec=pltpu.PrefetchScalarGridSpec(
            num_scalar_prefetch=1,
            grid=(steps,),
            in_specs=[whole(*panels[0].shape)] * peers
            + [
                pl.BlockSpec((group, rows, rows), lambda i, *_: (i, 0, 0)),
                arcs,
                arcs,
                pl.BlockSpec((1, group * rows), lambda i, *_: (0, i)),
                whole(scen_rows, rows),
                whole(*sums[0].shape),
                whole(*sums[0].shape),
            ],
            out_specs=[arcs, arcs, whole(scen_rows, rows), whole(*sums[0].shape)]
            + [whole(*kept)] * (peers // 2)
            + [whole(*shape) for shape in sent],
            scratch_shapes=[
                pltpu.VMEM((peers * node_blks, scen_rows, rows), jnp.bfloat16),
                pltpu.VMEM((peers * node_blks, scen_rows, rows), jnp.float32),
                pltpu.VMEM((scen_rows, group * rows), jnp.float32),
                pltpu.VMEM((scen_rows, rows), jnp.float32),
            ],
        ),
        compiler_params=params(peers),
        cost_estimate=pl.CostEstimate(
            flops=4 * scen_rows * heads.size,
            bytes_accessed=2 * heads.size + 14 * flows.size + 4 * peers * panels[0].size,
            transcendentals=0,
        ),
        name="head_step",
    )(places, *panels, heads, pulled, flows, costs, risk, *sums)
    half = peers // 2
    return *results[:4], results[4 : 4 + half], results[4 + half :]


def small_cost(*arrays):
    size = sum(a.size for a in arrays)
    return pl.CostEstimate(flops=size, bytes_accessed=2 * size, transcendentals=0)


def fold(kept, arrived, loss, extra, first, last):
    count = len(kept)
    node_blks, scen_rows, rows = kept[0].shape
    out_shape = [jax.ShapeDtypeStruct((node_blks + 1, scen_rows, rows), jnp.bfloat16)] * count
    if first:
        out_shape.append(jax.ShapeDtypeStruct(loss.shape, jnp.bfloat16))
    if not last:
        out_shape.append(jax.ShapeDtypeStruct(extra.shape, jnp.bfloat16))
    vmem = pl.BlockSpec(memory_space=pltpu.VMEM)
    results = pl.pallas_call(
        functools.partial(fold_kernel, count, first, last),
        out_shape=out_shape,
        in_specs=[vmem] * (count + 2) + [pl.BlockSpec(memory_space=pl.ANY) if last else vmem],
        out_specs=[vmem] * len(out_shape),
        compiler_params=pltpu.CompilerParams(vmem_limit_bytes=vmem_limit(8)),
        cost_estimate=small_cost(*kept, arrived),
        name="fold",
    )(*kept, arrived, loss, extra)
    return results[:count], results[count:]


def settle(kept, near, arrived, pair, base, risk, excess, level, sums, arc_total, scen_total, last):
    peers = 2 * (len(arrived) + 1)
    node_blks, scen_rows, rows = base.shape
    duals = (scen_rows, node_blks * rows) if last else base.shape
    return pl.pallas_call(
        functools.partial(settle_kernel, peers, arc_total, scen_total, last),
        out_shape=(
            jax.ShapeDtypeStruct(duals, jnp.float32),
            jax.ShapeDtypeStruct(base.shape, jnp.bfloat16),
            jax.ShapeDtypeStruct(risk.shape, jnp.float32),
            jax.ShapeDtypeStruct(risk.shape, jnp.float32),
            jax.ShapeDtypeStruct(level.shape, jnp.float32),
            jax.ShapeDtypeStruct(level.shape, jnp.float32),
        ),
        compiler_params=pltpu.CompilerParams(vmem_limit_bytes=vmem_limit(peers)),
        cost_estimate=small_cost(kept, near, *arrived, base),
        name="settle",
    )(kept, near, *arrived, pair, base, risk, excess, level, *sums)


def local_forward(index, bar, blocks, duals, demand, risk_sum, after):
    arc_blks, touches, rows, _ = blocks.shape
    scen_rows = bar.shape[0]
    group = GROUP
    steps = arc_blks // group
    return pl.pallas_call(
        functools.partial(local_forward_kernel, touches, group, steps),
        out_shape=(
            jax.ShapeDtypeStruct(duals.shape, jnp.float32),
            jax.ShapeDtypeStruct(risk_sum.shape, jnp.float32),
        ),
        grid_spec=pltpu.PrefetchScalarGridSpec(
            num_scalar_prefetch=1,
            grid=(steps,),
            in_specs=[
                pl.BlockSpec((scen_rows, group * rows), lambda i, *_: (0, i)),
                pl.BlockSpec((group, touches, rows, rows), lambda i, *_: (i, 0, 0, 0)),
                whole(*duals.shape),
                whole(*duals.shape),
                whole(*risk_sum.shape),
                pl.BlockSpec(memory_space=pl.ANY),
            ],
            out_specs=[whole(*duals.shape), whole(*risk_sum.shape)],
            scratch_shapes=[pltpu.VMEM(duals.shape, jnp.float32)],
        ),
        compiler_params=params(),
        cost_estimate=pl.CostEstimate(
            flops=2 * scen_rows * blocks.size, bytes_accessed=2 * blocks.size, transcendentals=0
        ),
        name="local_forward",
    )(index, bar, blocks, duals, demand, risk_sum, after)


def swap(value, axis, distance):
    size = lax.axis_size(axis)
    return lax.ppermute(value, axis, [(i, i ^ distance) for i in range(size)])


def gather_panels(own):
    size = lax.axis_size("net")
    panels = [own] + [None] * (size - 1)
    for distance in range(2, size, 2):
        panels[distance] = swap(own, "net", distance)
    for distance in range(0, size, 2):
        panels[distance + 1] = swap(panels[distance], "net", 1)
    return panels


def per_device(
    arc_flows,
    node_duals,
    demand,
    excess,
    risk_duals,
    threshold,
    arc_costs,
    local_blocks,
    head_blocks,
    local_index,
    head_index,
):
    rows = local_blocks.shape[-1]
    scen_rows = arc_flows.shape[0]
    node_blks = node_duals.shape[1] // rows
    net_size = lax.axis_size("net")
    arc_total = arc_flows.shape[1] * net_size
    scen_total = scen_rows * lax.axis_size("scen")
    local_ids = local_index.reshape(-1)
    costs = arc_costs.reshape(1, -1)
    distance = jnp.bitwise_xor(head_index // node_blks, lax.axis_index("net"))
    places = distance * node_blks + head_index % node_blks
    scen_size = lax.axis_size("scen")
    wide = (scen_rows, rows)
    flat = (8, rows)

    def to_blocks(panel):
        return panel.reshape(scen_rows, node_blks, rows).transpose(1, 0, 2)

    duals = to_blocks(node_duals)
    half = duals.astype(jnp.bfloat16)
    wanted = to_blocks(demand)
    flows = arc_flows
    excess_now = jnp.broadcast_to(excess[:, None], wide)
    risk = jnp.broadcast_to(risk_duals[:, None], wide)
    level = jnp.broadcast_to(threshold[:, None], flat)
    risk_sum = jnp.broadcast_to(jnp.sum(risk_duals), flat)
    for iteration in range(ROUNDS):
        panels = gather_panels(half)
        pulled, risk_sum = local_adjoint(
            local_ids, half, local_blocks, risk_sum, panels[2::2] if iteration else panels[5:6]
        )
        sums = (risk_sum, swap(risk_sum, "scen", 1))
        flows, bar, loss, risk_sum, kept, sends = head_step(
            places, panels, head_blocks, pulled, flows, costs, risk, sums
        )
        halves = len(kept)
        folded = [None] * halves
        pair, piece = loss, sends[0]
        for number in range(len(sends) - 1):
            half = halves - 1 - 2 * number
            (folded[half], folded[half - 1]), rest = fold(
                (kept[half], kept[half - 1]),
                swap(piece, "net", 1),
                pair,
                sends[number + 1],
                number == 0,
                False,
            )
            pair = rest[0] if number == 0 else pair
            piece = rest[-1]
        base, risk_sum = local_forward(
            local_ids, bar, local_blocks, duals, wanted, risk_sum, folded[2]
        )
        near = swap(piece, "net", 1)
        (folded[1],), _ = fold((kept[1],), near, pair, base, False, True)
        far = [swap(folded[half], "net", 2 * half) for half in range(1, halves)]
        stride = 2
        while 2 * stride < scen_size:
            risk_sum = risk_sum + swap(risk_sum, "scen", stride)
            stride *= 2
        sums = (risk_sum, swap(risk_sum, "scen", stride))
        duals, half, risk, excess_now, level, risk_sum = settle(
            kept[0],
            near,
            far,
            pair,
            base,
            risk,
            excess_now,
            level,
            sums,
            arc_total,
            scen_total,
            iteration == ROUNDS - 1,
        )
    return (flows, duals, excess_now[:, 0], risk[:, 0], level[0, :1])


def solution(mesh):
    placed = (
        P("scen", "net"),
        P("scen", "net"),
        P("scen", "net"),
        P("scen"),
        P("scen"),
        P(),
        P("net"),
        P("net", None, None, None),
        P("net", None, None),
        P("net", None),
        P("net"),
    )
    return jax.shard_map(
        per_device,
        mesh=mesh,
        in_specs=placed,
        out_specs=(P("scen", "net"), P("scen", "net"), P("scen"), P("scen"), P()),
        check_vma=False,
    )
```

time: 193 us -> 161 us (0.83); the launches traced: 190 us -> 161 us
  starting transfers between devices: 78.2 us -> 50.1 us
  between operations: 8.02 us -> 1.55 us
  waiting for transfers between devices: 57.2 us -> 62.5 us
    ppermute x48 -> x42, starting transfers between devices: 78.2 us -> 50.1 us  [swap(): return lax.ppermute(value, axis, [(i, i ^ distance) for i in range(size)])]
    ppermute x48 -> x42, waiting for transfers between devices: 57.2 us -> 62.5 us  [swap(): return lax.ppermute(value, axis, [(i, i ^ distance) for i in range(size)])]
  transfers between devices with their start and end apart: 48 -> 42, of which waited for: 16 -> 23; matrix products, arithmetic and copies ran while one was open for 2% -> 2% of each run, Pallas kernels for 14% -> 14%
where the time goes in v2:
time: 161 us
  waiting for transfers between devices  62.5 us (39%)
  starting transfers between devices  50.1 us (31%)
  Pallas kernels  35.5 us (22%)
  local copies, waits for them, and re-layouts  10 us (6%)
    ppermute x42, waiting for transfers between devices, swap(): return lax.ppermute(value, axis, [(i, i ^ distance) for i in range(size)])  62.5 us
    ppermute x42, starting transfers between devices, swap(): return lax.ppermute(value, axis, [(i, i ^ distance) for i in range(size)])  50.1 us
    pallas_call x3, Pallas kernels, local_adjoint(): pl.pallas_call(functools.partial(local_adjoint_kernel, touches, group), o...  12.8 us
    pallas_call x3, Pallas kernels, head_step(): pl.pallas_call(functools.partial(head_kernel, group, steps, peers), out_s...  11.3 us
    pallas_call x3, Pallas kernels, local_forward(): pl.pallas_call(functools.partial(local_forward_kernel, touches, group, st...  9.78 us
    unnamed x23, local copies, waits for them, and re-layouts  7.92 us
  transfers between devices with their start and end apart: 42, of which 23 were waited for; matrix products, arithmetic and copies ran while one was open for 2% of the time, Pallas kernels for 14%

profile of v2, /device:TPU:0, one launch (start us, length us, event | category | flops | bytes accessed | tf_op | source)
XLA Modules:
  0.0 161.0 jit_solution(14653597187535007409)
XLA Ops:
  1.6 4.1 %collective-permute-start.3 = (bf16[16,32,128]{2,1,0:T(8,128)(2,1)S(1)}, bf16[16,32,128]{2,1,0:T(8,128)(2,1)S(1)}, u32[]{:S(2)}, u32[]{:S(2)}) collective-permute-start(bf16[16,32,128]{2,1,0:T(8,128)(2,1)S(1)} %fusion.1.panel_ref.refs_0_), channel_id=1, source_target_pairs={{0,16},{4,20},{8,24},{12,28},{16,0},{20,4},{24,8},{28,12},{1,17},{... | collective-permute-start | bytes 393224 | tf_op jit(solution)/shard_map/ppermute | solution.py:401
  5.7 1.3 collective-permute-start.5
  7.3 8.4 %collective-permute-done.3.refs_4_ = bf16[16,32,128]{2,1,0:T(8,128)(2,1)S(1)} collective-permute-done((bf16[16,32,128]{2,1,0:T(8,128)(2,1)S(1)}, bf16[16,32,128]{2,1,0:T(8,128)(2,1)S(1)}, u32[]{:S(2)}, u32[]{:S(2)}) %collective-permute-start.3) | collective-permute-done | bytes 131104 | tf_op jit(solution)/shard_map/ppermute | solution.py:401
  15.7 1.8 %collective-permute-start.4 = (bf16[16,32,128]{2,1,0:T(8,128)(2,1)S(1)}, bf16[16,32,128]{2,1,0:T(8,128)(2,1)S(1)}, u32[]{:S(2)}, u32[]{:S(2)}) collective-permute-start(bf16[16,32,128]{2,1,0:T(8,128)(2,1)S(1)} %collective-permute-done.3.refs_4_), channel_id=1, source_target_pairs={{0,4},{4,0},{8,12},{12,8},{16,20},{20,16},{24,28},{28,24},{1,5},{5... | collective-permute-start | bytes 393224 | tf_op jit(solution)/shard_map/ppermute | solution.py:401
  18.6 1.3 reduce_sum.9
  19.9 1.8 %collective-permute-start.6 = (bf16[16,32,128]{2,1,0:T(8,128)(2,1)S(1)}, bf16[16,32,128]{2,1,0:T(8,128)(2,1)S(1)}, u32[]{:S(2)}, u32[]{:S(2)}) collective-permute-start(bf16[16,32,128]{2,1,0:T(8,128)(2,1)S(1)} %collective-permute-done.5.refs_6_), channel_id=1, source_target_pairs={{0,4},{4,0},{8,12},{12,8},{16,20},{20,16},{24,28},{28,24},{1,5},{5... | collective-permute-start | bytes 393224 | tf_op jit(solution)/shard_map/ppermute | solution.py:401
  22.6 3.4 %copy-done.1 = bf16[64,4,128,128]{3,2,1,0:T(8,128)(2,1)S(1)} copy-done((bf16[64,4,128,128]{3,2,1,0:T(8,128)(2,1)S(1)}, bf16[64,4,128,128]{3,2,1,0:T(8,128)(2,1)}, u32[]{:S(2)}) %copy-start.1) | copy-done | bytes 8388632
  26.0 4.3 %local_adjoint.3 = (f32[32,8192]{1,0:T(8,128)S(1)}, f32[8,128]{1,0:T(8,128)S(1)}) custom-call(s32[256]{0:T(256)S(1)} %reshape.26.index_ref, bf16[16,32,128]{2,1,0:T(8,128)(2,1)S(1)} %fusion.1.panel_ref.refs_0_, bf16[64,4,128,128]{3,2,1,0:T(8,128)(2,1)S(1)} %copy-done.1, f32[8,128]{1,0:T(8,128)S(1)} %broadcast_in_dim.10.sum_ref, ...), custom_call_target="tpu_custom_call" | custom-call | flops 268435456 | bytes 8388608 | tf_op jit(solution)/shard_map/local_adjoint/pallas_call | solution.py:235
  30.4 1.1 collective-permute-done.7.refs_14_
  31.5 1.6 copy-done.3
  33.1 1.2 copy-done.5
  34.3 3.5 %head_step.3 = (f32[32,8192]{1,0:T(8,128)S(1)}, bf16[32,8192]{1,0:T(8,128)(2,1)S(1)}, bf16[32,128]{1,0:T(8,128)(2,1)S(1)}, f32[8,128]{1,0:T(8,128)S(1)}, f32[16,...) custom-call(s32[64]{0:T(128)S(1)} %fusion.index_ref, ...), custom_call_target="tpu_custom_call" | custom-call | flops 134217728 | bytes 7864320 | tf_op jit(solution)/shard_map/head_step/pallas_call | solution.py:275
  37.9 1.9 %collective-permute-start.8 = (bf16[33,32,128]{2,1,0:T(8,128)(2,1)S(1)}, bf16[33,32,128]{2,1,0:T(8,128)(2,1)S(1)}, u32[]{:S(2)}, u32[]{:S(2)}) collective-permute-start(bf16[33,32,128]{2,1,0:T(8,128)(2,1)S(1)} %get-tuple-element.80), channel_id=1, source_target_pairs={{0,4},{4,0},{8,12},{12,8},{16,20},{20,16},{24,28},{28,24},{1,5},{5... | collective-permute-start | bytes 811016 | tf_op jit(solution)/shard_map/ppermute | solution.py:401
  39.8 6.8 %collective-permute-done.8.refs_2_ = bf16[33,32,128]{2,1,0:T(8,128)(2,1)S(1)} collective-permute-done((bf16[33,32,128]{2,1,0:T(8,128)(2,1)S(1)}, bf16[33,32,128]{2,1,0:T(8,128)(2,1)S(1)}, u32[]{:S(2)}, u32[]{:S(2)}) %collective-permute-start.8) | collective-permute-done | bytes 270368 | tf_op jit(solution)/shard_map/ppermute | solution.py:401
  46.7 1.8 %collective-permute-start.9 = (bf16[32,32,128]{2,1,0:T(8,128)(2,1)S(1)}, bf16[32,32,128]{2,1,0:T(8,128)(2,1)S(1)}, u32[]{:S(2)}, u32[]{:S(2)}) collective-permute-start(bf16[32,32,128]{2,1,0:T(8,128)(2,1)S(1)} %get-tuple-element.83), channel_id=1, source_target_pairs={{0,4},{4,0},{8,12},{12,8},{16,20},{20,16},{24,28},{28,24},{1,5},{5... | collective-permute-start | bytes 786440 | tf_op jit(solution)/shard_map/ppermute | solution.py:401
  48.5 2.7 %collective-permute-start.12 = (bf16[17,32,128]{2,1,0:T(8,128)(2,1)S(1)}, bf16[17,32,128]{2,1,0:T(8,128)(2,1)S(1)}, u32[]{:S(2)}, u32[]{:S(2)}) collective-permute-start(bf16[17,32,128]{2,1,0:T(8,128)(2,1)S(1)} %get-tuple-element.90), channel_id=1, source_target_pairs={{0,24},{4,28},{8,16},{12,20},{16,8},{20,12},{24,0},{28,4},{1,25},{... | collective-permute-start | bytes 417800 | tf_op jit(solution)/shard_map/ppermute | solution.py:401
  51.2 3.3 %local_forward.3 = (f32[16,32,128]{2,1,0:T(8,128)S(1)}, f32[8,128]{1,0:T(8,128)S(1)}) custom-call(s32[256]{0:T(256)S(1)} %reshape.26.index_ref, bf16[32,8192]{1,0:T(8,128)(2,1)S(1)} %get-tuple-element.86.bar_ref, bf16[64,4,128,128]{3,2,1,0:T(8,128)(2,1)S(1)} %copy-done.2, f32[16,32,128]{2,1,0:T(8,128)S(1)} %bitcast_bitcast_fusion.1.duals_ref, ...), custom_call_target="tpu_custom_call" | custom-call | flops 268435456 | bytes 8388608 | tf_op jit(solution)/shard_map/local_forward/pallas_call | solution.py:371
  54.5 1.8 %collective-permute-start.10 = (bf16[17,32,128]{2,1,0:T(8,128)(2,1)S(1)}, bf16[17,32,128]{2,1,0:T(8,128)(2,1)S(1)}, u32[]{:S(2)}, u32[]{:S(2)}) collective-permute-start(bf16[17,32,128]{2,1,0:T(8,128)(2,1)S(1)} %fold.7), channel_id=1, source_target_pairs={{0,8},{4,12},{8,0},{12,4},{16,24},{20,28},{24,16},{28,20},{1,9},{5... | collective-permute-start | bytes 417800 | tf_op jit(solution)/shard_map/ppermute | solution.py:401
  56.4 1.5 collective-permute-start.13
  58.5 1.4 collective-permute-done.13.refs_11_
  60.0 2.0 %collective-permute-done.11.refs_3_ = bf16[17,32,128]{2,1,0:T(8,128)(2,1)S(1)} collective-permute-done((bf16[17,32,128]{2,1,0:T(8,128)(2,1)S(1)}, bf16[17,32,128]{2,1,0:T(8,128)(2,1)S(1)}, u32[]{:S(2)}, u32[]{:S(2)}) %collective-permute-start.11) | collective-permute-done | bytes 139296 | tf_op jit(solution)/shard_map/ppermute | solution.py:401
  62.9 2.3 %collective-permute-start.19 = (bf16[16,32,128]{2,1,0:T(8,128)(2,1)S(1)}, bf16[16,32,128]{2,1,0:T(8,128)(2,1)S(1)}, u32[]{:S(2)}, u32[]{:S(2)}) collective-permute-start(bf16[16,32,128]{2,1,0:T(8,128)(2,1)S(1)} %get-tuple-element.92.panel_ref.refs_0_), channel_id=1, source_target_pairs={{0,24},{4,28},{8,16},{12,20},{16,8},{20,12},{24,0},{28,4},{1,25},{... | collective-permute-start | bytes 393224 | tf_op jit(solution)/shard_map/ppermute | solution.py:401
  65.2 2.2 %collective-permute-start.15 = (bf16[16,32,128]{2,1,0:T(8,128)(2,1)S(1)}, bf16[16,32,128]{2,1,0:T(8,128)(2,1)S(1)}, u32[]{:S(2)}, u32[]{:S(2)}) collective-permute-start(bf16[16,32,128]{2,1,0:T(8,128)(2,1)S(1)} %get-tuple-element.92.panel_ref.refs_0_), channel_id=1, source_target_pairs={{0,8},{4,12},{8,0},{12,4},{16,24},{20,28},{24,16},{28,20},{1,9},{5... | collective-permute-start | bytes 393224 | tf_op jit(solution)/shard_map/ppermute | solution.py:401
  67.4 1.0 collective-permute-start.14
  68.4 2.9 %collective-permute-done.19.refs_2_.refs_6_ = bf16[16,32,128]{2,1,0:T(8,128)(2,1)S(1)} collective-permute-done((bf16[16,32,128]{2,1,0:T(8,128)(2,1)S(1)}, bf16[16,32,128]{2,1,0:T(8,128)(2,1)S(1)}, u32[]{:S(2)}, u32[]{:S(2)}) %collective-permute-start.19) | collective-permute-done | bytes 131104 | tf_op jit(solution)/shard_map/ppermute | solution.py:401
  72.1 3.2 %collective-permute-done.17.refs_1_.refs_4_ = bf16[16,32,128]{2,1,0:T(8,128)(2,1)S(1)} collective-permute-done((bf16[16,32,128]{2,1,0:T(8,128)(2,1)S(1)}, bf16[16,32,128]{2,1,0:T(8,128)(2,1)S(1)}, u32[]{:S(2)}, u32[]{:S(2)}) %collective-permute-start.17) | collective-permute-done | bytes 131104 | tf_op jit(solution)/shard_map/ppermute | solution.py:401
  75.4 0.9 collective-permute-start.18
  76.3 1.1 collective-permute-start.16
  77.4 4.3 %local_adjoint.4 = (f32[32,8192]{1,0:T(8,128)S(1)}, f32[8,128]{1,0:T(8,128)S(1)}) custom-call(s32[256]{0:T(256)S(1)} %reshape.26.index_ref, bf16[16,32,128]{2,1,0:T(8,128)(2,1)S(1)} %get-tuple-element.92.panel_ref.refs_0_, bf16[64,4,128,128]{3,2,1,0:T(8,128)(2,1)S(1)} %copy-done.2, f32[8,128]{1,0:T(8,128)S(1)} %get-tuple-element.93.sum_ref, ...), custom_call_target="tpu_custom_call" | custom-call | flops 268435456 | bytes 8388608 | tf_op jit(solution)/shard_map/local_adjoint/pallas_call | solution.py:235
  81.7 1.1 collective-permute-done.21.refs_14_
  83.0 3.5 %head_step.4 = (f32[32,8192]{1,0:T(8,128)S(1)}, bf16[32,8192]{1,0:T(8,128)(2,1)S(1)}, bf16[32,128]{1,0:T(8,128)(2,1)S(1)}, f32[8,128]{1,0:T(8,128)S(1)}, f32[16,...) custom-call(s32[64]{0:T(128)S(1)} %fusion.index_ref, ...), custom_call_target="tpu_custom_call" | custom-call | flops 134217728 | bytes 7864320 | tf_op jit(solution)/shard_map/head_step/pallas_call | solution.py:275
  86.5 0.9 collective-permute-start.22
  87.4 7.6 %collective-permute-done.22.refs_2_ = bf16[33,32,128]{2,1,0:T(8,128)(2,1)S(1)} collective-permute-done((bf16[33,32,128]{2,1,0:T(8,128)(2,1)S(1)}, bf16[33,32,128]{2,1,0:T(8,128)(2,1)S(1)}, u32[]{:S(2)}, u32[]{:S(2)}) %collective-permute-start.22) | collective-permute-done | bytes 270368 | tf_op jit(solution)/shard_map/ppermute | solution.py:401
  95.2 1.0 collective-permute-start.23
  96.2 2.1 %collective-permute-start.26 = (bf16[17,32,128]{2,1,0:T(8,128)(2,1)S(1)}, bf16[17,32,128]{2,1,0:T(8,128)(2,1)S(1)}, u32[]{:S(2)}, u32[]{:S(2)}) collective-permute-start(bf16[17,32,128]{2,1,0:T(8,128)(2,1)S(1)} %get-tuple-element.112), channel_id=1, source_target_pairs={{0,24},{4,28},{8,16},{12,20},{16,8},{20,12},{24,0},{28,4},{1,25},{... | collective-permute-start | bytes 417800 | tf_op jit(solution)/shard_map/ppermute | solution.py:401
  98.2 3.3 %local_forward.4 = (f32[16,32,128]{2,1,0:T(8,128)S(1)}, f32[8,128]{1,0:T(8,128)S(1)}) custom-call(s32[256]{0:T(256)S(1)} %reshape.26.index_ref, bf16[32,8192]{1,0:T(8,128)(2,1)S(1)} %get-tuple-element.107.bar_ref, bf16[64,4,128,128]{3,2,1,0:T(8,128)(2,1)S(1)} %copy-done.2, f32[16,32,128]{2,1,0:T(8,128)S(1)} %get-tuple-element.108.duals_ref, ...), custom_call_target="tpu_custom_call" | custom-call | flops 268435456 | bytes 8388608 | tf_op jit(solution)/shard_map/local_forward/pallas_call | solution.py:371
  101.5 1.2 collective-permute-done.23.refs_1_
  102.7 1.2 collective-permute-start.24
  103.9 1.6 %collective-permute-start.27 = (f32[8,128]{1,0:T(8,128)S(1)}, f32[8,128]{1,0:T(8,128)S(1)}, u32[]{:S(2)}, u32[]{:S(2)}) collective-permute-start(f32[8,128]{1,0:T(8,128)S(1)} %get-tuple-element.115.refs_10_), channel_id=1, source_target_pairs={{0,2},{1,3},{2,0},{3,1},{4,6},{5,7},{6,4},{7,5},{8,10},{9,11},{10,... | collective-permute-start | bytes 12296 | tf_op jit(solution)/shard_map/ppermute | solution.py:401
  105.6 2.0 %collective-permute-done.27.refs_11_ = f32[8,128]{1,0:T(8,128)S(1)} collective-permute-done((f32[8,128]{1,0:T(8,128)S(1)}, f32[8,128]{1,0:T(8,128)S(1)}, u32[]{:S(2)}, u32[]{:S(2)}) %collective-permute-start.27) | collective-permute-done | bytes 4128 | tf_op jit(solution)/shard_map/ppermute | solution.py:401
  107.5 1.8 %collective-permute-done.25.refs_3_ = bf16[17,32,128]{2,1,0:T(8,128)(2,1)S(1)} collective-permute-done((bf16[17,32,128]{2,1,0:T(8,128)(2,1)S(1)}, bf16[17,32,128]{2,1,0:T(8,128)(2,1)S(1)}, u32[]{:S(2)}, u32[]{:S(2)}) %collective-permute-start.25) | collective-permute-done | bytes 139296 | tf_op jit(solution)/shard_map/ppermute | solution.py:401
  109.3 1.2 collective-permute-done.24.refs_2_
  110.7 1.6 collective-permute-start.33
  112.3 2.8 %collective-permute-start.29 = (bf16[16,32,128]{2,1,0:T(8,128)(2,1)S(1)}, bf16[16,32,128]{2,1,0:T(8,128)(2,1)S(1)}, u32[]{:S(2)}, u32[]{:S(2)}) collective-permute-start(bf16[16,32,128]{2,1,0:T(8,128)(2,1)S(1)} %get-tuple-element.116.panel_ref.refs_0_), channel_id=1, source_target_pairs={{0,8},{4,12},{8,0},{12,4},{16,24},{20,28},{24,16},{28,20},{1,9},{5... | collective-permute-start | bytes 393224 | tf_op jit(solution)/shard_map/ppermute | solution.py:401
  115.2 1.0 collective-permute-start.28
  116.2 2.8 %collective-permute-done.33.refs_2_.refs_6_ = bf16[16,32,128]{2,1,0:T(8,128)(2,1)S(1)} collective-permute-done((bf16[16,32,128]{2,1,0:T(8,128)(2,1)S(1)}, bf16[16,32,128]{2,1,0:T(8,128)(2,1)S(1)}, u32[]{:S(2)}, u32[]{:S(2)}) %collective-permute-start.33) | collective-permute-done | bytes 131104 | tf_op jit(solution)/shard_map/ppermute | solution.py:401
  119.0 1.0 collective-permute-start.34
  120.0 3.1 %collective-permute-done.31.refs_1_.refs_4_ = bf16[16,32,128]{2,1,0:T(8,128)(2,1)S(1)} collective-permute-done((bf16[16,32,128]{2,1,0:T(8,128)(2,1)S(1)}, bf16[16,32,128]{2,1,0:T(8,128)(2,1)S(1)}, u32[]{:S(2)}, u32[]{:S(2)}) %collective-permute-start.31) | collective-permute-done | bytes 131104 | tf_op jit(solution)/shard_map/ppermute | solution.py:401
  123.2 1.0 collective-permute-start.32
  124.2 1.0 collective-permute-start.30
  125.2 4.3 %local_adjoint.5 = (f32[32,8192]{1,0:T(8,128)S(1)}, f32[8,128]{1,0:T(8,128)S(1)}) custom-call(s32[256]{0:T(256)S(1)} %reshape.26.index_ref, bf16[16,32,128]{2,1,0:T(8,128)(2,1)S(1)} %get-tuple-element.116.panel_ref.refs_0_, bf16[64,4,128,128]{3,2,1,0:T(8,128)(2,1)S(1)} %copy-done.2, f32[8,128]{1,0:T(8,128)S(1)} %get-tuple-element.117.sum_ref, ...), custom_call_target="tpu_custom_call" | custom-call | flops 268435456 | bytes 8388608 | tf_op jit(solution)/shard_map/local_adjoint/pallas_call | solution.py:235
  129.5 1.1 collective-permute-done.35.refs_14_
  130.7 4.2 %head_step.5 = (f32[32,8192]{1,0:T(8,128)}, bf16[32,8192]{1,0:T(8,128)(2,1)S(1)}, bf16[32,128]{1,0:T(8,128)(2,1)S(1)}, f32[8,128]{1,0:T(8,128)S(1)}, f32[16,32,1...) custom-call(s32[64]{0:T(128)S(1)} %fusion.index_ref, ...), custom_call_target="tpu_custom_call" | custom-call | flops 134217728 | bytes 7864320 | tf_op jit(solution)/shard_map/head_step/pallas_call | solution.py:275
  134.9 1.0 collective-permute-start.36
  135.9 7.6 %collective-permute-done.36.refs_2_ = bf16[33,32,128]{2,1,0:T(8,128)(2,1)S(1)} collective-permute-done((bf16[33,32,128]{2,1,0:T(8,128)(2,1)S(1)}, bf16[33,32,128]{2,1,0:T(8,128)(2,1)S(1)}, u32[]{:S(2)}, u32[]{:S(2)}) %collective-permute-start.36) | collective-permute-done | bytes 270368 | tf_op jit(solution)/shard_map/ppermute | solution.py:401
  143.5 1.1 collective-permute-start.37
  144.6 2.1 %collective-permute-start.40 = (bf16[17,32,128]{2,1,0:T(8,128)(2,1)S(1)}, bf16[17,32,128]{2,1,0:T(8,128)(2,1)S(1)}, u32[]{:S(2)}, u32[]{:S(2)}) collective-permute-start(bf16[17,32,128]{2,1,0:T(8,128)(2,1)S(1)} %get-tuple-element.137), channel_id=1, source_target_pairs={{0,24},{4,28},{8,16},{12,20},{16,8},{20,12},{24,0},{28,4},{1,25},{... | collective-permute-start | bytes 417800 | tf_op jit(solution)/shard_map/ppermute | solution.py:401
  146.7 3.3 %local_forward.5 = (f32[16,32,128]{2,1,0:T(8,128)S(1)}, f32[8,128]{1,0:T(8,128)S(1)}) custom-call(s32[256]{0:T(256)S(1)} %reshape.26.index_ref, bf16[32,8192]{1,0:T(8,128)(2,1)S(1)} %get-tuple-element.132.bar_ref, bf16[64,4,128,128]{3,2,1,0:T(8,128)(2,1)S(1)} %copy-done.2, f32[16,32,128]{2,1,0:T(8,128)S(1)} %get-tuple-element.133.duals_ref, ...), custom_call_target="tpu_custom_call" | custom-call | flops 268435456 | bytes 8388608 | tf_op jit(solution)/shard_map/local_forward/pallas_call | solution.py:371
  149.9 1.2 collective-permute-done.37.refs_1_
  151.2 1.2 collective-permute-start.38
  152.4 1.6 collective-permute-start.41
  154.0 2.0 %collective-permute-done.41.refs_11_ = f32[8,128]{1,0:T(8,128)S(1)} collective-permute-done((f32[8,128]{1,0:T(8,128)S(1)}, f32[8,128]{1,0:T(8,128)S(1)}, u32[]{:S(2)}, u32[]{:S(2)}) %collective-permute-start.41) | collective-permute-done | bytes 4128 | tf_op jit(solution)/shard_map/ppermute | solution.py:401
  156.0 2.1 %collective-permute-done.39.refs_3_ = bf16[17,32,128]{2,1,0:T(8,128)(2,1)S(1)} collective-permute-done((bf16[17,32,128]{2,1,0:T(8,128)(2,1)S(1)}, bf16[17,32,128]{2,1,0:T(8,128)(2,1)S(1)}, u32[]{:S(2)}, u32[]{:S(2)}) %collective-permute-start.39) | collective-permute-done | bytes 139296 | tf_op jit(solution)/shard_map/ppermute | solution.py:401
  158.0 0.9 collective-permute-done.38.refs_2_
  (73 shorter events, 8.0 us)
Async XLA Ops:
  0.6 1.0 copy-start
  0.6 30.8 %copy-start.8 = (f32[32]{0:T(128)S(1)}, f32[32]{0:T(128)}, u32[]{:S(2)}) copy-start(f32[32]{0:T(128)} %param.15) | copy-start | bytes 388
  0.7 29.6 %copy-start.10 = (s32[64]{0:T(128)S(1)}, s32[64]{0:T(128)}, u32[]{:S(2)}) copy-start(s32[64]{0:T(128)} %param.21) | copy-start | bytes 772
  0.7 30.9 %copy-start.6 = (f32[8192]{0:T(1024)S(1)}, f32[8192]{0:T(1024)}, u32[]{:S(2)}) copy-start(f32[8192]{0:T(1024)} %param.17) | copy-start | bytes 98308
  0.7 47.8 %copy-start.7 = (f32[32,2048]{1,0:T(8,128)S(1)}, f32[32,2048]{1,0:T(8,128)}, u32[]{:S(2)}) copy-start(f32[32,2048]{1,0:T(8,128)} %param.13) | copy-start | bytes 786436
  1.6 14.1 %collective-permute-start.3 = (bf16[16,32,128]{2,1,0:T(8,128)(2,1)S(1)}, bf16[16,32,128]{2,1,0:T(8,128)(2,1)S(1)}, u32[]{:S(2)}, u32[]{:S(2)}) collective-permute-start(bf16[16,32,128]{2,1,0:T(8,128)(2,1)S(1)} %fusion.1.panel_ref.refs_0_), channel_id=1, source_target_pairs={{0,16},{4,20},{8,24},{12,28},{16,0},{20,4},{24,8},{28,12},{1,17},{... | collective-permute-start | bytes 393224 | tf_op jit(solution)/shard_map/ppermute | solution.py:401
  5.7 14.2 %collective-permute-start.5 = (bf16[16,32,128]{2,1,0:T(8,128)(2,1)S(1)}, bf16[16,32,128]{2,1,0:T(8,128)(2,1)S(1)}, u32[]{:S(2)}, u32[]{:S(2)}) collective-permute-start(bf16[16,32,128]{2,1,0:T(8,128)(2,1)S(1)} %fusion.1.panel_ref.refs_0_), channel_id=1, source_target_pairs={{0,24},{4,28},{8,16},{12,20},{16,8},{20,12},{24,0},{28,4},{1,25},{... | collective-permute-start | bytes 393224 | tf_op jit(solution)/shard_map/ppermute | solution.py:401
  7.1 14.7 %collective-permute-start.1 = (bf16[16,32,128]{2,1,0:T(8,128)(2,1)S(1)}, bf16[16,32,128]{2,1,0:T(8,128)(2,1)S(1)}, u32[]{:S(2)}, u32[]{:S(2)}) collective-permute-start(bf16[16,32,128]{2,1,0:T(8,128)(2,1)S(1)} %fusion.1.panel_ref.refs_0_), channel_id=1, source_target_pairs={{0,8},{4,12},{8,0},{12,4},{16,24},{20,28},{24,16},{28,20},{1,9},{5... | collective-permute-start | bytes 393224 | tf_op jit(solution)/shard_map/ppermute | solution.py:401
  15.7 6.2 %collective-permute-start.4 = (bf16[16,32,128]{2,1,0:T(8,128)(2,1)S(1)}, bf16[16,32,128]{2,1,0:T(8,128)(2,1)S(1)}, u32[]{:S(2)}, u32[]{:S(2)}) collective-permute-start(bf16[16,32,128]{2,1,0:T(8,128)(2,1)S(1)} %collective-permute-done.3.refs_4_), channel_id=1, source_target_pairs={{0,4},{4,0},{8,12},{12,8},{16,20},{20,16},{24,28},{28,24},{1,5},{5... | collective-permute-start | bytes 393224 | tf_op jit(solution)/shard_map/ppermute | solution.py:401
  17.6 12.8 %collective-permute-start = (bf16[16,32,128]{2,1,0:T(8,128)(2,1)S(1)}, bf16[16,32,128]{2,1,0:T(8,128)(2,1)S(1)}, u32[]{:S(2)}, u32[]{:S(2)}) collective-permute-start(bf16[16,32,128]{2,1,0:T(8,128)(2,1)S(1)} %fusion.1.panel_ref.refs_0_), channel_id=1, source_target_pairs={{0,4},{4,0},{8,12},{12,8},{16,20},{20,16},{24,28},{28,24},{1,5},{5... | collective-permute-start | bytes 393224 | tf_op jit(solution)/shard_map/ppermute | solution.py:401
  19.9 10.5 %collective-permute-start.6 = (bf16[16,32,128]{2,1,0:T(8,128)(2,1)S(1)}, bf16[16,32,128]{2,1,0:T(8,128)(2,1)S(1)}, u32[]{:S(2)}, u32[]{:S(2)}) collective-permute-start(bf16[16,32,128]{2,1,0:T(8,128)(2,1)S(1)} %collective-permute-done.5.refs_6_), channel_id=1, source_target_pairs={{0,4},{4,0},{8,12},{12,8},{16,20},{20,16},{24,28},{28,24},{1,5},{5... | collective-permute-start | bytes 393224 | tf_op jit(solution)/shard_map/ppermute | solution.py:401
  21.7 8.6 %collective-permute-start.2 = (bf16[16,32,128]{2,1,0:T(8,128)(2,1)S(1)}, bf16[16,32,128]{2,1,0:T(8,128)(2,1)S(1)}, u32[]{:S(2)}, u32[]{:S(2)}) collective-permute-start(bf16[16,32,128]{2,1,0:T(8,128)(2,1)S(1)} %collective-permute-done.1.refs_2_), channel_id=1, source_target_pairs={{0,4},{4,0},{8,12},{12,8},{16,20},{20,16},{24,28},{28,24},{1,5},{5... | collective-permute-start | bytes 393224 | tf_op jit(solution)/shard_map/ppermute | solution.py:401
  22.6 3.4 %copy-start.1 = (bf16[64,4,128,128]{3,2,1,0:T(8,128)(2,1)S(1)}, bf16[64,4,128,128]{3,2,1,0:T(8,128)(2,1)}, u32[]{:S(2)}) copy-start(bf16[64,4,128,128]{3,2,1,0:T(8,128)(2,1)} %blocks_ref.11) | copy-start | bytes 25165828
  26.0 25.3 %copy-start.2 = (bf16[64,4,128,128]{3,2,1,0:T(8,128)(2,1)S(1)}, bf16[64,4,128,128]{3,2,1,0:T(8,128)(2,1)}, u32[]{:S(2)}) copy-start(bf16[64,4,128,128]{3,2,1,0:T(8,128)(2,1)} %blocks_ref.11) | copy-start | bytes 25165828
  30.2 1.2 collective-permute-start.7
  31.5 1.6 copy-start.3
  33.1 1.2 copy-start.5
  34.3 28.3 %copy-start.9 = (f32[32]{0:T(128)S(1)}, f32[32]{0:T(128)}, u32[]{:S(2)}) copy-start(f32[32]{0:T(128)} %param.14) | copy-start | bytes 388
  37.9 8.7 %collective-permute-start.8 = (bf16[33,32,128]{2,1,0:T(8,128)(2,1)S(1)}, bf16[33,32,128]{2,1,0:T(8,128)(2,1)S(1)}, u32[]{:S(2)}, u32[]{:S(2)}) collective-permute-start(bf16[33,32,128]{2,1,0:T(8,128)(2,1)S(1)} %get-tuple-element.80), channel_id=1, source_target_pairs={{0,4},{4,0},{8,12},{12,8},{16,20},{20,16},{24,28},{28,24},{1,5},{5... | collective-permute-start | bytes 811016 | tf_op jit(solution)/shard_map/ppermute | solution.py:401
  46.7 7.8 %collective-permute-start.9 = (bf16[32,32,128]{2,1,0:T(8,128)(2,1)S(1)}, bf16[32,32,128]{2,1,0:T(8,128)(2,1)S(1)}, u32[]{:S(2)}, u32[]{:S(2)}) collective-permute-start(bf16[32,32,128]{2,1,0:T(8,128)(2,1)S(1)} %get-tuple-element.83), channel_id=1, source_target_pairs={{0,4},{4,0},{8,12},{12,8},{16,20},{20,16},{24,28},{28,24},{1,5},{5... | collective-permute-start | bytes 786440 | tf_op jit(solution)/shard_map/ppermute | solution.py:401
  48.5 11.4 %collective-permute-start.12 = (bf16[17,32,128]{2,1,0:T(8,128)(2,1)S(1)}, bf16[17,32,128]{2,1,0:T(8,128)(2,1)S(1)}, u32[]{:S(2)}, u32[]{:S(2)}) collective-permute-start(bf16[17,32,128]{2,1,0:T(8,128)(2,1)S(1)} %get-tuple-element.90), channel_id=1, source_target_pairs={{0,24},{4,28},{8,16},{12,20},{16,8},{20,12},{24,0},{28,4},{1,25},{... | collective-permute-start | bytes 417800 | tf_op jit(solution)/shard_map/ppermute | solution.py:401
  51.2 10.7 %collective-permute-start.11 = (bf16[17,32,128]{2,1,0:T(8,128)(2,1)S(1)}, bf16[17,32,128]{2,1,0:T(8,128)(2,1)S(1)}, u32[]{:S(2)}, u32[]{:S(2)}) collective-permute-start(bf16[17,32,128]{2,1,0:T(8,128)(2,1)S(1)} %get-tuple-element.88.after_ref), channel_id=1, source_target_pairs={{0,16},{4,20},{8,24},{12,28},{16,0},{20,4},{24,8},{28,12},{1,17},{... | collective-permute-start | bytes 417800 | tf_op jit(solution)/shard_map/ppermute | solution.py:401
  51.2 31.8 %copy-start.4 = (bf16[64,128,128]{2,1,0:T(8,128)(2,1)S(1)}, bf16[64,128,128]{2,1,0:T(8,128)(2,1)}, u32[]{:S(2)}) copy-start(bf16[64,128,128]{2,1,0:T(8,128)(2,1)} %refs_8_.5) | copy-start | bytes 6291460
  54.5 8.1 %collective-permute-start.10 = (bf16[17,32,128]{2,1,0:T(8,128)(2,1)S(1)}, bf16[17,32,128]{2,1,0:T(8,128)(2,1)S(1)}, u32[]{:S(2)}, u32[]{:S(2)}) collective-permute-start(bf16[17,32,128]{2,1,0:T(8,128)(2,1)S(1)} %fold.7), channel_id=1, source_target_pairs={{0,8},{4,12},{8,0},{12,4},{16,24},{20,28},{24,16},{28,20},{1,9},{5... | collective-permute-start | bytes 417800 | tf_op jit(solution)/shard_map/ppermute | solution.py:401
  56.4 3.6 %collective-permute-start.13 = (f32[8,128]{1,0:T(8,128)S(1)}, f32[8,128]{1,0:T(8,128)S(1)}, u32[]{:S(2)}, u32[]{:S(2)}) collective-permute-start(f32[8,128]{1,0:T(8,128)S(1)} %get-tuple-element.91.refs_10_), channel_id=1, source_target_pairs={{0,2},{1,3},{2,0},{3,1},{4,6},{5,7},{6,4},{7,5},{8,10},{9,11},{10,... | collective-permute-start | bytes 12296 | tf_op jit(solution)/shard_map/ppermute | solution.py:401
  62.9 8.3 %collective-permute-start.19 = (bf16[16,32,128]{2,1,0:T(8,128)(2,1)S(1)}, bf16[16,32,128]{2,1,0:T(8,128)(2,1)S(1)}, u32[]{:S(2)}, u32[]{:S(2)}) collective-permute-start(bf16[16,32,128]{2,1,0:T(8,128)(2,1)S(1)} %get-tuple-element.92.panel_ref.refs_0_), channel_id=1, source_target_pairs={{0,24},{4,28},{8,16},{12,20},{16,8},{20,12},{24,0},{28,4},{1,25},{... | collective-permute-start | bytes 393224 | tf_op jit(solution)/shard_map/ppermute | solution.py:401
  65.2 10.1 %collective-permute-start.17 = (bf16[16,32,128]{2,1,0:T(8,128)(2,1)S(1)}, bf16[16,32,128]{2,1,0:T(8,128)(2,1)S(1)}, u32[]{:S(2)}, u32[]{:S(2)}) collective-permute-start(bf16[16,32,128]{2,1,0:T(8,128)(2,1)S(1)} %get-tuple-element.92.panel_ref.refs_0_), channel_id=1, source_target_pairs={{0,16},{4,20},{8,24},{12,28},{16,0},{20,4},{24,8},{28,12},{1,17},{... | collective-permute-start | bytes 393224 | tf_op jit(solution)/shard_map/ppermute | solution.py:401
  65.2 11.1 %collective-permute-start.15 = (bf16[16,32,128]{2,1,0:T(8,128)(2,1)S(1)}, bf16[16,32,128]{2,1,0:T(8,128)(2,1)S(1)}, u32[]{:S(2)}, u32[]{:S(2)}) collective-permute-start(bf16[16,32,128]{2,1,0:T(8,128)(2,1)S(1)} %get-tuple-element.92.panel_ref.refs_0_), channel_id=1, source_target_pairs={{0,8},{4,12},{8,0},{12,4},{16,24},{20,28},{24,16},{28,20},{1,9},{5... | collective-permute-start | bytes 393224 | tf_op jit(solution)/shard_map/ppermute | solution.py:401
  67.4 14.3 %collective-permute-start.14 = (bf16[16,32,128]{2,1,0:T(8,128)(2,1)S(1)}, bf16[16,32,128]{2,1,0:T(8,128)(2,1)S(1)}, u32[]{:S(2)}, u32[]{:S(2)}) collective-permute-start(bf16[16,32,128]{2,1,0:T(8,128)(2,1)S(1)} %get-tuple-element.92.panel_ref.refs_0_), channel_id=1, source_target_pairs={{0,4},{4,0},{8,12},{12,8},{16,20},{20,16},{24,28},{28,24},{1,5},{5... | collective-permute-start | bytes 393224 | tf_op jit(solution)/shard_map/ppermute | solution.py:401
  71.2 11.6 %collective-permute-start.20 = (bf16[16,32,128]{2,1,0:T(8,128)(2,1)S(1)}, bf16[16,32,128]{2,1,0:T(8,128)(2,1)S(1)}, u32[]{:S(2)}, u32[]{:S(2)}) collective-permute-start(bf16[16,32,128]{2,1,0:T(8,128)(2,1)S(1)} %collective-permute-done.19.refs_2_.refs_6_), channel_id=1, source_target_pairs={{0,4},{4,0},{8,12},{12,8},{16,20},{20,16},{24,28},{28,24},{1,5},{5... | collective-permute-start | bytes 393224 | tf_op jit(solution)/shard_map/ppermute | solution.py:401
  75.4 7.5 %collective-permute-start.18 = (bf16[16,32,128]{2,1,0:T(8,128)(2,1)S(1)}, bf16[16,32,128]{2,1,0:T(8,128)(2,1)S(1)}, u32[]{:S(2)}, u32[]{:S(2)}) collective-permute-start(bf16[16,32,128]{2,1,0:T(8,128)(2,1)S(1)} %collective-permute-done.17.refs_1_.refs_4_), channel_id=1, source_target_pairs={{0,4},{4,0},{8,12},{12,8},{16,20},{20,16},{24,28},{28,24},{1,5},{5... | collective-permute-start | bytes 393224 | tf_op jit(solution)/shard_map/ppermute | solution.py:401
  76.3 6.7 %collective-permute-start.16 = (bf16[16,32,128]{2,1,0:T(8,128)(2,1)S(1)}, bf16[16,32,128]{2,1,0:T(8,128)(2,1)S(1)}, u32[]{:S(2)}, u32[]{:S(2)}) collective-permute-start(bf16[16,32,128]{2,1,0:T(8,128)(2,1)S(1)} %collective-permute-done.15.refs_0_.refs_2_), channel_id=1, source_target_pairs={{0,4},{4,0},{8,12},{12,8},{16,20},{20,16},{24,28},{28,24},{1,5},{5... | collective-permute-start | bytes 393224 | tf_op jit(solution)/shard_map/ppermute | solution.py:401
  81.7 1.2 collective-permute-start.21
  86.5 8.5 %collective-permute-start.22 = (bf16[33,32,128]{2,1,0:T(8,128)(2,1)S(1)}, bf16[33,32,128]{2,1,0:T(8,128)(2,1)S(1)}, u32[]{:S(2)}, u32[]{:S(2)}) collective-permute-start(bf16[33,32,128]{2,1,0:T(8,128)(2,1)S(1)} %get-tuple-element.101), channel_id=1, source_target_pairs={{0,4},{4,0},{8,12},{12,8},{16,20},{20,16},{24,28},{28,24},{1,5},{5... | collective-permute-start | bytes 811016 | tf_op jit(solution)/shard_map/ppermute | solution.py:401
  95.2 7.5 %collective-permute-start.23 = (bf16[32,32,128]{2,1,0:T(8,128)(2,1)S(1)}, bf16[32,32,128]{2,1,0:T(8,128)(2,1)S(1)}, u32[]{:S(2)}, u32[]{:S(2)}) collective-permute-start(bf16[32,32,128]{2,1,0:T(8,128)(2,1)S(1)} %get-tuple-element.104), channel_id=1, source_target_pairs={{0,4},{4,0},{8,12},{12,8},{16,20},{20,16},{24,28},{28,24},{1,5},{5... | collective-permute-start | bytes 786440 | tf_op jit(solution)/shard_map/ppermute | solution.py:401
  96.2 11.4 %collective-permute-start.26 = (bf16[17,32,128]{2,1,0:T(8,128)(2,1)S(1)}, bf16[17,32,128]{2,1,0:T(8,128)(2,1)S(1)}, u32[]{:S(2)}, u32[]{:S(2)}) collective-permute-start(bf16[17,32,128]{2,1,0:T(8,128)(2,1)S(1)} %get-tuple-element.112), channel_id=1, source_target_pairs={{0,24},{4,28},{8,16},{12,20},{16,8},{20,12},{24,0},{28,4},{1,25},{... | collective-permute-start | bytes 417800 | tf_op jit(solution)/shard_map/ppermute | solution.py:401
  98.2 11.1 %collective-permute-start.25 = (bf16[17,32,128]{2,1,0:T(8,128)(2,1)S(1)}, bf16[17,32,128]{2,1,0:T(8,128)(2,1)S(1)}, u32[]{:S(2)}, u32[]{:S(2)}) collective-permute-start(bf16[17,32,128]{2,1,0:T(8,128)(2,1)S(1)} %get-tuple-element.110.after_ref), channel_id=1, source_target_pairs={{0,16},{4,20},{8,24},{12,28},{16,0},{20,4},{24,8},{28,12},{1,17},{... | collective-permute-start | bytes 417800 | tf_op jit(solution)/shard_map/ppermute | solution.py:401
  102.7 7.8 %collective-permute-start.24 = (bf16[17,32,128]{2,1,0:T(8,128)(2,1)S(1)}, bf16[17,32,128]{2,1,0:T(8,128)(2,1)S(1)}, u32[]{:S(2)}, u32[]{:S(2)}) collective-permute-start(bf16[17,32,128]{2,1,0:T(8,128)(2,1)S(1)} %fold.9), channel_id=1, source_target_pairs={{0,8},{4,12},{8,0},{12,4},{16,24},{20,28},{24,16},{28,20},{1,9},{5... | collective-permute-start | bytes 417800 | tf_op jit(solution)/shard_map/ppermute | solution.py:401
  103.9 3.6 %collective-permute-start.27 = (f32[8,128]{1,0:T(8,128)S(1)}, f32[8,128]{1,0:T(8,128)S(1)}, u32[]{:S(2)}, u32[]{:S(2)}) collective-permute-start(f32[8,128]{1,0:T(8,128)S(1)} %get-tuple-element.115.refs_10_), channel_id=1, source_target_pairs={{0,2},{1,3},{2,0},{3,1},{4,6},{5,7},{6,4},{7,5},{8,10},{9,11},{10,... | collective-permute-start | bytes 12296 | tf_op jit(solution)/shard_map/ppermute | solution.py:401
  110.7 8.3 %collective-permute-start.33 = (bf16[16,32,128]{2,1,0:T(8,128)(2,1)S(1)}, bf16[16,32,128]{2,1,0:T(8,128)(2,1)S(1)}, u32[]{:S(2)}, u32[]{:S(2)}) collective-permute-start(bf16[16,32,128]{2,1,0:T(8,128)(2,1)S(1)} %get-tuple-element.116.panel_ref.refs_0_), channel_id=1, source_target_pairs={{0,24},{4,28},{8,16},{12,20},{16,8},{20,12},{24,0},{28,4},{1,25},{... | collective-permute-start | bytes 393224 | tf_op jit(solution)/shard_map/ppermute | solution.py:401
  112.3 10.8 %collective-permute-start.31 = (bf16[16,32,128]{2,1,0:T(8,128)(2,1)S(1)}, bf16[16,32,128]{2,1,0:T(8,128)(2,1)S(1)}, u32[]{:S(2)}, u32[]{:S(2)}) collective-permute-start(bf16[16,32,128]{2,1,0:T(8,128)(2,1)S(1)} %get-tuple-element.116.panel_ref.refs_0_), channel_id=1, source_target_pairs={{0,16},{4,20},{8,24},{12,28},{16,0},{20,4},{24,8},{28,12},{1,17},{... | collective-permute-start | bytes 393224 | tf_op jit(solution)/shard_map/ppermute | solution.py:401
  112.3 11.8 %collective-permute-start.29 = (bf16[16,32,128]{2,1,0:T(8,128)(2,1)S(1)}, bf16[16,32,128]{2,1,0:T(8,128)(2,1)S(1)}, u32[]{:S(2)}, u32[]{:S(2)}) collective-permute-start(bf16[16,32,128]{2,1,0:T(8,128)(2,1)S(1)} %get-tuple-element.116.panel_ref.refs_0_), channel_id=1, source_target_pairs={{0,8},{4,12},{8,0},{12,4},{16,24},{20,28},{24,16},{28,20},{1,9},{5... | collective-permute-start | bytes 393224 | tf_op jit(solution)/shard_map/ppermute | solution.py:401
  115.2 14.3 %collective-permute-start.28 = (bf16[16,32,128]{2,1,0:T(8,128)(2,1)S(1)}, bf16[16,32,128]{2,1,0:T(8,128)(2,1)S(1)}, u32[]{:S(2)}, u32[]{:S(2)}) collective-permute-start(bf16[16,32,128]{2,1,0:T(8,128)(2,1)S(1)} %get-tuple-element.116.panel_ref.refs_0_), channel_id=1, source_target_pairs={{0,4},{4,0},{8,12},{12,8},{16,20},{20,16},{24,28},{28,24},{1,5},{5... | collective-permute-start | bytes 393224 | tf_op jit(solution)/shard_map/ppermute | solution.py:401
  119.0 11.6 %collective-permute-start.34 = (bf16[16,32,128]{2,1,0:T(8,128)(2,1)S(1)}, bf16[16,32,128]{2,1,0:T(8,128)(2,1)S(1)}, u32[]{:S(2)}, u32[]{:S(2)}) collective-permute-start(bf16[16,32,128]{2,1,0:T(8,128)(2,1)S(1)} %collective-permute-done.33.refs_2_.refs_6_), channel_id=1, source_target_pairs={{0,4},{4,0},{8,12},{12,8},{16,20},{20,16},{24,28},{28,24},{1,5},{5... | collective-permute-start | bytes 393224 | tf_op jit(solution)/shard_map/ppermute | solution.py:401
  123.2 7.5 %collective-permute-start.32 = (bf16[16,32,128]{2,1,0:T(8,128)(2,1)S(1)}, bf16[16,32,128]{2,1,0:T(8,128)(2,1)S(1)}, u32[]{:S(2)}, u32[]{:S(2)}) collective-permute-start(bf16[16,32,128]{2,1,0:T(8,128)(2,1)S(1)} %collective-permute-done.31.refs_1_.refs_4_), channel_id=1, source_target_pairs={{0,4},{4,0},{8,12},{12,8},{16,20},{20,16},{24,28},{28,24},{1,5},{5... | collective-permute-start | bytes 393224 | tf_op jit(solution)/shard_map/ppermute | solution.py:401
  124.2 6.5 %collective-permute-start.30 = (bf16[16,32,128]{2,1,0:T(8,128)(2,1)S(1)}, bf16[16,32,128]{2,1,0:T(8,128)(2,1)S(1)}, u32[]{:S(2)}, u32[]{:S(2)}) collective-permute-start(bf16[16,32,128]{2,1,0:T(8,128)(2,1)S(1)} %collective-permute-done.29.refs_0_.refs_2_), channel_id=1, source_target_pairs={{0,4},{4,0},{8,12},{12,8},{16,20},{20,16},{24,28},{28,24},{1,5},{5... | collective-permute-start | bytes 393224 | tf_op jit(solution)/shard_map/ppermute | solution.py:401
  129.5 1.2 collective-permute-start.35
  134.9 8.6 %collective-permute-start.36 = (bf16[33,32,128]{2,1,0:T(8,128)(2,1)S(1)}, bf16[33,32,128]{2,1,0:T(8,128)(2,1)S(1)}, u32[]{:S(2)}, u32[]{:S(2)}) collective-permute-start(bf16[33,32,128]{2,1,0:T(8,128)(2,1)S(1)} %get-tuple-element.126), channel_id=1, source_target_pairs={{0,4},{4,0},{8,12},{12,8},{16,20},{20,16},{24,28},{28,24},{1,5},{5... | collective-permute-start | bytes 811016 | tf_op jit(solution)/shard_map/ppermute | solution.py:401
  143.5 7.6 %collective-permute-start.37 = (bf16[32,32,128]{2,1,0:T(8,128)(2,1)S(1)}, bf16[32,32,128]{2,1,0:T(8,128)(2,1)S(1)}, u32[]{:S(2)}, u32[]{:S(2)}) collective-permute-start(bf16[32,32,128]{2,1,0:T(8,128)(2,1)S(1)} %get-tuple-element.129), channel_id=1, source_target_pairs={{0,4},{4,0},{8,12},{12,8},{16,20},{20,16},{24,28},{28,24},{1,5},{5... | collective-permute-start | bytes 786440 | tf_op jit(solution)/shard_map/ppermute | solution.py:401
  144.6 11.4 %collective-permute-start.40 = (bf16[17,32,128]{2,1,0:T(8,128)(2,1)S(1)}, bf16[17,32,128]{2,1,0:T(8,128)(2,1)S(1)}, u32[]{:S(2)}, u32[]{:S(2)}) collective-permute-start(bf16[17,32,128]{2,1,0:T(8,128)(2,1)S(1)} %get-tuple-element.137), channel_id=1, source_target_pairs={{0,24},{4,28},{8,16},{12,20},{16,8},{20,12},{24,0},{28,4},{1,25},{... | collective-permute-start | bytes 417800 | tf_op jit(solution)/shard_map/ppermute | solution.py:401
  146.7 11.4 %collective-permute-start.39 = (bf16[17,32,128]{2,1,0:T(8,128)(2,1)S(1)}, bf16[17,32,128]{2,1,0:T(8,128)(2,1)S(1)}, u32[]{:S(2)}, u32[]{:S(2)}) collective-permute-start(bf16[17,32,128]{2,1,0:T(8,128)(2,1)S(1)} %get-tuple-element.135.after_ref), channel_id=1, source_target_pairs={{0,16},{4,20},{8,24},{12,28},{16,0},{20,4},{24,8},{28,12},{1,17},{... | collective-permute-start | bytes 417800 | tf_op jit(solution)/shard_map/ppermute | solution.py:401
  151.2 7.8 %collective-permute-start.38 = (bf16[17,32,128]{2,1,0:T(8,128)(2,1)S(1)}, bf16[17,32,128]{2,1,0:T(8,128)(2,1)S(1)}, u32[]{:S(2)}, u32[]{:S(2)}) collective-permute-start(bf16[17,32,128]{2,1,0:T(8,128)(2,1)S(1)} %fold.11), channel_id=1, source_target_pairs={{0,8},{4,12},{8,0},{12,4},{16,24},{20,28},{24,16},{28,20},{1,9},{5... | collective-permute-start | bytes 417800 | tf_op jit(solution)/shard_map/ppermute | solution.py:401
  152.4 3.6 %collective-permute-start.41 = (f32[8,128]{1,0:T(8,128)S(1)}, f32[8,128]{1,0:T(8,128)S(1)}, u32[]{:S(2)}, u32[]{:S(2)}) collective-permute-start(f32[8,128]{1,0:T(8,128)S(1)} %get-tuple-element.140.refs_10_), channel_id=1, source_target_pairs={{0,2},{1,3},{2,0},{3,1},{4,6},{5,7},{6,4},{7,5},{8,10},{9,11},{10,... | collective-permute-start | bytes 12296 | tf_op jit(solution)/shard_map/ppermute | solution.py:401

commit v3 on v2

v3 whole, which is shorter than its diff:
```python
import functools

import jax
import jax.numpy as jnp
from jax import lax
from jax.experimental import pallas as pl
from jax.experimental.pallas import tpu as pltpu
from jax.sharding import PartitionSpec as P

ROUNDS = 3

primal_step = 0.5
dual_step = 0.5
risk_step = 1.0
tail_weight = 2.0

MIB = 1024 * 1024
GROUP = 8
HEAD_GROUP = 16


def contract_last(left, right):
    return lax.dot_general(
        left, right, (((1,), (1,)), ((), ())), preferred_element_type=jnp.float32
    )


def local_adjoint_kernel(
    touches, group, index_ref, panel_ref, blocks_ref, *refs
):
    out_ref = refs[-1]
    rows = blocks_ref.shape[-1]
    first = pl.program_id(0) * group
    for member in range(group):
        left = jnp.concatenate(
            [panel_ref[index_ref[first + member, k]] for k in range(touches)], axis=1
        )
        right = jnp.concatenate([blocks_ref[member, k] for k in range(touches)], axis=1)
        out_ref[:, member * rows : (member + 1) * rows] = contract_last(left, right)


def to_parts(column, shape):
    high = column.astype(jnp.bfloat16).astype(jnp.float32)
    rest = column - high
    middle = rest.astype(jnp.bfloat16).astype(jnp.float32)
    low = rest - middle
    lane = lax.broadcasted_iota(jnp.int32, shape, 1)
    packed = jnp.where(
        lane == 0, high, jnp.where(lane == 1, middle, jnp.where(lane == 2, low, 0.0))
    )
    return packed.astype(jnp.bfloat16)


def from_parts(parts):
    return jnp.sum(parts.astype(jnp.float32), axis=1, keepdims=True)


def head_kernel(group, steps, peers, index_ref, *refs):
    panels, refs = refs[:peers], refs[peers:]
    heads_ref, pulled_ref, flows_ref, costs_ref, risk_ref, sum_ref, other_ref = refs[:7]
    flows_out, bar_out, sum_out, refs = *refs[7:10], refs[10:]
    kept, refs = refs[: peers // 2], refs[peers // 2 :]
    sends, (panel, terms, pulled, loss) = refs[:-4], refs[-4:]
    rows = heads_ref.shape[-1]
    node_blks = panels[0].shape[0]
    step = pl.program_id(0)
    first = step * group

    @pl.when(step == 0)
    def _():
        terms[...] = jnp.zeros_like(terms)
        loss[...] = jnp.zeros_like(loss)
        sum_out[...] = sum_ref[...] + other_ref[...]
        for peer in range(peers):
            panel[peer * node_blks : (peer + 1) * node_blks] = panels[peer][...]

    places = [index_ref[first + member] for member in range(group)]
    spans = [slice(member * rows, (member + 1) * rows) for member in range(group)]
    for member in range(group):
        pulled[:, spans[member]] = contract_last(panel[places[member]], heads_ref[member])
    risk = risk_ref[...]
    loss_sum = jnp.zeros_like(risk)
    for columns in spans:
        flows = flows_ref[:, columns]
        cost = costs_ref[:, columns]
        gradient = risk * cost - (pulled[:, columns] + pulled_ref[:, columns])
        flows_new = jnp.maximum(flows - primal_step * gradient, 0.0)
        bar = 2.0 * flows_new - flows
        flows_out[:, columns] = flows_new
        loss_sum += cost * bar
        bar_out[:, columns] = bar.astype(jnp.bfloat16)
    loss[...] += loss_sum
    products = [
        jnp.dot(bar_out[:, spans[m]], heads_ref[m], preferred_element_type=jnp.float32)
        for m in range(group)
    ]
    for member in range(group):
        terms[places[member]] += products[member]

    @pl.when(step == steps - 1)
    def _():
        loss_parts = to_parts(jnp.sum(loss[...], axis=1, keepdims=True), loss.shape)
        for out, distance in zip(kept, inner(peers)):
            out[...] = terms[distance * node_blks : (distance + 1) * node_blks]
        for out, distance in zip(sends, leaves(peers)):
            out[:node_blks] = terms[distance * node_blks : (distance + 1) * node_blks].astype(
                jnp.bfloat16
            )
        sends[-1][node_blks] = loss_parts


def last_hop(distance):
    return 2 if distance == 3 else distance & -distance


def children(distance, peers):
    return [k for k in range(1, peers) if k ^ last_hop(k) == distance]


def inner(peers):
    return [k for k in range(peers) if children(k, peers)]


def leaves(peers):
    return [k for k in range(peers) if not children(k, peers)]


def pair_sum(values):
    while len(values) > 1:
        values = [a + b for a, b in zip(values[::2], values[1::2])] + values[len(values) // 2 * 2 :]
    return values[0]


def fold_kernel(count, with_loss, extras, after, *refs):
    kept_ref, arrived, refs = refs[0], refs[1 : 1 + count], refs[1 + count :]
    node_blks = kept_ref.shape[0]
    if with_loss:
        loss_ref, refs = refs[0], refs[1:]
    extra_in, refs = refs[:extras], refs[extras + after :]
    out_ref, extra_out = refs[0], refs[1:]
    for block in range(node_blks):
        total = pair_sum([ref[block].astype(jnp.float32) for ref in arrived])
        out_ref[block] = (kept_ref[block] + total).astype(jnp.bfloat16)
    if with_loss:
        both = from_parts(loss_ref[loss_ref.shape[0] - 1]) + from_parts(arrived[-1][node_blks])
        out_ref[node_blks] = to_parts(both, loss_ref.shape[1:])
    for source, target in zip(extra_in, extra_out):
        target[...] = source[...]


def settle_kernel(count, arc_total, scen_total, last, *refs):
    kept_ref, arrived, refs = refs[0], refs[1 : 1 + count], refs[1 + count :]
    loss_ref, base_ref, risk_ref, excess_ref, level_ref, sum_ref, other_ref = refs[:7]
    duals_out, half_out, risk_out, excess_out, level_out, sum_out = refs[7:]
    node_blks, _, rows = base_ref.shape
    for block in range(node_blks):
        total = kept_ref[block] + pair_sum([ref[block].astype(jnp.float32) for ref in arrived])
        duals = base_ref[block] - dual_step * total
        if last:
            duals_out[:, block * rows : (block + 1) * rows] = duals
        else:
            duals_out[block] = duals
        half_out[block] = duals.astype(jnp.bfloat16)
    losses = from_parts(loss_ref[node_blks]) + from_parts(arrived[-1][node_blks])
    losses = losses / arc_total
    mean_risk = (sum_ref[...] + other_ref[...]) / scen_total
    level = level_ref[...]
    level_new = level - primal_step * (1.0 - mean_risk)
    level_bar = 2.0 * level_new - level
    level_out[...] = level_new
    risk = risk_ref[...]
    excess = excess_ref[...]
    excess_new = jnp.maximum(excess - primal_step * (tail_weight - risk), 0.0)
    excess_bar = 2.0 * excess_new - excess
    excess_out[...] = excess_new
    risk_new = jnp.maximum(risk + risk_step * (losses - excess_bar - level_bar[:1]), 0.0)
    risk_out[...] = risk_new
    sum_out[...] = jnp.broadcast_to(jnp.sum(risk_new, axis=0, keepdims=True), sum_out.shape)


def local_forward_kernel(
    touches,
    group,
    steps,
    index_ref,
    bar_ref,
    blocks_ref,
    duals_ref,
    demand_ref,
    out_ref,
    total,
):
    rows = blocks_ref.shape[-1]
    step = pl.program_id(0)
    first = step * group

    @pl.when(step == 0)
    def _():
        total[...] = jnp.zeros_like(total)

    for member in range(group):
        right = jnp.concatenate([blocks_ref[member, k] for k in range(touches)], axis=1)
        products = jnp.dot(
            bar_ref[:, member * rows : (member + 1) * rows],
            right,
            preferred_element_type=jnp.float32,
        )
        for k in range(touches):
            place = index_ref[first + member, k]
            total[place] += products[:, k * rows : (k + 1) * rows]

    @pl.when(step == steps - 1)
    def _():
        out_ref[...] = duals_ref[...] + dual_step * (demand_ref[...] - total[...])


def whole(*shape):
    return pl.BlockSpec(shape, lambda i, *_: (0,) * len(shape))


def vmem_limit(peers):
    return (8 + peers + peers // 4) * MIB


def params(peers=8):
    return pltpu.CompilerParams(
        dimension_semantics=("arbitrary",), vmem_limit_bytes=vmem_limit(peers)
    )


def local_adjoint(index, panel, blocks, after):
    arc_blks, touches, rows, _ = blocks.shape
    scen_rows = panel.shape[1]
    group = GROUP
    return pl.pallas_call(
        functools.partial(local_adjoint_kernel, touches, group),
        out_shape=jax.ShapeDtypeStruct((scen_rows, arc_blks * rows), jnp.float32),
        grid_spec=pltpu.PrefetchScalarGridSpec(
            num_scalar_prefetch=1,
            grid=(arc_blks // group,),
            in_specs=[
                whole(*panel.shape),
                pl.BlockSpec((group, touches, rows, rows), lambda i, *_: (i, 0, 0, 0)),
            ]
            + [pl.BlockSpec(memory_space=pl.ANY)] * len(after),
            out_specs=pl.BlockSpec((scen_rows, group * rows), lambda i, *_: (0, i)),
        ),
        compiler_params=params(),
        cost_estimate=pl.CostEstimate(
            flops=2 * scen_rows * blocks.size, bytes_accessed=2 * blocks.size, transcendentals=0
        ),
        name="local_adjoint",
    )(index, panel, blocks, *after)


def head_step(places, panels, heads, pulled, flows, costs, risk, sums):
    arc_blks, rows, _ = heads.shape
    scen_rows = flows.shape[0]
    peers = len(panels)
    node_blks = panels[0].shape[0]
    group = HEAD_GROUP
    steps = arc_blks // group
    kept = (node_blks, scen_rows, rows)
    sent = [kept] * (peers // 2)
    sent[-1] = (node_blks + 1, scen_rows, rows)
    arcs = pl.BlockSpec((scen_rows, group * rows), lambda i, *_: (0, i))
    results = pl.pallas_call(
        functools.partial(head_kernel, group, steps, peers),
        out_shape=[
            jax.ShapeDtypeStruct(flows.shape, jnp.float32),
            jax.ShapeDtypeStruct(flows.shape, jnp.bfloat16),
            jax.ShapeDtypeStruct(sums[0].shape, jnp.float32),
        ]
        + [jax.ShapeDtypeStruct(kept, jnp.float32)] * (peers // 2)
        + [jax.ShapeDtypeStruct(shape, jnp.bfloat16) for shape in sent],
        grid_spec=pltpu.PrefetchScalarGridSpec(
            num_scalar_prefetch=1,
            grid=(steps,),
            in_specs=[whole(*panels[0].shape)] * peers
            + [
                pl.BlockSpec((group, rows, rows), lambda i, *_: (i, 0, 0)),
                arcs,
                arcs,
                pl.BlockSpec((1, group * rows), lambda i, *_: (0, i)),
                whole(scen_rows, rows),
                whole(*sums[0].shape),
                whole(*sums[0].shape),
            ],
            out_specs=[arcs, arcs, whole(*sums[0].shape)]
            + [whole(*kept)] * (peers // 2)
            + [whole(*shape) for shape in sent],
            scratch_shapes=[
                pltpu.VMEM((peers * node_blks, scen_rows, rows), jnp.bfloat16),
                pltpu.VMEM((peers * node_blks, scen_rows, rows), jnp.float32),
                pltpu.VMEM((scen_rows, group * rows), jnp.float32),
                pltpu.VMEM((scen_rows, rows), jnp.float32),
            ],
        ),
        compiler_params=params(peers),
        cost_estimate=pl.CostEstimate(
            flops=4 * scen_rows * heads.size,
            bytes_accessed=2 * heads.size + 14 * flows.size + 4 * peers * panels[0].size,
            transcendentals=0,
        ),
        name="head_step",
    )(places, *panels, heads, pulled, flows, costs, risk, *sums)
    half = peers // 2
    kept = dict(zip(inner(peers), results[3 : 3 + half]))
    sends = dict(zip(leaves(peers), results[3 + half :]))
    return *results[:3], kept, sends


def small_cost(*arrays):
    size = sum(a.size for a in arrays)
    return pl.CostEstimate(flops=size, bytes_accessed=2 * size, transcendentals=0)


def fold(kept, arrived, loss, extras, after):
    node_blks, scen_rows, rows = kept.shape
    with_loss = loss is not None
    operands = [kept, *arrived] + ([loss] if with_loss else []) + list(extras)
    vmem = pl.BlockSpec(memory_space=pltpu.VMEM)
    out_shape = [jax.ShapeDtypeStruct((node_blks + with_loss, scen_rows, rows), jnp.bfloat16)]
    out_shape += [jax.ShapeDtypeStruct(extra.shape, extra.dtype) for extra in extras]
    results = pl.pallas_call(
        functools.partial(fold_kernel, len(arrived), with_loss, len(extras), len(after)),
        out_shape=out_shape,
        in_specs=[vmem] * len(operands) + [pl.BlockSpec(memory_space=pl.ANY)] * len(after),
        out_specs=[vmem] * len(out_shape),
        compiler_params=pltpu.CompilerParams(vmem_limit_bytes=vmem_limit(8)),
        cost_estimate=small_cost(*operands),
        name="fold",
    )(*operands, *after)
    return results[0], results[1:]


def settle(kept, arrived, loss, base, risk, excess, level, sums, arc_total, scen_total, last):
    node_blks, scen_rows, rows = base.shape
    duals = (scen_rows, node_blks * rows) if last else base.shape
    return pl.pallas_call(
        functools.partial(settle_kernel, len(arrived), arc_total, scen_total, last),
        out_shape=(
            jax.ShapeDtypeStruct(duals, jnp.float32),
            jax.ShapeDtypeStruct(base.shape, jnp.bfloat16),
            jax.ShapeDtypeStruct(risk.shape, jnp.float32),
            jax.ShapeDtypeStruct(risk.shape, jnp.float32),
            jax.ShapeDtypeStruct(level.shape, jnp.float32),
            jax.ShapeDtypeStruct(level.shape, jnp.float32),
        ),
        compiler_params=pltpu.CompilerParams(vmem_limit_bytes=vmem_limit(8)),
        cost_estimate=small_cost(kept, *arrived, base),
        name="settle",
    )(kept, *arrived, loss, base, risk, excess, level, *sums)


def local_forward(index, bar, blocks, duals, demand):
    arc_blks, touches, rows, _ = blocks.shape
    scen_rows = bar.shape[0]
    group = GROUP
    steps = arc_blks // group
    return pl.pallas_call(
        functools.partial(local_forward_kernel, touches, group, steps),
        out_shape=jax.ShapeDtypeStruct(duals.shape, jnp.float32),
        grid_spec=pltpu.PrefetchScalarGridSpec(
            num_scalar_prefetch=1,
            grid=(steps,),
            in_specs=[
                pl.BlockSpec((scen_rows, group * rows), lambda i, *_: (0, i)),
                pl.BlockSpec((group, touches, rows, rows), lambda i, *_: (i, 0, 0, 0)),
                whole(*duals.shape),
                whole(*duals.shape),
            ],
            out_specs=whole(*duals.shape),
            scratch_shapes=[pltpu.VMEM(duals.shape, jnp.float32)],
        ),
        compiler_params=params(),
        cost_estimate=pl.CostEstimate(
            flops=2 * scen_rows * blocks.size, bytes_accessed=2 * blocks.size, transcendentals=0
        ),
        name="local_forward",
    )(index, bar, blocks, duals, demand)


def relay(arrived, risk_sum, after):
    def kernel(arrived_ref, sum_ref, *refs):
        arrived_out, sum_out = refs[-2:]
        arrived_out[...] = arrived_ref[...]
        sum_out[...] = sum_ref[...]

    vmem = pl.BlockSpec(memory_space=pltpu.VMEM)
    return pl.pallas_call(
        kernel,
        out_shape=(
            jax.ShapeDtypeStruct(arrived.shape, arrived.dtype),
            jax.ShapeDtypeStruct(risk_sum.shape, risk_sum.dtype),
        ),
        in_specs=[vmem, vmem] + [pl.BlockSpec(memory_space=pl.ANY)] * len(after),
        out_specs=(vmem, vmem),
        compiler_params=pltpu.CompilerParams(vmem_limit_bytes=vmem_limit(8)),
        cost_estimate=small_cost(arrived),
        name="relay",
    )(arrived, risk_sum, *after)


def sum_rows(values, shape):
    def kernel(values_ref, out_ref):
        out_ref[...] = jnp.broadcast_to(jnp.sum(values_ref[...], axis=0, keepdims=True), shape)

    return pl.pallas_call(
        kernel,
        out_shape=jax.ShapeDtypeStruct(shape, jnp.float32),
        compiler_params=pltpu.CompilerParams(vmem_limit_bytes=vmem_limit(8)),
        cost_estimate=small_cost(values),
        name="sum_rows",
    )(values)


def swap(value, axis, distance):
    size = lax.axis_size(axis)
    return lax.ppermute(value, axis, [(i, i ^ distance) for i in range(size)])


def gather_panels(own, risk_sum, after):
    peers = lax.axis_size("net")
    panels = [own] + [None] * (peers - 1)
    for distance in sorted(range(1, peers), key=lambda k: (k.bit_count(), -k)):
        hop = last_hop(distance)
        panels[distance] = swap(panels[distance ^ hop], "net", hop)
        if distance == peers // 2:
            panels[distance], risk_sum = relay(panels[distance], risk_sum, after)
    return panels, risk_sum


def per_device(
    arc_flows,
    node_duals,
    demand,
    excess,
    risk_duals,
    threshold,
    arc_costs,
    local_blocks,
    head_blocks,
    local_index,
    head_index,
):
    rows = local_blocks.shape[-1]
    scen_rows = arc_flows.shape[0]
    node_blks = node_duals.shape[1] // rows
    net_size = lax.axis_size("net")
    arc_total = arc_flows.shape[1] * net_size
    scen_total = scen_rows * lax.axis_size("scen")
    costs = arc_costs.reshape(1, -1)
    distance = jnp.bitwise_xor(head_index // node_blks, lax.axis_index("net"))
    places = distance * node_blks + head_index % node_blks
    scen_size = lax.axis_size("scen")
    wide = (scen_rows, rows)
    flat = (8, rows)

    def to_blocks(panel):
        return panel.reshape(scen_rows, node_blks, rows).transpose(1, 0, 2)

    duals = to_blocks(node_duals)
    half = duals.astype(jnp.bfloat16)
    wanted = to_blocks(demand)
    flows = arc_flows
    excess_now = jnp.broadcast_to(excess[:, None], wide)
    risk = jnp.broadcast_to(risk_duals[:, None], wide)
    level = jnp.broadcast_to(threshold[:, None], flat)
    risk_sum = sum_rows(risk, flat)
    for iteration in range(ROUNDS):
        pulled = local_adjoint(local_index, half, local_blocks, ())
        panels, risk_sum = gather_panels(half, risk_sum, (pulled,))
        sums = (risk_sum, swap(risk_sum, "scen", 1))
        flows, bar, risk_sum, kept, sends = head_step(
            places, panels, head_blocks, pulled, flows, costs, risk, sums
        )
        base = local_forward(local_index, bar, local_blocks, duals, wanted)
        tops = sorted(inner(net_size), key=lambda k: (-k.bit_count(), -k))[:-1]
        loss = sends[net_size - 1]
        arrived = {}
        for top in tops:
            below = sorted(children(top, net_size))
            for k in below:
                arrived[k] = swap(sends[k], "net", last_hop(k))
            chain = net_size - 1 in below or loss_top in below
            after = (base,) if top == tops[0] else ()
            extras = (risk_sum,) if top == net_size // 2 else ()
            sends[top], passed = fold(
                kept[top], [arrived[k] for k in below], loss if chain else None, extras, after
            )
            if chain:
                loss_top, loss = top, sends[top]
            if extras:
                (risk_sum,) = passed
        below = sorted(children(0, net_size))
        arrived = [swap(sends[k], "net", last_hop(k)) for k in below]
        stride = 2
        while 2 * stride < scen_size:
            risk_sum = risk_sum + swap(risk_sum, "scen", stride)
            stride *= 2
        sums = (risk_sum, swap(risk_sum, "scen", stride))
        duals, half, risk, excess_now, level, risk_sum = settle(
            kept[0],
            arrived,
            loss,
            base,
            risk,
            excess_now,
            level,
            sums,
            arc_total,
            scen_total,
            iteration == ROUNDS - 1,
        )
    return (flows, duals, excess_now[:, 0], risk[:, 0], level[0, :1])


def solution(mesh):
    placed = (
        P("scen", "net"),
        P("scen", "net"),
        P("scen", "net"),
        P("scen"),
        P("scen"),
        P(),
        P("net"),
        P("net", None, None, None),
        P("net", None, None),
        P("net", None),
        P("net"),
    )
    return jax.shard_map(
        per_device,
        mesh=mesh,
        in_specs=placed,
        out_specs=(P("scen", "net"), P("scen", "net"), P("scen"), P("scen"), P()),
        check_vma=False,
    )
```

time: 161 us -> 145 us (0.901)
  waiting for transfers between devices: 62.5 us -> 48.5 us
  Pallas kernels: 35.5 us -> 38.9 us
  starting transfers between devices: 50.1 us -> 47.6 us
  local copies, waits for them, and re-layouts: 10 us -> 8.32 us
    ppermute x42 -> x48, waiting for transfers between devices: 62.5 us -> 48.5 us  [swap(): return lax.ppermute(value, axis, [(i, i ^ distance) for i in range(size)])]
    ppermute x42 -> x48, starting transfers between devices: 50.1 us -> 47.6 us  [swap(): return lax.ppermute(value, axis, [(i, i ^ distance) for i in range(size)])]
    unnamed x23 -> x19, local copies, waits for them, and re-layouts: 7.92 us -> 6.33 us
  transfers between devices with their start and end apart: 42 -> 48, of which waited for: 23 -> 33; matrix products, arithmetic and copies ran while one was open for 2% -> 1% of each run, Pallas kernels for 14% -> 18%
where the time goes in v3:
time: 145 us
  waiting for transfers between devices  48.5 us (33%)
  starting transfers between devices  47.6 us (33%)
  Pallas kernels  38.9 us (27%)
  local copies, waits for them, and re-layouts  8.32 us (6%)
  between operations  1.55 us (1%)
    ppermute x48, waiting for transfers between devices, swap(): return lax.ppermute(value, axis, [(i, i ^ distance) for i in range(size)])  48.5 us
    ppermute x48, starting transfers between devices, swap(): return lax.ppermute(value, axis, [(i, i ^ distance) for i in range(size)])  47.6 us
    pallas_call x3, Pallas kernels, local_adjoint(): pl.pallas_call(functools.partial(local_adjoint_kernel, touches, group), o...  14.4 us
    pallas_call x3, Pallas kernels, local_forward(): pl.pallas_call(functools.partial(local_forward_kernel, touches, group, st...  11.4 us
    pallas_call x3, Pallas kernels, head_step(): pl.pallas_call(functools.partial(head_kernel, group, steps, peers), out_s...  11.1 us
    unnamed x19, local copies, waits for them, and re-layouts  6.33 us
  transfers between devices with their start and end apart: 48, of which 33 were waited for; matrix products, arithmetic and copies ran while one was open for 1% of the time, Pallas kernels for 18%

profile of v3, /device:TPU:0, one launch (start us, length us, event | category | flops | bytes accessed | tf_op | source)
XLA Modules:
  0.0 144.8 jit_solution(7194831230435309817)
XLA Ops:
  0.7 0.9 copy-done
  1.6 4.1 %collective-permute-start.3 = (bf16[16,32,128]{2,1,0:T(8,128)(2,1)S(1)}, bf16[16,32,128]{2,1,0:T(8,128)(2,1)S(1)}, u32[]{:S(2)}, u32[]{:S(2)}) collective-permute-start(bf16[16,32,128]{2,1,0:T(8,128)(2,1)S(1)} %fusion.1.panel_ref.refs_0_), channel_id=1, source_target_pairs={{0,16},{4,20},{8,24},{12,28},{16,0},{20,4},{24,8},{28,12},{1,17},{... | collective-permute-start | bytes 393224 | tf_op jit(solution)/shard_map/ppermute | solution.py:420
  5.7 1.6 %collective-permute-start.1 = (bf16[16,32,128]{2,1,0:T(8,128)(2,1)S(1)}, bf16[16,32,128]{2,1,0:T(8,128)(2,1)S(1)}, u32[]{:S(2)}, u32[]{:S(2)}) collective-permute-start(bf16[16,32,128]{2,1,0:T(8,128)(2,1)S(1)} %fusion.1.panel_ref.refs_0_), channel_id=1, source_target_pairs={{0,8},{4,12},{8,0},{12,4},{16,24},{20,28},{24,16},{28,20},{1,9},{5... | collective-permute-start | bytes 393224 | tf_op jit(solution)/shard_map/ppermute | solution.py:420
  7.3 1.5 %collective-permute-start = (bf16[16,32,128]{2,1,0:T(8,128)(2,1)S(1)}, bf16[16,32,128]{2,1,0:T(8,128)(2,1)S(1)}, u32[]{:S(2)}, u32[]{:S(2)}) collective-permute-start(bf16[16,32,128]{2,1,0:T(8,128)(2,1)S(1)} %fusion.1.panel_ref.refs_0_), channel_id=1, source_target_pairs={{0,4},{4,0},{8,12},{12,8},{16,20},{20,16},{24,28},{28,24},{1,5},{5... | collective-permute-start | bytes 393224 | tf_op jit(solution)/shard_map/ppermute | solution.py:420
  10.3 3.4 %copy-done.1 = bf16[64,4,128,128]{3,2,1,0:T(8,128)(2,1)S(1)} copy-done((bf16[64,4,128,128]{3,2,1,0:T(8,128)(2,1)S(1)}, bf16[64,4,128,128]{3,2,1,0:T(8,128)(2,1)}, u32[]{:S(2)}) %copy-start.1) | copy-done | bytes 8388632
  13.7 4.8 %local_adjoint.3.refs_0_.refs_9_ = f32[32,8192]{1,0:T(8,128)S(1)} custom-call(s32[64,4]{1,0:T(8,128)S(1)} %copy.23.index_ref, bf16[16,32,128]{2,1,0:T(8,128)(2,1)S(1)} %fusion.1.panel_ref.refs_0_, bf16[64,4,128,128]{3,2,1,0:T(8,128)(2,1)S(1)} %copy-done.1), custom_call_target="tpu_custom_call" | custom-call | flops 268435456 | bytes 8388608 | tf_op jit(solution)/shard_map/local_adjoint/pallas_call | solution.py:235
  19.7 1.6 %collective-permute-start.2 = (bf16[16,32,128]{2,1,0:T(8,128)(2,1)S(1)}, bf16[16,32,128]{2,1,0:T(8,128)(2,1)S(1)}, u32[]{:S(2)}, u32[]{:S(2)}) collective-permute-start(bf16[16,32,128]{2,1,0:T(8,128)(2,1)S(1)} %collective-permute-done.refs_1_), channel_id=1, source_target_pairs={{0,8},{4,12},{8,0},{12,4},{16,24},{20,28},{24,16},{28,20},{1,9},{5... | collective-permute-start | bytes 393224 | tf_op jit(solution)/shard_map/ppermute | solution.py:420
  21.2 3.1 %collective-permute-done.5.refs_6_ = bf16[16,32,128]{2,1,0:T(8,128)(2,1)S(1)} collective-permute-done((bf16[16,32,128]{2,1,0:T(8,128)(2,1)S(1)}, bf16[16,32,128]{2,1,0:T(8,128)(2,1)S(1)}, u32[]{:S(2)}, u32[]{:S(2)}) %collective-permute-start.5) | collective-permute-done | bytes 131104 | tf_op jit(solution)/shard_map/ppermute | solution.py:420
  24.4 1.9 %collective-permute-done.2.refs_3_ = bf16[16,32,128]{2,1,0:T(8,128)(2,1)S(1)} collective-permute-done((bf16[16,32,128]{2,1,0:T(8,128)(2,1)S(1)}, bf16[16,32,128]{2,1,0:T(8,128)(2,1)S(1)}, u32[]{:S(2)}, u32[]{:S(2)}) %collective-permute-start.2) | collective-permute-done | bytes 131104 | tf_op jit(solution)/shard_map/ppermute | solution.py:420
  26.3 3.0 %collective-permute-done.6.refs_7_ = bf16[16,32,128]{2,1,0:T(8,128)(2,1)S(1)} collective-permute-done((bf16[16,32,128]{2,1,0:T(8,128)(2,1)S(1)}, bf16[16,32,128]{2,1,0:T(8,128)(2,1)S(1)}, u32[]{:S(2)}, u32[]{:S(2)}) %collective-permute-start.6) | collective-permute-done | bytes 131104 | tf_op jit(solution)/shard_map/ppermute | solution.py:420
  29.3 1.2 copy-done.4
  30.6 3.5 %head_step.3 = (f32[32,8192]{1,0:T(8,128)S(1)}, bf16[32,8192]{1,0:T(8,128)(2,1)S(1)}, f32[8,128]{1,0:T(8,128)S(1)}, f32[16,32,128]{2,1,0:T(8,128)S(1)}, f32[16,3...) custom-call(s32[64]{0:T(128)S(1)} %fusion.index_ref, ...), custom_call_target="tpu_custom_call" | custom-call | flops 134217728 | bytes 7864320 | tf_op jit(solution)/shard_map/head_step/pallas_call | solution.py:267
  34.2 3.8 %local_forward.3.refs_3_.refs_5_ = f32[16,32,128]{2,1,0:T(8,128)S(1)} custom-call(s32[64,4]{1,0:T(8,128)S(1)} %copy.23.index_ref, bf16[32,8192]{1,0:T(8,128)(2,1)S(1)} %get-tuple-element.76.bar_ref, bf16[64,4,128,128]{3,2,1,0:T(8,128)(2,1)S(1)} %copy-done.2, f32[16,32,128]{2,1,0:T(8,128)S(1)} %bitcast_bitcast_fusion.1.duals_ref, ...), custom_call_target="tpu_custom_call" | custom-call | flops 268435456 | bytes 8388608 | tf_op jit(solution)/shard_map/local_forward/pallas_call | solution.py:361
  38.0 1.2 collective-permute-done.12.refs_1_
  39.4 0.9 collective-permute-start.11
  40.2 1.9 %collective-permute-start.8 = (bf16[16,32,128]{2,1,0:T(8,128)(2,1)S(1)}, bf16[16,32,128]{2,1,0:T(8,128)(2,1)S(1)}, u32[]{:S(2)}, u32[]{:S(2)}) collective-permute-start(bf16[16,32,128]{2,1,0:T(8,128)(2,1)S(1)} %get-tuple-element.70), channel_id=1, source_target_pairs={{0,8},{4,12},{8,0},{12,4},{16,24},{20,28},{24,16},{28,20},{1,9},{5... | collective-permute-start | bytes 393224 | tf_op jit(solution)/shard_map/ppermute | solution.py:420
  42.2 2.8 %collective-permute-done.11.refs_1_ = bf16[16,32,128]{2,1,0:T(8,128)(2,1)S(1)} collective-permute-done((bf16[16,32,128]{2,1,0:T(8,128)(2,1)S(1)}, bf16[16,32,128]{2,1,0:T(8,128)(2,1)S(1)}, u32[]{:S(2)}, u32[]{:S(2)}) %collective-permute-start.11) | collective-permute-done | bytes 131104 | tf_op jit(solution)/shard_map/ppermute | solution.py:420
  45.0 2.0 %collective-permute-done.13.refs_2_ = bf16[17,32,128]{2,1,0:T(8,128)(2,1)S(1)} collective-permute-done((bf16[17,32,128]{2,1,0:T(8,128)(2,1)S(1)}, bf16[17,32,128]{2,1,0:T(8,128)(2,1)S(1)}, u32[]{:S(2)}, u32[]{:S(2)}) %collective-permute-start.13) | collective-permute-done | bytes 139296 | tf_op jit(solution)/shard_map/ppermute | solution.py:420
  47.7 1.0 collective-permute-done.8.refs_1_
  48.7 0.9 collective-permute-start.9
  49.6 1.5 %collective-permute-start.15 = (f32[8,128]{1,0:T(8,128)S(1)}, f32[8,128]{1,0:T(8,128)S(1)}, u32[]{:S(2)}, u32[]{:S(2)}) collective-permute-start(f32[8,128]{1,0:T(8,128)S(1)} %get-tuple-element.79.refs_9_), channel_id=1, source_target_pairs={{0,2},{1,3},{2,0},{3,1},{4,6},{5,7},{6,4},{7,5},{8,10},{9,11},{10,... | collective-permute-start | bytes 12296 | tf_op jit(solution)/shard_map/ppermute | solution.py:420
  52.6 2.1 %collective-permute-done.9.refs_1_ = bf16[16,32,128]{2,1,0:T(8,128)(2,1)S(1)} collective-permute-done((bf16[16,32,128]{2,1,0:T(8,128)(2,1)S(1)}, bf16[16,32,128]{2,1,0:T(8,128)(2,1)S(1)}, u32[]{:S(2)}, u32[]{:S(2)}) %collective-permute-start.9) | collective-permute-done | bytes 131104 | tf_op jit(solution)/shard_map/ppermute | solution.py:420
  54.6 2.7 %collective-permute-done.14.refs_3_ = bf16[17,32,128]{2,1,0:T(8,128)(2,1)S(1)} collective-permute-done((bf16[17,32,128]{2,1,0:T(8,128)(2,1)S(1)}, bf16[17,32,128]{2,1,0:T(8,128)(2,1)S(1)}, u32[]{:S(2)}, u32[]{:S(2)}) %collective-permute-start.14) | collective-permute-done | bytes 139296 | tf_op jit(solution)/shard_map/ppermute | solution.py:420
  57.6 0.8 collective-permute-start.16
  58.4 4.8 %local_adjoint.4.refs_0_.refs_9_ = f32[32,8192]{1,0:T(8,128)S(1)} custom-call(s32[64,4]{1,0:T(8,128)S(1)} %copy.23.index_ref, bf16[16,32,128]{2,1,0:T(8,128)(2,1)S(1)} %get-tuple-element.80.panel_ref.refs_0_, bf16[64,4,128,128]{3,2,1,0:T(8,128)(2,1)S(1)} %copy-done.2), custom_call_target="tpu_custom_call" | custom-call | flops 268435456 | bytes 8388608 | tf_op jit(solution)/shard_map/local_adjoint/pallas_call | solution.py:235
  63.7 2.0 %collective-permute-start.17 = (bf16[16,32,128]{2,1,0:T(8,128)(2,1)S(1)}, bf16[16,32,128]{2,1,0:T(8,128)(2,1)S(1)}, u32[]{:S(2)}, u32[]{:S(2)}) collective-permute-start(bf16[16,32,128]{2,1,0:T(8,128)(2,1)S(1)} %get-tuple-element.80.panel_ref.refs_0_), channel_id=1, source_target_pairs={{0,8},{4,12},{8,0},{12,4},{16,24},{20,28},{24,16},{28,20},{1,9},{5... | collective-permute-start | bytes 393224 | tf_op jit(solution)/shard_map/ppermute | solution.py:420
  65.7 0.9 collective-permute-start.20
  66.7 1.9 %collective-permute-done.21.refs_6_ = bf16[16,32,128]{2,1,0:T(8,128)(2,1)S(1)} collective-permute-done((bf16[16,32,128]{2,1,0:T(8,128)(2,1)S(1)}, bf16[16,32,128]{2,1,0:T(8,128)(2,1)S(1)}, u32[]{:S(2)}, u32[]{:S(2)}) %collective-permute-start.21) | collective-permute-done | bytes 131104 | tf_op jit(solution)/shard_map/ppermute | solution.py:420
  68.6 0.9 collective-permute-start.22
  70.7 0.9 collective-permute-done.18.refs_3_
  71.6 2.0 %collective-permute-done.22.refs_7_ = bf16[16,32,128]{2,1,0:T(8,128)(2,1)S(1)} collective-permute-done((bf16[16,32,128]{2,1,0:T(8,128)(2,1)S(1)}, bf16[16,32,128]{2,1,0:T(8,128)(2,1)S(1)}, u32[]{:S(2)}, u32[]{:S(2)}) %collective-permute-start.22) | collective-permute-done | bytes 131104 | tf_op jit(solution)/shard_map/ppermute | solution.py:420
  73.6 3.5 %head_step.4 = (f32[32,8192]{1,0:T(8,128)S(1)}, bf16[32,8192]{1,0:T(8,128)(2,1)S(1)}, f32[8,128]{1,0:T(8,128)S(1)}, f32[16,32,128]{2,1,0:T(8,128)S(1)}, f32[16,3...) custom-call(s32[64]{0:T(128)S(1)} %fusion.index_ref, ...), custom_call_target="tpu_custom_call" | custom-call | flops 134217728 | bytes 7864320 | tf_op jit(solution)/shard_map/head_step/pallas_call | solution.py:267
  77.1 1.0 collective-permute-start.28
  78.1 3.8 %local_forward.4.refs_3_.refs_5_ = f32[16,32,128]{2,1,0:T(8,128)S(1)} custom-call(s32[64,4]{1,0:T(8,128)S(1)} %copy.23.index_ref, bf16[32,8192]{1,0:T(8,128)(2,1)S(1)} %get-tuple-element.94.bar_ref, bf16[64,4,128,128]{3,2,1,0:T(8,128)(2,1)S(1)} %copy-done.2, f32[16,32,128]{2,1,0:T(8,128)S(1)} %get-tuple-element.95.duals_ref, ...), custom_call_target="tpu_custom_call" | custom-call | flops 268435456 | bytes 8388608 | tf_op jit(solution)/shard_map/local_forward/pallas_call | solution.py:361
  82.6 1.0 collective-permute-start.27
  83.6 1.9 %collective-permute-start.24 = (bf16[16,32,128]{2,1,0:T(8,128)(2,1)S(1)}, bf16[16,32,128]{2,1,0:T(8,128)(2,1)S(1)}, u32[]{:S(2)}, u32[]{:S(2)}) collective-permute-start(bf16[16,32,128]{2,1,0:T(8,128)(2,1)S(1)} %get-tuple-element.88), channel_id=1, source_target_pairs={{0,8},{4,12},{8,0},{12,4},{16,24},{20,28},{24,16},{28,20},{1,9},{5... | collective-permute-start | bytes 393224 | tf_op jit(solution)/shard_map/ppermute | solution.py:420
  85.5 2.1 %collective-permute-done.27.refs_1_ = bf16[16,32,128]{2,1,0:T(8,128)(2,1)S(1)} collective-permute-done((bf16[16,32,128]{2,1,0:T(8,128)(2,1)S(1)}, bf16[16,32,128]{2,1,0:T(8,128)(2,1)S(1)}, u32[]{:S(2)}, u32[]{:S(2)}) %collective-permute-start.27) | collective-permute-done | bytes 131104 | tf_op jit(solution)/shard_map/ppermute | solution.py:420
  87.6 1.6 %collective-permute-done.29.refs_2_ = bf16[17,32,128]{2,1,0:T(8,128)(2,1)S(1)} collective-permute-done((bf16[17,32,128]{2,1,0:T(8,128)(2,1)S(1)}, bf16[17,32,128]{2,1,0:T(8,128)(2,1)S(1)}, u32[]{:S(2)}, u32[]{:S(2)}) %collective-permute-start.29) | collective-permute-done | bytes 139296 | tf_op jit(solution)/shard_map/ppermute | solution.py:420
  89.4 2.4 %collective-permute-start.30 = (bf16[17,32,128]{2,1,0:T(8,128)(2,1)S(1)}, bf16[17,32,128]{2,1,0:T(8,128)(2,1)S(1)}, u32[]{:S(2)}, u32[]{:S(2)}) collective-permute-start(bf16[17,32,128]{2,1,0:T(8,128)(2,1)S(1)} %get-tuple-element.97.refs_4_), channel_id=1, source_target_pairs={{0,16},{4,20},{8,24},{12,28},{16,0},{20,4},{24,8},{28,12},{1,17},{... | collective-permute-start | bytes 417800 | tf_op jit(solution)/shard_map/ppermute | solution.py:420
  91.8 1.5 %collective-permute-start.26 = (bf16[16,32,128]{2,1,0:T(8,128)(2,1)S(1)}, bf16[16,32,128]{2,1,0:T(8,128)(2,1)S(1)}, u32[]{:S(2)}, u32[]{:S(2)}) collective-permute-start(bf16[16,32,128]{2,1,0:T(8,128)(2,1)S(1)} %get-tuple-element.89), channel_id=1, source_target_pairs={{0,8},{4,12},{8,0},{12,4},{16,24},{20,28},{24,16},{28,20},{1,9},{5... | collective-permute-start | bytes 393224 | tf_op jit(solution)/shard_map/ppermute | solution.py:420
  93.4 1.6 %collective-permute-start.25 = (bf16[16,32,128]{2,1,0:T(8,128)(2,1)S(1)}, bf16[16,32,128]{2,1,0:T(8,128)(2,1)S(1)}, u32[]{:S(2)}, u32[]{:S(2)}) collective-permute-start(bf16[16,32,128]{2,1,0:T(8,128)(2,1)S(1)} %fold.12), channel_id=1, source_target_pairs={{0,4},{4,0},{8,12},{12,8},{16,20},{20,16},{24,28},{28,24},{1,5},{5... | collective-permute-start | bytes 393224 | tf_op jit(solution)/shard_map/ppermute | solution.py:420
  95.0 1.5 %collective-permute-start.31 = (f32[8,128]{1,0:T(8,128)S(1)}, f32[8,128]{1,0:T(8,128)S(1)}, u32[]{:S(2)}, u32[]{:S(2)}) collective-permute-start(f32[8,128]{1,0:T(8,128)S(1)} %get-tuple-element.100.refs_9_), channel_id=1, source_target_pairs={{0,2},{1,3},{2,0},{3,1},{4,6},{5,7},{6,4},{7,5},{8,10},{9,11},{10,... | collective-permute-start | bytes 12296 | tf_op jit(solution)/shard_map/ppermute | solution.py:420
  96.5 1.4 collective-permute-done.26.refs_2_
  97.8 1.8 %collective-permute-done.25.refs_1_ = bf16[16,32,128]{2,1,0:T(8,128)(2,1)S(1)} collective-permute-done((bf16[16,32,128]{2,1,0:T(8,128)(2,1)S(1)}, bf16[16,32,128]{2,1,0:T(8,128)(2,1)S(1)}, u32[]{:S(2)}, u32[]{:S(2)}) %collective-permute-start.25) | collective-permute-done | bytes 131104 | tf_op jit(solution)/shard_map/ppermute | solution.py:420
  100.5 0.9 collective-permute-start.32
  101.3 4.8 %local_adjoint.5.refs_0_.refs_9_ = f32[32,8192]{1,0:T(8,128)S(1)} custom-call(s32[64,4]{1,0:T(8,128)S(1)} %copy.23.index_ref, bf16[16,32,128]{2,1,0:T(8,128)(2,1)S(1)} %get-tuple-element.101.panel_ref.refs_0_, bf16[64,4,128,128]{3,2,1,0:T(8,128)(2,1)S(1)} %copy-done.2), custom_call_target="tpu_custom_call" | custom-call | flops 268435456 | bytes 8388608 | tf_op jit(solution)/shard_map/local_adjoint/pallas_call | solution.py:235
  106.9 2.9 %collective-permute-start.37 = (bf16[16,32,128]{2,1,0:T(8,128)(2,1)S(1)}, bf16[16,32,128]{2,1,0:T(8,128)(2,1)S(1)}, u32[]{:S(2)}, u32[]{:S(2)}) collective-permute-start(bf16[16,32,128]{2,1,0:T(8,128)(2,1)S(1)} %get-tuple-element.103.refs_4_), channel_id=1, source_target_pairs={{0,8},{4,12},{8,0},{12,4},{16,24},{20,28},{24,16},{28,20},{1,9},{5... | collective-permute-start | bytes 393224 | tf_op jit(solution)/shard_map/ppermute | solution.py:420
  110.6 1.9 %collective-permute-start.34 = (bf16[16,32,128]{2,1,0:T(8,128)(2,1)S(1)}, bf16[16,32,128]{2,1,0:T(8,128)(2,1)S(1)}, u32[]{:S(2)}, u32[]{:S(2)}) collective-permute-start(bf16[16,32,128]{2,1,0:T(8,128)(2,1)S(1)} %collective-permute-done.32.refs_1_), channel_id=1, source_target_pairs={{0,8},{4,12},{8,0},{12,4},{16,24},{20,28},{24,16},{28,20},{1,9},{5... | collective-permute-start | bytes 393224 | tf_op jit(solution)/shard_map/ppermute | solution.py:420
  112.7 1.1 collective-permute-start.38
  113.8 0.9 collective-permute-done.33.refs_2_
  115.0 1.1 collective-permute-done.34.refs_3_
  116.1 1.5 %collective-permute-done.38.refs_7_ = bf16[16,32,128]{2,1,0:T(8,128)(2,1)S(1)} collective-permute-done((bf16[16,32,128]{2,1,0:T(8,128)(2,1)S(1)}, bf16[16,32,128]{2,1,0:T(8,128)(2,1)S(1)}, u32[]{:S(2)}, u32[]{:S(2)}) %collective-permute-start.38) | collective-permute-done | bytes 131104 | tf_op jit(solution)/shard_map/ppermute | solution.py:420
  117.7 4.1 %head_step.5 = (f32[32,8192]{1,0:T(8,128)}, bf16[32,8192]{1,0:T(8,128)(2,1)S(1)}, f32[8,128]{1,0:T(8,128)S(1)}, f32[16,32,128]{2,1,0:T(8,128)S(1)}, f32[16,32,12...) custom-call(s32[64]{0:T(128)S(1)} %fusion.index_ref, ...), custom_call_target="tpu_custom_call" | custom-call | flops 134217728 | bytes 7864320 | tf_op jit(solution)/shard_map/head_step/pallas_call | solution.py:267
  121.8 1.1 collective-permute-start.44
  122.9 3.8 %local_forward.5.refs_3_.refs_5_ = f32[16,32,128]{2,1,0:T(8,128)S(1)} custom-call(s32[64,4]{1,0:T(8,128)S(1)} %copy.23.index_ref, bf16[32,8192]{1,0:T(8,128)(2,1)S(1)} %get-tuple-element.116.bar_ref, bf16[64,4,128,128]{3,2,1,0:T(8,128)(2,1)S(1)} %copy-done.2, f32[16,32,128]{2,1,0:T(8,128)S(1)} %get-tuple-element.117.duals_ref, ...), custom_call_target="tpu_custom_call" | custom-call | flops 268435456 | bytes 8388608 | tf_op jit(solution)/shard_map/local_forward/pallas_call | solution.py:361
  127.0 2.3 %collective-permute-start.45 = (bf16[17,32,128]{2,1,0:T(8,128)(2,1)S(1)}, bf16[17,32,128]{2,1,0:T(8,128)(2,1)S(1)}, u32[]{:S(2)}, u32[]{:S(2)}) collective-permute-start(bf16[17,32,128]{2,1,0:T(8,128)(2,1)S(1)} %fold.16.refs_3_), channel_id=1, source_target_pairs={{0,8},{4,12},{8,0},{12,4},{16,24},{20,28},{24,16},{28,20},{1,9},{5... | collective-permute-start | bytes 417800 | tf_op jit(solution)/shard_map/ppermute | solution.py:420
  129.3 0.8 collective-permute-start.43
  130.2 5.4 %collective-permute-done.43.refs_1_ = bf16[16,32,128]{2,1,0:T(8,128)(2,1)S(1)} collective-permute-done((bf16[16,32,128]{2,1,0:T(8,128)(2,1)S(1)}, bf16[16,32,128]{2,1,0:T(8,128)(2,1)S(1)}, u32[]{:S(2)}, u32[]{:S(2)}) %collective-permute-start.43) | collective-permute-done | bytes 131104 | tf_op jit(solution)/shard_map/ppermute | solution.py:420
  136.8 1.1 collective-permute-start.41
  137.9 1.5 %collective-permute-start.47 = (f32[8,128]{1,0:T(8,128)S(1)}, f32[8,128]{1,0:T(8,128)S(1)}, u32[]{:S(2)}, u32[]{:S(2)}) collective-permute-start(f32[8,128]{1,0:T(8,128)S(1)} %get-tuple-element.122.refs_9_), channel_id=1, source_target_pairs={{0,2},{1,3},{2,0},{3,1},{4,6},{5,7},{6,4},{7,5},{8,10},{9,11},{10,... | collective-permute-start | bytes 12296 | tf_op jit(solution)/shard_map/ppermute | solution.py:420
  139.4 1.5 %collective-permute-done.42.refs_2_ = bf16[16,32,128]{2,1,0:T(8,128)(2,1)S(1)} collective-permute-done((bf16[16,32,128]{2,1,0:T(8,128)(2,1)S(1)}, bf16[16,32,128]{2,1,0:T(8,128)(2,1)S(1)}, u32[]{:S(2)}, u32[]{:S(2)}) %collective-permute-start.42) | collective-permute-done | bytes 131104 | tf_op jit(solution)/shard_map/ppermute | solution.py:420
  140.9 1.0 collective-permute-done.41.refs_1_
  141.8 1.0 collective-permute-done.46.refs_3_
  142.9 0.8 settle.5
  (85 shorter events, 12.9 us)
Async XLA Ops:
  0.6 1.0 copy-start
  0.6 23.7 %copy-start.8 = (s32[64]{0:T(128)S(1)}, s32[64]{0:T(128)}, u32[]{:S(2)}) copy-start(s32[64]{0:T(128)} %param.21) | copy-start | bytes 772
  0.7 28.7 %copy-start.5 = (f32[8192]{0:T(1024)S(1)}, f32[8192]{0:T(1024)}, u32[]{:S(2)}) copy-start(f32[8192]{0:T(1024)} %param.17) | copy-start | bytes 98308
  1.6 32.5 %copy-start.6 = (f32[32,2048]{1,0:T(8,128)S(1)}, f32[32,2048]{1,0:T(8,128)}, u32[]{:S(2)}) copy-start(f32[32,2048]{1,0:T(8,128)} %param.13) | copy-start | bytes 786436
  1.6 16.9 %collective-permute-start.3 = (bf16[16,32,128]{2,1,0:T(8,128)(2,1)S(1)}, bf16[16,32,128]{2,1,0:T(8,128)(2,1)S(1)}, u32[]{:S(2)}, u32[]{:S(2)}) collective-permute-start(bf16[16,32,128]{2,1,0:T(8,128)(2,1)S(1)} %fusion.1.panel_ref.refs_0_), channel_id=1, source_target_pairs={{0,16},{4,20},{8,24},{12,28},{16,0},{20,4},{24,8},{28,12},{1,17},{... | collective-permute-start | bytes 393224 | tf_op jit(solution)/shard_map/ppermute | solution.py:420
  5.7 18.7 %collective-permute-start.1 = (bf16[16,32,128]{2,1,0:T(8,128)(2,1)S(1)}, bf16[16,32,128]{2,1,0:T(8,128)(2,1)S(1)}, u32[]{:S(2)}, u32[]{:S(2)}) collective-permute-start(bf16[16,32,128]{2,1,0:T(8,128)(2,1)S(1)} %fusion.1.panel_ref.refs_0_), channel_id=1, source_target_pairs={{0,8},{4,12},{8,0},{12,4},{16,24},{20,28},{24,16},{28,20},{1,9},{5... | collective-permute-start | bytes 393224 | tf_op jit(solution)/shard_map/ppermute | solution.py:420
  7.3 12.4 %collective-permute-start = (bf16[16,32,128]{2,1,0:T(8,128)(2,1)S(1)}, bf16[16,32,128]{2,1,0:T(8,128)(2,1)S(1)}, u32[]{:S(2)}, u32[]{:S(2)}) collective-permute-start(bf16[16,32,128]{2,1,0:T(8,128)(2,1)S(1)} %fusion.1.panel_ref.refs_0_), channel_id=1, source_target_pairs={{0,4},{4,0},{8,12},{12,8},{16,20},{20,16},{24,28},{28,24},{1,5},{5... | collective-permute-start | bytes 393224 | tf_op jit(solution)/shard_map/ppermute | solution.py:420
  10.3 3.4 %copy-start.1 = (bf16[64,4,128,128]{3,2,1,0:T(8,128)(2,1)S(1)}, bf16[64,4,128,128]{3,2,1,0:T(8,128)(2,1)}, u32[]{:S(2)}) copy-start(bf16[64,4,128,128]{3,2,1,0:T(8,128)(2,1)} %blocks_ref.11) | copy-start | bytes 25165828
  13.7 15.7 %copy-start.3 = (bf16[64,128,128]{2,1,0:T(8,128)(2,1)S(1)}, bf16[64,128,128]{2,1,0:T(8,128)(2,1)}, u32[]{:S(2)}) copy-start(bf16[64,128,128]{2,1,0:T(8,128)(2,1)} %refs_8_.5) | copy-start | bytes 6291460
  13.7 20.5 %copy-start.2 = (bf16[64,4,128,128]{3,2,1,0:T(8,128)(2,1)S(1)}, bf16[64,4,128,128]{3,2,1,0:T(8,128)(2,1)}, u32[]{:S(2)}) copy-start(bf16[64,4,128,128]{3,2,1,0:T(8,128)(2,1)} %blocks_ref.11) | copy-start | bytes 25165828
  18.5 5.9 %collective-permute-start.5 = (bf16[16,32,128]{2,1,0:T(8,128)(2,1)S(1)}, bf16[16,32,128]{2,1,0:T(8,128)(2,1)S(1)}, u32[]{:S(2)}, u32[]{:S(2)}) collective-permute-start(bf16[16,32,128]{2,1,0:T(8,128)(2,1)S(1)} %get-tuple-element.66.refs_4_), channel_id=1, source_target_pairs={{0,8},{4,12},{8,0},{12,4},{16,24},{20,28},{24,16},{28,20},{1,9},{5... | collective-permute-start | bytes 393224 | tf_op jit(solution)/shard_map/ppermute | solution.py:420
  19.0 7.3 %collective-permute-start.4 = (bf16[16,32,128]{2,1,0:T(8,128)(2,1)S(1)}, bf16[16,32,128]{2,1,0:T(8,128)(2,1)S(1)}, u32[]{:S(2)}, u32[]{:S(2)}) collective-permute-start(bf16[16,32,128]{2,1,0:T(8,128)(2,1)S(1)} %get-tuple-element.66.refs_4_), channel_id=1, source_target_pairs={{0,4},{4,0},{8,12},{12,8},{16,20},{20,16},{24,28},{28,24},{1,5},{5... | collective-permute-start | bytes 393224 | tf_op jit(solution)/shard_map/ppermute | solution.py:420
  19.6 4.7 %collective-permute-start.7 = (f32[8,128]{1,0:T(8,128)S(1)}, f32[8,128]{1,0:T(8,128)S(1)}, u32[]{:S(2)}, u32[]{:S(2)}) collective-permute-start(f32[8,128]{1,0:T(8,128)S(1)} %get-tuple-element.67.refs_13_), channel_id=1, source_target_pairs={{0,1},{1,0},{2,3},{3,2},{4,5},{5,4},{6,7},{7,6},{8,9},{9,8},{10,11... | collective-permute-start | bytes 12296 | tf_op jit(solution)/shard_map/ppermute | solution.py:420
  19.7 6.7 %collective-permute-start.2 = (bf16[16,32,128]{2,1,0:T(8,128)(2,1)S(1)}, bf16[16,32,128]{2,1,0:T(8,128)(2,1)S(1)}, u32[]{:S(2)}, u32[]{:S(2)}) collective-permute-start(bf16[16,32,128]{2,1,0:T(8,128)(2,1)S(1)} %collective-permute-done.refs_1_), channel_id=1, source_target_pairs={{0,8},{4,12},{8,0},{12,4},{16,24},{20,28},{24,16},{28,20},{1,9},{5... | collective-permute-start | bytes 393224 | tf_op jit(solution)/shard_map/ppermute | solution.py:420
  24.4 5.0 %collective-permute-start.6 = (bf16[16,32,128]{2,1,0:T(8,128)(2,1)S(1)}, bf16[16,32,128]{2,1,0:T(8,128)(2,1)S(1)}, u32[]{:S(2)}, u32[]{:S(2)}) collective-permute-start(bf16[16,32,128]{2,1,0:T(8,128)(2,1)S(1)} %collective-permute-done.5.refs_6_), channel_id=1, source_target_pairs={{0,4},{4,0},{8,12},{12,8},{16,20},{20,16},{24,28},{28,24},{1,5},{5... | collective-permute-start | bytes 393224 | tf_op jit(solution)/shard_map/ppermute | solution.py:420
  29.3 1.2 copy-start.4
  30.6 26.7 %copy-start.7 = (f32[32]{0:T(128)S(1)}, f32[32]{0:T(128)}, u32[]{:S(2)}) copy-start(f32[32]{0:T(128)} %param.14) | copy-start | bytes 388
  34.0 5.1 %collective-permute-start.12 = (bf16[17,32,128]{2,1,0:T(8,128)(2,1)S(1)}, bf16[17,32,128]{2,1,0:T(8,128)(2,1)S(1)}, u32[]{:S(2)}, u32[]{:S(2)}) collective-permute-start(bf16[17,32,128]{2,1,0:T(8,128)(2,1)S(1)} %get-tuple-element.75.refs_2_), channel_id=1, source_target_pairs={{0,4},{4,0},{8,12},{12,8},{16,20},{20,16},{24,28},{28,24},{1,5},{5... | collective-permute-start | bytes 417800 | tf_op jit(solution)/shard_map/ppermute | solution.py:420
  39.3 7.7 %collective-permute-start.13 = (bf16[17,32,128]{2,1,0:T(8,128)(2,1)S(1)}, bf16[17,32,128]{2,1,0:T(8,128)(2,1)S(1)}, u32[]{:S(2)}, u32[]{:S(2)}) collective-permute-start(bf16[17,32,128]{2,1,0:T(8,128)(2,1)S(1)} %fold.10.refs_3_), channel_id=1, source_target_pairs={{0,8},{4,12},{8,0},{12,4},{16,24},{20,28},{24,16},{28,20},{1,9},{5... | collective-permute-start | bytes 417800 | tf_op jit(solution)/shard_map/ppermute | solution.py:420
  39.4 5.6 %collective-permute-start.11 = (bf16[16,32,128]{2,1,0:T(8,128)(2,1)S(1)}, bf16[16,32,128]{2,1,0:T(8,128)(2,1)S(1)}, u32[]{:S(2)}, u32[]{:S(2)}) collective-permute-start(bf16[16,32,128]{2,1,0:T(8,128)(2,1)S(1)} %get-tuple-element.73), channel_id=1, source_target_pairs={{0,4},{4,0},{8,12},{12,8},{16,20},{20,16},{24,28},{28,24},{1,5},{5... | collective-permute-start | bytes 393224 | tf_op jit(solution)/shard_map/ppermute | solution.py:420
  40.2 8.5 %collective-permute-start.8 = (bf16[16,32,128]{2,1,0:T(8,128)(2,1)S(1)}, bf16[16,32,128]{2,1,0:T(8,128)(2,1)S(1)}, u32[]{:S(2)}, u32[]{:S(2)}) collective-permute-start(bf16[16,32,128]{2,1,0:T(8,128)(2,1)S(1)} %get-tuple-element.70), channel_id=1, source_target_pairs={{0,8},{4,12},{8,0},{12,4},{16,24},{20,28},{24,16},{28,20},{1,9},{5... | collective-permute-start | bytes 393224 | tf_op jit(solution)/shard_map/ppermute | solution.py:420
  47.1 10.2 %collective-permute-start.14 = (bf16[17,32,128]{2,1,0:T(8,128)(2,1)S(1)}, bf16[17,32,128]{2,1,0:T(8,128)(2,1)S(1)}, u32[]{:S(2)}, u32[]{:S(2)}) collective-permute-start(bf16[17,32,128]{2,1,0:T(8,128)(2,1)S(1)} %get-tuple-element.78.refs_4_), channel_id=1, source_target_pairs={{0,16},{4,20},{8,24},{12,28},{16,0},{20,4},{24,8},{28,12},{1,17},{... | collective-permute-start | bytes 417800 | tf_op jit(solution)/shard_map/ppermute | solution.py:420
  47.1 5.4 %collective-permute-start.10 = (bf16[16,32,128]{2,1,0:T(8,128)(2,1)S(1)}, bf16[16,32,128]{2,1,0:T(8,128)(2,1)S(1)}, u32[]{:S(2)}, u32[]{:S(2)}) collective-permute-start(bf16[16,32,128]{2,1,0:T(8,128)(2,1)S(1)} %get-tuple-element.71), channel_id=1, source_target_pairs={{0,8},{4,12},{8,0},{12,4},{16,24},{20,28},{24,16},{28,20},{1,9},{5... | collective-permute-start | bytes 393224 | tf_op jit(solution)/shard_map/ppermute | solution.py:420
  48.7 5.9 %collective-permute-start.9 = (bf16[16,32,128]{2,1,0:T(8,128)(2,1)S(1)}, bf16[16,32,128]{2,1,0:T(8,128)(2,1)S(1)}, u32[]{:S(2)}, u32[]{:S(2)}) collective-permute-start(bf16[16,32,128]{2,1,0:T(8,128)(2,1)S(1)} %fold.9), channel_id=1, source_target_pairs={{0,4},{4,0},{8,12},{12,8},{16,20},{20,16},{24,28},{28,24},{1,5},{5... | collective-permute-start | bytes 393224 | tf_op jit(solution)/shard_map/ppermute | solution.py:420
  49.6 5.0 %collective-permute-start.15 = (f32[8,128]{1,0:T(8,128)S(1)}, f32[8,128]{1,0:T(8,128)S(1)}, u32[]{:S(2)}, u32[]{:S(2)}) collective-permute-start(f32[8,128]{1,0:T(8,128)S(1)} %get-tuple-element.79.refs_9_), channel_id=1, source_target_pairs={{0,2},{1,3},{2,0},{3,1},{4,6},{5,7},{6,4},{7,5},{8,10},{9,11},{10,... | collective-permute-start | bytes 12296 | tf_op jit(solution)/shard_map/ppermute | solution.py:420
  57.5 6.0 %collective-permute-start.19 = (bf16[16,32,128]{2,1,0:T(8,128)(2,1)S(1)}, bf16[16,32,128]{2,1,0:T(8,128)(2,1)S(1)}, u32[]{:S(2)}, u32[]{:S(2)}) collective-permute-start(bf16[16,32,128]{2,1,0:T(8,128)(2,1)S(1)} %get-tuple-element.80.panel_ref.refs_0_), channel_id=1, source_target_pairs={{0,16},{4,20},{8,24},{12,28},{16,0},{20,4},{24,8},{28,12},{1,17},{... | collective-permute-start | bytes 393224 | tf_op jit(solution)/shard_map/ppermute | solution.py:420
  57.6 9.0 %collective-permute-start.16 = (bf16[16,32,128]{2,1,0:T(8,128)(2,1)S(1)}, bf16[16,32,128]{2,1,0:T(8,128)(2,1)S(1)}, u32[]{:S(2)}, u32[]{:S(2)}) collective-permute-start(bf16[16,32,128]{2,1,0:T(8,128)(2,1)S(1)} %get-tuple-element.80.panel_ref.refs_0_), channel_id=1, source_target_pairs={{0,4},{4,0},{8,12},{12,8},{16,20},{20,16},{24,28},{28,24},{1,5},{5... | collective-permute-start | bytes 393224 | tf_op jit(solution)/shard_map/ppermute | solution.py:420
  63.6 5.0 %collective-permute-start.21 = (bf16[16,32,128]{2,1,0:T(8,128)(2,1)S(1)}, bf16[16,32,128]{2,1,0:T(8,128)(2,1)S(1)}, u32[]{:S(2)}, u32[]{:S(2)}) collective-permute-start(bf16[16,32,128]{2,1,0:T(8,128)(2,1)S(1)} %get-tuple-element.82.refs_4_), channel_id=1, source_target_pairs={{0,8},{4,12},{8,0},{12,4},{16,24},{20,28},{24,16},{28,20},{1,9},{5... | collective-permute-start | bytes 393224 | tf_op jit(solution)/shard_map/ppermute | solution.py:420
  63.7 6.4 %collective-permute-start.17 = (bf16[16,32,128]{2,1,0:T(8,128)(2,1)S(1)}, bf16[16,32,128]{2,1,0:T(8,128)(2,1)S(1)}, u32[]{:S(2)}, u32[]{:S(2)}) collective-permute-start(bf16[16,32,128]{2,1,0:T(8,128)(2,1)S(1)} %get-tuple-element.80.panel_ref.refs_0_), channel_id=1, source_target_pairs={{0,8},{4,12},{8,0},{12,4},{16,24},{20,28},{24,16},{28,20},{1,9},{5... | collective-permute-start | bytes 393224 | tf_op jit(solution)/shard_map/ppermute | solution.py:420
  65.7 5.9 %collective-permute-start.20 = (bf16[16,32,128]{2,1,0:T(8,128)(2,1)S(1)}, bf16[16,32,128]{2,1,0:T(8,128)(2,1)S(1)}, u32[]{:S(2)}, u32[]{:S(2)}) collective-permute-start(bf16[16,32,128]{2,1,0:T(8,128)(2,1)S(1)} %get-tuple-element.82.refs_4_), channel_id=1, source_target_pairs={{0,4},{4,0},{8,12},{12,8},{16,20},{20,16},{24,28},{28,24},{1,5},{5... | collective-permute-start | bytes 393224 | tf_op jit(solution)/shard_map/ppermute | solution.py:420
  66.6 5.0 %collective-permute-start.18 = (bf16[16,32,128]{2,1,0:T(8,128)(2,1)S(1)}, bf16[16,32,128]{2,1,0:T(8,128)(2,1)S(1)}, u32[]{:S(2)}, u32[]{:S(2)}) collective-permute-start(bf16[16,32,128]{2,1,0:T(8,128)(2,1)S(1)} %collective-permute-done.16.refs_1_), channel_id=1, source_target_pairs={{0,8},{4,12},{8,0},{12,4},{16,24},{20,28},{24,16},{28,20},{1,9},{5... | collective-permute-start | bytes 393224 | tf_op jit(solution)/shard_map/ppermute | solution.py:420
  68.6 5.0 %collective-permute-start.22 = (bf16[16,32,128]{2,1,0:T(8,128)(2,1)S(1)}, bf16[16,32,128]{2,1,0:T(8,128)(2,1)S(1)}, u32[]{:S(2)}, u32[]{:S(2)}) collective-permute-start(bf16[16,32,128]{2,1,0:T(8,128)(2,1)S(1)} %collective-permute-done.21.refs_6_), channel_id=1, source_target_pairs={{0,4},{4,0},{8,12},{12,8},{16,20},{20,16},{24,28},{28,24},{1,5},{5... | collective-permute-start | bytes 393224 | tf_op jit(solution)/shard_map/ppermute | solution.py:420
  69.6 1.2 collective-permute-start.23
  77.1 5.4 %collective-permute-start.28 = (bf16[17,32,128]{2,1,0:T(8,128)(2,1)S(1)}, bf16[17,32,128]{2,1,0:T(8,128)(2,1)S(1)}, u32[]{:S(2)}, u32[]{:S(2)}) collective-permute-start(bf16[17,32,128]{2,1,0:T(8,128)(2,1)S(1)} %get-tuple-element.93.refs_2_), channel_id=1, source_target_pairs={{0,4},{4,0},{8,12},{12,8},{16,20},{20,16},{24,28},{28,24},{1,5},{5... | collective-permute-start | bytes 417800 | tf_op jit(solution)/shard_map/ppermute | solution.py:420
  82.5 6.7 %collective-permute-start.29 = (bf16[17,32,128]{2,1,0:T(8,128)(2,1)S(1)}, bf16[17,32,128]{2,1,0:T(8,128)(2,1)S(1)}, u32[]{:S(2)}, u32[]{:S(2)}) collective-permute-start(bf16[17,32,128]{2,1,0:T(8,128)(2,1)S(1)} %fold.13.refs_3_), channel_id=1, source_target_pairs={{0,8},{4,12},{8,0},{12,4},{16,24},{20,28},{24,16},{28,20},{1,9},{5... | collective-permute-start | bytes 417800 | tf_op jit(solution)/shard_map/ppermute | solution.py:420
  82.6 5.0 %collective-permute-start.27 = (bf16[16,32,128]{2,1,0:T(8,128)(2,1)S(1)}, bf16[16,32,128]{2,1,0:T(8,128)(2,1)S(1)}, u32[]{:S(2)}, u32[]{:S(2)}) collective-permute-start(bf16[16,32,128]{2,1,0:T(8,128)(2,1)S(1)} %get-tuple-element.91), channel_id=1, source_target_pairs={{0,4},{4,0},{8,12},{12,8},{16,20},{20,16},{24,28},{28,24},{1,5},{5... | collective-permute-start | bytes 393224 | tf_op jit(solution)/shard_map/ppermute | solution.py:420
  83.6 9.7 %collective-permute-start.24 = (bf16[16,32,128]{2,1,0:T(8,128)(2,1)S(1)}, bf16[16,32,128]{2,1,0:T(8,128)(2,1)S(1)}, u32[]{:S(2)}, u32[]{:S(2)}) collective-permute-start(bf16[16,32,128]{2,1,0:T(8,128)(2,1)S(1)} %get-tuple-element.88), channel_id=1, source_target_pairs={{0,8},{4,12},{8,0},{12,4},{16,24},{20,28},{24,16},{28,20},{1,9},{5... | collective-permute-start | bytes 393224 | tf_op jit(solution)/shard_map/ppermute | solution.py:420
  89.4 10.2 %collective-permute-start.30 = (bf16[17,32,128]{2,1,0:T(8,128)(2,1)S(1)}, bf16[17,32,128]{2,1,0:T(8,128)(2,1)S(1)}, u32[]{:S(2)}, u32[]{:S(2)}) collective-permute-start(bf16[17,32,128]{2,1,0:T(8,128)(2,1)S(1)} %get-tuple-element.97.refs_4_), channel_id=1, source_target_pairs={{0,16},{4,20},{8,24},{12,28},{16,0},{20,4},{24,8},{28,12},{1,17},{... | collective-permute-start | bytes 417800 | tf_op jit(solution)/shard_map/ppermute | solution.py:420
  91.8 6.0 %collective-permute-start.26 = (bf16[16,32,128]{2,1,0:T(8,128)(2,1)S(1)}, bf16[16,32,128]{2,1,0:T(8,128)(2,1)S(1)}, u32[]{:S(2)}, u32[]{:S(2)}) collective-permute-start(bf16[16,32,128]{2,1,0:T(8,128)(2,1)S(1)} %get-tuple-element.89), channel_id=1, source_target_pairs={{0,8},{4,12},{8,0},{12,4},{16,24},{20,28},{24,16},{28,20},{1,9},{5... | collective-permute-start | bytes 393224 | tf_op jit(solution)/shard_map/ppermute | solution.py:420
  93.4 6.3 %collective-permute-start.25 = (bf16[16,32,128]{2,1,0:T(8,128)(2,1)S(1)}, bf16[16,32,128]{2,1,0:T(8,128)(2,1)S(1)}, u32[]{:S(2)}, u32[]{:S(2)}) collective-permute-start(bf16[16,32,128]{2,1,0:T(8,128)(2,1)S(1)} %fold.12), channel_id=1, source_target_pairs={{0,4},{4,0},{8,12},{12,8},{16,20},{20,16},{24,28},{28,24},{1,5},{5... | collective-permute-start | bytes 393224 | tf_op jit(solution)/shard_map/ppermute | solution.py:420
  95.0 4.6 %collective-permute-start.31 = (f32[8,128]{1,0:T(8,128)S(1)}, f32[8,128]{1,0:T(8,128)S(1)}, u32[]{:S(2)}, u32[]{:S(2)}) collective-permute-start(f32[8,128]{1,0:T(8,128)S(1)} %get-tuple-element.100.refs_9_), channel_id=1, source_target_pairs={{0,2},{1,3},{2,0},{3,1},{4,6},{5,7},{6,4},{7,5},{8,10},{9,11},{10,... | collective-permute-start | bytes 12296 | tf_op jit(solution)/shard_map/ppermute | solution.py:420
  99.8 7.1 %collective-permute-start.35 = (bf16[16,32,128]{2,1,0:T(8,128)(2,1)S(1)}, bf16[16,32,128]{2,1,0:T(8,128)(2,1)S(1)}, u32[]{:S(2)}, u32[]{:S(2)}) collective-permute-start(bf16[16,32,128]{2,1,0:T(8,128)(2,1)S(1)} %get-tuple-element.101.panel_ref.refs_0_), channel_id=1, source_target_pairs={{0,16},{4,20},{8,24},{12,28},{16,0},{20,4},{24,8},{28,12},{1,17},{... | collective-permute-start | bytes 393224 | tf_op jit(solution)/shard_map/ppermute | solution.py:420
  100.5 10.1 %collective-permute-start.32 = (bf16[16,32,128]{2,1,0:T(8,128)(2,1)S(1)}, bf16[16,32,128]{2,1,0:T(8,128)(2,1)S(1)}, u32[]{:S(2)}, u32[]{:S(2)}) collective-permute-start(bf16[16,32,128]{2,1,0:T(8,128)(2,1)S(1)} %get-tuple-element.101.panel_ref.refs_0_), channel_id=1, source_target_pairs={{0,4},{4,0},{8,12},{12,8},{16,20},{20,16},{24,28},{28,24},{1,5},{5... | collective-permute-start | bytes 393224 | tf_op jit(solution)/shard_map/ppermute | solution.py:420
  106.9 5.8 %collective-permute-start.37 = (bf16[16,32,128]{2,1,0:T(8,128)(2,1)S(1)}, bf16[16,32,128]{2,1,0:T(8,128)(2,1)S(1)}, u32[]{:S(2)}, u32[]{:S(2)}) collective-permute-start(bf16[16,32,128]{2,1,0:T(8,128)(2,1)S(1)} %get-tuple-element.103.refs_4_), channel_id=1, source_target_pairs={{0,8},{4,12},{8,0},{12,4},{16,24},{20,28},{24,16},{28,20},{1,9},{5... | collective-permute-start | bytes 393224 | tf_op jit(solution)/shard_map/ppermute | solution.py:420
  109.7 5.0 %collective-permute-start.33 = (bf16[16,32,128]{2,1,0:T(8,128)(2,1)S(1)}, bf16[16,32,128]{2,1,0:T(8,128)(2,1)S(1)}, u32[]{:S(2)}, u32[]{:S(2)}) collective-permute-start(bf16[16,32,128]{2,1,0:T(8,128)(2,1)S(1)} %get-tuple-element.101.panel_ref.refs_0_), channel_id=1, source_target_pairs={{0,8},{4,12},{8,0},{12,4},{16,24},{20,28},{24,16},{28,20},{1,9},{5... | collective-permute-start | bytes 393224 | tf_op jit(solution)/shard_map/ppermute | solution.py:420
  109.8 6.3 %collective-permute-start.36 = (bf16[16,32,128]{2,1,0:T(8,128)(2,1)S(1)}, bf16[16,32,128]{2,1,0:T(8,128)(2,1)S(1)}, u32[]{:S(2)}, u32[]{:S(2)}) collective-permute-start(bf16[16,32,128]{2,1,0:T(8,128)(2,1)S(1)} %get-tuple-element.103.refs_4_), channel_id=1, source_target_pairs={{0,4},{4,0},{8,12},{12,8},{16,20},{20,16},{24,28},{28,24},{1,5},{5... | collective-permute-start | bytes 393224 | tf_op jit(solution)/shard_map/ppermute | solution.py:420
  110.6 5.5 %collective-permute-start.34 = (bf16[16,32,128]{2,1,0:T(8,128)(2,1)S(1)}, bf16[16,32,128]{2,1,0:T(8,128)(2,1)S(1)}, u32[]{:S(2)}, u32[]{:S(2)}) collective-permute-start(bf16[16,32,128]{2,1,0:T(8,128)(2,1)S(1)} %collective-permute-done.32.refs_1_), channel_id=1, source_target_pairs={{0,8},{4,12},{8,0},{12,4},{16,24},{20,28},{24,16},{28,20},{1,9},{5... | collective-permute-start | bytes 393224 | tf_op jit(solution)/shard_map/ppermute | solution.py:420
  112.7 5.0 %collective-permute-start.38 = (bf16[16,32,128]{2,1,0:T(8,128)(2,1)S(1)}, bf16[16,32,128]{2,1,0:T(8,128)(2,1)S(1)}, u32[]{:S(2)}, u32[]{:S(2)}) collective-permute-start(bf16[16,32,128]{2,1,0:T(8,128)(2,1)S(1)} %collective-permute-done.37.refs_6_), channel_id=1, source_target_pairs={{0,4},{4,0},{8,12},{12,8},{16,20},{20,16},{24,28},{28,24},{1,5},{5... | collective-permute-start | bytes 393224 | tf_op jit(solution)/shard_map/ppermute | solution.py:420
  113.8 1.2 collective-permute-start.39
  121.8 5.1 %collective-permute-start.44 = (bf16[17,32,128]{2,1,0:T(8,128)(2,1)S(1)}, bf16[17,32,128]{2,1,0:T(8,128)(2,1)S(1)}, u32[]{:S(2)}, u32[]{:S(2)}) collective-permute-start(bf16[17,32,128]{2,1,0:T(8,128)(2,1)S(1)} %get-tuple-element.115.refs_2_), channel_id=1, source_target_pairs={{0,4},{4,0},{8,12},{12,8},{16,20},{20,16},{24,28},{28,24},{1,5},{5... | collective-permute-start | bytes 417800 | tf_op jit(solution)/shard_map/ppermute | solution.py:420
  127.0 8.6 %collective-permute-start.45 = (bf16[17,32,128]{2,1,0:T(8,128)(2,1)S(1)}, bf16[17,32,128]{2,1,0:T(8,128)(2,1)S(1)}, u32[]{:S(2)}, u32[]{:S(2)}) collective-permute-start(bf16[17,32,128]{2,1,0:T(8,128)(2,1)S(1)} %fold.16.refs_3_), channel_id=1, source_target_pairs={{0,8},{4,12},{8,0},{12,4},{16,24},{20,28},{24,16},{28,20},{1,9},{5... | collective-permute-start | bytes 417800 | tf_op jit(solution)/shard_map/ppermute | solution.py:420
  129.3 6.3 %collective-permute-start.43 = (bf16[16,32,128]{2,1,0:T(8,128)(2,1)S(1)}, bf16[16,32,128]{2,1,0:T(8,128)(2,1)S(1)}, u32[]{:S(2)}, u32[]{:S(2)}) collective-permute-start(bf16[16,32,128]{2,1,0:T(8,128)(2,1)S(1)} %get-tuple-element.113), channel_id=1, source_target_pairs={{0,4},{4,0},{8,12},{12,8},{16,20},{20,16},{24,28},{28,24},{1,5},{5... | collective-permute-start | bytes 393224 | tf_op jit(solution)/shard_map/ppermute | solution.py:420
  130.1 6.7 %collective-permute-start.40 = (bf16[16,32,128]{2,1,0:T(8,128)(2,1)S(1)}, bf16[16,32,128]{2,1,0:T(8,128)(2,1)S(1)}, u32[]{:S(2)}, u32[]{:S(2)}) collective-permute-start(bf16[16,32,128]{2,1,0:T(8,128)(2,1)S(1)} %get-tuple-element.110), channel_id=1, source_target_pairs={{0,8},{4,12},{8,0},{12,4},{16,24},{20,28},{24,16},{28,20},{1,9},{5... | collective-permute-start | bytes 393224 | tf_op jit(solution)/shard_map/ppermute | solution.py:420
  135.7 7.2 %collective-permute-start.46 = (bf16[17,32,128]{2,1,0:T(8,128)(2,1)S(1)}, bf16[17,32,128]{2,1,0:T(8,128)(2,1)S(1)}, u32[]{:S(2)}, u32[]{:S(2)}) collective-permute-start(bf16[17,32,128]{2,1,0:T(8,128)(2,1)S(1)} %get-tuple-element.119.refs_4_), channel_id=1, source_target_pairs={{0,16},{4,20},{8,24},{12,28},{16,0},{20,4},{24,8},{28,12},{1,17},{... | collective-permute-start | bytes 417800 | tf_op jit(solution)/shard_map/ppermute | solution.py:420
  135.8 5.1 %collective-permute-start.42 = (bf16[16,32,128]{2,1,0:T(8,128)(2,1)S(1)}, bf16[16,32,128]{2,1,0:T(8,128)(2,1)S(1)}, u32[]{:S(2)}, u32[]{:S(2)}) collective-permute-start(bf16[16,32,128]{2,1,0:T(8,128)(2,1)S(1)} %get-tuple-element.111), channel_id=1, source_target_pairs={{0,8},{4,12},{8,0},{12,4},{16,24},{20,28},{24,16},{28,20},{1,9},{5... | collective-permute-start | bytes 393224 | tf_op jit(solution)/shard_map/ppermute | solution.py:420
  136.8 5.0 %collective-permute-start.41 = (bf16[16,32,128]{2,1,0:T(8,128)(2,1)S(1)}, bf16[16,32,128]{2,1,0:T(8,128)(2,1)S(1)}, u32[]{:S(2)}, u32[]{:S(2)}) collective-permute-start(bf16[16,32,128]{2,1,0:T(8,128)(2,1)S(1)} %fold.15), channel_id=1, source_target_pairs={{0,4},{4,0},{8,12},{12,8},{16,20},{20,16},{24,28},{28,24},{1,5},{5... | collective-permute-start | bytes 393224 | tf_op jit(solution)/shard_map/ppermute | solution.py:420
  137.9 3.9 %collective-permute-start.47 = (f32[8,128]{1,0:T(8,128)S(1)}, f32[8,128]{1,0:T(8,128)S(1)}, u32[]{:S(2)}, u32[]{:S(2)}) collective-permute-start(f32[8,128]{1,0:T(8,128)S(1)} %get-tuple-element.122.refs_9_), channel_id=1, source_target_pairs={{0,2},{1,3},{2,0},{3,1},{4,6},{5,7},{6,4},{7,5},{8,10},{9,11},{10,... | collective-permute-start | bytes 12296 | tf_op jit(solution)/shard_map/ppermute | solution.py:420

commit v4 on v3

--- a/solution.py
+++ b/solution.py
@@ -17,6 +17,7 @@
 MIB = 1024 * 1024
 GROUP = 8
 HEAD_GROUP = 16
+KERNEL_COST = 100000
 
 
 def contract_last(left, right):
@@ -55,10 +56,10 @@
     return jnp.sum(parts.astype(jnp.float32), axis=1, keepdims=True)
 
 
-def head_kernel(group, steps, peers, index_ref, *refs):
+def head_kernel(group, steps, peers, late, scen_total, index_ref, *refs):
     panels, refs = refs[:peers], refs[peers:]
-    heads_ref, pulled_ref, flows_ref, costs_ref, risk_ref, sum_ref, other_ref = refs[:7]
-    flows_out, bar_out, sum_out, refs = *refs[7:10], refs[10:]
+    heads_ref, pulled_ref, flows_ref, costs_ref, risk_ref, level_ref, sum_ref, other_ref = refs[:8]
+    flows_out, bar_out, risk_out, level_out, sum_out, refs = *refs[8:13], refs[13:]
     kept, refs = refs[: peers // 2], refs[peers // 2 :]
     sends, (panel, terms, pulled, loss) = refs[:-4], refs[-4:]
     rows = heads_ref.shape[-1]
@@ -70,7 +71,17 @@
     def _():
         terms[...] = jnp.zeros_like(terms)
         loss[...] = jnp.zeros_like(loss)
-        sum_out[...] = sum_ref[...] + other_ref[...]
+        risk_total = sum_ref[...] + other_ref[...]
+        if late:
+            level_new, level_bar = next_level(level_ref[...], risk_total, scen_total)
+            risk_start = jnp.maximum(risk_ref[...] - risk_step * level_bar[:1], 0.0)
+            risk_out[...] = risk_start
+            level_out[...] = level_new
+            sum_out[...] = add_rows(risk_start, sum_out.shape)
+        else:
+            risk_out[...] = risk_ref[...]
+            level_out[...] = level_ref[...]
+            sum_out[...] = risk_total
         for peer in range(peers):
             panel[peer * node_blks : (peer + 1) * node_blks] = panels[peer][...]
 
@@ -78,7 +89,7 @@
     spans = [slice(member * rows, (member + 1) * rows) for member in range(group)]
     for member in range(group):
         pulled[:, spans[member]] = contract_last(panel[places[member]], heads_ref[member])
-    risk = risk_ref[...]
+    risk = risk_out[...]
     loss_sum = jnp.zeros_like(risk)
     for columns in spans:
         flows = flows_ref[:, columns]
@@ -131,24 +142,43 @@
     return values[0]
 
 
-def fold_kernel(count, with_loss, extras, after, *refs):
-    kept_ref, arrived, refs = refs[0], refs[1 : 1 + count], refs[1 + count :]
-    node_blks = kept_ref.shape[0]
+def fold_kernel(counts, with_loss, extras, after, *refs):
+    inputs, refs = refs[: sum(counts) + len(counts)], refs[sum(counts) + len(counts) :]
     if with_loss:
         loss_ref, refs = refs[0], refs[1:]
     extra_in, refs = refs[:extras], refs[extras + after :]
-    out_ref, extra_out = refs[0], refs[1:]
-    for block in range(node_blks):
-        total = pair_sum([ref[block].astype(jnp.float32) for ref in arrived])
-        out_ref[block] = (kept_ref[block] + total).astype(jnp.bfloat16)
-    if with_loss:
-        both = from_parts(loss_ref[loss_ref.shape[0] - 1]) + from_parts(arrived[-1][node_blks])
-        out_ref[node_blks] = to_parts(both, loss_ref.shape[1:])
+    outs, extra_out = refs[: len(counts)], refs[len(counts) :]
+    node_blks = inputs[0].shape[0]
+    for number, (count, out_ref) in enumerate(zip(counts, outs)):
+        kept_ref, arrived, inputs = inputs[0], inputs[1 : 1 + count], inputs[1 + count :]
+        for block in range(node_blks):
+            total = pair_sum([ref[block].astype(jnp.float32) for ref in arrived])
+            out_ref[block] = (kept_ref[block] + total).astype(jnp.bfloat16)
+        if with_loss and number == 0:
+            both = from_parts(loss_ref[loss_ref.shape[0] - 1]) + from_parts(arrived[-1][node_blks])
+            out_ref[node_blks] = to_parts(both, loss_ref.shape[1:])
     for source, target in zip(extra_in, extra_out):
         target[...] = source[...]
 
 
-def settle_kernel(count, arc_total, scen_total, last, *refs):
+def next_level(level, risk_total, scen_total):
+    level_new = level - primal_step * (1.0 - risk_total / scen_total)
+    return level_new, 2.0 * level_new - level
+
+
+def add_rows(values, shape):
+    return jnp.broadcast_to(jnp.sum(values, axis=0, keepdims=True), shape)
+
+
+def as_row(values):
+    rows = values.shape[0]
+    picked = lax.broadcasted_iota(jnp.int32, values.shape, 0) == lax.broadcasted_iota(
+        jnp.int32, values.shape, 1
+    )
+    return jnp.sum(jnp.where(picked, values, 0.0), axis=0, keepdims=True)[:, :rows]
+
+
+def settle_kernel(count, arc_total, scen_total, kind, *refs):
     kept_ref, arrived, refs = refs[0], refs[1 : 1 + count], refs[1 + count :]
     loss_ref, base_ref, risk_ref, excess_ref, level_ref, sum_ref, other_ref = refs[:7]
     duals_out, half_out, risk_out, excess_out, level_out, sum_out = refs[7:]
@@ -156,26 +186,34 @@
     for block in range(node_blks):
         total = kept_ref[block] + pair_sum([ref[block].astype(jnp.float32) for ref in arrived])
         duals = base_ref[block] - dual_step * total
-        if last:
+        if kind == "last":
             duals_out[:, block * rows : (block + 1) * rows] = duals
         else:
             duals_out[block] = duals
-        half_out[block] = duals.astype(jnp.bfloat16)
+            half_out[block] = duals.astype(jnp.bfloat16)
     losses = from_parts(loss_ref[node_blks]) + from_parts(arrived[-1][node_blks])
     losses = losses / arc_total
-    mean_risk = (sum_ref[...] + other_ref[...]) / scen_total
-    level = level_ref[...]
-    level_new = level - primal_step * (1.0 - mean_risk)
-    level_bar = 2.0 * level_new - level
-    level_out[...] = level_new
     risk = risk_ref[...]
     excess = excess_ref[...]
     excess_new = jnp.maximum(excess - primal_step * (tail_weight - risk), 0.0)
     excess_bar = 2.0 * excess_new - excess
-    excess_out[...] = excess_new
-    risk_new = jnp.maximum(risk + risk_step * (losses - excess_bar - level_bar[:1]), 0.0)
-    risk_out[...] = risk_new
-    sum_out[...] = jnp.broadcast_to(jnp.sum(risk_new, axis=0, keepdims=True), sum_out.shape)
+    risk_new = risk + risk_step * (losses - excess_bar)
+    if kind == "early":
+        risk_out[...] = risk_new
+        excess_out[...] = excess_new
+        return
+    risk_total = sum_ref[...] if kind == "first" else sum_ref[...] + other_ref[...]
+    level_new, level_bar = next_level(level_ref[...], risk_total, scen_total)
+    risk_new = jnp.maximum(risk_new - risk_step * level_bar[:1], 0.0)
+    if kind == "last":
+        risk_out[...] = as_row(risk_new)
+        excess_out[...] = as_row(excess_new)
+        level_out[...] = level_new[:1, :1]
+    else:
+        risk_out[...] = risk_new
+        excess_out[...] = excess_new
+        level_out[...] = level_new
+        sum_out[...] = add_rows(risk_new, sum_out.shape)
 
 
 def local_forward_kernel(
@@ -187,6 +225,7 @@
     blocks_ref,
     duals_ref,
     demand_ref,
+    after_ref,
     out_ref,
     total,
 ):
@@ -247,13 +286,13 @@
         ),
         compiler_params=params(),
         cost_estimate=pl.CostEstimate(
-            flops=2 * scen_rows * blocks.size, bytes_accessed=2 * blocks.size, transcendentals=0
+            flops=KERNEL_COST, bytes_accessed=KERNEL_COST, transcendentals=0
         ),
         name="local_adjoint",
     )(index, panel, blocks, *after)
 
 
-def head_step(places, panels, heads, pulled, flows, costs, risk, sums):
+def head_step(places, panels, heads, pulled, flows, costs, risk, level, sums, late, scen_total):
     arc_blks, rows, _ = heads.shape
     scen_rows = flows.shape[0]
     peers = len(panels)
@@ -265,11 +304,13 @@
     sent[-1] = (node_blks + 1, scen_rows, rows)
     arcs = pl.BlockSpec((scen_rows, group * rows), lambda i, *_: (0, i))
     results = pl.pallas_call(
-        functools.partial(head_kernel, group, steps, peers),
+        functools.partial(head_kernel, group, steps, peers, late, scen_total),
         out_shape=[
             jax.ShapeDtypeStruct(flows.shape, jnp.float32),
             jax.ShapeDtypeStruct(flows.shape, jnp.bfloat16),
-            jax.ShapeDtypeStruct(sums[0].shape, jnp.float32),
+            jax.ShapeDtypeStruct(risk.shape, jnp.float32),
+            jax.ShapeDtypeStruct(level.shape, jnp.float32),
+            jax.ShapeDtypeStruct(level.shape, jnp.float32),
         ]
         + [jax.ShapeDtypeStruct(kept, jnp.float32)] * (peers // 2)
         + [jax.ShapeDtypeStruct(shape, jnp.bfloat16) for shape in sent],
@@ -283,10 +324,11 @@
                 arcs,
                 pl.BlockSpec((1, group * rows), lambda i, *_: (0, i)),
                 whole(scen_rows, rows),
-                whole(*sums[0].shape),
-                whole(*sums[0].shape),
+                whole(*level.shape),
+                whole(*level.shape),
+                whole(*level.shape),
             ],
-            out_specs=[arcs, arcs, whole(*sums[0].shape)]
+            out_specs=[arcs, arcs, whole(scen_rows, rows), whole(*level.shape), whole(*level.shape)]
             + [whole(*kept)] * (peers // 2)
             + [whole(*shape) for shape in sent],
             scratch_shapes=[
@@ -303,11 +345,11 @@
             transcendentals=0,
         ),
         name="head_step",
-    )(places, *panels, heads, pulled, flows, costs, risk, *sums)
+    )(places, *panels, heads, pulled, flows, costs, risk, level, *sums)
     half = peers // 2
-    kept = dict(zip(inner(peers), results[3 : 3 + half]))
-    sends = dict(zip(leaves(peers), results[3 + half :]))
-    return *results[:3], kept, sends
+    kept = dict(zip(inner(peers), results[5 : 5 + half]))
+    sends = dict(zip(leaves(peers), results[5 + half :]))
+    return *results[:5], kept, sends
 
 
 def small_cost(*arrays):
@@ -315,15 +357,20 @@
     return pl.CostEstimate(flops=size, bytes_accessed=2 * size, transcendentals=0)
 
 
-def fold(kept, arrived, loss, extras, after):
-    node_blks, scen_rows, rows = kept.shape
+def fold(tops, loss, extras, after):
+    node_blks, scen_rows, rows = tops[0][0].shape
     with_loss = loss is not None
-    operands = [kept, *arrived] + ([loss] if with_loss else []) + list(extras)
+    operands = [array for kept, arrived in tops for array in (kept, *arrived)]
+    operands += ([loss] if with_loss else []) + list(extras)
     vmem = pl.BlockSpec(memory_space=pltpu.VMEM)
-    out_shape = [jax.ShapeDtypeStruct((node_blks + with_loss, scen_rows, rows), jnp.bfloat16)]
+    out_shape = [
+        jax.ShapeDtypeStruct((node_blks + (with_loss and number == 0), scen_rows, rows), jnp.bfloat16)
+        for number in range(len(tops))
+    ]
     out_shape += [jax.ShapeDtypeStruct(extra.shape, extra.dtype) for extra in extras]
+    counts = [len(arrived) for _, arrived in tops]
     results = pl.pallas_call(
-        functools.partial(fold_kernel, len(arrived), with_loss, len(extras), len(after)),
+        functools.partial(fold_kernel, counts, with_loss, len(extras), len(after)),
         out_shape=out_shape,
         in_specs=[vmem] * len(operands) + [pl.BlockSpec(memory_space=pl.ANY)] * len(after),
         out_specs=[vmem] * len(out_shape),
@@ -331,20 +378,20 @@
         cost_estimate=small_cost(*operands),
         name="fold",
     )(*operands, *after)
-    return results[0], results[1:]
-
-
-def settle(kept, arrived, loss, base, risk, excess, level, sums, arc_total, scen_total, last):
+    return results[: len(tops)], results[len(tops) :]
+
+
+def settle(kept, arrived, loss, base, risk, excess, level, sums, arc_total, scen_total, kind):
     node_blks, scen_rows, rows = base.shape
-    duals = (scen_rows, node_blks * rows) if last else base.shape
+    last = kind == "last"
     return pl.pallas_call(
-        functools.partial(settle_kernel, len(arrived), arc_total, scen_total, last),
+        functools.partial(settle_kernel, len(arrived), arc_total, scen_total, kind),
         out_shape=(
-            jax.ShapeDtypeStruct(duals, jnp.float32),
+            jax.ShapeDtypeStruct((scen_rows, node_blks * rows) if last else base.shape, jnp.float32),
             jax.ShapeDtypeStruct(base.shape, jnp.bfloat16),
-            jax.ShapeDtypeStruct(risk.shape, jnp.float32),
-            jax.ShapeDtypeStruct(risk.shape, jnp.float32),
-            jax.ShapeDtypeStruct(level.shape, jnp.float32),
+            jax.ShapeDtypeStruct((1, scen_rows) if last else risk.shape, jnp.float32),
+            jax.ShapeDtypeStruct((1, scen_rows) if last else risk.shape, jnp.float32),
+            jax.ShapeDtypeStruct((1, 1) if last else level.shape, jnp.float32),
             jax.ShapeDtypeStruct(level.shape, jnp.float32),
         ),
         compiler_params=pltpu.CompilerParams(vmem_limit_bytes=vmem_limit(8)),
@@ -353,7 +400,7 @@
     )(kept, *arrived, loss, base, risk, excess, level, *sums)
 
 
-def local_forward(index, bar, blocks, duals, demand):
+def local_forward(index, bar, blocks, duals, demand, after):
     arc_blks, touches, rows, _ = blocks.shape
     scen_rows = bar.shape[0]
     group = GROUP
@@ -369,16 +416,17 @@
                 pl.BlockSpec((group, touches, rows, rows), lambda i, *_: (i, 0, 0, 0)),
                 whole(*duals.shape),
                 whole(*duals.shape),
+                pl.BlockSpec(memory_space=pl.ANY),
             ],
             out_specs=whole(*duals.shape),
             scratch_shapes=[pltpu.VMEM(duals.shape, jnp.float32)],
         ),
         compiler_params=params(),
         cost_estimate=pl.CostEstimate(
-            flops=2 * scen_rows * blocks.size, bytes_accessed=2 * blocks.size, transcendentals=0
+            flops=KERNEL_COST, bytes_accessed=KERNEL_COST, transcendentals=0
         ),
         name="local_forward",
-    )(index, bar, blocks, duals, demand)
+    )(index, bar, blocks, duals, demand, after)
 
 
 def relay(arrived, risk_sum, after):
@@ -404,7 +452,7 @@
 
 def sum_rows(values, shape):
     def kernel(values_ref, out_ref):
-        out_ref[...] = jnp.broadcast_to(jnp.sum(values_ref[...], axis=0, keepdims=True), shape)
+        out_ref[...] = add_rows(values_ref[...], shape)
 
     return pl.pallas_call(
         kernel,
@@ -420,14 +468,31 @@
     return lax.ppermute(value, axis, [(i, i ^ distance) for i in range(size)])
 
 
+def exchange_lowest(distance):
+    return (distance & ~3) | ((distance & 1) << 1) | ((distance >> 1) & 1)
+
+
+def swap_net(value, distance):
+    net_size, scen_size = lax.axis_size("net"), lax.axis_size("scen")
+    pairs = []
+    for net in range(net_size):
+        for scen in range(scen_size):
+            hop = exchange_lowest(distance) if scen % 2 else distance
+            pairs.append((net * scen_size + scen, (net ^ hop) * scen_size + scen))
+    return lax.ppermute(value, ("net", "scen"), pairs)
+
+
 def gather_panels(own, risk_sum, after):
     peers = lax.axis_size("net")
     panels = [own] + [None] * (peers - 1)
-    for distance in sorted(range(1, peers), key=lambda k: (k.bit_count(), -k)):
+    order = sorted(range(1, peers), key=lambda k: (k.bit_count(), -k))
+    for distance in order:
         hop = last_hop(distance)
-        panels[distance] = swap(panels[distance ^ hop], "net", hop)
-        if distance == peers // 2:
-            panels[distance], risk_sum = relay(panels[distance], risk_sum, after)
+        panels[distance] = swap_net(panels[distance ^ hop], hop)
+        if distance == 1:
+            far = peers // 2
+            firsts = tuple(panels[k] for k in order if k.bit_count() == 1 and k != far)
+            panels[far], risk_sum = relay(panels[far], risk_sum, after + firsts)
     return panels, risk_sum
 
 
@@ -452,6 +517,7 @@
     scen_total = scen_rows * lax.axis_size("scen")
     costs = arc_costs.reshape(1, -1)
     distance = jnp.bitwise_xor(head_index // node_blks, lax.axis_index("net"))
+    distance = jnp.where(lax.axis_index("scen") % 2 == 1, exchange_lowest(distance), distance)
     places = distance * node_blks + head_index % node_blks
     scen_size = lax.axis_size("scen")
     wide = (scen_rows, rows)
@@ -468,39 +534,67 @@
     risk = jnp.broadcast_to(risk_duals[:, None], wide)
     level = jnp.broadcast_to(threshold[:, None], flat)
     risk_sum = sum_rows(risk, flat)
+    early = [1 << bit for bit in range(1, scen_size.bit_length() - 1)][::-1]
+    zero = jnp.zeros_like(risk_sum)
     for iteration in range(ROUNDS):
+        kind = "first" if iteration == 0 else "last" if iteration == ROUNDS - 1 else "early"
         pulled = local_adjoint(local_index, half, local_blocks, ())
-        panels, risk_sum = gather_panels(half, risk_sum, (pulled,))
-        sums = (risk_sum, swap(risk_sum, "scen", 1))
-        flows, bar, risk_sum, kept, sends = head_step(
-            places, panels, head_blocks, pulled, flows, costs, risk, sums
+        if kind == "first":
+            panels, _ = gather_panels(half, risk_sum, (pulled,))
+            for stride in early + [1]:
+                risk_sum = risk_sum + swap(risk_sum, "scen", stride)
+            sums = (risk_sum, zero)
+        else:
+            panels, risk_sum = gather_panels(half, risk_sum, (pulled,))
+            if kind == "early":
+                for stride in early[:-1]:
+                    risk_sum = risk_sum + swap(risk_sum, "scen", stride)
+                sums = (risk_sum, swap(risk_sum, "scen", early[-1]))
+            else:
+                sums = (risk_sum, swap(risk_sum, "scen", 1))
+        flows, bar, risk, level, risk_sum, kept, sends = head_step(
+            places,
+            panels,
+            head_blocks,
+            pulled,
+            flows,
+            costs,
+            risk,
+            level,
+            sums,
+            kind == "last",
+            scen_total,
         )
-        base = local_forward(local_index, bar, local_blocks, duals, wanted)
+        after = ()
+        if kind == "last":
+            risk_sum = risk_sum + swap(risk_sum, "scen", 1)
+            after = (risk_sum,)
         tops = sorted(inner(net_size), key=lambda k: (-k.bit_count(), -k))[:-1]
-        loss = sends[net_size - 1]
-        arrived = {}
-        for top in tops:
-            below = sorted(children(top, net_size))
-            for k in below:
-                arrived[k] = swap(sends[k], "net", last_hop(k))
-            chain = net_size - 1 in below or loss_top in below
-            after = (base,) if top == tops[0] else ()
-            extras = (risk_sum,) if top == net_size // 2 else ()
-            sends[top], passed = fold(
-                kept[top], [arrived[k] for k in below], loss if chain else None, extras, after
-            )
+        groups = [(tops[0], 1)] + [(top,) for top in tops[1:] if top != 1]
+        loss, loss_top = sends[net_size - 1], net_size - 1
+        for group in groups:
+            terms = []
+            for top in group:
+                below = sorted(children(top, net_size))
+                terms.append((kept[top], [swap_net(sends[k], last_hop(k)) for k in below]))
+            chain = loss_top ^ last_hop(loss_top) == group[0]
+            extras = (risk_sum,) if group[0] == net_size // 2 and kind == "last" else ()
+            folded, passed = fold(terms, loss if chain else None, extras, after)
+            sends.update(zip(group, folded))
+            after = ()
             if chain:
-                loss_top, loss = top, sends[top]
+                loss_top, loss = group[0], folded[0]
             if extras:
                 (risk_sum,) = passed
+        base = local_forward(local_index, bar, local_blocks, duals, wanted, loss)
         below = sorted(children(0, net_size))
-        arrived = [swap(sends[k], "net", last_hop(k)) for k in below]
-        stride = 2
-        while 2 * stride < scen_size:
-            risk_sum = risk_sum + swap(risk_sum, "scen", stride)
-            stride *= 2
-        sums = (risk_sum, swap(risk_sum, "scen", stride))
-        duals, half, risk, excess_now, level, risk_sum = settle(
+        arrived = [swap_net(sends[k], last_hop(k)) for k in below]
+        sums = (risk_sum, zero)
+        if kind == "last":
+            for stride in early[:-1]:
+                risk_sum = risk_sum + swap(risk_sum, "scen", stride)
+            sums = (risk_sum, swap(risk_sum, "scen", early[-1]))
+        duals, half, risk, excess_now, level_next, sum_next = settle(
             kept[0],
             arrived,
             loss,
@@ -511,9 +605,11 @@
             sums,
             arc_total,
             scen_total,
-            iteration == ROUNDS - 1,
+            kind,
         )
-    return (flows, duals, excess_now[:, 0], risk[:, 0], level[0, :1])
+        if kind != "early":
+            level, risk_sum = level_next, sum_next
+    return (flows, duals, excess_now.reshape(-1), risk.reshape(-1), level.reshape(-1))
 
 
 def solution(mesh):

time: 145 us -> 154 us (1.062)
  starting transfers between devices: 47.6 us -> 54 us
  waiting for transfers between devices: 48.5 us -> 42.3 us
  Pallas kernels: 38.9 us -> 43.5 us
  local copies, waits for them, and re-layouts: 8.32 us -> 12.2 us
    ppermute x0 -> x42, starting transfers between devices: none -> 48.6 us  [swap_net(): return lax.ppermute(value, ('net', 'scen'), pairs)]
    ppermute x48 -> x6, starting transfers between devices: 47.6 us -> 5.33 us  [swap(): return lax.ppermute(value, axis, [(i, i ^ distance) for i in range(size)])]
    ppermute x48 -> x6, waiting for transfers between devices: 48.5 us -> 6.51 us  [swap(): return lax.ppermute(value, axis, [(i, i ^ distance) for i in range(size)])]
    ppermute x0 -> x42, waiting for transfers between devices: none -> 35.8 us  [swap_net(): return lax.ppermute(value, ('net', 'scen'), pairs)]
    unnamed x19 -> x21, local copies, waits for them, and re-layouts: 6.33 us -> 9.7 us
    pallas_call x12 -> x9, Pallas kernels: 11.9 us -> 13.5 us  [the longest x3 12.8 us: head_step(): pl.pallas_call(functools.partial(head_kernel, group, steps, peers, late,...]
    pallas_call x3, Pallas kernels: 0.03 us -> 1.6 us  [relay(): pl.pallas_call(kernel, out_shape=(jax.ShapeDtypeStruct(arrived.shape, arr...]
  transfers between devices with their start and end apart: 48 -> 48, of which waited for: 33 -> 17; matrix products, arithmetic and copies ran while one was open for 1% -> 2% of each run, Pallas kernels for 18% -> 18%
where the time goes in v4:
time: 154 us
  starting transfers between devices  54 us (35%)
  Pallas kernels  43.5 us (28%)
  waiting for transfers between devices  42.3 us (27%)
  local copies, waits for them, and re-layouts  12.2 us (8%)
  between operations  1.61 us (1%)
    ppermute x42, starting transfers between devices, swap_net(): return lax.ppermute(value, ('net', 'scen'), pairs)  48.6 us
    ppermute x42, waiting for transfers between devices, swap_net(): return lax.ppermute(value, ('net', 'scen'), pairs)  35.8 us
    pallas_call x3, Pallas kernels, local_adjoint(): pl.pallas_call(functools.partial(local_adjoint_kernel, touches, group), o...  15.3 us
    pallas_call x3, Pallas kernels, head_step(): pl.pallas_call(functools.partial(head_kernel, group, steps, peers, late,...  12.8 us
    pallas_call x3, Pallas kernels, local_forward(): pl.pallas_call(functools.partial(local_forward_kernel, touches, group, st...  11.5 us
    unnamed x21, local copies, waits for them, and re-layouts  9.7 us
    ppermute x6, waiting for transfers between devices, swap(): return lax.ppermute(value, axis, [(i, i ^ distance) for i in range(size)])  6.51 us
    ppermute x6, starting transfers between devices, swap(): return lax.ppermute(value, axis, [(i, i ^ distance) for i in range(size)])  5.33 us
  transfers between devices with their start and end apart: 48, of which 17 were waited for; matrix products, arithmetic and copies ran while one was open for 2% of the time, Pallas kernels for 18%

profile of v4, /device:TPU:0, one launch (start us, length us, event | category | flops | bytes accessed | tf_op | source)
XLA Modules:
  0.0 153.5 jit_solution(3002627321157132401)
XLA Ops:
  0.7 0.9 copy-done
  2.3 4.0 %collective-permute-start.3 = (bf16[16,32,128]{2,1,0:T(8,128)(2,1)}, bf16[16,32,128]{2,1,0:T(8,128)(2,1)}, u32[]{:S(2)}, u32[]{:S(2)}) collective-permute-start(bf16[16,32,128]{2,1,0:T(8,128)(2,1)} %fusion.2.panel_ref.refs_0_), channel_id=1, source_target_pairs={{0,16},{1,17},{2,18},{3,19},{4,20},{5,21},{6,22},{7,23},{8,24},{9,... | collective-permute-start | bytes 393224 | tf_op jit(solution)/shard_map/ppermute | solution.py:482
  6.3 1.6 %collective-permute-start.1 = (bf16[16,32,128]{2,1,0:T(8,128)(2,1)}, bf16[16,32,128]{2,1,0:T(8,128)(2,1)}, u32[]{:S(2)}, u32[]{:S(2)}) collective-permute-start(bf16[16,32,128]{2,1,0:T(8,128)(2,1)} %fusion.2.panel_ref.refs_0_), channel_id=1, source_target_pairs={{0,8},{1,5},{2,10},{3,7},{4,12},{5,1},{6,14},{7,3},{8,0},{9,13},{1... | collective-permute-start | bytes 393224 | tf_op jit(solution)/shard_map/ppermute | solution.py:482
  7.9 1.5 collective-permute-start
  10.9 3.4 %copy-done.1 = bf16[64,4,128,128]{3,2,1,0:T(8,128)(2,1)S(1)} copy-done((bf16[64,4,128,128]{3,2,1,0:T(8,128)(2,1)S(1)}, bf16[64,4,128,128]{3,2,1,0:T(8,128)(2,1)}, u32[]{:S(2)}) %copy-start.1) | copy-done | bytes 8388632
  14.3 5.7 %local_adjoint.3.refs_0_.refs_9_ = f32[32,8192]{1,0:T(8,128)S(1)} custom-call(s32[64,4]{1,0:T(8,128)S(1)} %copy.23.index_ref, bf16[16,32,128]{2,1,0:T(8,128)(2,1)} %fusion.2.panel_ref.refs_0_, bf16[64,4,128,128]{3,2,1,0:T(8,128)(2,1)S(1)} %copy-done.1), custom_call_target="tpu_custom_call" | custom-call | flops 100000 | bytes 100000 | tf_op jit(solution)/shard_map/local_adjoint/pallas_call | solution.py:274
  20.0 1.6 %relay.3 = (bf16[16,32,128]{2,1,0:T(8,128)(2,1)}, f32[8,128]{1,0:T(8,128)}) custom-call(bf16[16,32,128]{2,1,0:T(8,128)(2,1)} %collective-permute-done.3.arrived_ref, f32[8,128]{1,0:T(8,128)S(1)} %sum_rows.1.sum_ref, f32[32,8192]{1,0:T(8,128)S(1)} %local_adjoint.3.refs_0_.refs_9_, bf16[16,32,128]{2,1,0:T(8,128)(2,1)} %collective-permute-done.1.refs_1_.refs_2_, ...), custom_call_target="tpu_custom_call" | custom-call | flops 65536 | bytes 131072 | tf_op jit(solution)/shard_map/relay/pallas_call | solution.py:439
  22.0 1.5 collective-permute-start.7
  23.5 2.1 %collective-permute-done.7 = f32[8,128]{1,0:T(8,128)S(1)} collective-permute-done((f32[8,128]{1,0:T(8,128)S(1)}, f32[8,128]{1,0:T(8,128)S(1)}, u32[]{:S(2)}, u32[]{:S(2)}) %collective-permute-start.7) | collective-permute-done | bytes 4128 | tf_op jit(solution)/shard_map/ppermute | solution.py:468
  26.2 1.6 %collective-permute-start.2 = (bf16[16,32,128]{2,1,0:T(8,128)(2,1)}, bf16[16,32,128]{2,1,0:T(8,128)(2,1)S(1)}, u32[]{:S(2)}, u32[]{:S(2)}) collective-permute-start(bf16[16,32,128]{2,1,0:T(8,128)(2,1)} %collective-permute-done.refs_2_.refs_1_), channel_id=1, source_target_pairs={{0,8},{1,5},{2,10},{3,7},{4,12},{5,1},{6,14},{7,3},{8,0},{9,13},{1... | collective-permute-start | bytes 393224 | tf_op jit(solution)/shard_map/ppermute | solution.py:482
  27.7 1.5 collective-permute-start.6
  29.9 2.8 %collective-permute-done.2.refs_3_ = bf16[16,32,128]{2,1,0:T(8,128)(2,1)S(1)} collective-permute-done((bf16[16,32,128]{2,1,0:T(8,128)(2,1)}, bf16[16,32,128]{2,1,0:T(8,128)(2,1)S(1)}, u32[]{:S(2)}, u32[]{:S(2)}) %collective-permute-start.2) | collective-permute-done | bytes 131104 | tf_op jit(solution)/shard_map/ppermute | solution.py:482
  32.7 0.9 collective-permute-done.6.refs_7_
  33.6 1.2 copy-done.4
  34.9 5.0 %head_step.3 = (f32[32,8192]{1,0:T(8,128)S(1)}, bf16[32,8192]{1,0:T(8,128)(2,1)S(1)}, f32[32,128]{1,0:T(8,128)S(1)}, f32[8,128]{1,0:T(8,128)S(1)}, f32[8,128]{1,...) custom-call(s32[64]{0:T(128)S(1)} %fusion.index_ref, ...), custom_call_target="tpu_custom_call" | custom-call | flops 134217728 | bytes 7864320 | tf_op jit(solution)/shard_map/head_step/pallas_call | solution.py:306
  39.8 0.9 collective-permute-start.9
  40.7 1.1 collective-permute-start.10
  41.7 1.5 collective-permute-start.13
  43.2 3.2 %collective-permute-done.10.refs_3_ = bf16[16,32,128]{2,1,0:T(8,128)(2,1)S(1)} collective-permute-done((bf16[16,32,128]{2,1,0:T(8,128)(2,1)S(1)}, bf16[16,32,128]{2,1,0:T(8,128)(2,1)S(1)}, u32[]{:S(2)}, u32[]{:S(2)}) %collective-permute-start.10) | collective-permute-done | bytes 131104 | tf_op jit(solution)/shard_map/ppermute | solution.py:482
  46.6 1.6 %collective-permute-start.14 = (bf16[17,32,128]{2,1,0:T(8,128)(2,1)S(1)}, bf16[17,32,128]{2,1,0:T(8,128)(2,1)S(1)}, u32[]{:S(2)}, u32[]{:S(2)}) collective-permute-start(bf16[17,32,128]{2,1,0:T(8,128)(2,1)S(1)} %get-tuple-element.81.refs_3_), channel_id=1, source_target_pairs={{0,8},{1,5},{2,10},{3,7},{4,12},{5,1},{6,14},{7,3},{8,0},{9,13},{1... | collective-permute-start | bytes 417800 | tf_op jit(solution)/shard_map/ppermute | solution.py:482
  48.7 1.5 %collective-permute-start.11 = (bf16[16,32,128]{2,1,0:T(8,128)(2,1)S(1)}, bf16[16,32,128]{2,1,0:T(8,128)(2,1)S(1)}, u32[]{:S(2)}, u32[]{:S(2)}) collective-permute-start(bf16[16,32,128]{2,1,0:T(8,128)(2,1)S(1)} %get-tuple-element.77), channel_id=1, source_target_pairs={{0,4},{1,9},{2,6},{3,11},{4,0},{5,13},{6,2},{7,15},{8,12},{9,1},{1... | collective-permute-start | bytes 393224 | tf_op jit(solution)/shard_map/ppermute | solution.py:482
  50.3 2.5 %collective-permute-done.14.refs_2_ = bf16[17,32,128]{2,1,0:T(8,128)(2,1)S(1)} collective-permute-done((bf16[17,32,128]{2,1,0:T(8,128)(2,1)S(1)}, bf16[17,32,128]{2,1,0:T(8,128)(2,1)S(1)}, u32[]{:S(2)}, u32[]{:S(2)}) %collective-permute-start.14) | collective-permute-done | bytes 139296 | tf_op jit(solution)/shard_map/ppermute | solution.py:482
  53.2 1.0 bitcast_bitcast_fusion.demand_ref
  54.2 3.4 %copy-done.2 = bf16[64,4,128,128]{3,2,1,0:T(8,128)(2,1)S(1)} copy-done((bf16[64,4,128,128]{3,2,1,0:T(8,128)(2,1)S(1)}, bf16[64,4,128,128]{3,2,1,0:T(8,128)(2,1)}, u32[]{:S(2)}) %copy-start.2) | copy-done | bytes 8388632
  57.6 3.8 %local_forward.3.refs_5_ = f32[16,32,128]{2,1,0:T(8,128)S(1)} custom-call(s32[64,4]{1,0:T(8,128)S(1)} %copy.23.index_ref, bf16[32,8192]{1,0:T(8,128)(2,1)S(1)} %get-tuple-element.82.bar_ref, bf16[64,4,128,128]{3,2,1,0:T(8,128)(2,1)S(1)} %copy-done.2, f32[16,32,128]{2,1,0:T(8,128)S(1)} %bitcast_bitcast_fusion.1.duals_ref, ...), custom_call_target="tpu_custom_call" | custom-call | flops 100000 | bytes 100000 | tf_op jit(solution)/shard_map/local_forward/pallas_call | solution.py:408
  61.7 2.7 %collective-permute-start.19 = (bf16[16,32,128]{2,1,0:T(8,128)(2,1)S(1)}, bf16[16,32,128]{2,1,0:T(8,128)(2,1)S(1)}, u32[]{:S(2)}, u32[]{:S(2)}) collective-permute-start(bf16[16,32,128]{2,1,0:T(8,128)(2,1)S(1)} %get-tuple-element.86.panel_ref.refs_0_), channel_id=1, source_target_pairs={{0,16},{1,17},{2,18},{3,19},{4,20},{5,21},{6,22},{7,23},{8,24},{9,... | collective-permute-start | bytes 393224 | tf_op jit(solution)/shard_map/ppermute | solution.py:482
  64.4 1.1 collective-permute-start.17
  65.4 1.3 collective-permute-start.16
  66.8 4.8 %local_adjoint.4.refs_0_.refs_9_ = f32[32,8192]{1,0:T(8,128)S(1)} custom-call(s32[64,4]{1,0:T(8,128)S(1)} %copy.23.index_ref, bf16[16,32,128]{2,1,0:T(8,128)(2,1)S(1)} %get-tuple-element.86.panel_ref.refs_0_, bf16[64,4,128,128]{3,2,1,0:T(8,128)(2,1)S(1)} %bitcast.27), custom_call_target="tpu_custom_call" | custom-call | flops 100000 | bytes 100000 | tf_op jit(solution)/shard_map/local_adjoint/pallas_call | solution.py:274
  72.5 0.9 collective-permute-start.20
  73.3 1.2 collective-permute-start.18
  74.6 2.5 %collective-permute-done.21.refs_6_ = bf16[16,32,128]{2,1,0:T(8,128)(2,1)S(1)} collective-permute-done((bf16[16,32,128]{2,1,0:T(8,128)(2,1)S(1)}, bf16[16,32,128]{2,1,0:T(8,128)(2,1)S(1)}, u32[]{:S(2)}, u32[]{:S(2)}) %collective-permute-start.21) | collective-permute-done | bytes 131104 | tf_op jit(solution)/shard_map/ppermute | solution.py:482
  77.0 1.3 collective-permute-start.22
  78.4 1.5 collective-permute-start.23
  79.9 2.1 %collective-permute-done.23.refs_15_ = f32[8,128]{1,0:T(8,128)S(1)} collective-permute-done((f32[8,128]{1,0:T(8,128)S(1)}, f32[8,128]{1,0:T(8,128)S(1)}, u32[]{:S(2)}, u32[]{:S(2)}) %collective-permute-start.23) | collective-permute-done | bytes 4128 | tf_op jit(solution)/shard_map/ppermute | solution.py:468
  82.0 3.6 %head_step.4 = (f32[32,8192]{1,0:T(8,128)S(1)}, bf16[32,8192]{1,0:T(8,128)(2,1)S(1)}, f32[32,128]{1,0:T(8,128)S(1)}, f32[8,128]{1,0:T(8,128)S(1)}, f32[8,128]{1,...) custom-call(s32[64]{0:T(128)S(1)} %fusion.index_ref, ...), custom_call_target="tpu_custom_call" | custom-call | flops 134217728 | bytes 7864320 | tf_op jit(solution)/shard_map/head_step/pallas_call | solution.py:306
  85.6 1.4 collective-permute-start.24
  87.0 1.0 collective-permute-start.25
  88.0 4.0 %collective-permute-done.25.refs_3_ = bf16[16,32,128]{2,1,0:T(8,128)(2,1)S(1)} collective-permute-done((bf16[16,32,128]{2,1,0:T(8,128)(2,1)S(1)}, bf16[16,32,128]{2,1,0:T(8,128)(2,1)S(1)}, u32[]{:S(2)}, u32[]{:S(2)}) %collective-permute-start.25) | collective-permute-done | bytes 131104 | tf_op jit(solution)/shard_map/ppermute | solution.py:482
  92.1 1.1 collective-permute-start.29
  93.9 4.2 %collective-permute-done.28.refs_1_ = bf16[16,32,128]{2,1,0:T(8,128)(2,1)S(1)} collective-permute-done((bf16[16,32,128]{2,1,0:T(8,128)(2,1)S(1)}, bf16[16,32,128]{2,1,0:T(8,128)(2,1)S(1)}, u32[]{:S(2)}, u32[]{:S(2)}) %collective-permute-start.28) | collective-permute-done | bytes 131104 | tf_op jit(solution)/shard_map/ppermute | solution.py:482
  98.4 1.1 collective-permute-start.30
  99.5 1.0 collective-permute-start.27
  101.3 3.8 %local_forward.4.refs_5_ = f32[16,32,128]{2,1,0:T(8,128)S(1)} custom-call(s32[64,4]{1,0:T(8,128)S(1)} %copy.23.index_ref, bf16[32,8192]{1,0:T(8,128)(2,1)S(1)} %get-tuple-element.103.bar_ref, bf16[64,4,128,128]{3,2,1,0:T(8,128)(2,1)S(1)} %bitcast.27, f32[16,32,128]{2,1,0:T(8,128)S(1)} %get-tuple-element.104.duals_ref, ...), custom_call_target="tpu_custom_call" | custom-call | flops 100000 | bytes 100000 | tf_op jit(solution)/shard_map/local_forward/pallas_call | solution.py:408
  105.1 2.9 %collective-permute-done.27.refs_2_ = bf16[16,32,128]{2,1,0:T(8,128)(2,1)S(1)} collective-permute-done((bf16[16,32,128]{2,1,0:T(8,128)(2,1)S(1)}, bf16[16,32,128]{2,1,0:T(8,128)(2,1)S(1)}, u32[]{:S(2)}, u32[]{:S(2)}) %collective-permute-start.27) | collective-permute-done | bytes 131104 | tf_op jit(solution)/shard_map/ppermute | solution.py:482
  108.7 1.9 %collective-permute-start.32 = (bf16[16,32,128]{2,1,0:T(8,128)(2,1)S(1)}, bf16[16,32,128]{2,1,0:T(8,128)(2,1)S(1)}, u32[]{:S(2)}, u32[]{:S(2)}) collective-permute-start(bf16[16,32,128]{2,1,0:T(8,128)(2,1)S(1)} %get-tuple-element.109.panel_ref.refs_0_), channel_id=1, source_target_pairs={{0,8},{1,5},{2,10},{3,7},{4,12},{5,1},{6,14},{7,3},{8,0},{9,13},{1... | collective-permute-start | bytes 393224 | tf_op jit(solution)/shard_map/ppermute | solution.py:482
  110.5 1.2 collective-permute-start.31
  111.7 4.8 %local_adjoint.5.refs_0_.refs_9_ = f32[32,8192]{1,0:T(8,128)S(1)} custom-call(s32[64,4]{1,0:T(8,128)S(1)} %copy.23.index_ref, bf16[16,32,128]{2,1,0:T(8,128)(2,1)S(1)} %get-tuple-element.109.panel_ref.refs_0_, bf16[64,4,128,128]{3,2,1,0:T(8,128)(2,1)S(1)} %bitcast.27), custom_call_target="tpu_custom_call" | custom-call | flops 100000 | bytes 100000 | tf_op jit(solution)/shard_map/local_adjoint/pallas_call | solution.py:274
  116.7 1.7 %collective-permute-start.35 = (bf16[16,32,128]{2,1,0:T(8,128)(2,1)S(1)}, bf16[16,32,128]{2,1,0:T(8,128)(2,1)S(1)}, u32[]{:S(2)}, u32[]{:S(2)}) collective-permute-start(bf16[16,32,128]{2,1,0:T(8,128)(2,1)S(1)} %get-tuple-element.110.refs_4_), channel_id=1, source_target_pairs={{0,4},{1,9},{2,6},{3,11},{4,0},{5,13},{6,2},{7,15},{8,12},{9,1},{1... | collective-permute-start | bytes 393224 | tf_op jit(solution)/shard_map/ppermute | solution.py:482
  118.5 1.1 collective-permute-start.33
  119.5 2.1 %collective-permute-done.36.refs_6_ = bf16[16,32,128]{2,1,0:T(8,128)(2,1)S(1)} collective-permute-done((bf16[16,32,128]{2,1,0:T(8,128)(2,1)S(1)}, bf16[16,32,128]{2,1,0:T(8,128)(2,1)S(1)}, u32[]{:S(2)}, u32[]{:S(2)}) %collective-permute-start.36) | collective-permute-done | bytes 131104 | tf_op jit(solution)/shard_map/ppermute | solution.py:482
  121.6 0.8 collective-permute-start.37
  122.5 1.2 collective-permute-done.38.refs_15_
  123.6 3.0 %collective-permute-done.37.refs_7_ = bf16[16,32,128]{2,1,0:T(8,128)(2,1)S(1)} collective-permute-done((bf16[16,32,128]{2,1,0:T(8,128)(2,1)S(1)}, bf16[16,32,128]{2,1,0:T(8,128)(2,1)S(1)}, u32[]{:S(2)}, u32[]{:S(2)}) %collective-permute-start.37) | collective-permute-done | bytes 131104 | tf_op jit(solution)/shard_map/ppermute | solution.py:482
  126.6 4.2 %head_step.5 = (f32[32,8192]{1,0:T(8,128)}, bf16[32,8192]{1,0:T(8,128)(2,1)S(1)}, f32[32,128]{1,0:T(8,128)S(1)}, f32[8,128]{1,0:T(8,128)S(1)}, f32[8,128]{1,0:T(...) custom-call(s32[64]{0:T(128)S(1)} %fusion.index_ref, ...), custom_call_target="tpu_custom_call" | custom-call | flops 134217728 | bytes 7864320 | tf_op jit(solution)/shard_map/head_step/pallas_call | solution.py:306
  130.8 0.8 collective-permute-start.39
  131.7 1.0 collective-permute-start.40
  132.6 1.2 collective-permute-done.41
  133.8 2.8 %collective-permute-done.40.refs_3_ = bf16[16,32,128]{2,1,0:T(8,128)(2,1)S(1)} collective-permute-done((bf16[16,32,128]{2,1,0:T(8,128)(2,1)S(1)}, bf16[16,32,128]{2,1,0:T(8,128)(2,1)S(1)}, u32[]{:S(2)}, u32[]{:S(2)}) %collective-permute-start.40) | collective-permute-done | bytes 131104 | tf_op jit(solution)/shard_map/ppermute | solution.py:482
  136.8 1.0 collective-permute-start.45
  138.1 4.7 %collective-permute-done.44.refs_1_ = bf16[16,32,128]{2,1,0:T(8,128)(2,1)S(1)} collective-permute-done((bf16[16,32,128]{2,1,0:T(8,128)(2,1)S(1)}, bf16[16,32,128]{2,1,0:T(8,128)(2,1)S(1)}, u32[]{:S(2)}, u32[]{:S(2)}) %collective-permute-start.44) | collective-permute-done | bytes 131104 | tf_op jit(solution)/shard_map/ppermute | solution.py:482
  142.9 3.4 %collective-permute-start.46 = (bf16[17,32,128]{2,1,0:T(8,128)(2,1)S(1)}, bf16[17,32,128]{2,1,0:T(8,128)(2,1)S(1)}, u32[]{:S(2)}, u32[]{:S(2)}) collective-permute-start(bf16[17,32,128]{2,1,0:T(8,128)(2,1)S(1)} %get-tuple-element.126.after_ref.refs_4_), channel_id=1, source_target_pairs={{0,16},{1,17},{2,18},{3,19},{4,20},{5,21},{6,22},{7,23},{8,24},{9,... | collective-permute-start | bytes 417800 | tf_op jit(solution)/shard_map/ppermute | solution.py:482
  146.5 2.3 %collective-permute-start.47 = (f32[8,128]{1,0:T(8,128)S(1)}, f32[8,128]{1,0:T(8,128)S(1)}, u32[]{:S(2)}, u32[]{:S(2)}) collective-permute-start(f32[8,128]{1,0:T(8,128)S(1)} %get-tuple-element.132.refs_9_), channel_id=1, source_target_pairs={{0,2},{1,3},{2,0},{3,1},{4,6},{5,7},{6,4},{7,5},{8,10},{9,11},{10,... | collective-permute-start | bytes 12296 | tf_op jit(solution)/shard_map/ppermute | solution.py:468
  148.8 3.8 %local_forward.5.refs_5_ = f32[16,32,128]{2,1,0:T(8,128)S(1)} custom-call(s32[64,4]{1,0:T(8,128)S(1)} %copy.23.index_ref, bf16[32,8192]{1,0:T(8,128)(2,1)S(1)} %get-tuple-element.127.bar_ref, bf16[64,4,128,128]{3,2,1,0:T(8,128)(2,1)S(1)} %bitcast.27, f32[16,32,128]{2,1,0:T(8,128)S(1)} %get-tuple-element.128.duals_ref, ...), custom_call_target="tpu_custom_call" | custom-call | flops 100000 | bytes 100000 | tf_op jit(solution)/shard_map/local_forward/pallas_call | solution.py:408
  (87 shorter events, 9.8 us)
Async XLA Ops:
  0.6 1.0 copy-start
  0.6 28.6 %copy-start.7 = (s32[64]{0:T(128)S(1)}, s32[64]{0:T(128)}, u32[]{:S(2)}) copy-start(s32[64]{0:T(128)} %param.21) | copy-start | bytes 772
  0.7 33.0 %copy-start.5 = (f32[8192]{0:T(1024)S(1)}, f32[8192]{0:T(1024)}, u32[]{:S(2)}) copy-start(f32[8192]{0:T(1024)} %param.17) | copy-start | bytes 98308
  2.3 17.7 %collective-permute-start.3 = (bf16[16,32,128]{2,1,0:T(8,128)(2,1)}, bf16[16,32,128]{2,1,0:T(8,128)(2,1)}, u32[]{:S(2)}, u32[]{:S(2)}) collective-permute-start(bf16[16,32,128]{2,1,0:T(8,128)(2,1)} %fusion.2.panel_ref.refs_0_), channel_id=1, source_target_pairs={{0,16},{1,17},{2,18},{3,19},{4,20},{5,21},{6,22},{7,23},{8,24},{9,... | collective-permute-start | bytes 393224 | tf_op jit(solution)/shard_map/ppermute | solution.py:482
  6.3 13.7 %collective-permute-start.1 = (bf16[16,32,128]{2,1,0:T(8,128)(2,1)}, bf16[16,32,128]{2,1,0:T(8,128)(2,1)}, u32[]{:S(2)}, u32[]{:S(2)}) collective-permute-start(bf16[16,32,128]{2,1,0:T(8,128)(2,1)} %fusion.2.panel_ref.refs_0_), channel_id=1, source_target_pairs={{0,8},{1,5},{2,10},{3,7},{4,12},{5,1},{6,14},{7,3},{8,0},{9,13},{1... | collective-permute-start | bytes 393224 | tf_op jit(solution)/shard_map/ppermute | solution.py:482
  7.9 12.1 %collective-permute-start = (bf16[16,32,128]{2,1,0:T(8,128)(2,1)}, bf16[16,32,128]{2,1,0:T(8,128)(2,1)}, u32[]{:S(2)}, u32[]{:S(2)}) collective-permute-start(bf16[16,32,128]{2,1,0:T(8,128)(2,1)} %fusion.2.panel_ref.refs_0_), channel_id=1, source_target_pairs={{0,4},{1,9},{2,6},{3,11},{4,0},{5,13},{6,2},{7,15},{8,12},{9,1},{1... | collective-permute-start | bytes 393224 | tf_op jit(solution)/shard_map/ppermute | solution.py:482
  10.9 3.4 %copy-start.1 = (bf16[64,4,128,128]{3,2,1,0:T(8,128)(2,1)S(1)}, bf16[64,4,128,128]{3,2,1,0:T(8,128)(2,1)}, u32[]{:S(2)}) copy-start(bf16[64,4,128,128]{3,2,1,0:T(8,128)(2,1)} %blocks_ref.11) | copy-start | bytes 25165828
  14.3 19.4 %copy-start.3 = (bf16[64,128,128]{2,1,0:T(8,128)(2,1)S(1)}, bf16[64,128,128]{2,1,0:T(8,128)(2,1)}, u32[]{:S(2)}) copy-start(bf16[64,128,128]{2,1,0:T(8,128)(2,1)} %refs_8_.5) | copy-start | bytes 6291460
  21.6 6.2 %collective-permute-start.5 = (bf16[16,32,128]{2,1,0:T(8,128)(2,1)}, bf16[16,32,128]{2,1,0:T(8,128)(2,1)}, u32[]{:S(2)}, u32[]{:S(2)}) collective-permute-start(bf16[16,32,128]{2,1,0:T(8,128)(2,1)} %get-tuple-element.71.refs_4_), channel_id=1, source_target_pairs={{0,8},{1,5},{2,10},{3,7},{4,12},{5,1},{6,14},{7,3},{8,0},{9,13},{1... | collective-permute-start | bytes 393224 | tf_op jit(solution)/shard_map/ppermute | solution.py:482
  22.0 3.6 %collective-permute-start.7 = (f32[8,128]{1,0:T(8,128)S(1)}, f32[8,128]{1,0:T(8,128)S(1)}, u32[]{:S(2)}, u32[]{:S(2)}) collective-permute-start(f32[8,128]{1,0:T(8,128)S(1)} %sum_rows.1.sum_ref), channel_id=1, source_target_pairs={{0,2},{1,3},{2,0},{3,1},{4,6},{5,7},{6,4},{7,5},{8,10},{9,11},{10,... | collective-permute-start | bytes 12296 | tf_op jit(solution)/shard_map/ppermute | solution.py:468
  25.6 4.3 %collective-permute-start.8 = (f32[8,128]{1,0:T(8,128)S(1)}, f32[8,128]{1,0:T(8,128)S(1)}, u32[]{:S(2)}, u32[]{:S(2)}) collective-permute-start(f32[8,128]{1,0:T(8,128)S(1)} %add.26), channel_id=1, source_target_pairs={{0,1},{1,0},{2,3},{3,2},{4,5},{5,4},{6,7},{7,6},{8,9},{9,8},{10,11... | collective-permute-start | bytes 12296 | tf_op jit(solution)/shard_map/ppermute | solution.py:468
  25.6 7.1 %collective-permute-start.4 = (bf16[16,32,128]{2,1,0:T(8,128)(2,1)}, bf16[16,32,128]{2,1,0:T(8,128)(2,1)S(1)}, u32[]{:S(2)}, u32[]{:S(2)}) collective-permute-start(bf16[16,32,128]{2,1,0:T(8,128)(2,1)} %get-tuple-element.71.refs_4_), channel_id=1, source_target_pairs={{0,4},{1,9},{2,6},{3,11},{4,0},{5,13},{6,2},{7,15},{8,12},{9,1},{1... | collective-permute-start | bytes 393224 | tf_op jit(solution)/shard_map/ppermute | solution.py:482
  26.2 6.6 %collective-permute-start.2 = (bf16[16,32,128]{2,1,0:T(8,128)(2,1)}, bf16[16,32,128]{2,1,0:T(8,128)(2,1)S(1)}, u32[]{:S(2)}, u32[]{:S(2)}) collective-permute-start(bf16[16,32,128]{2,1,0:T(8,128)(2,1)} %collective-permute-done.refs_2_.refs_1_), channel_id=1, source_target_pairs={{0,8},{1,5},{2,10},{3,7},{4,12},{5,1},{6,14},{7,3},{8,0},{9,13},{1... | collective-permute-start | bytes 393224 | tf_op jit(solution)/shard_map/ppermute | solution.py:482
  27.7 5.9 %collective-permute-start.6 = (bf16[16,32,128]{2,1,0:T(8,128)(2,1)}, bf16[16,32,128]{2,1,0:T(8,128)(2,1)S(1)}, u32[]{:S(2)}, u32[]{:S(2)}) collective-permute-start(bf16[16,32,128]{2,1,0:T(8,128)(2,1)} %collective-permute-done.5.refs_6_), channel_id=1, source_target_pairs={{0,4},{1,9},{2,6},{3,11},{4,0},{5,13},{6,2},{7,15},{8,12},{9,1},{1... | collective-permute-start | bytes 393224 | tf_op jit(solution)/shard_map/ppermute | solution.py:482
  33.6 1.2 copy-start.4
  34.9 26.6 %copy-start.6 = (f32[32]{0:T(128)S(1)}, f32[32]{0:T(128)}, u32[]{:S(2)}) copy-start(f32[32]{0:T(128)} %param.14) | copy-start | bytes 388
  34.9 31.9 %slice-start = ((s8[8388608]{0:T(1024)(128)(4,1)}), s8[4194304]{0:T(1024)(128)(4,1)S(1)}, s32[]{:S(2)}) async-start(s8[8388608]{0:T(1024)(128)(4,1)} %bitcast.26), calls=%async_computation | async-start | bytes 8388608
  39.8 6.6 %collective-permute-start.9 = (bf16[17,32,128]{2,1,0:T(8,128)(2,1)S(1)}, bf16[17,32,128]{2,1,0:T(8,128)(2,1)S(1)}, u32[]{:S(2)}, u32[]{:S(2)}) collective-permute-start(bf16[17,32,128]{2,1,0:T(8,128)(2,1)S(1)} %get-tuple-element.74.refs_4_), channel_id=1, source_target_pairs={{0,4},{1,9},{2,6},{3,11},{4,0},{5,13},{6,2},{7,15},{8,12},{9,1},{1... | collective-permute-start | bytes 417800 | tf_op jit(solution)/shard_map/ppermute | solution.py:482
  40.7 5.8 %collective-permute-start.10 = (bf16[16,32,128]{2,1,0:T(8,128)(2,1)S(1)}, bf16[16,32,128]{2,1,0:T(8,128)(2,1)S(1)}, u32[]{:S(2)}, u32[]{:S(2)}) collective-permute-start(bf16[16,32,128]{2,1,0:T(8,128)(2,1)S(1)} %get-tuple-element.76), channel_id=1, source_target_pairs={{0,8},{1,5},{2,10},{3,7},{4,12},{5,1},{6,14},{7,3},{8,0},{9,13},{1... | collective-permute-start | bytes 393224 | tf_op jit(solution)/shard_map/ppermute | solution.py:482
  41.7 8.5 %collective-permute-start.13 = (bf16[16,32,128]{2,1,0:T(8,128)(2,1)S(1)}, bf16[16,32,128]{2,1,0:T(8,128)(2,1)S(1)}, u32[]{:S(2)}, u32[]{:S(2)}) collective-permute-start(bf16[16,32,128]{2,1,0:T(8,128)(2,1)S(1)} %get-tuple-element.80), channel_id=1, source_target_pairs={{0,4},{1,9},{2,6},{3,11},{4,0},{5,13},{6,2},{7,15},{8,12},{9,1},{1... | collective-permute-start | bytes 393224 | tf_op jit(solution)/shard_map/ppermute | solution.py:482
  46.6 6.2 %collective-permute-start.14 = (bf16[17,32,128]{2,1,0:T(8,128)(2,1)S(1)}, bf16[17,32,128]{2,1,0:T(8,128)(2,1)S(1)}, u32[]{:S(2)}, u32[]{:S(2)}) collective-permute-start(bf16[17,32,128]{2,1,0:T(8,128)(2,1)S(1)} %get-tuple-element.81.refs_3_), channel_id=1, source_target_pairs={{0,8},{1,5},{2,10},{3,7},{4,12},{5,1},{6,14},{7,3},{8,0},{9,13},{1... | collective-permute-start | bytes 417800 | tf_op jit(solution)/shard_map/ppermute | solution.py:482
  48.2 13.2 %collective-permute-start.12 = (bf16[16,32,128]{2,1,0:T(8,128)(2,1)S(1)}, bf16[16,32,128]{2,1,0:T(8,128)(2,1)S(1)}, u32[]{:S(2)}, u32[]{:S(2)}) collective-permute-start(bf16[16,32,128]{2,1,0:T(8,128)(2,1)S(1)} %get-tuple-element.78), channel_id=1, source_target_pairs={{0,8},{1,5},{2,10},{3,7},{4,12},{5,1},{6,14},{7,3},{8,0},{9,13},{1... | collective-permute-start | bytes 393224 | tf_op jit(solution)/shard_map/ppermute | solution.py:482
  48.7 12.7 %collective-permute-start.11 = (bf16[16,32,128]{2,1,0:T(8,128)(2,1)S(1)}, bf16[16,32,128]{2,1,0:T(8,128)(2,1)S(1)}, u32[]{:S(2)}, u32[]{:S(2)}) collective-permute-start(bf16[16,32,128]{2,1,0:T(8,128)(2,1)S(1)} %get-tuple-element.77), channel_id=1, source_target_pairs={{0,4},{1,9},{2,6},{3,11},{4,0},{5,13},{6,2},{7,15},{8,12},{9,1},{1... | collective-permute-start | bytes 393224 | tf_op jit(solution)/shard_map/ppermute | solution.py:482
  52.9 8.5 %collective-permute-start.15 = (bf16[17,32,128]{2,1,0:T(8,128)(2,1)S(1)}, bf16[17,32,128]{2,1,0:T(8,128)(2,1)S(1)}, u32[]{:S(2)}, u32[]{:S(2)}) collective-permute-start(bf16[17,32,128]{2,1,0:T(8,128)(2,1)S(1)} %fold.7.after_ref.refs_4_), channel_id=1, source_target_pairs={{0,16},{1,17},{2,18},{3,19},{4,20},{5,21},{6,22},{7,23},{8,24},{9,... | collective-permute-start | bytes 417800 | tf_op jit(solution)/shard_map/ppermute | solution.py:482
  54.2 3.4 %copy-start.2 = (bf16[64,4,128,128]{3,2,1,0:T(8,128)(2,1)S(1)}, bf16[64,4,128,128]{3,2,1,0:T(8,128)(2,1)}, u32[]{:S(2)}) copy-start(bf16[64,4,128,128]{3,2,1,0:T(8,128)(2,1)} %blocks_ref.11) | copy-start | bytes 25165828
  57.6 9.2 %slice-start.1 = ((s8[8388608]{0:T(1024)(128)(4,1)}), s8[4194304]{0:T(1024)(128)(4,1)S(1)}, s32[]{:S(2)}) async-start(s8[8388608]{0:T(1024)(128)(4,1)} %bitcast.26), calls=%async_computation.1 | async-start | bytes 8388608
  61.7 9.9 %collective-permute-start.19 = (bf16[16,32,128]{2,1,0:T(8,128)(2,1)S(1)}, bf16[16,32,128]{2,1,0:T(8,128)(2,1)S(1)}, u32[]{:S(2)}, u32[]{:S(2)}) collective-permute-start(bf16[16,32,128]{2,1,0:T(8,128)(2,1)S(1)} %get-tuple-element.86.panel_ref.refs_0_), channel_id=1, source_target_pairs={{0,16},{1,17},{2,18},{3,19},{4,20},{5,21},{6,22},{7,23},{8,24},{9,... | collective-permute-start | bytes 393224 | tf_op jit(solution)/shard_map/ppermute | solution.py:482
  64.4 7.2 %collective-permute-start.17 = (bf16[16,32,128]{2,1,0:T(8,128)(2,1)S(1)}, bf16[16,32,128]{2,1,0:T(8,128)(2,1)S(1)}, u32[]{:S(2)}, u32[]{:S(2)}) collective-permute-start(bf16[16,32,128]{2,1,0:T(8,128)(2,1)S(1)} %get-tuple-element.86.panel_ref.refs_0_), channel_id=1, source_target_pairs={{0,8},{1,5},{2,10},{3,7},{4,12},{5,1},{6,14},{7,3},{8,0},{9,13},{1... | collective-permute-start | bytes 393224 | tf_op jit(solution)/shard_map/ppermute | solution.py:482
  65.4 6.2 %collective-permute-start.16 = (bf16[16,32,128]{2,1,0:T(8,128)(2,1)S(1)}, bf16[16,32,128]{2,1,0:T(8,128)(2,1)S(1)}, u32[]{:S(2)}, u32[]{:S(2)}) collective-permute-start(bf16[16,32,128]{2,1,0:T(8,128)(2,1)S(1)} %get-tuple-element.86.panel_ref.refs_0_), channel_id=1, source_target_pairs={{0,4},{1,9},{2,6},{3,11},{4,0},{5,13},{6,2},{7,15},{8,12},{9,1},{1... | collective-permute-start | bytes 393224 | tf_op jit(solution)/shard_map/ppermute | solution.py:482
  71.6 5.4 %collective-permute-start.21 = (bf16[16,32,128]{2,1,0:T(8,128)(2,1)S(1)}, bf16[16,32,128]{2,1,0:T(8,128)(2,1)S(1)}, u32[]{:S(2)}, u32[]{:S(2)}) collective-permute-start(bf16[16,32,128]{2,1,0:T(8,128)(2,1)S(1)} %get-tuple-element.88.refs_4_), channel_id=1, source_target_pairs={{0,8},{1,5},{2,10},{3,7},{4,12},{5,1},{6,14},{7,3},{8,0},{9,13},{1... | collective-permute-start | bytes 393224 | tf_op jit(solution)/shard_map/ppermute | solution.py:482
  72.5 9.5 %collective-permute-start.20 = (bf16[16,32,128]{2,1,0:T(8,128)(2,1)S(1)}, bf16[16,32,128]{2,1,0:T(8,128)(2,1)S(1)}, u32[]{:S(2)}, u32[]{:S(2)}) collective-permute-start(bf16[16,32,128]{2,1,0:T(8,128)(2,1)S(1)} %get-tuple-element.88.refs_4_), channel_id=1, source_target_pairs={{0,4},{1,9},{2,6},{3,11},{4,0},{5,13},{6,2},{7,15},{8,12},{9,1},{1... | collective-permute-start | bytes 393224 | tf_op jit(solution)/shard_map/ppermute | solution.py:482
  73.3 8.7 %collective-permute-start.18 = (bf16[16,32,128]{2,1,0:T(8,128)(2,1)S(1)}, bf16[16,32,128]{2,1,0:T(8,128)(2,1)S(1)}, u32[]{:S(2)}, u32[]{:S(2)}) collective-permute-start(bf16[16,32,128]{2,1,0:T(8,128)(2,1)S(1)} %collective-permute-done.16.refs_2_.refs_1_), channel_id=1, source_target_pairs={{0,8},{1,5},{2,10},{3,7},{4,12},{5,1},{6,14},{7,3},{8,0},{9,13},{1... | collective-permute-start | bytes 393224 | tf_op jit(solution)/shard_map/ppermute | solution.py:482
  77.0 5.0 %collective-permute-start.22 = (bf16[16,32,128]{2,1,0:T(8,128)(2,1)S(1)}, bf16[16,32,128]{2,1,0:T(8,128)(2,1)S(1)}, u32[]{:S(2)}, u32[]{:S(2)}) collective-permute-start(bf16[16,32,128]{2,1,0:T(8,128)(2,1)S(1)} %collective-permute-done.21.refs_6_), channel_id=1, source_target_pairs={{0,4},{1,9},{2,6},{3,11},{4,0},{5,13},{6,2},{7,15},{8,12},{9,1},{1... | collective-permute-start | bytes 393224 | tf_op jit(solution)/shard_map/ppermute | solution.py:482
  78.4 3.6 %collective-permute-start.23 = (f32[8,128]{1,0:T(8,128)S(1)}, f32[8,128]{1,0:T(8,128)S(1)}, u32[]{:S(2)}, u32[]{:S(2)}) collective-permute-start(f32[8,128]{1,0:T(8,128)S(1)} %get-tuple-element.92.refs_14_), channel_id=1, source_target_pairs={{0,2},{1,3},{2,0},{3,1},{4,6},{5,7},{6,4},{7,5},{8,10},{9,11},{10,... | collective-permute-start | bytes 12296 | tf_op jit(solution)/shard_map/ppermute | solution.py:468
  85.6 6.3 %collective-permute-start.24 = (bf16[17,32,128]{2,1,0:T(8,128)(2,1)S(1)}, bf16[17,32,128]{2,1,0:T(8,128)(2,1)S(1)}, u32[]{:S(2)}, u32[]{:S(2)}) collective-permute-start(bf16[17,32,128]{2,1,0:T(8,128)(2,1)S(1)} %get-tuple-element.95.refs_4_), channel_id=1, source_target_pairs={{0,4},{1,9},{2,6},{3,11},{4,0},{5,13},{6,2},{7,15},{8,12},{9,1},{1... | collective-permute-start | bytes 417800 | tf_op jit(solution)/shard_map/ppermute | solution.py:482
  87.0 5.0 %collective-permute-start.25 = (bf16[16,32,128]{2,1,0:T(8,128)(2,1)S(1)}, bf16[16,32,128]{2,1,0:T(8,128)(2,1)S(1)}, u32[]{:S(2)}, u32[]{:S(2)}) collective-permute-start(bf16[16,32,128]{2,1,0:T(8,128)(2,1)S(1)} %get-tuple-element.97), channel_id=1, source_target_pairs={{0,8},{1,5},{2,10},{3,7},{4,12},{5,1},{6,14},{7,3},{8,0},{9,13},{1... | collective-permute-start | bytes 393224 | tf_op jit(solution)/shard_map/ppermute | solution.py:482
  92.1 6.2 %collective-permute-start.29 = (bf16[17,32,128]{2,1,0:T(8,128)(2,1)S(1)}, bf16[17,32,128]{2,1,0:T(8,128)(2,1)S(1)}, u32[]{:S(2)}, u32[]{:S(2)}) collective-permute-start(bf16[17,32,128]{2,1,0:T(8,128)(2,1)S(1)} %get-tuple-element.102.refs_3_), channel_id=1, source_target_pairs={{0,8},{1,5},{2,10},{3,7},{4,12},{5,1},{6,14},{7,3},{8,0},{9,13},{1... | collective-permute-start | bytes 417800 | tf_op jit(solution)/shard_map/ppermute | solution.py:482
  93.1 5.0 %collective-permute-start.28 = (bf16[16,32,128]{2,1,0:T(8,128)(2,1)S(1)}, bf16[16,32,128]{2,1,0:T(8,128)(2,1)S(1)}, u32[]{:S(2)}, u32[]{:S(2)}) collective-permute-start(bf16[16,32,128]{2,1,0:T(8,128)(2,1)S(1)} %get-tuple-element.101), channel_id=1, source_target_pairs={{0,4},{1,9},{2,6},{3,11},{4,0},{5,13},{6,2},{7,15},{8,12},{9,1},{1... | collective-permute-start | bytes 393224 | tf_op jit(solution)/shard_map/ppermute | solution.py:482
  98.4 9.7 %collective-permute-start.30 = (bf16[17,32,128]{2,1,0:T(8,128)(2,1)S(1)}, bf16[17,32,128]{2,1,0:T(8,128)(2,1)S(1)}, u32[]{:S(2)}, u32[]{:S(2)}) collective-permute-start(bf16[17,32,128]{2,1,0:T(8,128)(2,1)S(1)} %fold.9.after_ref.refs_4_), channel_id=1, source_target_pairs={{0,16},{1,17},{2,18},{3,19},{4,20},{5,21},{6,22},{7,23},{8,24},{9,... | collective-permute-start | bytes 417800 | tf_op jit(solution)/shard_map/ppermute | solution.py:482
  99.5 8.5 %collective-permute-start.27 = (bf16[16,32,128]{2,1,0:T(8,128)(2,1)S(1)}, bf16[16,32,128]{2,1,0:T(8,128)(2,1)S(1)}, u32[]{:S(2)}, u32[]{:S(2)}) collective-permute-start(bf16[16,32,128]{2,1,0:T(8,128)(2,1)S(1)} %get-tuple-element.99), channel_id=1, source_target_pairs={{0,8},{1,5},{2,10},{3,7},{4,12},{5,1},{6,14},{7,3},{8,0},{9,13},{1... | collective-permute-start | bytes 393224 | tf_op jit(solution)/shard_map/ppermute | solution.py:482
  100.5 7.5 %collective-permute-start.26 = (bf16[16,32,128]{2,1,0:T(8,128)(2,1)S(1)}, bf16[16,32,128]{2,1,0:T(8,128)(2,1)S(1)}, u32[]{:S(2)}, u32[]{:S(2)}) collective-permute-start(bf16[16,32,128]{2,1,0:T(8,128)(2,1)S(1)} %get-tuple-element.98), channel_id=1, source_target_pairs={{0,4},{1,9},{2,6},{3,11},{4,0},{5,13},{6,2},{7,15},{8,12},{9,1},{1... | collective-permute-start | bytes 393224 | tf_op jit(solution)/shard_map/ppermute | solution.py:482
  108.7 7.9 %collective-permute-start.34 = (bf16[16,32,128]{2,1,0:T(8,128)(2,1)S(1)}, bf16[16,32,128]{2,1,0:T(8,128)(2,1)S(1)}, u32[]{:S(2)}, u32[]{:S(2)}) collective-permute-start(bf16[16,32,128]{2,1,0:T(8,128)(2,1)S(1)} %get-tuple-element.109.panel_ref.refs_0_), channel_id=1, source_target_pairs={{0,16},{1,17},{2,18},{3,19},{4,20},{5,21},{6,22},{7,23},{8,24},{9,... | collective-permute-start | bytes 393224 | tf_op jit(solution)/shard_map/ppermute | solution.py:482
  108.7 7.9 %collective-permute-start.32 = (bf16[16,32,128]{2,1,0:T(8,128)(2,1)S(1)}, bf16[16,32,128]{2,1,0:T(8,128)(2,1)S(1)}, u32[]{:S(2)}, u32[]{:S(2)}) collective-permute-start(bf16[16,32,128]{2,1,0:T(8,128)(2,1)S(1)} %get-tuple-element.109.panel_ref.refs_0_), channel_id=1, source_target_pairs={{0,8},{1,5},{2,10},{3,7},{4,12},{5,1},{6,14},{7,3},{8,0},{9,13},{1... | collective-permute-start | bytes 393224 | tf_op jit(solution)/shard_map/ppermute | solution.py:482
  110.5 6.0 %collective-permute-start.31 = (bf16[16,32,128]{2,1,0:T(8,128)(2,1)S(1)}, bf16[16,32,128]{2,1,0:T(8,128)(2,1)S(1)}, u32[]{:S(2)}, u32[]{:S(2)}) collective-permute-start(bf16[16,32,128]{2,1,0:T(8,128)(2,1)S(1)} %get-tuple-element.109.panel_ref.refs_0_), channel_id=1, source_target_pairs={{0,4},{1,9},{2,6},{3,11},{4,0},{5,13},{6,2},{7,15},{8,12},{9,1},{1... | collective-permute-start | bytes 393224 | tf_op jit(solution)/shard_map/ppermute | solution.py:482
  116.6 5.0 %collective-permute-start.36 = (bf16[16,32,128]{2,1,0:T(8,128)(2,1)S(1)}, bf16[16,32,128]{2,1,0:T(8,128)(2,1)S(1)}, u32[]{:S(2)}, u32[]{:S(2)}) collective-permute-start(bf16[16,32,128]{2,1,0:T(8,128)(2,1)S(1)} %get-tuple-element.110.refs_4_), channel_id=1, source_target_pairs={{0,8},{1,5},{2,10},{3,7},{4,12},{5,1},{6,14},{7,3},{8,0},{9,13},{1... | collective-permute-start | bytes 393224 | tf_op jit(solution)/shard_map/ppermute | solution.py:482
  116.7 6.9 %collective-permute-start.35 = (bf16[16,32,128]{2,1,0:T(8,128)(2,1)S(1)}, bf16[16,32,128]{2,1,0:T(8,128)(2,1)S(1)}, u32[]{:S(2)}, u32[]{:S(2)}) collective-permute-start(bf16[16,32,128]{2,1,0:T(8,128)(2,1)S(1)} %get-tuple-element.110.refs_4_), channel_id=1, source_target_pairs={{0,4},{1,9},{2,6},{3,11},{4,0},{5,13},{6,2},{7,15},{8,12},{9,1},{1... | collective-permute-start | bytes 393224 | tf_op jit(solution)/shard_map/ppermute | solution.py:482
  118.5 5.2 %collective-permute-start.33 = (bf16[16,32,128]{2,1,0:T(8,128)(2,1)S(1)}, bf16[16,32,128]{2,1,0:T(8,128)(2,1)S(1)}, u32[]{:S(2)}, u32[]{:S(2)}) collective-permute-start(bf16[16,32,128]{2,1,0:T(8,128)(2,1)S(1)} %collective-permute-done.31.refs_2_.refs_1_), channel_id=1, source_target_pairs={{0,8},{1,5},{2,10},{3,7},{4,12},{5,1},{6,14},{7,3},{8,0},{9,13},{1... | collective-permute-start | bytes 393224 | tf_op jit(solution)/shard_map/ppermute | solution.py:482
  121.6 5.0 %collective-permute-start.37 = (bf16[16,32,128]{2,1,0:T(8,128)(2,1)S(1)}, bf16[16,32,128]{2,1,0:T(8,128)(2,1)S(1)}, u32[]{:S(2)}, u32[]{:S(2)}) collective-permute-start(bf16[16,32,128]{2,1,0:T(8,128)(2,1)S(1)} %collective-permute-done.36.refs_6_), channel_id=1, source_target_pairs={{0,4},{1,9},{2,6},{3,11},{4,0},{5,13},{6,2},{7,15},{8,12},{9,1},{1... | collective-permute-start | bytes 393224 | tf_op jit(solution)/shard_map/ppermute | solution.py:482
  122.5 1.2 collective-permute-start.38
  130.8 5.8 %collective-permute-start.39 = (bf16[17,32,128]{2,1,0:T(8,128)(2,1)S(1)}, bf16[17,32,128]{2,1,0:T(8,128)(2,1)S(1)}, u32[]{:S(2)}, u32[]{:S(2)}) collective-permute-start(bf16[17,32,128]{2,1,0:T(8,128)(2,1)S(1)} %get-tuple-element.117.refs_4_), channel_id=1, source_target_pairs={{0,4},{1,9},{2,6},{3,11},{4,0},{5,13},{6,2},{7,15},{8,12},{9,1},{1... | collective-permute-start | bytes 417800 | tf_op jit(solution)/shard_map/ppermute | solution.py:482
  131.7 5.0 %collective-permute-start.40 = (bf16[16,32,128]{2,1,0:T(8,128)(2,1)S(1)}, bf16[16,32,128]{2,1,0:T(8,128)(2,1)S(1)}, u32[]{:S(2)}, u32[]{:S(2)}) collective-permute-start(bf16[16,32,128]{2,1,0:T(8,128)(2,1)S(1)} %get-tuple-element.119), channel_id=1, source_target_pairs={{0,8},{1,5},{2,10},{3,7},{4,12},{5,1},{6,14},{7,3},{8,0},{9,13},{1... | collective-permute-start | bytes 393224 | tf_op jit(solution)/shard_map/ppermute | solution.py:482
  132.6 1.2 collective-permute-start.41
  136.8 6.0 %collective-permute-start.45 = (bf16[17,32,128]{2,1,0:T(8,128)(2,1)S(1)}, bf16[17,32,128]{2,1,0:T(8,128)(2,1)S(1)}, u32[]{:S(2)}, u32[]{:S(2)}) collective-permute-start(bf16[17,32,128]{2,1,0:T(8,128)(2,1)S(1)} %get-tuple-element.125.refs_3_), channel_id=1, source_target_pairs={{0,8},{1,5},{2,10},{3,7},{4,12},{5,1},{6,14},{7,3},{8,0},{9,13},{1... | collective-permute-start | bytes 417800 | tf_op jit(solution)/shard_map/ppermute | solution.py:482
  137.8 5.0 %collective-permute-start.44 = (bf16[16,32,128]{2,1,0:T(8,128)(2,1)S(1)}, bf16[16,32,128]{2,1,0:T(8,128)(2,1)S(1)}, u32[]{:S(2)}, u32[]{:S(2)}) collective-permute-start(bf16[16,32,128]{2,1,0:T(8,128)(2,1)S(1)} %get-tuple-element.124), channel_id=1, source_target_pairs={{0,4},{1,9},{2,6},{3,11},{4,0},{5,13},{6,2},{7,15},{8,12},{9,1},{1... | collective-permute-start | bytes 393224 | tf_op jit(solution)/shard_map/ppermute | solution.py:482
  142.9 9.8 %collective-permute-start.46 = (bf16[17,32,128]{2,1,0:T(8,128)(2,1)S(1)}, bf16[17,32,128]{2,1,0:T(8,128)(2,1)S(1)}, u32[]{:S(2)}, u32[]{:S(2)}) collective-permute-start(bf16[17,32,128]{2,1,0:T(8,128)(2,1)S(1)} %get-tuple-element.126.after_ref.refs_4_), channel_id=1, source_target_pairs={{0,16},{1,17},{2,18},{3,19},{4,20},{5,21},{6,22},{7,23},{8,24},{9,... | collective-permute-start | bytes 417800 | tf_op jit(solution)/shard_map/ppermute | solution.py:482
  146.3 6.4 %collective-permute-start.43 = (bf16[16,32,128]{2,1,0:T(8,128)(2,1)S(1)}, bf16[16,32,128]{2,1,0:T(8,128)(2,1)S(1)}, u32[]{:S(2)}, u32[]{:S(2)}) collective-permute-start(bf16[16,32,128]{2,1,0:T(8,128)(2,1)S(1)} %get-tuple-element.122), channel_id=1, source_target_pairs={{0,8},{1,5},{2,10},{3,7},{4,12},{5,1},{6,14},{7,3},{8,0},{9,13},{1... | collective-permute-start | bytes 393224 | tf_op jit(solution)/shard_map/ppermute | solution.py:482
  146.5 6.2 %collective-permute-start.42 = (bf16[16,32,128]{2,1,0:T(8,128)(2,1)S(1)}, bf16[16,32,128]{2,1,0:T(8,128)(2,1)S(1)}, u32[]{:S(2)}, u32[]{:S(2)}) collective-permute-start(bf16[16,32,128]{2,1,0:T(8,128)(2,1)S(1)} %get-tuple-element.121), channel_id=1, source_target_pairs={{0,4},{1,9},{2,6},{3,11},{4,0},{5,13},{6,2},{7,15},{8,12},{9,1},{1... | collective-permute-start | bytes 393224 | tf_op jit(solution)/shard_map/ppermute | solution.py:482
  146.5 6.1 %collective-permute-start.47 = (f32[8,128]{1,0:T(8,128)S(1)}, f32[8,128]{1,0:T(8,128)S(1)}, u32[]{:S(2)}, u32[]{:S(2)}) collective-permute-start(f32[8,128]{1,0:T(8,128)S(1)} %get-tuple-element.132.refs_9_), channel_id=1, source_target_pairs={{0,2},{1,3},{2,0},{3,1},{4,6},{5,7},{6,4},{7,5},{8,10},{9,11},{10,... | collective-permute-start | bytes 12296 | tf_op jit(solution)/shard_map/ppermute | solution.py:468

commit v5 on v4

--- a/solution.py
+++ b/solution.py
@@ -17,7 +17,6 @@
 MIB = 1024 * 1024
 GROUP = 8
 HEAD_GROUP = 16
-KERNEL_COST = 100000
 
 
 def contract_last(left, right):
@@ -27,14 +26,14 @@
 
 
 def local_adjoint_kernel(
-    touches, group, index_ref, panel_ref, blocks_ref, *refs
+    touches, group, index_ref, panel_ref, blocks_ref, out_ref, token_ref
 ):
-    out_ref = refs[-1]
+    token_ref[...] = jnp.zeros_like(token_ref)
     rows = blocks_ref.shape[-1]
     first = pl.program_id(0) * group
     for member in range(group):
         left = jnp.concatenate(
-            [panel_ref[index_ref[first + member, k]] for k in range(touches)], axis=1
+            [panel_ref[index_ref[k, first + member]] for k in range(touches)], axis=1
         )
         right = jnp.concatenate([blocks_ref[member, k] for k in range(touches)], axis=1)
         out_ref[:, member * rows : (member + 1) * rows] = contract_last(left, right)
@@ -202,7 +201,7 @@
         risk_out[...] = risk_new
         excess_out[...] = excess_new
         return
-    risk_total = sum_ref[...] if kind == "first" else sum_ref[...] + other_ref[...]
+    risk_total = sum_ref[...] + other_ref[...]
     level_new, level_bar = next_level(level_ref[...], risk_total, scen_total)
     risk_new = jnp.maximum(risk_new - risk_step * level_bar[:1], 0.0)
     if kind == "last":
@@ -245,12 +244,14 @@
             preferred_element_type=jnp.float32,
         )
         for k in range(touches):
-            place = index_ref[first + member, k]
+            place = index_ref[k, first + member]
             total[place] += products[:, k * rows : (k + 1) * rows]
 
     @pl.when(step == steps - 1)
     def _():
-        out_ref[...] = duals_ref[...] + dual_step * (demand_ref[...] - total[...])
+        for block in range(total.shape[0]):
+            demand = demand_ref[:, block * rows : (block + 1) * rows]
+            out_ref[block] = duals_ref[block] + dual_step * (demand - total[block])
 
 
 def whole(*shape):
@@ -267,29 +268,34 @@
     )
 
 
-def local_adjoint(index, panel, blocks, after):
+def local_adjoint(index, panel, blocks):
     arc_blks, touches, rows, _ = blocks.shape
     scen_rows = panel.shape[1]
     group = GROUP
     return pl.pallas_call(
         functools.partial(local_adjoint_kernel, touches, group),
-        out_shape=jax.ShapeDtypeStruct((scen_rows, arc_blks * rows), jnp.float32),
+        out_shape=(
+            jax.ShapeDtypeStruct((scen_rows, arc_blks * rows), jnp.float32),
+            jax.ShapeDtypeStruct((8, rows), jnp.float32),
+        ),
         grid_spec=pltpu.PrefetchScalarGridSpec(
             num_scalar_prefetch=1,
             grid=(arc_blks // group,),
             in_specs=[
                 whole(*panel.shape),
                 pl.BlockSpec((group, touches, rows, rows), lambda i, *_: (i, 0, 0, 0)),
-            ]
-            + [pl.BlockSpec(memory_space=pl.ANY)] * len(after),
-            out_specs=pl.BlockSpec((scen_rows, group * rows), lambda i, *_: (0, i)),
+            ],
+            out_specs=(
+                pl.BlockSpec((scen_rows, group * rows), lambda i, *_: (0, i)),
+                whole(8, rows),
+            ),
         ),
         compiler_params=params(),
         cost_estimate=pl.CostEstimate(
-            flops=KERNEL_COST, bytes_accessed=KERNEL_COST, transcendentals=0
+            flops=2 * scen_rows * blocks.size, bytes_accessed=2 * blocks.size, transcendentals=0
         ),
         name="local_adjoint",
-    )(index, panel, blocks, *after)
+    )(index, panel, blocks)
 
 
 def head_step(places, panels, heads, pulled, flows, costs, risk, level, sums, late, scen_total):
@@ -415,7 +421,7 @@
                 pl.BlockSpec((scen_rows, group * rows), lambda i, *_: (0, i)),
                 pl.BlockSpec((group, touches, rows, rows), lambda i, *_: (i, 0, 0, 0)),
                 whole(*duals.shape),
-                whole(*duals.shape),
+                whole(*demand.shape),
                 pl.BlockSpec(memory_space=pl.ANY),
             ],
             out_specs=whole(*duals.shape),
@@ -423,7 +429,7 @@
         ),
         compiler_params=params(),
         cost_estimate=pl.CostEstimate(
-            flops=KERNEL_COST, bytes_accessed=KERNEL_COST, transcendentals=0
+            flops=2 * scen_rows * blocks.size, bytes_accessed=2 * blocks.size, transcendentals=0
         ),
         name="local_forward",
     )(index, bar, blocks, duals, demand, after)
@@ -450,17 +456,27 @@
     )(arrived, risk_sum, *after)
 
 
-def sum_rows(values, shape):
-    def kernel(values_ref, out_ref):
-        out_ref[...] = add_rows(values_ref[...], shape)
-
+def prepare_kernel(risk_ref, excess_ref, level_ref, after, risk_out, excess_out, level_out, sum_out):
+    scen_rows = risk_out.shape[0]
+    square = (scen_rows, scen_rows)
+    same = lax.broadcasted_iota(jnp.int32, square, 0) == lax.broadcasted_iota(jnp.int32, square, 1)
+    for row_ref, out in ((risk_ref, risk_out), (excess_ref, excess_out)):
+        column = jnp.sum(jnp.where(same, row_ref[...], 0.0), axis=1, keepdims=True)
+        out[...] = jnp.broadcast_to(column, out.shape)
+    level_out[...] = jnp.broadcast_to(level_ref[...], level_out.shape)
+    sum_out[...] = add_rows(risk_out[...], sum_out.shape)
+
+
+def prepare(risk, excess, level, rows, after):
+    wide, flat = (risk.shape[0], rows), (8, rows)
     return pl.pallas_call(
-        kernel,
-        out_shape=jax.ShapeDtypeStruct(shape, jnp.float32),
+        prepare_kernel,
+        out_shape=[jax.ShapeDtypeStruct(shape, jnp.float32) for shape in (wide, wide, flat, flat)],
+        in_specs=[pl.BlockSpec(memory_space=pltpu.VMEM)] * 3 + [pl.BlockSpec(memory_space=pl.ANY)],
         compiler_params=pltpu.CompilerParams(vmem_limit_bytes=vmem_limit(8)),
-        cost_estimate=small_cost(values),
-        name="sum_rows",
-    )(values)
+        cost_estimate=small_cost(risk),
+        name="prepare",
+    )(risk.reshape(1, -1), excess.reshape(1, -1), level.reshape(1, 1), after)
 
 
 def swap(value, axis, distance):
@@ -491,8 +507,7 @@
         panels[distance] = swap_net(panels[distance ^ hop], hop)
         if distance == 1:
             far = peers // 2
-            firsts = tuple(panels[k] for k in order if k.bit_count() == 1 and k != far)
-            panels[far], risk_sum = relay(panels[far], risk_sum, after + firsts)
+            panels[far], risk_sum = relay(panels[far], risk_sum, after)
     return panels, risk_sum
 
 
@@ -516,42 +531,31 @@
     arc_total = arc_flows.shape[1] * net_size
     scen_total = scen_rows * lax.axis_size("scen")
     costs = arc_costs.reshape(1, -1)
+    touched = local_index.T
     distance = jnp.bitwise_xor(head_index // node_blks, lax.axis_index("net"))
     distance = jnp.where(lax.axis_index("scen") % 2 == 1, exchange_lowest(distance), distance)
     places = distance * node_blks + head_index % node_blks
     scen_size = lax.axis_size("scen")
-    wide = (scen_rows, rows)
-    flat = (8, rows)
-
-    def to_blocks(panel):
-        return panel.reshape(scen_rows, node_blks, rows).transpose(1, 0, 2)
-
-    duals = to_blocks(node_duals)
+    duals = node_duals.reshape(scen_rows, node_blks, rows).transpose(1, 0, 2)
     half = duals.astype(jnp.bfloat16)
-    wanted = to_blocks(demand)
+    risk_sum = jnp.zeros((8, rows), jnp.float32)
     flows = arc_flows
-    excess_now = jnp.broadcast_to(excess[:, None], wide)
-    risk = jnp.broadcast_to(risk_duals[:, None], wide)
-    level = jnp.broadcast_to(threshold[:, None], flat)
-    risk_sum = sum_rows(risk, flat)
     early = [1 << bit for bit in range(1, scen_size.bit_length() - 1)][::-1]
     zero = jnp.zeros_like(risk_sum)
     for iteration in range(ROUNDS):
         kind = "first" if iteration == 0 else "last" if iteration == ROUNDS - 1 else "early"
-        pulled = local_adjoint(local_index, half, local_blocks, ())
+        pulled, token = local_adjoint(touched, half, local_blocks)
+        panels, risk_sum = gather_panels(half, risk_sum, (token,))
         if kind == "first":
-            panels, _ = gather_panels(half, risk_sum, (pulled,))
-            for stride in early + [1]:
+            risk, excess_now, level, risk_sum = prepare(
+                risk_duals, excess, threshold, rows, panels[net_size // 2]
+            )
+        if kind == "early":
+            for stride in early[:-1]:
                 risk_sum = risk_sum + swap(risk_sum, "scen", stride)
-            sums = (risk_sum, zero)
+            sums = (risk_sum, swap(risk_sum, "scen", early[-1]))
         else:
-            panels, risk_sum = gather_panels(half, risk_sum, (pulled,))
-            if kind == "early":
-                for stride in early[:-1]:
-                    risk_sum = risk_sum + swap(risk_sum, "scen", stride)
-                sums = (risk_sum, swap(risk_sum, "scen", early[-1]))
-            else:
-                sums = (risk_sum, swap(risk_sum, "scen", 1))
+            sums = (risk_sum, swap(risk_sum, "scen", 1))
         flows, bar, risk, level, risk_sum, kept, sends = head_step(
             places,
             panels,
@@ -572,13 +576,15 @@
         tops = sorted(inner(net_size), key=lambda k: (-k.bit_count(), -k))[:-1]
         groups = [(tops[0], 1)] + [(top,) for top in tops[1:] if top != 1]
         loss, loss_top = sends[net_size - 1], net_size - 1
+        direct = swap_net(sends[2], 2)
+        after += (direct,)
         for group in groups:
             terms = []
             for top in group:
                 below = sorted(children(top, net_size))
                 terms.append((kept[top], [swap_net(sends[k], last_hop(k)) for k in below]))
             chain = loss_top ^ last_hop(loss_top) == group[0]
-            extras = (risk_sum,) if group[0] == net_size // 2 and kind == "last" else ()
+            extras = (risk_sum,) if group[0] == net_size // 2 and kind != "early" else ()
             folded, passed = fold(terms, loss if chain else None, extras, after)
             sends.update(zip(group, folded))
             after = ()
@@ -586,11 +592,11 @@
                 loss_top, loss = group[0], folded[0]
             if extras:
                 (risk_sum,) = passed
-        base = local_forward(local_index, bar, local_blocks, duals, wanted, loss)
+        base = local_forward(touched, bar, local_blocks, duals, demand, loss)
         below = sorted(children(0, net_size))
-        arrived = [swap_net(sends[k], last_hop(k)) for k in below]
+        arrived = [direct if k == 2 else swap_net(sends[k], last_hop(k)) for k in below]
         sums = (risk_sum, zero)
-        if kind == "last":
+        if kind != "early":
             for stride in early[:-1]:
                 risk_sum = risk_sum + swap(risk_sum, "scen", stride)
             sums = (risk_sum, swap(risk_sum, "scen", early[-1]))

time: 154 us -> 149 us (0.968)
  Pallas kernels: 43.5 us -> 37.3 us
  waiting for transfers between devices: 42.3 us -> 43.9 us
    ppermute x42, waiting for transfers between devices: 35.8 us -> 40.2 us  [swap_net(): return lax.ppermute(value, ('net', 'scen'), pairs)]
    ppermute x6, waiting for transfers between devices: 6.51 us -> 3.68 us  [swap(): return lax.ppermute(value, axis, [(i, i ^ distance) for i in range(size)])]
    ppermute x42, starting transfers between devices: 48.6 us -> 51.1 us  [swap_net(): return lax.ppermute(value, ('net', 'scen'), pairs)]
    pallas_call x3, Pallas kernels: 15.3 us -> 12.9 us  [local_adjoint(): pl.pallas_call(functools.partial(local_adjoint_kernel, touches, group), o...]
    unnamed x21 -> x32, local copies, waits for them, and re-layouts: 9.7 us -> 11.9 us
    ppermute x6, starting transfers between devices: 5.33 us -> 3.3 us  [swap(): return lax.ppermute(value, axis, [(i, i ^ distance) for i in range(size)])]
  transfers between devices with their start and end apart: 48 -> 48, of which waited for: 17 -> 27; matrix products, arithmetic and copies ran while one was open for 2% -> 0% of each run, Pallas kernels for 18% -> 16%
where the time goes in v5:
time: 149 us
  starting transfers between devices  54.4 us (37%)
  waiting for transfers between devices  43.9 us (29%)
  Pallas kernels  37.3 us (25%)
  local copies, waits for them, and re-layouts  11.9 us (8%)
  between operations  1.54 us (1%)
    ppermute x42, starting transfers between devices, swap_net(): return lax.ppermute(value, ('net', 'scen'), pairs)  51.1 us
    ppermute x42, waiting for transfers between devices, swap_net(): return lax.ppermute(value, ('net', 'scen'), pairs)  40.2 us
    pallas_call x3, Pallas kernels, local_adjoint(): pl.pallas_call(functools.partial(local_adjoint_kernel, touches, group), o...  12.9 us
    unnamed x32, local copies, waits for them, and re-layouts  11.9 us
    pallas_call x3, Pallas kernels, head_step(): pl.pallas_call(functools.partial(head_kernel, group, steps, peers, late,...  11.4 us
    pallas_call x3, Pallas kernels, local_forward(): pl.pallas_call(functools.partial(local_forward_kernel, touches, group, st...  9.95 us
    ppermute x6, waiting for transfers between devices, swap(): return lax.ppermute(value, axis, [(i, i ^ distance) for i in range(size)])  3.68 us
    ppermute x6, starting transfers between devices, swap(): return lax.ppermute(value, axis, [(i, i ^ distance) for i in range(size)])  3.3 us
  transfers between devices with their start and end apart: 48, of which 27 were waited for; matrix products, arithmetic and copies ran while one was open for 0% of the time, Pallas kernels for 16%

profile of v5, /device:TPU:0, one launch (start us, length us, event | category | flops | bytes accessed | tf_op | source)
XLA Modules:
  0.0 149.1 jit_solution(10699796013028224677)
XLA Ops:
  0.7 1.0 copy-done
  1.7 4.1 %collective-permute-start.3 = (bf16[16,32,128]{2,1,0:T(8,128)(2,1)S(1)}, bf16[16,32,128]{2,1,0:T(8,128)(2,1)S(1)}, u32[]{:S(2)}, u32[]{:S(2)}) collective-permute-start(bf16[16,32,128]{2,1,0:T(8,128)(2,1)S(1)} %fusion.2.panel_ref.refs_0_), channel_id=1, source_target_pairs={{0,16},{1,17},{2,18},{3,19},{4,20},{5,21},{6,22},{7,23},{8,24},{9,... | collective-permute-start | bytes 393224 | tf_op jit(solution)/shard_map/ppermute | solution.py:498
  5.8 1.5 collective-permute-start
  7.3 3.4 %copy-done.1 = bf16[64,4,128,128]{3,2,1,0:T(8,128)(2,1)S(1)} copy-done((bf16[64,4,128,128]{3,2,1,0:T(8,128)(2,1)S(1)}, bf16[64,4,128,128]{3,2,1,0:T(8,128)(2,1)}, u32[]{:S(2)}) %copy-start.1) | copy-done | bytes 8388632
  11.3 4.3 %local_adjoint.3 = (f32[32,8192]{1,0:T(8,128)S(1)}, f32[8,128]{1,0:T(8,128)S(1)}) custom-call(s32[4,64]{1,0:T(4,128)S(1)} %bitcast.27, bf16[16,32,128]{2,1,0:T(8,128)(2,1)S(1)} %fusion.2.panel_ref.refs_0_, bf16[64,4,128,128]{3,2,1,0:T(8,128)(2,1)S(1)} %copy-done.1), custom_call_target="tpu_custom_call" | custom-call | flops 268435456 | bytes 8388608 | tf_op jit(solution)/shard_map/local_adjoint/pallas_call | solution.py:275
  15.6 1.0 copy-done.6
  17.2 1.6 %collective-permute-start.5 = (bf16[16,32,128]{2,1,0:T(8,128)(2,1)S(1)}, bf16[16,32,128]{2,1,0:T(8,128)(2,1)S(1)}, u32[]{:S(2)}, u32[]{:S(2)}) collective-permute-start(bf16[16,32,128]{2,1,0:T(8,128)(2,1)S(1)} %get-tuple-element.84.after.refs_4_), channel_id=1, source_target_pairs={{0,8},{1,5},{2,10},{3,7},{4,12},{5,1},{6,14},{7,3},{8,0},{9,13},{1... | collective-permute-start | bytes 393224 | tf_op jit(solution)/shard_map/ppermute | solution.py:498
  20.7 1.6 %collective-permute-start.2 = (bf16[16,32,128]{2,1,0:T(8,128)(2,1)S(1)}, bf16[16,32,128]{2,1,0:T(8,128)(2,1)S(1)}, u32[]{:S(2)}, u32[]{:S(2)}) collective-permute-start(bf16[16,32,128]{2,1,0:T(8,128)(2,1)S(1)} %collective-permute-done.refs_1_), channel_id=1, source_target_pairs={{0,8},{1,5},{2,10},{3,7},{4,12},{5,1},{6,14},{7,3},{8,0},{9,13},{1... | collective-permute-start | bytes 393224 | tf_op jit(solution)/shard_map/ppermute | solution.py:498
  23.9 1.1 collective-permute-done.1.refs_2_
  25.0 2.7 %collective-permute-done.2.refs_3_ = bf16[16,32,128]{2,1,0:T(8,128)(2,1)S(1)} collective-permute-done((bf16[16,32,128]{2,1,0:T(8,128)(2,1)S(1)}, bf16[16,32,128]{2,1,0:T(8,128)(2,1)S(1)}, u32[]{:S(2)}, u32[]{:S(2)}) %collective-permute-start.2) | collective-permute-done | bytes 131104 | tf_op jit(solution)/shard_map/ppermute | solution.py:498
  28.1 1.2 copy-done.5
  29.3 1.2 copy-done.7
  30.5 3.6 %head_step.3 = (f32[32,8192]{1,0:T(8,128)S(1)}, bf16[32,8192]{1,0:T(8,128)(2,1)S(1)}, f32[32,128]{1,0:T(8,128)S(1)}, f32[8,128]{1,0:T(8,128)S(1)}, f32[8,128]{1,...) custom-call(s32[64]{0:T(128)S(1)} %fusion.index_ref, ...), custom_call_target="tpu_custom_call" | custom-call | flops 134217728 | bytes 7864320 | tf_op jit(solution)/shard_map/head_step/pallas_call | solution.py:312
  34.1 0.8 collective-permute-start.8
  34.9 1.5 %collective-permute-start.9 = (bf16[16,32,128]{2,1,0:T(8,128)(2,1)S(1)}, bf16[16,32,128]{2,1,0:T(8,128)(2,1)S(1)}, u32[]{:S(2)}, u32[]{:S(2)}) collective-permute-start(bf16[16,32,128]{2,1,0:T(8,128)(2,1)S(1)} %get-tuple-element.93), channel_id=1, source_target_pairs={{0,8},{1,5},{2,10},{3,7},{4,12},{5,1},{6,14},{7,3},{8,0},{9,13},{1... | collective-permute-start | bytes 393224 | tf_op jit(solution)/shard_map/ppermute | solution.py:498
  37.0 2.9 %collective-permute-done.9.refs_3_ = bf16[16,32,128]{2,1,0:T(8,128)(2,1)S(1)} collective-permute-done((bf16[16,32,128]{2,1,0:T(8,128)(2,1)S(1)}, bf16[16,32,128]{2,1,0:T(8,128)(2,1)S(1)}, u32[]{:S(2)}, u32[]{:S(2)}) %collective-permute-start.9) | collective-permute-done | bytes 131104 | tf_op jit(solution)/shard_map/ppermute | solution.py:498
  39.9 1.5 %collective-permute-done.10.refs_5_.refs_2_ = bf16[16,32,128]{2,1,0:T(8,128)(2,1)S(1)} collective-permute-done((bf16[16,32,128]{2,1,0:T(8,128)(2,1)S(1)}, bf16[16,32,128]{2,1,0:T(8,128)(2,1)S(1)}, u32[]{:S(2)}, u32[]{:S(2)}) %collective-permute-start.10) | collective-permute-done | bytes 131104 | tf_op jit(solution)/shard_map/ppermute | solution.py:498
  41.6 1.5 collective-permute-start.13
  43.0 1.3 collective-permute-start.12
  45.0 2.9 %collective-permute-done.12.refs_1_ = bf16[16,32,128]{2,1,0:T(8,128)(2,1)S(1)} collective-permute-done((bf16[16,32,128]{2,1,0:T(8,128)(2,1)S(1)}, bf16[16,32,128]{2,1,0:T(8,128)(2,1)S(1)}, u32[]{:S(2)}, u32[]{:S(2)}) %collective-permute-start.12) | collective-permute-done | bytes 131104 | tf_op jit(solution)/shard_map/ppermute | solution.py:498
  48.7 1.6 %collective-permute-start.15 = (f32[8,128]{1,0:T(8,128)S(1)}, f32[8,128]{1,0:T(8,128)S(1)}, u32[]{:S(2)}, u32[]{:S(2)}) collective-permute-start(f32[8,128]{1,0:T(8,128)S(1)} %get-tuple-element.105.refs_9_), channel_id=1, source_target_pairs={{0,2},{1,3},{2,0},{3,1},{4,6},{5,7},{6,4},{7,5},{8,10},{9,11},{10,... | collective-permute-start | bytes 12296 | tf_op jit(solution)/shard_map/ppermute | solution.py:484
  50.3 3.4 %copy-done.2 = bf16[64,4,128,128]{3,2,1,0:T(8,128)(2,1)S(1)} copy-done((bf16[64,4,128,128]{3,2,1,0:T(8,128)(2,1)S(1)}, bf16[64,4,128,128]{3,2,1,0:T(8,128)(2,1)}, u32[]{:S(2)}) %copy-start.2) | copy-done | bytes 8388632
  53.6 3.3 %local_forward.3.refs_5_ = f32[16,32,128]{2,1,0:T(8,128)S(1)} custom-call(s32[4,64]{1,0:T(4,128)S(1)} %bitcast.28, bf16[32,8192]{1,0:T(8,128)(2,1)S(1)} %get-tuple-element.101.bar_ref, bf16[64,4,128,128]{3,2,1,0:T(8,128)(2,1)S(1)} %copy-done.2, f32[16,32,128]{2,1,0:T(8,128)S(1)} %bitcast_bitcast_fusion.duals_ref, f32[32,2048]{1,0:T(8,128)S(1)} %copy-done.4, ...), custom_call_target="tpu_custom_call" | custom-call | flops 268435456 | bytes 8388608 | tf_op jit(solution)/shard_map/local_forward/pallas_call | solution.py:414
  57.2 2.7 %collective-permute-start.19 = (bf16[16,32,128]{2,1,0:T(8,128)(2,1)S(1)}, bf16[16,32,128]{2,1,0:T(8,128)(2,1)S(1)}, u32[]{:S(2)}, u32[]{:S(2)}) collective-permute-start(bf16[16,32,128]{2,1,0:T(8,128)(2,1)S(1)} %get-tuple-element.106.panel_ref.refs_0_), channel_id=1, source_target_pairs={{0,16},{1,17},{2,18},{3,19},{4,20},{5,21},{6,22},{7,23},{8,24},{9,... | collective-permute-start | bytes 393224 | tf_op jit(solution)/shard_map/ppermute | solution.py:498
  59.9 1.2 collective-permute-start.16
  61.1 4.3 %local_adjoint.4 = (f32[32,8192]{1,0:T(8,128)S(1)}, f32[8,128]{1,0:T(8,128)S(1)}) custom-call(s32[4,64]{1,0:T(4,128)S(1)} %bitcast.29, bf16[16,32,128]{2,1,0:T(8,128)(2,1)S(1)} %get-tuple-element.106.panel_ref.refs_0_, bf16[64,4,128,128]{3,2,1,0:T(8,128)(2,1)S(1)} %bitcast.23), custom_call_target="tpu_custom_call" | custom-call | flops 268435456 | bytes 8388608 | tf_op jit(solution)/shard_map/local_adjoint/pallas_call | solution.py:275
  65.4 1.5 %collective-permute-start.21 = (bf16[16,32,128]{2,1,0:T(8,128)(2,1)S(1)}, bf16[16,32,128]{2,1,0:T(8,128)(2,1)S(1)}, u32[]{:S(2)}, u32[]{:S(2)}) collective-permute-start(bf16[16,32,128]{2,1,0:T(8,128)(2,1)S(1)} %get-tuple-element.109.refs_4_), channel_id=1, source_target_pairs={{0,8},{1,5},{2,10},{3,7},{4,12},{5,1},{6,14},{7,3},{8,0},{9,13},{1... | collective-permute-start | bytes 393224 | tf_op jit(solution)/shard_map/ppermute | solution.py:498
  67.5 1.6 %collective-permute-start.20 = (bf16[16,32,128]{2,1,0:T(8,128)(2,1)S(1)}, bf16[16,32,128]{2,1,0:T(8,128)(2,1)S(1)}, u32[]{:S(2)}, u32[]{:S(2)}) collective-permute-start(bf16[16,32,128]{2,1,0:T(8,128)(2,1)S(1)} %get-tuple-element.109.refs_4_), channel_id=1, source_target_pairs={{0,4},{1,9},{2,6},{3,11},{4,0},{5,13},{6,2},{7,15},{8,12},{9,1},{1... | collective-permute-start | bytes 393224 | tf_op jit(solution)/shard_map/ppermute | solution.py:498
  69.7 2.0 %collective-permute-done.21.refs_6_ = bf16[16,32,128]{2,1,0:T(8,128)(2,1)S(1)} collective-permute-done((bf16[16,32,128]{2,1,0:T(8,128)(2,1)S(1)}, bf16[16,32,128]{2,1,0:T(8,128)(2,1)S(1)}, u32[]{:S(2)}, u32[]{:S(2)}) %collective-permute-start.21) | collective-permute-done | bytes 131104 | tf_op jit(solution)/shard_map/ppermute | solution.py:498
  71.8 1.4 collective-permute-start.22
  73.2 1.4 collective-permute-done.17.refs_2_
  74.6 2.2 %collective-permute-done.23.refs_15_ = f32[8,128]{1,0:T(8,128)S(1)} collective-permute-done((f32[8,128]{1,0:T(8,128)S(1)}, f32[8,128]{1,0:T(8,128)S(1)}, u32[]{:S(2)}, u32[]{:S(2)}) %collective-permute-start.23) | collective-permute-done | bytes 4128 | tf_op jit(solution)/shard_map/ppermute | solution.py:484
  76.8 3.6 %head_step.4 = (f32[32,8192]{1,0:T(8,128)S(1)}, bf16[32,8192]{1,0:T(8,128)(2,1)S(1)}, f32[32,128]{1,0:T(8,128)S(1)}, f32[8,128]{1,0:T(8,128)S(1)}, f32[8,128]{1,...) custom-call(s32[64]{0:T(128)S(1)} %fusion.index_ref, ...), custom_call_target="tpu_custom_call" | custom-call | flops 134217728 | bytes 7864320 | tf_op jit(solution)/shard_map/head_step/pallas_call | solution.py:312
  80.5 1.4 collective-permute-start.24
  82.6 1.3 collective-permute-start.26
  83.9 2.9 %collective-permute-done.25.refs_3_ = bf16[16,32,128]{2,1,0:T(8,128)(2,1)S(1)} collective-permute-done((bf16[16,32,128]{2,1,0:T(8,128)(2,1)S(1)}, bf16[16,32,128]{2,1,0:T(8,128)(2,1)S(1)}, u32[]{:S(2)}, u32[]{:S(2)}) %collective-permute-start.25) | collective-permute-done | bytes 131104 | tf_op jit(solution)/shard_map/ppermute | solution.py:498
  86.8 1.4 collective-permute-done.26.refs_5_.refs_2_
  89.8 4.2 %collective-permute-done.28.refs_1_ = bf16[16,32,128]{2,1,0:T(8,128)(2,1)S(1)} collective-permute-done((bf16[16,32,128]{2,1,0:T(8,128)(2,1)S(1)}, bf16[16,32,128]{2,1,0:T(8,128)(2,1)S(1)}, u32[]{:S(2)}, u32[]{:S(2)}) %collective-permute-start.28) | collective-permute-done | bytes 131104 | tf_op jit(solution)/shard_map/ppermute | solution.py:498
  94.2 3.2 %collective-permute-start.30 = (bf16[17,32,128]{2,1,0:T(8,128)(2,1)S(1)}, bf16[17,32,128]{2,1,0:T(8,128)(2,1)S(1)}, u32[]{:S(2)}, u32[]{:S(2)}) collective-permute-start(bf16[17,32,128]{2,1,0:T(8,128)(2,1)S(1)} %fold.9.after_ref.refs_4_), channel_id=1, source_target_pairs={{0,16},{1,17},{2,18},{3,19},{4,20},{5,21},{6,22},{7,23},{8,24},{9,... | collective-permute-start | bytes 417800 | tf_op jit(solution)/shard_map/ppermute | solution.py:498
  98.2 3.3 %local_forward.4.refs_5_ = f32[16,32,128]{2,1,0:T(8,128)S(1)} custom-call(s32[4,64]{1,0:T(4,128)S(1)} %bitcast.30, bf16[32,8192]{1,0:T(8,128)(2,1)S(1)} %get-tuple-element.125.bar_ref, bf16[64,4,128,128]{3,2,1,0:T(8,128)(2,1)S(1)} %bitcast.23, f32[16,32,128]{2,1,0:T(8,128)S(1)} %get-tuple-element.126.duals_ref, f32[32,2048]{1,0:T(8,128)S(1)} %copy-done.4, ...), custom_call_target="tpu_custom_call" | custom-call | flops 268435456 | bytes 8388608 | tf_op jit(solution)/shard_map/local_forward/pallas_call | solution.py:414
  101.5 0.9 collective-permute-done.27.refs_1_
  102.4 1.9 %collective-permute-done.30.refs_3_ = bf16[17,32,128]{2,1,0:T(8,128)(2,1)S(1)} collective-permute-done((bf16[17,32,128]{2,1,0:T(8,128)(2,1)S(1)}, bf16[17,32,128]{2,1,0:T(8,128)(2,1)S(1)}, u32[]{:S(2)}, u32[]{:S(2)}) %collective-permute-start.30) | collective-permute-done | bytes 139296 | tf_op jit(solution)/shard_map/ppermute | solution.py:498
  104.9 1.1 collective-permute-start.31
  106.0 4.3 %local_adjoint.5 = (f32[32,8192]{1,0:T(8,128)S(1)}, f32[8,128]{1,0:T(8,128)S(1)}) custom-call(s32[4,64]{1,0:T(4,128)S(1)} %bitcast.31, bf16[16,32,128]{2,1,0:T(8,128)(2,1)S(1)} %get-tuple-element.131.panel_ref.refs_0_, bf16[64,4,128,128]{3,2,1,0:T(8,128)(2,1)S(1)} %bitcast.23), custom_call_target="tpu_custom_call" | custom-call | flops 268435456 | bytes 8388608 | tf_op jit(solution)/shard_map/local_adjoint/pallas_call | solution.py:275
  110.2 2.0 %collective-permute-done.34.arrived_ref = bf16[16,32,128]{2,1,0:T(8,128)(2,1)S(1)} collective-permute-done((bf16[16,32,128]{2,1,0:T(8,128)(2,1)S(1)}, bf16[16,32,128]{2,1,0:T(8,128)(2,1)S(1)}, u32[]{:S(2)}, u32[]{:S(2)}) %collective-permute-start.34) | collective-permute-done | bytes 131104 | tf_op jit(solution)/shard_map/ppermute | solution.py:498
  112.3 2.6 %collective-permute-start.36 = (bf16[16,32,128]{2,1,0:T(8,128)(2,1)S(1)}, bf16[16,32,128]{2,1,0:T(8,128)(2,1)S(1)}, u32[]{:S(2)}, u32[]{:S(2)}) collective-permute-start(bf16[16,32,128]{2,1,0:T(8,128)(2,1)S(1)} %get-tuple-element.133.refs_4_), channel_id=1, source_target_pairs={{0,8},{1,5},{2,10},{3,7},{4,12},{5,1},{6,14},{7,3},{8,0},{9,13},{1... | collective-permute-start | bytes 393224 | tf_op jit(solution)/shard_map/ppermute | solution.py:498
  115.1 1.9 %collective-permute-start.33 = (bf16[16,32,128]{2,1,0:T(8,128)(2,1)S(1)}, bf16[16,32,128]{2,1,0:T(8,128)(2,1)S(1)}, u32[]{:S(2)}, u32[]{:S(2)}) collective-permute-start(bf16[16,32,128]{2,1,0:T(8,128)(2,1)S(1)} %collective-permute-done.31.refs_1_), channel_id=1, source_target_pairs={{0,8},{1,5},{2,10},{3,7},{4,12},{5,1},{6,14},{7,3},{8,0},{9,13},{1... | collective-permute-start | bytes 393224 | tf_op jit(solution)/shard_map/ppermute | solution.py:498
  117.8 1.1 collective-permute-start.37
  119.0 0.9 collective-permute-done.32.refs_2_
  120.1 1.1 collective-permute-done.33.refs_3_
  121.3 1.5 %collective-permute-done.37.refs_7_ = bf16[16,32,128]{2,1,0:T(8,128)(2,1)S(1)} collective-permute-done((bf16[16,32,128]{2,1,0:T(8,128)(2,1)S(1)}, bf16[16,32,128]{2,1,0:T(8,128)(2,1)S(1)}, u32[]{:S(2)}, u32[]{:S(2)}) %collective-permute-start.37) | collective-permute-done | bytes 131104 | tf_op jit(solution)/shard_map/ppermute | solution.py:498
  122.8 4.2 %head_step.5 = (f32[32,8192]{1,0:T(8,128)}, bf16[32,8192]{1,0:T(8,128)(2,1)S(1)}, f32[32,128]{1,0:T(8,128)S(1)}, f32[8,128]{1,0:T(8,128)S(1)}, f32[8,128]{1,0:T(...) custom-call(s32[64]{0:T(128)S(1)} %fusion.index_ref, ...), custom_call_target="tpu_custom_call" | custom-call | flops 134217728 | bytes 7864320 | tf_op jit(solution)/shard_map/head_step/pallas_call | solution.py:312
  127.1 1.1 collective-permute-start.39
  128.2 1.0 collective-permute-start.40
  129.2 1.0 collective-permute-start.42
  130.2 1.2 collective-permute-done.41
  131.4 1.8 %collective-permute-done.40.refs_3_ = bf16[16,32,128]{2,1,0:T(8,128)(2,1)S(1)} collective-permute-done((bf16[16,32,128]{2,1,0:T(8,128)(2,1)S(1)}, bf16[16,32,128]{2,1,0:T(8,128)(2,1)S(1)}, u32[]{:S(2)}, u32[]{:S(2)}) %collective-permute-start.40) | collective-permute-done | bytes 131104 | tf_op jit(solution)/shard_map/ppermute | solution.py:498
  133.1 1.4 collective-permute-done.42.refs_6_.refs_2_
  134.6 1.1 collective-permute-start.45
  135.7 2.0 %collective-permute-start.44 = (bf16[16,32,128]{2,1,0:T(8,128)(2,1)S(1)}, bf16[16,32,128]{2,1,0:T(8,128)(2,1)S(1)}, u32[]{:S(2)}, u32[]{:S(2)}) collective-permute-start(bf16[16,32,128]{2,1,0:T(8,128)(2,1)S(1)} %get-tuple-element.148), channel_id=1, source_target_pairs={{0,4},{1,9},{2,6},{3,11},{4,0},{5,13},{6,2},{7,15},{8,12},{9,1},{1... | collective-permute-start | bytes 393224 | tf_op jit(solution)/shard_map/ppermute | solution.py:498
  137.7 3.0 %collective-permute-done.44.refs_1_ = bf16[16,32,128]{2,1,0:T(8,128)(2,1)S(1)} collective-permute-done((bf16[16,32,128]{2,1,0:T(8,128)(2,1)S(1)}, bf16[16,32,128]{2,1,0:T(8,128)(2,1)S(1)}, u32[]{:S(2)}, u32[]{:S(2)}) %collective-permute-start.44) | collective-permute-done | bytes 131104 | tf_op jit(solution)/shard_map/ppermute | solution.py:498
  140.8 1.7 %collective-permute-start.46 = (bf16[17,32,128]{2,1,0:T(8,128)(2,1)S(1)}, bf16[17,32,128]{2,1,0:T(8,128)(2,1)S(1)}, u32[]{:S(2)}, u32[]{:S(2)}) collective-permute-start(bf16[17,32,128]{2,1,0:T(8,128)(2,1)S(1)} %get-tuple-element.150.after_ref.refs_4_), channel_id=1, source_target_pairs={{0,16},{1,17},{2,18},{3,19},{4,20},{5,21},{6,22},{7,23},{8,24},{9,... | collective-permute-start | bytes 417800 | tf_op jit(solution)/shard_map/ppermute | solution.py:498
  142.9 1.6 %collective-permute-start.47 = (f32[8,128]{1,0:T(8,128)S(1)}, f32[8,128]{1,0:T(8,128)S(1)}, u32[]{:S(2)}, u32[]{:S(2)}) collective-permute-start(f32[8,128]{1,0:T(8,128)S(1)} %get-tuple-element.156.refs_9_), channel_id=1, source_target_pairs={{0,2},{1,3},{2,0},{3,1},{4,6},{5,7},{6,4},{7,5},{8,10},{9,11},{10,... | collective-permute-start | bytes 12296 | tf_op jit(solution)/shard_map/ppermute | solution.py:484
  144.6 3.3 %local_forward.5.refs_5_ = f32[16,32,128]{2,1,0:T(8,128)S(1)} custom-call(s32[4,64]{1,0:T(4,128)S(1)} %bitcast.32, bf16[32,8192]{1,0:T(8,128)(2,1)S(1)} %get-tuple-element.151.bar_ref, bf16[64,4,128,128]{3,2,1,0:T(8,128)(2,1)S(1)} %bitcast.23, f32[16,32,128]{2,1,0:T(8,128)S(1)} %get-tuple-element.152.duals_ref, f32[32,2048]{1,0:T(8,128)S(1)} %copy-done.4, ...), custom_call_target="tpu_custom_call" | custom-call | flops 268435456 | bytes 8388608 | tf_op jit(solution)/shard_map/local_forward/pallas_call | solution.py:414
  (92 shorter events, 15.0 us)
Async XLA Ops:
  0.6 1.0 copy-start
  0.6 49.6 %copy-start.10 = (s32[64,4]{0,1:T(4,128)S(1)}, s32[64,4]{0,1:T(4,128)}, u32[]{:S(2)}) copy-start(s32[64,4]{0,1:T(4,128)} %param.20) | copy-start | bytes 3076
  0.7 19.8 %copy-start.11 = (f32[32]{0:T(128)S(1)}, f32[32]{0:T(128)}, u32[]{:S(2)}) copy-start(f32[32]{0:T(128)} %param.15) | copy-start | bytes 388
  0.7 19.8 %copy-start.12 = (f32[32]{0:T(128)S(1)}, f32[32]{0:T(128)}, u32[]{:S(2)}) copy-start(f32[32]{0:T(128)} %param.14) | copy-start | bytes 388
  0.7 23.2 %copy-start.13 = (s32[64]{0:T(128)S(1)}, s32[64]{0:T(128)}, u32[]{:S(2)}) copy-start(s32[64]{0:T(128)} %param.21) | copy-start | bytes 772
  0.7 27.4 %copy-start.8 = (f32[8192]{0:T(1024)S(1)}, f32[8192]{0:T(1024)}, u32[]{:S(2)}) copy-start(f32[8192]{0:T(1024)} %param.17) | copy-start | bytes 98308
  1.7 48.6 %copy-start.4 = (f32[32,2048]{1,0:T(8,128)S(1)}, f32[32,2048]{1,0:T(8,128)}, u32[]{:S(2)}) copy-start(f32[32,2048]{1,0:T(8,128)} %demand_ref.5) | copy-start | bytes 786436
  1.7 14.9 %collective-permute-start.3 = (bf16[16,32,128]{2,1,0:T(8,128)(2,1)S(1)}, bf16[16,32,128]{2,1,0:T(8,128)(2,1)S(1)}, u32[]{:S(2)}, u32[]{:S(2)}) collective-permute-start(bf16[16,32,128]{2,1,0:T(8,128)(2,1)S(1)} %fusion.2.panel_ref.refs_0_), channel_id=1, source_target_pairs={{0,16},{1,17},{2,18},{3,19},{4,20},{5,21},{6,22},{7,23},{8,24},{9,... | collective-permute-start | bytes 393224 | tf_op jit(solution)/shard_map/ppermute | solution.py:498
  5.8 14.9 %collective-permute-start = (bf16[16,32,128]{2,1,0:T(8,128)(2,1)S(1)}, bf16[16,32,128]{2,1,0:T(8,128)(2,1)S(1)}, u32[]{:S(2)}, u32[]{:S(2)}) collective-permute-start(bf16[16,32,128]{2,1,0:T(8,128)(2,1)S(1)} %fusion.2.panel_ref.refs_0_), channel_id=1, source_target_pairs={{0,4},{1,9},{2,6},{3,11},{4,0},{5,13},{6,2},{7,15},{8,12},{9,1},{1... | collective-permute-start | bytes 393224 | tf_op jit(solution)/shard_map/ppermute | solution.py:498
  7.3 3.4 %copy-start.1 = (bf16[64,4,128,128]{3,2,1,0:T(8,128)(2,1)S(1)}, bf16[64,4,128,128]{3,2,1,0:T(8,128)(2,1)}, u32[]{:S(2)}) copy-start(bf16[64,4,128,128]{3,2,1,0:T(8,128)(2,1)} %blocks_ref.11) | copy-start | bytes 25165828
  10.7 0.7 copy-start.9
  11.3 16.7 %copy-start.3 = (bf16[64,128,128]{2,1,0:T(8,128)(2,1)S(1)}, bf16[64,128,128]{2,1,0:T(8,128)(2,1)}, u32[]{:S(2)}) copy-start(bf16[64,128,128]{2,1,0:T(8,128)(2,1)} %refs_8_.5) | copy-start | bytes 6291460
  15.6 1.0 copy-start.6
  17.2 5.9 %collective-permute-start.5 = (bf16[16,32,128]{2,1,0:T(8,128)(2,1)S(1)}, bf16[16,32,128]{2,1,0:T(8,128)(2,1)S(1)}, u32[]{:S(2)}, u32[]{:S(2)}) collective-permute-start(bf16[16,32,128]{2,1,0:T(8,128)(2,1)S(1)} %get-tuple-element.84.after.refs_4_), channel_id=1, source_target_pairs={{0,8},{1,5},{2,10},{3,7},{4,12},{5,1},{6,14},{7,3},{8,0},{9,13},{1... | collective-permute-start | bytes 393224 | tf_op jit(solution)/shard_map/ppermute | solution.py:498
  18.8 6.2 %collective-permute-start.1 = (bf16[16,32,128]{2,1,0:T(8,128)(2,1)S(1)}, bf16[16,32,128]{2,1,0:T(8,128)(2,1)S(1)}, u32[]{:S(2)}, u32[]{:S(2)}) collective-permute-start(bf16[16,32,128]{2,1,0:T(8,128)(2,1)S(1)} %fusion.2.panel_ref.refs_0_), channel_id=1, source_target_pairs={{0,8},{1,5},{2,10},{3,7},{4,12},{5,1},{6,14},{7,3},{8,0},{9,13},{1... | collective-permute-start | bytes 393224 | tf_op jit(solution)/shard_map/ppermute | solution.py:498
  19.9 7.8 %collective-permute-start.4 = (bf16[16,32,128]{2,1,0:T(8,128)(2,1)S(1)}, bf16[16,32,128]{2,1,0:T(8,128)(2,1)S(1)}, u32[]{:S(2)}, u32[]{:S(2)}) collective-permute-start(bf16[16,32,128]{2,1,0:T(8,128)(2,1)S(1)} %get-tuple-element.84.after.refs_4_), channel_id=1, source_target_pairs={{0,4},{1,9},{2,6},{3,11},{4,0},{5,13},{6,2},{7,15},{8,12},{9,1},{1... | collective-permute-start | bytes 393224 | tf_op jit(solution)/shard_map/ppermute | solution.py:498
  20.6 4.4 %collective-permute-start.7 = (f32[8,128]{1,0:T(8,128)S(1)}, f32[8,128]{1,0:T(8,128)S(1)}, u32[]{:S(2)}, u32[]{:S(2)}) collective-permute-start(f32[8,128]{1,0:T(8,128)S(1)} %get-tuple-element.88.refs_14_), channel_id=1, source_target_pairs={{0,1},{1,0},{2,3},{3,2},{4,5},{5,4},{6,7},{7,6},{8,9},{9,8},{10,11... | collective-permute-start | bytes 12296 | tf_op jit(solution)/shard_map/ppermute | solution.py:484
  20.7 7.0 %collective-permute-start.2 = (bf16[16,32,128]{2,1,0:T(8,128)(2,1)S(1)}, bf16[16,32,128]{2,1,0:T(8,128)(2,1)S(1)}, u32[]{:S(2)}, u32[]{:S(2)}) collective-permute-start(bf16[16,32,128]{2,1,0:T(8,128)(2,1)S(1)} %collective-permute-done.refs_1_), channel_id=1, source_target_pairs={{0,8},{1,5},{2,10},{3,7},{4,12},{5,1},{6,14},{7,3},{8,0},{9,13},{1... | collective-permute-start | bytes 393224 | tf_op jit(solution)/shard_map/ppermute | solution.py:498
  23.1 5.0 %collective-permute-start.6 = (bf16[16,32,128]{2,1,0:T(8,128)(2,1)S(1)}, bf16[16,32,128]{2,1,0:T(8,128)(2,1)S(1)}, u32[]{:S(2)}, u32[]{:S(2)}) collective-permute-start(bf16[16,32,128]{2,1,0:T(8,128)(2,1)S(1)} %collective-permute-done.5.refs_6_), channel_id=1, source_target_pairs={{0,4},{1,9},{2,6},{3,11},{4,0},{5,13},{6,2},{7,15},{8,12},{9,1},{1... | collective-permute-start | bytes 393224 | tf_op jit(solution)/shard_map/ppermute | solution.py:498
  28.1 1.2 copy-start.5
  29.3 1.2 copy-start.7
  30.5 30.6 %slice-start = ((s8[8388608]{0:T(1024)(128)(4,1)}), s8[4194304]{0:T(1024)(128)(4,1)S(1)}, s32[]{:S(2)}) async-start(s8[8388608]{0:T(1024)(128)(4,1)} %bitcast.22), calls=%async_computation | async-start | bytes 8388608
  34.1 7.3 %collective-permute-start.8 = (bf16[17,32,128]{2,1,0:T(8,128)(2,1)S(1)}, bf16[17,32,128]{2,1,0:T(8,128)(2,1)S(1)}, u32[]{:S(2)}, u32[]{:S(2)}) collective-permute-start(bf16[17,32,128]{2,1,0:T(8,128)(2,1)S(1)} %get-tuple-element.91.refs_4_), channel_id=1, source_target_pairs={{0,4},{1,9},{2,6},{3,11},{4,0},{5,13},{6,2},{7,15},{8,12},{9,1},{1... | collective-permute-start | bytes 417800 | tf_op jit(solution)/shard_map/ppermute | solution.py:498
  34.9 5.0 %collective-permute-start.9 = (bf16[16,32,128]{2,1,0:T(8,128)(2,1)S(1)}, bf16[16,32,128]{2,1,0:T(8,128)(2,1)S(1)}, u32[]{:S(2)}, u32[]{:S(2)}) collective-permute-start(bf16[16,32,128]{2,1,0:T(8,128)(2,1)S(1)} %get-tuple-element.93), channel_id=1, source_target_pairs={{0,8},{1,5},{2,10},{3,7},{4,12},{5,1},{6,14},{7,3},{8,0},{9,13},{1... | collective-permute-start | bytes 393224 | tf_op jit(solution)/shard_map/ppermute | solution.py:498
  36.5 5.0 %collective-permute-start.10 = (bf16[16,32,128]{2,1,0:T(8,128)(2,1)S(1)}, bf16[16,32,128]{2,1,0:T(8,128)(2,1)S(1)}, u32[]{:S(2)}, u32[]{:S(2)}) collective-permute-start(bf16[16,32,128]{2,1,0:T(8,128)(2,1)S(1)} %get-tuple-element.94), channel_id=1, source_target_pairs={{0,8},{1,5},{2,10},{3,7},{4,12},{5,1},{6,14},{7,3},{8,0},{9,13},{1... | collective-permute-start | bytes 393224 | tf_op jit(solution)/shard_map/ppermute | solution.py:498
  41.6 6.6 %collective-permute-start.13 = (bf16[17,32,128]{2,1,0:T(8,128)(2,1)S(1)}, bf16[17,32,128]{2,1,0:T(8,128)(2,1)S(1)}, u32[]{:S(2)}, u32[]{:S(2)}) collective-permute-start(bf16[17,32,128]{2,1,0:T(8,128)(2,1)S(1)} %get-tuple-element.98.refs_3_), channel_id=1, source_target_pairs={{0,8},{1,5},{2,10},{3,7},{4,12},{5,1},{6,14},{7,3},{8,0},{9,13},{1... | collective-permute-start | bytes 417800 | tf_op jit(solution)/shard_map/ppermute | solution.py:498
  43.0 5.0 %collective-permute-start.12 = (bf16[16,32,128]{2,1,0:T(8,128)(2,1)S(1)}, bf16[16,32,128]{2,1,0:T(8,128)(2,1)S(1)}, u32[]{:S(2)}, u32[]{:S(2)}) collective-permute-start(bf16[16,32,128]{2,1,0:T(8,128)(2,1)S(1)} %get-tuple-element.97), channel_id=1, source_target_pairs={{0,4},{1,9},{2,6},{3,11},{4,0},{5,13},{6,2},{7,15},{8,12},{9,1},{1... | collective-permute-start | bytes 393224 | tf_op jit(solution)/shard_map/ppermute | solution.py:498
  44.3 12.7 %collective-permute-start.11 = (bf16[16,32,128]{2,1,0:T(8,128)(2,1)S(1)}, bf16[16,32,128]{2,1,0:T(8,128)(2,1)S(1)}, u32[]{:S(2)}, u32[]{:S(2)}) collective-permute-start(bf16[16,32,128]{2,1,0:T(8,128)(2,1)S(1)} %get-tuple-element.95), channel_id=1, source_target_pairs={{0,4},{1,9},{2,6},{3,11},{4,0},{5,13},{6,2},{7,15},{8,12},{9,1},{1... | collective-permute-start | bytes 393224 | tf_op jit(solution)/shard_map/ppermute | solution.py:498
  48.3 8.7 %collective-permute-start.14 = (bf16[17,32,128]{2,1,0:T(8,128)(2,1)S(1)}, bf16[17,32,128]{2,1,0:T(8,128)(2,1)S(1)}, u32[]{:S(2)}, u32[]{:S(2)}) collective-permute-start(bf16[17,32,128]{2,1,0:T(8,128)(2,1)S(1)} %get-tuple-element.100.after_ref.refs_4_), channel_id=1, source_target_pairs={{0,16},{1,17},{2,18},{3,19},{4,20},{5,21},{6,22},{7,23},{8,24},{9,... | collective-permute-start | bytes 417800 | tf_op jit(solution)/shard_map/ppermute | solution.py:498
  48.7 8.3 %collective-permute-start.15 = (f32[8,128]{1,0:T(8,128)S(1)}, f32[8,128]{1,0:T(8,128)S(1)}, u32[]{:S(2)}, u32[]{:S(2)}) collective-permute-start(f32[8,128]{1,0:T(8,128)S(1)} %get-tuple-element.105.refs_9_), channel_id=1, source_target_pairs={{0,2},{1,3},{2,0},{3,1},{4,6},{5,7},{6,4},{7,5},{8,10},{9,11},{10,... | collective-permute-start | bytes 12296 | tf_op jit(solution)/shard_map/ppermute | solution.py:484
  50.3 3.4 %copy-start.2 = (bf16[64,4,128,128]{3,2,1,0:T(8,128)(2,1)S(1)}, bf16[64,4,128,128]{3,2,1,0:T(8,128)(2,1)}, u32[]{:S(2)}) copy-start(bf16[64,4,128,128]{3,2,1,0:T(8,128)(2,1)} %blocks_ref.11) | copy-start | bytes 25165828
  53.6 7.4 %slice-start.1 = ((s8[8388608]{0:T(1024)(128)(4,1)}), s8[4194304]{0:T(1024)(128)(4,1)S(1)}, s32[]{:S(2)}) async-start(s8[8388608]{0:T(1024)(128)(4,1)} %bitcast.22), calls=%async_computation.1 | async-start | bytes 8388608
  57.2 8.2 %collective-permute-start.19 = (bf16[16,32,128]{2,1,0:T(8,128)(2,1)S(1)}, bf16[16,32,128]{2,1,0:T(8,128)(2,1)S(1)}, u32[]{:S(2)}, u32[]{:S(2)}) collective-permute-start(bf16[16,32,128]{2,1,0:T(8,128)(2,1)S(1)} %get-tuple-element.106.panel_ref.refs_0_), channel_id=1, source_target_pairs={{0,16},{1,17},{2,18},{3,19},{4,20},{5,21},{6,22},{7,23},{8,24},{9,... | collective-permute-start | bytes 393224 | tf_op jit(solution)/shard_map/ppermute | solution.py:498
  59.9 9.2 %collective-permute-start.16 = (bf16[16,32,128]{2,1,0:T(8,128)(2,1)S(1)}, bf16[16,32,128]{2,1,0:T(8,128)(2,1)S(1)}, u32[]{:S(2)}, u32[]{:S(2)}) collective-permute-start(bf16[16,32,128]{2,1,0:T(8,128)(2,1)S(1)} %get-tuple-element.106.panel_ref.refs_0_), channel_id=1, source_target_pairs={{0,4},{1,9},{2,6},{3,11},{4,0},{5,13},{6,2},{7,15},{8,12},{9,1},{1... | collective-permute-start | bytes 393224 | tf_op jit(solution)/shard_map/ppermute | solution.py:498
  65.4 6.4 %collective-permute-start.21 = (bf16[16,32,128]{2,1,0:T(8,128)(2,1)S(1)}, bf16[16,32,128]{2,1,0:T(8,128)(2,1)S(1)}, u32[]{:S(2)}, u32[]{:S(2)}) collective-permute-start(bf16[16,32,128]{2,1,0:T(8,128)(2,1)S(1)} %get-tuple-element.109.refs_4_), channel_id=1, source_target_pairs={{0,8},{1,5},{2,10},{3,7},{4,12},{5,1},{6,14},{7,3},{8,0},{9,13},{1... | collective-permute-start | bytes 393224 | tf_op jit(solution)/shard_map/ppermute | solution.py:498
  66.9 7.7 %collective-permute-start.17 = (bf16[16,32,128]{2,1,0:T(8,128)(2,1)S(1)}, bf16[16,32,128]{2,1,0:T(8,128)(2,1)S(1)}, u32[]{:S(2)}, u32[]{:S(2)}) collective-permute-start(bf16[16,32,128]{2,1,0:T(8,128)(2,1)S(1)} %get-tuple-element.106.panel_ref.refs_0_), channel_id=1, source_target_pairs={{0,8},{1,5},{2,10},{3,7},{4,12},{5,1},{6,14},{7,3},{8,0},{9,13},{1... | collective-permute-start | bytes 393224 | tf_op jit(solution)/shard_map/ppermute | solution.py:498
  67.5 9.3 %collective-permute-start.20 = (bf16[16,32,128]{2,1,0:T(8,128)(2,1)S(1)}, bf16[16,32,128]{2,1,0:T(8,128)(2,1)S(1)}, u32[]{:S(2)}, u32[]{:S(2)}) collective-permute-start(bf16[16,32,128]{2,1,0:T(8,128)(2,1)S(1)} %get-tuple-element.109.refs_4_), channel_id=1, source_target_pairs={{0,4},{1,9},{2,6},{3,11},{4,0},{5,13},{6,2},{7,15},{8,12},{9,1},{1... | collective-permute-start | bytes 393224 | tf_op jit(solution)/shard_map/ppermute | solution.py:498
  69.0 7.8 %collective-permute-start.18 = (bf16[16,32,128]{2,1,0:T(8,128)(2,1)S(1)}, bf16[16,32,128]{2,1,0:T(8,128)(2,1)S(1)}, u32[]{:S(2)}, u32[]{:S(2)}) collective-permute-start(bf16[16,32,128]{2,1,0:T(8,128)(2,1)S(1)} %collective-permute-done.16.refs_1_), channel_id=1, source_target_pairs={{0,8},{1,5},{2,10},{3,7},{4,12},{5,1},{6,14},{7,3},{8,0},{9,13},{1... | collective-permute-start | bytes 393224 | tf_op jit(solution)/shard_map/ppermute | solution.py:498
  71.8 5.1 %collective-permute-start.22 = (bf16[16,32,128]{2,1,0:T(8,128)(2,1)S(1)}, bf16[16,32,128]{2,1,0:T(8,128)(2,1)S(1)}, u32[]{:S(2)}, u32[]{:S(2)}) collective-permute-start(bf16[16,32,128]{2,1,0:T(8,128)(2,1)S(1)} %collective-permute-done.21.refs_6_), channel_id=1, source_target_pairs={{0,4},{1,9},{2,6},{3,11},{4,0},{5,13},{6,2},{7,15},{8,12},{9,1},{1... | collective-permute-start | bytes 393224 | tf_op jit(solution)/shard_map/ppermute | solution.py:498
  73.2 3.6 %collective-permute-start.23 = (f32[8,128]{1,0:T(8,128)S(1)}, f32[8,128]{1,0:T(8,128)S(1)}, u32[]{:S(2)}, u32[]{:S(2)}) collective-permute-start(f32[8,128]{1,0:T(8,128)S(1)} %get-tuple-element.114.refs_14_), channel_id=1, source_target_pairs={{0,2},{1,3},{2,0},{3,1},{4,6},{5,7},{6,4},{7,5},{8,10},{9,11},{10,... | collective-permute-start | bytes 12296 | tf_op jit(solution)/shard_map/ppermute | solution.py:484
  80.5 7.7 %collective-permute-start.24 = (bf16[17,32,128]{2,1,0:T(8,128)(2,1)S(1)}, bf16[17,32,128]{2,1,0:T(8,128)(2,1)S(1)}, u32[]{:S(2)}, u32[]{:S(2)}) collective-permute-start(bf16[17,32,128]{2,1,0:T(8,128)(2,1)S(1)} %get-tuple-element.117.refs_4_), channel_id=1, source_target_pairs={{0,4},{1,9},{2,6},{3,11},{4,0},{5,13},{6,2},{7,15},{8,12},{9,1},{1... | collective-permute-start | bytes 417800 | tf_op jit(solution)/shard_map/ppermute | solution.py:498
  81.8 5.0 %collective-permute-start.25 = (bf16[16,32,128]{2,1,0:T(8,128)(2,1)S(1)}, bf16[16,32,128]{2,1,0:T(8,128)(2,1)S(1)}, u32[]{:S(2)}, u32[]{:S(2)}) collective-permute-start(bf16[16,32,128]{2,1,0:T(8,128)(2,1)S(1)} %get-tuple-element.119), channel_id=1, source_target_pairs={{0,8},{1,5},{2,10},{3,7},{4,12},{5,1},{6,14},{7,3},{8,0},{9,13},{1... | collective-permute-start | bytes 393224 | tf_op jit(solution)/shard_map/ppermute | solution.py:498
  82.6 5.6 %collective-permute-start.26 = (bf16[16,32,128]{2,1,0:T(8,128)(2,1)S(1)}, bf16[16,32,128]{2,1,0:T(8,128)(2,1)S(1)}, u32[]{:S(2)}, u32[]{:S(2)}) collective-permute-start(bf16[16,32,128]{2,1,0:T(8,128)(2,1)S(1)} %get-tuple-element.120), channel_id=1, source_target_pairs={{0,8},{1,5},{2,10},{3,7},{4,12},{5,1},{6,14},{7,3},{8,0},{9,13},{1... | collective-permute-start | bytes 393224 | tf_op jit(solution)/shard_map/ppermute | solution.py:498
  88.3 5.8 %collective-permute-start.29 = (bf16[17,32,128]{2,1,0:T(8,128)(2,1)S(1)}, bf16[17,32,128]{2,1,0:T(8,128)(2,1)S(1)}, u32[]{:S(2)}, u32[]{:S(2)}) collective-permute-start(bf16[17,32,128]{2,1,0:T(8,128)(2,1)S(1)} %get-tuple-element.124.refs_3_), channel_id=1, source_target_pairs={{0,8},{1,5},{2,10},{3,7},{4,12},{5,1},{6,14},{7,3},{8,0},{9,13},{1... | collective-permute-start | bytes 417800 | tf_op jit(solution)/shard_map/ppermute | solution.py:498
  89.1 5.0 %collective-permute-start.28 = (bf16[16,32,128]{2,1,0:T(8,128)(2,1)S(1)}, bf16[16,32,128]{2,1,0:T(8,128)(2,1)S(1)}, u32[]{:S(2)}, u32[]{:S(2)}) collective-permute-start(bf16[16,32,128]{2,1,0:T(8,128)(2,1)S(1)} %get-tuple-element.123), channel_id=1, source_target_pairs={{0,4},{1,9},{2,6},{3,11},{4,0},{5,13},{6,2},{7,15},{8,12},{9,1},{1... | collective-permute-start | bytes 393224 | tf_op jit(solution)/shard_map/ppermute | solution.py:498
  94.2 10.1 %collective-permute-start.30 = (bf16[17,32,128]{2,1,0:T(8,128)(2,1)S(1)}, bf16[17,32,128]{2,1,0:T(8,128)(2,1)S(1)}, u32[]{:S(2)}, u32[]{:S(2)}) collective-permute-start(bf16[17,32,128]{2,1,0:T(8,128)(2,1)S(1)} %fold.9.after_ref.refs_4_), channel_id=1, source_target_pairs={{0,16},{1,17},{2,18},{3,19},{4,20},{5,21},{6,22},{7,23},{8,24},{9,... | collective-permute-start | bytes 417800 | tf_op jit(solution)/shard_map/ppermute | solution.py:498
  97.4 5.0 %collective-permute-start.27 = (bf16[16,32,128]{2,1,0:T(8,128)(2,1)S(1)}, bf16[16,32,128]{2,1,0:T(8,128)(2,1)S(1)}, u32[]{:S(2)}, u32[]{:S(2)}) collective-permute-start(bf16[16,32,128]{2,1,0:T(8,128)(2,1)S(1)} %get-tuple-element.121), channel_id=1, source_target_pairs={{0,4},{1,9},{2,6},{3,11},{4,0},{5,13},{6,2},{7,15},{8,12},{9,1},{1... | collective-permute-start | bytes 393224 | tf_op jit(solution)/shard_map/ppermute | solution.py:498
  104.9 7.4 %collective-permute-start.34 = (bf16[16,32,128]{2,1,0:T(8,128)(2,1)S(1)}, bf16[16,32,128]{2,1,0:T(8,128)(2,1)S(1)}, u32[]{:S(2)}, u32[]{:S(2)}) collective-permute-start(bf16[16,32,128]{2,1,0:T(8,128)(2,1)S(1)} %get-tuple-element.131.panel_ref.refs_0_), channel_id=1, source_target_pairs={{0,16},{1,17},{2,18},{3,19},{4,20},{5,21},{6,22},{7,23},{8,24},{9,... | collective-permute-start | bytes 393224 | tf_op jit(solution)/shard_map/ppermute | solution.py:498
  104.9 10.2 %collective-permute-start.31 = (bf16[16,32,128]{2,1,0:T(8,128)(2,1)S(1)}, bf16[16,32,128]{2,1,0:T(8,128)(2,1)S(1)}, u32[]{:S(2)}, u32[]{:S(2)}) collective-permute-start(bf16[16,32,128]{2,1,0:T(8,128)(2,1)S(1)} %get-tuple-element.131.panel_ref.refs_0_), channel_id=1, source_target_pairs={{0,4},{1,9},{2,6},{3,11},{4,0},{5,13},{6,2},{7,15},{8,12},{9,1},{1... | collective-permute-start | bytes 393224 | tf_op jit(solution)/shard_map/ppermute | solution.py:498
  112.3 5.6 %collective-permute-start.36 = (bf16[16,32,128]{2,1,0:T(8,128)(2,1)S(1)}, bf16[16,32,128]{2,1,0:T(8,128)(2,1)S(1)}, u32[]{:S(2)}, u32[]{:S(2)}) collective-permute-start(bf16[16,32,128]{2,1,0:T(8,128)(2,1)S(1)} %get-tuple-element.133.refs_4_), channel_id=1, source_target_pairs={{0,8},{1,5},{2,10},{3,7},{4,12},{5,1},{6,14},{7,3},{8,0},{9,13},{1... | collective-permute-start | bytes 393224 | tf_op jit(solution)/shard_map/ppermute | solution.py:498
  114.9 5.0 %collective-permute-start.32 = (bf16[16,32,128]{2,1,0:T(8,128)(2,1)S(1)}, bf16[16,32,128]{2,1,0:T(8,128)(2,1)S(1)}, u32[]{:S(2)}, u32[]{:S(2)}) collective-permute-start(bf16[16,32,128]{2,1,0:T(8,128)(2,1)S(1)} %get-tuple-element.131.panel_ref.refs_0_), channel_id=1, source_target_pairs={{0,8},{1,5},{2,10},{3,7},{4,12},{5,1},{6,14},{7,3},{8,0},{9,13},{1... | collective-permute-start | bytes 393224 | tf_op jit(solution)/shard_map/ppermute | solution.py:498
  115.0 6.3 %collective-permute-start.35 = (bf16[16,32,128]{2,1,0:T(8,128)(2,1)S(1)}, bf16[16,32,128]{2,1,0:T(8,128)(2,1)S(1)}, u32[]{:S(2)}, u32[]{:S(2)}) collective-permute-start(bf16[16,32,128]{2,1,0:T(8,128)(2,1)S(1)} %get-tuple-element.133.refs_4_), channel_id=1, source_target_pairs={{0,4},{1,9},{2,6},{3,11},{4,0},{5,13},{6,2},{7,15},{8,12},{9,1},{1... | collective-permute-start | bytes 393224 | tf_op jit(solution)/shard_map/ppermute | solution.py:498
  115.1 6.2 %collective-permute-start.33 = (bf16[16,32,128]{2,1,0:T(8,128)(2,1)S(1)}, bf16[16,32,128]{2,1,0:T(8,128)(2,1)S(1)}, u32[]{:S(2)}, u32[]{:S(2)}) collective-permute-start(bf16[16,32,128]{2,1,0:T(8,128)(2,1)S(1)} %collective-permute-done.31.refs_1_), channel_id=1, source_target_pairs={{0,8},{1,5},{2,10},{3,7},{4,12},{5,1},{6,14},{7,3},{8,0},{9,13},{1... | collective-permute-start | bytes 393224 | tf_op jit(solution)/shard_map/ppermute | solution.py:498
  117.8 5.0 %collective-permute-start.37 = (bf16[16,32,128]{2,1,0:T(8,128)(2,1)S(1)}, bf16[16,32,128]{2,1,0:T(8,128)(2,1)S(1)}, u32[]{:S(2)}, u32[]{:S(2)}) collective-permute-start(bf16[16,32,128]{2,1,0:T(8,128)(2,1)S(1)} %collective-permute-done.36.refs_6_), channel_id=1, source_target_pairs={{0,4},{1,9},{2,6},{3,11},{4,0},{5,13},{6,2},{7,15},{8,12},{9,1},{1... | collective-permute-start | bytes 393224 | tf_op jit(solution)/shard_map/ppermute | solution.py:498
  119.0 1.2 collective-permute-start.38
  127.1 7.5 %collective-permute-start.39 = (bf16[17,32,128]{2,1,0:T(8,128)(2,1)S(1)}, bf16[17,32,128]{2,1,0:T(8,128)(2,1)S(1)}, u32[]{:S(2)}, u32[]{:S(2)}) collective-permute-start(bf16[17,32,128]{2,1,0:T(8,128)(2,1)S(1)} %get-tuple-element.141.refs_4_), channel_id=1, source_target_pairs={{0,4},{1,9},{2,6},{3,11},{4,0},{5,13},{6,2},{7,15},{8,12},{9,1},{1... | collective-permute-start | bytes 417800 | tf_op jit(solution)/shard_map/ppermute | solution.py:498
  128.2 5.0 %collective-permute-start.40 = (bf16[16,32,128]{2,1,0:T(8,128)(2,1)S(1)}, bf16[16,32,128]{2,1,0:T(8,128)(2,1)S(1)}, u32[]{:S(2)}, u32[]{:S(2)}) collective-permute-start(bf16[16,32,128]{2,1,0:T(8,128)(2,1)S(1)} %get-tuple-element.143), channel_id=1, source_target_pairs={{0,8},{1,5},{2,10},{3,7},{4,12},{5,1},{6,14},{7,3},{8,0},{9,13},{1... | collective-permute-start | bytes 393224 | tf_op jit(solution)/shard_map/ppermute | solution.py:498
  129.2 5.4 %collective-permute-start.42 = (bf16[16,32,128]{2,1,0:T(8,128)(2,1)S(1)}, bf16[16,32,128]{2,1,0:T(8,128)(2,1)S(1)}, u32[]{:S(2)}, u32[]{:S(2)}) collective-permute-start(bf16[16,32,128]{2,1,0:T(8,128)(2,1)S(1)} %get-tuple-element.145), channel_id=1, source_target_pairs={{0,8},{1,5},{2,10},{3,7},{4,12},{5,1},{6,14},{7,3},{8,0},{9,13},{1... | collective-permute-start | bytes 393224 | tf_op jit(solution)/shard_map/ppermute | solution.py:498
  130.2 1.2 collective-permute-start.41
  134.6 6.0 %collective-permute-start.45 = (bf16[17,32,128]{2,1,0:T(8,128)(2,1)S(1)}, bf16[17,32,128]{2,1,0:T(8,128)(2,1)S(1)}, u32[]{:S(2)}, u32[]{:S(2)}) collective-permute-start(bf16[17,32,128]{2,1,0:T(8,128)(2,1)S(1)} %get-tuple-element.149.refs_3_), channel_id=1, source_target_pairs={{0,8},{1,5},{2,10},{3,7},{4,12},{5,1},{6,14},{7,3},{8,0},{9,13},{1... | collective-permute-start | bytes 417800 | tf_op jit(solution)/shard_map/ppermute | solution.py:498
  135.7 5.0 %collective-permute-start.44 = (bf16[16,32,128]{2,1,0:T(8,128)(2,1)S(1)}, bf16[16,32,128]{2,1,0:T(8,128)(2,1)S(1)}, u32[]{:S(2)}, u32[]{:S(2)}) collective-permute-start(bf16[16,32,128]{2,1,0:T(8,128)(2,1)S(1)} %get-tuple-element.148), channel_id=1, source_target_pairs={{0,4},{1,9},{2,6},{3,11},{4,0},{5,13},{6,2},{7,15},{8,12},{9,1},{1... | collective-permute-start | bytes 393224 | tf_op jit(solution)/shard_map/ppermute | solution.py:498
  140.8 7.5 %collective-permute-start.46 = (bf16[17,32,128]{2,1,0:T(8,128)(2,1)S(1)}, bf16[17,32,128]{2,1,0:T(8,128)(2,1)S(1)}, u32[]{:S(2)}, u32[]{:S(2)}) collective-permute-start(bf16[17,32,128]{2,1,0:T(8,128)(2,1)S(1)} %get-tuple-element.150.after_ref.refs_4_), channel_id=1, source_target_pairs={{0,16},{1,17},{2,18},{3,19},{4,20},{5,21},{6,22},{7,23},{8,24},{9,... | collective-permute-start | bytes 417800 | tf_op jit(solution)/shard_map/ppermute | solution.py:498
  142.5 5.4 %collective-permute-start.43 = (bf16[16,32,128]{2,1,0:T(8,128)(2,1)S(1)}, bf16[16,32,128]{2,1,0:T(8,128)(2,1)S(1)}, u32[]{:S(2)}, u32[]{:S(2)}) collective-permute-start(bf16[16,32,128]{2,1,0:T(8,128)(2,1)S(1)} %get-tuple-element.146), channel_id=1, source_target_pairs={{0,4},{1,9},{2,6},{3,11},{4,0},{5,13},{6,2},{7,15},{8,12},{9,1},{1... | collective-permute-start | bytes 393224 | tf_op jit(solution)/shard_map/ppermute | solution.py:498
  142.9 5.0 %collective-permute-start.47 = (f32[8,128]{1,0:T(8,128)S(1)}, f32[8,128]{1,0:T(8,128)S(1)}, u32[]{:S(2)}, u32[]{:S(2)}) collective-permute-start(f32[8,128]{1,0:T(8,128)S(1)} %get-tuple-element.156.refs_9_), channel_id=1, source_target_pairs={{0,2},{1,3},{2,0},{3,1},{4,6},{5,7},{6,4},{7,5},{8,10},{9,11},{10,... | collective-permute-start | bytes 12296 | tf_op jit(solution)/shard_map/ppermute | solution.py:484

commit v6 on v5

--- a/solution.py
+++ b/solution.py
@@ -17,6 +17,7 @@
 MIB = 1024 * 1024
 GROUP = 8
 HEAD_GROUP = 16
+SMALL_VMEM = 6 * MIB
 
 
 def contract_last(left, right):
@@ -258,14 +259,8 @@
     return pl.BlockSpec(shape, lambda i, *_: (0,) * len(shape))
 
 
-def vmem_limit(peers):
-    return (8 + peers + peers // 4) * MIB
-
-
-def params(peers=8):
-    return pltpu.CompilerParams(
-        dimension_semantics=("arbitrary",), vmem_limit_bytes=vmem_limit(peers)
-    )
+def params(limit):
+    return pltpu.CompilerParams(dimension_semantics=("arbitrary",), vmem_limit_bytes=limit)
 
 
 def local_adjoint(index, panel, blocks):
@@ -290,7 +285,7 @@
                 whole(8, rows),
             ),
         ),
-        compiler_params=params(),
+        compiler_params=params(SMALL_VMEM),
         cost_estimate=pl.CostEstimate(
             flops=2 * scen_rows * blocks.size, bytes_accessed=2 * blocks.size, transcendentals=0
         ),
@@ -344,7 +339,7 @@
                 pltpu.VMEM((scen_rows, rows), jnp.float32),
             ],
         ),
-        compiler_params=params(peers),
+        compiler_params=params((4 + peers + peers // 4) * MIB),
         cost_estimate=pl.CostEstimate(
             flops=4 * scen_rows * heads.size,
             bytes_accessed=2 * heads.size + 14 * flows.size + 4 * peers * panels[0].size,
@@ -380,7 +375,7 @@
         out_shape=out_shape,
         in_specs=[vmem] * len(operands) + [pl.BlockSpec(memory_space=pl.ANY)] * len(after),
         out_specs=[vmem] * len(out_shape),
-        compiler_params=pltpu.CompilerParams(vmem_limit_bytes=vmem_limit(8)),
+        compiler_params=pltpu.CompilerParams(vmem_limit_bytes=SMALL_VMEM),
         cost_estimate=small_cost(*operands),
         name="fold",
     )(*operands, *after)
@@ -400,7 +395,7 @@
             jax.ShapeDtypeStruct((1, 1) if last else level.shape, jnp.float32),
             jax.ShapeDtypeStruct(level.shape, jnp.float32),
         ),
-        compiler_params=pltpu.CompilerParams(vmem_limit_bytes=vmem_limit(8)),
+        compiler_params=pltpu.CompilerParams(vmem_limit_bytes=SMALL_VMEM),
         cost_estimate=small_cost(kept, *arrived, base),
         name="settle",
     )(kept, *arrived, loss, base, risk, excess, level, *sums)
@@ -427,7 +422,7 @@
             out_specs=whole(*duals.shape),
             scratch_shapes=[pltpu.VMEM(duals.shape, jnp.float32)],
         ),
-        compiler_params=params(),
+        compiler_params=params(SMALL_VMEM),
         cost_estimate=pl.CostEstimate(
             flops=2 * scen_rows * blocks.size, bytes_accessed=2 * blocks.size, transcendentals=0
         ),
@@ -450,13 +445,14 @@
         ),
         in_specs=[vmem, vmem] + [pl.BlockSpec(memory_space=pl.ANY)] * len(after),
         out_specs=(vmem, vmem),
-        compiler_params=pltpu.CompilerParams(vmem_limit_bytes=vmem_limit(8)),
+        compiler_params=pltpu.CompilerParams(vmem_limit_bytes=SMALL_VMEM),
         cost_estimate=small_cost(arrived),
         name="relay",
     )(arrived, risk_sum, *after)
 
 
-def prepare_kernel(risk_ref, excess_ref, level_ref, after, risk_out, excess_out, level_out, sum_out):
+def prepare_kernel(risk_ref, excess_ref, level_ref, *refs):
+    risk_out, excess_out, level_out, sum_out = refs[-4:]
     scen_rows = risk_out.shape[0]
     square = (scen_rows, scen_rows)
     same = lax.broadcasted_iota(jnp.int32, square, 0) == lax.broadcasted_iota(jnp.int32, square, 1)
@@ -472,11 +468,12 @@
     return pl.pallas_call(
         prepare_kernel,
         out_shape=[jax.ShapeDtypeStruct(shape, jnp.float32) for shape in (wide, wide, flat, flat)],
-        in_specs=[pl.BlockSpec(memory_space=pltpu.VMEM)] * 3 + [pl.BlockSpec(memory_space=pl.ANY)],
-        compiler_params=pltpu.CompilerParams(vmem_limit_bytes=vmem_limit(8)),
+        in_specs=[pl.BlockSpec(memory_space=pltpu.VMEM)] * 3
+        + [pl.BlockSpec(memory_space=pl.ANY)] * len(after),
+        compiler_params=pltpu.CompilerParams(vmem_limit_bytes=SMALL_VMEM),
         cost_estimate=small_cost(risk),
         name="prepare",
-    )(risk.reshape(1, -1), excess.reshape(1, -1), level.reshape(1, 1), after)
+    )(risk.reshape(1, -1), excess.reshape(1, -1), level.reshape(1, 1), *after)
 
 
 def swap(value, axis, distance):
@@ -548,7 +545,11 @@
         panels, risk_sum = gather_panels(half, risk_sum, (token,))
         if kind == "first":
             risk, excess_now, level, risk_sum = prepare(
-                risk_duals, excess, threshold, rows, panels[net_size // 2]
+                risk_duals,
+                excess,
+                threshold,
+                rows,
+                (panels[net_size // 2], head_blocks, arc_flows),
             )
         if kind == "early":
             for stride in early[:-1]:
@@ -574,15 +575,20 @@
             risk_sum = risk_sum + swap(risk_sum, "scen", 1)
             after = (risk_sum,)
         tops = sorted(inner(net_size), key=lambda k: (-k.bit_count(), -k))[:-1]
-        groups = [(tops[0], 1)] + [(top,) for top in tops[1:] if top != 1]
+        groups = [(top,) for top in tops if top != 1] + [(1,)]
         loss, loss_top = sends[net_size - 1], net_size - 1
-        direct = swap_net(sends[2], 2)
-        after += (direct,)
+        ahead = {5: swap_net(sends[5], last_hop(5))}
+        after += (ahead[5],)
         for group in groups:
             terms = []
             for top in group:
                 below = sorted(children(top, net_size))
-                terms.append((kept[top], [swap_net(sends[k], last_hop(k)) for k in below]))
+                terms.append(
+                    (
+                        kept[top],
+                        [ahead[k] if k in ahead else swap_net(sends[k], last_hop(k)) for k in below],
+                    )
+                )
             chain = loss_top ^ last_hop(loss_top) == group[0]
             extras = (risk_sum,) if group[0] == net_size // 2 and kind != "early" else ()
             folded, passed = fold(terms, loss if chain else None, extras, after)
@@ -594,7 +600,7 @@
                 (risk_sum,) = passed
         base = local_forward(touched, bar, local_blocks, duals, demand, loss)
         below = sorted(children(0, net_size))
-        arrived = [direct if k == 2 else swap_net(sends[k], last_hop(k)) for k in below]
+        arrived = [swap_net(sends[k], last_hop(k)) for k in below]
         sums = (risk_sum, zero)
         if kind != "early":
             for stride in early[:-1]:

time: 149 us -> 151 us (1.013)
    ppermute x6, waiting for transfers between devices: 3.68 us -> 5.37 us  [swap(): return lax.ppermute(value, axis, [(i, i ^ distance) for i in range(size)])]
  transfers between devices with their start and end apart: 48 -> 48, of which waited for: 27 -> 23; matrix products, arithmetic and copies ran while one was open for 0% -> 0% of each run, Pallas kernels for 16% -> 16%
where the time goes in v6:
time: 151 us; the launch traced here: 150 us
  starting transfers between devices  53.4 us (35%)
  waiting for transfers between devices  44.4 us (29%)
  Pallas kernels  38.7 us (26%)
  local copies, waits for them, and re-layouts  11.4 us (8%)
  between operations  1.57 us (1%)
    ppermute x42, starting transfers between devices, swap_net(): return lax.ppermute(value, ('net', 'scen'), pairs)  50.7 us
    ppermute x42, waiting for transfers between devices, swap_net(): return lax.ppermute(value, ('net', 'scen'), pairs)  39 us
    pallas_call x3, Pallas kernels, local_adjoint(): pl.pallas_call(functools.partial(local_adjoint_kernel, touches, group), o...  12.9 us
    pallas_call x3, Pallas kernels, head_step(): pl.pallas_call(functools.partial(head_kernel, group, steps, peers, late,...  12.7 us
    unnamed x32, local copies, waits for them, and re-layouts  11.4 us
    pallas_call x3, Pallas kernels, local_forward(): pl.pallas_call(functools.partial(local_forward_kernel, touches, group, st...  9.93 us
    ppermute x6, waiting for transfers between devices, swap(): return lax.ppermute(value, axis, [(i, i ^ distance) for i in range(size)])  5.37 us
  transfers between devices with their start and end apart: 48, of which 23 were waited for; matrix products, arithmetic and copies ran while one was open for 0% of the time, Pallas kernels for 16%

profile of v6, /device:TPU:0, one launch (start us, length us, event | category | flops | bytes accessed | tf_op | source)
XLA Modules:
  0.0 150.2 jit_solution(14107005221518558128)
XLA Ops:
  0.7 0.9 copy-done
  1.6 4.1 %collective-permute-start.3 = (bf16[16,32,128]{2,1,0:T(8,128)(2,1)S(1)}, bf16[16,32,128]{2,1,0:T(8,128)(2,1)S(1)}, u32[]{:S(2)}, u32[]{:S(2)}) collective-permute-start(bf16[16,32,128]{2,1,0:T(8,128)(2,1)S(1)} %fusion.2.panel_ref.refs_0_), channel_id=1, source_target_pairs={{0,16},{1,17},{2,18},{3,19},{4,20},{5,21},{6,22},{7,23},{8,24},{9,... | collective-permute-start | bytes 393224 | tf_op jit(solution)/shard_map/ppermute | solution.py:495
  5.7 1.5 collective-permute-start
  7.2 3.4 %copy-done.1 = bf16[64,4,128,128]{3,2,1,0:T(8,128)(2,1)S(1)} copy-done((bf16[64,4,128,128]{3,2,1,0:T(8,128)(2,1)S(1)}, bf16[64,4,128,128]{3,2,1,0:T(8,128)(2,1)}, u32[]{:S(2)}) %copy-start.1) | copy-done | bytes 8388632
  10.6 0.7 copy-done.10
  11.3 4.3 %local_adjoint.3 = (f32[32,8192]{1,0:T(8,128)S(1)}, f32[8,128]{1,0:T(8,128)S(1)}) custom-call(s32[4,64]{1,0:T(4,128)S(1)} %bitcast.27, bf16[16,32,128]{2,1,0:T(8,128)(2,1)S(1)} %fusion.2.panel_ref.refs_0_, bf16[64,4,128,128]{3,2,1,0:T(8,128)(2,1)S(1)} %copy-done.1), custom_call_target="tpu_custom_call" | custom-call | flops 268435456 | bytes 8388608 | tf_op jit(solution)/shard_map/local_adjoint/pallas_call | solution.py:270
  15.6 1.0 copy-done.6
  17.2 1.6 %collective-permute-start.5 = (bf16[16,32,128]{2,1,0:T(8,128)(2,1)}, bf16[16,32,128]{2,1,0:T(8,128)(2,1)}, u32[]{:S(2)}, u32[]{:S(2)}) collective-permute-start(bf16[16,32,128]{2,1,0:T(8,128)(2,1)} %get-tuple-element.78.refs_0_.refs_4_), channel_id=1, source_target_pairs={{0,8},{1,5},{2,10},{3,7},{4,12},{5,1},{6,14},{7,3},{8,0},{9,13},{1... | collective-permute-start | bytes 393224 | tf_op jit(solution)/shard_map/ppermute | solution.py:495
  20.8 1.6 %collective-permute-start.2 = (bf16[16,32,128]{2,1,0:T(8,128)(2,1)}, bf16[16,32,128]{2,1,0:T(8,128)(2,1)S(1)}, u32[]{:S(2)}, u32[]{:S(2)}) collective-permute-start(bf16[16,32,128]{2,1,0:T(8,128)(2,1)} %collective-permute-done.refs_1_), channel_id=1, source_target_pairs={{0,8},{1,5},{2,10},{3,7},{4,12},{5,1},{6,14},{7,3},{8,0},{9,13},{1... | collective-permute-start | bytes 393224 | tf_op jit(solution)/shard_map/ppermute | solution.py:495
  22.4 0.9 collective-permute-done.5.refs_6_
  23.9 0.7 fusion.index_ref
  24.6 0.7 collective-permute-done.1.refs_2_
  25.3 2.6 %collective-permute-done.2.refs_3_ = bf16[16,32,128]{2,1,0:T(8,128)(2,1)S(1)} collective-permute-done((bf16[16,32,128]{2,1,0:T(8,128)(2,1)}, bf16[16,32,128]{2,1,0:T(8,128)(2,1)S(1)}, u32[]{:S(2)}, u32[]{:S(2)}) %collective-permute-start.2) | collective-permute-done | bytes 131104 | tf_op jit(solution)/shard_map/ppermute | solution.py:495
  28.5 1.2 copy-done.7
  29.8 0.8 copy-done.8
  30.5 4.9 %head_step.3 = (f32[32,8192]{1,0:T(8,128)S(1)}, bf16[32,8192]{1,0:T(8,128)(2,1)S(1)}, f32[32,128]{1,0:T(8,128)S(1)}, f32[8,128]{1,0:T(8,128)S(1)}, f32[8,128]{1,...) custom-call(s32[64]{0:T(128)S(1)} %fusion.index_ref, ...), custom_call_target="tpu_custom_call" | custom-call | flops 134217728 | bytes 7864320 | tf_op jit(solution)/shard_map/head_step/pallas_call | solution.py:307
  36.0 1.5 collective-permute-start.11
  37.5 4.4 %collective-permute-done.11.refs_3_.refs_1_ = bf16[16,32,128]{2,1,0:T(8,128)(2,1)S(1)} collective-permute-done((bf16[16,32,128]{2,1,0:T(8,128)(2,1)S(1)}, bf16[16,32,128]{2,1,0:T(8,128)(2,1)S(1)}, u32[]{:S(2)}, u32[]{:S(2)}) %collective-permute-start.11) | collective-permute-done | bytes 131104 | tf_op jit(solution)/shard_map/ppermute | solution.py:495
  42.1 1.7 %collective-permute-start.13 = (bf16[17,32,128]{2,1,0:T(8,128)(2,1)S(1)}, bf16[17,32,128]{2,1,0:T(8,128)(2,1)S(1)}, u32[]{:S(2)}, u32[]{:S(2)}) collective-permute-start(bf16[17,32,128]{2,1,0:T(8,128)(2,1)S(1)} %fold.10.refs_3_), channel_id=1, source_target_pairs={{0,8},{1,5},{2,10},{3,7},{4,12},{5,1},{6,14},{7,3},{8,0},{9,13},{1... | collective-permute-start | bytes 417800 | tf_op jit(solution)/shard_map/ppermute | solution.py:495
  44.1 1.6 %collective-permute-start.10 = (bf16[16,32,128]{2,1,0:T(8,128)(2,1)S(1)}, bf16[16,32,128]{2,1,0:T(8,128)(2,1)S(1)}, u32[]{:S(2)}, u32[]{:S(2)}) collective-permute-start(bf16[16,32,128]{2,1,0:T(8,128)(2,1)S(1)} %get-tuple-element.86), channel_id=1, source_target_pairs={{0,8},{1,5},{2,10},{3,7},{4,12},{5,1},{6,14},{7,3},{8,0},{9,13},{1... | collective-permute-start | bytes 393224 | tf_op jit(solution)/shard_map/ppermute | solution.py:495
  45.8 2.9 %collective-permute-done.8.refs_1_ = bf16[16,32,128]{2,1,0:T(8,128)(2,1)S(1)} collective-permute-done((bf16[16,32,128]{2,1,0:T(8,128)(2,1)S(1)}, bf16[16,32,128]{2,1,0:T(8,128)(2,1)S(1)}, u32[]{:S(2)}, u32[]{:S(2)}) %collective-permute-start.8) | collective-permute-done | bytes 131104 | tf_op jit(solution)/shard_map/ppermute | solution.py:495
  48.8 0.7 collective-permute-start.9
  50.0 1.6 %collective-permute-start.15 = (f32[8,128]{1,0:T(8,128)S(1)}, f32[8,128]{1,0:T(8,128)S(1)}, u32[]{:S(2)}, u32[]{:S(2)}) collective-permute-start(f32[8,128]{1,0:T(8,128)S(1)} %get-tuple-element.97.refs_9_), channel_id=1, source_target_pairs={{0,2},{1,3},{2,0},{3,1},{4,6},{5,7},{6,4},{7,5},{8,10},{9,11},{10,... | collective-permute-start | bytes 12296 | tf_op jit(solution)/shard_map/ppermute | solution.py:481
  51.6 3.4 %copy-done.2 = bf16[64,4,128,128]{3,2,1,0:T(8,128)(2,1)S(1)} copy-done((bf16[64,4,128,128]{3,2,1,0:T(8,128)(2,1)S(1)}, bf16[64,4,128,128]{3,2,1,0:T(8,128)(2,1)}, u32[]{:S(2)}) %copy-start.2) | copy-done | bytes 8388632
  55.0 3.3 %local_forward.3.refs_5_ = f32[16,32,128]{2,1,0:T(8,128)S(1)} custom-call(s32[4,64]{1,0:T(4,128)S(1)} %bitcast.28, bf16[32,8192]{1,0:T(8,128)(2,1)S(1)} %get-tuple-element.93.bar_ref, bf16[64,4,128,128]{3,2,1,0:T(8,128)(2,1)S(1)} %copy-done.2, f32[16,32,128]{2,1,0:T(8,128)S(1)} %bitcast_bitcast_fusion.duals_ref, f32[32,2048]{1,0:T(8,128)S(1)} %copy-done.5, ...), custom_call_target="tpu_custom_call" | custom-call | flops 268435456 | bytes 8388608 | tf_op jit(solution)/shard_map/local_forward/pallas_call | solution.py:409
  58.6 2.7 %collective-permute-start.19 = (bf16[16,32,128]{2,1,0:T(8,128)(2,1)S(1)}, bf16[16,32,128]{2,1,0:T(8,128)(2,1)S(1)}, u32[]{:S(2)}, u32[]{:S(2)}) collective-permute-start(bf16[16,32,128]{2,1,0:T(8,128)(2,1)S(1)} %get-tuple-element.98.panel_ref.refs_0_), channel_id=1, source_target_pairs={{0,16},{1,17},{2,18},{3,19},{4,20},{5,21},{6,22},{7,23},{8,24},{9,... | collective-permute-start | bytes 393224 | tf_op jit(solution)/shard_map/ppermute | solution.py:495
  61.3 1.3 collective-permute-start.16
  62.6 4.3 %local_adjoint.4 = (f32[32,8192]{1,0:T(8,128)S(1)}, f32[8,128]{1,0:T(8,128)S(1)}) custom-call(s32[4,64]{1,0:T(4,128)S(1)} %bitcast.29, bf16[16,32,128]{2,1,0:T(8,128)(2,1)S(1)} %get-tuple-element.98.panel_ref.refs_0_, bf16[64,4,128,128]{3,2,1,0:T(8,128)(2,1)S(1)} %bitcast.23), custom_call_target="tpu_custom_call" | custom-call | flops 268435456 | bytes 8388608 | tf_op jit(solution)/shard_map/local_adjoint/pallas_call | solution.py:270
  66.9 1.6 %collective-permute-start.21 = (bf16[16,32,128]{2,1,0:T(8,128)(2,1)S(1)}, bf16[16,32,128]{2,1,0:T(8,128)(2,1)S(1)}, u32[]{:S(2)}, u32[]{:S(2)}) collective-permute-start(bf16[16,32,128]{2,1,0:T(8,128)(2,1)S(1)} %get-tuple-element.101.refs_4_), channel_id=1, source_target_pairs={{0,8},{1,5},{2,10},{3,7},{4,12},{5,1},{6,14},{7,3},{8,0},{9,13},{1... | collective-permute-start | bytes 393224 | tf_op jit(solution)/shard_map/ppermute | solution.py:495
  69.0 0.7 collective-permute-start.20
  69.7 1.5 collective-permute-start.18
  71.2 1.6 %collective-permute-done.21.refs_6_ = bf16[16,32,128]{2,1,0:T(8,128)(2,1)S(1)} collective-permute-done((bf16[16,32,128]{2,1,0:T(8,128)(2,1)S(1)}, bf16[16,32,128]{2,1,0:T(8,128)(2,1)S(1)}, u32[]{:S(2)}, u32[]{:S(2)}) %collective-permute-start.21) | collective-permute-done | bytes 131104 | tf_op jit(solution)/shard_map/ppermute | solution.py:495
  72.9 0.9 collective-permute-start.22
  74.3 3.0 %collective-permute-done.23.refs_15_ = f32[8,128]{1,0:T(8,128)S(1)} collective-permute-done((f32[8,128]{1,0:T(8,128)S(1)}, f32[8,128]{1,0:T(8,128)S(1)}, u32[]{:S(2)}, u32[]{:S(2)}) %collective-permute-start.23) | collective-permute-done | bytes 4128 | tf_op jit(solution)/shard_map/ppermute | solution.py:481
  77.8 3.6 %head_step.4 = (f32[32,8192]{1,0:T(8,128)S(1)}, bf16[32,8192]{1,0:T(8,128)(2,1)S(1)}, f32[32,128]{1,0:T(8,128)S(1)}, f32[8,128]{1,0:T(8,128)S(1)}, f32[8,128]{1,...) custom-call(s32[64]{0:T(128)S(1)} %fusion.index_ref, ...), custom_call_target="tpu_custom_call" | custom-call | flops 134217728 | bytes 7864320 | tf_op jit(solution)/shard_map/head_step/pallas_call | solution.py:307
  81.4 0.9 collective-permute-start.28
  82.3 1.2 collective-permute-start.27
  83.5 6.8 %collective-permute-done.27.refs_3_.refs_1_ = bf16[16,32,128]{2,1,0:T(8,128)(2,1)S(1)} collective-permute-done((bf16[16,32,128]{2,1,0:T(8,128)(2,1)S(1)}, bf16[16,32,128]{2,1,0:T(8,128)(2,1)S(1)}, u32[]{:S(2)}, u32[]{:S(2)}) %collective-permute-start.27) | collective-permute-done | bytes 131104 | tf_op jit(solution)/shard_map/ppermute | solution.py:495
  90.4 1.5 collective-permute-start.29
  92.5 3.7 %collective-permute-done.29.refs_2_ = bf16[17,32,128]{2,1,0:T(8,128)(2,1)S(1)} collective-permute-done((bf16[17,32,128]{2,1,0:T(8,128)(2,1)S(1)}, bf16[17,32,128]{2,1,0:T(8,128)(2,1)S(1)}, u32[]{:S(2)}, u32[]{:S(2)}) %collective-permute-start.29) | collective-permute-done | bytes 139296 | tf_op jit(solution)/shard_map/ppermute | solution.py:495
  96.5 1.5 collective-permute-start.26
  98.0 2.4 %collective-permute-start.25 = (bf16[16,32,128]{2,1,0:T(8,128)(2,1)S(1)}, bf16[16,32,128]{2,1,0:T(8,128)(2,1)S(1)}, u32[]{:S(2)}, u32[]{:S(2)}) collective-permute-start(bf16[16,32,128]{2,1,0:T(8,128)(2,1)S(1)} %fold.12), channel_id=1, source_target_pairs={{0,4},{1,9},{2,6},{3,11},{4,0},{5,13},{6,2},{7,15},{8,12},{9,1},{1... | collective-permute-start | bytes 393224 | tf_op jit(solution)/shard_map/ppermute | solution.py:495
  100.4 3.3 %local_forward.4.refs_5_ = f32[16,32,128]{2,1,0:T(8,128)S(1)} custom-call(s32[4,64]{1,0:T(4,128)S(1)} %bitcast.30, bf16[32,8192]{1,0:T(8,128)(2,1)S(1)} %get-tuple-element.115.bar_ref, bf16[64,4,128,128]{3,2,1,0:T(8,128)(2,1)S(1)} %bitcast.23, f32[16,32,128]{2,1,0:T(8,128)S(1)} %get-tuple-element.116.duals_ref, f32[32,2048]{1,0:T(8,128)S(1)} %copy-done.5, ...), custom_call_target="tpu_custom_call" | custom-call | flops 268435456 | bytes 8388608 | tf_op jit(solution)/shard_map/local_forward/pallas_call | solution.py:409
  103.9 1.5 collective-permute-done.30.refs_3_
  106.6 1.8 %collective-permute-start.31 = (bf16[16,32,128]{2,1,0:T(8,128)(2,1)S(1)}, bf16[16,32,128]{2,1,0:T(8,128)(2,1)S(1)}, u32[]{:S(2)}, u32[]{:S(2)}) collective-permute-start(bf16[16,32,128]{2,1,0:T(8,128)(2,1)S(1)} %get-tuple-element.121.panel_ref.refs_0_), channel_id=1, source_target_pairs={{0,4},{1,9},{2,6},{3,11},{4,0},{5,13},{6,2},{7,15},{8,12},{9,1},{1... | collective-permute-start | bytes 393224 | tf_op jit(solution)/shard_map/ppermute | solution.py:495
  108.4 4.3 %local_adjoint.5 = (f32[32,8192]{1,0:T(8,128)S(1)}, f32[8,128]{1,0:T(8,128)S(1)}) custom-call(s32[4,64]{1,0:T(4,128)S(1)} %bitcast.31, bf16[16,32,128]{2,1,0:T(8,128)(2,1)S(1)} %get-tuple-element.121.panel_ref.refs_0_, bf16[64,4,128,128]{3,2,1,0:T(8,128)(2,1)S(1)} %bitcast.23), custom_call_target="tpu_custom_call" | custom-call | flops 268435456 | bytes 8388608 | tf_op jit(solution)/shard_map/local_adjoint/pallas_call | solution.py:270
  113.0 1.6 %collective-permute-start.36 = (bf16[16,32,128]{2,1,0:T(8,128)(2,1)S(1)}, bf16[16,32,128]{2,1,0:T(8,128)(2,1)S(1)}, u32[]{:S(2)}, u32[]{:S(2)}) collective-permute-start(bf16[16,32,128]{2,1,0:T(8,128)(2,1)S(1)} %get-tuple-element.123.refs_4_), channel_id=1, source_target_pairs={{0,8},{1,5},{2,10},{3,7},{4,12},{5,1},{6,14},{7,3},{8,0},{9,13},{1... | collective-permute-start | bytes 393224 | tf_op jit(solution)/shard_map/ppermute | solution.py:495
  115.1 1.5 %collective-permute-start.35 = (bf16[16,32,128]{2,1,0:T(8,128)(2,1)S(1)}, bf16[16,32,128]{2,1,0:T(8,128)(2,1)S(1)}, u32[]{:S(2)}, u32[]{:S(2)}) collective-permute-start(bf16[16,32,128]{2,1,0:T(8,128)(2,1)S(1)} %get-tuple-element.123.refs_4_), channel_id=1, source_target_pairs={{0,4},{1,9},{2,6},{3,11},{4,0},{5,13},{6,2},{7,15},{8,12},{9,1},{1... | collective-permute-start | bytes 393224 | tf_op jit(solution)/shard_map/ppermute | solution.py:495
  117.3 0.8 collective-permute-done.36.refs_6_
  118.1 1.5 %collective-permute-start.37 = (bf16[16,32,128]{2,1,0:T(8,128)(2,1)S(1)}, bf16[16,32,128]{2,1,0:T(8,128)(2,1)S(1)}, u32[]{:S(2)}, u32[]{:S(2)}) collective-permute-start(bf16[16,32,128]{2,1,0:T(8,128)(2,1)S(1)} %collective-permute-done.36.refs_6_), channel_id=1, source_target_pairs={{0,4},{1,9},{2,6},{3,11},{4,0},{5,13},{6,2},{7,15},{8,12},{9,1},{1... | collective-permute-start | bytes 393224 | tf_op jit(solution)/shard_map/ppermute | solution.py:495
  119.6 1.2 collective-permute-done.38.refs_15_
  120.8 0.9 collective-permute-done.33.refs_3_
  121.7 1.4 collective-permute-done.37.refs_7_
  123.0 4.2 %head_step.5 = (f32[32,8192]{1,0:T(8,128)}, bf16[32,8192]{1,0:T(8,128)(2,1)S(1)}, f32[32,128]{1,0:T(8,128)S(1)}, f32[8,128]{1,0:T(8,128)S(1)}, f32[8,128]{1,0:T(...) custom-call(s32[64]{0:T(128)S(1)} %fusion.index_ref, ...), custom_call_target="tpu_custom_call" | custom-call | flops 134217728 | bytes 7864320 | tf_op jit(solution)/shard_map/head_step/pallas_call | solution.py:307
  127.3 1.5 %collective-permute-start.43 = (bf16[17,32,128]{2,1,0:T(8,128)(2,1)S(1)}, bf16[17,32,128]{2,1,0:T(8,128)(2,1)S(1)}, u32[]{:S(2)}, u32[]{:S(2)}) collective-permute-start(bf16[17,32,128]{2,1,0:T(8,128)(2,1)S(1)} %get-tuple-element.136.refs_2_), channel_id=1, source_target_pairs={{0,4},{1,9},{2,6},{3,11},{4,0},{5,13},{6,2},{7,15},{8,12},{9,1},{1... | collective-permute-start | bytes 417800 | tf_op jit(solution)/shard_map/ppermute | solution.py:495
  129.3 1.2 collective-permute-done.44
  130.5 3.7 %collective-permute-done.42.refs_4_.refs_1_ = bf16[16,32,128]{2,1,0:T(8,128)(2,1)S(1)} collective-permute-done((bf16[16,32,128]{2,1,0:T(8,128)(2,1)S(1)}, bf16[16,32,128]{2,1,0:T(8,128)(2,1)S(1)}, u32[]{:S(2)}, u32[]{:S(2)}) %collective-permute-start.42) | collective-permute-done | bytes 131104 | tf_op jit(solution)/shard_map/ppermute | solution.py:495
  134.3 1.4 collective-permute-start.45
  135.7 0.7 collective-permute-start.39
  136.4 4.9 %collective-permute-done.45.refs_2_ = bf16[17,32,128]{2,1,0:T(8,128)(2,1)S(1)} collective-permute-done((bf16[17,32,128]{2,1,0:T(8,128)(2,1)S(1)}, bf16[17,32,128]{2,1,0:T(8,128)(2,1)S(1)}, u32[]{:S(2)}, u32[]{:S(2)}) %collective-permute-start.45) | collective-permute-done | bytes 139296 | tf_op jit(solution)/shard_map/ppermute | solution.py:495
  141.4 1.4 collective-permute-start.46
  142.7 1.6 %collective-permute-start.41 = (bf16[16,32,128]{2,1,0:T(8,128)(2,1)S(1)}, bf16[16,32,128]{2,1,0:T(8,128)(2,1)S(1)}, u32[]{:S(2)}, u32[]{:S(2)}) collective-permute-start(bf16[16,32,128]{2,1,0:T(8,128)(2,1)S(1)} %get-tuple-element.132), channel_id=1, source_target_pairs={{0,8},{1,5},{2,10},{3,7},{4,12},{5,1},{6,14},{7,3},{8,0},{9,13},{1... | collective-permute-start | bytes 393224 | tf_op jit(solution)/shard_map/ppermute | solution.py:495
  145.5 3.3 %local_forward.5.refs_5_ = f32[16,32,128]{2,1,0:T(8,128)S(1)} custom-call(s32[4,64]{1,0:T(4,128)S(1)} %bitcast.32, bf16[32,8192]{1,0:T(8,128)(2,1)S(1)} %get-tuple-element.139.bar_ref, bf16[64,4,128,128]{3,2,1,0:T(8,128)(2,1)S(1)} %bitcast.23, f32[16,32,128]{2,1,0:T(8,128)S(1)} %get-tuple-element.140.duals_ref, f32[32,2048]{1,0:T(8,128)S(1)} %copy-done.5, ...), custom_call_target="tpu_custom_call" | custom-call | flops 268435456 | bytes 8388608 | tf_op jit(solution)/shard_map/local_forward/pallas_call | solution.py:409
  149.4 0.8 settle.5
  (95 shorter events, 13.1 us)
Async XLA Ops:
  0.6 1.0 copy-start
  0.6 19.9 %copy-start.12 = (f32[32]{0:T(128)S(1)}, f32[32]{0:T(128)}, u32[]{:S(2)}) copy-start(f32[32]{0:T(128)} %param.15) | copy-start | bytes 388
  0.7 19.9 %copy-start.13 = (f32[32]{0:T(128)S(1)}, f32[32]{0:T(128)}, u32[]{:S(2)}) copy-start(f32[32]{0:T(128)} %param.14) | copy-start | bytes 388
  1.6 14.9 %collective-permute-start.3 = (bf16[16,32,128]{2,1,0:T(8,128)(2,1)S(1)}, bf16[16,32,128]{2,1,0:T(8,128)(2,1)S(1)}, u32[]{:S(2)}, u32[]{:S(2)}) collective-permute-start(bf16[16,32,128]{2,1,0:T(8,128)(2,1)S(1)} %fusion.2.panel_ref.refs_0_), channel_id=1, source_target_pairs={{0,16},{1,17},{2,18},{3,19},{4,20},{5,21},{6,22},{7,23},{8,24},{9,... | collective-permute-start | bytes 393224 | tf_op jit(solution)/shard_map/ppermute | solution.py:495
  5.7 15.0 %collective-permute-start = (bf16[16,32,128]{2,1,0:T(8,128)(2,1)S(1)}, bf16[16,32,128]{2,1,0:T(8,128)(2,1)}, u32[]{:S(2)}, u32[]{:S(2)}) collective-permute-start(bf16[16,32,128]{2,1,0:T(8,128)(2,1)S(1)} %fusion.2.panel_ref.refs_0_), channel_id=1, source_target_pairs={{0,4},{1,9},{2,6},{3,11},{4,0},{5,13},{6,2},{7,15},{8,12},{9,1},{1... | collective-permute-start | bytes 393224 | tf_op jit(solution)/shard_map/ppermute | solution.py:495
  7.2 3.4 %copy-start.1 = (bf16[64,4,128,128]{3,2,1,0:T(8,128)(2,1)S(1)}, bf16[64,4,128,128]{3,2,1,0:T(8,128)(2,1)}, u32[]{:S(2)}) copy-start(bf16[64,4,128,128]{3,2,1,0:T(8,128)(2,1)} %blocks_ref.11) | copy-start | bytes 25165828
  10.6 0.7 copy-start.10
  11.3 9.3 %copy-start.3 = (bf16[64,128,128]{2,1,0:T(8,128)(2,1)S(1)}, bf16[64,128,128]{2,1,0:T(8,128)(2,1)}, u32[]{:S(2)}) copy-start(bf16[64,128,128]{2,1,0:T(8,128)(2,1)} %refs_8_.5) | copy-start | bytes 6291460
  11.3 9.3 %copy-start.4 = (f32[32,8192]{1,0:T(8,128)S(1)}, f32[32,8192]{1,0:T(8,128)}, u32[]{:S(2)}) copy-start(f32[32,8192]{1,0:T(8,128)} %refs_10_.1) | copy-start | bytes 3145732
  11.3 40.3 %copy-start.11 = (s32[64,4]{0,1:T(4,128)S(1)}, s32[64,4]{0,1:T(4,128)}, u32[]{:S(2)}) copy-start(s32[64,4]{0,1:T(4,128)} %param.20) | copy-start | bytes 3076
  15.6 1.0 copy-start.6
  17.2 6.1 %collective-permute-start.5 = (bf16[16,32,128]{2,1,0:T(8,128)(2,1)}, bf16[16,32,128]{2,1,0:T(8,128)(2,1)}, u32[]{:S(2)}, u32[]{:S(2)}) collective-permute-start(bf16[16,32,128]{2,1,0:T(8,128)(2,1)} %get-tuple-element.78.refs_0_.refs_4_), channel_id=1, source_target_pairs={{0,8},{1,5},{2,10},{3,7},{4,12},{5,1},{6,14},{7,3},{8,0},{9,13},{1... | collective-permute-start | bytes 393224 | tf_op jit(solution)/shard_map/ppermute | solution.py:495
  18.8 6.5 %collective-permute-start.1 = (bf16[16,32,128]{2,1,0:T(8,128)(2,1)S(1)}, bf16[16,32,128]{2,1,0:T(8,128)(2,1)}, u32[]{:S(2)}, u32[]{:S(2)}) collective-permute-start(bf16[16,32,128]{2,1,0:T(8,128)(2,1)S(1)} %fusion.2.panel_ref.refs_0_), channel_id=1, source_target_pairs={{0,8},{1,5},{2,10},{3,7},{4,12},{5,1},{6,14},{7,3},{8,0},{9,13},{1... | collective-permute-start | bytes 393224 | tf_op jit(solution)/shard_map/ppermute | solution.py:495
  19.3 32.4 %copy-start.5 = (f32[32,2048]{1,0:T(8,128)S(1)}, f32[32,2048]{1,0:T(8,128)}, u32[]{:S(2)}) copy-start(f32[32,2048]{1,0:T(8,128)} %demand_ref.5) | copy-start | bytes 786436
  19.9 7.9 %collective-permute-start.4 = (bf16[16,32,128]{2,1,0:T(8,128)(2,1)}, bf16[16,32,128]{2,1,0:T(8,128)(2,1)S(1)}, u32[]{:S(2)}, u32[]{:S(2)}) collective-permute-start(bf16[16,32,128]{2,1,0:T(8,128)(2,1)} %get-tuple-element.78.refs_0_.refs_4_), channel_id=1, source_target_pairs={{0,4},{1,9},{2,6},{3,11},{4,0},{5,13},{6,2},{7,15},{8,12},{9,1},{1... | collective-permute-start | bytes 393224 | tf_op jit(solution)/shard_map/ppermute | solution.py:495
  20.7 4.6 %collective-permute-start.7 = (f32[8,128]{1,0:T(8,128)S(1)}, f32[8,128]{1,0:T(8,128)S(1)}, u32[]{:S(2)}, u32[]{:S(2)}) collective-permute-start(f32[8,128]{1,0:T(8,128)S(1)} %get-tuple-element.82.refs_14_), channel_id=1, source_target_pairs={{0,1},{1,0},{2,3},{3,2},{4,5},{5,4},{6,7},{7,6},{8,9},{9,8},{10,11... | collective-permute-start | bytes 12296 | tf_op jit(solution)/shard_map/ppermute | solution.py:481
  20.8 7.1 %collective-permute-start.2 = (bf16[16,32,128]{2,1,0:T(8,128)(2,1)}, bf16[16,32,128]{2,1,0:T(8,128)(2,1)S(1)}, u32[]{:S(2)}, u32[]{:S(2)}) collective-permute-start(bf16[16,32,128]{2,1,0:T(8,128)(2,1)} %collective-permute-done.refs_1_), channel_id=1, source_target_pairs={{0,8},{1,5},{2,10},{3,7},{4,12},{5,1},{6,14},{7,3},{8,0},{9,13},{1... | collective-permute-start | bytes 393224 | tf_op jit(solution)/shard_map/ppermute | solution.py:495
  23.3 5.2 %collective-permute-start.6 = (bf16[16,32,128]{2,1,0:T(8,128)(2,1)}, bf16[16,32,128]{2,1,0:T(8,128)(2,1)S(1)}, u32[]{:S(2)}, u32[]{:S(2)}) collective-permute-start(bf16[16,32,128]{2,1,0:T(8,128)(2,1)} %collective-permute-done.5.refs_6_), channel_id=1, source_target_pairs={{0,4},{1,9},{2,6},{3,11},{4,0},{5,13},{6,2},{7,15},{8,12},{9,1},{1... | collective-permute-start | bytes 393224 | tf_op jit(solution)/shard_map/ppermute | solution.py:495
  28.5 1.2 copy-start.7
  29.7 0.8 copy-start.8
  30.5 32.1 %slice-start = ((s8[8388608]{0:T(1024)(128)(4,1)}), s8[4194304]{0:T(1024)(128)(4,1)S(1)}, s32[]{:S(2)}) async-start(s8[8388608]{0:T(1024)(128)(4,1)} %bitcast.22), calls=%async_computation | async-start | bytes 8388608
  35.4 6.5 %collective-permute-start.12 = (bf16[17,32,128]{2,1,0:T(8,128)(2,1)S(1)}, bf16[17,32,128]{2,1,0:T(8,128)(2,1)S(1)}, u32[]{:S(2)}, u32[]{:S(2)}) collective-permute-start(bf16[17,32,128]{2,1,0:T(8,128)(2,1)S(1)} %get-tuple-element.90.refs_2_), channel_id=1, source_target_pairs={{0,4},{1,9},{2,6},{3,11},{4,0},{5,13},{6,2},{7,15},{8,12},{9,1},{1... | collective-permute-start | bytes 417800 | tf_op jit(solution)/shard_map/ppermute | solution.py:495
  36.0 5.9 %collective-permute-start.11 = (bf16[16,32,128]{2,1,0:T(8,128)(2,1)S(1)}, bf16[16,32,128]{2,1,0:T(8,128)(2,1)S(1)}, u32[]{:S(2)}, u32[]{:S(2)}) collective-permute-start(bf16[16,32,128]{2,1,0:T(8,128)(2,1)S(1)} %get-tuple-element.88), channel_id=1, source_target_pairs={{0,4},{1,9},{2,6},{3,11},{4,0},{5,13},{6,2},{7,15},{8,12},{9,1},{1... | collective-permute-start | bytes 393224 | tf_op jit(solution)/shard_map/ppermute | solution.py:495
  42.1 7.4 %collective-permute-start.13 = (bf16[17,32,128]{2,1,0:T(8,128)(2,1)S(1)}, bf16[17,32,128]{2,1,0:T(8,128)(2,1)S(1)}, u32[]{:S(2)}, u32[]{:S(2)}) collective-permute-start(bf16[17,32,128]{2,1,0:T(8,128)(2,1)S(1)} %fold.10.refs_3_), channel_id=1, source_target_pairs={{0,8},{1,5},{2,10},{3,7},{4,12},{5,1},{6,14},{7,3},{8,0},{9,13},{1... | collective-permute-start | bytes 417800 | tf_op jit(solution)/shard_map/ppermute | solution.py:495
  43.8 5.0 %collective-permute-start.8 = (bf16[16,32,128]{2,1,0:T(8,128)(2,1)S(1)}, bf16[16,32,128]{2,1,0:T(8,128)(2,1)S(1)}, u32[]{:S(2)}, u32[]{:S(2)}) collective-permute-start(bf16[16,32,128]{2,1,0:T(8,128)(2,1)S(1)} %get-tuple-element.85), channel_id=1, source_target_pairs={{0,8},{1,5},{2,10},{3,7},{4,12},{5,1},{6,14},{7,3},{8,0},{9,13},{1... | collective-permute-start | bytes 393224 | tf_op jit(solution)/shard_map/ppermute | solution.py:495
  44.1 14.2 %collective-permute-start.10 = (bf16[16,32,128]{2,1,0:T(8,128)(2,1)S(1)}, bf16[16,32,128]{2,1,0:T(8,128)(2,1)S(1)}, u32[]{:S(2)}, u32[]{:S(2)}) collective-permute-start(bf16[16,32,128]{2,1,0:T(8,128)(2,1)S(1)} %get-tuple-element.86), channel_id=1, source_target_pairs={{0,8},{1,5},{2,10},{3,7},{4,12},{5,1},{6,14},{7,3},{8,0},{9,13},{1... | collective-permute-start | bytes 393224 | tf_op jit(solution)/shard_map/ppermute | solution.py:495
  48.8 9.6 %collective-permute-start.9 = (bf16[16,32,128]{2,1,0:T(8,128)(2,1)S(1)}, bf16[16,32,128]{2,1,0:T(8,128)(2,1)S(1)}, u32[]{:S(2)}, u32[]{:S(2)}) collective-permute-start(bf16[16,32,128]{2,1,0:T(8,128)(2,1)S(1)} %fold.9), channel_id=1, source_target_pairs={{0,4},{1,9},{2,6},{3,11},{4,0},{5,13},{6,2},{7,15},{8,12},{9,1},{1... | collective-permute-start | bytes 393224 | tf_op jit(solution)/shard_map/ppermute | solution.py:495
  49.6 8.8 %collective-permute-start.14 = (bf16[17,32,128]{2,1,0:T(8,128)(2,1)S(1)}, bf16[17,32,128]{2,1,0:T(8,128)(2,1)S(1)}, u32[]{:S(2)}, u32[]{:S(2)}) collective-permute-start(bf16[17,32,128]{2,1,0:T(8,128)(2,1)S(1)} %get-tuple-element.92.after_ref.refs_4_), channel_id=1, source_target_pairs={{0,16},{1,17},{2,18},{3,19},{4,20},{5,21},{6,22},{7,23},{8,24},{9,... | collective-permute-start | bytes 417800 | tf_op jit(solution)/shard_map/ppermute | solution.py:495
  50.0 8.4 %collective-permute-start.15 = (f32[8,128]{1,0:T(8,128)S(1)}, f32[8,128]{1,0:T(8,128)S(1)}, u32[]{:S(2)}, u32[]{:S(2)}) collective-permute-start(f32[8,128]{1,0:T(8,128)S(1)} %get-tuple-element.97.refs_9_), channel_id=1, source_target_pairs={{0,2},{1,3},{2,0},{3,1},{4,6},{5,7},{6,4},{7,5},{8,10},{9,11},{10,... | collective-permute-start | bytes 12296 | tf_op jit(solution)/shard_map/ppermute | solution.py:481
  51.6 3.4 %copy-start.2 = (bf16[64,4,128,128]{3,2,1,0:T(8,128)(2,1)S(1)}, bf16[64,4,128,128]{3,2,1,0:T(8,128)(2,1)}, u32[]{:S(2)}) copy-start(bf16[64,4,128,128]{3,2,1,0:T(8,128)(2,1)} %blocks_ref.11) | copy-start | bytes 25165828
  55.0 7.6 %slice-start.1 = ((s8[8388608]{0:T(1024)(128)(4,1)}), s8[4194304]{0:T(1024)(128)(4,1)S(1)}, s32[]{:S(2)}) async-start(s8[8388608]{0:T(1024)(128)(4,1)} %bitcast.22), calls=%async_computation.1 | async-start | bytes 8388608
  55.0 22.8 %copy-start.9 = (f32[8192]{0:T(1024)S(1)}, f32[8192]{0:T(1024)}, u32[]{:S(2)}) copy-start(f32[8192]{0:T(1024)} %param.17) | copy-start | bytes 98308
  58.6 8.3 %collective-permute-start.19 = (bf16[16,32,128]{2,1,0:T(8,128)(2,1)S(1)}, bf16[16,32,128]{2,1,0:T(8,128)(2,1)S(1)}, u32[]{:S(2)}, u32[]{:S(2)}) collective-permute-start(bf16[16,32,128]{2,1,0:T(8,128)(2,1)S(1)} %get-tuple-element.98.panel_ref.refs_0_), channel_id=1, source_target_pairs={{0,16},{1,17},{2,18},{3,19},{4,20},{5,21},{6,22},{7,23},{8,24},{9,... | collective-permute-start | bytes 393224 | tf_op jit(solution)/shard_map/ppermute | solution.py:495
  61.3 8.5 %collective-permute-start.16 = (bf16[16,32,128]{2,1,0:T(8,128)(2,1)S(1)}, bf16[16,32,128]{2,1,0:T(8,128)(2,1)S(1)}, u32[]{:S(2)}, u32[]{:S(2)}) collective-permute-start(bf16[16,32,128]{2,1,0:T(8,128)(2,1)S(1)} %get-tuple-element.98.panel_ref.refs_0_), channel_id=1, source_target_pairs={{0,4},{1,9},{2,6},{3,11},{4,0},{5,13},{6,2},{7,15},{8,12},{9,1},{1... | collective-permute-start | bytes 393224 | tf_op jit(solution)/shard_map/ppermute | solution.py:495
  66.9 5.9 %collective-permute-start.21 = (bf16[16,32,128]{2,1,0:T(8,128)(2,1)S(1)}, bf16[16,32,128]{2,1,0:T(8,128)(2,1)S(1)}, u32[]{:S(2)}, u32[]{:S(2)}) collective-permute-start(bf16[16,32,128]{2,1,0:T(8,128)(2,1)S(1)} %get-tuple-element.101.refs_4_), channel_id=1, source_target_pairs={{0,8},{1,5},{2,10},{3,7},{4,12},{5,1},{6,14},{7,3},{8,0},{9,13},{1... | collective-permute-start | bytes 393224 | tf_op jit(solution)/shard_map/ppermute | solution.py:495
  68.5 5.8 %collective-permute-start.17 = (bf16[16,32,128]{2,1,0:T(8,128)(2,1)S(1)}, bf16[16,32,128]{2,1,0:T(8,128)(2,1)S(1)}, u32[]{:S(2)}, u32[]{:S(2)}) collective-permute-start(bf16[16,32,128]{2,1,0:T(8,128)(2,1)S(1)} %get-tuple-element.98.panel_ref.refs_0_), channel_id=1, source_target_pairs={{0,8},{1,5},{2,10},{3,7},{4,12},{5,1},{6,14},{7,3},{8,0},{9,13},{1... | collective-permute-start | bytes 393224 | tf_op jit(solution)/shard_map/ppermute | solution.py:495
  69.0 8.3 %collective-permute-start.20 = (bf16[16,32,128]{2,1,0:T(8,128)(2,1)S(1)}, bf16[16,32,128]{2,1,0:T(8,128)(2,1)S(1)}, u32[]{:S(2)}, u32[]{:S(2)}) collective-permute-start(bf16[16,32,128]{2,1,0:T(8,128)(2,1)S(1)} %get-tuple-element.101.refs_4_), channel_id=1, source_target_pairs={{0,4},{1,9},{2,6},{3,11},{4,0},{5,13},{6,2},{7,15},{8,12},{9,1},{1... | collective-permute-start | bytes 393224 | tf_op jit(solution)/shard_map/ppermute | solution.py:495
  69.7 7.6 %collective-permute-start.18 = (bf16[16,32,128]{2,1,0:T(8,128)(2,1)S(1)}, bf16[16,32,128]{2,1,0:T(8,128)(2,1)S(1)}, u32[]{:S(2)}, u32[]{:S(2)}) collective-permute-start(bf16[16,32,128]{2,1,0:T(8,128)(2,1)S(1)} %collective-permute-done.16.refs_1_), channel_id=1, source_target_pairs={{0,8},{1,5},{2,10},{3,7},{4,12},{5,1},{6,14},{7,3},{8,0},{9,13},{1... | collective-permute-start | bytes 393224 | tf_op jit(solution)/shard_map/ppermute | solution.py:495
  72.9 5.0 %collective-permute-start.22 = (bf16[16,32,128]{2,1,0:T(8,128)(2,1)S(1)}, bf16[16,32,128]{2,1,0:T(8,128)(2,1)S(1)}, u32[]{:S(2)}, u32[]{:S(2)}) collective-permute-start(bf16[16,32,128]{2,1,0:T(8,128)(2,1)S(1)} %collective-permute-done.21.refs_6_), channel_id=1, source_target_pairs={{0,4},{1,9},{2,6},{3,11},{4,0},{5,13},{6,2},{7,15},{8,12},{9,1},{1... | collective-permute-start | bytes 393224 | tf_op jit(solution)/shard_map/ppermute | solution.py:495
  73.7 3.6 %collective-permute-start.23 = (f32[8,128]{1,0:T(8,128)S(1)}, f32[8,128]{1,0:T(8,128)S(1)}, u32[]{:S(2)}, u32[]{:S(2)}) collective-permute-start(f32[8,128]{1,0:T(8,128)S(1)} %get-tuple-element.106.refs_14_), channel_id=1, source_target_pairs={{0,2},{1,3},{2,0},{3,1},{4,6},{5,7},{6,4},{7,5},{8,10},{9,11},{10,... | collective-permute-start | bytes 12296 | tf_op jit(solution)/shard_map/ppermute | solution.py:481
  81.4 8.9 %collective-permute-start.28 = (bf16[17,32,128]{2,1,0:T(8,128)(2,1)S(1)}, bf16[17,32,128]{2,1,0:T(8,128)(2,1)S(1)}, u32[]{:S(2)}, u32[]{:S(2)}) collective-permute-start(bf16[17,32,128]{2,1,0:T(8,128)(2,1)S(1)} %get-tuple-element.114.refs_2_), channel_id=1, source_target_pairs={{0,4},{1,9},{2,6},{3,11},{4,0},{5,13},{6,2},{7,15},{8,12},{9,1},{1... | collective-permute-start | bytes 417800 | tf_op jit(solution)/shard_map/ppermute | solution.py:495
  82.3 7.9 %collective-permute-start.27 = (bf16[16,32,128]{2,1,0:T(8,128)(2,1)S(1)}, bf16[16,32,128]{2,1,0:T(8,128)(2,1)S(1)}, u32[]{:S(2)}, u32[]{:S(2)}) collective-permute-start(bf16[16,32,128]{2,1,0:T(8,128)(2,1)S(1)} %get-tuple-element.112), channel_id=1, source_target_pairs={{0,4},{1,9},{2,6},{3,11},{4,0},{5,13},{6,2},{7,15},{8,12},{9,1},{1... | collective-permute-start | bytes 393224 | tf_op jit(solution)/shard_map/ppermute | solution.py:495
  90.4 5.8 %collective-permute-start.29 = (bf16[17,32,128]{2,1,0:T(8,128)(2,1)S(1)}, bf16[17,32,128]{2,1,0:T(8,128)(2,1)S(1)}, u32[]{:S(2)}, u32[]{:S(2)}) collective-permute-start(bf16[17,32,128]{2,1,0:T(8,128)(2,1)S(1)} %fold.13.refs_3_), channel_id=1, source_target_pairs={{0,8},{1,5},{2,10},{3,7},{4,12},{5,1},{6,14},{7,3},{8,0},{9,13},{1... | collective-permute-start | bytes 417800 | tf_op jit(solution)/shard_map/ppermute | solution.py:495
  91.9 6.1 %collective-permute-start.24 = (bf16[16,32,128]{2,1,0:T(8,128)(2,1)S(1)}, bf16[16,32,128]{2,1,0:T(8,128)(2,1)S(1)}, u32[]{:S(2)}, u32[]{:S(2)}) collective-permute-start(bf16[16,32,128]{2,1,0:T(8,128)(2,1)S(1)} %get-tuple-element.109), channel_id=1, source_target_pairs={{0,8},{1,5},{2,10},{3,7},{4,12},{5,1},{6,14},{7,3},{8,0},{9,13},{1... | collective-permute-start | bytes 393224 | tf_op jit(solution)/shard_map/ppermute | solution.py:495
  96.3 9.1 %collective-permute-start.30 = (bf16[17,32,128]{2,1,0:T(8,128)(2,1)S(1)}, bf16[17,32,128]{2,1,0:T(8,128)(2,1)S(1)}, u32[]{:S(2)}, u32[]{:S(2)}) collective-permute-start(bf16[17,32,128]{2,1,0:T(8,128)(2,1)S(1)} %fold.14.after_ref.refs_4_), channel_id=1, source_target_pairs={{0,16},{1,17},{2,18},{3,19},{4,20},{5,21},{6,22},{7,23},{8,24},{9,... | collective-permute-start | bytes 417800 | tf_op jit(solution)/shard_map/ppermute | solution.py:495
  96.5 7.4 %collective-permute-start.26 = (bf16[16,32,128]{2,1,0:T(8,128)(2,1)S(1)}, bf16[16,32,128]{2,1,0:T(8,128)(2,1)S(1)}, u32[]{:S(2)}, u32[]{:S(2)}) collective-permute-start(bf16[16,32,128]{2,1,0:T(8,128)(2,1)S(1)} %get-tuple-element.110), channel_id=1, source_target_pairs={{0,8},{1,5},{2,10},{3,7},{4,12},{5,1},{6,14},{7,3},{8,0},{9,13},{1... | collective-permute-start | bytes 393224 | tf_op jit(solution)/shard_map/ppermute | solution.py:495
  98.0 5.9 %collective-permute-start.25 = (bf16[16,32,128]{2,1,0:T(8,128)(2,1)S(1)}, bf16[16,32,128]{2,1,0:T(8,128)(2,1)S(1)}, u32[]{:S(2)}, u32[]{:S(2)}) collective-permute-start(bf16[16,32,128]{2,1,0:T(8,128)(2,1)S(1)} %fold.12), channel_id=1, source_target_pairs={{0,4},{1,9},{2,6},{3,11},{4,0},{5,13},{6,2},{7,15},{8,12},{9,1},{1... | collective-permute-start | bytes 393224 | tf_op jit(solution)/shard_map/ppermute | solution.py:495
  106.0 7.1 %collective-permute-start.34 = (bf16[16,32,128]{2,1,0:T(8,128)(2,1)S(1)}, bf16[16,32,128]{2,1,0:T(8,128)(2,1)S(1)}, u32[]{:S(2)}, u32[]{:S(2)}) collective-permute-start(bf16[16,32,128]{2,1,0:T(8,128)(2,1)S(1)} %get-tuple-element.121.panel_ref.refs_0_), channel_id=1, source_target_pairs={{0,16},{1,17},{2,18},{3,19},{4,20},{5,21},{6,22},{7,23},{8,24},{9,... | collective-permute-start | bytes 393224 | tf_op jit(solution)/shard_map/ppermute | solution.py:495
  106.6 10.1 %collective-permute-start.31 = (bf16[16,32,128]{2,1,0:T(8,128)(2,1)S(1)}, bf16[16,32,128]{2,1,0:T(8,128)(2,1)S(1)}, u32[]{:S(2)}, u32[]{:S(2)}) collective-permute-start(bf16[16,32,128]{2,1,0:T(8,128)(2,1)S(1)} %get-tuple-element.121.panel_ref.refs_0_), channel_id=1, source_target_pairs={{0,4},{1,9},{2,6},{3,11},{4,0},{5,13},{6,2},{7,15},{8,12},{9,1},{1... | collective-permute-start | bytes 393224 | tf_op jit(solution)/shard_map/ppermute | solution.py:495
  113.0 5.0 %collective-permute-start.36 = (bf16[16,32,128]{2,1,0:T(8,128)(2,1)S(1)}, bf16[16,32,128]{2,1,0:T(8,128)(2,1)S(1)}, u32[]{:S(2)}, u32[]{:S(2)}) collective-permute-start(bf16[16,32,128]{2,1,0:T(8,128)(2,1)S(1)} %get-tuple-element.123.refs_4_), channel_id=1, source_target_pairs={{0,8},{1,5},{2,10},{3,7},{4,12},{5,1},{6,14},{7,3},{8,0},{9,13},{1... | collective-permute-start | bytes 393224 | tf_op jit(solution)/shard_map/ppermute | solution.py:495
  114.6 5.0 %collective-permute-start.32 = (bf16[16,32,128]{2,1,0:T(8,128)(2,1)S(1)}, bf16[16,32,128]{2,1,0:T(8,128)(2,1)S(1)}, u32[]{:S(2)}, u32[]{:S(2)}) collective-permute-start(bf16[16,32,128]{2,1,0:T(8,128)(2,1)S(1)} %get-tuple-element.121.panel_ref.refs_0_), channel_id=1, source_target_pairs={{0,8},{1,5},{2,10},{3,7},{4,12},{5,1},{6,14},{7,3},{8,0},{9,13},{1... | collective-permute-start | bytes 393224 | tf_op jit(solution)/shard_map/ppermute | solution.py:495
  115.1 6.5 %collective-permute-start.35 = (bf16[16,32,128]{2,1,0:T(8,128)(2,1)S(1)}, bf16[16,32,128]{2,1,0:T(8,128)(2,1)S(1)}, u32[]{:S(2)}, u32[]{:S(2)}) collective-permute-start(bf16[16,32,128]{2,1,0:T(8,128)(2,1)S(1)} %get-tuple-element.123.refs_4_), channel_id=1, source_target_pairs={{0,4},{1,9},{2,6},{3,11},{4,0},{5,13},{6,2},{7,15},{8,12},{9,1},{1... | collective-permute-start | bytes 393224 | tf_op jit(solution)/shard_map/ppermute | solution.py:495
  116.7 5.0 %collective-permute-start.33 = (bf16[16,32,128]{2,1,0:T(8,128)(2,1)S(1)}, bf16[16,32,128]{2,1,0:T(8,128)(2,1)S(1)}, u32[]{:S(2)}, u32[]{:S(2)}) collective-permute-start(bf16[16,32,128]{2,1,0:T(8,128)(2,1)S(1)} %collective-permute-done.31.refs_1_), channel_id=1, source_target_pairs={{0,8},{1,5},{2,10},{3,7},{4,12},{5,1},{6,14},{7,3},{8,0},{9,13},{1... | collective-permute-start | bytes 393224 | tf_op jit(solution)/shard_map/ppermute | solution.py:495
  118.1 5.0 %collective-permute-start.37 = (bf16[16,32,128]{2,1,0:T(8,128)(2,1)S(1)}, bf16[16,32,128]{2,1,0:T(8,128)(2,1)S(1)}, u32[]{:S(2)}, u32[]{:S(2)}) collective-permute-start(bf16[16,32,128]{2,1,0:T(8,128)(2,1)S(1)} %collective-permute-done.36.refs_6_), channel_id=1, source_target_pairs={{0,4},{1,9},{2,6},{3,11},{4,0},{5,13},{6,2},{7,15},{8,12},{9,1},{1... | collective-permute-start | bytes 393224 | tf_op jit(solution)/shard_map/ppermute | solution.py:495
  119.6 1.2 collective-permute-start.38
  127.3 6.9 %collective-permute-start.43 = (bf16[17,32,128]{2,1,0:T(8,128)(2,1)S(1)}, bf16[17,32,128]{2,1,0:T(8,128)(2,1)S(1)}, u32[]{:S(2)}, u32[]{:S(2)}) collective-permute-start(bf16[17,32,128]{2,1,0:T(8,128)(2,1)S(1)} %get-tuple-element.136.refs_2_), channel_id=1, source_target_pairs={{0,4},{1,9},{2,6},{3,11},{4,0},{5,13},{6,2},{7,15},{8,12},{9,1},{1... | collective-permute-start | bytes 417800 | tf_op jit(solution)/shard_map/ppermute | solution.py:495
  128.8 5.3 %collective-permute-start.42 = (bf16[16,32,128]{2,1,0:T(8,128)(2,1)S(1)}, bf16[16,32,128]{2,1,0:T(8,128)(2,1)S(1)}, u32[]{:S(2)}, u32[]{:S(2)}) collective-permute-start(bf16[16,32,128]{2,1,0:T(8,128)(2,1)S(1)} %get-tuple-element.134), channel_id=1, source_target_pairs={{0,4},{1,9},{2,6},{3,11},{4,0},{5,13},{6,2},{7,15},{8,12},{9,1},{1... | collective-permute-start | bytes 393224 | tf_op jit(solution)/shard_map/ppermute | solution.py:495
  129.3 1.2 collective-permute-start.44
  134.3 6.9 %collective-permute-start.45 = (bf16[17,32,128]{2,1,0:T(8,128)(2,1)S(1)}, bf16[17,32,128]{2,1,0:T(8,128)(2,1)S(1)}, u32[]{:S(2)}, u32[]{:S(2)}) collective-permute-start(bf16[17,32,128]{2,1,0:T(8,128)(2,1)S(1)} %fold.16.refs_3_), channel_id=1, source_target_pairs={{0,8},{1,5},{2,10},{3,7},{4,12},{5,1},{6,14},{7,3},{8,0},{9,13},{1... | collective-permute-start | bytes 417800 | tf_op jit(solution)/shard_map/ppermute | solution.py:495
  135.7 8.6 %collective-permute-start.39 = (bf16[16,32,128]{2,1,0:T(8,128)(2,1)S(1)}, bf16[16,32,128]{2,1,0:T(8,128)(2,1)S(1)}, u32[]{:S(2)}, u32[]{:S(2)}) collective-permute-start(bf16[16,32,128]{2,1,0:T(8,128)(2,1)S(1)} %get-tuple-element.131), channel_id=1, source_target_pairs={{0,8},{1,5},{2,10},{3,7},{4,12},{5,1},{6,14},{7,3},{8,0},{9,13},{1... | collective-permute-start | bytes 393224 | tf_op jit(solution)/shard_map/ppermute | solution.py:495
  141.4 8.0 %collective-permute-start.46 = (bf16[17,32,128]{2,1,0:T(8,128)(2,1)S(1)}, bf16[17,32,128]{2,1,0:T(8,128)(2,1)S(1)}, u32[]{:S(2)}, u32[]{:S(2)}) collective-permute-start(bf16[17,32,128]{2,1,0:T(8,128)(2,1)S(1)} %get-tuple-element.138.after_ref.refs_4_), channel_id=1, source_target_pairs={{0,16},{1,17},{2,18},{3,19},{4,20},{5,21},{6,22},{7,23},{8,24},{9,... | collective-permute-start | bytes 417800 | tf_op jit(solution)/shard_map/ppermute | solution.py:495
  142.7 6.4 %collective-permute-start.41 = (bf16[16,32,128]{2,1,0:T(8,128)(2,1)S(1)}, bf16[16,32,128]{2,1,0:T(8,128)(2,1)S(1)}, u32[]{:S(2)}, u32[]{:S(2)}) collective-permute-start(bf16[16,32,128]{2,1,0:T(8,128)(2,1)S(1)} %get-tuple-element.132), channel_id=1, source_target_pairs={{0,8},{1,5},{2,10},{3,7},{4,12},{5,1},{6,14},{7,3},{8,0},{9,13},{1... | collective-permute-start | bytes 393224 | tf_op jit(solution)/shard_map/ppermute | solution.py:495
  144.3 5.0 %collective-permute-start.40 = (bf16[16,32,128]{2,1,0:T(8,128)(2,1)S(1)}, bf16[16,32,128]{2,1,0:T(8,128)(2,1)S(1)}, u32[]{:S(2)}, u32[]{:S(2)}) collective-permute-start(bf16[16,32,128]{2,1,0:T(8,128)(2,1)S(1)} %fold.15), channel_id=1, source_target_pairs={{0,4},{1,9},{2,6},{3,11},{4,0},{5,13},{6,2},{7,15},{8,12},{9,1},{1... | collective-permute-start | bytes 393224 | tf_op jit(solution)/shard_map/ppermute | solution.py:495
  145.0 4.4 %collective-permute-start.47 = (f32[8,128]{1,0:T(8,128)S(1)}, f32[8,128]{1,0:T(8,128)S(1)}, u32[]{:S(2)}, u32[]{:S(2)}) collective-permute-start(f32[8,128]{1,0:T(8,128)S(1)} %get-tuple-element.144.refs_9_), channel_id=1, source_target_pairs={{0,2},{1,3},{2,0},{3,1},{4,6},{5,7},{6,4},{7,5},{8,10},{9,11},{10,... | collective-permute-start | bytes 12296 | tf_op jit(solution)/shard_map/ppermute | solution.py:481

commit v7 on v6

--- a/solution.py
+++ b/solution.py
@@ -142,12 +142,12 @@
     return values[0]
 
 
-def fold_kernel(counts, with_loss, extras, after, *refs):
+def fold_kernel(counts, with_loss, sums, after, *refs):
     inputs, refs = refs[: sum(counts) + len(counts)], refs[sum(counts) + len(counts) :]
     if with_loss:
         loss_ref, refs = refs[0], refs[1:]
-    extra_in, refs = refs[:extras], refs[extras + after :]
-    outs, extra_out = refs[: len(counts)], refs[len(counts) :]
+    sum_in, refs = refs[:sums], refs[sums + after :]
+    outs, sum_out = refs[: len(counts)], refs[len(counts) :]
     node_blks = inputs[0].shape[0]
     for number, (count, out_ref) in enumerate(zip(counts, outs)):
         kept_ref, arrived, inputs = inputs[0], inputs[1 : 1 + count], inputs[1 + count :]
@@ -157,8 +157,8 @@
         if with_loss and number == 0:
             both = from_parts(loss_ref[loss_ref.shape[0] - 1]) + from_parts(arrived[-1][node_blks])
             out_ref[node_blks] = to_parts(both, loss_ref.shape[1:])
-    for source, target in zip(extra_in, extra_out):
-        target[...] = source[...]
+    for out in sum_out:
+        out[...] = functools.reduce(jnp.add, [ref[...] for ref in sum_in])
 
 
 def next_level(level, risk_total, scen_total):
@@ -358,20 +358,20 @@
     return pl.CostEstimate(flops=size, bytes_accessed=2 * size, transcendentals=0)
 
 
-def fold(tops, loss, extras, after):
+def fold(tops, loss, sums, after):
     node_blks, scen_rows, rows = tops[0][0].shape
     with_loss = loss is not None
     operands = [array for kept, arrived in tops for array in (kept, *arrived)]
-    operands += ([loss] if with_loss else []) + list(extras)
+    operands += ([loss] if with_loss else []) + list(sums)
     vmem = pl.BlockSpec(memory_space=pltpu.VMEM)
     out_shape = [
         jax.ShapeDtypeStruct((node_blks + (with_loss and number == 0), scen_rows, rows), jnp.bfloat16)
         for number in range(len(tops))
     ]
-    out_shape += [jax.ShapeDtypeStruct(extra.shape, extra.dtype) for extra in extras]
+    out_shape += [jax.ShapeDtypeStruct(array.shape, array.dtype) for array in sums[:1]]
     counts = [len(arrived) for _, arrived in tops]
     results = pl.pallas_call(
-        functools.partial(fold_kernel, counts, with_loss, len(extras), len(after)),
+        functools.partial(fold_kernel, counts, with_loss, len(sums), len(after)),
         out_shape=out_shape,
         in_specs=[vmem] * len(operands) + [pl.BlockSpec(memory_space=pl.ANY)] * len(after),
         out_specs=[vmem] * len(out_shape),
@@ -451,8 +451,12 @@
     )(arrived, risk_sum, *after)
 
 
-def prepare_kernel(risk_ref, excess_ref, level_ref, *refs):
-    risk_out, excess_out, level_out, sum_out = refs[-4:]
+def prepare_kernel(node_blks, risk_ref, excess_ref, level_ref, head_ref, *refs):
+    risk_out, excess_out, level_out, sum_out, places_out = refs[-5:]
+    head = head_ref[...]
+    owner = lax.div(head, node_blks)
+    distance = jnp.bitwise_xor(owner, lax.axis_index("net"))
+    places_out[...] = head + (distance - owner) * node_blks
     scen_rows = risk_out.shape[0]
     square = (scen_rows, scen_rows)
     same = lax.broadcasted_iota(jnp.int32, square, 0) == lax.broadcasted_iota(jnp.int32, square, 1)
@@ -463,36 +467,23 @@
     sum_out[...] = add_rows(risk_out[...], sum_out.shape)
 
 
-def prepare(risk, excess, level, rows, after):
+def prepare(risk, excess, level, heads, rows, node_blks, after):
     wide, flat = (risk.shape[0], rows), (8, rows)
     return pl.pallas_call(
-        prepare_kernel,
-        out_shape=[jax.ShapeDtypeStruct(shape, jnp.float32) for shape in (wide, wide, flat, flat)],
-        in_specs=[pl.BlockSpec(memory_space=pltpu.VMEM)] * 3
+        functools.partial(prepare_kernel, node_blks),
+        out_shape=[jax.ShapeDtypeStruct(shape, jnp.float32) for shape in (wide, wide, flat, flat)]
+        + [jax.ShapeDtypeStruct((1, heads.shape[0]), jnp.int32)],
+        in_specs=[pl.BlockSpec(memory_space=pltpu.VMEM)] * 4
         + [pl.BlockSpec(memory_space=pl.ANY)] * len(after),
         compiler_params=pltpu.CompilerParams(vmem_limit_bytes=SMALL_VMEM),
         cost_estimate=small_cost(risk),
         name="prepare",
-    )(risk.reshape(1, -1), excess.reshape(1, -1), level.reshape(1, 1), *after)
+    )(risk.reshape(1, -1), excess.reshape(1, -1), level.reshape(1, 1), heads.reshape(1, -1), *after)
 
 
 def swap(value, axis, distance):
     size = lax.axis_size(axis)
     return lax.ppermute(value, axis, [(i, i ^ distance) for i in range(size)])
-
-
-def exchange_lowest(distance):
-    return (distance & ~3) | ((distance & 1) << 1) | ((distance >> 1) & 1)
-
-
-def swap_net(value, distance):
-    net_size, scen_size = lax.axis_size("net"), lax.axis_size("scen")
-    pairs = []
-    for net in range(net_size):
-        for scen in range(scen_size):
-            hop = exchange_lowest(distance) if scen % 2 else distance
-            pairs.append((net * scen_size + scen, (net ^ hop) * scen_size + scen))
-    return lax.ppermute(value, ("net", "scen"), pairs)
 
 
 def gather_panels(own, risk_sum, after):
@@ -501,7 +492,7 @@
     order = sorted(range(1, peers), key=lambda k: (k.bit_count(), -k))
     for distance in order:
         hop = last_hop(distance)
-        panels[distance] = swap_net(panels[distance ^ hop], hop)
+        panels[distance] = swap(panels[distance ^ hop], "net", hop)
         if distance == 1:
             far = peers // 2
             panels[far], risk_sum = relay(panels[far], risk_sum, after)
@@ -529,28 +520,26 @@
     scen_total = scen_rows * lax.axis_size("scen")
     costs = arc_costs.reshape(1, -1)
     touched = local_index.T
-    distance = jnp.bitwise_xor(head_index // node_blks, lax.axis_index("net"))
-    distance = jnp.where(lax.axis_index("scen") % 2 == 1, exchange_lowest(distance), distance)
-    places = distance * node_blks + head_index % node_blks
     scen_size = lax.axis_size("scen")
     duals = node_duals.reshape(scen_rows, node_blks, rows).transpose(1, 0, 2)
     half = duals.astype(jnp.bfloat16)
-    risk_sum = jnp.zeros((8, rows), jnp.float32)
     flows = arc_flows
     early = [1 << bit for bit in range(1, scen_size.bit_length() - 1)][::-1]
-    zero = jnp.zeros_like(risk_sum)
     for iteration in range(ROUNDS):
         kind = "first" if iteration == 0 else "last" if iteration == ROUNDS - 1 else "early"
         pulled, token = local_adjoint(touched, half, local_blocks)
-        panels, risk_sum = gather_panels(half, risk_sum, (token,))
+        panels, risk_sum = gather_panels(half, token if kind == "first" else risk_sum, (token,))
         if kind == "first":
-            risk, excess_now, level, risk_sum = prepare(
+            risk, excess_now, level, risk_sum, places = prepare(
                 risk_duals,
                 excess,
                 threshold,
+                head_index,
                 rows,
+                node_blks,
                 (panels[net_size // 2], head_blocks, arc_flows),
             )
+            places = places.reshape(-1)
         if kind == "early":
             for stride in early[:-1]:
                 risk_sum = risk_sum + swap(risk_sum, "scen", stride)
@@ -571,13 +560,14 @@
             scen_total,
         )
         after = ()
+        risk_sums = () if kind == "early" else (risk_sum,)
         if kind == "last":
-            risk_sum = risk_sum + swap(risk_sum, "scen", 1)
-            after = (risk_sum,)
+            after = (swap(risk_sum, "scen", 1),)
+            risk_sums += after
         tops = sorted(inner(net_size), key=lambda k: (-k.bit_count(), -k))[:-1]
         groups = [(top,) for top in tops if top != 1] + [(1,)]
         loss, loss_top = sends[net_size - 1], net_size - 1
-        ahead = {5: swap_net(sends[5], last_hop(5))}
+        ahead = {5: swap(sends[5], "net", last_hop(5))}
         after += (ahead[5],)
         for group in groups:
             terms = []
@@ -586,22 +576,24 @@
                 terms.append(
                     (
                         kept[top],
-                        [ahead[k] if k in ahead else swap_net(sends[k], last_hop(k)) for k in below],
+                        [ahead[k] if k in ahead else swap(sends[k], "net", last_hop(k)) for k in below],
                     )
                 )
             chain = loss_top ^ last_hop(loss_top) == group[0]
-            extras = (risk_sum,) if group[0] == net_size // 2 and kind != "early" else ()
-            folded, passed = fold(terms, loss if chain else None, extras, after)
+            sums = risk_sums if group[0] == net_size // 2 else ()
+            if group == (1,):
+                after = (loss,)
+            folded, passed = fold(terms, loss if chain else None, sums, after)
             sends.update(zip(group, folded))
             after = ()
             if chain:
                 loss_top, loss = group[0], folded[0]
-            if extras:
+            if sums:
                 (risk_sum,) = passed
         base = local_forward(touched, bar, local_blocks, duals, demand, loss)
         below = sorted(children(0, net_size))
-        arrived = [swap_net(sends[k], last_hop(k)) for k in below]
-        sums = (risk_sum, zero)
+        arrived = [swap(sends[k], "net", last_hop(k)) for k in below]
+        sums = (risk_sum, risk_sum)
         if kind != "early":
             for stride in early[:-1]:
                 risk_sum = risk_sum + swap(risk_sum, "scen", stride)

time: 151 us -> 148 us (0.980)
  local copies, waits for them, and re-layouts: 11.4 us -> 5.05 us
  starting transfers between devices: 53.4 us -> 56.4 us
  waiting for transfers between devices: 44.4 us -> 47.3 us
    ppermute x6 -> x48, starting transfers between devices: 2.72 us -> 56.4 us  [swap(): return lax.ppermute(value, axis, [(i, i ^ distance) for i in range(size)])]
    ppermute x42 -> x0, starting transfers between devices: 50.7 us -> none  [swap_net(): return lax.ppermute(value, ('net', 'scen'), pairs)]
    ppermute x6 -> x48, waiting for transfers between devices: 5.37 us -> 47.3 us  [swap(): return lax.ppermute(value, axis, [(i, i ^ distance) for i in range(size)])]
    ppermute x42 -> x0, waiting for transfers between devices: 39 us -> none  [swap_net(): return lax.ppermute(value, ('net', 'scen'), pairs)]
    unnamed x32 -> x26, local copies, waits for them, and re-layouts: 11.4 us -> 5.01 us
  transfers between devices with their start and end apart: 48 -> 48, of which waited for: 23 -> 24; matrix products, arithmetic and copies ran while one was open for 0% -> 0% of each run, Pallas kernels for 16% -> 16%
where the time goes in v7:
time: 148 us
  starting transfers between devices  56.4 us (38%)
  waiting for transfers between devices  47.3 us (32%)
  Pallas kernels  37.2 us (25%)
  local copies, waits for them, and re-layouts  5.05 us (3%)
  between operations  1.61 us (1%)
    ppermute x48, starting transfers between devices, swap(): return lax.ppermute(value, axis, [(i, i ^ distance) for i in range(size)])  56.4 us
    ppermute x48, waiting for transfers between devices, swap(): return lax.ppermute(value, axis, [(i, i ^ distance) for i in range(size)])  47.3 us
    pallas_call x3, Pallas kernels, local_adjoint(): pl.pallas_call(functools.partial(local_adjoint_kernel, touches, group), o...  12.9 us
    pallas_call x3, Pallas kernels, head_step(): pl.pallas_call(functools.partial(head_kernel, group, steps, peers, late,...  11.4 us
    pallas_call x3, Pallas kernels, local_forward(): pl.pallas_call(functools.partial(local_forward_kernel, touches, group, st...  9.87 us
    unnamed x26, local copies, waits for them, and re-layouts  5.01 us
  transfers between devices with their start and end apart: 48, of which 24 were waited for; matrix products, arithmetic and copies ran while one was open for 0% of the time, Pallas kernels for 16%

profile of v7, /device:TPU:0, one launch (start us, length us, event | category | flops | bytes accessed | tf_op | source)
XLA Modules:
  0.0 147.6 jit_solution(12154759440267604789)
XLA Ops:
  0.7 0.9 copy-done
  1.6 4.1 %collective-permute-start = (bf16[16,32,128]{2,1,0:T(8,128)(2,1)S(1)}, bf16[16,32,128]{2,1,0:T(8,128)(2,1)S(1)}, u32[]{:S(2)}, u32[]{:S(2)}) collective-permute-start(bf16[16,32,128]{2,1,0:T(8,128)(2,1)S(1)} %fusion.panel_ref.refs_0_), channel_id=1, source_target_pairs={{0,16},{4,20},{8,24},{12,28},{16,0},{20,4},{24,8},{28,12},{1,17},{... | collective-permute-start | bytes 393224 | tf_op jit(solution)/shard_map/ppermute | solution.py:486
  5.7 1.5 %collective-permute-start.1 = (bf16[16,32,128]{2,1,0:T(8,128)(2,1)S(1)}, bf16[16,32,128]{2,1,0:T(8,128)(2,1)S(1)}, u32[]{:S(2)}, u32[]{:S(2)}) collective-permute-start(bf16[16,32,128]{2,1,0:T(8,128)(2,1)S(1)} %fusion.panel_ref.refs_0_), channel_id=1, source_target_pairs={{0,4},{4,0},{8,12},{12,8},{16,20},{20,16},{24,28},{28,24},{1,5},{5... | collective-permute-start | bytes 393224 | tf_op jit(solution)/shard_map/ppermute | solution.py:486
  7.2 3.4 %copy-done.1 = bf16[64,4,128,128]{3,2,1,0:T(8,128)(2,1)S(1)} copy-done((bf16[64,4,128,128]{3,2,1,0:T(8,128)(2,1)S(1)}, bf16[64,4,128,128]{3,2,1,0:T(8,128)(2,1)}, u32[]{:S(2)}) %copy-start.1) | copy-done | bytes 8388632
  10.6 0.7 copy-done.6
  11.3 4.3 %local_adjoint.3 = (f32[32,8192]{1,0:T(8,128)S(1)}, f32[8,128]{1,0:T(8,128)S(1)}) custom-call(s32[4,64]{1,0:T(4,128)S(1)} %bitcast.29, bf16[16,32,128]{2,1,0:T(8,128)(2,1)S(1)} %fusion.panel_ref.refs_0_, bf16[64,4,128,128]{3,2,1,0:T(8,128)(2,1)S(1)} %copy-done.1), custom_call_target="tpu_custom_call" | custom-call | flops 268435456 | bytes 8388608 | tf_op jit(solution)/shard_map/local_adjoint/pallas_call | solution.py:270
  16.2 1.6 %collective-permute-start.5 = (bf16[16,32,128]{2,1,0:T(8,128)(2,1)S(1)}, bf16[16,32,128]{2,1,0:T(8,128)(2,1)S(1)}, u32[]{:S(2)}, u32[]{:S(2)}) collective-permute-start(bf16[16,32,128]{2,1,0:T(8,128)(2,1)S(1)} %get-tuple-element.79.refs_0_.refs_4_), channel_id=1, source_target_pairs={{0,8},{4,12},{8,0},{12,4},{16,24},{20,28},{24,16},{28,20},{1,9},{5... | collective-permute-start | bytes 393224 | tf_op jit(solution)/shard_map/ppermute | solution.py:486
  18.8 1.6 %collective-permute-start.3 = (bf16[16,32,128]{2,1,0:T(8,128)(2,1)S(1)}, bf16[16,32,128]{2,1,0:T(8,128)(2,1)S(1)}, u32[]{:S(2)}, u32[]{:S(2)}) collective-permute-start(bf16[16,32,128]{2,1,0:T(8,128)(2,1)S(1)} %collective-permute-done.1.refs_1_), channel_id=1, source_target_pairs={{0,8},{4,12},{8,0},{12,4},{16,24},{20,28},{24,16},{28,20},{1,9},{5... | collective-permute-start | bytes 393224 | tf_op jit(solution)/shard_map/ppermute | solution.py:486
  20.4 2.3 %collective-permute-done.5.refs_6_ = bf16[16,32,128]{2,1,0:T(8,128)(2,1)S(1)} collective-permute-done((bf16[16,32,128]{2,1,0:T(8,128)(2,1)S(1)}, bf16[16,32,128]{2,1,0:T(8,128)(2,1)S(1)}, u32[]{:S(2)}, u32[]{:S(2)}) %collective-permute-start.5) | collective-permute-done | bytes 131104 | tf_op jit(solution)/shard_map/ppermute | solution.py:486
  24.1 1.0 collective-permute-done.2.refs_2_
  25.2 1.3 collective-permute-done.3.refs_3_
  26.5 1.1 collective-permute-done.6.refs_7_
  27.6 3.6 %head_step.3 = (f32[32,8192]{1,0:T(8,128)S(1)}, bf16[32,8192]{1,0:T(8,128)(2,1)S(1)}, f32[32,128]{1,0:T(8,128)S(1)}, f32[8,128]{1,0:T(8,128)S(1)}, f32[8,128]{1,...) custom-call(s32[64]{0:T(128)S(1)} %bitcast.35, ...), custom_call_target="tpu_custom_call" | custom-call | flops 134217728 | bytes 7864320 | tf_op jit(solution)/shard_map/head_step/pallas_call | solution.py:307
  31.8 1.5 %collective-permute-start.9 = (bf16[16,32,128]{2,1,0:T(8,128)(2,1)S(1)}, bf16[16,32,128]{2,1,0:T(8,128)(2,1)S(1)}, u32[]{:S(2)}, u32[]{:S(2)}) collective-permute-start(bf16[16,32,128]{2,1,0:T(8,128)(2,1)S(1)} %get-tuple-element.89), channel_id=1, source_target_pairs={{0,4},{4,0},{8,12},{12,8},{16,20},{20,16},{24,28},{28,24},{1,5},{5... | collective-permute-start | bytes 393224 | tf_op jit(solution)/shard_map/ppermute | solution.py:486
  33.3 4.4 %collective-permute-done.9.refs_3_.refs_1_ = bf16[16,32,128]{2,1,0:T(8,128)(2,1)S(1)} collective-permute-done((bf16[16,32,128]{2,1,0:T(8,128)(2,1)S(1)}, bf16[16,32,128]{2,1,0:T(8,128)(2,1)S(1)}, u32[]{:S(2)}, u32[]{:S(2)}) %collective-permute-start.9) | collective-permute-done | bytes 131104 | tf_op jit(solution)/shard_map/ppermute | solution.py:486
  37.8 1.6 %collective-permute-start.11 = (bf16[17,32,128]{2,1,0:T(8,128)(2,1)S(1)}, bf16[17,32,128]{2,1,0:T(8,128)(2,1)S(1)}, u32[]{:S(2)}, u32[]{:S(2)}) collective-permute-start(bf16[17,32,128]{2,1,0:T(8,128)(2,1)S(1)} %fold.9.refs_3_), channel_id=1, source_target_pairs={{0,8},{4,12},{8,0},{12,4},{16,24},{20,28},{24,16},{28,20},{1,9},{5... | collective-permute-start | bytes 417800 | tf_op jit(solution)/shard_map/ppermute | solution.py:486
  39.9 1.6 %collective-permute-start.13 = (bf16[16,32,128]{2,1,0:T(8,128)(2,1)S(1)}, bf16[16,32,128]{2,1,0:T(8,128)(2,1)S(1)}, u32[]{:S(2)}, u32[]{:S(2)}) collective-permute-start(bf16[16,32,128]{2,1,0:T(8,128)(2,1)S(1)} %get-tuple-element.94), channel_id=1, source_target_pairs={{0,8},{4,12},{8,0},{12,4},{16,24},{20,28},{24,16},{28,20},{1,9},{5... | collective-permute-start | bytes 393224 | tf_op jit(solution)/shard_map/ppermute | solution.py:486
  41.5 3.0 %collective-permute-done.11.refs_2_ = bf16[17,32,128]{2,1,0:T(8,128)(2,1)S(1)} collective-permute-done((bf16[17,32,128]{2,1,0:T(8,128)(2,1)S(1)}, bf16[17,32,128]{2,1,0:T(8,128)(2,1)S(1)}, u32[]{:S(2)}, u32[]{:S(2)}) %collective-permute-start.11) | collective-permute-done | bytes 139296 | tf_op jit(solution)/shard_map/ppermute | solution.py:486
  44.7 1.2 collective-permute-done.8.refs_1_
  45.9 2.5 %collective-permute-start.12 = (bf16[16,32,128]{2,1,0:T(8,128)(2,1)S(1)}, bf16[16,32,128]{2,1,0:T(8,128)(2,1)S(1)}, u32[]{:S(2)}, u32[]{:S(2)}) collective-permute-start(bf16[16,32,128]{2,1,0:T(8,128)(2,1)S(1)} %fold.11), channel_id=1, source_target_pairs={{0,4},{4,0},{8,12},{12,8},{16,20},{20,16},{24,28},{28,24},{1,5},{5... | collective-permute-start | bytes 393224 | tf_op jit(solution)/shard_map/ppermute | solution.py:486
  48.5 1.6 %collective-permute-start.15 = (f32[8,128]{1,0:T(8,128)S(1)}, f32[8,128]{1,0:T(8,128)S(1)}, u32[]{:S(2)}, u32[]{:S(2)}) collective-permute-start(f32[8,128]{1,0:T(8,128)S(1)} %get-tuple-element.99.refs_9_), channel_id=1, source_target_pairs={{0,2},{1,3},{2,0},{3,1},{4,6},{5,7},{6,4},{7,5},{8,10},{9,11},{10,... | collective-permute-start | bytes 12296 | tf_op jit(solution)/shard_map/ppermute | solution.py:486
  50.1 3.3 %local_forward.3.refs_5_ = f32[16,32,128]{2,1,0:T(8,128)S(1)} custom-call(s32[4,64]{1,0:T(4,128)S(1)} %bitcast.30, bf16[32,8192]{1,0:T(8,128)(2,1)S(1)} %get-tuple-element.95.bar_ref, bf16[64,4,128,128]{3,2,1,0:T(8,128)(2,1)S(1)} %bitcast.25, f32[16,32,128]{2,1,0:T(8,128)S(1)} %bitcast_bitcast_fusion.duals_ref, f32[32,2048]{1,0:T(8,128)S(1)} %copy-done.4, ...), custom_call_target="tpu_custom_call" | custom-call | flops 268435456 | bytes 8388608 | tf_op jit(solution)/shard_map/local_forward/pallas_call | solution.py:409
  54.0 1.4 collective-permute-start.19
  55.4 2.2 %collective-permute-start.16 = (bf16[16,32,128]{2,1,0:T(8,128)(2,1)S(1)}, bf16[16,32,128]{2,1,0:T(8,128)(2,1)S(1)}, u32[]{:S(2)}, u32[]{:S(2)}) collective-permute-start(bf16[16,32,128]{2,1,0:T(8,128)(2,1)S(1)} %get-tuple-element.100.panel_ref.refs_0_), channel_id=1, source_target_pairs={{0,4},{4,0},{8,12},{12,8},{16,20},{20,16},{24,28},{28,24},{1,5},{5... | collective-permute-start | bytes 393224 | tf_op jit(solution)/shard_map/ppermute | solution.py:486
  57.5 4.3 %local_adjoint.4 = (f32[32,8192]{1,0:T(8,128)S(1)}, f32[8,128]{1,0:T(8,128)S(1)}) custom-call(s32[4,64]{1,0:T(4,128)S(1)} %bitcast.31, bf16[16,32,128]{2,1,0:T(8,128)(2,1)S(1)} %get-tuple-element.100.panel_ref.refs_0_, bf16[64,4,128,128]{3,2,1,0:T(8,128)(2,1)S(1)} %bitcast.25), custom_call_target="tpu_custom_call" | custom-call | flops 268435456 | bytes 8388608 | tf_op jit(solution)/shard_map/local_adjoint/pallas_call | solution.py:270
  61.9 1.8 %collective-permute-start.21 = (bf16[16,32,128]{2,1,0:T(8,128)(2,1)S(1)}, bf16[16,32,128]{2,1,0:T(8,128)(2,1)S(1)}, u32[]{:S(2)}, u32[]{:S(2)}) collective-permute-start(bf16[16,32,128]{2,1,0:T(8,128)(2,1)S(1)} %get-tuple-element.103.refs_4_), channel_id=1, source_target_pairs={{0,8},{4,12},{8,0},{12,4},{16,24},{20,28},{24,16},{28,20},{1,9},{5... | collective-permute-start | bytes 393224 | tf_op jit(solution)/shard_map/ppermute | solution.py:486
  64.0 2.2 %collective-permute-start.20 = (bf16[16,32,128]{2,1,0:T(8,128)(2,1)S(1)}, bf16[16,32,128]{2,1,0:T(8,128)(2,1)S(1)}, u32[]{:S(2)}, u32[]{:S(2)}) collective-permute-start(bf16[16,32,128]{2,1,0:T(8,128)(2,1)S(1)} %get-tuple-element.103.refs_4_), channel_id=1, source_target_pairs={{0,4},{4,0},{8,12},{12,8},{16,20},{20,16},{24,28},{28,24},{1,5},{5... | collective-permute-start | bytes 393224 | tf_op jit(solution)/shard_map/ppermute | solution.py:486
  66.2 0.7 collective-permute-done.21.refs_6_
  66.9 2.2 %collective-permute-start.22 = (bf16[16,32,128]{2,1,0:T(8,128)(2,1)S(1)}, bf16[16,32,128]{2,1,0:T(8,128)(2,1)S(1)}, u32[]{:S(2)}, u32[]{:S(2)}) collective-permute-start(bf16[16,32,128]{2,1,0:T(8,128)(2,1)S(1)} %collective-permute-done.21.refs_6_), channel_id=1, source_target_pairs={{0,4},{4,0},{8,12},{12,8},{16,20},{20,16},{24,28},{28,24},{1,5},{5... | collective-permute-start | bytes 393224 | tf_op jit(solution)/shard_map/ppermute | solution.py:486
  69.1 1.6 %collective-permute-start.23 = (f32[8,128]{1,0:T(8,128)S(1)}, f32[8,128]{1,0:T(8,128)S(1)}, u32[]{:S(2)}, u32[]{:S(2)}) collective-permute-start(f32[8,128]{1,0:T(8,128)S(1)} %get-tuple-element.108.refs_14_), channel_id=1, source_target_pairs={{0,2},{1,3},{2,0},{3,1},{4,6},{5,7},{6,4},{7,5},{8,10},{9,11},{10,... | collective-permute-start | bytes 12296 | tf_op jit(solution)/shard_map/ppermute | solution.py:486
  70.6 2.0 %collective-permute-done.23.refs_15_ = f32[8,128]{1,0:T(8,128)S(1)} collective-permute-done((f32[8,128]{1,0:T(8,128)S(1)}, f32[8,128]{1,0:T(8,128)S(1)}, u32[]{:S(2)}, u32[]{:S(2)}) %collective-permute-start.23) | collective-permute-done | bytes 4128 | tf_op jit(solution)/shard_map/ppermute | solution.py:486
  72.7 0.7 collective-permute-done.22.refs_7_
  73.4 3.6 %head_step.4 = (f32[32,8192]{1,0:T(8,128)S(1)}, bf16[32,8192]{1,0:T(8,128)(2,1)S(1)}, f32[32,128]{1,0:T(8,128)S(1)}, f32[8,128]{1,0:T(8,128)S(1)}, f32[8,128]{1,...) custom-call(s32[64]{0:T(128)S(1)} %bitcast.36, ...), custom_call_target="tpu_custom_call" | custom-call | flops 134217728 | bytes 7864320 | tf_op jit(solution)/shard_map/head_step/pallas_call | solution.py:307
  76.9 2.1 %collective-permute-start.26 = (bf16[17,32,128]{2,1,0:T(8,128)(2,1)S(1)}, bf16[17,32,128]{2,1,0:T(8,128)(2,1)S(1)}, u32[]{:S(2)}, u32[]{:S(2)}) collective-permute-start(bf16[17,32,128]{2,1,0:T(8,128)(2,1)S(1)} %get-tuple-element.115.refs_2_), channel_id=1, source_target_pairs={{0,4},{4,0},{8,12},{12,8},{16,20},{20,16},{24,28},{28,24},{1,5},{5... | collective-permute-start | bytes 417800 | tf_op jit(solution)/shard_map/ppermute | solution.py:486
  79.1 6.2 %collective-permute-done.25.refs_3_.refs_1_ = bf16[16,32,128]{2,1,0:T(8,128)(2,1)S(1)} collective-permute-done((bf16[16,32,128]{2,1,0:T(8,128)(2,1)S(1)}, bf16[16,32,128]{2,1,0:T(8,128)(2,1)S(1)}, u32[]{:S(2)}, u32[]{:S(2)}) %collective-permute-start.25) | collective-permute-done | bytes 131104 | tf_op jit(solution)/shard_map/ppermute | solution.py:486
  86.0 1.5 %collective-permute-start.24 = (bf16[16,32,128]{2,1,0:T(8,128)(2,1)S(1)}, bf16[16,32,128]{2,1,0:T(8,128)(2,1)S(1)}, u32[]{:S(2)}, u32[]{:S(2)}) collective-permute-start(bf16[16,32,128]{2,1,0:T(8,128)(2,1)S(1)} %get-tuple-element.111), channel_id=1, source_target_pairs={{0,8},{4,12},{8,0},{12,4},{16,24},{20,28},{24,16},{28,20},{1,9},{5... | collective-permute-start | bytes 393224 | tf_op jit(solution)/shard_map/ppermute | solution.py:486
  87.5 3.7 %collective-permute-done.27.refs_2_ = bf16[17,32,128]{2,1,0:T(8,128)(2,1)S(1)} collective-permute-done((bf16[17,32,128]{2,1,0:T(8,128)(2,1)S(1)}, bf16[17,32,128]{2,1,0:T(8,128)(2,1)S(1)}, u32[]{:S(2)}, u32[]{:S(2)}) %collective-permute-start.27) | collective-permute-done | bytes 139296 | tf_op jit(solution)/shard_map/ppermute | solution.py:486
  91.3 2.2 %collective-permute-start.30 = (bf16[17,32,128]{2,1,0:T(8,128)(2,1)S(1)}, bf16[17,32,128]{2,1,0:T(8,128)(2,1)S(1)}, u32[]{:S(2)}, u32[]{:S(2)}) collective-permute-start(bf16[17,32,128]{2,1,0:T(8,128)(2,1)S(1)} %fold.13.refs_2_.after_ref.refs_4_), channel_id=1, source_target_pairs={{0,16},{4,20},{8,24},{12,28},{16,0},{20,4},{24,8},{28,12},{1,17},{... | collective-permute-start | bytes 417800 | tf_op jit(solution)/shard_map/ppermute | solution.py:486
  93.6 0.8 collective-permute-start.29
  94.4 0.8 collective-permute-start.28
  95.2 3.3 %local_forward.4.refs_5_ = f32[16,32,128]{2,1,0:T(8,128)S(1)} custom-call(s32[4,64]{1,0:T(4,128)S(1)} %bitcast.32, bf16[32,8192]{1,0:T(8,128)(2,1)S(1)} %get-tuple-element.117.bar_ref, bf16[64,4,128,128]{3,2,1,0:T(8,128)(2,1)S(1)} %bitcast.25, f32[16,32,128]{2,1,0:T(8,128)S(1)} %get-tuple-element.118.duals_ref, f32[32,2048]{1,0:T(8,128)S(1)} %copy-done.4, ...), custom_call_target="tpu_custom_call" | custom-call | flops 268435456 | bytes 8388608 | tf_op jit(solution)/shard_map/local_forward/pallas_call | solution.py:409
  98.5 2.6 %collective-permute-done.29.refs_2_ = bf16[16,32,128]{2,1,0:T(8,128)(2,1)S(1)} collective-permute-done((bf16[16,32,128]{2,1,0:T(8,128)(2,1)S(1)}, bf16[16,32,128]{2,1,0:T(8,128)(2,1)S(1)}, u32[]{:S(2)}, u32[]{:S(2)}) %collective-permute-start.29) | collective-permute-done | bytes 131104 | tf_op jit(solution)/shard_map/ppermute | solution.py:486
  101.8 2.1 %collective-permute-start.31 = (bf16[16,32,128]{2,1,0:T(8,128)(2,1)S(1)}, bf16[16,32,128]{2,1,0:T(8,128)(2,1)S(1)}, u32[]{:S(2)}, u32[]{:S(2)}) collective-permute-start(bf16[16,32,128]{2,1,0:T(8,128)(2,1)S(1)} %get-tuple-element.123.panel_ref.refs_0_), channel_id=1, source_target_pairs={{0,4},{4,0},{8,12},{12,8},{16,20},{20,16},{24,28},{28,24},{1,5},{5... | collective-permute-start | bytes 393224 | tf_op jit(solution)/shard_map/ppermute | solution.py:486
  103.9 4.3 %local_adjoint.5 = (f32[32,8192]{1,0:T(8,128)S(1)}, f32[8,128]{1,0:T(8,128)S(1)}) custom-call(s32[4,64]{1,0:T(4,128)S(1)} %bitcast.33, bf16[16,32,128]{2,1,0:T(8,128)(2,1)S(1)} %get-tuple-element.123.panel_ref.refs_0_, bf16[64,4,128,128]{3,2,1,0:T(8,128)(2,1)S(1)} %bitcast.25), custom_call_target="tpu_custom_call" | custom-call | flops 268435456 | bytes 8388608 | tf_op jit(solution)/shard_map/local_adjoint/pallas_call | solution.py:270
  108.2 0.8 collective-permute-done.34.arrived_ref
  109.6 1.5 %collective-permute-start.32 = (bf16[16,32,128]{2,1,0:T(8,128)(2,1)S(1)}, bf16[16,32,128]{2,1,0:T(8,128)(2,1)S(1)}, u32[]{:S(2)}, u32[]{:S(2)}) collective-permute-start(bf16[16,32,128]{2,1,0:T(8,128)(2,1)S(1)} %get-tuple-element.123.panel_ref.refs_0_), channel_id=1, source_target_pairs={{0,8},{4,12},{8,0},{12,4},{16,24},{20,28},{24,16},{28,20},{1,9},{5... | collective-permute-start | bytes 393224 | tf_op jit(solution)/shard_map/ppermute | solution.py:486
  111.1 0.9 collective-permute-start.35
  112.2 1.8 %collective-permute-done.36.refs_6_ = bf16[16,32,128]{2,1,0:T(8,128)(2,1)S(1)} collective-permute-done((bf16[16,32,128]{2,1,0:T(8,128)(2,1)S(1)}, bf16[16,32,128]{2,1,0:T(8,128)(2,1)S(1)}, u32[]{:S(2)}, u32[]{:S(2)}) %collective-permute-start.36) | collective-permute-done | bytes 131104 | tf_op jit(solution)/shard_map/ppermute | solution.py:486
  114.0 0.9 collective-permute-start.37
  115.4 0.7 collective-permute-done.38.refs_15_
  116.1 0.9 collective-permute-done.33.refs_3_
  116.9 2.0 %collective-permute-done.37.refs_7_ = bf16[16,32,128]{2,1,0:T(8,128)(2,1)S(1)} collective-permute-done((bf16[16,32,128]{2,1,0:T(8,128)(2,1)S(1)}, bf16[16,32,128]{2,1,0:T(8,128)(2,1)S(1)}, u32[]{:S(2)}, u32[]{:S(2)}) %collective-permute-start.37) | collective-permute-done | bytes 131104 | tf_op jit(solution)/shard_map/ppermute | solution.py:486
  119.0 4.2 %head_step.5 = (f32[32,8192]{1,0:T(8,128)}, bf16[32,8192]{1,0:T(8,128)(2,1)S(1)}, f32[32,128]{1,0:T(8,128)S(1)}, f32[8,128]{1,0:T(8,128)S(1)}, f32[8,128]{1,0:T(...) custom-call(s32[64]{0:T(128)S(1)} %bitcast.37, ...), custom_call_target="tpu_custom_call" | custom-call | flops 134217728 | bytes 7864320 | tf_op jit(solution)/shard_map/head_step/pallas_call | solution.py:307
  123.2 0.9 collective-permute-start.41
  124.1 1.1 collective-permute-start.40
  125.3 1.2 collective-permute-done.42.refs_3_.refs_5_
  126.4 3.3 %collective-permute-done.40.refs_4_.refs_1_ = bf16[16,32,128]{2,1,0:T(8,128)(2,1)S(1)} collective-permute-done((bf16[16,32,128]{2,1,0:T(8,128)(2,1)S(1)}, bf16[16,32,128]{2,1,0:T(8,128)(2,1)S(1)}, u32[]{:S(2)}, u32[]{:S(2)}) %collective-permute-start.40) | collective-permute-done | bytes 131104 | tf_op jit(solution)/shard_map/ppermute | solution.py:486
  130.4 1.5 %collective-permute-start.39 = (bf16[16,32,128]{2,1,0:T(8,128)(2,1)S(1)}, bf16[16,32,128]{2,1,0:T(8,128)(2,1)S(1)}, u32[]{:S(2)}, u32[]{:S(2)}) collective-permute-start(bf16[16,32,128]{2,1,0:T(8,128)(2,1)S(1)} %get-tuple-element.133), channel_id=1, source_target_pairs={{0,8},{4,12},{8,0},{12,4},{16,24},{20,28},{24,16},{28,20},{1,9},{5... | collective-permute-start | bytes 393224 | tf_op jit(solution)/shard_map/ppermute | solution.py:486
  131.9 5.4 %collective-permute-done.43.refs_2_ = bf16[17,32,128]{2,1,0:T(8,128)(2,1)S(1)} collective-permute-done((bf16[17,32,128]{2,1,0:T(8,128)(2,1)S(1)}, bf16[17,32,128]{2,1,0:T(8,128)(2,1)S(1)}, u32[]{:S(2)}, u32[]{:S(2)}) %collective-permute-start.43) | collective-permute-done | bytes 139296 | tf_op jit(solution)/shard_map/ppermute | solution.py:486
  137.4 1.8 %collective-permute-start.45 = (bf16[16,32,128]{2,1,0:T(8,128)(2,1)S(1)}, bf16[16,32,128]{2,1,0:T(8,128)(2,1)S(1)}, u32[]{:S(2)}, u32[]{:S(2)}) collective-permute-start(bf16[16,32,128]{2,1,0:T(8,128)(2,1)S(1)} %get-tuple-element.140), channel_id=1, source_target_pairs={{0,8},{4,12},{8,0},{12,4},{16,24},{20,28},{24,16},{28,20},{1,9},{5... | collective-permute-start | bytes 393224 | tf_op jit(solution)/shard_map/ppermute | solution.py:486
  139.3 2.6 %collective-permute-start.44 = (bf16[16,32,128]{2,1,0:T(8,128)(2,1)S(1)}, bf16[16,32,128]{2,1,0:T(8,128)(2,1)S(1)}, u32[]{:S(2)}, u32[]{:S(2)}) collective-permute-start(bf16[16,32,128]{2,1,0:T(8,128)(2,1)S(1)} %fold.17), channel_id=1, source_target_pairs={{0,4},{4,0},{8,12},{12,8},{16,20},{20,16},{24,28},{28,24},{1,5},{5... | collective-permute-start | bytes 393224 | tf_op jit(solution)/shard_map/ppermute | solution.py:486
  141.9 1.5 %collective-permute-start.47 = (f32[8,128]{1,0:T(8,128)S(1)}, f32[8,128]{1,0:T(8,128)S(1)}, u32[]{:S(2)}, u32[]{:S(2)}) collective-permute-start(f32[8,128]{1,0:T(8,128)S(1)} %get-tuple-element.146.refs_9_), channel_id=1, source_target_pairs={{0,2},{1,3},{2,0},{3,1},{4,6},{5,7},{6,4},{7,5},{8,10},{9,11},{10,... | collective-permute-start | bytes 12296 | tf_op jit(solution)/shard_map/ppermute | solution.py:486
  143.4 3.3 %local_forward.5.refs_5_ = f32[16,32,128]{2,1,0:T(8,128)S(1)} custom-call(s32[4,64]{1,0:T(4,128)S(1)} %bitcast.34, bf16[32,8192]{1,0:T(8,128)(2,1)S(1)} %get-tuple-element.141.bar_ref, bf16[64,4,128,128]{3,2,1,0:T(8,128)(2,1)S(1)} %bitcast.25, f32[16,32,128]{2,1,0:T(8,128)S(1)} %get-tuple-element.142.duals_ref, f32[32,2048]{1,0:T(8,128)S(1)} %copy-done.4, ...), custom_call_target="tpu_custom_call" | custom-call | flops 268435456 | bytes 8388608 | tf_op jit(solution)/shard_map/local_forward/pallas_call | solution.py:409
  146.8 0.8 settle.5
  (86 shorter events, 8.7 us)
Async XLA Ops:
  0.6 1.0 copy-start
  0.6 23.2 %copy-start.10 = (s32[64]{0:T(128)S(1)}, s32[64]{0:T(128)}, u32[]{:S(2)}) copy-start(s32[64]{0:T(128)} %param.21) | copy-start | bytes 772
  0.7 23.2 %copy-start.8 = (f32[32]{0:T(128)S(1)}, f32[32]{0:T(128)}, u32[]{:S(2)}) copy-start(f32[32]{0:T(128)} %param.15) | copy-start | bytes 388
  0.7 23.2 %copy-start.9 = (f32[32]{0:T(128)S(1)}, f32[32]{0:T(128)}, u32[]{:S(2)}) copy-start(f32[32]{0:T(128)} %param.14) | copy-start | bytes 388
  0.7 26.9 %copy-start.5 = (f32[8192]{0:T(1024)S(1)}, f32[8192]{0:T(1024)}, u32[]{:S(2)}) copy-start(f32[8192]{0:T(1024)} %param.17) | copy-start | bytes 98308
  1.6 14.0 %collective-permute-start = (bf16[16,32,128]{2,1,0:T(8,128)(2,1)S(1)}, bf16[16,32,128]{2,1,0:T(8,128)(2,1)S(1)}, u32[]{:S(2)}, u32[]{:S(2)}) collective-permute-start(bf16[16,32,128]{2,1,0:T(8,128)(2,1)S(1)} %fusion.panel_ref.refs_0_), channel_id=1, source_target_pairs={{0,16},{4,20},{8,24},{12,28},{16,0},{20,4},{24,8},{28,12},{1,17},{... | collective-permute-start | bytes 393224 | tf_op jit(solution)/shard_map/ppermute | solution.py:486
  5.7 13.1 %collective-permute-start.1 = (bf16[16,32,128]{2,1,0:T(8,128)(2,1)S(1)}, bf16[16,32,128]{2,1,0:T(8,128)(2,1)S(1)}, u32[]{:S(2)}, u32[]{:S(2)}) collective-permute-start(bf16[16,32,128]{2,1,0:T(8,128)(2,1)S(1)} %fusion.panel_ref.refs_0_), channel_id=1, source_target_pairs={{0,4},{4,0},{8,12},{12,8},{16,20},{20,16},{24,28},{28,24},{1,5},{5... | collective-permute-start | bytes 393224 | tf_op jit(solution)/shard_map/ppermute | solution.py:486
  7.2 3.4 %copy-start.1 = (bf16[64,4,128,128]{3,2,1,0:T(8,128)(2,1)S(1)}, bf16[64,4,128,128]{3,2,1,0:T(8,128)(2,1)}, u32[]{:S(2)}) copy-start(bf16[64,4,128,128]{3,2,1,0:T(8,128)(2,1)} %blocks_ref.11) | copy-start | bytes 25165828
  10.6 0.7 copy-start.6
  11.3 12.6 %copy-start.2 = (bf16[64,128,128]{2,1,0:T(8,128)(2,1)S(1)}, bf16[64,128,128]{2,1,0:T(8,128)(2,1)}, u32[]{:S(2)}) copy-start(bf16[64,128,128]{2,1,0:T(8,128)(2,1)} %refs_8_.5) | copy-start | bytes 6291460
  11.3 12.6 %copy-start.3 = (f32[32,8192]{1,0:T(8,128)S(1)}, f32[32,8192]{1,0:T(8,128)}, u32[]{:S(2)}) copy-start(f32[32,8192]{1,0:T(8,128)} %refs_10_.1) | copy-start | bytes 3145732
  11.3 38.8 %slice-start = ((s8[8388608]{0:T(1024)(128)(4,1)}), s8[4194304]{0:T(1024)(128)(4,1)S(1)}, s32[]{:S(2)}) async-start(s8[8388608]{0:T(1024)(128)(4,1)} %bitcast.24), calls=%async_computation | async-start | bytes 8388608
  11.3 38.8 %copy-start.4 = (f32[32,2048]{1,0:T(8,128)S(1)}, f32[32,2048]{1,0:T(8,128)}, u32[]{:S(2)}) copy-start(f32[32,2048]{1,0:T(8,128)} %demand_ref.5) | copy-start | bytes 786436
  16.2 6.4 %collective-permute-start.5 = (bf16[16,32,128]{2,1,0:T(8,128)(2,1)S(1)}, bf16[16,32,128]{2,1,0:T(8,128)(2,1)S(1)}, u32[]{:S(2)}, u32[]{:S(2)}) collective-permute-start(bf16[16,32,128]{2,1,0:T(8,128)(2,1)S(1)} %get-tuple-element.79.refs_0_.refs_4_), channel_id=1, source_target_pairs={{0,8},{4,12},{8,0},{12,4},{16,24},{20,28},{24,16},{28,20},{1,9},{5... | collective-permute-start | bytes 393224 | tf_op jit(solution)/shard_map/ppermute | solution.py:486
  17.8 7.3 %collective-permute-start.2 = (bf16[16,32,128]{2,1,0:T(8,128)(2,1)S(1)}, bf16[16,32,128]{2,1,0:T(8,128)(2,1)S(1)}, u32[]{:S(2)}, u32[]{:S(2)}) collective-permute-start(bf16[16,32,128]{2,1,0:T(8,128)(2,1)S(1)} %fusion.panel_ref.refs_0_), channel_id=1, source_target_pairs={{0,8},{4,12},{8,0},{12,4},{16,24},{20,28},{24,16},{28,20},{1,9},{5... | collective-permute-start | bytes 393224 | tf_op jit(solution)/shard_map/ppermute | solution.py:486
  18.2 8.3 %collective-permute-start.4 = (bf16[16,32,128]{2,1,0:T(8,128)(2,1)S(1)}, bf16[16,32,128]{2,1,0:T(8,128)(2,1)S(1)}, u32[]{:S(2)}, u32[]{:S(2)}) collective-permute-start(bf16[16,32,128]{2,1,0:T(8,128)(2,1)S(1)} %get-tuple-element.79.refs_0_.refs_4_), channel_id=1, source_target_pairs={{0,4},{4,0},{8,12},{12,8},{16,20},{20,16},{24,28},{28,24},{1,5},{5... | collective-permute-start | bytes 393224 | tf_op jit(solution)/shard_map/ppermute | solution.py:486
  18.8 7.7 %collective-permute-start.3 = (bf16[16,32,128]{2,1,0:T(8,128)(2,1)S(1)}, bf16[16,32,128]{2,1,0:T(8,128)(2,1)S(1)}, u32[]{:S(2)}, u32[]{:S(2)}) collective-permute-start(bf16[16,32,128]{2,1,0:T(8,128)(2,1)S(1)} %collective-permute-done.1.refs_1_), channel_id=1, source_target_pairs={{0,8},{4,12},{8,0},{12,4},{16,24},{20,28},{24,16},{28,20},{1,9},{5... | collective-permute-start | bytes 393224 | tf_op jit(solution)/shard_map/ppermute | solution.py:486
  22.6 5.0 %collective-permute-start.6 = (bf16[16,32,128]{2,1,0:T(8,128)(2,1)S(1)}, bf16[16,32,128]{2,1,0:T(8,128)(2,1)S(1)}, u32[]{:S(2)}, u32[]{:S(2)}) collective-permute-start(bf16[16,32,128]{2,1,0:T(8,128)(2,1)S(1)} %collective-permute-done.5.refs_6_), channel_id=1, source_target_pairs={{0,4},{4,0},{8,12},{12,8},{16,20},{20,16},{24,28},{28,24},{1,5},{5... | collective-permute-start | bytes 393224 | tf_op jit(solution)/shard_map/ppermute | solution.py:486
  23.9 26.2 %slice-start.1 = ((s8[8388608]{0:T(1024)(128)(4,1)}), s8[4194304]{0:T(1024)(128)(4,1)S(1)}, s32[]{:S(2)}) async-start(s8[8388608]{0:T(1024)(128)(4,1)} %bitcast.24), calls=%async_computation.1 | async-start | bytes 8388608
  24.0 1.2 collective-permute-start.7
  27.6 29.9 %copy-start.7 = (s32[64,4]{0,1:T(4,128)S(1)}, s32[64,4]{0,1:T(4,128)}, u32[]{:S(2)}) copy-start(s32[64,4]{0,1:T(4,128)} %param.20) | copy-start | bytes 3076
  31.2 6.5 %collective-permute-start.10 = (bf16[17,32,128]{2,1,0:T(8,128)(2,1)S(1)}, bf16[17,32,128]{2,1,0:T(8,128)(2,1)S(1)}, u32[]{:S(2)}, u32[]{:S(2)}) collective-permute-start(bf16[17,32,128]{2,1,0:T(8,128)(2,1)S(1)} %get-tuple-element.91.refs_2_), channel_id=1, source_target_pairs={{0,4},{4,0},{8,12},{12,8},{16,20},{20,16},{24,28},{28,24},{1,5},{5... | collective-permute-start | bytes 417800 | tf_op jit(solution)/shard_map/ppermute | solution.py:486
  31.8 5.9 %collective-permute-start.9 = (bf16[16,32,128]{2,1,0:T(8,128)(2,1)S(1)}, bf16[16,32,128]{2,1,0:T(8,128)(2,1)S(1)}, u32[]{:S(2)}, u32[]{:S(2)}) collective-permute-start(bf16[16,32,128]{2,1,0:T(8,128)(2,1)S(1)} %get-tuple-element.89), channel_id=1, source_target_pairs={{0,4},{4,0},{8,12},{12,8},{16,20},{20,16},{24,28},{28,24},{1,5},{5... | collective-permute-start | bytes 393224 | tf_op jit(solution)/shard_map/ppermute | solution.py:486
  37.8 6.7 %collective-permute-start.11 = (bf16[17,32,128]{2,1,0:T(8,128)(2,1)S(1)}, bf16[17,32,128]{2,1,0:T(8,128)(2,1)S(1)}, u32[]{:S(2)}, u32[]{:S(2)}) collective-permute-start(bf16[17,32,128]{2,1,0:T(8,128)(2,1)S(1)} %fold.9.refs_3_), channel_id=1, source_target_pairs={{0,8},{4,12},{8,0},{12,4},{16,24},{20,28},{24,16},{28,20},{1,9},{5... | collective-permute-start | bytes 417800 | tf_op jit(solution)/shard_map/ppermute | solution.py:486
  39.5 6.4 %collective-permute-start.8 = (bf16[16,32,128]{2,1,0:T(8,128)(2,1)S(1)}, bf16[16,32,128]{2,1,0:T(8,128)(2,1)S(1)}, u32[]{:S(2)}, u32[]{:S(2)}) collective-permute-start(bf16[16,32,128]{2,1,0:T(8,128)(2,1)S(1)} %get-tuple-element.87), channel_id=1, source_target_pairs={{0,8},{4,12},{8,0},{12,4},{16,24},{20,28},{24,16},{28,20},{1,9},{5... | collective-permute-start | bytes 393224 | tf_op jit(solution)/shard_map/ppermute | solution.py:486
  39.9 13.5 %collective-permute-start.13 = (bf16[16,32,128]{2,1,0:T(8,128)(2,1)S(1)}, bf16[16,32,128]{2,1,0:T(8,128)(2,1)S(1)}, u32[]{:S(2)}, u32[]{:S(2)}) collective-permute-start(bf16[16,32,128]{2,1,0:T(8,128)(2,1)S(1)} %get-tuple-element.94), channel_id=1, source_target_pairs={{0,8},{4,12},{8,0},{12,4},{16,24},{20,28},{24,16},{28,20},{1,9},{5... | collective-permute-start | bytes 393224 | tf_op jit(solution)/shard_map/ppermute | solution.py:486
  44.6 9.2 %collective-permute-start.14 = (bf16[17,32,128]{2,1,0:T(8,128)(2,1)S(1)}, bf16[17,32,128]{2,1,0:T(8,128)(2,1)S(1)}, u32[]{:S(2)}, u32[]{:S(2)}) collective-permute-start(bf16[17,32,128]{2,1,0:T(8,128)(2,1)S(1)} %get-tuple-element.93.refs_2_.after_ref.refs_4_), channel_id=1, source_target_pairs={{0,16},{4,20},{8,24},{12,28},{16,0},{20,4},{24,8},{28,12},{1,17},{... | collective-permute-start | bytes 417800 | tf_op jit(solution)/shard_map/ppermute | solution.py:486
  45.9 7.5 %collective-permute-start.12 = (bf16[16,32,128]{2,1,0:T(8,128)(2,1)S(1)}, bf16[16,32,128]{2,1,0:T(8,128)(2,1)S(1)}, u32[]{:S(2)}, u32[]{:S(2)}) collective-permute-start(bf16[16,32,128]{2,1,0:T(8,128)(2,1)S(1)} %fold.11), channel_id=1, source_target_pairs={{0,4},{4,0},{8,12},{12,8},{16,20},{20,16},{24,28},{28,24},{1,5},{5... | collective-permute-start | bytes 393224 | tf_op jit(solution)/shard_map/ppermute | solution.py:486
  48.5 4.9 %collective-permute-start.15 = (f32[8,128]{1,0:T(8,128)S(1)}, f32[8,128]{1,0:T(8,128)S(1)}, u32[]{:S(2)}, u32[]{:S(2)}) collective-permute-start(f32[8,128]{1,0:T(8,128)S(1)} %get-tuple-element.99.refs_9_), channel_id=1, source_target_pairs={{0,2},{1,3},{2,0},{3,1},{4,6},{5,7},{6,4},{7,5},{8,10},{9,11},{10,... | collective-permute-start | bytes 12296 | tf_op jit(solution)/shard_map/ppermute | solution.py:486
  54.0 7.9 %collective-permute-start.19 = (bf16[16,32,128]{2,1,0:T(8,128)(2,1)S(1)}, bf16[16,32,128]{2,1,0:T(8,128)(2,1)S(1)}, u32[]{:S(2)}, u32[]{:S(2)}) collective-permute-start(bf16[16,32,128]{2,1,0:T(8,128)(2,1)S(1)} %get-tuple-element.100.panel_ref.refs_0_), channel_id=1, source_target_pairs={{0,16},{4,20},{8,24},{12,28},{16,0},{20,4},{24,8},{28,12},{1,17},{... | collective-permute-start | bytes 393224 | tf_op jit(solution)/shard_map/ppermute | solution.py:486
  55.4 10.7 %collective-permute-start.16 = (bf16[16,32,128]{2,1,0:T(8,128)(2,1)S(1)}, bf16[16,32,128]{2,1,0:T(8,128)(2,1)S(1)}, u32[]{:S(2)}, u32[]{:S(2)}) collective-permute-start(bf16[16,32,128]{2,1,0:T(8,128)(2,1)S(1)} %get-tuple-element.100.panel_ref.refs_0_), channel_id=1, source_target_pairs={{0,4},{4,0},{8,12},{12,8},{16,20},{20,16},{24,28},{28,24},{1,5},{5... | collective-permute-start | bytes 393224 | tf_op jit(solution)/shard_map/ppermute | solution.py:486
  61.9 5.0 %collective-permute-start.21 = (bf16[16,32,128]{2,1,0:T(8,128)(2,1)S(1)}, bf16[16,32,128]{2,1,0:T(8,128)(2,1)S(1)}, u32[]{:S(2)}, u32[]{:S(2)}) collective-permute-start(bf16[16,32,128]{2,1,0:T(8,128)(2,1)S(1)} %get-tuple-element.103.refs_4_), channel_id=1, source_target_pairs={{0,8},{4,12},{8,0},{12,4},{16,24},{20,28},{24,16},{28,20},{1,9},{5... | collective-permute-start | bytes 393224 | tf_op jit(solution)/shard_map/ppermute | solution.py:486
  63.7 6.9 %collective-permute-start.17 = (bf16[16,32,128]{2,1,0:T(8,128)(2,1)S(1)}, bf16[16,32,128]{2,1,0:T(8,128)(2,1)S(1)}, u32[]{:S(2)}, u32[]{:S(2)}) collective-permute-start(bf16[16,32,128]{2,1,0:T(8,128)(2,1)S(1)} %get-tuple-element.100.panel_ref.refs_0_), channel_id=1, source_target_pairs={{0,8},{4,12},{8,0},{12,4},{16,24},{20,28},{24,16},{28,20},{1,9},{5... | collective-permute-start | bytes 393224 | tf_op jit(solution)/shard_map/ppermute | solution.py:486
  64.0 8.7 %collective-permute-start.20 = (bf16[16,32,128]{2,1,0:T(8,128)(2,1)S(1)}, bf16[16,32,128]{2,1,0:T(8,128)(2,1)S(1)}, u32[]{:S(2)}, u32[]{:S(2)}) collective-permute-start(bf16[16,32,128]{2,1,0:T(8,128)(2,1)S(1)} %get-tuple-element.103.refs_4_), channel_id=1, source_target_pairs={{0,4},{4,0},{8,12},{12,8},{16,20},{20,16},{24,28},{28,24},{1,5},{5... | collective-permute-start | bytes 393224 | tf_op jit(solution)/shard_map/ppermute | solution.py:486
  66.1 6.5 %collective-permute-start.18 = (bf16[16,32,128]{2,1,0:T(8,128)(2,1)S(1)}, bf16[16,32,128]{2,1,0:T(8,128)(2,1)S(1)}, u32[]{:S(2)}, u32[]{:S(2)}) collective-permute-start(bf16[16,32,128]{2,1,0:T(8,128)(2,1)S(1)} %collective-permute-done.16.refs_1_), channel_id=1, source_target_pairs={{0,8},{4,12},{8,0},{12,4},{16,24},{20,28},{24,16},{28,20},{1,9},{5... | collective-permute-start | bytes 393224 | tf_op jit(solution)/shard_map/ppermute | solution.py:486
  66.9 6.5 %collective-permute-start.22 = (bf16[16,32,128]{2,1,0:T(8,128)(2,1)S(1)}, bf16[16,32,128]{2,1,0:T(8,128)(2,1)S(1)}, u32[]{:S(2)}, u32[]{:S(2)}) collective-permute-start(bf16[16,32,128]{2,1,0:T(8,128)(2,1)S(1)} %collective-permute-done.21.refs_6_), channel_id=1, source_target_pairs={{0,4},{4,0},{8,12},{12,8},{16,20},{20,16},{24,28},{28,24},{1,5},{5... | collective-permute-start | bytes 393224 | tf_op jit(solution)/shard_map/ppermute | solution.py:486
  69.1 3.6 %collective-permute-start.23 = (f32[8,128]{1,0:T(8,128)S(1)}, f32[8,128]{1,0:T(8,128)S(1)}, u32[]{:S(2)}, u32[]{:S(2)}) collective-permute-start(f32[8,128]{1,0:T(8,128)S(1)} %get-tuple-element.108.refs_14_), channel_id=1, source_target_pairs={{0,2},{1,3},{2,0},{3,1},{4,6},{5,7},{6,4},{7,5},{8,10},{9,11},{10,... | collective-permute-start | bytes 12296 | tf_op jit(solution)/shard_map/ppermute | solution.py:486
  76.9 8.4 %collective-permute-start.26 = (bf16[17,32,128]{2,1,0:T(8,128)(2,1)S(1)}, bf16[17,32,128]{2,1,0:T(8,128)(2,1)S(1)}, u32[]{:S(2)}, u32[]{:S(2)}) collective-permute-start(bf16[17,32,128]{2,1,0:T(8,128)(2,1)S(1)} %get-tuple-element.115.refs_2_), channel_id=1, source_target_pairs={{0,4},{4,0},{8,12},{12,8},{16,20},{20,16},{24,28},{28,24},{1,5},{5... | collective-permute-start | bytes 417800 | tf_op jit(solution)/shard_map/ppermute | solution.py:486
  79.1 6.3 %collective-permute-start.25 = (bf16[16,32,128]{2,1,0:T(8,128)(2,1)S(1)}, bf16[16,32,128]{2,1,0:T(8,128)(2,1)S(1)}, u32[]{:S(2)}, u32[]{:S(2)}) collective-permute-start(bf16[16,32,128]{2,1,0:T(8,128)(2,1)S(1)} %get-tuple-element.113), channel_id=1, source_target_pairs={{0,4},{4,0},{8,12},{12,8},{16,20},{20,16},{24,28},{28,24},{1,5},{5... | collective-permute-start | bytes 393224 | tf_op jit(solution)/shard_map/ppermute | solution.py:486
  85.4 5.8 %collective-permute-start.27 = (bf16[17,32,128]{2,1,0:T(8,128)(2,1)S(1)}, bf16[17,32,128]{2,1,0:T(8,128)(2,1)S(1)}, u32[]{:S(2)}, u32[]{:S(2)}) collective-permute-start(bf16[17,32,128]{2,1,0:T(8,128)(2,1)S(1)} %fold.12.refs_3_), channel_id=1, source_target_pairs={{0,8},{4,12},{8,0},{12,4},{16,24},{20,28},{24,16},{28,20},{1,9},{5... | collective-permute-start | bytes 417800 | tf_op jit(solution)/shard_map/ppermute | solution.py:486
  86.0 8.4 %collective-permute-start.24 = (bf16[16,32,128]{2,1,0:T(8,128)(2,1)S(1)}, bf16[16,32,128]{2,1,0:T(8,128)(2,1)S(1)}, u32[]{:S(2)}, u32[]{:S(2)}) collective-permute-start(bf16[16,32,128]{2,1,0:T(8,128)(2,1)S(1)} %get-tuple-element.111), channel_id=1, source_target_pairs={{0,8},{4,12},{8,0},{12,4},{16,24},{20,28},{24,16},{28,20},{1,9},{5... | collective-permute-start | bytes 393224 | tf_op jit(solution)/shard_map/ppermute | solution.py:486
  91.3 9.8 %collective-permute-start.30 = (bf16[17,32,128]{2,1,0:T(8,128)(2,1)S(1)}, bf16[17,32,128]{2,1,0:T(8,128)(2,1)S(1)}, u32[]{:S(2)}, u32[]{:S(2)}) collective-permute-start(bf16[17,32,128]{2,1,0:T(8,128)(2,1)S(1)} %fold.13.refs_2_.after_ref.refs_4_), channel_id=1, source_target_pairs={{0,16},{4,20},{8,24},{12,28},{16,0},{20,4},{24,8},{28,12},{1,17},{... | collective-permute-start | bytes 417800 | tf_op jit(solution)/shard_map/ppermute | solution.py:486
  93.6 7.5 %collective-permute-start.29 = (bf16[16,32,128]{2,1,0:T(8,128)(2,1)S(1)}, bf16[16,32,128]{2,1,0:T(8,128)(2,1)S(1)}, u32[]{:S(2)}, u32[]{:S(2)}) collective-permute-start(bf16[16,32,128]{2,1,0:T(8,128)(2,1)S(1)} %get-tuple-element.116), channel_id=1, source_target_pairs={{0,8},{4,12},{8,0},{12,4},{16,24},{20,28},{24,16},{28,20},{1,9},{5... | collective-permute-start | bytes 393224 | tf_op jit(solution)/shard_map/ppermute | solution.py:486
  94.4 6.7 %collective-permute-start.28 = (bf16[16,32,128]{2,1,0:T(8,128)(2,1)S(1)}, bf16[16,32,128]{2,1,0:T(8,128)(2,1)S(1)}, u32[]{:S(2)}, u32[]{:S(2)}) collective-permute-start(bf16[16,32,128]{2,1,0:T(8,128)(2,1)S(1)} %fold.14), channel_id=1, source_target_pairs={{0,4},{4,0},{8,12},{12,8},{16,20},{20,16},{24,28},{28,24},{1,5},{5... | collective-permute-start | bytes 393224 | tf_op jit(solution)/shard_map/ppermute | solution.py:486
  101.7 7.3 %collective-permute-start.34 = (bf16[16,32,128]{2,1,0:T(8,128)(2,1)S(1)}, bf16[16,32,128]{2,1,0:T(8,128)(2,1)S(1)}, u32[]{:S(2)}, u32[]{:S(2)}) collective-permute-start(bf16[16,32,128]{2,1,0:T(8,128)(2,1)S(1)} %get-tuple-element.123.panel_ref.refs_0_), channel_id=1, source_target_pairs={{0,16},{4,20},{8,24},{12,28},{16,0},{20,4},{24,8},{28,12},{1,17},{... | collective-permute-start | bytes 393224 | tf_op jit(solution)/shard_map/ppermute | solution.py:486
  101.8 10.2 %collective-permute-start.31 = (bf16[16,32,128]{2,1,0:T(8,128)(2,1)S(1)}, bf16[16,32,128]{2,1,0:T(8,128)(2,1)S(1)}, u32[]{:S(2)}, u32[]{:S(2)}) collective-permute-start(bf16[16,32,128]{2,1,0:T(8,128)(2,1)S(1)} %get-tuple-element.123.panel_ref.refs_0_), channel_id=1, source_target_pairs={{0,4},{4,0},{8,12},{12,8},{16,20},{20,16},{24,28},{28,24},{1,5},{5... | collective-permute-start | bytes 393224 | tf_op jit(solution)/shard_map/ppermute | solution.py:486
  109.0 5.0 %collective-permute-start.36 = (bf16[16,32,128]{2,1,0:T(8,128)(2,1)S(1)}, bf16[16,32,128]{2,1,0:T(8,128)(2,1)S(1)}, u32[]{:S(2)}, u32[]{:S(2)}) collective-permute-start(bf16[16,32,128]{2,1,0:T(8,128)(2,1)S(1)} %get-tuple-element.125.refs_4_), channel_id=1, source_target_pairs={{0,8},{4,12},{8,0},{12,4},{16,24},{20,28},{24,16},{28,20},{1,9},{5... | collective-permute-start | bytes 393224 | tf_op jit(solution)/shard_map/ppermute | solution.py:486
  109.6 5.8 %collective-permute-start.32 = (bf16[16,32,128]{2,1,0:T(8,128)(2,1)S(1)}, bf16[16,32,128]{2,1,0:T(8,128)(2,1)S(1)}, u32[]{:S(2)}, u32[]{:S(2)}) collective-permute-start(bf16[16,32,128]{2,1,0:T(8,128)(2,1)S(1)} %get-tuple-element.123.panel_ref.refs_0_), channel_id=1, source_target_pairs={{0,8},{4,12},{8,0},{12,4},{16,24},{20,28},{24,16},{28,20},{1,9},{5... | collective-permute-start | bytes 393224 | tf_op jit(solution)/shard_map/ppermute | solution.py:486
  111.1 5.9 %collective-permute-start.35 = (bf16[16,32,128]{2,1,0:T(8,128)(2,1)S(1)}, bf16[16,32,128]{2,1,0:T(8,128)(2,1)S(1)}, u32[]{:S(2)}, u32[]{:S(2)}) collective-permute-start(bf16[16,32,128]{2,1,0:T(8,128)(2,1)S(1)} %get-tuple-element.125.refs_4_), channel_id=1, source_target_pairs={{0,4},{4,0},{8,12},{12,8},{16,20},{20,16},{24,28},{28,24},{1,5},{5... | collective-permute-start | bytes 393224 | tf_op jit(solution)/shard_map/ppermute | solution.py:486
  112.0 5.0 %collective-permute-start.33 = (bf16[16,32,128]{2,1,0:T(8,128)(2,1)S(1)}, bf16[16,32,128]{2,1,0:T(8,128)(2,1)S(1)}, u32[]{:S(2)}, u32[]{:S(2)}) collective-permute-start(bf16[16,32,128]{2,1,0:T(8,128)(2,1)S(1)} %collective-permute-done.31.refs_1_), channel_id=1, source_target_pairs={{0,8},{4,12},{8,0},{12,4},{16,24},{20,28},{24,16},{28,20},{1,9},{5... | collective-permute-start | bytes 393224 | tf_op jit(solution)/shard_map/ppermute | solution.py:486
  114.0 5.0 %collective-permute-start.37 = (bf16[16,32,128]{2,1,0:T(8,128)(2,1)S(1)}, bf16[16,32,128]{2,1,0:T(8,128)(2,1)S(1)}, u32[]{:S(2)}, u32[]{:S(2)}) collective-permute-start(bf16[16,32,128]{2,1,0:T(8,128)(2,1)S(1)} %collective-permute-done.36.refs_6_), channel_id=1, source_target_pairs={{0,4},{4,0},{8,12},{12,8},{16,20},{20,16},{24,28},{28,24},{1,5},{5... | collective-permute-start | bytes 393224 | tf_op jit(solution)/shard_map/ppermute | solution.py:486
  114.9 1.2 collective-permute-start.38
  123.2 6.5 %collective-permute-start.41 = (bf16[17,32,128]{2,1,0:T(8,128)(2,1)S(1)}, bf16[17,32,128]{2,1,0:T(8,128)(2,1)S(1)}, u32[]{:S(2)}, u32[]{:S(2)}) collective-permute-start(bf16[17,32,128]{2,1,0:T(8,128)(2,1)S(1)} %get-tuple-element.137.refs_2_), channel_id=1, source_target_pairs={{0,4},{4,0},{8,12},{12,8},{16,20},{20,16},{24,28},{28,24},{1,5},{5... | collective-permute-start | bytes 417800 | tf_op jit(solution)/shard_map/ppermute | solution.py:486
  124.1 5.6 %collective-permute-start.40 = (bf16[16,32,128]{2,1,0:T(8,128)(2,1)S(1)}, bf16[16,32,128]{2,1,0:T(8,128)(2,1)S(1)}, u32[]{:S(2)}, u32[]{:S(2)}) collective-permute-start(bf16[16,32,128]{2,1,0:T(8,128)(2,1)S(1)} %get-tuple-element.135), channel_id=1, source_target_pairs={{0,4},{4,0},{8,12},{12,8},{16,20},{20,16},{24,28},{28,24},{1,5},{5... | collective-permute-start | bytes 393224 | tf_op jit(solution)/shard_map/ppermute | solution.py:486
  125.2 1.2 collective-permute-start.42
  129.8 7.5 %collective-permute-start.43 = (bf16[17,32,128]{2,1,0:T(8,128)(2,1)S(1)}, bf16[17,32,128]{2,1,0:T(8,128)(2,1)S(1)}, u32[]{:S(2)}, u32[]{:S(2)}) collective-permute-start(bf16[17,32,128]{2,1,0:T(8,128)(2,1)S(1)} %fold.15.refs_3_), channel_id=1, source_target_pairs={{0,8},{4,12},{8,0},{12,4},{16,24},{20,28},{24,16},{28,20},{1,9},{5... | collective-permute-start | bytes 417800 | tf_op jit(solution)/shard_map/ppermute | solution.py:486
  130.4 8.9 %collective-permute-start.39 = (bf16[16,32,128]{2,1,0:T(8,128)(2,1)S(1)}, bf16[16,32,128]{2,1,0:T(8,128)(2,1)S(1)}, u32[]{:S(2)}, u32[]{:S(2)}) collective-permute-start(bf16[16,32,128]{2,1,0:T(8,128)(2,1)S(1)} %get-tuple-element.133), channel_id=1, source_target_pairs={{0,8},{4,12},{8,0},{12,4},{16,24},{20,28},{24,16},{28,20},{1,9},{5... | collective-permute-start | bytes 393224 | tf_op jit(solution)/shard_map/ppermute | solution.py:486
  137.4 9.4 %collective-permute-start.46 = (bf16[17,32,128]{2,1,0:T(8,128)(2,1)S(1)}, bf16[17,32,128]{2,1,0:T(8,128)(2,1)S(1)}, u32[]{:S(2)}, u32[]{:S(2)}) collective-permute-start(bf16[17,32,128]{2,1,0:T(8,128)(2,1)S(1)} %get-tuple-element.139.refs_2_.after_ref.refs_4_), channel_id=1, source_target_pairs={{0,16},{4,20},{8,24},{12,28},{16,0},{20,4},{24,8},{28,12},{1,17},{... | collective-permute-start | bytes 417800 | tf_op jit(solution)/shard_map/ppermute | solution.py:486
  137.4 9.3 %collective-permute-start.45 = (bf16[16,32,128]{2,1,0:T(8,128)(2,1)S(1)}, bf16[16,32,128]{2,1,0:T(8,128)(2,1)S(1)}, u32[]{:S(2)}, u32[]{:S(2)}) collective-permute-start(bf16[16,32,128]{2,1,0:T(8,128)(2,1)S(1)} %get-tuple-element.140), channel_id=1, source_target_pairs={{0,8},{4,12},{8,0},{12,4},{16,24},{20,28},{24,16},{28,20},{1,9},{5... | collective-permute-start | bytes 393224 | tf_op jit(solution)/shard_map/ppermute | solution.py:486
  139.3 7.5 %collective-permute-start.44 = (bf16[16,32,128]{2,1,0:T(8,128)(2,1)S(1)}, bf16[16,32,128]{2,1,0:T(8,128)(2,1)S(1)}, u32[]{:S(2)}, u32[]{:S(2)}) collective-permute-start(bf16[16,32,128]{2,1,0:T(8,128)(2,1)S(1)} %fold.17), channel_id=1, source_target_pairs={{0,4},{4,0},{8,12},{12,8},{16,20},{20,16},{24,28},{28,24},{1,5},{5... | collective-permute-start | bytes 393224 | tf_op jit(solution)/shard_map/ppermute | solution.py:486
  141.9 4.8 %collective-permute-start.47 = (f32[8,128]{1,0:T(8,128)S(1)}, f32[8,128]{1,0:T(8,128)S(1)}, u32[]{:S(2)}, u32[]{:S(2)}) collective-permute-start(f32[8,128]{1,0:T(8,128)S(1)} %get-tuple-element.146.refs_9_), channel_id=1, source_target_pairs={{0,2},{1,3},{2,0},{3,1},{4,6},{5,7},{6,4},{7,5},{8,10},{9,11},{10,... | collective-permute-start | bytes 12296 | tf_op jit(solution)/shard_map/ppermute | solution.py:486

commit v8 on v7

--- a/solution.py
+++ b/solution.py
@@ -56,10 +56,10 @@
     return jnp.sum(parts.astype(jnp.float32), axis=1, keepdims=True)
 
 
-def head_kernel(group, steps, peers, late, scen_total, index_ref, *refs):
+def head_kernel(group, steps, peers, index_ref, *refs):
     panels, refs = refs[:peers], refs[peers:]
-    heads_ref, pulled_ref, flows_ref, costs_ref, risk_ref, level_ref, sum_ref, other_ref = refs[:8]
-    flows_out, bar_out, risk_out, level_out, sum_out, refs = *refs[8:13], refs[13:]
+    heads_ref, pulled_ref, flows_ref, costs_ref, risk_ref, sum_ref, other_ref = refs[:7]
+    flows_out, bar_out, sum_out, refs = *refs[7:10], refs[10:]
     kept, refs = refs[: peers // 2], refs[peers // 2 :]
     sends, (panel, terms, pulled, loss) = refs[:-4], refs[-4:]
     rows = heads_ref.shape[-1]
@@ -71,17 +71,7 @@
     def _():
         terms[...] = jnp.zeros_like(terms)
         loss[...] = jnp.zeros_like(loss)
-        risk_total = sum_ref[...] + other_ref[...]
-        if late:
-            level_new, level_bar = next_level(level_ref[...], risk_total, scen_total)
-            risk_start = jnp.maximum(risk_ref[...] - risk_step * level_bar[:1], 0.0)
-            risk_out[...] = risk_start
-            level_out[...] = level_new
-            sum_out[...] = add_rows(risk_start, sum_out.shape)
-        else:
-            risk_out[...] = risk_ref[...]
-            level_out[...] = level_ref[...]
-            sum_out[...] = risk_total
+        sum_out[...] = sum_ref[...] + other_ref[...]
         for peer in range(peers):
             panel[peer * node_blks : (peer + 1) * node_blks] = panels[peer][...]
 
@@ -89,7 +79,7 @@
     spans = [slice(member * rows, (member + 1) * rows) for member in range(group)]
     for member in range(group):
         pulled[:, spans[member]] = contract_last(panel[places[member]], heads_ref[member])
-    risk = risk_out[...]
+    risk = risk_ref[...]
     loss_sum = jnp.zeros_like(risk)
     for columns in spans:
         flows = flows_ref[:, columns]
@@ -178,7 +168,7 @@
     return jnp.sum(jnp.where(picked, values, 0.0), axis=0, keepdims=True)[:, :rows]
 
 
-def settle_kernel(count, arc_total, scen_total, kind, *refs):
+def settle_kernel(count, arc_total, scen_total, last, *refs):
     kept_ref, arrived, refs = refs[0], refs[1 : 1 + count], refs[1 + count :]
     loss_ref, base_ref, risk_ref, excess_ref, level_ref, sum_ref, other_ref = refs[:7]
     duals_out, half_out, risk_out, excess_out, level_out, sum_out = refs[7:]
@@ -186,7 +176,7 @@
     for block in range(node_blks):
         total = kept_ref[block] + pair_sum([ref[block].astype(jnp.float32) for ref in arrived])
         duals = base_ref[block] - dual_step * total
-        if kind == "last":
+        if last:
             duals_out[:, block * rows : (block + 1) * rows] = duals
         else:
             duals_out[block] = duals
@@ -198,14 +188,10 @@
     excess_new = jnp.maximum(excess - primal_step * (tail_weight - risk), 0.0)
     excess_bar = 2.0 * excess_new - excess
     risk_new = risk + risk_step * (losses - excess_bar)
-    if kind == "early":
-        risk_out[...] = risk_new
-        excess_out[...] = excess_new
-        return
     risk_total = sum_ref[...] + other_ref[...]
     level_new, level_bar = next_level(level_ref[...], risk_total, scen_total)
     risk_new = jnp.maximum(risk_new - risk_step * level_bar[:1], 0.0)
-    if kind == "last":
+    if last:
         risk_out[...] = as_row(risk_new)
         excess_out[...] = as_row(excess_new)
         level_out[...] = level_new[:1, :1]
@@ -225,7 +211,6 @@
     blocks_ref,
     duals_ref,
     demand_ref,
-    after_ref,
     out_ref,
     total,
 ):
@@ -293,7 +278,7 @@
     )(index, panel, blocks)
 
 
-def head_step(places, panels, heads, pulled, flows, costs, risk, level, sums, late, scen_total):
+def head_step(places, panels, heads, pulled, flows, costs, risk, sums):
     arc_blks, rows, _ = heads.shape
     scen_rows = flows.shape[0]
     peers = len(panels)
@@ -305,13 +290,11 @@
     sent[-1] = (node_blks + 1, scen_rows, rows)
     arcs = pl.BlockSpec((scen_rows, group * rows), lambda i, *_: (0, i))
     results = pl.pallas_call(
-        functools.partial(head_kernel, group, steps, peers, late, scen_total),
+        functools.partial(head_kernel, group, steps, peers),
         out_shape=[
             jax.ShapeDtypeStruct(flows.shape, jnp.float32),
             jax.ShapeDtypeStruct(flows.shape, jnp.bfloat16),
-            jax.ShapeDtypeStruct(risk.shape, jnp.float32),
-            jax.ShapeDtypeStruct(level.shape, jnp.float32),
-            jax.ShapeDtypeStruct(level.shape, jnp.float32),
+            jax.ShapeDtypeStruct(sums[0].shape, jnp.float32),
         ]
         + [jax.ShapeDtypeStruct(kept, jnp.float32)] * (peers // 2)
         + [jax.ShapeDtypeStruct(shape, jnp.bfloat16) for shape in sent],
@@ -325,11 +308,10 @@
                 arcs,
                 pl.BlockSpec((1, group * rows), lambda i, *_: (0, i)),
                 whole(scen_rows, rows),
-                whole(*level.shape),
-                whole(*level.shape),
-                whole(*level.shape),
+                whole(*sums[0].shape),
+                whole(*sums[0].shape),
             ],
-            out_specs=[arcs, arcs, whole(scen_rows, rows), whole(*level.shape), whole(*level.shape)]
+            out_specs=[arcs, arcs, whole(*sums[0].shape)]
             + [whole(*kept)] * (peers // 2)
             + [whole(*shape) for shape in sent],
             scratch_shapes=[
@@ -346,11 +328,11 @@
             transcendentals=0,
         ),
         name="head_step",
-    )(places, *panels, heads, pulled, flows, costs, risk, level, *sums)
+    )(places, *panels, heads, pulled, flows, costs, risk, *sums)
     half = peers // 2
-    kept = dict(zip(inner(peers), results[5 : 5 + half]))
-    sends = dict(zip(leaves(peers), results[5 + half :]))
-    return *results[:5], kept, sends
+    kept = dict(zip(inner(peers), results[3 : 3 + half]))
+    sends = dict(zip(leaves(peers), results[3 + half :]))
+    return *results[:3], kept, sends
 
 
 def small_cost(*arrays):
@@ -382,11 +364,10 @@
     return results[: len(tops)], results[len(tops) :]
 
 
-def settle(kept, arrived, loss, base, risk, excess, level, sums, arc_total, scen_total, kind):
+def settle(kept, arrived, loss, base, risk, excess, level, sums, arc_total, scen_total, last):
     node_blks, scen_rows, rows = base.shape
-    last = kind == "last"
     return pl.pallas_call(
-        functools.partial(settle_kernel, len(arrived), arc_total, scen_total, kind),
+        functools.partial(settle_kernel, len(arrived), arc_total, scen_total, last),
         out_shape=(
             jax.ShapeDtypeStruct((scen_rows, node_blks * rows) if last else base.shape, jnp.float32),
             jax.ShapeDtypeStruct(base.shape, jnp.bfloat16),
@@ -401,7 +382,7 @@
     )(kept, *arrived, loss, base, risk, excess, level, *sums)
 
 
-def local_forward(index, bar, blocks, duals, demand, after):
+def local_forward(index, bar, blocks, duals, demand):
     arc_blks, touches, rows, _ = blocks.shape
     scen_rows = bar.shape[0]
     group = GROUP
@@ -417,7 +398,6 @@
                 pl.BlockSpec((group, touches, rows, rows), lambda i, *_: (i, 0, 0, 0)),
                 whole(*duals.shape),
                 whole(*demand.shape),
-                pl.BlockSpec(memory_space=pl.ANY),
             ],
             out_specs=whole(*duals.shape),
             scratch_shapes=[pltpu.VMEM(duals.shape, jnp.float32)],
@@ -427,7 +407,7 @@
             flops=2 * scen_rows * blocks.size, bytes_accessed=2 * blocks.size, transcendentals=0
         ),
         name="local_forward",
-    )(index, bar, blocks, duals, demand, after)
+    )(index, bar, blocks, duals, demand)
 
 
 def relay(arrived, risk_sum, after):
@@ -524,12 +504,12 @@
     duals = node_duals.reshape(scen_rows, node_blks, rows).transpose(1, 0, 2)
     half = duals.astype(jnp.bfloat16)
     flows = arc_flows
-    early = [1 << bit for bit in range(1, scen_size.bit_length() - 1)][::-1]
+    strides = [1 << bit for bit in range(1, scen_size.bit_length() - 1)][::-1]
     for iteration in range(ROUNDS):
-        kind = "first" if iteration == 0 else "last" if iteration == ROUNDS - 1 else "early"
+        first, last = iteration == 0, iteration == ROUNDS - 1
         pulled, token = local_adjoint(touched, half, local_blocks)
-        panels, risk_sum = gather_panels(half, token if kind == "first" else risk_sum, (token,))
-        if kind == "first":
+        panels, risk_sum = gather_panels(half, token if first else risk_sum, (token,))
+        if first:
             risk, excess_now, level, risk_sum, places = prepare(
                 risk_duals,
                 excess,
@@ -540,35 +520,16 @@
                 (panels[net_size // 2], head_blocks, arc_flows),
             )
             places = places.reshape(-1)
-        if kind == "early":
-            for stride in early[:-1]:
-                risk_sum = risk_sum + swap(risk_sum, "scen", stride)
-            sums = (risk_sum, swap(risk_sum, "scen", early[-1]))
-        else:
-            sums = (risk_sum, swap(risk_sum, "scen", 1))
-        flows, bar, risk, level, risk_sum, kept, sends = head_step(
-            places,
-            panels,
-            head_blocks,
-            pulled,
-            flows,
-            costs,
-            risk,
-            level,
-            sums,
-            kind == "last",
-            scen_total,
+        sums = (risk_sum, swap(risk_sum, "scen", 1))
+        flows, bar, risk_sum, kept, sends = head_step(
+            places, panels, head_blocks, pulled, flows, costs, risk, sums
         )
-        after = ()
-        risk_sums = () if kind == "early" else (risk_sum,)
-        if kind == "last":
-            after = (swap(risk_sum, "scen", 1),)
-            risk_sums += after
+        base = local_forward(touched, bar, local_blocks, duals, demand)
         tops = sorted(inner(net_size), key=lambda k: (-k.bit_count(), -k))[:-1]
         groups = [(top,) for top in tops if top != 1] + [(1,)]
         loss, loss_top = sends[net_size - 1], net_size - 1
         ahead = {5: swap(sends[5], "net", last_hop(5))}
-        after += (ahead[5],)
+        after = (ahead[5], base)
         for group in groups:
             terms = []
             for top in group:
@@ -580,7 +541,7 @@
                     )
                 )
             chain = loss_top ^ last_hop(loss_top) == group[0]
-            sums = risk_sums if group[0] == net_size // 2 else ()
+            sums = (risk_sum,) if group[0] == net_size // 2 else ()
             if group == (1,):
                 after = (loss,)
             folded, passed = fold(terms, loss if chain else None, sums, after)
@@ -590,15 +551,12 @@
                 loss_top, loss = group[0], folded[0]
             if sums:
                 (risk_sum,) = passed
-        base = local_forward(touched, bar, local_blocks, duals, demand, loss)
         below = sorted(children(0, net_size))
         arrived = [swap(sends[k], "net", last_hop(k)) for k in below]
-        sums = (risk_sum, risk_sum)
-        if kind != "early":
-            for stride in early[:-1]:
-                risk_sum = risk_sum + swap(risk_sum, "scen", stride)
-            sums = (risk_sum, swap(risk_sum, "scen", early[-1]))
-        duals, half, risk, excess_now, level_next, sum_next = settle(
+        for stride in strides[:-1]:
+            risk_sum = risk_sum + swap(risk_sum, "scen", stride)
+        sums = (risk_sum, swap(risk_sum, "scen", strides[-1]))
+        duals, half, risk, excess_now, level, risk_sum = settle(
             kept[0],
             arrived,
             loss,
@@ -609,10 +567,8 @@
             sums,
             arc_total,
             scen_total,
-            kind,
+            last,
         )
-        if kind != "early":
-            level, risk_sum = level_next, sum_next
     return (flows, duals, excess_now.reshape(-1), risk.reshape(-1), level.reshape(-1))
 
 

time: 148 us -> 143 us (0.966)
  starting transfers between devices: 56.4 us -> 46 us
  waiting for transfers between devices: 47.3 us -> 53.5 us
    ppermute x48, starting transfers between devices: 56.4 us -> 46 us  [swap(): return lax.ppermute(value, axis, [(i, i ^ distance) for i in range(size)])]
    ppermute x48, waiting for transfers between devices: 47.3 us -> 53.5 us  [swap(): return lax.ppermute(value, axis, [(i, i ^ distance) for i in range(size)])]
  transfers between devices with their start and end apart: 48 -> 48, of which waited for: 24 -> 34; matrix products, arithmetic and copies ran while one was open for 0% -> 0% of each run, Pallas kernels for 16% -> 17%
where the time goes in v8:
time: 143 us
  waiting for transfers between devices  53.5 us (37%)
  starting transfers between devices  46 us (32%)
  Pallas kernels  36.8 us (26%)
  local copies, waits for them, and re-layouts  5.05 us (4%)
  between operations  1.61 us (1%)
    ppermute x48, waiting for transfers between devices, swap(): return lax.ppermute(value, axis, [(i, i ^ distance) for i in range(size)])  53.5 us
    ppermute x48, starting transfers between devices, swap(): return lax.ppermute(value, axis, [(i, i ^ distance) for i in range(size)])  46 us
    pallas_call x3, Pallas kernels, local_adjoint(): pl.pallas_call(functools.partial(local_adjoint_kernel, touches, group), o...  12.9 us
    pallas_call x3, Pallas kernels, head_step(): pl.pallas_call(functools.partial(head_kernel, group, steps, peers), out_s...  11.2 us
    pallas_call x3, Pallas kernels, local_forward(): pl.pallas_call(functools.partial(local_forward_kernel, touches, group, st...  10 us
    unnamed x26, local copies, waits for them, and re-layouts  5.01 us
  transfers between devices with their start and end apart: 48, of which 34 were waited for; matrix products, arithmetic and copies ran while one was open for 0% of the time, Pallas kernels for 17%

profile of v8, /device:TPU:0, one launch (start us, length us, event | category | flops | bytes accessed | tf_op | source)
XLA Modules:
  0.0 143.0 jit_solution(17681063797625550582)
XLA Ops:
  0.7 0.9 copy-done
  1.6 4.1 %collective-permute-start = (bf16[16,32,128]{2,1,0:T(8,128)(2,1)S(1)}, bf16[16,32,128]{2,1,0:T(8,128)(2,1)S(1)}, u32[]{:S(2)}, u32[]{:S(2)}) collective-permute-start(bf16[16,32,128]{2,1,0:T(8,128)(2,1)S(1)} %fusion.panel_ref.refs_0_), channel_id=1, source_target_pairs={{0,16},{4,20},{8,24},{12,28},{16,0},{20,4},{24,8},{28,12},{1,17},{... | collective-permute-start | bytes 393224 | tf_op jit(solution)/shard_map/ppermute | solution.py:466
  5.7 1.5 %collective-permute-start.1 = (bf16[16,32,128]{2,1,0:T(8,128)(2,1)S(1)}, bf16[16,32,128]{2,1,0:T(8,128)(2,1)S(1)}, u32[]{:S(2)}, u32[]{:S(2)}) collective-permute-start(bf16[16,32,128]{2,1,0:T(8,128)(2,1)S(1)} %fusion.panel_ref.refs_0_), channel_id=1, source_target_pairs={{0,4},{4,0},{8,12},{12,8},{16,20},{20,16},{24,28},{28,24},{1,5},{5... | collective-permute-start | bytes 393224 | tf_op jit(solution)/shard_map/ppermute | solution.py:466
  7.2 3.4 %copy-done.1 = bf16[64,4,128,128]{3,2,1,0:T(8,128)(2,1)S(1)} copy-done((bf16[64,4,128,128]{3,2,1,0:T(8,128)(2,1)S(1)}, bf16[64,4,128,128]{3,2,1,0:T(8,128)(2,1)}, u32[]{:S(2)}) %copy-start.1) | copy-done | bytes 8388632
  11.3 4.3 %local_adjoint.3 = (f32[32,8192]{1,0:T(8,128)S(1)}, f32[8,128]{1,0:T(8,128)S(1)}) custom-call(s32[4,64]{1,0:T(4,128)S(1)} %bitcast.29, bf16[16,32,128]{2,1,0:T(8,128)(2,1)S(1)} %fusion.panel_ref.refs_0_, bf16[64,4,128,128]{3,2,1,0:T(8,128)(2,1)S(1)} %copy-done.1), custom_call_target="tpu_custom_call" | custom-call | flops 268435456 | bytes 8388608 | tf_op jit(solution)/shard_map/local_adjoint/pallas_call | solution.py:255
  16.2 1.6 %collective-permute-start.5 = (bf16[16,32,128]{2,1,0:T(8,128)(2,1)S(1)}, bf16[16,32,128]{2,1,0:T(8,128)(2,1)S(1)}, u32[]{:S(2)}, u32[]{:S(2)}) collective-permute-start(bf16[16,32,128]{2,1,0:T(8,128)(2,1)S(1)} %get-tuple-element.77.refs_0_.refs_4_), channel_id=1, source_target_pairs={{0,8},{4,12},{8,0},{12,4},{16,24},{20,28},{24,16},{28,20},{1,9},{5... | collective-permute-start | bytes 393224 | tf_op jit(solution)/shard_map/ppermute | solution.py:466
  18.8 1.6 %collective-permute-start.3 = (bf16[16,32,128]{2,1,0:T(8,128)(2,1)S(1)}, bf16[16,32,128]{2,1,0:T(8,128)(2,1)S(1)}, u32[]{:S(2)}, u32[]{:S(2)}) collective-permute-start(bf16[16,32,128]{2,1,0:T(8,128)(2,1)S(1)} %collective-permute-done.1.refs_1_), channel_id=1, source_target_pairs={{0,8},{4,12},{8,0},{12,4},{16,24},{20,28},{24,16},{28,20},{1,9},{5... | collective-permute-start | bytes 393224 | tf_op jit(solution)/shard_map/ppermute | solution.py:466
  20.4 2.3 %collective-permute-done.5.refs_6_ = bf16[16,32,128]{2,1,0:T(8,128)(2,1)S(1)} collective-permute-done((bf16[16,32,128]{2,1,0:T(8,128)(2,1)S(1)}, bf16[16,32,128]{2,1,0:T(8,128)(2,1)S(1)}, u32[]{:S(2)}, u32[]{:S(2)}) %collective-permute-start.5) | collective-permute-done | bytes 131104 | tf_op jit(solution)/shard_map/ppermute | solution.py:466
  24.1 1.0 collective-permute-done.2.refs_2_
  25.2 1.3 collective-permute-done.3.refs_3_
  26.5 1.1 collective-permute-done.6.refs_7_
  27.6 3.5 %head_step.3 = (f32[32,8192]{1,0:T(8,128)S(1)}, bf16[32,8192]{1,0:T(8,128)(2,1)S(1)}, f32[8,128]{1,0:T(8,128)S(1)}, f32[16,32,128]{2,1,0:T(8,128)S(1)}, f32[16,3...) custom-call(s32[64]{0:T(128)S(1)} %bitcast.35, ...), custom_call_target="tpu_custom_call" | custom-call | flops 134217728 | bytes 7864320 | tf_op jit(solution)/shard_map/head_step/pallas_call | solution.py:292
  31.7 1.5 %collective-permute-start.10 = (bf16[17,32,128]{2,1,0:T(8,128)(2,1)S(1)}, bf16[17,32,128]{2,1,0:T(8,128)(2,1)S(1)}, u32[]{:S(2)}, u32[]{:S(2)}) collective-permute-start(bf16[17,32,128]{2,1,0:T(8,128)(2,1)S(1)} %get-tuple-element.88.refs_2_), channel_id=1, source_target_pairs={{0,4},{4,0},{8,12},{12,8},{16,20},{20,16},{24,28},{28,24},{1,5},{5... | collective-permute-start | bytes 417800 | tf_op jit(solution)/shard_map/ppermute | solution.py:466
  33.3 3.3 %local_forward.3.refs_4_.refs_5_ = f32[16,32,128]{2,1,0:T(8,128)S(1)} custom-call(s32[4,64]{1,0:T(4,128)S(1)} %bitcast.30, bf16[32,8192]{1,0:T(8,128)(2,1)S(1)} %get-tuple-element.89.bar_ref, bf16[64,4,128,128]{3,2,1,0:T(8,128)(2,1)S(1)} %bitcast.25, f32[16,32,128]{2,1,0:T(8,128)S(1)} %bitcast_bitcast_fusion.duals_ref, f32[32,2048]{1,0:T(8,128)S(1)} %copy-done.4), custom_call_target="tpu_custom_call" | custom-call | flops 268435456 | bytes 8388608 | tf_op jit(solution)/shard_map/local_forward/pallas_call | solution.py:390
  36.6 1.0 collective-permute-done.10.refs_1_
  37.8 1.6 %collective-permute-start.11 = (bf16[17,32,128]{2,1,0:T(8,128)(2,1)S(1)}, bf16[17,32,128]{2,1,0:T(8,128)(2,1)S(1)}, u32[]{:S(2)}, u32[]{:S(2)}) collective-permute-start(bf16[17,32,128]{2,1,0:T(8,128)(2,1)S(1)} %fold.9.refs_3_), channel_id=1, source_target_pairs={{0,8},{4,12},{8,0},{12,4},{16,24},{20,28},{24,16},{28,20},{1,9},{5... | collective-permute-start | bytes 417800 | tf_op jit(solution)/shard_map/ppermute | solution.py:466
  39.9 5.9 %collective-permute-done.11.refs_2_ = bf16[17,32,128]{2,1,0:T(8,128)(2,1)S(1)} collective-permute-done((bf16[17,32,128]{2,1,0:T(8,128)(2,1)S(1)}, bf16[17,32,128]{2,1,0:T(8,128)(2,1)S(1)}, u32[]{:S(2)}, u32[]{:S(2)}) %collective-permute-start.11) | collective-permute-done | bytes 139296 | tf_op jit(solution)/shard_map/ppermute | solution.py:466
  46.2 0.9 collective-permute-done.8.refs_1_
  47.2 1.3 collective-permute-start.12
  48.5 1.5 %collective-permute-start.15 = (f32[8,128]{1,0:T(8,128)S(1)}, f32[8,128]{1,0:T(8,128)S(1)}, u32[]{:S(2)}, u32[]{:S(2)}) collective-permute-start(f32[8,128]{1,0:T(8,128)S(1)} %get-tuple-element.95.refs_9_), channel_id=1, source_target_pairs={{0,2},{1,3},{2,0},{3,1},{4,6},{5,7},{6,4},{7,5},{8,10},{9,11},{10,... | collective-permute-start | bytes 12296 | tf_op jit(solution)/shard_map/ppermute | solution.py:466
  50.1 1.3 collective-permute-done.13.refs_2_
  51.4 0.8 collective-permute-done.15.refs_10_
  52.8 2.6 %collective-permute-done.14.refs_3_ = bf16[17,32,128]{2,1,0:T(8,128)(2,1)S(1)} collective-permute-done((bf16[17,32,128]{2,1,0:T(8,128)(2,1)S(1)}, bf16[17,32,128]{2,1,0:T(8,128)(2,1)S(1)}, u32[]{:S(2)}, u32[]{:S(2)}) %collective-permute-start.14) | collective-permute-done | bytes 139296 | tf_op jit(solution)/shard_map/ppermute | solution.py:466
  55.7 1.3 collective-permute-start.16
  57.0 4.3 %local_adjoint.4 = (f32[32,8192]{1,0:T(8,128)S(1)}, f32[8,128]{1,0:T(8,128)S(1)}) custom-call(s32[4,64]{1,0:T(4,128)S(1)} %bitcast.31, bf16[16,32,128]{2,1,0:T(8,128)(2,1)S(1)} %get-tuple-element.96.panel_ref.refs_0_, bf16[64,4,128,128]{3,2,1,0:T(8,128)(2,1)S(1)} %bitcast.25), custom_call_target="tpu_custom_call" | custom-call | flops 268435456 | bytes 8388608 | tf_op jit(solution)/shard_map/local_adjoint/pallas_call | solution.py:255
  61.3 0.9 collective-permute-done.19.arrived_ref
  62.3 2.0 %collective-permute-start.17 = (bf16[16,32,128]{2,1,0:T(8,128)(2,1)S(1)}, bf16[16,32,128]{2,1,0:T(8,128)(2,1)S(1)}, u32[]{:S(2)}, u32[]{:S(2)}) collective-permute-start(bf16[16,32,128]{2,1,0:T(8,128)(2,1)S(1)} %get-tuple-element.96.panel_ref.refs_0_), channel_id=1, source_target_pairs={{0,8},{4,12},{8,0},{12,4},{16,24},{20,28},{24,16},{28,20},{1,9},{5... | collective-permute-start | bytes 393224 | tf_op jit(solution)/shard_map/ppermute | solution.py:466
  64.3 1.1 collective-permute-start.18
  65.4 1.8 %collective-permute-done.21.refs_6_ = bf16[16,32,128]{2,1,0:T(8,128)(2,1)S(1)} collective-permute-done((bf16[16,32,128]{2,1,0:T(8,128)(2,1)S(1)}, bf16[16,32,128]{2,1,0:T(8,128)(2,1)S(1)}, u32[]{:S(2)}, u32[]{:S(2)}) %collective-permute-start.21) | collective-permute-done | bytes 131104 | tf_op jit(solution)/shard_map/ppermute | solution.py:466
  67.3 1.4 collective-permute-done.17.refs_2_
  68.7 1.4 collective-permute-done.18.refs_3_
  70.1 2.2 %collective-permute-done.22.refs_7_ = bf16[16,32,128]{2,1,0:T(8,128)(2,1)S(1)} collective-permute-done((bf16[16,32,128]{2,1,0:T(8,128)(2,1)S(1)}, bf16[16,32,128]{2,1,0:T(8,128)(2,1)S(1)}, u32[]{:S(2)}, u32[]{:S(2)}) %collective-permute-start.22) | collective-permute-done | bytes 131104 | tf_op jit(solution)/shard_map/ppermute | solution.py:466
  72.2 3.5 %head_step.4 = (f32[32,8192]{1,0:T(8,128)S(1)}, bf16[32,8192]{1,0:T(8,128)(2,1)S(1)}, f32[8,128]{1,0:T(8,128)S(1)}, f32[16,32,128]{2,1,0:T(8,128)S(1)}, f32[16,3...) custom-call(s32[64]{0:T(128)S(1)} %bitcast.36, ...), custom_call_target="tpu_custom_call" | custom-call | flops 134217728 | bytes 7864320 | tf_op jit(solution)/shard_map/head_step/pallas_call | solution.py:292
  75.8 2.0 %collective-permute-start.25 = (bf16[16,32,128]{2,1,0:T(8,128)(2,1)S(1)}, bf16[16,32,128]{2,1,0:T(8,128)(2,1)S(1)}, u32[]{:S(2)}, u32[]{:S(2)}) collective-permute-start(bf16[16,32,128]{2,1,0:T(8,128)(2,1)S(1)} %get-tuple-element.108), channel_id=1, source_target_pairs={{0,4},{4,0},{8,12},{12,8},{16,20},{20,16},{24,28},{28,24},{1,5},{5... | collective-permute-start | bytes 393224 | tf_op jit(solution)/shard_map/ppermute | solution.py:466
  77.8 3.3 %local_forward.4.refs_4_.refs_5_ = f32[16,32,128]{2,1,0:T(8,128)S(1)} custom-call(s32[4,64]{1,0:T(4,128)S(1)} %bitcast.32, bf16[32,8192]{1,0:T(8,128)(2,1)S(1)} %get-tuple-element.111.bar_ref, bf16[64,4,128,128]{3,2,1,0:T(8,128)(2,1)S(1)} %bitcast.25, f32[16,32,128]{2,1,0:T(8,128)S(1)} %get-tuple-element.112.duals_ref, f32[32,2048]{1,0:T(8,128)S(1)} %copy-done.4), custom_call_target="tpu_custom_call" | custom-call | flops 268435456 | bytes 8388608 | tf_op jit(solution)/shard_map/local_forward/pallas_call | solution.py:390
  81.2 1.1 collective-permute-done.25.refs_3_.refs_1_
  82.5 2.0 %collective-permute-start.24 = (bf16[16,32,128]{2,1,0:T(8,128)(2,1)S(1)}, bf16[16,32,128]{2,1,0:T(8,128)(2,1)S(1)}, u32[]{:S(2)}, u32[]{:S(2)}) collective-permute-start(bf16[16,32,128]{2,1,0:T(8,128)(2,1)S(1)} %get-tuple-element.106), channel_id=1, source_target_pairs={{0,8},{4,12},{8,0},{12,4},{16,24},{20,28},{24,16},{28,20},{1,9},{5... | collective-permute-start | bytes 393224 | tf_op jit(solution)/shard_map/ppermute | solution.py:466
  84.5 4.9 %collective-permute-done.27.refs_2_ = bf16[17,32,128]{2,1,0:T(8,128)(2,1)S(1)} collective-permute-done((bf16[17,32,128]{2,1,0:T(8,128)(2,1)S(1)}, bf16[17,32,128]{2,1,0:T(8,128)(2,1)S(1)}, u32[]{:S(2)}, u32[]{:S(2)}) %collective-permute-start.27) | collective-permute-done | bytes 139296 | tf_op jit(solution)/shard_map/ppermute | solution.py:466
  89.5 1.0 collective-permute-start.30
  90.5 1.7 %collective-permute-start.29 = (bf16[16,32,128]{2,1,0:T(8,128)(2,1)S(1)}, bf16[16,32,128]{2,1,0:T(8,128)(2,1)S(1)}, u32[]{:S(2)}, u32[]{:S(2)}) collective-permute-start(bf16[16,32,128]{2,1,0:T(8,128)(2,1)S(1)} %get-tuple-element.115), channel_id=1, source_target_pairs={{0,8},{4,12},{8,0},{12,4},{16,24},{20,28},{24,16},{28,20},{1,9},{5... | collective-permute-start | bytes 393224 | tf_op jit(solution)/shard_map/ppermute | solution.py:466
  92.2 0.8 collective-permute-start.28
  93.0 1.2 collective-permute-start.31
  94.2 1.9 %collective-permute-done.29.refs_2_ = bf16[16,32,128]{2,1,0:T(8,128)(2,1)S(1)} collective-permute-done((bf16[16,32,128]{2,1,0:T(8,128)(2,1)S(1)}, bf16[16,32,128]{2,1,0:T(8,128)(2,1)S(1)}, u32[]{:S(2)}, u32[]{:S(2)}) %collective-permute-start.29) | collective-permute-done | bytes 131104 | tf_op jit(solution)/shard_map/ppermute | solution.py:466
  97.3 1.5 %collective-permute-done.30.refs_3_ = bf16[17,32,128]{2,1,0:T(8,128)(2,1)S(1)} collective-permute-done((bf16[17,32,128]{2,1,0:T(8,128)(2,1)S(1)}, bf16[17,32,128]{2,1,0:T(8,128)(2,1)S(1)}, u32[]{:S(2)}, u32[]{:S(2)}) %collective-permute-start.30) | collective-permute-done | bytes 139296 | tf_op jit(solution)/shard_map/ppermute | solution.py:466
  99.0 1.3 collective-permute-start.32
  100.3 4.3 %local_adjoint.5 = (f32[32,8192]{1,0:T(8,128)S(1)}, f32[8,128]{1,0:T(8,128)S(1)}) custom-call(s32[4,64]{1,0:T(4,128)S(1)} %bitcast.33, bf16[16,32,128]{2,1,0:T(8,128)(2,1)S(1)} %get-tuple-element.119.panel_ref.refs_0_, bf16[64,4,128,128]{3,2,1,0:T(8,128)(2,1)S(1)} %bitcast.25), custom_call_target="tpu_custom_call" | custom-call | flops 268435456 | bytes 8388608 | tf_op jit(solution)/shard_map/local_adjoint/pallas_call | solution.py:255
  104.6 1.7 %collective-permute-done.35.arrived_ref = bf16[16,32,128]{2,1,0:T(8,128)(2,1)S(1)} collective-permute-done((bf16[16,32,128]{2,1,0:T(8,128)(2,1)S(1)}, bf16[16,32,128]{2,1,0:T(8,128)(2,1)S(1)}, u32[]{:S(2)}, u32[]{:S(2)}) %collective-permute-start.35) | collective-permute-done | bytes 131104 | tf_op jit(solution)/shard_map/ppermute | solution.py:466
  106.3 1.5 %collective-permute-start.37 = (bf16[16,32,128]{2,1,0:T(8,128)(2,1)S(1)}, bf16[16,32,128]{2,1,0:T(8,128)(2,1)S(1)}, u32[]{:S(2)}, u32[]{:S(2)}) collective-permute-start(bf16[16,32,128]{2,1,0:T(8,128)(2,1)S(1)} %get-tuple-element.122.refs_4_), channel_id=1, source_target_pairs={{0,8},{4,12},{8,0},{12,4},{16,24},{20,28},{24,16},{28,20},{1,9},{5... | collective-permute-start | bytes 393224 | tf_op jit(solution)/shard_map/ppermute | solution.py:466
  109.1 1.7 %collective-permute-start.34 = (bf16[16,32,128]{2,1,0:T(8,128)(2,1)S(1)}, bf16[16,32,128]{2,1,0:T(8,128)(2,1)S(1)}, u32[]{:S(2)}, u32[]{:S(2)}) collective-permute-start(bf16[16,32,128]{2,1,0:T(8,128)(2,1)S(1)} %collective-permute-done.32.refs_1_), channel_id=1, source_target_pairs={{0,8},{4,12},{8,0},{12,4},{16,24},{20,28},{24,16},{28,20},{1,9},{5... | collective-permute-start | bytes 393224 | tf_op jit(solution)/shard_map/ppermute | solution.py:466
  112.0 0.8 collective-permute-done.33.refs_2_
  113.2 1.0 collective-permute-done.34.refs_3_
  114.2 2.1 %collective-permute-done.38.refs_7_ = bf16[16,32,128]{2,1,0:T(8,128)(2,1)S(1)} collective-permute-done((bf16[16,32,128]{2,1,0:T(8,128)(2,1)S(1)}, bf16[16,32,128]{2,1,0:T(8,128)(2,1)S(1)}, u32[]{:S(2)}, u32[]{:S(2)}) %collective-permute-start.38) | collective-permute-done | bytes 131104 | tf_op jit(solution)/shard_map/ppermute | solution.py:466
  116.3 4.2 %head_step.5 = (f32[32,8192]{1,0:T(8,128)}, bf16[32,8192]{1,0:T(8,128)(2,1)S(1)}, f32[8,128]{1,0:T(8,128)S(1)}, f32[16,32,128]{2,1,0:T(8,128)S(1)}, f32[16,32,12...) custom-call(s32[64]{0:T(128)S(1)} %bitcast.37, ...), custom_call_target="tpu_custom_call" | custom-call | flops 134217728 | bytes 7864320 | tf_op jit(solution)/shard_map/head_step/pallas_call | solution.py:292
  121.1 1.4 collective-permute-start.41
  122.5 3.3 %local_forward.5.refs_4_.refs_5_ = f32[16,32,128]{2,1,0:T(8,128)S(1)} custom-call(s32[4,64]{1,0:T(4,128)S(1)} %bitcast.34, bf16[32,8192]{1,0:T(8,128)(2,1)S(1)} %get-tuple-element.135.bar_ref, bf16[64,4,128,128]{3,2,1,0:T(8,128)(2,1)S(1)} %bitcast.25, f32[16,32,128]{2,1,0:T(8,128)S(1)} %get-tuple-element.136.duals_ref, f32[32,2048]{1,0:T(8,128)S(1)} %copy-done.4), custom_call_target="tpu_custom_call" | custom-call | flops 268435456 | bytes 8388608 | tf_op jit(solution)/shard_map/local_forward/pallas_call | solution.py:390
  125.9 1.1 collective-permute-done.41.refs_3_.refs_1_
  127.1 1.5 %collective-permute-start.43 = (bf16[17,32,128]{2,1,0:T(8,128)(2,1)S(1)}, bf16[17,32,128]{2,1,0:T(8,128)(2,1)S(1)}, u32[]{:S(2)}, u32[]{:S(2)}) collective-permute-start(bf16[17,32,128]{2,1,0:T(8,128)(2,1)S(1)} %fold.15.refs_3_), channel_id=1, source_target_pairs={{0,8},{4,12},{8,0},{12,4},{16,24},{20,28},{24,16},{28,20},{1,9},{5... | collective-permute-start | bytes 417800 | tf_op jit(solution)/shard_map/ppermute | solution.py:466
  129.1 5.9 %collective-permute-done.43.refs_2_ = bf16[17,32,128]{2,1,0:T(8,128)(2,1)S(1)} collective-permute-done((bf16[17,32,128]{2,1,0:T(8,128)(2,1)S(1)}, bf16[17,32,128]{2,1,0:T(8,128)(2,1)S(1)}, u32[]{:S(2)}, u32[]{:S(2)}) %collective-permute-start.43) | collective-permute-done | bytes 139296 | tf_op jit(solution)/shard_map/ppermute | solution.py:466
  135.3 1.7 %collective-permute-start.45 = (bf16[16,32,128]{2,1,0:T(8,128)(2,1)S(1)}, bf16[16,32,128]{2,1,0:T(8,128)(2,1)S(1)}, u32[]{:S(2)}, u32[]{:S(2)}) collective-permute-start(bf16[16,32,128]{2,1,0:T(8,128)(2,1)S(1)} %get-tuple-element.139), channel_id=1, source_target_pairs={{0,8},{4,12},{8,0},{12,4},{16,24},{20,28},{24,16},{28,20},{1,9},{5... | collective-permute-start | bytes 393224 | tf_op jit(solution)/shard_map/ppermute | solution.py:466
  137.0 1.5 %collective-permute-start.44 = (bf16[16,32,128]{2,1,0:T(8,128)(2,1)S(1)}, bf16[16,32,128]{2,1,0:T(8,128)(2,1)S(1)}, u32[]{:S(2)}, u32[]{:S(2)}) collective-permute-start(bf16[16,32,128]{2,1,0:T(8,128)(2,1)S(1)} %fold.17), channel_id=1, source_target_pairs={{0,4},{4,0},{8,12},{12,8},{16,20},{20,16},{24,28},{28,24},{1,5},{5... | collective-permute-start | bytes 393224 | tf_op jit(solution)/shard_map/ppermute | solution.py:466
  138.5 1.1 collective-permute-start.47
  139.6 0.8 collective-permute-done.45.refs_2_
  140.4 1.7 %collective-permute-done.47.refs_10_ = f32[8,128]{1,0:T(8,128)S(1)} collective-permute-done((f32[8,128]{1,0:T(8,128)S(1)}, f32[8,128]{1,0:T(8,128)S(1)}, u32[]{:S(2)}, u32[]{:S(2)}) %collective-permute-start.47) | collective-permute-done | bytes 4128 | tf_op jit(solution)/shard_map/ppermute | solution.py:466
  142.1 0.8 settle.5
  (86 shorter events, 12.3 us)
Async XLA Ops:
  0.6 1.0 copy-start
  0.6 23.2 %copy-start.10 = (s32[64]{0:T(128)S(1)}, s32[64]{0:T(128)}, u32[]{:S(2)}) copy-start(s32[64]{0:T(128)} %param.21) | copy-start | bytes 772
  0.7 23.2 %copy-start.8 = (f32[32]{0:T(128)S(1)}, f32[32]{0:T(128)}, u32[]{:S(2)}) copy-start(f32[32]{0:T(128)} %param.15) | copy-start | bytes 388
  0.7 23.2 %copy-start.9 = (f32[32]{0:T(128)S(1)}, f32[32]{0:T(128)}, u32[]{:S(2)}) copy-start(f32[32]{0:T(128)} %param.14) | copy-start | bytes 388
  0.7 26.9 %copy-start.5 = (f32[8192]{0:T(1024)S(1)}, f32[8192]{0:T(1024)}, u32[]{:S(2)}) copy-start(f32[8192]{0:T(1024)} %param.17) | copy-start | bytes 98308
  1.6 14.0 %collective-permute-start = (bf16[16,32,128]{2,1,0:T(8,128)(2,1)S(1)}, bf16[16,32,128]{2,1,0:T(8,128)(2,1)S(1)}, u32[]{:S(2)}, u32[]{:S(2)}) collective-permute-start(bf16[16,32,128]{2,1,0:T(8,128)(2,1)S(1)} %fusion.panel_ref.refs_0_), channel_id=1, source_target_pairs={{0,16},{4,20},{8,24},{12,28},{16,0},{20,4},{24,8},{28,12},{1,17},{... | collective-permute-start | bytes 393224 | tf_op jit(solution)/shard_map/ppermute | solution.py:466
  5.7 13.1 %collective-permute-start.1 = (bf16[16,32,128]{2,1,0:T(8,128)(2,1)S(1)}, bf16[16,32,128]{2,1,0:T(8,128)(2,1)S(1)}, u32[]{:S(2)}, u32[]{:S(2)}) collective-permute-start(bf16[16,32,128]{2,1,0:T(8,128)(2,1)S(1)} %fusion.panel_ref.refs_0_), channel_id=1, source_target_pairs={{0,4},{4,0},{8,12},{12,8},{16,20},{20,16},{24,28},{28,24},{1,5},{5... | collective-permute-start | bytes 393224 | tf_op jit(solution)/shard_map/ppermute | solution.py:466
  7.2 3.4 %copy-start.1 = (bf16[64,4,128,128]{3,2,1,0:T(8,128)(2,1)S(1)}, bf16[64,4,128,128]{3,2,1,0:T(8,128)(2,1)}, u32[]{:S(2)}) copy-start(bf16[64,4,128,128]{3,2,1,0:T(8,128)(2,1)} %blocks_ref.11) | copy-start | bytes 25165828
  10.6 0.7 copy-start.6
  11.3 12.6 %copy-start.2 = (bf16[64,128,128]{2,1,0:T(8,128)(2,1)S(1)}, bf16[64,128,128]{2,1,0:T(8,128)(2,1)}, u32[]{:S(2)}) copy-start(bf16[64,128,128]{2,1,0:T(8,128)(2,1)} %refs_8_.5) | copy-start | bytes 6291460
  11.3 12.6 %copy-start.3 = (f32[32,8192]{1,0:T(8,128)S(1)}, f32[32,8192]{1,0:T(8,128)}, u32[]{:S(2)}) copy-start(f32[32,8192]{1,0:T(8,128)} %refs_10_.1) | copy-start | bytes 3145732
  11.3 22.0 %slice-start = ((s8[8388608]{0:T(1024)(128)(4,1)}), s8[4194304]{0:T(1024)(128)(4,1)S(1)}, s32[]{:S(2)}) async-start(s8[8388608]{0:T(1024)(128)(4,1)} %bitcast.24), calls=%async_computation | async-start | bytes 8388608
  11.3 22.0 %copy-start.4 = (f32[32,2048]{1,0:T(8,128)S(1)}, f32[32,2048]{1,0:T(8,128)}, u32[]{:S(2)}) copy-start(f32[32,2048]{1,0:T(8,128)} %demand_ref.5) | copy-start | bytes 786436
  16.2 6.4 %collective-permute-start.5 = (bf16[16,32,128]{2,1,0:T(8,128)(2,1)S(1)}, bf16[16,32,128]{2,1,0:T(8,128)(2,1)S(1)}, u32[]{:S(2)}, u32[]{:S(2)}) collective-permute-start(bf16[16,32,128]{2,1,0:T(8,128)(2,1)S(1)} %get-tuple-element.77.refs_0_.refs_4_), channel_id=1, source_target_pairs={{0,8},{4,12},{8,0},{12,4},{16,24},{20,28},{24,16},{28,20},{1,9},{5... | collective-permute-start | bytes 393224 | tf_op jit(solution)/shard_map/ppermute | solution.py:466
  17.8 7.3 %collective-permute-start.2 = (bf16[16,32,128]{2,1,0:T(8,128)(2,1)S(1)}, bf16[16,32,128]{2,1,0:T(8,128)(2,1)S(1)}, u32[]{:S(2)}, u32[]{:S(2)}) collective-permute-start(bf16[16,32,128]{2,1,0:T(8,128)(2,1)S(1)} %fusion.panel_ref.refs_0_), channel_id=1, source_target_pairs={{0,8},{4,12},{8,0},{12,4},{16,24},{20,28},{24,16},{28,20},{1,9},{5... | collective-permute-start | bytes 393224 | tf_op jit(solution)/shard_map/ppermute | solution.py:466
  18.2 8.3 %collective-permute-start.4 = (bf16[16,32,128]{2,1,0:T(8,128)(2,1)S(1)}, bf16[16,32,128]{2,1,0:T(8,128)(2,1)S(1)}, u32[]{:S(2)}, u32[]{:S(2)}) collective-permute-start(bf16[16,32,128]{2,1,0:T(8,128)(2,1)S(1)} %get-tuple-element.77.refs_0_.refs_4_), channel_id=1, source_target_pairs={{0,4},{4,0},{8,12},{12,8},{16,20},{20,16},{24,28},{28,24},{1,5},{5... | collective-permute-start | bytes 393224 | tf_op jit(solution)/shard_map/ppermute | solution.py:466
  18.8 7.7 %collective-permute-start.3 = (bf16[16,32,128]{2,1,0:T(8,128)(2,1)S(1)}, bf16[16,32,128]{2,1,0:T(8,128)(2,1)S(1)}, u32[]{:S(2)}, u32[]{:S(2)}) collective-permute-start(bf16[16,32,128]{2,1,0:T(8,128)(2,1)S(1)} %collective-permute-done.1.refs_1_), channel_id=1, source_target_pairs={{0,8},{4,12},{8,0},{12,4},{16,24},{20,28},{24,16},{28,20},{1,9},{5... | collective-permute-start | bytes 393224 | tf_op jit(solution)/shard_map/ppermute | solution.py:466
  22.6 5.0 %collective-permute-start.6 = (bf16[16,32,128]{2,1,0:T(8,128)(2,1)S(1)}, bf16[16,32,128]{2,1,0:T(8,128)(2,1)S(1)}, u32[]{:S(2)}, u32[]{:S(2)}) collective-permute-start(bf16[16,32,128]{2,1,0:T(8,128)(2,1)S(1)} %collective-permute-done.5.refs_6_), channel_id=1, source_target_pairs={{0,4},{4,0},{8,12},{12,8},{16,20},{20,16},{24,28},{28,24},{1,5},{5... | collective-permute-start | bytes 393224 | tf_op jit(solution)/shard_map/ppermute | solution.py:466
  23.9 9.4 %slice-start.1 = ((s8[8388608]{0:T(1024)(128)(4,1)}), s8[4194304]{0:T(1024)(128)(4,1)S(1)}, s32[]{:S(2)}) async-start(s8[8388608]{0:T(1024)(128)(4,1)} %bitcast.24), calls=%async_computation.1 | async-start | bytes 8388608
  24.0 1.2 collective-permute-start.7
  27.6 29.4 %copy-start.7 = (s32[64,4]{0,1:T(4,128)S(1)}, s32[64,4]{0,1:T(4,128)}, u32[]{:S(2)}) copy-start(s32[64,4]{0,1:T(4,128)} %param.20) | copy-start | bytes 3076
  31.1 5.5 %collective-permute-start.9 = (bf16[16,32,128]{2,1,0:T(8,128)(2,1)S(1)}, bf16[16,32,128]{2,1,0:T(8,128)(2,1)S(1)}, u32[]{:S(2)}, u32[]{:S(2)}) collective-permute-start(bf16[16,32,128]{2,1,0:T(8,128)(2,1)S(1)} %get-tuple-element.86), channel_id=1, source_target_pairs={{0,4},{4,0},{8,12},{12,8},{16,20},{20,16},{24,28},{28,24},{1,5},{5... | collective-permute-start | bytes 393224 | tf_op jit(solution)/shard_map/ppermute | solution.py:466
  31.7 5.9 %collective-permute-start.10 = (bf16[17,32,128]{2,1,0:T(8,128)(2,1)S(1)}, bf16[17,32,128]{2,1,0:T(8,128)(2,1)S(1)}, u32[]{:S(2)}, u32[]{:S(2)}) collective-permute-start(bf16[17,32,128]{2,1,0:T(8,128)(2,1)S(1)} %get-tuple-element.88.refs_2_), channel_id=1, source_target_pairs={{0,4},{4,0},{8,12},{12,8},{16,20},{20,16},{24,28},{28,24},{1,5},{5... | collective-permute-start | bytes 417800 | tf_op jit(solution)/shard_map/ppermute | solution.py:466
  37.8 8.0 %collective-permute-start.11 = (bf16[17,32,128]{2,1,0:T(8,128)(2,1)S(1)}, bf16[17,32,128]{2,1,0:T(8,128)(2,1)S(1)}, u32[]{:S(2)}, u32[]{:S(2)}) collective-permute-start(bf16[17,32,128]{2,1,0:T(8,128)(2,1)S(1)} %fold.9.refs_3_), channel_id=1, source_target_pairs={{0,8},{4,12},{8,0},{12,4},{16,24},{20,28},{24,16},{28,20},{1,9},{5... | collective-permute-start | bytes 417800 | tf_op jit(solution)/shard_map/ppermute | solution.py:466
  39.4 7.8 %collective-permute-start.8 = (bf16[16,32,128]{2,1,0:T(8,128)(2,1)S(1)}, bf16[16,32,128]{2,1,0:T(8,128)(2,1)S(1)}, u32[]{:S(2)}, u32[]{:S(2)}) collective-permute-start(bf16[16,32,128]{2,1,0:T(8,128)(2,1)S(1)} %get-tuple-element.84), channel_id=1, source_target_pairs={{0,8},{4,12},{8,0},{12,4},{16,24},{20,28},{24,16},{28,20},{1,9},{5... | collective-permute-start | bytes 393224 | tf_op jit(solution)/shard_map/ppermute | solution.py:466
  45.9 9.6 %collective-permute-start.14 = (bf16[17,32,128]{2,1,0:T(8,128)(2,1)S(1)}, bf16[17,32,128]{2,1,0:T(8,128)(2,1)S(1)}, u32[]{:S(2)}, u32[]{:S(2)}) collective-permute-start(bf16[17,32,128]{2,1,0:T(8,128)(2,1)S(1)} %get-tuple-element.91.refs_2_.refs_4_), channel_id=1, source_target_pairs={{0,16},{4,20},{8,24},{12,28},{16,0},{20,4},{24,8},{28,12},{1,17},{... | collective-permute-start | bytes 417800 | tf_op jit(solution)/shard_map/ppermute | solution.py:466
  45.9 5.4 %collective-permute-start.13 = (bf16[16,32,128]{2,1,0:T(8,128)(2,1)S(1)}, bf16[16,32,128]{2,1,0:T(8,128)(2,1)S(1)}, u32[]{:S(2)}, u32[]{:S(2)}) collective-permute-start(bf16[16,32,128]{2,1,0:T(8,128)(2,1)S(1)} %get-tuple-element.92), channel_id=1, source_target_pairs={{0,8},{4,12},{8,0},{12,4},{16,24},{20,28},{24,16},{28,20},{1,9},{5... | collective-permute-start | bytes 393224 | tf_op jit(solution)/shard_map/ppermute | solution.py:466
  47.2 5.6 %collective-permute-start.12 = (bf16[16,32,128]{2,1,0:T(8,128)(2,1)S(1)}, bf16[16,32,128]{2,1,0:T(8,128)(2,1)S(1)}, u32[]{:S(2)}, u32[]{:S(2)}) collective-permute-start(bf16[16,32,128]{2,1,0:T(8,128)(2,1)S(1)} %fold.11), channel_id=1, source_target_pairs={{0,4},{4,0},{8,12},{12,8},{16,20},{20,16},{24,28},{28,24},{1,5},{5... | collective-permute-start | bytes 393224 | tf_op jit(solution)/shard_map/ppermute | solution.py:466
  48.5 3.6 %collective-permute-start.15 = (f32[8,128]{1,0:T(8,128)S(1)}, f32[8,128]{1,0:T(8,128)S(1)}, u32[]{:S(2)}, u32[]{:S(2)}) collective-permute-start(f32[8,128]{1,0:T(8,128)S(1)} %get-tuple-element.95.refs_9_), channel_id=1, source_target_pairs={{0,2},{1,3},{2,0},{3,1},{4,6},{5,7},{6,4},{7,5},{8,10},{9,11},{10,... | collective-permute-start | bytes 12296 | tf_op jit(solution)/shard_map/ppermute | solution.py:466
  55.6 6.6 %collective-permute-start.19 = (bf16[16,32,128]{2,1,0:T(8,128)(2,1)S(1)}, bf16[16,32,128]{2,1,0:T(8,128)(2,1)S(1)}, u32[]{:S(2)}, u32[]{:S(2)}) collective-permute-start(bf16[16,32,128]{2,1,0:T(8,128)(2,1)S(1)} %get-tuple-element.96.panel_ref.refs_0_), channel_id=1, source_target_pairs={{0,16},{4,20},{8,24},{12,28},{16,0},{20,4},{24,8},{28,12},{1,17},{... | collective-permute-start | bytes 393224 | tf_op jit(solution)/shard_map/ppermute | solution.py:466
  55.7 8.6 %collective-permute-start.16 = (bf16[16,32,128]{2,1,0:T(8,128)(2,1)S(1)}, bf16[16,32,128]{2,1,0:T(8,128)(2,1)S(1)}, u32[]{:S(2)}, u32[]{:S(2)}) collective-permute-start(bf16[16,32,128]{2,1,0:T(8,128)(2,1)S(1)} %get-tuple-element.96.panel_ref.refs_0_), channel_id=1, source_target_pairs={{0,4},{4,0},{8,12},{12,8},{16,20},{20,16},{24,28},{28,24},{1,5},{5... | collective-permute-start | bytes 393224 | tf_op jit(solution)/shard_map/ppermute | solution.py:466
  62.2 5.0 %collective-permute-start.21 = (bf16[16,32,128]{2,1,0:T(8,128)(2,1)S(1)}, bf16[16,32,128]{2,1,0:T(8,128)(2,1)S(1)}, u32[]{:S(2)}, u32[]{:S(2)}) collective-permute-start(bf16[16,32,128]{2,1,0:T(8,128)(2,1)S(1)} %get-tuple-element.99.refs_4_), channel_id=1, source_target_pairs={{0,8},{4,12},{8,0},{12,4},{16,24},{20,28},{24,16},{28,20},{1,9},{5... | collective-permute-start | bytes 393224 | tf_op jit(solution)/shard_map/ppermute | solution.py:466
  62.3 6.4 %collective-permute-start.17 = (bf16[16,32,128]{2,1,0:T(8,128)(2,1)S(1)}, bf16[16,32,128]{2,1,0:T(8,128)(2,1)S(1)}, u32[]{:S(2)}, u32[]{:S(2)}) collective-permute-start(bf16[16,32,128]{2,1,0:T(8,128)(2,1)S(1)} %get-tuple-element.96.panel_ref.refs_0_), channel_id=1, source_target_pairs={{0,8},{4,12},{8,0},{12,4},{16,24},{20,28},{24,16},{28,20},{1,9},{5... | collective-permute-start | bytes 393224 | tf_op jit(solution)/shard_map/ppermute | solution.py:466
  64.3 5.8 %collective-permute-start.20 = (bf16[16,32,128]{2,1,0:T(8,128)(2,1)S(1)}, bf16[16,32,128]{2,1,0:T(8,128)(2,1)S(1)}, u32[]{:S(2)}, u32[]{:S(2)}) collective-permute-start(bf16[16,32,128]{2,1,0:T(8,128)(2,1)S(1)} %get-tuple-element.99.refs_4_), channel_id=1, source_target_pairs={{0,4},{4,0},{8,12},{12,8},{16,20},{20,16},{24,28},{28,24},{1,5},{5... | collective-permute-start | bytes 393224 | tf_op jit(solution)/shard_map/ppermute | solution.py:466
  64.3 5.7 %collective-permute-start.18 = (bf16[16,32,128]{2,1,0:T(8,128)(2,1)S(1)}, bf16[16,32,128]{2,1,0:T(8,128)(2,1)S(1)}, u32[]{:S(2)}, u32[]{:S(2)}) collective-permute-start(bf16[16,32,128]{2,1,0:T(8,128)(2,1)S(1)} %collective-permute-done.16.refs_1_), channel_id=1, source_target_pairs={{0,8},{4,12},{8,0},{12,4},{16,24},{20,28},{24,16},{28,20},{1,9},{5... | collective-permute-start | bytes 393224 | tf_op jit(solution)/shard_map/ppermute | solution.py:466
  67.2 5.0 %collective-permute-start.22 = (bf16[16,32,128]{2,1,0:T(8,128)(2,1)S(1)}, bf16[16,32,128]{2,1,0:T(8,128)(2,1)S(1)}, u32[]{:S(2)}, u32[]{:S(2)}) collective-permute-start(bf16[16,32,128]{2,1,0:T(8,128)(2,1)S(1)} %collective-permute-done.21.refs_6_), channel_id=1, source_target_pairs={{0,4},{4,0},{8,12},{12,8},{16,20},{20,16},{24,28},{28,24},{1,5},{5... | collective-permute-start | bytes 393224 | tf_op jit(solution)/shard_map/ppermute | solution.py:466
  67.2 1.4 collective-permute-start.23
  75.7 6.5 %collective-permute-start.26 = (bf16[17,32,128]{2,1,0:T(8,128)(2,1)S(1)}, bf16[17,32,128]{2,1,0:T(8,128)(2,1)S(1)}, u32[]{:S(2)}, u32[]{:S(2)}) collective-permute-start(bf16[17,32,128]{2,1,0:T(8,128)(2,1)S(1)} %get-tuple-element.110.refs_2_), channel_id=1, source_target_pairs={{0,4},{4,0},{8,12},{12,8},{16,20},{20,16},{24,28},{28,24},{1,5},{5... | collective-permute-start | bytes 417800 | tf_op jit(solution)/shard_map/ppermute | solution.py:466
  75.8 6.4 %collective-permute-start.25 = (bf16[16,32,128]{2,1,0:T(8,128)(2,1)S(1)}, bf16[16,32,128]{2,1,0:T(8,128)(2,1)S(1)}, u32[]{:S(2)}, u32[]{:S(2)}) collective-permute-start(bf16[16,32,128]{2,1,0:T(8,128)(2,1)S(1)} %get-tuple-element.108), channel_id=1, source_target_pairs={{0,4},{4,0},{8,12},{12,8},{16,20},{20,16},{24,28},{28,24},{1,5},{5... | collective-permute-start | bytes 393224 | tf_op jit(solution)/shard_map/ppermute | solution.py:466
  82.4 7.0 %collective-permute-start.27 = (bf16[17,32,128]{2,1,0:T(8,128)(2,1)S(1)}, bf16[17,32,128]{2,1,0:T(8,128)(2,1)S(1)}, u32[]{:S(2)}, u32[]{:S(2)}) collective-permute-start(bf16[17,32,128]{2,1,0:T(8,128)(2,1)S(1)} %fold.12.refs_3_), channel_id=1, source_target_pairs={{0,8},{4,12},{8,0},{12,4},{16,24},{20,28},{24,16},{28,20},{1,9},{5... | collective-permute-start | bytes 417800 | tf_op jit(solution)/shard_map/ppermute | solution.py:466
  82.5 9.7 %collective-permute-start.24 = (bf16[16,32,128]{2,1,0:T(8,128)(2,1)S(1)}, bf16[16,32,128]{2,1,0:T(8,128)(2,1)S(1)}, u32[]{:S(2)}, u32[]{:S(2)}) collective-permute-start(bf16[16,32,128]{2,1,0:T(8,128)(2,1)S(1)} %get-tuple-element.106), channel_id=1, source_target_pairs={{0,8},{4,12},{8,0},{12,4},{16,24},{20,28},{24,16},{28,20},{1,9},{5... | collective-permute-start | bytes 393224 | tf_op jit(solution)/shard_map/ppermute | solution.py:466
  89.5 9.3 %collective-permute-start.30 = (bf16[17,32,128]{2,1,0:T(8,128)(2,1)S(1)}, bf16[17,32,128]{2,1,0:T(8,128)(2,1)S(1)}, u32[]{:S(2)}, u32[]{:S(2)}) collective-permute-start(bf16[17,32,128]{2,1,0:T(8,128)(2,1)S(1)} %get-tuple-element.114.refs_2_.refs_4_), channel_id=1, source_target_pairs={{0,16},{4,20},{8,24},{12,28},{16,0},{20,4},{24,8},{28,12},{1,17},{... | collective-permute-start | bytes 417800 | tf_op jit(solution)/shard_map/ppermute | solution.py:466
  90.5 5.6 %collective-permute-start.29 = (bf16[16,32,128]{2,1,0:T(8,128)(2,1)S(1)}, bf16[16,32,128]{2,1,0:T(8,128)(2,1)S(1)}, u32[]{:S(2)}, u32[]{:S(2)}) collective-permute-start(bf16[16,32,128]{2,1,0:T(8,128)(2,1)S(1)} %get-tuple-element.115), channel_id=1, source_target_pairs={{0,8},{4,12},{8,0},{12,4},{16,24},{20,28},{24,16},{28,20},{1,9},{5... | collective-permute-start | bytes 393224 | tf_op jit(solution)/shard_map/ppermute | solution.py:466
  92.2 5.0 %collective-permute-start.28 = (bf16[16,32,128]{2,1,0:T(8,128)(2,1)S(1)}, bf16[16,32,128]{2,1,0:T(8,128)(2,1)S(1)}, u32[]{:S(2)}, u32[]{:S(2)}) collective-permute-start(bf16[16,32,128]{2,1,0:T(8,128)(2,1)S(1)} %fold.14), channel_id=1, source_target_pairs={{0,4},{4,0},{8,12},{12,8},{16,20},{20,16},{24,28},{28,24},{1,5},{5... | collective-permute-start | bytes 393224 | tf_op jit(solution)/shard_map/ppermute | solution.py:466
  93.0 3.6 %collective-permute-start.31 = (f32[8,128]{1,0:T(8,128)S(1)}, f32[8,128]{1,0:T(8,128)S(1)}, u32[]{:S(2)}, u32[]{:S(2)}) collective-permute-start(f32[8,128]{1,0:T(8,128)S(1)} %get-tuple-element.118.refs_9_), channel_id=1, source_target_pairs={{0,2},{1,3},{2,0},{3,1},{4,6},{5,7},{6,4},{7,5},{8,10},{9,11},{10,... | collective-permute-start | bytes 12296 | tf_op jit(solution)/shard_map/ppermute | solution.py:466
  98.9 7.4 %collective-permute-start.35 = (bf16[16,32,128]{2,1,0:T(8,128)(2,1)S(1)}, bf16[16,32,128]{2,1,0:T(8,128)(2,1)S(1)}, u32[]{:S(2)}, u32[]{:S(2)}) collective-permute-start(bf16[16,32,128]{2,1,0:T(8,128)(2,1)S(1)} %get-tuple-element.119.panel_ref.refs_0_), channel_id=1, source_target_pairs={{0,16},{4,20},{8,24},{12,28},{16,0},{20,4},{24,8},{28,12},{1,17},{... | collective-permute-start | bytes 393224 | tf_op jit(solution)/shard_map/ppermute | solution.py:466
  99.0 10.0 %collective-permute-start.32 = (bf16[16,32,128]{2,1,0:T(8,128)(2,1)S(1)}, bf16[16,32,128]{2,1,0:T(8,128)(2,1)S(1)}, u32[]{:S(2)}, u32[]{:S(2)}) collective-permute-start(bf16[16,32,128]{2,1,0:T(8,128)(2,1)S(1)} %get-tuple-element.119.panel_ref.refs_0_), channel_id=1, source_target_pairs={{0,4},{4,0},{8,12},{12,8},{16,20},{20,16},{24,28},{28,24},{1,5},{5... | collective-permute-start | bytes 393224 | tf_op jit(solution)/shard_map/ppermute | solution.py:466
  106.3 5.0 %collective-permute-start.37 = (bf16[16,32,128]{2,1,0:T(8,128)(2,1)S(1)}, bf16[16,32,128]{2,1,0:T(8,128)(2,1)S(1)}, u32[]{:S(2)}, u32[]{:S(2)}) collective-permute-start(bf16[16,32,128]{2,1,0:T(8,128)(2,1)S(1)} %get-tuple-element.122.refs_4_), channel_id=1, source_target_pairs={{0,8},{4,12},{8,0},{12,4},{16,24},{20,28},{24,16},{28,20},{1,9},{5... | collective-permute-start | bytes 393224 | tf_op jit(solution)/shard_map/ppermute | solution.py:466
  107.8 5.0 %collective-permute-start.33 = (bf16[16,32,128]{2,1,0:T(8,128)(2,1)S(1)}, bf16[16,32,128]{2,1,0:T(8,128)(2,1)S(1)}, u32[]{:S(2)}, u32[]{:S(2)}) collective-permute-start(bf16[16,32,128]{2,1,0:T(8,128)(2,1)S(1)} %get-tuple-element.119.panel_ref.refs_0_), channel_id=1, source_target_pairs={{0,8},{4,12},{8,0},{12,4},{16,24},{20,28},{24,16},{28,20},{1,9},{5... | collective-permute-start | bytes 393224 | tf_op jit(solution)/shard_map/ppermute | solution.py:466
  108.4 5.8 %collective-permute-start.36 = (bf16[16,32,128]{2,1,0:T(8,128)(2,1)S(1)}, bf16[16,32,128]{2,1,0:T(8,128)(2,1)S(1)}, u32[]{:S(2)}, u32[]{:S(2)}) collective-permute-start(bf16[16,32,128]{2,1,0:T(8,128)(2,1)S(1)} %get-tuple-element.122.refs_4_), channel_id=1, source_target_pairs={{0,4},{4,0},{8,12},{12,8},{16,20},{20,16},{24,28},{28,24},{1,5},{5... | collective-permute-start | bytes 393224 | tf_op jit(solution)/shard_map/ppermute | solution.py:466
  109.1 5.1 %collective-permute-start.34 = (bf16[16,32,128]{2,1,0:T(8,128)(2,1)S(1)}, bf16[16,32,128]{2,1,0:T(8,128)(2,1)S(1)}, u32[]{:S(2)}, u32[]{:S(2)}) collective-permute-start(bf16[16,32,128]{2,1,0:T(8,128)(2,1)S(1)} %collective-permute-done.32.refs_1_), channel_id=1, source_target_pairs={{0,8},{4,12},{8,0},{12,4},{16,24},{20,28},{24,16},{28,20},{1,9},{5... | collective-permute-start | bytes 393224 | tf_op jit(solution)/shard_map/ppermute | solution.py:466
  111.3 5.0 %collective-permute-start.38 = (bf16[16,32,128]{2,1,0:T(8,128)(2,1)S(1)}, bf16[16,32,128]{2,1,0:T(8,128)(2,1)S(1)}, u32[]{:S(2)}, u32[]{:S(2)}) collective-permute-start(bf16[16,32,128]{2,1,0:T(8,128)(2,1)S(1)} %collective-permute-done.37.refs_6_), channel_id=1, source_target_pairs={{0,4},{4,0},{8,12},{12,8},{16,20},{20,16},{24,28},{28,24},{1,5},{5... | collective-permute-start | bytes 393224 | tf_op jit(solution)/shard_map/ppermute | solution.py:466
  112.0 1.2 collective-permute-start.39
  120.5 6.5 %collective-permute-start.42 = (bf16[17,32,128]{2,1,0:T(8,128)(2,1)S(1)}, bf16[17,32,128]{2,1,0:T(8,128)(2,1)S(1)}, u32[]{:S(2)}, u32[]{:S(2)}) collective-permute-start(bf16[17,32,128]{2,1,0:T(8,128)(2,1)S(1)} %get-tuple-element.134.refs_2_), channel_id=1, source_target_pairs={{0,4},{4,0},{8,12},{12,8},{16,20},{20,16},{24,28},{28,24},{1,5},{5... | collective-permute-start | bytes 417800 | tf_op jit(solution)/shard_map/ppermute | solution.py:466
  121.1 5.8 %collective-permute-start.41 = (bf16[16,32,128]{2,1,0:T(8,128)(2,1)S(1)}, bf16[16,32,128]{2,1,0:T(8,128)(2,1)S(1)}, u32[]{:S(2)}, u32[]{:S(2)}) collective-permute-start(bf16[16,32,128]{2,1,0:T(8,128)(2,1)S(1)} %get-tuple-element.132), channel_id=1, source_target_pairs={{0,4},{4,0},{8,12},{12,8},{16,20},{20,16},{24,28},{28,24},{1,5},{5... | collective-permute-start | bytes 393224 | tf_op jit(solution)/shard_map/ppermute | solution.py:466
  127.1 8.0 %collective-permute-start.43 = (bf16[17,32,128]{2,1,0:T(8,128)(2,1)S(1)}, bf16[17,32,128]{2,1,0:T(8,128)(2,1)S(1)}, u32[]{:S(2)}, u32[]{:S(2)}) collective-permute-start(bf16[17,32,128]{2,1,0:T(8,128)(2,1)S(1)} %fold.15.refs_3_), channel_id=1, source_target_pairs={{0,8},{4,12},{8,0},{12,4},{16,24},{20,28},{24,16},{28,20},{1,9},{5... | collective-permute-start | bytes 417800 | tf_op jit(solution)/shard_map/ppermute | solution.py:466
  128.5 8.4 %collective-permute-start.40 = (bf16[16,32,128]{2,1,0:T(8,128)(2,1)S(1)}, bf16[16,32,128]{2,1,0:T(8,128)(2,1)S(1)}, u32[]{:S(2)}, u32[]{:S(2)}) collective-permute-start(bf16[16,32,128]{2,1,0:T(8,128)(2,1)S(1)} %get-tuple-element.130), channel_id=1, source_target_pairs={{0,8},{4,12},{8,0},{12,4},{16,24},{20,28},{24,16},{28,20},{1,9},{5... | collective-permute-start | bytes 393224 | tf_op jit(solution)/shard_map/ppermute | solution.py:466
  135.2 7.0 %collective-permute-start.46 = (bf16[17,32,128]{2,1,0:T(8,128)(2,1)S(1)}, bf16[17,32,128]{2,1,0:T(8,128)(2,1)S(1)}, u32[]{:S(2)}, u32[]{:S(2)}) collective-permute-start(bf16[17,32,128]{2,1,0:T(8,128)(2,1)S(1)} %get-tuple-element.138.refs_2_.refs_4_), channel_id=1, source_target_pairs={{0,16},{4,20},{8,24},{12,28},{16,0},{20,4},{24,8},{28,12},{1,17},{... | collective-permute-start | bytes 417800 | tf_op jit(solution)/shard_map/ppermute | solution.py:466
  135.3 5.1 %collective-permute-start.45 = (bf16[16,32,128]{2,1,0:T(8,128)(2,1)S(1)}, bf16[16,32,128]{2,1,0:T(8,128)(2,1)S(1)}, u32[]{:S(2)}, u32[]{:S(2)}) collective-permute-start(bf16[16,32,128]{2,1,0:T(8,128)(2,1)S(1)} %get-tuple-element.139), channel_id=1, source_target_pairs={{0,8},{4,12},{8,0},{12,4},{16,24},{20,28},{24,16},{28,20},{1,9},{5... | collective-permute-start | bytes 393224 | tf_op jit(solution)/shard_map/ppermute | solution.py:466
  137.0 5.1 %collective-permute-start.44 = (bf16[16,32,128]{2,1,0:T(8,128)(2,1)S(1)}, bf16[16,32,128]{2,1,0:T(8,128)(2,1)S(1)}, u32[]{:S(2)}, u32[]{:S(2)}) collective-permute-start(bf16[16,32,128]{2,1,0:T(8,128)(2,1)S(1)} %fold.17), channel_id=1, source_target_pairs={{0,4},{4,0},{8,12},{12,8},{16,20},{20,16},{24,28},{28,24},{1,5},{5... | collective-permute-start | bytes 393224 | tf_op jit(solution)/shard_map/ppermute | solution.py:466
  138.5 3.6 %collective-permute-start.47 = (f32[8,128]{1,0:T(8,128)S(1)}, f32[8,128]{1,0:T(8,128)S(1)}, u32[]{:S(2)}, u32[]{:S(2)}) collective-permute-start(f32[8,128]{1,0:T(8,128)S(1)} %get-tuple-element.142.refs_9_), channel_id=1, source_target_pairs={{0,2},{1,3},{2,0},{3,1},{4,6},{5,7},{6,4},{7,5},{8,10},{9,11},{10,... | collective-permute-start | bytes 12296 | tf_op jit(solution)/shard_map/ppermute | solution.py:466

commit v9 on v8

--- a/solution.py
+++ b/solution.py
@@ -111,7 +111,7 @@
 
 
 def last_hop(distance):
-    return 2 if distance == 3 else distance & -distance
+    return distance & -distance
 
 
 def children(distance, peers):
@@ -475,7 +475,7 @@
         panels[distance] = swap(panels[distance ^ hop], "net", hop)
         if distance == 1:
             far = peers // 2
-            panels[far], risk_sum = relay(panels[far], risk_sum, after)
+            panels[far], risk_sum = relay(panels[far], risk_sum, (*after, panels[2], panels[1]))
     return panels, risk_sum
 
 
@@ -526,7 +526,7 @@
         )
         base = local_forward(touched, bar, local_blocks, duals, demand)
         tops = sorted(inner(net_size), key=lambda k: (-k.bit_count(), -k))[:-1]
-        groups = [(top,) for top in tops if top != 1] + [(1,)]
+        groups = [(top,) for top in tops]
         loss, loss_top = sends[net_size - 1], net_size - 1
         ahead = {5: swap(sends[5], "net", last_hop(5))}
         after = (ahead[5], base)
@@ -542,7 +542,7 @@
                 )
             chain = loss_top ^ last_hop(loss_top) == group[0]
             sums = (risk_sum,) if group[0] == net_size // 2 else ()
-            if group == (1,):
+            if loss_top == net_size // 2:
                 after = (loss,)
             folded, passed = fold(terms, loss if chain else None, sums, after)
             sends.update(zip(group, folded))

time: 143 us -> 148 us (1.035)
  starting transfers between devices: 46 us -> 51.1 us
    ppermute x48, starting transfers between devices: 46 us -> 51.1 us  [swap(): return lax.ppermute(value, axis, [(i, i ^ distance) for i in range(size)])]
  transfers between devices with their start and end apart: 48 -> 48, of which waited for: 34 -> 26; matrix products, arithmetic and copies ran while one was open for 0% -> 0% of each run, Pallas kernels for 17% -> 16%
where the time goes in v9:
time: 148 us
  waiting for transfers between devices  53 us (36%)
  starting transfers between devices  51.1 us (35%)
  Pallas kernels  36.8 us (25%)
  local copies, waits for them, and re-layouts  5.05 us (3%)
  between operations  1.64 us (1%)
    ppermute x48, waiting for transfers between devices, swap(): return lax.ppermute(value, axis, [(i, i ^ distance) for i in range(size)])  53 us
    ppermute x48, starting transfers between devices, swap(): return lax.ppermute(value, axis, [(i, i ^ distance) for i in range(size)])  51.1 us
    pallas_call x3, Pallas kernels, local_adjoint(): pl.pallas_call(functools.partial(local_adjoint_kernel, touches, group), o...  12.9 us
    pallas_call x3, Pallas kernels, head_step(): pl.pallas_call(functools.partial(head_kernel, group, steps, peers), out_s...  11.2 us
    pallas_call x3, Pallas kernels, local_forward(): pl.pallas_call(functools.partial(local_forward_kernel, touches, group, st...  10 us
    unnamed x26, local copies, waits for them, and re-layouts  5.01 us
  transfers between devices with their start and end apart: 48, of which 26 were waited for; matrix products, arithmetic and copies ran while one was open for 0% of the time, Pallas kernels for 16%

profile of v9, /device:TPU:0, one launch (start us, length us, event | category | flops | bytes accessed | tf_op | source)
XLA Modules:
  0.0 147.5 jit_solution(8582891109071110526)
XLA Ops:
  0.7 0.9 copy-done
  1.6 3.0 %collective-permute-start.2 = (bf16[16,32,128]{2,1,0:T(8,128)(2,1)S(1)}, bf16[16,32,128]{2,1,0:T(8,128)(2,1)S(1)}, u32[]{:S(2)}, u32[]{:S(2)}) collective-permute-start(bf16[16,32,128]{2,1,0:T(8,128)(2,1)S(1)} %fusion.panel_ref.refs_0_), channel_id=1, source_target_pairs={{0,4},{4,0},{8,12},{12,8},{16,20},{20,16},{24,28},{28,24},{1,5},{5... | collective-permute-start | bytes 393224 | tf_op jit(solution)/shard_map/ppermute | solution.py:466
  4.6 1.6 %collective-permute-start.1 = (bf16[16,32,128]{2,1,0:T(8,128)(2,1)S(1)}, bf16[16,32,128]{2,1,0:T(8,128)(2,1)S(1)}, u32[]{:S(2)}, u32[]{:S(2)}) collective-permute-start(bf16[16,32,128]{2,1,0:T(8,128)(2,1)S(1)} %fusion.panel_ref.refs_0_), channel_id=1, source_target_pairs={{0,8},{4,12},{8,0},{12,4},{16,24},{20,28},{24,16},{28,20},{1,9},{5... | collective-permute-start | bytes 393224 | tf_op jit(solution)/shard_map/ppermute | solution.py:466
  6.2 2.6 %collective-permute-start = (bf16[16,32,128]{2,1,0:T(8,128)(2,1)S(1)}, bf16[16,32,128]{2,1,0:T(8,128)(2,1)S(1)}, u32[]{:S(2)}, u32[]{:S(2)}) collective-permute-start(bf16[16,32,128]{2,1,0:T(8,128)(2,1)S(1)} %fusion.panel_ref.refs_0_), channel_id=1, source_target_pairs={{0,16},{4,20},{8,24},{12,28},{16,0},{20,4},{24,8},{28,12},{1,17},{... | collective-permute-start | bytes 393224 | tf_op jit(solution)/shard_map/ppermute | solution.py:466
  8.8 3.4 %copy-done.1 = bf16[64,4,128,128]{3,2,1,0:T(8,128)(2,1)S(1)} copy-done((bf16[64,4,128,128]{3,2,1,0:T(8,128)(2,1)S(1)}, bf16[64,4,128,128]{3,2,1,0:T(8,128)(2,1)}, u32[]{:S(2)}) %copy-start.1) | copy-done | bytes 8388632
  12.2 0.7 copy-done.6
  12.9 4.3 %local_adjoint.3 = (f32[32,8192]{1,0:T(8,128)S(1)}, f32[8,128]{1,0:T(8,128)S(1)}) custom-call(s32[4,64]{1,0:T(4,128)S(1)} %bitcast.29, bf16[16,32,128]{2,1,0:T(8,128)(2,1)S(1)} %fusion.panel_ref.refs_0_, bf16[64,4,128,128]{3,2,1,0:T(8,128)(2,1)S(1)} %copy-done.1), custom_call_target="tpu_custom_call" | custom-call | flops 268435456 | bytes 8388608 | tf_op jit(solution)/shard_map/local_adjoint/pallas_call | solution.py:255
  18.8 1.5 %collective-permute-start.3 = (bf16[16,32,128]{2,1,0:T(8,128)(2,1)S(1)}, bf16[16,32,128]{2,1,0:T(8,128)(2,1)S(1)}, u32[]{:S(2)}, u32[]{:S(2)}) collective-permute-start(bf16[16,32,128]{2,1,0:T(8,128)(2,1)S(1)} %collective-permute-done.1.refs_1_.refs_2_), channel_id=1, source_target_pairs={{0,4},{4,0},{8,12},{12,8},{16,20},{20,16},{24,28},{28,24},{1,5},{5... | collective-permute-start | bytes 393224 | tf_op jit(solution)/shard_map/ppermute | solution.py:466
  20.3 2.5 %collective-permute-done.5.refs_6_ = bf16[16,32,128]{2,1,0:T(8,128)(2,1)S(1)} collective-permute-done((bf16[16,32,128]{2,1,0:T(8,128)(2,1)S(1)}, bf16[16,32,128]{2,1,0:T(8,128)(2,1)S(1)}, u32[]{:S(2)}, u32[]{:S(2)}) %collective-permute-start.5) | collective-permute-done | bytes 131104 | tf_op jit(solution)/shard_map/ppermute | solution.py:466
  24.2 1.2 collective-permute-done.7.refs_14_
  25.4 1.2 collective-permute-done.3.refs_3_
  26.6 1.4 collective-permute-done.6.refs_7_
  28.0 3.5 %head_step.3 = (f32[32,8192]{1,0:T(8,128)S(1)}, bf16[32,8192]{1,0:T(8,128)(2,1)S(1)}, f32[8,128]{1,0:T(8,128)S(1)}, f32[16,32,128]{2,1,0:T(8,128)S(1)}, f32[16,3...) custom-call(s32[64]{0:T(128)S(1)} %bitcast.35, ...), custom_call_target="tpu_custom_call" | custom-call | flops 134217728 | bytes 7864320 | tf_op jit(solution)/shard_map/head_step/pallas_call | solution.py:292
  32.1 1.5 %collective-permute-start.11 = (bf16[17,32,128]{2,1,0:T(8,128)(2,1)S(1)}, bf16[17,32,128]{2,1,0:T(8,128)(2,1)S(1)}, u32[]{:S(2)}, u32[]{:S(2)}) collective-permute-start(bf16[17,32,128]{2,1,0:T(8,128)(2,1)S(1)} %get-tuple-element.89.refs_2_), channel_id=1, source_target_pairs={{0,4},{4,0},{8,12},{12,8},{16,20},{20,16},{24,28},{28,24},{1,5},{5... | collective-permute-start | bytes 417800 | tf_op jit(solution)/shard_map/ppermute | solution.py:466
  33.7 3.3 %local_forward.3.refs_4_.refs_5_ = f32[16,32,128]{2,1,0:T(8,128)S(1)} custom-call(s32[4,64]{1,0:T(4,128)S(1)} %bitcast.30, bf16[32,8192]{1,0:T(8,128)(2,1)S(1)} %get-tuple-element.90.bar_ref, bf16[64,4,128,128]{3,2,1,0:T(8,128)(2,1)S(1)} %bitcast.25, f32[16,32,128]{2,1,0:T(8,128)S(1)} %bitcast_bitcast_fusion.duals_ref, f32[32,2048]{1,0:T(8,128)S(1)} %copy-done.4), custom_call_target="tpu_custom_call" | custom-call | flops 268435456 | bytes 8388608 | tf_op jit(solution)/shard_map/local_forward/pallas_call | solution.py:390
  37.0 1.1 collective-permute-done.11.refs_1_
  38.3 1.5 %collective-permute-start.12 = (bf16[17,32,128]{2,1,0:T(8,128)(2,1)S(1)}, bf16[17,32,128]{2,1,0:T(8,128)(2,1)S(1)}, u32[]{:S(2)}, u32[]{:S(2)}) collective-permute-start(bf16[17,32,128]{2,1,0:T(8,128)(2,1)S(1)} %fold.9.refs_3_), channel_id=1, source_target_pairs={{0,8},{4,12},{8,0},{12,4},{16,24},{20,28},{24,16},{28,20},{1,9},{5... | collective-permute-start | bytes 417800 | tf_op jit(solution)/shard_map/ppermute | solution.py:466
  40.4 3.4 %collective-permute-done.12.refs_2_ = bf16[17,32,128]{2,1,0:T(8,128)(2,1)S(1)} collective-permute-done((bf16[17,32,128]{2,1,0:T(8,128)(2,1)S(1)}, bf16[17,32,128]{2,1,0:T(8,128)(2,1)S(1)}, u32[]{:S(2)}, u32[]{:S(2)}) %collective-permute-start.12) | collective-permute-done | bytes 139296 | tf_op jit(solution)/shard_map/ppermute | solution.py:466
  44.0 1.0 collective-permute-start.8
  45.2 2.4 %collective-permute-start.13 = (bf16[16,32,128]{2,1,0:T(8,128)(2,1)S(1)}, bf16[16,32,128]{2,1,0:T(8,128)(2,1)S(1)}, u32[]{:S(2)}, u32[]{:S(2)}) collective-permute-start(bf16[16,32,128]{2,1,0:T(8,128)(2,1)S(1)} %fold.11), channel_id=1, source_target_pairs={{0,8},{4,12},{8,0},{12,4},{16,24},{20,28},{24,16},{28,20},{1,9},{5... | collective-permute-start | bytes 393224 | tf_op jit(solution)/shard_map/ppermute | solution.py:466
  47.6 1.5 %collective-permute-start.15 = (f32[8,128]{1,0:T(8,128)S(1)}, f32[8,128]{1,0:T(8,128)S(1)}, u32[]{:S(2)}, u32[]{:S(2)}) collective-permute-start(f32[8,128]{1,0:T(8,128)S(1)} %get-tuple-element.95.refs_9_), channel_id=1, source_target_pairs={{0,2},{1,3},{2,0},{3,1},{4,6},{5,7},{6,4},{7,5},{8,10},{9,11},{10,... | collective-permute-start | bytes 12296 | tf_op jit(solution)/shard_map/ppermute | solution.py:466
  49.1 2.1 %collective-permute-done.15.refs_10_ = f32[8,128]{1,0:T(8,128)S(1)} collective-permute-done((f32[8,128]{1,0:T(8,128)S(1)}, f32[8,128]{1,0:T(8,128)S(1)}, u32[]{:S(2)}, u32[]{:S(2)}) %collective-permute-start.15) | collective-permute-done | bytes 4128 | tf_op jit(solution)/shard_map/ppermute | solution.py:466
  51.2 1.8 %collective-permute-done.13.refs_2_ = bf16[16,32,128]{2,1,0:T(8,128)(2,1)S(1)} collective-permute-done((bf16[16,32,128]{2,1,0:T(8,128)(2,1)S(1)}, bf16[16,32,128]{2,1,0:T(8,128)(2,1)S(1)}, u32[]{:S(2)}, u32[]{:S(2)}) %collective-permute-start.13) | collective-permute-done | bytes 131104 | tf_op jit(solution)/shard_map/ppermute | solution.py:466
  53.2 3.4 %collective-permute-start.19 = (bf16[16,32,128]{2,1,0:T(8,128)(2,1)S(1)}, bf16[16,32,128]{2,1,0:T(8,128)(2,1)S(1)}, u32[]{:S(2)}, u32[]{:S(2)}) collective-permute-start(bf16[16,32,128]{2,1,0:T(8,128)(2,1)S(1)} %get-tuple-element.96.panel_ref.refs_0_), channel_id=1, source_target_pairs={{0,16},{4,20},{8,24},{12,28},{16,0},{20,4},{24,8},{28,12},{1,17},{... | collective-permute-start | bytes 393224 | tf_op jit(solution)/shard_map/ppermute | solution.py:466
  56.6 0.8 collective-permute-start.17
  57.3 1.3 collective-permute-start.16
  58.7 4.3 %local_adjoint.4 = (f32[32,8192]{1,0:T(8,128)S(1)}, f32[8,128]{1,0:T(8,128)S(1)}) custom-call(s32[4,64]{1,0:T(4,128)S(1)} %bitcast.31, bf16[16,32,128]{2,1,0:T(8,128)(2,1)S(1)} %get-tuple-element.96.panel_ref.refs_0_, bf16[64,4,128,128]{3,2,1,0:T(8,128)(2,1)S(1)} %bitcast.25), custom_call_target="tpu_custom_call" | custom-call | flops 268435456 | bytes 8388608 | tf_op jit(solution)/shard_map/local_adjoint/pallas_call | solution.py:255
  63.0 0.7 collective-permute-done.16.refs_2_.refs_1_
  64.2 0.8 collective-permute-start.20
  65.0 1.2 collective-permute-start.18
  66.2 2.5 %collective-permute-done.21.refs_6_ = bf16[16,32,128]{2,1,0:T(8,128)(2,1)S(1)} collective-permute-done((bf16[16,32,128]{2,1,0:T(8,128)(2,1)S(1)}, bf16[16,32,128]{2,1,0:T(8,128)(2,1)S(1)}, u32[]{:S(2)}, u32[]{:S(2)}) %collective-permute-start.21) | collective-permute-done | bytes 131104 | tf_op jit(solution)/shard_map/ppermute | solution.py:466
  69.2 1.2 collective-permute-done.23.refs_14_
  70.6 3.1 %collective-permute-done.22.refs_7_ = bf16[16,32,128]{2,1,0:T(8,128)(2,1)S(1)} collective-permute-done((bf16[16,32,128]{2,1,0:T(8,128)(2,1)S(1)}, bf16[16,32,128]{2,1,0:T(8,128)(2,1)S(1)}, u32[]{:S(2)}, u32[]{:S(2)}) %collective-permute-start.22) | collective-permute-done | bytes 131104 | tf_op jit(solution)/shard_map/ppermute | solution.py:466
  73.7 3.5 %head_step.4 = (f32[32,8192]{1,0:T(8,128)S(1)}, bf16[32,8192]{1,0:T(8,128)(2,1)S(1)}, f32[8,128]{1,0:T(8,128)S(1)}, f32[16,32,128]{2,1,0:T(8,128)S(1)}, f32[16,3...) custom-call(s32[64]{0:T(128)S(1)} %bitcast.36, ...), custom_call_target="tpu_custom_call" | custom-call | flops 134217728 | bytes 7864320 | tf_op jit(solution)/shard_map/head_step/pallas_call | solution.py:292
  77.8 1.5 %collective-permute-start.26 = (bf16[16,32,128]{2,1,0:T(8,128)(2,1)S(1)}, bf16[16,32,128]{2,1,0:T(8,128)(2,1)S(1)}, u32[]{:S(2)}, u32[]{:S(2)}) collective-permute-start(bf16[16,32,128]{2,1,0:T(8,128)(2,1)S(1)} %get-tuple-element.109), channel_id=1, source_target_pairs={{0,4},{4,0},{8,12},{12,8},{16,20},{20,16},{24,28},{28,24},{1,5},{5... | collective-permute-start | bytes 393224 | tf_op jit(solution)/shard_map/ppermute | solution.py:466
  79.3 3.3 %local_forward.4.refs_4_.refs_5_ = f32[16,32,128]{2,1,0:T(8,128)S(1)} custom-call(s32[4,64]{1,0:T(4,128)S(1)} %bitcast.32, bf16[32,8192]{1,0:T(8,128)(2,1)S(1)} %get-tuple-element.112.bar_ref, bf16[64,4,128,128]{3,2,1,0:T(8,128)(2,1)S(1)} %bitcast.25, f32[16,32,128]{2,1,0:T(8,128)S(1)} %get-tuple-element.113.duals_ref, f32[32,2048]{1,0:T(8,128)S(1)} %copy-done.4), custom_call_target="tpu_custom_call" | custom-call | flops 268435456 | bytes 8388608 | tf_op jit(solution)/shard_map/local_forward/pallas_call | solution.py:390
  82.6 2.0 %collective-permute-done.26.refs_3_.refs_1_ = bf16[16,32,128]{2,1,0:T(8,128)(2,1)S(1)} collective-permute-done((bf16[16,32,128]{2,1,0:T(8,128)(2,1)S(1)}, bf16[16,32,128]{2,1,0:T(8,128)(2,1)S(1)}, u32[]{:S(2)}, u32[]{:S(2)}) %collective-permute-start.26) | collective-permute-done | bytes 131104 | tf_op jit(solution)/shard_map/ppermute | solution.py:466
  85.2 6.8 %collective-permute-done.28.refs_2_ = bf16[17,32,128]{2,1,0:T(8,128)(2,1)S(1)} collective-permute-done((bf16[17,32,128]{2,1,0:T(8,128)(2,1)S(1)}, bf16[17,32,128]{2,1,0:T(8,128)(2,1)S(1)}, u32[]{:S(2)}, u32[]{:S(2)}) %collective-permute-start.28) | collective-permute-done | bytes 139296 | tf_op jit(solution)/shard_map/ppermute | solution.py:466
  92.9 1.4 collective-permute-start.29
  94.3 1.5 %collective-permute-start.31 = (f32[8,128]{1,0:T(8,128)S(1)}, f32[8,128]{1,0:T(8,128)S(1)}, u32[]{:S(2)}, u32[]{:S(2)}) collective-permute-start(f32[8,128]{1,0:T(8,128)S(1)} %get-tuple-element.118.refs_9_), channel_id=1, source_target_pairs={{0,2},{1,3},{2,0},{3,1},{4,6},{5,7},{6,4},{7,5},{8,10},{9,11},{10,... | collective-permute-start | bytes 12296 | tf_op jit(solution)/shard_map/ppermute | solution.py:466
  95.8 2.4 %collective-permute-done.24.refs_1_ = bf16[16,32,128]{2,1,0:T(8,128)(2,1)S(1)} collective-permute-done((bf16[16,32,128]{2,1,0:T(8,128)(2,1)S(1)}, bf16[16,32,128]{2,1,0:T(8,128)(2,1)S(1)}, u32[]{:S(2)}, u32[]{:S(2)}) %collective-permute-start.24) | collective-permute-done | bytes 131104 | tf_op jit(solution)/shard_map/ppermute | solution.py:466
  98.3 2.5 %collective-permute-done.29.refs_2_ = bf16[16,32,128]{2,1,0:T(8,128)(2,1)S(1)} collective-permute-done((bf16[16,32,128]{2,1,0:T(8,128)(2,1)S(1)}, bf16[16,32,128]{2,1,0:T(8,128)(2,1)S(1)}, u32[]{:S(2)}, u32[]{:S(2)}) %collective-permute-start.29) | collective-permute-done | bytes 131104 | tf_op jit(solution)/shard_map/ppermute | solution.py:466
  101.4 2.4 %collective-permute-start.33 = (bf16[16,32,128]{2,1,0:T(8,128)(2,1)S(1)}, bf16[16,32,128]{2,1,0:T(8,128)(2,1)S(1)}, u32[]{:S(2)}, u32[]{:S(2)}) collective-permute-start(bf16[16,32,128]{2,1,0:T(8,128)(2,1)S(1)} %get-tuple-element.119.panel_ref.refs_0_), channel_id=1, source_target_pairs={{0,8},{4,12},{8,0},{12,4},{16,24},{20,28},{24,16},{28,20},{1,9},{5... | collective-permute-start | bytes 393224 | tf_op jit(solution)/shard_map/ppermute | solution.py:466
  103.8 1.3 collective-permute-start.32
  105.1 4.3 %local_adjoint.5 = (f32[32,8192]{1,0:T(8,128)S(1)}, f32[8,128]{1,0:T(8,128)S(1)}) custom-call(s32[4,64]{1,0:T(4,128)S(1)} %bitcast.33, bf16[16,32,128]{2,1,0:T(8,128)(2,1)S(1)} %get-tuple-element.119.panel_ref.refs_0_, bf16[64,4,128,128]{3,2,1,0:T(8,128)(2,1)S(1)} %bitcast.25), custom_call_target="tpu_custom_call" | custom-call | flops 268435456 | bytes 8388608 | tf_op jit(solution)/shard_map/local_adjoint/pallas_call | solution.py:255
  109.7 0.7 collective-permute-start.37
  110.4 1.2 collective-permute-start.36
  111.5 0.9 collective-permute-start.34
  112.4 2.3 %collective-permute-done.37.refs_6_ = bf16[16,32,128]{2,1,0:T(8,128)(2,1)S(1)} collective-permute-done((bf16[16,32,128]{2,1,0:T(8,128)(2,1)S(1)}, bf16[16,32,128]{2,1,0:T(8,128)(2,1)S(1)}, u32[]{:S(2)}, u32[]{:S(2)}) %collective-permute-start.37) | collective-permute-done | bytes 131104 | tf_op jit(solution)/shard_map/ppermute | solution.py:466
  114.7 1.0 collective-permute-start.38
  115.8 1.2 collective-permute-done.39.refs_14_
  116.9 2.8 %collective-permute-done.38.refs_7_ = bf16[16,32,128]{2,1,0:T(8,128)(2,1)S(1)} collective-permute-done((bf16[16,32,128]{2,1,0:T(8,128)(2,1)S(1)}, bf16[16,32,128]{2,1,0:T(8,128)(2,1)S(1)}, u32[]{:S(2)}, u32[]{:S(2)}) %collective-permute-start.38) | collective-permute-done | bytes 131104 | tf_op jit(solution)/shard_map/ppermute | solution.py:466
  119.7 4.2 %head_step.5 = (f32[32,8192]{1,0:T(8,128)}, bf16[32,8192]{1,0:T(8,128)(2,1)S(1)}, f32[8,128]{1,0:T(8,128)S(1)}, f32[16,32,128]{2,1,0:T(8,128)S(1)}, f32[16,32,12...) custom-call(s32[64]{0:T(128)S(1)} %bitcast.37, ...), custom_call_target="tpu_custom_call" | custom-call | flops 134217728 | bytes 7864320 | tf_op jit(solution)/shard_map/head_step/pallas_call | solution.py:292
  123.9 1.0 collective-permute-start.43
  124.9 1.0 collective-permute-start.42
  125.9 3.3 %local_forward.5.refs_4_.refs_5_ = f32[16,32,128]{2,1,0:T(8,128)S(1)} custom-call(s32[4,64]{1,0:T(4,128)S(1)} %bitcast.34, bf16[32,8192]{1,0:T(8,128)(2,1)S(1)} %get-tuple-element.136.bar_ref, bf16[64,4,128,128]{3,2,1,0:T(8,128)(2,1)S(1)} %bitcast.25, f32[16,32,128]{2,1,0:T(8,128)S(1)} %get-tuple-element.137.duals_ref, f32[32,2048]{1,0:T(8,128)S(1)} %copy-done.4), custom_call_target="tpu_custom_call" | custom-call | flops 268435456 | bytes 8388608 | tf_op jit(solution)/shard_map/local_forward/pallas_call | solution.py:390
  129.2 1.5 %collective-permute-done.42.refs_3_.refs_1_ = bf16[16,32,128]{2,1,0:T(8,128)(2,1)S(1)} collective-permute-done((bf16[16,32,128]{2,1,0:T(8,128)(2,1)S(1)}, bf16[16,32,128]{2,1,0:T(8,128)(2,1)S(1)}, u32[]{:S(2)}, u32[]{:S(2)}) %collective-permute-start.42) | collective-permute-done | bytes 131104 | tf_op jit(solution)/shard_map/ppermute | solution.py:466
  131.1 1.2 collective-permute-start.41
  132.3 6.4 %collective-permute-done.44.refs_2_ = bf16[17,32,128]{2,1,0:T(8,128)(2,1)S(1)} collective-permute-done((bf16[17,32,128]{2,1,0:T(8,128)(2,1)S(1)}, bf16[17,32,128]{2,1,0:T(8,128)(2,1)S(1)}, u32[]{:S(2)}, u32[]{:S(2)}) %collective-permute-start.44) | collective-permute-done | bytes 139296 | tf_op jit(solution)/shard_map/ppermute | solution.py:466
  138.9 1.6 %collective-permute-start.40 = (bf16[16,32,128]{2,1,0:T(8,128)(2,1)S(1)}, bf16[16,32,128]{2,1,0:T(8,128)(2,1)S(1)}, u32[]{:S(2)}, u32[]{:S(2)}) collective-permute-start(bf16[16,32,128]{2,1,0:T(8,128)(2,1)S(1)} %get-tuple-element.129), channel_id=1, source_target_pairs={{0,4},{4,0},{8,12},{12,8},{16,20},{20,16},{24,28},{28,24},{1,5},{5... | collective-permute-start | bytes 393224 | tf_op jit(solution)/shard_map/ppermute | solution.py:466
  140.5 2.5 %collective-permute-start.45 = (bf16[16,32,128]{2,1,0:T(8,128)(2,1)S(1)}, bf16[16,32,128]{2,1,0:T(8,128)(2,1)S(1)}, u32[]{:S(2)}, u32[]{:S(2)}) collective-permute-start(bf16[16,32,128]{2,1,0:T(8,128)(2,1)S(1)} %fold.17), channel_id=1, source_target_pairs={{0,8},{4,12},{8,0},{12,4},{16,24},{20,28},{24,16},{28,20},{1,9},{5... | collective-permute-start | bytes 393224 | tf_op jit(solution)/shard_map/ppermute | solution.py:466
  143.1 1.5 %collective-permute-start.47 = (f32[8,128]{1,0:T(8,128)S(1)}, f32[8,128]{1,0:T(8,128)S(1)}, u32[]{:S(2)}, u32[]{:S(2)}) collective-permute-start(f32[8,128]{1,0:T(8,128)S(1)} %get-tuple-element.142.refs_9_), channel_id=1, source_target_pairs={{0,2},{1,3},{2,0},{3,1},{4,6},{5,7},{6,4},{7,5},{8,10},{9,11},{10,... | collective-permute-start | bytes 12296 | tf_op jit(solution)/shard_map/ppermute | solution.py:466
  144.6 2.1 %collective-permute-done.47.refs_10_ = f32[8,128]{1,0:T(8,128)S(1)} collective-permute-done((f32[8,128]{1,0:T(8,128)S(1)}, f32[8,128]{1,0:T(8,128)S(1)}, u32[]{:S(2)}, u32[]{:S(2)}) %collective-permute-start.47) | collective-permute-done | bytes 4128 | tf_op jit(solution)/shard_map/ppermute | solution.py:466
  146.7 0.8 settle.5
  (86 shorter events, 8.9 us)
Async XLA Ops:
  0.6 1.0 copy-start
  0.6 23.3 %copy-start.10 = (s32[64]{0:T(128)S(1)}, s32[64]{0:T(128)}, u32[]{:S(2)}) copy-start(s32[64]{0:T(128)} %param.21) | copy-start | bytes 772
  0.7 23.3 %copy-start.8 = (f32[32]{0:T(128)S(1)}, f32[32]{0:T(128)}, u32[]{:S(2)}) copy-start(f32[32]{0:T(128)} %param.15) | copy-start | bytes 388
  0.7 23.3 %copy-start.9 = (f32[32]{0:T(128)S(1)}, f32[32]{0:T(128)}, u32[]{:S(2)}) copy-start(f32[32]{0:T(128)} %param.14) | copy-start | bytes 388
  0.7 27.3 %copy-start.5 = (f32[8192]{0:T(1024)S(1)}, f32[8192]{0:T(1024)}, u32[]{:S(2)}) copy-start(f32[8192]{0:T(1024)} %param.17) | copy-start | bytes 98308
  1.6 15.5 %collective-permute-start.2 = (bf16[16,32,128]{2,1,0:T(8,128)(2,1)S(1)}, bf16[16,32,128]{2,1,0:T(8,128)(2,1)S(1)}, u32[]{:S(2)}, u32[]{:S(2)}) collective-permute-start(bf16[16,32,128]{2,1,0:T(8,128)(2,1)S(1)} %fusion.panel_ref.refs_0_), channel_id=1, source_target_pairs={{0,4},{4,0},{8,12},{12,8},{16,20},{20,16},{24,28},{28,24},{1,5},{5... | collective-permute-start | bytes 393224 | tf_op jit(solution)/shard_map/ppermute | solution.py:466
  4.6 12.6 %collective-permute-start.1 = (bf16[16,32,128]{2,1,0:T(8,128)(2,1)S(1)}, bf16[16,32,128]{2,1,0:T(8,128)(2,1)S(1)}, u32[]{:S(2)}, u32[]{:S(2)}) collective-permute-start(bf16[16,32,128]{2,1,0:T(8,128)(2,1)S(1)} %fusion.panel_ref.refs_0_), channel_id=1, source_target_pairs={{0,8},{4,12},{8,0},{12,4},{16,24},{20,28},{24,16},{28,20},{1,9},{5... | collective-permute-start | bytes 393224 | tf_op jit(solution)/shard_map/ppermute | solution.py:466
  6.2 11.0 %collective-permute-start = (bf16[16,32,128]{2,1,0:T(8,128)(2,1)S(1)}, bf16[16,32,128]{2,1,0:T(8,128)(2,1)S(1)}, u32[]{:S(2)}, u32[]{:S(2)}) collective-permute-start(bf16[16,32,128]{2,1,0:T(8,128)(2,1)S(1)} %fusion.panel_ref.refs_0_), channel_id=1, source_target_pairs={{0,16},{4,20},{8,24},{12,28},{16,0},{20,4},{24,8},{28,12},{1,17},{... | collective-permute-start | bytes 393224 | tf_op jit(solution)/shard_map/ppermute | solution.py:466
  8.8 3.4 %copy-start.1 = (bf16[64,4,128,128]{3,2,1,0:T(8,128)(2,1)S(1)}, bf16[64,4,128,128]{3,2,1,0:T(8,128)(2,1)}, u32[]{:S(2)}) copy-start(bf16[64,4,128,128]{3,2,1,0:T(8,128)(2,1)} %blocks_ref.11) | copy-start | bytes 25165828
  12.2 0.7 copy-start.6
  12.8 11.1 %copy-start.2 = (bf16[64,128,128]{2,1,0:T(8,128)(2,1)S(1)}, bf16[64,128,128]{2,1,0:T(8,128)(2,1)}, u32[]{:S(2)}) copy-start(bf16[64,128,128]{2,1,0:T(8,128)(2,1)} %refs_8_.5) | copy-start | bytes 6291460
  12.8 11.1 %copy-start.3 = (f32[32,8192]{1,0:T(8,128)S(1)}, f32[32,8192]{1,0:T(8,128)}, u32[]{:S(2)}) copy-start(f32[32,8192]{1,0:T(8,128)} %refs_10_.1) | copy-start | bytes 3145732
  12.9 20.8 %slice-start = ((s8[8388608]{0:T(1024)(128)(4,1)}), s8[4194304]{0:T(1024)(128)(4,1)S(1)}, s32[]{:S(2)}) async-start(s8[8388608]{0:T(1024)(128)(4,1)} %bitcast.24), calls=%async_computation | async-start | bytes 8388608
  12.9 20.8 %copy-start.4 = (f32[32,2048]{1,0:T(8,128)S(1)}, f32[32,2048]{1,0:T(8,128)}, u32[]{:S(2)}) copy-start(f32[32,2048]{1,0:T(8,128)} %demand_ref.5) | copy-start | bytes 786436
  17.8 5.0 %collective-permute-start.5 = (bf16[16,32,128]{2,1,0:T(8,128)(2,1)S(1)}, bf16[16,32,128]{2,1,0:T(8,128)(2,1)S(1)}, u32[]{:S(2)}, u32[]{:S(2)}) collective-permute-start(bf16[16,32,128]{2,1,0:T(8,128)(2,1)S(1)} %get-tuple-element.77.refs_0_.refs_4_), channel_id=1, source_target_pairs={{0,8},{4,12},{8,0},{12,4},{16,24},{20,28},{24,16},{28,20},{1,9},{5... | collective-permute-start | bytes 393224 | tf_op jit(solution)/shard_map/ppermute | solution.py:466
  18.2 8.3 %collective-permute-start.4 = (bf16[16,32,128]{2,1,0:T(8,128)(2,1)S(1)}, bf16[16,32,128]{2,1,0:T(8,128)(2,1)S(1)}, u32[]{:S(2)}, u32[]{:S(2)}) collective-permute-start(bf16[16,32,128]{2,1,0:T(8,128)(2,1)S(1)} %get-tuple-element.77.refs_0_.refs_4_), channel_id=1, source_target_pairs={{0,4},{4,0},{8,12},{12,8},{16,20},{20,16},{24,28},{28,24},{1,5},{5... | collective-permute-start | bytes 393224 | tf_op jit(solution)/shard_map/ppermute | solution.py:466
  18.8 7.8 %collective-permute-start.3 = (bf16[16,32,128]{2,1,0:T(8,128)(2,1)S(1)}, bf16[16,32,128]{2,1,0:T(8,128)(2,1)S(1)}, u32[]{:S(2)}, u32[]{:S(2)}) collective-permute-start(bf16[16,32,128]{2,1,0:T(8,128)(2,1)S(1)} %collective-permute-done.1.refs_1_.refs_2_), channel_id=1, source_target_pairs={{0,4},{4,0},{8,12},{12,8},{16,20},{20,16},{24,28},{28,24},{1,5},{5... | collective-permute-start | bytes 393224 | tf_op jit(solution)/shard_map/ppermute | solution.py:466
  22.8 5.2 %collective-permute-start.6 = (bf16[16,32,128]{2,1,0:T(8,128)(2,1)S(1)}, bf16[16,32,128]{2,1,0:T(8,128)(2,1)S(1)}, u32[]{:S(2)}, u32[]{:S(2)}) collective-permute-start(bf16[16,32,128]{2,1,0:T(8,128)(2,1)S(1)} %collective-permute-done.5.refs_6_), channel_id=1, source_target_pairs={{0,4},{4,0},{8,12},{12,8},{16,20},{20,16},{24,28},{28,24},{1,5},{5... | collective-permute-start | bytes 393224 | tf_op jit(solution)/shard_map/ppermute | solution.py:466
  24.0 9.7 %slice-start.1 = ((s8[8388608]{0:T(1024)(128)(4,1)}), s8[4194304]{0:T(1024)(128)(4,1)S(1)}, s32[]{:S(2)}) async-start(s8[8388608]{0:T(1024)(128)(4,1)} %bitcast.24), calls=%async_computation.1 | async-start | bytes 8388608
  24.1 1.2 collective-permute-start.7
  28.0 30.7 %copy-start.7 = (s32[64,4]{0,1:T(4,128)S(1)}, s32[64,4]{0,1:T(4,128)}, u32[]{:S(2)}) copy-start(s32[64,4]{0,1:T(4,128)} %param.20) | copy-start | bytes 3076
  31.5 5.5 %collective-permute-start.10 = (bf16[16,32,128]{2,1,0:T(8,128)(2,1)S(1)}, bf16[16,32,128]{2,1,0:T(8,128)(2,1)S(1)}, u32[]{:S(2)}, u32[]{:S(2)}) collective-permute-start(bf16[16,32,128]{2,1,0:T(8,128)(2,1)S(1)} %get-tuple-element.87), channel_id=1, source_target_pairs={{0,4},{4,0},{8,12},{12,8},{16,20},{20,16},{24,28},{28,24},{1,5},{5... | collective-permute-start | bytes 393224 | tf_op jit(solution)/shard_map/ppermute | solution.py:466
  32.1 6.1 %collective-permute-start.11 = (bf16[17,32,128]{2,1,0:T(8,128)(2,1)S(1)}, bf16[17,32,128]{2,1,0:T(8,128)(2,1)S(1)}, u32[]{:S(2)}, u32[]{:S(2)}) collective-permute-start(bf16[17,32,128]{2,1,0:T(8,128)(2,1)S(1)} %get-tuple-element.89.refs_2_), channel_id=1, source_target_pairs={{0,4},{4,0},{8,12},{12,8},{16,20},{20,16},{24,28},{28,24},{1,5},{5... | collective-permute-start | bytes 417800 | tf_op jit(solution)/shard_map/ppermute | solution.py:466
  38.3 5.5 %collective-permute-start.12 = (bf16[17,32,128]{2,1,0:T(8,128)(2,1)S(1)}, bf16[17,32,128]{2,1,0:T(8,128)(2,1)S(1)}, u32[]{:S(2)}, u32[]{:S(2)}) collective-permute-start(bf16[17,32,128]{2,1,0:T(8,128)(2,1)S(1)} %fold.9.refs_3_), channel_id=1, source_target_pairs={{0,8},{4,12},{8,0},{12,4},{16,24},{20,28},{24,16},{28,20},{1,9},{5... | collective-permute-start | bytes 417800 | tf_op jit(solution)/shard_map/ppermute | solution.py:466
  39.8 5.4 %collective-permute-start.9 = (bf16[16,32,128]{2,1,0:T(8,128)(2,1)S(1)}, bf16[16,32,128]{2,1,0:T(8,128)(2,1)S(1)}, u32[]{:S(2)}, u32[]{:S(2)}) collective-permute-start(bf16[16,32,128]{2,1,0:T(8,128)(2,1)S(1)} %get-tuple-element.85), channel_id=1, source_target_pairs={{0,4},{4,0},{8,12},{12,8},{16,20},{20,16},{24,28},{28,24},{1,5},{5... | collective-permute-start | bytes 393224 | tf_op jit(solution)/shard_map/ppermute | solution.py:466
  43.9 9.1 %collective-permute-start.14 = (bf16[17,32,128]{2,1,0:T(8,128)(2,1)S(1)}, bf16[17,32,128]{2,1,0:T(8,128)(2,1)S(1)}, u32[]{:S(2)}, u32[]{:S(2)}) collective-permute-start(bf16[17,32,128]{2,1,0:T(8,128)(2,1)S(1)} %get-tuple-element.92.refs_2_.refs_4_), channel_id=1, source_target_pairs={{0,16},{4,20},{8,24},{12,28},{16,0},{20,4},{24,8},{28,12},{1,17},{... | collective-permute-start | bytes 417800 | tf_op jit(solution)/shard_map/ppermute | solution.py:466
  44.0 5.1 %collective-permute-start.8 = (bf16[16,32,128]{2,1,0:T(8,128)(2,1)S(1)}, bf16[16,32,128]{2,1,0:T(8,128)(2,1)S(1)}, u32[]{:S(2)}, u32[]{:S(2)}) collective-permute-start(bf16[16,32,128]{2,1,0:T(8,128)(2,1)S(1)} %get-tuple-element.83), channel_id=1, source_target_pairs={{0,4},{4,0},{8,12},{12,8},{16,20},{20,16},{24,28},{28,24},{1,5},{5... | collective-permute-start | bytes 393224 | tf_op jit(solution)/shard_map/ppermute | solution.py:466
  45.2 7.8 %collective-permute-start.13 = (bf16[16,32,128]{2,1,0:T(8,128)(2,1)S(1)}, bf16[16,32,128]{2,1,0:T(8,128)(2,1)S(1)}, u32[]{:S(2)}, u32[]{:S(2)}) collective-permute-start(bf16[16,32,128]{2,1,0:T(8,128)(2,1)S(1)} %fold.11), channel_id=1, source_target_pairs={{0,8},{4,12},{8,0},{12,4},{16,24},{20,28},{24,16},{28,20},{1,9},{5... | collective-permute-start | bytes 393224 | tf_op jit(solution)/shard_map/ppermute | solution.py:466
  47.6 3.6 %collective-permute-start.15 = (f32[8,128]{1,0:T(8,128)S(1)}, f32[8,128]{1,0:T(8,128)S(1)}, u32[]{:S(2)}, u32[]{:S(2)}) collective-permute-start(f32[8,128]{1,0:T(8,128)S(1)} %get-tuple-element.95.refs_9_), channel_id=1, source_target_pairs={{0,2},{1,3},{2,0},{3,1},{4,6},{5,7},{6,4},{7,5},{8,10},{9,11},{10,... | collective-permute-start | bytes 12296 | tf_op jit(solution)/shard_map/ppermute | solution.py:466
  53.2 9.8 %collective-permute-start.19 = (bf16[16,32,128]{2,1,0:T(8,128)(2,1)S(1)}, bf16[16,32,128]{2,1,0:T(8,128)(2,1)S(1)}, u32[]{:S(2)}, u32[]{:S(2)}) collective-permute-start(bf16[16,32,128]{2,1,0:T(8,128)(2,1)S(1)} %get-tuple-element.96.panel_ref.refs_0_), channel_id=1, source_target_pairs={{0,16},{4,20},{8,24},{12,28},{16,0},{20,4},{24,8},{28,12},{1,17},{... | collective-permute-start | bytes 393224 | tf_op jit(solution)/shard_map/ppermute | solution.py:466
  56.6 6.4 %collective-permute-start.17 = (bf16[16,32,128]{2,1,0:T(8,128)(2,1)S(1)}, bf16[16,32,128]{2,1,0:T(8,128)(2,1)S(1)}, u32[]{:S(2)}, u32[]{:S(2)}) collective-permute-start(bf16[16,32,128]{2,1,0:T(8,128)(2,1)S(1)} %get-tuple-element.96.panel_ref.refs_0_), channel_id=1, source_target_pairs={{0,8},{4,12},{8,0},{12,4},{16,24},{20,28},{24,16},{28,20},{1,9},{5... | collective-permute-start | bytes 393224 | tf_op jit(solution)/shard_map/ppermute | solution.py:466
  57.3 6.3 %collective-permute-start.16 = (bf16[16,32,128]{2,1,0:T(8,128)(2,1)S(1)}, bf16[16,32,128]{2,1,0:T(8,128)(2,1)S(1)}, u32[]{:S(2)}, u32[]{:S(2)}) collective-permute-start(bf16[16,32,128]{2,1,0:T(8,128)(2,1)S(1)} %get-tuple-element.96.panel_ref.refs_0_), channel_id=1, source_target_pairs={{0,4},{4,0},{8,12},{12,8},{16,20},{20,16},{24,28},{28,24},{1,5},{5... | collective-permute-start | bytes 393224 | tf_op jit(solution)/shard_map/ppermute | solution.py:466
  63.7 5.0 %collective-permute-start.21 = (bf16[16,32,128]{2,1,0:T(8,128)(2,1)S(1)}, bf16[16,32,128]{2,1,0:T(8,128)(2,1)S(1)}, u32[]{:S(2)}, u32[]{:S(2)}) collective-permute-start(bf16[16,32,128]{2,1,0:T(8,128)(2,1)S(1)} %get-tuple-element.99.refs_4_), channel_id=1, source_target_pairs={{0,8},{4,12},{8,0},{12,4},{16,24},{20,28},{24,16},{28,20},{1,9},{5... | collective-permute-start | bytes 393224 | tf_op jit(solution)/shard_map/ppermute | solution.py:466
  64.2 6.4 %collective-permute-start.20 = (bf16[16,32,128]{2,1,0:T(8,128)(2,1)S(1)}, bf16[16,32,128]{2,1,0:T(8,128)(2,1)S(1)}, u32[]{:S(2)}, u32[]{:S(2)}) collective-permute-start(bf16[16,32,128]{2,1,0:T(8,128)(2,1)S(1)} %get-tuple-element.99.refs_4_), channel_id=1, source_target_pairs={{0,4},{4,0},{8,12},{12,8},{16,20},{20,16},{24,28},{28,24},{1,5},{5... | collective-permute-start | bytes 393224 | tf_op jit(solution)/shard_map/ppermute | solution.py:466
  65.0 5.5 %collective-permute-start.18 = (bf16[16,32,128]{2,1,0:T(8,128)(2,1)S(1)}, bf16[16,32,128]{2,1,0:T(8,128)(2,1)S(1)}, u32[]{:S(2)}, u32[]{:S(2)}) collective-permute-start(bf16[16,32,128]{2,1,0:T(8,128)(2,1)S(1)} %collective-permute-done.17.refs_1_.refs_2_), channel_id=1, source_target_pairs={{0,4},{4,0},{8,12},{12,8},{16,20},{20,16},{24,28},{28,24},{1,5},{5... | collective-permute-start | bytes 393224 | tf_op jit(solution)/shard_map/ppermute | solution.py:466
  68.7 5.0 %collective-permute-start.22 = (bf16[16,32,128]{2,1,0:T(8,128)(2,1)S(1)}, bf16[16,32,128]{2,1,0:T(8,128)(2,1)S(1)}, u32[]{:S(2)}, u32[]{:S(2)}) collective-permute-start(bf16[16,32,128]{2,1,0:T(8,128)(2,1)S(1)} %collective-permute-done.21.refs_6_), channel_id=1, source_target_pairs={{0,4},{4,0},{8,12},{12,8},{16,20},{20,16},{24,28},{28,24},{1,5},{5... | collective-permute-start | bytes 393224 | tf_op jit(solution)/shard_map/ppermute | solution.py:466
  69.2 1.2 collective-permute-start.23
  77.2 7.5 %collective-permute-start.27 = (bf16[17,32,128]{2,1,0:T(8,128)(2,1)S(1)}, bf16[17,32,128]{2,1,0:T(8,128)(2,1)S(1)}, u32[]{:S(2)}, u32[]{:S(2)}) collective-permute-start(bf16[17,32,128]{2,1,0:T(8,128)(2,1)S(1)} %get-tuple-element.111.refs_2_), channel_id=1, source_target_pairs={{0,4},{4,0},{8,12},{12,8},{16,20},{20,16},{24,28},{28,24},{1,5},{5... | collective-permute-start | bytes 417800 | tf_op jit(solution)/shard_map/ppermute | solution.py:466
  77.8 6.9 %collective-permute-start.26 = (bf16[16,32,128]{2,1,0:T(8,128)(2,1)S(1)}, bf16[16,32,128]{2,1,0:T(8,128)(2,1)S(1)}, u32[]{:S(2)}, u32[]{:S(2)}) collective-permute-start(bf16[16,32,128]{2,1,0:T(8,128)(2,1)S(1)} %get-tuple-element.109), channel_id=1, source_target_pairs={{0,4},{4,0},{8,12},{12,8},{16,20},{20,16},{24,28},{28,24},{1,5},{5... | collective-permute-start | bytes 393224 | tf_op jit(solution)/shard_map/ppermute | solution.py:466
  84.8 7.2 %collective-permute-start.28 = (bf16[17,32,128]{2,1,0:T(8,128)(2,1)S(1)}, bf16[17,32,128]{2,1,0:T(8,128)(2,1)S(1)}, u32[]{:S(2)}, u32[]{:S(2)}) collective-permute-start(bf16[17,32,128]{2,1,0:T(8,128)(2,1)S(1)} %fold.12.refs_3_), channel_id=1, source_target_pairs={{0,8},{4,12},{8,0},{12,4},{16,24},{20,28},{24,16},{28,20},{1,9},{5... | collective-permute-start | bytes 417800 | tf_op jit(solution)/shard_map/ppermute | solution.py:466
  84.9 8.0 %collective-permute-start.25 = (bf16[16,32,128]{2,1,0:T(8,128)(2,1)S(1)}, bf16[16,32,128]{2,1,0:T(8,128)(2,1)S(1)}, u32[]{:S(2)}, u32[]{:S(2)}) collective-permute-start(bf16[16,32,128]{2,1,0:T(8,128)(2,1)S(1)} %get-tuple-element.107), channel_id=1, source_target_pairs={{0,4},{4,0},{8,12},{12,8},{16,20},{20,16},{24,28},{28,24},{1,5},{5... | collective-permute-start | bytes 393224 | tf_op jit(solution)/shard_map/ppermute | solution.py:466
  92.2 8.6 %collective-permute-start.30 = (bf16[17,32,128]{2,1,0:T(8,128)(2,1)S(1)}, bf16[17,32,128]{2,1,0:T(8,128)(2,1)S(1)}, u32[]{:S(2)}, u32[]{:S(2)}) collective-permute-start(bf16[17,32,128]{2,1,0:T(8,128)(2,1)S(1)} %get-tuple-element.115.refs_2_.refs_4_), channel_id=1, source_target_pairs={{0,16},{4,20},{8,24},{12,28},{16,0},{20,4},{24,8},{28,12},{1,17},{... | collective-permute-start | bytes 417800 | tf_op jit(solution)/shard_map/ppermute | solution.py:466
  92.2 6.0 %collective-permute-start.24 = (bf16[16,32,128]{2,1,0:T(8,128)(2,1)S(1)}, bf16[16,32,128]{2,1,0:T(8,128)(2,1)S(1)}, u32[]{:S(2)}, u32[]{:S(2)}) collective-permute-start(bf16[16,32,128]{2,1,0:T(8,128)(2,1)S(1)} %get-tuple-element.105), channel_id=1, source_target_pairs={{0,4},{4,0},{8,12},{12,8},{16,20},{20,16},{24,28},{28,24},{1,5},{5... | collective-permute-start | bytes 393224 | tf_op jit(solution)/shard_map/ppermute | solution.py:466
  92.9 7.8 %collective-permute-start.29 = (bf16[16,32,128]{2,1,0:T(8,128)(2,1)S(1)}, bf16[16,32,128]{2,1,0:T(8,128)(2,1)S(1)}, u32[]{:S(2)}, u32[]{:S(2)}) collective-permute-start(bf16[16,32,128]{2,1,0:T(8,128)(2,1)S(1)} %fold.14), channel_id=1, source_target_pairs={{0,8},{4,12},{8,0},{12,4},{16,24},{20,28},{24,16},{28,20},{1,9},{5... | collective-permute-start | bytes 393224 | tf_op jit(solution)/shard_map/ppermute | solution.py:466
  94.3 4.0 %collective-permute-start.31 = (f32[8,128]{1,0:T(8,128)S(1)}, f32[8,128]{1,0:T(8,128)S(1)}, u32[]{:S(2)}, u32[]{:S(2)}) collective-permute-start(f32[8,128]{1,0:T(8,128)S(1)} %get-tuple-element.118.refs_9_), channel_id=1, source_target_pairs={{0,2},{1,3},{2,0},{3,1},{4,6},{5,7},{6,4},{7,5},{8,10},{9,11},{10,... | collective-permute-start | bytes 12296 | tf_op jit(solution)/shard_map/ppermute | solution.py:466
  100.9 8.5 %collective-permute-start.35 = (bf16[16,32,128]{2,1,0:T(8,128)(2,1)S(1)}, bf16[16,32,128]{2,1,0:T(8,128)(2,1)S(1)}, u32[]{:S(2)}, u32[]{:S(2)}) collective-permute-start(bf16[16,32,128]{2,1,0:T(8,128)(2,1)S(1)} %get-tuple-element.119.panel_ref.refs_0_), channel_id=1, source_target_pairs={{0,16},{4,20},{8,24},{12,28},{16,0},{20,4},{24,8},{28,12},{1,17},{... | collective-permute-start | bytes 393224 | tf_op jit(solution)/shard_map/ppermute | solution.py:466
  101.4 8.0 %collective-permute-start.33 = (bf16[16,32,128]{2,1,0:T(8,128)(2,1)S(1)}, bf16[16,32,128]{2,1,0:T(8,128)(2,1)S(1)}, u32[]{:S(2)}, u32[]{:S(2)}) collective-permute-start(bf16[16,32,128]{2,1,0:T(8,128)(2,1)S(1)} %get-tuple-element.119.panel_ref.refs_0_), channel_id=1, source_target_pairs={{0,8},{4,12},{8,0},{12,4},{16,24},{20,28},{24,16},{28,20},{1,9},{5... | collective-permute-start | bytes 393224 | tf_op jit(solution)/shard_map/ppermute | solution.py:466
  103.8 5.8 %collective-permute-start.32 = (bf16[16,32,128]{2,1,0:T(8,128)(2,1)S(1)}, bf16[16,32,128]{2,1,0:T(8,128)(2,1)S(1)}, u32[]{:S(2)}, u32[]{:S(2)}) collective-permute-start(bf16[16,32,128]{2,1,0:T(8,128)(2,1)S(1)} %get-tuple-element.119.panel_ref.refs_0_), channel_id=1, source_target_pairs={{0,4},{4,0},{8,12},{12,8},{16,20},{20,16},{24,28},{28,24},{1,5},{5... | collective-permute-start | bytes 393224 | tf_op jit(solution)/shard_map/ppermute | solution.py:466
  109.7 5.0 %collective-permute-start.37 = (bf16[16,32,128]{2,1,0:T(8,128)(2,1)S(1)}, bf16[16,32,128]{2,1,0:T(8,128)(2,1)S(1)}, u32[]{:S(2)}, u32[]{:S(2)}) collective-permute-start(bf16[16,32,128]{2,1,0:T(8,128)(2,1)S(1)} %get-tuple-element.122.refs_4_), channel_id=1, source_target_pairs={{0,8},{4,12},{8,0},{12,4},{16,24},{20,28},{24,16},{28,20},{1,9},{5... | collective-permute-start | bytes 393224 | tf_op jit(solution)/shard_map/ppermute | solution.py:466
  110.4 6.6 %collective-permute-start.36 = (bf16[16,32,128]{2,1,0:T(8,128)(2,1)S(1)}, bf16[16,32,128]{2,1,0:T(8,128)(2,1)S(1)}, u32[]{:S(2)}, u32[]{:S(2)}) collective-permute-start(bf16[16,32,128]{2,1,0:T(8,128)(2,1)S(1)} %get-tuple-element.122.refs_4_), channel_id=1, source_target_pairs={{0,4},{4,0},{8,12},{12,8},{16,20},{20,16},{24,28},{28,24},{1,5},{5... | collective-permute-start | bytes 393224 | tf_op jit(solution)/shard_map/ppermute | solution.py:466
  111.5 5.4 %collective-permute-start.34 = (bf16[16,32,128]{2,1,0:T(8,128)(2,1)S(1)}, bf16[16,32,128]{2,1,0:T(8,128)(2,1)S(1)}, u32[]{:S(2)}, u32[]{:S(2)}) collective-permute-start(bf16[16,32,128]{2,1,0:T(8,128)(2,1)S(1)} %collective-permute-done.33.refs_1_.refs_2_), channel_id=1, source_target_pairs={{0,4},{4,0},{8,12},{12,8},{16,20},{20,16},{24,28},{28,24},{1,5},{5... | collective-permute-start | bytes 393224 | tf_op jit(solution)/shard_map/ppermute | solution.py:466
  114.7 5.0 %collective-permute-start.38 = (bf16[16,32,128]{2,1,0:T(8,128)(2,1)S(1)}, bf16[16,32,128]{2,1,0:T(8,128)(2,1)S(1)}, u32[]{:S(2)}, u32[]{:S(2)}) collective-permute-start(bf16[16,32,128]{2,1,0:T(8,128)(2,1)S(1)} %collective-permute-done.37.refs_6_), channel_id=1, source_target_pairs={{0,4},{4,0},{8,12},{12,8},{16,20},{20,16},{24,28},{28,24},{1,5},{5... | collective-permute-start | bytes 393224 | tf_op jit(solution)/shard_map/ppermute | solution.py:466
  115.8 1.2 collective-permute-start.39
  123.9 6.9 %collective-permute-start.43 = (bf16[17,32,128]{2,1,0:T(8,128)(2,1)S(1)}, bf16[17,32,128]{2,1,0:T(8,128)(2,1)S(1)}, u32[]{:S(2)}, u32[]{:S(2)}) collective-permute-start(bf16[17,32,128]{2,1,0:T(8,128)(2,1)S(1)} %get-tuple-element.135.refs_2_), channel_id=1, source_target_pairs={{0,4},{4,0},{8,12},{12,8},{16,20},{20,16},{24,28},{28,24},{1,5},{5... | collective-permute-start | bytes 417800 | tf_op jit(solution)/shard_map/ppermute | solution.py:466
  124.9 5.9 %collective-permute-start.42 = (bf16[16,32,128]{2,1,0:T(8,128)(2,1)S(1)}, bf16[16,32,128]{2,1,0:T(8,128)(2,1)S(1)}, u32[]{:S(2)}, u32[]{:S(2)}) collective-permute-start(bf16[16,32,128]{2,1,0:T(8,128)(2,1)S(1)} %get-tuple-element.133), channel_id=1, source_target_pairs={{0,4},{4,0},{8,12},{12,8},{16,20},{20,16},{24,28},{28,24},{1,5},{5... | collective-permute-start | bytes 393224 | tf_op jit(solution)/shard_map/ppermute | solution.py:466
  130.9 7.8 %collective-permute-start.44 = (bf16[17,32,128]{2,1,0:T(8,128)(2,1)S(1)}, bf16[17,32,128]{2,1,0:T(8,128)(2,1)S(1)}, u32[]{:S(2)}, u32[]{:S(2)}) collective-permute-start(bf16[17,32,128]{2,1,0:T(8,128)(2,1)S(1)} %fold.15.refs_3_), channel_id=1, source_target_pairs={{0,8},{4,12},{8,0},{12,4},{16,24},{20,28},{24,16},{28,20},{1,9},{5... | collective-permute-start | bytes 417800 | tf_op jit(solution)/shard_map/ppermute | solution.py:466
  131.1 9.4 %collective-permute-start.41 = (bf16[16,32,128]{2,1,0:T(8,128)(2,1)S(1)}, bf16[16,32,128]{2,1,0:T(8,128)(2,1)S(1)}, u32[]{:S(2)}, u32[]{:S(2)}) collective-permute-start(bf16[16,32,128]{2,1,0:T(8,128)(2,1)S(1)} %get-tuple-element.131), channel_id=1, source_target_pairs={{0,4},{4,0},{8,12},{12,8},{16,20},{20,16},{24,28},{28,24},{1,5},{5... | collective-permute-start | bytes 393224 | tf_op jit(solution)/shard_map/ppermute | solution.py:466
  138.8 7.9 %collective-permute-start.46 = (bf16[17,32,128]{2,1,0:T(8,128)(2,1)S(1)}, bf16[17,32,128]{2,1,0:T(8,128)(2,1)S(1)}, u32[]{:S(2)}, u32[]{:S(2)}) collective-permute-start(bf16[17,32,128]{2,1,0:T(8,128)(2,1)S(1)} %get-tuple-element.139.refs_2_.refs_4_), channel_id=1, source_target_pairs={{0,16},{4,20},{8,24},{12,28},{16,0},{20,4},{24,8},{28,12},{1,17},{... | collective-permute-start | bytes 417800 | tf_op jit(solution)/shard_map/ppermute | solution.py:466
  138.9 5.7 %collective-permute-start.40 = (bf16[16,32,128]{2,1,0:T(8,128)(2,1)S(1)}, bf16[16,32,128]{2,1,0:T(8,128)(2,1)S(1)}, u32[]{:S(2)}, u32[]{:S(2)}) collective-permute-start(bf16[16,32,128]{2,1,0:T(8,128)(2,1)S(1)} %get-tuple-element.129), channel_id=1, source_target_pairs={{0,4},{4,0},{8,12},{12,8},{16,20},{20,16},{24,28},{28,24},{1,5},{5... | collective-permute-start | bytes 393224 | tf_op jit(solution)/shard_map/ppermute | solution.py:466
  140.5 6.2 %collective-permute-start.45 = (bf16[16,32,128]{2,1,0:T(8,128)(2,1)S(1)}, bf16[16,32,128]{2,1,0:T(8,128)(2,1)S(1)}, u32[]{:S(2)}, u32[]{:S(2)}) collective-permute-start(bf16[16,32,128]{2,1,0:T(8,128)(2,1)S(1)} %fold.17), channel_id=1, source_target_pairs={{0,8},{4,12},{8,0},{12,4},{16,24},{20,28},{24,16},{28,20},{1,9},{5... | collective-permute-start | bytes 393224 | tf_op jit(solution)/shard_map/ppermute | solution.py:466
  143.1 3.6 %collective-permute-start.47 = (f32[8,128]{1,0:T(8,128)S(1)}, f32[8,128]{1,0:T(8,128)S(1)}, u32[]{:S(2)}, u32[]{:S(2)}) collective-permute-start(f32[8,128]{1,0:T(8,128)S(1)} %get-tuple-element.142.refs_9_), channel_id=1, source_target_pairs={{0,2},{1,3},{2,0},{3,1},{4,6},{5,7},{6,4},{7,5},{8,10},{9,11},{10,... | collective-permute-start | bytes 12296 | tf_op jit(solution)/shard_map/ppermute | solution.py:466

commit v10 on v8

--- a/solution.py
+++ b/solution.py
@@ -16,7 +16,7 @@
 
 MIB = 1024 * 1024
 GROUP = 8
-HEAD_GROUP = 16
+HEAD_GROUP = 32
 SMALL_VMEM = 6 * MIB
 
 
@@ -528,8 +528,8 @@
         tops = sorted(inner(net_size), key=lambda k: (-k.bit_count(), -k))[:-1]
         groups = [(top,) for top in tops if top != 1] + [(1,)]
         loss, loss_top = sends[net_size - 1], net_size - 1
-        ahead = {5: swap(sends[5], "net", last_hop(5))}
-        after = (ahead[5], base)
+        ahead = {k: swap(sends[k], "net", last_hop(k)) for k in (5, 2)}
+        after = (ahead[5], ahead[2], base)
         for group in groups:
             terms = []
             for top in group:
@@ -541,9 +541,11 @@
                     )
                 )
             chain = loss_top ^ last_hop(loss_top) == group[0]
-            sums = (risk_sum,) if group[0] == net_size // 2 else ()
+            sums = (risk_sum,) if group[0] == tops[0] else ()
             if group == (1,):
                 after = (loss,)
+            if group[0] == net_size // 2:
+                after = risk_sums[1:]
             folded, passed = fold(terms, loss if chain else None, sums, after)
             sends.update(zip(group, folded))
             after = ()
@@ -551,11 +553,11 @@
                 loss_top, loss = group[0], folded[0]
             if sums:
                 (risk_sum,) = passed
+                for stride in strides[:-1]:
+                    risk_sum = risk_sum + swap(risk_sum, "scen", stride)
+                risk_sums = (risk_sum, swap(risk_sum, "scen", strides[-1]))
         below = sorted(children(0, net_size))
-        arrived = [swap(sends[k], "net", last_hop(k)) for k in below]
-        for stride in strides[:-1]:
-            risk_sum = risk_sum + swap(risk_sum, "scen", stride)
-        sums = (risk_sum, swap(risk_sum, "scen", strides[-1]))
+        arrived = [ahead[k] if k in ahead else swap(sends[k], "net", last_hop(k)) for k in below]
         duals, half, risk, excess_now, level, risk_sum = settle(
             kept[0],
             arrived,
@@ -564,7 +566,7 @@
             risk,
             excess_now,
             level,
-            sums,
+            risk_sums,
             arc_total,
             scen_total,
             last,

time: 143 us -> 142 us (level)
  waiting for transfers between devices: 53.5 us -> 49 us
  starting transfers between devices: 46 us -> 50 us
    ppermute x48, waiting for transfers between devices: 53.5 us -> 49 us  [swap(): return lax.ppermute(value, axis, [(i, i ^ distance) for i in range(size)])]
    ppermute x48, starting transfers between devices: 46 us -> 50 us  [swap(): return lax.ppermute(value, axis, [(i, i ^ distance) for i in range(size)])]
  transfers between devices with their start and end apart: 48 -> 48, of which waited for: 34 -> 35; matrix products, arithmetic and copies ran while one was open for 0% -> 0% of each run, Pallas kernels for 17% -> 17%
where the time goes in v10:
time: 142 us; the launch traced here: 141 us
  starting transfers between devices  50 us (35%)
  waiting for transfers between devices  49 us (35%)
  Pallas kernels  35.8 us (25%)
  local copies, waits for them, and re-layouts  5.05 us (4%)
  between operations  1.6 us (1%)
    ppermute x48, starting transfers between devices, swap(): return lax.ppermute(value, axis, [(i, i ^ distance) for i in range(size)])  50 us
    ppermute x48, waiting for transfers between devices, swap(): return lax.ppermute(value, axis, [(i, i ^ distance) for i in range(size)])  49 us
    pallas_call x3, Pallas kernels, local_adjoint(): pl.pallas_call(functools.partial(local_adjoint_kernel, touches, group), o...  12.9 us
    pallas_call x3, Pallas kernels, head_step(): pl.pallas_call(functools.partial(head_kernel, group, steps, peers), out_s...  10.2 us
    pallas_call x3, Pallas kernels, local_forward(): pl.pallas_call(functools.partial(local_forward_kernel, touches, group, st...  9.99 us
    unnamed x26, local copies, waits for them, and re-layouts  5.01 us
  transfers between devices with their start and end apart: 48, of which 35 were waited for; matrix products, arithmetic and copies ran while one was open for 0% of the time, Pallas kernels for 17%

profile of v10, /device:TPU:0, one launch (start us, length us, event | category | flops | bytes accessed | tf_op | source)
XLA Modules:
  0.0 141.4 jit_solution(15538711951832075296)
XLA Ops:
  0.7 0.9 copy-done
  1.6 4.1 %collective-permute-start = (bf16[16,32,128]{2,1,0:T(8,128)(2,1)S(1)}, bf16[16,32,128]{2,1,0:T(8,128)(2,1)S(1)}, u32[]{:S(2)}, u32[]{:S(2)}) collective-permute-start(bf16[16,32,128]{2,1,0:T(8,128)(2,1)S(1)} %fusion.panel_ref.refs_0_), channel_id=1, source_target_pairs={{0,16},{4,20},{8,24},{12,28},{16,0},{20,4},{24,8},{28,12},{1,17},{... | collective-permute-start | bytes 393224 | tf_op jit(solution)/shard_map/ppermute | solution.py:466
  5.7 1.5 %collective-permute-start.1 = (bf16[16,32,128]{2,1,0:T(8,128)(2,1)S(1)}, bf16[16,32,128]{2,1,0:T(8,128)(2,1)S(1)}, u32[]{:S(2)}, u32[]{:S(2)}) collective-permute-start(bf16[16,32,128]{2,1,0:T(8,128)(2,1)S(1)} %fusion.panel_ref.refs_0_), channel_id=1, source_target_pairs={{0,4},{4,0},{8,12},{12,8},{16,20},{20,16},{24,28},{28,24},{1,5},{5... | collective-permute-start | bytes 393224 | tf_op jit(solution)/shard_map/ppermute | solution.py:466
  7.2 3.4 %copy-done.1 = bf16[64,4,128,128]{3,2,1,0:T(8,128)(2,1)S(1)} copy-done((bf16[64,4,128,128]{3,2,1,0:T(8,128)(2,1)S(1)}, bf16[64,4,128,128]{3,2,1,0:T(8,128)(2,1)}, u32[]{:S(2)}) %copy-start.1) | copy-done | bytes 8388632
  11.3 4.3 %local_adjoint.3 = (f32[32,8192]{1,0:T(8,128)S(1)}, f32[8,128]{1,0:T(8,128)S(1)}) custom-call(s32[4,64]{1,0:T(4,128)S(1)} %bitcast.29, bf16[16,32,128]{2,1,0:T(8,128)(2,1)S(1)} %fusion.panel_ref.refs_0_, bf16[64,4,128,128]{3,2,1,0:T(8,128)(2,1)S(1)} %copy-done.1), custom_call_target="tpu_custom_call" | custom-call | flops 268435456 | bytes 8388608 | tf_op jit(solution)/shard_map/local_adjoint/pallas_call | solution.py:255
  16.2 1.6 %collective-permute-start.5 = (bf16[16,32,128]{2,1,0:T(8,128)(2,1)S(1)}, bf16[16,32,128]{2,1,0:T(8,128)(2,1)S(1)}, u32[]{:S(2)}, u32[]{:S(2)}) collective-permute-start(bf16[16,32,128]{2,1,0:T(8,128)(2,1)S(1)} %get-tuple-element.77.refs_0_.refs_4_), channel_id=1, source_target_pairs={{0,8},{4,12},{8,0},{12,4},{16,24},{20,28},{24,16},{28,20},{1,9},{5... | collective-permute-start | bytes 393224 | tf_op jit(solution)/shard_map/ppermute | solution.py:466
  18.8 1.6 %collective-permute-start.3 = (bf16[16,32,128]{2,1,0:T(8,128)(2,1)S(1)}, bf16[16,32,128]{2,1,0:T(8,128)(2,1)S(1)}, u32[]{:S(2)}, u32[]{:S(2)}) collective-permute-start(bf16[16,32,128]{2,1,0:T(8,128)(2,1)S(1)} %collective-permute-done.1.refs_1_), channel_id=1, source_target_pairs={{0,8},{4,12},{8,0},{12,4},{16,24},{20,28},{24,16},{28,20},{1,9},{5... | collective-permute-start | bytes 393224 | tf_op jit(solution)/shard_map/ppermute | solution.py:466
  20.4 2.3 %collective-permute-done.5.refs_6_ = bf16[16,32,128]{2,1,0:T(8,128)(2,1)S(1)} collective-permute-done((bf16[16,32,128]{2,1,0:T(8,128)(2,1)S(1)}, bf16[16,32,128]{2,1,0:T(8,128)(2,1)S(1)}, u32[]{:S(2)}, u32[]{:S(2)}) %collective-permute-start.5) | collective-permute-done | bytes 131104 | tf_op jit(solution)/shard_map/ppermute | solution.py:466
  24.1 1.0 collective-permute-done.2.refs_2_
  25.2 1.3 collective-permute-done.3.refs_3_
  26.5 1.1 collective-permute-done.6.refs_7_
  27.6 3.2 %head_step.3 = (f32[32,8192]{1,0:T(8,128)S(1)}, bf16[32,8192]{1,0:T(8,128)(2,1)S(1)}, f32[8,128]{1,0:T(8,128)S(1)}, f32[16,32,128]{2,1,0:T(8,128)S(1)}, f32[16,3...) custom-call(s32[64]{0:T(128)S(1)} %bitcast.35, ...), custom_call_target="tpu_custom_call" | custom-call | flops 134217728 | bytes 7864320 | tf_op jit(solution)/shard_map/head_step/pallas_call | solution.py:292
  31.4 1.6 %collective-permute-start.11 = (bf16[16,32,128]{2,1,0:T(8,128)(2,1)S(1)}, bf16[16,32,128]{2,1,0:T(8,128)(2,1)S(1)}, u32[]{:S(2)}, u32[]{:S(2)}) collective-permute-start(bf16[16,32,128]{2,1,0:T(8,128)(2,1)S(1)} %get-tuple-element.90), channel_id=1, source_target_pairs={{0,8},{4,12},{8,0},{12,4},{16,24},{20,28},{24,16},{28,20},{1,9},{5... | collective-permute-start | bytes 393224 | tf_op jit(solution)/shard_map/ppermute | solution.py:466
  33.0 1.5 %collective-permute-start.10 = (bf16[17,32,128]{2,1,0:T(8,128)(2,1)S(1)}, bf16[17,32,128]{2,1,0:T(8,128)(2,1)S(1)}, u32[]{:S(2)}, u32[]{:S(2)}) collective-permute-start(bf16[17,32,128]{2,1,0:T(8,128)(2,1)S(1)} %get-tuple-element.88.refs_2_), channel_id=1, source_target_pairs={{0,4},{4,0},{8,12},{12,8},{16,20},{20,16},{24,28},{28,24},{1,5},{5... | collective-permute-start | bytes 417800 | tf_op jit(solution)/shard_map/ppermute | solution.py:466
  34.5 3.3 %local_forward.3.refs_6_.refs_5_ = f32[16,32,128]{2,1,0:T(8,128)S(1)} custom-call(s32[4,64]{1,0:T(4,128)S(1)} %bitcast.30, bf16[32,8192]{1,0:T(8,128)(2,1)S(1)} %get-tuple-element.91.bar_ref, bf16[64,4,128,128]{3,2,1,0:T(8,128)(2,1)S(1)} %bitcast.25, f32[16,32,128]{2,1,0:T(8,128)S(1)} %bitcast_bitcast_fusion.duals_ref, f32[32,2048]{1,0:T(8,128)S(1)} %copy-done.4), custom_call_target="tpu_custom_call" | custom-call | flops 268435456 | bytes 8388608 | tf_op jit(solution)/shard_map/local_forward/pallas_call | solution.py:390
  39.1 1.3 collective-permute-start.8
  40.4 1.5 %collective-permute-start.13 = (f32[8,128]{1,0:T(8,128)S(1)}, f32[8,128]{1,0:T(8,128)S(1)}, u32[]{:S(2)}, u32[]{:S(2)}) collective-permute-start(f32[8,128]{1,0:T(8,128)S(1)} %get-tuple-element.93.refs_9_), channel_id=1, source_target_pairs={{0,2},{1,3},{2,0},{3,1},{4,6},{5,7},{6,4},{7,5},{8,10},{9,11},{10,... | collective-permute-start | bytes 12296 | tf_op jit(solution)/shard_map/ppermute | solution.py:466
  41.9 2.1 %collective-permute-done.13.refs_4_.refs_10_ = f32[8,128]{1,0:T(8,128)S(1)} collective-permute-done((f32[8,128]{1,0:T(8,128)S(1)}, f32[8,128]{1,0:T(8,128)S(1)}, u32[]{:S(2)}, u32[]{:S(2)}) %collective-permute-start.13) | collective-permute-done | bytes 4128 | tf_op jit(solution)/shard_map/ppermute | solution.py:466
  44.5 1.1 collective-permute-done.8.refs_1_
  45.6 2.0 %collective-permute-start.14 = (bf16[16,32,128]{2,1,0:T(8,128)(2,1)S(1)}, bf16[16,32,128]{2,1,0:T(8,128)(2,1)S(1)}, u32[]{:S(2)}, u32[]{:S(2)}) collective-permute-start(bf16[16,32,128]{2,1,0:T(8,128)(2,1)S(1)} %fold.11), channel_id=1, source_target_pairs={{0,4},{4,0},{8,12},{12,8},{16,20},{20,16},{24,28},{28,24},{1,5},{5... | collective-permute-start | bytes 393224 | tf_op jit(solution)/shard_map/ppermute | solution.py:466
  47.6 4.0 %collective-permute-done.14.refs_1_ = bf16[16,32,128]{2,1,0:T(8,128)(2,1)S(1)} collective-permute-done((bf16[16,32,128]{2,1,0:T(8,128)(2,1)S(1)}, bf16[16,32,128]{2,1,0:T(8,128)(2,1)S(1)}, u32[]{:S(2)}, u32[]{:S(2)}) %collective-permute-start.14) | collective-permute-done | bytes 131104 | tf_op jit(solution)/shard_map/ppermute | solution.py:466
  51.7 2.5 %collective-permute-done.15.refs_3_ = bf16[17,32,128]{2,1,0:T(8,128)(2,1)S(1)} collective-permute-done((bf16[17,32,128]{2,1,0:T(8,128)(2,1)S(1)}, bf16[17,32,128]{2,1,0:T(8,128)(2,1)S(1)}, u32[]{:S(2)}, u32[]{:S(2)}) %collective-permute-start.15) | collective-permute-done | bytes 139296 | tf_op jit(solution)/shard_map/ppermute | solution.py:466
  54.5 1.3 collective-permute-start.16
  55.8 4.3 %local_adjoint.4 = (f32[32,8192]{1,0:T(8,128)S(1)}, f32[8,128]{1,0:T(8,128)S(1)}) custom-call(s32[4,64]{1,0:T(4,128)S(1)} %bitcast.31, bf16[16,32,128]{2,1,0:T(8,128)(2,1)S(1)} %get-tuple-element.96.panel_ref.refs_0_, bf16[64,4,128,128]{3,2,1,0:T(8,128)(2,1)S(1)} %bitcast.25), custom_call_target="tpu_custom_call" | custom-call | flops 268435456 | bytes 8388608 | tf_op jit(solution)/shard_map/local_adjoint/pallas_call | solution.py:255
  61.0 2.0 %collective-permute-start.17 = (bf16[16,32,128]{2,1,0:T(8,128)(2,1)S(1)}, bf16[16,32,128]{2,1,0:T(8,128)(2,1)S(1)}, u32[]{:S(2)}, u32[]{:S(2)}) collective-permute-start(bf16[16,32,128]{2,1,0:T(8,128)(2,1)S(1)} %get-tuple-element.96.panel_ref.refs_0_), channel_id=1, source_target_pairs={{0,8},{4,12},{8,0},{12,4},{16,24},{20,28},{24,16},{28,20},{1,9},{5... | collective-permute-start | bytes 393224 | tf_op jit(solution)/shard_map/ppermute | solution.py:466
  63.0 1.3 collective-permute-start.20
  64.4 1.6 %collective-permute-done.21.refs_6_ = bf16[16,32,128]{2,1,0:T(8,128)(2,1)S(1)} collective-permute-done((bf16[16,32,128]{2,1,0:T(8,128)(2,1)S(1)}, bf16[16,32,128]{2,1,0:T(8,128)(2,1)S(1)}, u32[]{:S(2)}, u32[]{:S(2)}) %collective-permute-start.21) | collective-permute-done | bytes 131104 | tf_op jit(solution)/shard_map/ppermute | solution.py:466
  65.9 1.3 collective-permute-start.22
  67.3 1.1 collective-permute-done.23.refs_14_
  68.4 0.9 collective-permute-done.18.refs_3_
  69.2 1.6 %collective-permute-done.22.refs_7_ = bf16[16,32,128]{2,1,0:T(8,128)(2,1)S(1)} collective-permute-done((bf16[16,32,128]{2,1,0:T(8,128)(2,1)S(1)}, bf16[16,32,128]{2,1,0:T(8,128)(2,1)S(1)}, u32[]{:S(2)}, u32[]{:S(2)}) %collective-permute-start.22) | collective-permute-done | bytes 131104 | tf_op jit(solution)/shard_map/ppermute | solution.py:466
  70.9 3.2 %head_step.4 = (f32[32,8192]{1,0:T(8,128)S(1)}, bf16[32,8192]{1,0:T(8,128)(2,1)S(1)}, f32[8,128]{1,0:T(8,128)S(1)}, f32[16,32,128]{2,1,0:T(8,128)S(1)}, f32[16,3...) custom-call(s32[64]{0:T(128)S(1)} %bitcast.36, ...), custom_call_target="tpu_custom_call" | custom-call | flops 134217728 | bytes 7864320 | tf_op jit(solution)/shard_map/head_step/pallas_call | solution.py:292
  74.1 1.4 collective-permute-start.26
  76.6 3.3 %local_forward.4.refs_6_.refs_5_ = f32[16,32,128]{2,1,0:T(8,128)S(1)} custom-call(s32[4,64]{1,0:T(4,128)S(1)} %bitcast.32, bf16[32,8192]{1,0:T(8,128)(2,1)S(1)} %get-tuple-element.113.bar_ref, bf16[64,4,128,128]{3,2,1,0:T(8,128)(2,1)S(1)} %bitcast.25, f32[16,32,128]{2,1,0:T(8,128)S(1)} %get-tuple-element.114.duals_ref, f32[32,2048]{1,0:T(8,128)S(1)} %copy-done.4), custom_call_target="tpu_custom_call" | custom-call | flops 268435456 | bytes 8388608 | tf_op jit(solution)/shard_map/local_forward/pallas_call | solution.py:390
  80.6 1.8 %collective-permute-done.27.refs_5_.refs_2_ = bf16[16,32,128]{2,1,0:T(8,128)(2,1)S(1)} collective-permute-done((bf16[16,32,128]{2,1,0:T(8,128)(2,1)S(1)}, bf16[16,32,128]{2,1,0:T(8,128)(2,1)S(1)}, u32[]{:S(2)}, u32[]{:S(2)}) %collective-permute-start.27) | collective-permute-done | bytes 131104 | tf_op jit(solution)/shard_map/ppermute | solution.py:466
  82.5 2.0 %collective-permute-start.24 = (bf16[16,32,128]{2,1,0:T(8,128)(2,1)S(1)}, bf16[16,32,128]{2,1,0:T(8,128)(2,1)S(1)}, u32[]{:S(2)}, u32[]{:S(2)}) collective-permute-start(bf16[16,32,128]{2,1,0:T(8,128)(2,1)S(1)} %get-tuple-element.106), channel_id=1, source_target_pairs={{0,8},{4,12},{8,0},{12,4},{16,24},{20,28},{24,16},{28,20},{1,9},{5... | collective-permute-start | bytes 393224 | tf_op jit(solution)/shard_map/ppermute | solution.py:466
  84.5 1.6 %collective-permute-start.29 = (f32[8,128]{1,0:T(8,128)S(1)}, f32[8,128]{1,0:T(8,128)S(1)}, u32[]{:S(2)}, u32[]{:S(2)}) collective-permute-start(f32[8,128]{1,0:T(8,128)S(1)} %get-tuple-element.116.refs_9_), channel_id=1, source_target_pairs={{0,2},{1,3},{2,0},{3,1},{4,6},{5,7},{6,4},{7,5},{8,10},{9,11},{10,... | collective-permute-start | bytes 12296 | tf_op jit(solution)/shard_map/ppermute | solution.py:466
  86.2 2.0 %collective-permute-done.29.refs_4_.refs_10_ = f32[8,128]{1,0:T(8,128)S(1)} collective-permute-done((f32[8,128]{1,0:T(8,128)S(1)}, f32[8,128]{1,0:T(8,128)S(1)}, u32[]{:S(2)}, u32[]{:S(2)}) %collective-permute-start.29) | collective-permute-done | bytes 4128 | tf_op jit(solution)/shard_map/ppermute | solution.py:466
  88.2 0.9 collective-permute-done.28.refs_2_
  89.2 1.3 collective-permute-start.31
  90.6 1.4 collective-permute-start.30
  91.9 4.2 %collective-permute-done.30.refs_1_ = bf16[16,32,128]{2,1,0:T(8,128)(2,1)S(1)} collective-permute-done((bf16[16,32,128]{2,1,0:T(8,128)(2,1)S(1)}, bf16[16,32,128]{2,1,0:T(8,128)(2,1)S(1)}, u32[]{:S(2)}, u32[]{:S(2)}) %collective-permute-start.30) | collective-permute-done | bytes 131104 | tf_op jit(solution)/shard_map/ppermute | solution.py:466
  96.1 1.5 %collective-permute-done.31.refs_3_ = bf16[17,32,128]{2,1,0:T(8,128)(2,1)S(1)} collective-permute-done((bf16[17,32,128]{2,1,0:T(8,128)(2,1)S(1)}, bf16[17,32,128]{2,1,0:T(8,128)(2,1)S(1)}, u32[]{:S(2)}, u32[]{:S(2)}) %collective-permute-start.31) | collective-permute-done | bytes 139296 | tf_op jit(solution)/shard_map/ppermute | solution.py:466
  97.9 1.2 collective-permute-start.32
  99.1 4.3 %local_adjoint.5 = (f32[32,8192]{1,0:T(8,128)S(1)}, f32[8,128]{1,0:T(8,128)S(1)}) custom-call(s32[4,64]{1,0:T(4,128)S(1)} %bitcast.33, bf16[16,32,128]{2,1,0:T(8,128)(2,1)S(1)} %get-tuple-element.119.panel_ref.refs_0_, bf16[64,4,128,128]{3,2,1,0:T(8,128)(2,1)S(1)} %bitcast.25), custom_call_target="tpu_custom_call" | custom-call | flops 268435456 | bytes 8388608 | tf_op jit(solution)/shard_map/local_adjoint/pallas_call | solution.py:255
  103.3 1.5 %collective-permute-done.35.arrived_ref = bf16[16,32,128]{2,1,0:T(8,128)(2,1)S(1)} collective-permute-done((bf16[16,32,128]{2,1,0:T(8,128)(2,1)S(1)}, bf16[16,32,128]{2,1,0:T(8,128)(2,1)S(1)}, u32[]{:S(2)}, u32[]{:S(2)}) %collective-permute-start.35) | collective-permute-done | bytes 131104 | tf_op jit(solution)/shard_map/ppermute | solution.py:466
  105.6 1.3 collective-permute-start.33
  107.0 0.9 collective-permute-start.36
  107.9 1.0 collective-permute-start.34
  108.9 1.0 collective-permute-done.37.refs_6_
  109.9 0.9 collective-permute-start.38
  112.0 0.9 collective-permute-done.34.refs_3_
  112.9 2.0 %collective-permute-done.38.refs_7_ = bf16[16,32,128]{2,1,0:T(8,128)(2,1)S(1)} collective-permute-done((bf16[16,32,128]{2,1,0:T(8,128)(2,1)S(1)}, bf16[16,32,128]{2,1,0:T(8,128)(2,1)S(1)}, u32[]{:S(2)}, u32[]{:S(2)}) %collective-permute-start.38) | collective-permute-done | bytes 131104 | tf_op jit(solution)/shard_map/ppermute | solution.py:466
  114.9 3.9 %head_step.5 = (f32[32,8192]{1,0:T(8,128)}, bf16[32,8192]{1,0:T(8,128)(2,1)S(1)}, f32[8,128]{1,0:T(8,128)S(1)}, f32[16,32,128]{2,1,0:T(8,128)S(1)}, f32[16,32,12...) custom-call(s32[64]{0:T(128)S(1)} %bitcast.37, ...), custom_call_target="tpu_custom_call" | custom-call | flops 134217728 | bytes 7864320 | tf_op jit(solution)/shard_map/head_step/pallas_call | solution.py:292
  118.7 0.9 collective-permute-start.42
  119.7 1.1 collective-permute-start.41
  121.5 3.3 %local_forward.5.refs_6_.refs_5_ = f32[16,32,128]{2,1,0:T(8,128)S(1)} custom-call(s32[4,64]{1,0:T(4,128)S(1)} %bitcast.34, bf16[32,8192]{1,0:T(8,128)(2,1)S(1)} %get-tuple-element.137.bar_ref, bf16[64,4,128,128]{3,2,1,0:T(8,128)(2,1)S(1)} %bitcast.25, f32[16,32,128]{2,1,0:T(8,128)S(1)} %get-tuple-element.138.duals_ref, f32[32,2048]{1,0:T(8,128)S(1)} %copy-done.4), custom_call_target="tpu_custom_call" | custom-call | flops 268435456 | bytes 8388608 | tf_op jit(solution)/shard_map/local_forward/pallas_call | solution.py:390
  125.2 1.8 %collective-permute-done.43.refs_5_.refs_2_ = bf16[16,32,128]{2,1,0:T(8,128)(2,1)S(1)} collective-permute-done((bf16[16,32,128]{2,1,0:T(8,128)(2,1)S(1)}, bf16[16,32,128]{2,1,0:T(8,128)(2,1)S(1)}, u32[]{:S(2)}, u32[]{:S(2)}) %collective-permute-start.43) | collective-permute-done | bytes 131104 | tf_op jit(solution)/shard_map/ppermute | solution.py:466
  127.7 1.5 %collective-permute-start.40 = (bf16[16,32,128]{2,1,0:T(8,128)(2,1)S(1)}, bf16[16,32,128]{2,1,0:T(8,128)(2,1)S(1)}, u32[]{:S(2)}, u32[]{:S(2)}) collective-permute-start(bf16[16,32,128]{2,1,0:T(8,128)(2,1)S(1)} %get-tuple-element.130), channel_id=1, source_target_pairs={{0,8},{4,12},{8,0},{12,4},{16,24},{20,28},{24,16},{28,20},{1,9},{5... | collective-permute-start | bytes 393224 | tf_op jit(solution)/shard_map/ppermute | solution.py:466
  129.2 1.3 collective-permute-start.45
  130.6 2.3 %collective-permute-done.45.refs_4_.refs_10_ = f32[8,128]{1,0:T(8,128)S(1)} collective-permute-done((f32[8,128]{1,0:T(8,128)S(1)}, f32[8,128]{1,0:T(8,128)S(1)}, u32[]{:S(2)}, u32[]{:S(2)}) %collective-permute-start.45) | collective-permute-done | bytes 4128 | tf_op jit(solution)/shard_map/ppermute | solution.py:466
  133.1 1.5 %collective-permute-start.47 = (bf16[17,32,128]{2,1,0:T(8,128)(2,1)S(1)}, bf16[17,32,128]{2,1,0:T(8,128)(2,1)S(1)}, u32[]{:S(2)}, u32[]{:S(2)}) collective-permute-start(bf16[17,32,128]{2,1,0:T(8,128)(2,1)S(1)} %fold.16.refs_2_.refs_4_), channel_id=1, source_target_pairs={{0,16},{4,20},{8,24},{12,28},{16,0},{20,4},{24,8},{28,12},{1,17},{... | collective-permute-start | bytes 417800 | tf_op jit(solution)/shard_map/ppermute | solution.py:466
  135.2 1.1 collective-permute-start.46
  136.3 3.9 %collective-permute-done.46.refs_1_ = bf16[16,32,128]{2,1,0:T(8,128)(2,1)S(1)} collective-permute-done((bf16[16,32,128]{2,1,0:T(8,128)(2,1)S(1)}, bf16[16,32,128]{2,1,0:T(8,128)(2,1)S(1)}, u32[]{:S(2)}, u32[]{:S(2)}) %collective-permute-start.46) | collective-permute-done | bytes 131104 | tf_op jit(solution)/shard_map/ppermute | solution.py:466
  (86 shorter events, 15.0 us)
Async XLA Ops:
  0.6 1.0 copy-start
  0.6 23.2 %copy-start.10 = (s32[64]{0:T(128)S(1)}, s32[64]{0:T(128)}, u32[]{:S(2)}) copy-start(s32[64]{0:T(128)} %param.21) | copy-start | bytes 772
  0.7 23.2 %copy-start.8 = (f32[32]{0:T(128)S(1)}, f32[32]{0:T(128)}, u32[]{:S(2)}) copy-start(f32[32]{0:T(128)} %param.15) | copy-start | bytes 388
  0.7 23.2 %copy-start.9 = (f32[32]{0:T(128)S(1)}, f32[32]{0:T(128)}, u32[]{:S(2)}) copy-start(f32[32]{0:T(128)} %param.14) | copy-start | bytes 388
  0.7 26.9 %copy-start.5 = (f32[8192]{0:T(1024)S(1)}, f32[8192]{0:T(1024)}, u32[]{:S(2)}) copy-start(f32[8192]{0:T(1024)} %param.17) | copy-start | bytes 98308
  1.6 14.0 %collective-permute-start = (bf16[16,32,128]{2,1,0:T(8,128)(2,1)S(1)}, bf16[16,32,128]{2,1,0:T(8,128)(2,1)S(1)}, u32[]{:S(2)}, u32[]{:S(2)}) collective-permute-start(bf16[16,32,128]{2,1,0:T(8,128)(2,1)S(1)} %fusion.panel_ref.refs_0_), channel_id=1, source_target_pairs={{0,16},{4,20},{8,24},{12,28},{16,0},{20,4},{24,8},{28,12},{1,17},{... | collective-permute-start | bytes 393224 | tf_op jit(solution)/shard_map/ppermute | solution.py:466
  5.7 13.1 %collective-permute-start.1 = (bf16[16,32,128]{2,1,0:T(8,128)(2,1)S(1)}, bf16[16,32,128]{2,1,0:T(8,128)(2,1)S(1)}, u32[]{:S(2)}, u32[]{:S(2)}) collective-permute-start(bf16[16,32,128]{2,1,0:T(8,128)(2,1)S(1)} %fusion.panel_ref.refs_0_), channel_id=1, source_target_pairs={{0,4},{4,0},{8,12},{12,8},{16,20},{20,16},{24,28},{28,24},{1,5},{5... | collective-permute-start | bytes 393224 | tf_op jit(solution)/shard_map/ppermute | solution.py:466
  7.2 3.4 %copy-start.1 = (bf16[64,4,128,128]{3,2,1,0:T(8,128)(2,1)S(1)}, bf16[64,4,128,128]{3,2,1,0:T(8,128)(2,1)}, u32[]{:S(2)}) copy-start(bf16[64,4,128,128]{3,2,1,0:T(8,128)(2,1)} %blocks_ref.11) | copy-start | bytes 25165828
  10.6 0.7 copy-start.6
  11.3 12.6 %copy-start.2 = (bf16[64,128,128]{2,1,0:T(8,128)(2,1)S(1)}, bf16[64,128,128]{2,1,0:T(8,128)(2,1)}, u32[]{:S(2)}) copy-start(bf16[64,128,128]{2,1,0:T(8,128)(2,1)} %refs_8_.5) | copy-start | bytes 6291460
  11.3 12.6 %copy-start.3 = (f32[32,8192]{1,0:T(8,128)S(1)}, f32[32,8192]{1,0:T(8,128)}, u32[]{:S(2)}) copy-start(f32[32,8192]{1,0:T(8,128)} %refs_10_.1) | copy-start | bytes 3145732
  11.3 23.2 %slice-start = ((s8[8388608]{0:T(1024)(128)(4,1)}), s8[4194304]{0:T(1024)(128)(4,1)S(1)}, s32[]{:S(2)}) async-start(s8[8388608]{0:T(1024)(128)(4,1)} %bitcast.24), calls=%async_computation | async-start | bytes 8388608
  11.3 23.2 %copy-start.4 = (f32[32,2048]{1,0:T(8,128)S(1)}, f32[32,2048]{1,0:T(8,128)}, u32[]{:S(2)}) copy-start(f32[32,2048]{1,0:T(8,128)} %demand_ref.5) | copy-start | bytes 786436
  16.2 6.4 %collective-permute-start.5 = (bf16[16,32,128]{2,1,0:T(8,128)(2,1)S(1)}, bf16[16,32,128]{2,1,0:T(8,128)(2,1)S(1)}, u32[]{:S(2)}, u32[]{:S(2)}) collective-permute-start(bf16[16,32,128]{2,1,0:T(8,128)(2,1)S(1)} %get-tuple-element.77.refs_0_.refs_4_), channel_id=1, source_target_pairs={{0,8},{4,12},{8,0},{12,4},{16,24},{20,28},{24,16},{28,20},{1,9},{5... | collective-permute-start | bytes 393224 | tf_op jit(solution)/shard_map/ppermute | solution.py:466
  17.8 7.3 %collective-permute-start.2 = (bf16[16,32,128]{2,1,0:T(8,128)(2,1)S(1)}, bf16[16,32,128]{2,1,0:T(8,128)(2,1)S(1)}, u32[]{:S(2)}, u32[]{:S(2)}) collective-permute-start(bf16[16,32,128]{2,1,0:T(8,128)(2,1)S(1)} %fusion.panel_ref.refs_0_), channel_id=1, source_target_pairs={{0,8},{4,12},{8,0},{12,4},{16,24},{20,28},{24,16},{28,20},{1,9},{5... | collective-permute-start | bytes 393224 | tf_op jit(solution)/shard_map/ppermute | solution.py:466
  18.2 8.3 %collective-permute-start.4 = (bf16[16,32,128]{2,1,0:T(8,128)(2,1)S(1)}, bf16[16,32,128]{2,1,0:T(8,128)(2,1)S(1)}, u32[]{:S(2)}, u32[]{:S(2)}) collective-permute-start(bf16[16,32,128]{2,1,0:T(8,128)(2,1)S(1)} %get-tuple-element.77.refs_0_.refs_4_), channel_id=1, source_target_pairs={{0,4},{4,0},{8,12},{12,8},{16,20},{20,16},{24,28},{28,24},{1,5},{5... | collective-permute-start | bytes 393224 | tf_op jit(solution)/shard_map/ppermute | solution.py:466
  18.8 7.7 %collective-permute-start.3 = (bf16[16,32,128]{2,1,0:T(8,128)(2,1)S(1)}, bf16[16,32,128]{2,1,0:T(8,128)(2,1)S(1)}, u32[]{:S(2)}, u32[]{:S(2)}) collective-permute-start(bf16[16,32,128]{2,1,0:T(8,128)(2,1)S(1)} %collective-permute-done.1.refs_1_), channel_id=1, source_target_pairs={{0,8},{4,12},{8,0},{12,4},{16,24},{20,28},{24,16},{28,20},{1,9},{5... | collective-permute-start | bytes 393224 | tf_op jit(solution)/shard_map/ppermute | solution.py:466
  22.6 5.0 %collective-permute-start.6 = (bf16[16,32,128]{2,1,0:T(8,128)(2,1)S(1)}, bf16[16,32,128]{2,1,0:T(8,128)(2,1)S(1)}, u32[]{:S(2)}, u32[]{:S(2)}) collective-permute-start(bf16[16,32,128]{2,1,0:T(8,128)(2,1)S(1)} %collective-permute-done.5.refs_6_), channel_id=1, source_target_pairs={{0,4},{4,0},{8,12},{12,8},{16,20},{20,16},{24,28},{28,24},{1,5},{5... | collective-permute-start | bytes 393224 | tf_op jit(solution)/shard_map/ppermute | solution.py:466
  23.9 10.6 %slice-start.1 = ((s8[8388608]{0:T(1024)(128)(4,1)}), s8[4194304]{0:T(1024)(128)(4,1)S(1)}, s32[]{:S(2)}) async-start(s8[8388608]{0:T(1024)(128)(4,1)} %bitcast.24), calls=%async_computation.1 | async-start | bytes 8388608
  24.0 1.2 collective-permute-start.7
  27.6 28.2 %copy-start.7 = (s32[64,4]{0,1:T(4,128)S(1)}, s32[64,4]{0,1:T(4,128)}, u32[]{:S(2)}) copy-start(s32[64,4]{0,1:T(4,128)} %param.20) | copy-start | bytes 3076
  30.8 7.1 %collective-permute-start.9 = (bf16[16,32,128]{2,1,0:T(8,128)(2,1)S(1)}, bf16[16,32,128]{2,1,0:T(8,128)(2,1)S(1)}, u32[]{:S(2)}, u32[]{:S(2)}) collective-permute-start(bf16[16,32,128]{2,1,0:T(8,128)(2,1)S(1)} %get-tuple-element.86), channel_id=1, source_target_pairs={{0,4},{4,0},{8,12},{12,8},{16,20},{20,16},{24,28},{28,24},{1,5},{5... | collective-permute-start | bytes 393224 | tf_op jit(solution)/shard_map/ppermute | solution.py:466
  31.4 6.5 %collective-permute-start.11 = (bf16[16,32,128]{2,1,0:T(8,128)(2,1)S(1)}, bf16[16,32,128]{2,1,0:T(8,128)(2,1)S(1)}, u32[]{:S(2)}, u32[]{:S(2)}) collective-permute-start(bf16[16,32,128]{2,1,0:T(8,128)(2,1)S(1)} %get-tuple-element.90), channel_id=1, source_target_pairs={{0,8},{4,12},{8,0},{12,4},{16,24},{20,28},{24,16},{28,20},{1,9},{5... | collective-permute-start | bytes 393224 | tf_op jit(solution)/shard_map/ppermute | solution.py:466
  33.0 5.2 %collective-permute-start.10 = (bf16[17,32,128]{2,1,0:T(8,128)(2,1)S(1)}, bf16[17,32,128]{2,1,0:T(8,128)(2,1)S(1)}, u32[]{:S(2)}, u32[]{:S(2)}) collective-permute-start(bf16[17,32,128]{2,1,0:T(8,128)(2,1)S(1)} %get-tuple-element.88.refs_2_), channel_id=1, source_target_pairs={{0,4},{4,0},{8,12},{12,8},{16,20},{20,16},{24,28},{28,24},{1,5},{5... | collective-permute-start | bytes 417800 | tf_op jit(solution)/shard_map/ppermute | solution.py:466
  38.3 5.7 %collective-permute-start.12 = (bf16[17,32,128]{2,1,0:T(8,128)(2,1)S(1)}, bf16[17,32,128]{2,1,0:T(8,128)(2,1)S(1)}, u32[]{:S(2)}, u32[]{:S(2)}) collective-permute-start(bf16[17,32,128]{2,1,0:T(8,128)(2,1)S(1)} %get-tuple-element.92.refs_3_), channel_id=1, source_target_pairs={{0,8},{4,12},{8,0},{12,4},{16,24},{20,28},{24,16},{28,20},{1,9},{5... | collective-permute-start | bytes 417800 | tf_op jit(solution)/shard_map/ppermute | solution.py:466
  39.1 6.5 %collective-permute-start.8 = (bf16[16,32,128]{2,1,0:T(8,128)(2,1)S(1)}, bf16[16,32,128]{2,1,0:T(8,128)(2,1)S(1)}, u32[]{:S(2)}, u32[]{:S(2)}) collective-permute-start(bf16[16,32,128]{2,1,0:T(8,128)(2,1)S(1)} %get-tuple-element.84), channel_id=1, source_target_pairs={{0,8},{4,12},{8,0},{12,4},{16,24},{20,28},{24,16},{28,20},{1,9},{5... | collective-permute-start | bytes 393224 | tf_op jit(solution)/shard_map/ppermute | solution.py:466
  40.4 3.6 %collective-permute-start.13 = (f32[8,128]{1,0:T(8,128)S(1)}, f32[8,128]{1,0:T(8,128)S(1)}, u32[]{:S(2)}, u32[]{:S(2)}) collective-permute-start(f32[8,128]{1,0:T(8,128)S(1)} %get-tuple-element.93.refs_9_), channel_id=1, source_target_pairs={{0,2},{1,3},{2,0},{3,1},{4,6},{5,7},{6,4},{7,5},{8,10},{9,11},{10,... | collective-permute-start | bytes 12296 | tf_op jit(solution)/shard_map/ppermute | solution.py:466
  44.1 10.1 %collective-permute-start.15 = (bf16[17,32,128]{2,1,0:T(8,128)(2,1)S(1)}, bf16[17,32,128]{2,1,0:T(8,128)(2,1)S(1)}, u32[]{:S(2)}, u32[]{:S(2)}) collective-permute-start(bf16[17,32,128]{2,1,0:T(8,128)(2,1)S(1)} %fold.10.refs_2_.refs_4_), channel_id=1, source_target_pairs={{0,16},{4,20},{8,24},{12,28},{16,0},{20,4},{24,8},{28,12},{1,17},{... | collective-permute-start | bytes 417800 | tf_op jit(solution)/shard_map/ppermute | solution.py:466
  45.6 6.0 %collective-permute-start.14 = (bf16[16,32,128]{2,1,0:T(8,128)(2,1)S(1)}, bf16[16,32,128]{2,1,0:T(8,128)(2,1)S(1)}, u32[]{:S(2)}, u32[]{:S(2)}) collective-permute-start(bf16[16,32,128]{2,1,0:T(8,128)(2,1)S(1)} %fold.11), channel_id=1, source_target_pairs={{0,4},{4,0},{8,12},{12,8},{16,20},{20,16},{24,28},{28,24},{1,5},{5... | collective-permute-start | bytes 393224 | tf_op jit(solution)/shard_map/ppermute | solution.py:466
  54.4 6.5 %collective-permute-start.19 = (bf16[16,32,128]{2,1,0:T(8,128)(2,1)S(1)}, bf16[16,32,128]{2,1,0:T(8,128)(2,1)S(1)}, u32[]{:S(2)}, u32[]{:S(2)}) collective-permute-start(bf16[16,32,128]{2,1,0:T(8,128)(2,1)S(1)} %get-tuple-element.96.panel_ref.refs_0_), channel_id=1, source_target_pairs={{0,16},{4,20},{8,24},{12,28},{16,0},{20,4},{24,8},{28,12},{1,17},{... | collective-permute-start | bytes 393224 | tf_op jit(solution)/shard_map/ppermute | solution.py:466
  54.5 9.8 %collective-permute-start.16 = (bf16[16,32,128]{2,1,0:T(8,128)(2,1)S(1)}, bf16[16,32,128]{2,1,0:T(8,128)(2,1)S(1)}, u32[]{:S(2)}, u32[]{:S(2)}) collective-permute-start(bf16[16,32,128]{2,1,0:T(8,128)(2,1)S(1)} %get-tuple-element.96.panel_ref.refs_0_), channel_id=1, source_target_pairs={{0,4},{4,0},{8,12},{12,8},{16,20},{20,16},{24,28},{28,24},{1,5},{5... | collective-permute-start | bytes 393224 | tf_op jit(solution)/shard_map/ppermute | solution.py:466
  60.9 5.0 %collective-permute-start.21 = (bf16[16,32,128]{2,1,0:T(8,128)(2,1)S(1)}, bf16[16,32,128]{2,1,0:T(8,128)(2,1)S(1)}, u32[]{:S(2)}, u32[]{:S(2)}) collective-permute-start(bf16[16,32,128]{2,1,0:T(8,128)(2,1)S(1)} %get-tuple-element.99.refs_4_), channel_id=1, source_target_pairs={{0,8},{4,12},{8,0},{12,4},{16,24},{20,28},{24,16},{28,20},{1,9},{5... | collective-permute-start | bytes 393224 | tf_op jit(solution)/shard_map/ppermute | solution.py:466
  61.0 6.4 %collective-permute-start.17 = (bf16[16,32,128]{2,1,0:T(8,128)(2,1)S(1)}, bf16[16,32,128]{2,1,0:T(8,128)(2,1)S(1)}, u32[]{:S(2)}, u32[]{:S(2)}) collective-permute-start(bf16[16,32,128]{2,1,0:T(8,128)(2,1)S(1)} %get-tuple-element.96.panel_ref.refs_0_), channel_id=1, source_target_pairs={{0,8},{4,12},{8,0},{12,4},{16,24},{20,28},{24,16},{28,20},{1,9},{5... | collective-permute-start | bytes 393224 | tf_op jit(solution)/shard_map/ppermute | solution.py:466
  63.0 6.3 %collective-permute-start.20 = (bf16[16,32,128]{2,1,0:T(8,128)(2,1)S(1)}, bf16[16,32,128]{2,1,0:T(8,128)(2,1)S(1)}, u32[]{:S(2)}, u32[]{:S(2)}) collective-permute-start(bf16[16,32,128]{2,1,0:T(8,128)(2,1)S(1)} %get-tuple-element.99.refs_4_), channel_id=1, source_target_pairs={{0,4},{4,0},{8,12},{12,8},{16,20},{20,16},{24,28},{28,24},{1,5},{5... | collective-permute-start | bytes 393224 | tf_op jit(solution)/shard_map/ppermute | solution.py:466
  64.3 5.0 %collective-permute-start.18 = (bf16[16,32,128]{2,1,0:T(8,128)(2,1)S(1)}, bf16[16,32,128]{2,1,0:T(8,128)(2,1)S(1)}, u32[]{:S(2)}, u32[]{:S(2)}) collective-permute-start(bf16[16,32,128]{2,1,0:T(8,128)(2,1)S(1)} %collective-permute-done.16.refs_1_), channel_id=1, source_target_pairs={{0,8},{4,12},{8,0},{12,4},{16,24},{20,28},{24,16},{28,20},{1,9},{5... | collective-permute-start | bytes 393224 | tf_op jit(solution)/shard_map/ppermute | solution.py:466
  65.9 5.0 %collective-permute-start.22 = (bf16[16,32,128]{2,1,0:T(8,128)(2,1)S(1)}, bf16[16,32,128]{2,1,0:T(8,128)(2,1)S(1)}, u32[]{:S(2)}, u32[]{:S(2)}) collective-permute-start(bf16[16,32,128]{2,1,0:T(8,128)(2,1)S(1)} %collective-permute-done.21.refs_6_), channel_id=1, source_target_pairs={{0,4},{4,0},{8,12},{12,8},{16,20},{20,16},{24,28},{28,24},{1,5},{5... | collective-permute-start | bytes 393224 | tf_op jit(solution)/shard_map/ppermute | solution.py:466
  67.2 1.2 collective-permute-start.23
  74.1 8.3 %collective-permute-start.26 = (bf16[17,32,128]{2,1,0:T(8,128)(2,1)S(1)}, bf16[17,32,128]{2,1,0:T(8,128)(2,1)S(1)}, u32[]{:S(2)}, u32[]{:S(2)}) collective-permute-start(bf16[17,32,128]{2,1,0:T(8,128)(2,1)S(1)} %get-tuple-element.110.refs_2_), channel_id=1, source_target_pairs={{0,4},{4,0},{8,12},{12,8},{16,20},{20,16},{24,28},{28,24},{1,5},{5... | collective-permute-start | bytes 417800 | tf_op jit(solution)/shard_map/ppermute | solution.py:466
  75.4 5.2 %collective-permute-start.25 = (bf16[16,32,128]{2,1,0:T(8,128)(2,1)S(1)}, bf16[16,32,128]{2,1,0:T(8,128)(2,1)S(1)}, u32[]{:S(2)}, u32[]{:S(2)}) collective-permute-start(bf16[16,32,128]{2,1,0:T(8,128)(2,1)S(1)} %get-tuple-element.108), channel_id=1, source_target_pairs={{0,4},{4,0},{8,12},{12,8},{16,20},{20,16},{24,28},{28,24},{1,5},{5... | collective-permute-start | bytes 393224 | tf_op jit(solution)/shard_map/ppermute | solution.py:466
  76.2 6.2 %collective-permute-start.27 = (bf16[16,32,128]{2,1,0:T(8,128)(2,1)S(1)}, bf16[16,32,128]{2,1,0:T(8,128)(2,1)S(1)}, u32[]{:S(2)}, u32[]{:S(2)}) collective-permute-start(bf16[16,32,128]{2,1,0:T(8,128)(2,1)S(1)} %get-tuple-element.112), channel_id=1, source_target_pairs={{0,8},{4,12},{8,0},{12,4},{16,24},{20,28},{24,16},{28,20},{1,9},{5... | collective-permute-start | bytes 393224 | tf_op jit(solution)/shard_map/ppermute | solution.py:466
  82.5 6.6 %collective-permute-start.28 = (bf16[17,32,128]{2,1,0:T(8,128)(2,1)S(1)}, bf16[17,32,128]{2,1,0:T(8,128)(2,1)S(1)}, u32[]{:S(2)}, u32[]{:S(2)}) collective-permute-start(bf16[17,32,128]{2,1,0:T(8,128)(2,1)S(1)} %get-tuple-element.115.refs_3_), channel_id=1, source_target_pairs={{0,8},{4,12},{8,0},{12,4},{16,24},{20,28},{24,16},{28,20},{1,9},{5... | collective-permute-start | bytes 417800 | tf_op jit(solution)/shard_map/ppermute | solution.py:466
  82.5 8.0 %collective-permute-start.24 = (bf16[16,32,128]{2,1,0:T(8,128)(2,1)S(1)}, bf16[16,32,128]{2,1,0:T(8,128)(2,1)S(1)}, u32[]{:S(2)}, u32[]{:S(2)}) collective-permute-start(bf16[16,32,128]{2,1,0:T(8,128)(2,1)S(1)} %get-tuple-element.106), channel_id=1, source_target_pairs={{0,8},{4,12},{8,0},{12,4},{16,24},{20,28},{24,16},{28,20},{1,9},{5... | collective-permute-start | bytes 393224 | tf_op jit(solution)/shard_map/ppermute | solution.py:466
  84.5 3.6 %collective-permute-start.29 = (f32[8,128]{1,0:T(8,128)S(1)}, f32[8,128]{1,0:T(8,128)S(1)}, u32[]{:S(2)}, u32[]{:S(2)}) collective-permute-start(f32[8,128]{1,0:T(8,128)S(1)} %get-tuple-element.116.refs_9_), channel_id=1, source_target_pairs={{0,2},{1,3},{2,0},{3,1},{4,6},{5,7},{6,4},{7,5},{8,10},{9,11},{10,... | collective-permute-start | bytes 12296 | tf_op jit(solution)/shard_map/ppermute | solution.py:466
  89.2 8.4 %collective-permute-start.31 = (bf16[17,32,128]{2,1,0:T(8,128)(2,1)S(1)}, bf16[17,32,128]{2,1,0:T(8,128)(2,1)S(1)}, u32[]{:S(2)}, u32[]{:S(2)}) collective-permute-start(bf16[17,32,128]{2,1,0:T(8,128)(2,1)S(1)} %fold.13.refs_2_.refs_4_), channel_id=1, source_target_pairs={{0,16},{4,20},{8,24},{12,28},{16,0},{20,4},{24,8},{28,12},{1,17},{... | collective-permute-start | bytes 417800 | tf_op jit(solution)/shard_map/ppermute | solution.py:466
  90.6 5.6 %collective-permute-start.30 = (bf16[16,32,128]{2,1,0:T(8,128)(2,1)S(1)}, bf16[16,32,128]{2,1,0:T(8,128)(2,1)S(1)}, u32[]{:S(2)}, u32[]{:S(2)}) collective-permute-start(bf16[16,32,128]{2,1,0:T(8,128)(2,1)S(1)} %fold.14), channel_id=1, source_target_pairs={{0,4},{4,0},{8,12},{12,8},{16,20},{20,16},{24,28},{28,24},{1,5},{5... | collective-permute-start | bytes 393224 | tf_op jit(solution)/shard_map/ppermute | solution.py:466
  97.8 7.0 %collective-permute-start.35 = (bf16[16,32,128]{2,1,0:T(8,128)(2,1)S(1)}, bf16[16,32,128]{2,1,0:T(8,128)(2,1)S(1)}, u32[]{:S(2)}, u32[]{:S(2)}) collective-permute-start(bf16[16,32,128]{2,1,0:T(8,128)(2,1)S(1)} %get-tuple-element.119.panel_ref.refs_0_), channel_id=1, source_target_pairs={{0,16},{4,20},{8,24},{12,28},{16,0},{20,4},{24,8},{28,12},{1,17},{... | collective-permute-start | bytes 393224 | tf_op jit(solution)/shard_map/ppermute | solution.py:466
  97.9 10.0 %collective-permute-start.32 = (bf16[16,32,128]{2,1,0:T(8,128)(2,1)S(1)}, bf16[16,32,128]{2,1,0:T(8,128)(2,1)S(1)}, u32[]{:S(2)}, u32[]{:S(2)}) collective-permute-start(bf16[16,32,128]{2,1,0:T(8,128)(2,1)S(1)} %get-tuple-element.119.panel_ref.refs_0_), channel_id=1, source_target_pairs={{0,4},{4,0},{8,12},{12,8},{16,20},{20,16},{24,28},{28,24},{1,5},{5... | collective-permute-start | bytes 393224 | tf_op jit(solution)/shard_map/ppermute | solution.py:466
  104.9 5.0 %collective-permute-start.37 = (bf16[16,32,128]{2,1,0:T(8,128)(2,1)S(1)}, bf16[16,32,128]{2,1,0:T(8,128)(2,1)S(1)}, u32[]{:S(2)}, u32[]{:S(2)}) collective-permute-start(bf16[16,32,128]{2,1,0:T(8,128)(2,1)S(1)} %get-tuple-element.122.refs_4_), channel_id=1, source_target_pairs={{0,8},{4,12},{8,0},{12,4},{16,24},{20,28},{24,16},{28,20},{1,9},{5... | collective-permute-start | bytes 393224 | tf_op jit(solution)/shard_map/ppermute | solution.py:466
  105.6 5.7 %collective-permute-start.33 = (bf16[16,32,128]{2,1,0:T(8,128)(2,1)S(1)}, bf16[16,32,128]{2,1,0:T(8,128)(2,1)S(1)}, u32[]{:S(2)}, u32[]{:S(2)}) collective-permute-start(bf16[16,32,128]{2,1,0:T(8,128)(2,1)S(1)} %get-tuple-element.119.panel_ref.refs_0_), channel_id=1, source_target_pairs={{0,8},{4,12},{8,0},{12,4},{16,24},{20,28},{24,16},{28,20},{1,9},{5... | collective-permute-start | bytes 393224 | tf_op jit(solution)/shard_map/ppermute | solution.py:466
  107.0 5.9 %collective-permute-start.36 = (bf16[16,32,128]{2,1,0:T(8,128)(2,1)S(1)}, bf16[16,32,128]{2,1,0:T(8,128)(2,1)S(1)}, u32[]{:S(2)}, u32[]{:S(2)}) collective-permute-start(bf16[16,32,128]{2,1,0:T(8,128)(2,1)S(1)} %get-tuple-element.122.refs_4_), channel_id=1, source_target_pairs={{0,4},{4,0},{8,12},{12,8},{16,20},{20,16},{24,28},{28,24},{1,5},{5... | collective-permute-start | bytes 393224 | tf_op jit(solution)/shard_map/ppermute | solution.py:466
  107.9 5.0 %collective-permute-start.34 = (bf16[16,32,128]{2,1,0:T(8,128)(2,1)S(1)}, bf16[16,32,128]{2,1,0:T(8,128)(2,1)S(1)}, u32[]{:S(2)}, u32[]{:S(2)}) collective-permute-start(bf16[16,32,128]{2,1,0:T(8,128)(2,1)S(1)} %collective-permute-done.32.refs_1_), channel_id=1, source_target_pairs={{0,8},{4,12},{8,0},{12,4},{16,24},{20,28},{24,16},{28,20},{1,9},{5... | collective-permute-start | bytes 393224 | tf_op jit(solution)/shard_map/ppermute | solution.py:466
  109.9 5.0 %collective-permute-start.38 = (bf16[16,32,128]{2,1,0:T(8,128)(2,1)S(1)}, bf16[16,32,128]{2,1,0:T(8,128)(2,1)S(1)}, u32[]{:S(2)}, u32[]{:S(2)}) collective-permute-start(bf16[16,32,128]{2,1,0:T(8,128)(2,1)S(1)} %collective-permute-done.37.refs_6_), channel_id=1, source_target_pairs={{0,4},{4,0},{8,12},{12,8},{16,20},{20,16},{24,28},{28,24},{1,5},{5... | collective-permute-start | bytes 393224 | tf_op jit(solution)/shard_map/ppermute | solution.py:466
  110.8 1.2 collective-permute-start.39
  118.7 8.3 %collective-permute-start.42 = (bf16[17,32,128]{2,1,0:T(8,128)(2,1)S(1)}, bf16[17,32,128]{2,1,0:T(8,128)(2,1)S(1)}, u32[]{:S(2)}, u32[]{:S(2)}) collective-permute-start(bf16[17,32,128]{2,1,0:T(8,128)(2,1)S(1)} %get-tuple-element.134.refs_2_), channel_id=1, source_target_pairs={{0,4},{4,0},{8,12},{12,8},{16,20},{20,16},{24,28},{28,24},{1,5},{5... | collective-permute-start | bytes 417800 | tf_op jit(solution)/shard_map/ppermute | solution.py:466
  119.7 5.5 %collective-permute-start.41 = (bf16[16,32,128]{2,1,0:T(8,128)(2,1)S(1)}, bf16[16,32,128]{2,1,0:T(8,128)(2,1)S(1)}, u32[]{:S(2)}, u32[]{:S(2)}) collective-permute-start(bf16[16,32,128]{2,1,0:T(8,128)(2,1)S(1)} %get-tuple-element.132), channel_id=1, source_target_pairs={{0,4},{4,0},{8,12},{12,8},{16,20},{20,16},{24,28},{28,24},{1,5},{5... | collective-permute-start | bytes 393224 | tf_op jit(solution)/shard_map/ppermute | solution.py:466
  120.8 6.3 %collective-permute-start.43 = (bf16[16,32,128]{2,1,0:T(8,128)(2,1)S(1)}, bf16[16,32,128]{2,1,0:T(8,128)(2,1)S(1)}, u32[]{:S(2)}, u32[]{:S(2)}) collective-permute-start(bf16[16,32,128]{2,1,0:T(8,128)(2,1)S(1)} %get-tuple-element.136), channel_id=1, source_target_pairs={{0,8},{4,12},{8,0},{12,4},{16,24},{20,28},{24,16},{28,20},{1,9},{5... | collective-permute-start | bytes 393224 | tf_op jit(solution)/shard_map/ppermute | solution.py:466
  127.1 5.8 %collective-permute-start.44 = (bf16[17,32,128]{2,1,0:T(8,128)(2,1)S(1)}, bf16[17,32,128]{2,1,0:T(8,128)(2,1)S(1)}, u32[]{:S(2)}, u32[]{:S(2)}) collective-permute-start(bf16[17,32,128]{2,1,0:T(8,128)(2,1)S(1)} %get-tuple-element.139.refs_3_), channel_id=1, source_target_pairs={{0,8},{4,12},{8,0},{12,4},{16,24},{20,28},{24,16},{28,20},{1,9},{5... | collective-permute-start | bytes 417800 | tf_op jit(solution)/shard_map/ppermute | solution.py:466
  127.7 7.5 %collective-permute-start.40 = (bf16[16,32,128]{2,1,0:T(8,128)(2,1)S(1)}, bf16[16,32,128]{2,1,0:T(8,128)(2,1)S(1)}, u32[]{:S(2)}, u32[]{:S(2)}) collective-permute-start(bf16[16,32,128]{2,1,0:T(8,128)(2,1)S(1)} %get-tuple-element.130), channel_id=1, source_target_pairs={{0,8},{4,12},{8,0},{12,4},{16,24},{20,28},{24,16},{28,20},{1,9},{5... | collective-permute-start | bytes 393224 | tf_op jit(solution)/shard_map/ppermute | solution.py:466
  129.2 3.6 %collective-permute-start.45 = (f32[8,128]{1,0:T(8,128)S(1)}, f32[8,128]{1,0:T(8,128)S(1)}, u32[]{:S(2)}, u32[]{:S(2)}) collective-permute-start(f32[8,128]{1,0:T(8,128)S(1)} %get-tuple-element.140.refs_9_), channel_id=1, source_target_pairs={{0,2},{1,3},{2,0},{3,1},{4,6},{5,7},{6,4},{7,5},{8,10},{9,11},{10,... | collective-permute-start | bytes 12296 | tf_op jit(solution)/shard_map/ppermute | solution.py:466
  133.1 7.5 %collective-permute-start.47 = (bf16[17,32,128]{2,1,0:T(8,128)(2,1)S(1)}, bf16[17,32,128]{2,1,0:T(8,128)(2,1)S(1)}, u32[]{:S(2)}, u32[]{:S(2)}) collective-permute-start(bf16[17,32,128]{2,1,0:T(8,128)(2,1)S(1)} %fold.16.refs_2_.refs_4_), channel_id=1, source_target_pairs={{0,16},{4,20},{8,24},{12,28},{16,0},{20,4},{24,8},{28,12},{1,17},{... | collective-permute-start | bytes 417800 | tf_op jit(solution)/shard_map/ppermute | solution.py:466
  135.2 5.0 %collective-permute-start.46 = (bf16[16,32,128]{2,1,0:T(8,128)(2,1)S(1)}, bf16[16,32,128]{2,1,0:T(8,128)(2,1)S(1)}, u32[]{:S(2)}, u32[]{:S(2)}) collective-permute-start(bf16[16,32,128]{2,1,0:T(8,128)(2,1)S(1)} %fold.17), channel_id=1, source_target_pairs={{0,4},{4,0},{8,12},{12,8},{16,20},{20,16},{24,28},{28,24},{1,5},{5... | collective-permute-start | bytes 393224 | tf_op jit(solution)/shard_map/ppermute | solution.py:466

commit v11 on v10

--- a/solution.py
+++ b/solution.py
@@ -528,8 +528,8 @@
         tops = sorted(inner(net_size), key=lambda k: (-k.bit_count(), -k))[:-1]
         groups = [(top,) for top in tops if top != 1] + [(1,)]
         loss, loss_top = sends[net_size - 1], net_size - 1
-        ahead = {k: swap(sends[k], "net", last_hop(k)) for k in (5, 2)}
-        after = (ahead[5], ahead[2], base)
+        ahead = {k: swap(sends[k], "net", last_hop(k)) for k in (2,)}
+        after = (ahead[2], base)
         for group in groups:
             terms = []
             for top in group:

time: 142 us -> 141 us (level)
  transfers between devices with their start and end apart: 48 -> 48, of which waited for: 35 -> 31; matrix products, arithmetic and copies ran while one was open for 0% -> 0% of each run, Pallas kernels for 17% -> 17%
where the time goes in v11:
time: 141 us
  starting transfers between devices  50 us (35%)
  waiting for transfers between devices  48.7 us (35%)
  Pallas kernels  35.8 us (25%)
  local copies, waits for them, and re-layouts  5.05 us (4%)
  between operations  1.59 us (1%)
    ppermute x48, starting transfers between devices, swap(): return lax.ppermute(value, axis, [(i, i ^ distance) for i in range(size)])  50 us
    ppermute x48, waiting for transfers between devices, swap(): return lax.ppermute(value, axis, [(i, i ^ distance) for i in range(size)])  48.7 us
    pallas_call x3, Pallas kernels, local_adjoint(): pl.pallas_call(functools.partial(local_adjoint_kernel, touches, group), o...  12.9 us
    pallas_call x3, Pallas kernels, head_step(): pl.pallas_call(functools.partial(head_kernel, group, steps, peers), out_s...  10.2 us
    pallas_call x3, Pallas kernels, local_forward(): pl.pallas_call(functools.partial(local_forward_kernel, touches, group, st...  10 us
    unnamed x26, local copies, waits for them, and re-layouts  5.01 us
  transfers between devices with their start and end apart: 48, of which 31 were waited for; matrix products, arithmetic and copies ran while one was open for 0% of the time, Pallas kernels for 17%

profile of v11, /device:TPU:0, one launch (start us, length us, event | category | flops | bytes accessed | tf_op | source)
XLA Modules:
  0.0 141.2 jit_solution(2933594405619115758)
XLA Ops:
  0.7 0.9 copy-done
  1.6 4.1 %collective-permute-start = (bf16[16,32,128]{2,1,0:T(8,128)(2,1)S(1)}, bf16[16,32,128]{2,1,0:T(8,128)(2,1)S(1)}, u32[]{:S(2)}, u32[]{:S(2)}) collective-permute-start(bf16[16,32,128]{2,1,0:T(8,128)(2,1)S(1)} %fusion.panel_ref.refs_0_), channel_id=1, source_target_pairs={{0,16},{4,20},{8,24},{12,28},{16,0},{20,4},{24,8},{28,12},{1,17},{... | collective-permute-start | bytes 393224 | tf_op jit(solution)/shard_map/ppermute | solution.py:466
  5.7 1.5 %collective-permute-start.1 = (bf16[16,32,128]{2,1,0:T(8,128)(2,1)S(1)}, bf16[16,32,128]{2,1,0:T(8,128)(2,1)S(1)}, u32[]{:S(2)}, u32[]{:S(2)}) collective-permute-start(bf16[16,32,128]{2,1,0:T(8,128)(2,1)S(1)} %fusion.panel_ref.refs_0_), channel_id=1, source_target_pairs={{0,4},{4,0},{8,12},{12,8},{16,20},{20,16},{24,28},{28,24},{1,5},{5... | collective-permute-start | bytes 393224 | tf_op jit(solution)/shard_map/ppermute | solution.py:466
  7.2 3.4 %copy-done.1 = bf16[64,4,128,128]{3,2,1,0:T(8,128)(2,1)S(1)} copy-done((bf16[64,4,128,128]{3,2,1,0:T(8,128)(2,1)S(1)}, bf16[64,4,128,128]{3,2,1,0:T(8,128)(2,1)}, u32[]{:S(2)}) %copy-start.1) | copy-done | bytes 8388632
  10.6 0.7 copy-done.6
  11.3 4.3 %local_adjoint.3 = (f32[32,8192]{1,0:T(8,128)S(1)}, f32[8,128]{1,0:T(8,128)S(1)}) custom-call(s32[4,64]{1,0:T(4,128)S(1)} %bitcast.29, bf16[16,32,128]{2,1,0:T(8,128)(2,1)S(1)} %fusion.panel_ref.refs_0_, bf16[64,4,128,128]{3,2,1,0:T(8,128)(2,1)S(1)} %copy-done.1), custom_call_target="tpu_custom_call" | custom-call | flops 268435456 | bytes 8388608 | tf_op jit(solution)/shard_map/local_adjoint/pallas_call | solution.py:255
  16.2 1.6 %collective-permute-start.5 = (bf16[16,32,128]{2,1,0:T(8,128)(2,1)S(1)}, bf16[16,32,128]{2,1,0:T(8,128)(2,1)S(1)}, u32[]{:S(2)}, u32[]{:S(2)}) collective-permute-start(bf16[16,32,128]{2,1,0:T(8,128)(2,1)S(1)} %get-tuple-element.77.refs_0_.refs_4_), channel_id=1, source_target_pairs={{0,8},{4,12},{8,0},{12,4},{16,24},{20,28},{24,16},{28,20},{1,9},{5... | collective-permute-start | bytes 393224 | tf_op jit(solution)/shard_map/ppermute | solution.py:466
  18.8 1.6 %collective-permute-start.3 = (bf16[16,32,128]{2,1,0:T(8,128)(2,1)S(1)}, bf16[16,32,128]{2,1,0:T(8,128)(2,1)S(1)}, u32[]{:S(2)}, u32[]{:S(2)}) collective-permute-start(bf16[16,32,128]{2,1,0:T(8,128)(2,1)S(1)} %collective-permute-done.1.refs_1_), channel_id=1, source_target_pairs={{0,8},{4,12},{8,0},{12,4},{16,24},{20,28},{24,16},{28,20},{1,9},{5... | collective-permute-start | bytes 393224 | tf_op jit(solution)/shard_map/ppermute | solution.py:466
  20.4 2.3 %collective-permute-done.5.refs_6_ = bf16[16,32,128]{2,1,0:T(8,128)(2,1)S(1)} collective-permute-done((bf16[16,32,128]{2,1,0:T(8,128)(2,1)S(1)}, bf16[16,32,128]{2,1,0:T(8,128)(2,1)S(1)}, u32[]{:S(2)}, u32[]{:S(2)}) %collective-permute-start.5) | collective-permute-done | bytes 131104 | tf_op jit(solution)/shard_map/ppermute | solution.py:466
  24.1 1.0 collective-permute-done.2.refs_2_
  25.2 1.3 collective-permute-done.3.refs_3_
  26.5 1.1 collective-permute-done.6.refs_7_
  27.6 3.2 %head_step.3 = (f32[32,8192]{1,0:T(8,128)S(1)}, bf16[32,8192]{1,0:T(8,128)(2,1)S(1)}, f32[8,128]{1,0:T(8,128)S(1)}, f32[16,32,128]{2,1,0:T(8,128)S(1)}, f32[16,3...) custom-call(s32[64]{0:T(128)S(1)} %bitcast.35, ...), custom_call_target="tpu_custom_call" | custom-call | flops 134217728 | bytes 7864320 | tf_op jit(solution)/shard_map/head_step/pallas_call | solution.py:292
  30.8 1.6 %collective-permute-start.11 = (bf16[16,32,128]{2,1,0:T(8,128)(2,1)S(1)}, bf16[16,32,128]{2,1,0:T(8,128)(2,1)S(1)}, u32[]{:S(2)}, u32[]{:S(2)}) collective-permute-start(bf16[16,32,128]{2,1,0:T(8,128)(2,1)S(1)} %get-tuple-element.90), channel_id=1, source_target_pairs={{0,8},{4,12},{8,0},{12,4},{16,24},{20,28},{24,16},{28,20},{1,9},{5... | collective-permute-start | bytes 393224 | tf_op jit(solution)/shard_map/ppermute | solution.py:466
  33.0 3.3 %local_forward.3.refs_5_ = f32[16,32,128]{2,1,0:T(8,128)S(1)} custom-call(s32[4,64]{1,0:T(4,128)S(1)} %bitcast.30, bf16[32,8192]{1,0:T(8,128)(2,1)S(1)} %get-tuple-element.91.bar_ref, bf16[64,4,128,128]{3,2,1,0:T(8,128)(2,1)S(1)} %bitcast.25, f32[16,32,128]{2,1,0:T(8,128)S(1)} %bitcast_bitcast_fusion.duals_ref, f32[32,2048]{1,0:T(8,128)S(1)} %copy-done.4), custom_call_target="tpu_custom_call" | custom-call | flops 268435456 | bytes 8388608 | tf_op jit(solution)/shard_map/local_forward/pallas_call | solution.py:390
  36.4 1.1 collective-permute-done.10.refs_1_
  38.6 1.6 %collective-permute-start.8 = (bf16[16,32,128]{2,1,0:T(8,128)(2,1)S(1)}, bf16[16,32,128]{2,1,0:T(8,128)(2,1)S(1)}, u32[]{:S(2)}, u32[]{:S(2)}) collective-permute-start(bf16[16,32,128]{2,1,0:T(8,128)(2,1)S(1)} %get-tuple-element.84), channel_id=1, source_target_pairs={{0,8},{4,12},{8,0},{12,4},{16,24},{20,28},{24,16},{28,20},{1,9},{5... | collective-permute-start | bytes 393224 | tf_op jit(solution)/shard_map/ppermute | solution.py:466
  40.2 1.5 %collective-permute-start.13 = (f32[8,128]{1,0:T(8,128)S(1)}, f32[8,128]{1,0:T(8,128)S(1)}, u32[]{:S(2)}, u32[]{:S(2)}) collective-permute-start(f32[8,128]{1,0:T(8,128)S(1)} %get-tuple-element.93.refs_9_), channel_id=1, source_target_pairs={{0,2},{1,3},{2,0},{3,1},{4,6},{5,7},{6,4},{7,5},{8,10},{9,11},{10,... | collective-permute-start | bytes 12296 | tf_op jit(solution)/shard_map/ppermute | solution.py:466
  41.7 1.6 %collective-permute-done.9.refs_1_ = bf16[16,32,128]{2,1,0:T(8,128)(2,1)S(1)} collective-permute-done((bf16[16,32,128]{2,1,0:T(8,128)(2,1)S(1)}, bf16[16,32,128]{2,1,0:T(8,128)(2,1)S(1)}, u32[]{:S(2)}, u32[]{:S(2)}) %collective-permute-start.9) | collective-permute-done | bytes 131104 | tf_op jit(solution)/shard_map/ppermute | solution.py:466
  45.0 1.1 collective-permute-start.14
  46.0 5.1 %collective-permute-done.14.refs_1_ = bf16[16,32,128]{2,1,0:T(8,128)(2,1)S(1)} collective-permute-done((bf16[16,32,128]{2,1,0:T(8,128)(2,1)S(1)}, bf16[16,32,128]{2,1,0:T(8,128)(2,1)S(1)}, u32[]{:S(2)}, u32[]{:S(2)}) %collective-permute-start.14) | collective-permute-done | bytes 131104 | tf_op jit(solution)/shard_map/ppermute | solution.py:466
  51.1 2.2 %collective-permute-done.15.refs_3_ = bf16[17,32,128]{2,1,0:T(8,128)(2,1)S(1)} collective-permute-done((bf16[17,32,128]{2,1,0:T(8,128)(2,1)S(1)}, bf16[17,32,128]{2,1,0:T(8,128)(2,1)S(1)}, u32[]{:S(2)}, u32[]{:S(2)}) %collective-permute-start.15) | collective-permute-done | bytes 139296 | tf_op jit(solution)/shard_map/ppermute | solution.py:466
  53.6 2.4 %collective-permute-start.16 = (bf16[16,32,128]{2,1,0:T(8,128)(2,1)S(1)}, bf16[16,32,128]{2,1,0:T(8,128)(2,1)S(1)}, u32[]{:S(2)}, u32[]{:S(2)}) collective-permute-start(bf16[16,32,128]{2,1,0:T(8,128)(2,1)S(1)} %get-tuple-element.96.panel_ref.refs_0_), channel_id=1, source_target_pairs={{0,4},{4,0},{8,12},{12,8},{16,20},{20,16},{24,28},{28,24},{1,5},{5... | collective-permute-start | bytes 393224 | tf_op jit(solution)/shard_map/ppermute | solution.py:466
  56.0 4.3 %local_adjoint.4 = (f32[32,8192]{1,0:T(8,128)S(1)}, f32[8,128]{1,0:T(8,128)S(1)}) custom-call(s32[4,64]{1,0:T(4,128)S(1)} %bitcast.31, bf16[16,32,128]{2,1,0:T(8,128)(2,1)S(1)} %get-tuple-element.96.panel_ref.refs_0_, bf16[64,4,128,128]{3,2,1,0:T(8,128)(2,1)S(1)} %bitcast.25), custom_call_target="tpu_custom_call" | custom-call | flops 268435456 | bytes 8388608 | tf_op jit(solution)/shard_map/local_adjoint/pallas_call | solution.py:255
  60.6 2.0 %collective-permute-start.17 = (bf16[16,32,128]{2,1,0:T(8,128)(2,1)S(1)}, bf16[16,32,128]{2,1,0:T(8,128)(2,1)S(1)}, u32[]{:S(2)}, u32[]{:S(2)}) collective-permute-start(bf16[16,32,128]{2,1,0:T(8,128)(2,1)S(1)} %get-tuple-element.96.panel_ref.refs_0_), channel_id=1, source_target_pairs={{0,8},{4,12},{8,0},{12,4},{16,24},{20,28},{24,16},{28,20},{1,9},{5... | collective-permute-start | bytes 393224 | tf_op jit(solution)/shard_map/ppermute | solution.py:466
  62.6 1.4 collective-permute-start.20
  64.6 1.0 collective-permute-done.21.refs_6_
  65.5 1.4 collective-permute-start.22
  66.9 1.2 collective-permute-done.23.refs_14_
  68.1 0.9 collective-permute-done.18.refs_3_
  68.9 1.5 %collective-permute-done.22.refs_7_ = bf16[16,32,128]{2,1,0:T(8,128)(2,1)S(1)} collective-permute-done((bf16[16,32,128]{2,1,0:T(8,128)(2,1)S(1)}, bf16[16,32,128]{2,1,0:T(8,128)(2,1)S(1)}, u32[]{:S(2)}, u32[]{:S(2)}) %collective-permute-start.22) | collective-permute-done | bytes 131104 | tf_op jit(solution)/shard_map/ppermute | solution.py:466
  70.5 3.2 %head_step.4 = (f32[32,8192]{1,0:T(8,128)S(1)}, bf16[32,8192]{1,0:T(8,128)(2,1)S(1)}, f32[8,128]{1,0:T(8,128)S(1)}, f32[16,32,128]{2,1,0:T(8,128)S(1)}, f32[16,3...) custom-call(s32[64]{0:T(128)S(1)} %bitcast.36, ...), custom_call_target="tpu_custom_call" | custom-call | flops 134217728 | bytes 7864320 | tf_op jit(solution)/shard_map/head_step/pallas_call | solution.py:292
  73.7 1.5 %collective-permute-start.26 = (bf16[17,32,128]{2,1,0:T(8,128)(2,1)S(1)}, bf16[17,32,128]{2,1,0:T(8,128)(2,1)S(1)}, u32[]{:S(2)}, u32[]{:S(2)}) collective-permute-start(bf16[17,32,128]{2,1,0:T(8,128)(2,1)S(1)} %get-tuple-element.110.refs_2_), channel_id=1, source_target_pairs={{0,4},{4,0},{8,12},{12,8},{16,20},{20,16},{24,28},{28,24},{1,5},{5... | collective-permute-start | bytes 417800 | tf_op jit(solution)/shard_map/ppermute | solution.py:466
  75.7 3.3 %local_forward.4.refs_5_ = f32[16,32,128]{2,1,0:T(8,128)S(1)} custom-call(s32[4,64]{1,0:T(4,128)S(1)} %bitcast.32, bf16[32,8192]{1,0:T(8,128)(2,1)S(1)} %get-tuple-element.113.bar_ref, bf16[64,4,128,128]{3,2,1,0:T(8,128)(2,1)S(1)} %bitcast.25, f32[16,32,128]{2,1,0:T(8,128)S(1)} %get-tuple-element.114.duals_ref, f32[32,2048]{1,0:T(8,128)S(1)} %copy-done.4), custom_call_target="tpu_custom_call" | custom-call | flops 268435456 | bytes 8388608 | tf_op jit(solution)/shard_map/local_forward/pallas_call | solution.py:390
  79.1 2.4 %collective-permute-done.27.refs_4_.refs_2_ = bf16[16,32,128]{2,1,0:T(8,128)(2,1)S(1)} collective-permute-done((bf16[16,32,128]{2,1,0:T(8,128)(2,1)S(1)}, bf16[16,32,128]{2,1,0:T(8,128)(2,1)S(1)}, u32[]{:S(2)}, u32[]{:S(2)}) %collective-permute-start.27) | collective-permute-done | bytes 131104 | tf_op jit(solution)/shard_map/ppermute | solution.py:466
  81.9 1.9 %collective-permute-start.24 = (bf16[16,32,128]{2,1,0:T(8,128)(2,1)S(1)}, bf16[16,32,128]{2,1,0:T(8,128)(2,1)S(1)}, u32[]{:S(2)}, u32[]{:S(2)}) collective-permute-start(bf16[16,32,128]{2,1,0:T(8,128)(2,1)S(1)} %get-tuple-element.106), channel_id=1, source_target_pairs={{0,8},{4,12},{8,0},{12,4},{16,24},{20,28},{24,16},{28,20},{1,9},{5... | collective-permute-start | bytes 393224 | tf_op jit(solution)/shard_map/ppermute | solution.py:466
  83.9 1.5 %collective-permute-start.29 = (f32[8,128]{1,0:T(8,128)S(1)}, f32[8,128]{1,0:T(8,128)S(1)}, u32[]{:S(2)}, u32[]{:S(2)}) collective-permute-start(f32[8,128]{1,0:T(8,128)S(1)} %get-tuple-element.116.refs_9_), channel_id=1, source_target_pairs={{0,2},{1,3},{2,0},{3,1},{4,6},{5,7},{6,4},{7,5},{8,10},{9,11},{10,... | collective-permute-start | bytes 12296 | tf_op jit(solution)/shard_map/ppermute | solution.py:466
  85.4 2.4 %collective-permute-done.25.refs_1_ = bf16[16,32,128]{2,1,0:T(8,128)(2,1)S(1)} collective-permute-done((bf16[16,32,128]{2,1,0:T(8,128)(2,1)S(1)}, bf16[16,32,128]{2,1,0:T(8,128)(2,1)S(1)}, u32[]{:S(2)}, u32[]{:S(2)}) %collective-permute-start.25) | collective-permute-done | bytes 131104 | tf_op jit(solution)/shard_map/ppermute | solution.py:466
  88.0 2.7 %collective-permute-start.31 = (bf16[17,32,128]{2,1,0:T(8,128)(2,1)S(1)}, bf16[17,32,128]{2,1,0:T(8,128)(2,1)S(1)}, u32[]{:S(2)}, u32[]{:S(2)}) collective-permute-start(bf16[17,32,128]{2,1,0:T(8,128)(2,1)S(1)} %fold.13.refs_2_.refs_4_), channel_id=1, source_target_pairs={{0,16},{4,20},{8,24},{12,28},{16,0},{20,4},{24,8},{28,12},{1,17},{... | collective-permute-start | bytes 417800 | tf_op jit(solution)/shard_map/ppermute | solution.py:466
  90.7 0.7 collective-permute-start.30
  91.4 4.3 %collective-permute-done.30.refs_1_ = bf16[16,32,128]{2,1,0:T(8,128)(2,1)S(1)} collective-permute-done((bf16[16,32,128]{2,1,0:T(8,128)(2,1)S(1)}, bf16[16,32,128]{2,1,0:T(8,128)(2,1)S(1)}, u32[]{:S(2)}, u32[]{:S(2)}) %collective-permute-start.30) | collective-permute-done | bytes 131104 | tf_op jit(solution)/shard_map/ppermute | solution.py:466
  95.8 2.1 %collective-permute-done.31.refs_3_ = bf16[17,32,128]{2,1,0:T(8,128)(2,1)S(1)} collective-permute-done((bf16[17,32,128]{2,1,0:T(8,128)(2,1)S(1)}, bf16[17,32,128]{2,1,0:T(8,128)(2,1)S(1)}, u32[]{:S(2)}, u32[]{:S(2)}) %collective-permute-start.31) | collective-permute-done | bytes 139296 | tf_op jit(solution)/shard_map/ppermute | solution.py:466
  98.5 4.3 %local_adjoint.5 = (f32[32,8192]{1,0:T(8,128)S(1)}, f32[8,128]{1,0:T(8,128)S(1)}) custom-call(s32[4,64]{1,0:T(4,128)S(1)} %bitcast.33, bf16[16,32,128]{2,1,0:T(8,128)(2,1)S(1)} %get-tuple-element.119.panel_ref.refs_0_, bf16[64,4,128,128]{3,2,1,0:T(8,128)(2,1)S(1)} %bitcast.25), custom_call_target="tpu_custom_call" | custom-call | flops 268435456 | bytes 8388608 | tf_op jit(solution)/shard_map/local_adjoint/pallas_call | solution.py:255
  102.8 2.0 %collective-permute-done.35.arrived_ref = bf16[16,32,128]{2,1,0:T(8,128)(2,1)S(1)} collective-permute-done((bf16[16,32,128]{2,1,0:T(8,128)(2,1)S(1)}, bf16[16,32,128]{2,1,0:T(8,128)(2,1)S(1)}, u32[]{:S(2)}, u32[]{:S(2)}) %collective-permute-start.35) | collective-permute-done | bytes 131104 | tf_op jit(solution)/shard_map/ppermute | solution.py:466
  104.8 1.4 %collective-permute-start.37 = (bf16[16,32,128]{2,1,0:T(8,128)(2,1)S(1)}, bf16[16,32,128]{2,1,0:T(8,128)(2,1)S(1)}, u32[]{:S(2)}, u32[]{:S(2)}) collective-permute-start(bf16[16,32,128]{2,1,0:T(8,128)(2,1)S(1)} %get-tuple-element.122.refs_4_), channel_id=1, source_target_pairs={{0,8},{4,12},{8,0},{12,4},{16,24},{20,28},{24,16},{28,20},{1,9},{5... | collective-permute-start | bytes 393224 | tf_op jit(solution)/shard_map/ppermute | solution.py:466
  106.2 0.7 collective-permute-start.33
  106.9 1.0 collective-permute-start.36
  108.5 1.3 collective-permute-done.37.refs_6_
  109.8 1.0 collective-permute-start.38
  111.2 0.8 collective-permute-done.39.refs_14_
  112.0 0.9 collective-permute-done.34.refs_3_
  112.9 1.9 %collective-permute-done.38.refs_7_ = bf16[16,32,128]{2,1,0:T(8,128)(2,1)S(1)} collective-permute-done((bf16[16,32,128]{2,1,0:T(8,128)(2,1)S(1)}, bf16[16,32,128]{2,1,0:T(8,128)(2,1)S(1)}, u32[]{:S(2)}, u32[]{:S(2)}) %collective-permute-start.38) | collective-permute-done | bytes 131104 | tf_op jit(solution)/shard_map/ppermute | solution.py:466
  114.8 3.9 %head_step.5 = (f32[32,8192]{1,0:T(8,128)}, bf16[32,8192]{1,0:T(8,128)(2,1)S(1)}, f32[8,128]{1,0:T(8,128)S(1)}, f32[16,32,128]{2,1,0:T(8,128)S(1)}, f32[16,32,12...) custom-call(s32[64]{0:T(128)S(1)} %bitcast.37, ...), custom_call_target="tpu_custom_call" | custom-call | flops 134217728 | bytes 7864320 | tf_op jit(solution)/shard_map/head_step/pallas_call | solution.py:292
  118.7 1.0 collective-permute-start.42
  120.3 3.3 %local_forward.5.refs_5_ = f32[16,32,128]{2,1,0:T(8,128)S(1)} custom-call(s32[4,64]{1,0:T(4,128)S(1)} %bitcast.34, bf16[32,8192]{1,0:T(8,128)(2,1)S(1)} %get-tuple-element.137.bar_ref, bf16[64,4,128,128]{3,2,1,0:T(8,128)(2,1)S(1)} %bitcast.25, f32[16,32,128]{2,1,0:T(8,128)S(1)} %get-tuple-element.138.duals_ref, f32[32,2048]{1,0:T(8,128)S(1)} %copy-done.4), custom_call_target="tpu_custom_call" | custom-call | flops 268435456 | bytes 8388608 | tf_op jit(solution)/shard_map/local_forward/pallas_call | solution.py:390
  123.6 1.7 %collective-permute-done.43.refs_4_.refs_2_ = bf16[16,32,128]{2,1,0:T(8,128)(2,1)S(1)} collective-permute-done((bf16[16,32,128]{2,1,0:T(8,128)(2,1)S(1)}, bf16[16,32,128]{2,1,0:T(8,128)(2,1)S(1)}, u32[]{:S(2)}, u32[]{:S(2)}) %collective-permute-start.43) | collective-permute-done | bytes 131104 | tf_op jit(solution)/shard_map/ppermute | solution.py:466
  126.0 2.5 %collective-permute-start.41 = (bf16[16,32,128]{2,1,0:T(8,128)(2,1)S(1)}, bf16[16,32,128]{2,1,0:T(8,128)(2,1)S(1)}, u32[]{:S(2)}, u32[]{:S(2)}) collective-permute-start(bf16[16,32,128]{2,1,0:T(8,128)(2,1)S(1)} %get-tuple-element.132), channel_id=1, source_target_pairs={{0,4},{4,0},{8,12},{12,8},{16,20},{20,16},{24,28},{28,24},{1,5},{5... | collective-permute-start | bytes 393224 | tf_op jit(solution)/shard_map/ppermute | solution.py:466
  129.1 1.5 %collective-permute-start.45 = (f32[8,128]{1,0:T(8,128)S(1)}, f32[8,128]{1,0:T(8,128)S(1)}, u32[]{:S(2)}, u32[]{:S(2)}) collective-permute-start(f32[8,128]{1,0:T(8,128)S(1)} %get-tuple-element.140.refs_9_), channel_id=1, source_target_pairs={{0,2},{1,3},{2,0},{3,1},{4,6},{5,7},{6,4},{7,5},{8,10},{9,11},{10,... | collective-permute-start | bytes 12296 | tf_op jit(solution)/shard_map/ppermute | solution.py:466
  130.6 2.1 %collective-permute-done.41.refs_1_ = bf16[16,32,128]{2,1,0:T(8,128)(2,1)S(1)} collective-permute-done((bf16[16,32,128]{2,1,0:T(8,128)(2,1)S(1)}, bf16[16,32,128]{2,1,0:T(8,128)(2,1)S(1)}, u32[]{:S(2)}, u32[]{:S(2)}) %collective-permute-start.41) | collective-permute-done | bytes 131104 | tf_op jit(solution)/shard_map/ppermute | solution.py:466
  132.9 1.8 %collective-permute-start.47 = (bf16[17,32,128]{2,1,0:T(8,128)(2,1)S(1)}, bf16[17,32,128]{2,1,0:T(8,128)(2,1)S(1)}, u32[]{:S(2)}, u32[]{:S(2)}) collective-permute-start(bf16[17,32,128]{2,1,0:T(8,128)(2,1)S(1)} %fold.16.refs_2_.refs_4_), channel_id=1, source_target_pairs={{0,16},{4,20},{8,24},{12,28},{16,0},{20,4},{24,8},{28,12},{1,17},{... | collective-permute-start | bytes 417800 | tf_op jit(solution)/shard_map/ppermute | solution.py:466
  134.7 1.0 collective-permute-start.46
  135.7 4.0 %collective-permute-done.46.refs_1_ = bf16[16,32,128]{2,1,0:T(8,128)(2,1)S(1)} collective-permute-done((bf16[16,32,128]{2,1,0:T(8,128)(2,1)S(1)}, bf16[16,32,128]{2,1,0:T(8,128)(2,1)S(1)}, u32[]{:S(2)}, u32[]{:S(2)}) %collective-permute-start.46) | collective-permute-done | bytes 131104 | tf_op jit(solution)/shard_map/ppermute | solution.py:466
  139.7 0.6 collective-permute-done.47.refs_3_
  140.4 0.8 settle.5
  (86 shorter events, 12.0 us)
Async XLA Ops:
  0.6 1.0 copy-start
  0.6 23.2 %copy-start.10 = (s32[64]{0:T(128)S(1)}, s32[64]{0:T(128)}, u32[]{:S(2)}) copy-start(s32[64]{0:T(128)} %param.21) | copy-start | bytes 772
  0.7 23.2 %copy-start.8 = (f32[32]{0:T(128)S(1)}, f32[32]{0:T(128)}, u32[]{:S(2)}) copy-start(f32[32]{0:T(128)} %param.15) | copy-start | bytes 388
  0.7 23.2 %copy-start.9 = (f32[32]{0:T(128)S(1)}, f32[32]{0:T(128)}, u32[]{:S(2)}) copy-start(f32[32]{0:T(128)} %param.14) | copy-start | bytes 388
  0.7 26.9 %copy-start.5 = (f32[8192]{0:T(1024)S(1)}, f32[8192]{0:T(1024)}, u32[]{:S(2)}) copy-start(f32[8192]{0:T(1024)} %param.17) | copy-start | bytes 98308
  1.6 14.0 %collective-permute-start = (bf16[16,32,128]{2,1,0:T(8,128)(2,1)S(1)}, bf16[16,32,128]{2,1,0:T(8,128)(2,1)S(1)}, u32[]{:S(2)}, u32[]{:S(2)}) collective-permute-start(bf16[16,32,128]{2,1,0:T(8,128)(2,1)S(1)} %fusion.panel_ref.refs_0_), channel_id=1, source_target_pairs={{0,16},{4,20},{8,24},{12,28},{16,0},{20,4},{24,8},{28,12},{1,17},{... | collective-permute-start | bytes 393224 | tf_op jit(solution)/shard_map/ppermute | solution.py:466
  5.7 13.0 %collective-permute-start.1 = (bf16[16,32,128]{2,1,0:T(8,128)(2,1)S(1)}, bf16[16,32,128]{2,1,0:T(8,128)(2,1)S(1)}, u32[]{:S(2)}, u32[]{:S(2)}) collective-permute-start(bf16[16,32,128]{2,1,0:T(8,128)(2,1)S(1)} %fusion.panel_ref.refs_0_), channel_id=1, source_target_pairs={{0,4},{4,0},{8,12},{12,8},{16,20},{20,16},{24,28},{28,24},{1,5},{5... | collective-permute-start | bytes 393224 | tf_op jit(solution)/shard_map/ppermute | solution.py:466
  7.2 3.4 %copy-start.1 = (bf16[64,4,128,128]{3,2,1,0:T(8,128)(2,1)S(1)}, bf16[64,4,128,128]{3,2,1,0:T(8,128)(2,1)}, u32[]{:S(2)}) copy-start(bf16[64,4,128,128]{3,2,1,0:T(8,128)(2,1)} %blocks_ref.11) | copy-start | bytes 25165828
  10.6 0.7 copy-start.6
  11.3 12.6 %copy-start.2 = (bf16[64,128,128]{2,1,0:T(8,128)(2,1)S(1)}, bf16[64,128,128]{2,1,0:T(8,128)(2,1)}, u32[]{:S(2)}) copy-start(bf16[64,128,128]{2,1,0:T(8,128)(2,1)} %refs_8_.5) | copy-start | bytes 6291460
  11.3 12.6 %copy-start.3 = (f32[32,8192]{1,0:T(8,128)S(1)}, f32[32,8192]{1,0:T(8,128)}, u32[]{:S(2)}) copy-start(f32[32,8192]{1,0:T(8,128)} %refs_10_.1) | copy-start | bytes 3145732
  11.3 21.7 %slice-start = ((s8[8388608]{0:T(1024)(128)(4,1)}), s8[4194304]{0:T(1024)(128)(4,1)S(1)}, s32[]{:S(2)}) async-start(s8[8388608]{0:T(1024)(128)(4,1)} %bitcast.24), calls=%async_computation | async-start | bytes 8388608
  11.3 21.7 %copy-start.4 = (f32[32,2048]{1,0:T(8,128)S(1)}, f32[32,2048]{1,0:T(8,128)}, u32[]{:S(2)}) copy-start(f32[32,2048]{1,0:T(8,128)} %demand_ref.5) | copy-start | bytes 786436
  16.2 6.4 %collective-permute-start.5 = (bf16[16,32,128]{2,1,0:T(8,128)(2,1)S(1)}, bf16[16,32,128]{2,1,0:T(8,128)(2,1)S(1)}, u32[]{:S(2)}, u32[]{:S(2)}) collective-permute-start(bf16[16,32,128]{2,1,0:T(8,128)(2,1)S(1)} %get-tuple-element.77.refs_0_.refs_4_), channel_id=1, source_target_pairs={{0,8},{4,12},{8,0},{12,4},{16,24},{20,28},{24,16},{28,20},{1,9},{5... | collective-permute-start | bytes 393224 | tf_op jit(solution)/shard_map/ppermute | solution.py:466
  17.8 7.3 %collective-permute-start.2 = (bf16[16,32,128]{2,1,0:T(8,128)(2,1)S(1)}, bf16[16,32,128]{2,1,0:T(8,128)(2,1)S(1)}, u32[]{:S(2)}, u32[]{:S(2)}) collective-permute-start(bf16[16,32,128]{2,1,0:T(8,128)(2,1)S(1)} %fusion.panel_ref.refs_0_), channel_id=1, source_target_pairs={{0,8},{4,12},{8,0},{12,4},{16,24},{20,28},{24,16},{28,20},{1,9},{5... | collective-permute-start | bytes 393224 | tf_op jit(solution)/shard_map/ppermute | solution.py:466
  18.2 8.3 %collective-permute-start.4 = (bf16[16,32,128]{2,1,0:T(8,128)(2,1)S(1)}, bf16[16,32,128]{2,1,0:T(8,128)(2,1)S(1)}, u32[]{:S(2)}, u32[]{:S(2)}) collective-permute-start(bf16[16,32,128]{2,1,0:T(8,128)(2,1)S(1)} %get-tuple-element.77.refs_0_.refs_4_), channel_id=1, source_target_pairs={{0,4},{4,0},{8,12},{12,8},{16,20},{20,16},{24,28},{28,24},{1,5},{5... | collective-permute-start | bytes 393224 | tf_op jit(solution)/shard_map/ppermute | solution.py:466
  18.8 7.7 %collective-permute-start.3 = (bf16[16,32,128]{2,1,0:T(8,128)(2,1)S(1)}, bf16[16,32,128]{2,1,0:T(8,128)(2,1)S(1)}, u32[]{:S(2)}, u32[]{:S(2)}) collective-permute-start(bf16[16,32,128]{2,1,0:T(8,128)(2,1)S(1)} %collective-permute-done.1.refs_1_), channel_id=1, source_target_pairs={{0,8},{4,12},{8,0},{12,4},{16,24},{20,28},{24,16},{28,20},{1,9},{5... | collective-permute-start | bytes 393224 | tf_op jit(solution)/shard_map/ppermute | solution.py:466
  22.6 5.0 %collective-permute-start.6 = (bf16[16,32,128]{2,1,0:T(8,128)(2,1)S(1)}, bf16[16,32,128]{2,1,0:T(8,128)(2,1)S(1)}, u32[]{:S(2)}, u32[]{:S(2)}) collective-permute-start(bf16[16,32,128]{2,1,0:T(8,128)(2,1)S(1)} %collective-permute-done.5.refs_6_), channel_id=1, source_target_pairs={{0,4},{4,0},{8,12},{12,8},{16,20},{20,16},{24,28},{28,24},{1,5},{5... | collective-permute-start | bytes 393224 | tf_op jit(solution)/shard_map/ppermute | solution.py:466
  23.9 9.2 %slice-start.1 = ((s8[8388608]{0:T(1024)(128)(4,1)}), s8[4194304]{0:T(1024)(128)(4,1)S(1)}, s32[]{:S(2)}) async-start(s8[8388608]{0:T(1024)(128)(4,1)} %bitcast.24), calls=%async_computation.1 | async-start | bytes 8388608
  24.0 1.2 collective-permute-start.7
  27.6 28.4 %copy-start.7 = (s32[64,4]{0,1:T(4,128)S(1)}, s32[64,4]{0,1:T(4,128)}, u32[]{:S(2)}) copy-start(s32[64,4]{0,1:T(4,128)} %param.20) | copy-start | bytes 3076
  30.8 5.6 %collective-permute-start.11 = (bf16[16,32,128]{2,1,0:T(8,128)(2,1)S(1)}, bf16[16,32,128]{2,1,0:T(8,128)(2,1)S(1)}, u32[]{:S(2)}, u32[]{:S(2)}) collective-permute-start(bf16[16,32,128]{2,1,0:T(8,128)(2,1)S(1)} %get-tuple-element.90), channel_id=1, source_target_pairs={{0,8},{4,12},{8,0},{12,4},{16,24},{20,28},{24,16},{28,20},{1,9},{5... | collective-permute-start | bytes 393224 | tf_op jit(solution)/shard_map/ppermute | solution.py:466
  32.4 5.1 %collective-permute-start.10 = (bf16[17,32,128]{2,1,0:T(8,128)(2,1)S(1)}, bf16[17,32,128]{2,1,0:T(8,128)(2,1)S(1)}, u32[]{:S(2)}, u32[]{:S(2)}) collective-permute-start(bf16[17,32,128]{2,1,0:T(8,128)(2,1)S(1)} %get-tuple-element.88.refs_2_), channel_id=1, source_target_pairs={{0,4},{4,0},{8,12},{12,8},{16,20},{20,16},{24,28},{28,24},{1,5},{5... | collective-permute-start | bytes 417800 | tf_op jit(solution)/shard_map/ppermute | solution.py:466
  37.6 6.2 %collective-permute-start.12 = (bf16[17,32,128]{2,1,0:T(8,128)(2,1)S(1)}, bf16[17,32,128]{2,1,0:T(8,128)(2,1)S(1)}, u32[]{:S(2)}, u32[]{:S(2)}) collective-permute-start(bf16[17,32,128]{2,1,0:T(8,128)(2,1)S(1)} %get-tuple-element.92.refs_3_), channel_id=1, source_target_pairs={{0,8},{4,12},{8,0},{12,4},{16,24},{20,28},{24,16},{28,20},{1,9},{5... | collective-permute-start | bytes 417800 | tf_op jit(solution)/shard_map/ppermute | solution.py:466
  38.1 5.2 %collective-permute-start.9 = (bf16[16,32,128]{2,1,0:T(8,128)(2,1)S(1)}, bf16[16,32,128]{2,1,0:T(8,128)(2,1)S(1)}, u32[]{:S(2)}, u32[]{:S(2)}) collective-permute-start(bf16[16,32,128]{2,1,0:T(8,128)(2,1)S(1)} %get-tuple-element.86), channel_id=1, source_target_pairs={{0,4},{4,0},{8,12},{12,8},{16,20},{20,16},{24,28},{28,24},{1,5},{5... | collective-permute-start | bytes 393224 | tf_op jit(solution)/shard_map/ppermute | solution.py:466
  38.6 6.3 %collective-permute-start.8 = (bf16[16,32,128]{2,1,0:T(8,128)(2,1)S(1)}, bf16[16,32,128]{2,1,0:T(8,128)(2,1)S(1)}, u32[]{:S(2)}, u32[]{:S(2)}) collective-permute-start(bf16[16,32,128]{2,1,0:T(8,128)(2,1)S(1)} %get-tuple-element.84), channel_id=1, source_target_pairs={{0,8},{4,12},{8,0},{12,4},{16,24},{20,28},{24,16},{28,20},{1,9},{5... | collective-permute-start | bytes 393224 | tf_op jit(solution)/shard_map/ppermute | solution.py:466
  40.2 3.6 %collective-permute-start.13 = (f32[8,128]{1,0:T(8,128)S(1)}, f32[8,128]{1,0:T(8,128)S(1)}, u32[]{:S(2)}, u32[]{:S(2)}) collective-permute-start(f32[8,128]{1,0:T(8,128)S(1)} %get-tuple-element.93.refs_9_), channel_id=1, source_target_pairs={{0,2},{1,3},{2,0},{3,1},{4,6},{5,7},{6,4},{7,5},{8,10},{9,11},{10,... | collective-permute-start | bytes 12296 | tf_op jit(solution)/shard_map/ppermute | solution.py:466
  44.0 9.4 %collective-permute-start.15 = (bf16[17,32,128]{2,1,0:T(8,128)(2,1)S(1)}, bf16[17,32,128]{2,1,0:T(8,128)(2,1)S(1)}, u32[]{:S(2)}, u32[]{:S(2)}) collective-permute-start(bf16[17,32,128]{2,1,0:T(8,128)(2,1)S(1)} %fold.10.refs_2_.refs_4_), channel_id=1, source_target_pairs={{0,16},{4,20},{8,24},{12,28},{16,0},{20,4},{24,8},{28,12},{1,17},{... | collective-permute-start | bytes 417800 | tf_op jit(solution)/shard_map/ppermute | solution.py:466
  45.0 6.1 %collective-permute-start.14 = (bf16[16,32,128]{2,1,0:T(8,128)(2,1)S(1)}, bf16[16,32,128]{2,1,0:T(8,128)(2,1)S(1)}, u32[]{:S(2)}, u32[]{:S(2)}) collective-permute-start(bf16[16,32,128]{2,1,0:T(8,128)(2,1)S(1)} %fold.11), channel_id=1, source_target_pairs={{0,4},{4,0},{8,12},{12,8},{16,20},{20,16},{24,28},{28,24},{1,5},{5... | collective-permute-start | bytes 393224 | tf_op jit(solution)/shard_map/ppermute | solution.py:466
  53.5 6.9 %collective-permute-start.19 = (bf16[16,32,128]{2,1,0:T(8,128)(2,1)S(1)}, bf16[16,32,128]{2,1,0:T(8,128)(2,1)S(1)}, u32[]{:S(2)}, u32[]{:S(2)}) collective-permute-start(bf16[16,32,128]{2,1,0:T(8,128)(2,1)S(1)} %get-tuple-element.96.panel_ref.refs_0_), channel_id=1, source_target_pairs={{0,16},{4,20},{8,24},{12,28},{16,0},{20,4},{24,8},{28,12},{1,17},{... | collective-permute-start | bytes 393224 | tf_op jit(solution)/shard_map/ppermute | solution.py:466
  53.6 10.4 %collective-permute-start.16 = (bf16[16,32,128]{2,1,0:T(8,128)(2,1)S(1)}, bf16[16,32,128]{2,1,0:T(8,128)(2,1)S(1)}, u32[]{:S(2)}, u32[]{:S(2)}) collective-permute-start(bf16[16,32,128]{2,1,0:T(8,128)(2,1)S(1)} %get-tuple-element.96.panel_ref.refs_0_), channel_id=1, source_target_pairs={{0,4},{4,0},{8,12},{12,8},{16,20},{20,16},{24,28},{28,24},{1,5},{5... | collective-permute-start | bytes 393224 | tf_op jit(solution)/shard_map/ppermute | solution.py:466
  60.5 5.0 %collective-permute-start.21 = (bf16[16,32,128]{2,1,0:T(8,128)(2,1)S(1)}, bf16[16,32,128]{2,1,0:T(8,128)(2,1)S(1)}, u32[]{:S(2)}, u32[]{:S(2)}) collective-permute-start(bf16[16,32,128]{2,1,0:T(8,128)(2,1)S(1)} %get-tuple-element.99.refs_4_), channel_id=1, source_target_pairs={{0,8},{4,12},{8,0},{12,4},{16,24},{20,28},{24,16},{28,20},{1,9},{5... | collective-permute-start | bytes 393224 | tf_op jit(solution)/shard_map/ppermute | solution.py:466
  60.6 6.4 %collective-permute-start.17 = (bf16[16,32,128]{2,1,0:T(8,128)(2,1)S(1)}, bf16[16,32,128]{2,1,0:T(8,128)(2,1)S(1)}, u32[]{:S(2)}, u32[]{:S(2)}) collective-permute-start(bf16[16,32,128]{2,1,0:T(8,128)(2,1)S(1)} %get-tuple-element.96.panel_ref.refs_0_), channel_id=1, source_target_pairs={{0,8},{4,12},{8,0},{12,4},{16,24},{20,28},{24,16},{28,20},{1,9},{5... | collective-permute-start | bytes 393224 | tf_op jit(solution)/shard_map/ppermute | solution.py:466
  62.6 6.4 %collective-permute-start.20 = (bf16[16,32,128]{2,1,0:T(8,128)(2,1)S(1)}, bf16[16,32,128]{2,1,0:T(8,128)(2,1)S(1)}, u32[]{:S(2)}, u32[]{:S(2)}) collective-permute-start(bf16[16,32,128]{2,1,0:T(8,128)(2,1)S(1)} %get-tuple-element.99.refs_4_), channel_id=1, source_target_pairs={{0,4},{4,0},{8,12},{12,8},{16,20},{20,16},{24,28},{28,24},{1,5},{5... | collective-permute-start | bytes 393224 | tf_op jit(solution)/shard_map/ppermute | solution.py:466
  64.0 5.0 %collective-permute-start.18 = (bf16[16,32,128]{2,1,0:T(8,128)(2,1)S(1)}, bf16[16,32,128]{2,1,0:T(8,128)(2,1)S(1)}, u32[]{:S(2)}, u32[]{:S(2)}) collective-permute-start(bf16[16,32,128]{2,1,0:T(8,128)(2,1)S(1)} %collective-permute-done.16.refs_1_), channel_id=1, source_target_pairs={{0,8},{4,12},{8,0},{12,4},{16,24},{20,28},{24,16},{28,20},{1,9},{5... | collective-permute-start | bytes 393224 | tf_op jit(solution)/shard_map/ppermute | solution.py:466
  65.5 5.0 %collective-permute-start.22 = (bf16[16,32,128]{2,1,0:T(8,128)(2,1)S(1)}, bf16[16,32,128]{2,1,0:T(8,128)(2,1)S(1)}, u32[]{:S(2)}, u32[]{:S(2)}) collective-permute-start(bf16[16,32,128]{2,1,0:T(8,128)(2,1)S(1)} %collective-permute-done.21.refs_6_), channel_id=1, source_target_pairs={{0,4},{4,0},{8,12},{12,8},{16,20},{20,16},{24,28},{28,24},{1,5},{5... | collective-permute-start | bytes 393224 | tf_op jit(solution)/shard_map/ppermute | solution.py:466
  66.9 1.2 collective-permute-start.23
  73.7 7.8 %collective-permute-start.26 = (bf16[17,32,128]{2,1,0:T(8,128)(2,1)S(1)}, bf16[17,32,128]{2,1,0:T(8,128)(2,1)S(1)}, u32[]{:S(2)}, u32[]{:S(2)}) collective-permute-start(bf16[17,32,128]{2,1,0:T(8,128)(2,1)S(1)} %get-tuple-element.110.refs_2_), channel_id=1, source_target_pairs={{0,4},{4,0},{8,12},{12,8},{16,20},{20,16},{24,28},{28,24},{1,5},{5... | collective-permute-start | bytes 417800 | tf_op jit(solution)/shard_map/ppermute | solution.py:466
  75.1 6.4 %collective-permute-start.27 = (bf16[16,32,128]{2,1,0:T(8,128)(2,1)S(1)}, bf16[16,32,128]{2,1,0:T(8,128)(2,1)S(1)}, u32[]{:S(2)}, u32[]{:S(2)}) collective-permute-start(bf16[16,32,128]{2,1,0:T(8,128)(2,1)S(1)} %get-tuple-element.112), channel_id=1, source_target_pairs={{0,8},{4,12},{8,0},{12,4},{16,24},{20,28},{24,16},{28,20},{1,9},{5... | collective-permute-start | bytes 393224 | tf_op jit(solution)/shard_map/ppermute | solution.py:466
  81.6 6.3 %collective-permute-start.28 = (bf16[17,32,128]{2,1,0:T(8,128)(2,1)S(1)}, bf16[17,32,128]{2,1,0:T(8,128)(2,1)S(1)}, u32[]{:S(2)}, u32[]{:S(2)}) collective-permute-start(bf16[17,32,128]{2,1,0:T(8,128)(2,1)S(1)} %get-tuple-element.115.refs_3_), channel_id=1, source_target_pairs={{0,8},{4,12},{8,0},{12,4},{16,24},{20,28},{24,16},{28,20},{1,9},{5... | collective-permute-start | bytes 417800 | tf_op jit(solution)/shard_map/ppermute | solution.py:466
  81.9 5.9 %collective-permute-start.25 = (bf16[16,32,128]{2,1,0:T(8,128)(2,1)S(1)}, bf16[16,32,128]{2,1,0:T(8,128)(2,1)S(1)}, u32[]{:S(2)}, u32[]{:S(2)}) collective-permute-start(bf16[16,32,128]{2,1,0:T(8,128)(2,1)S(1)} %get-tuple-element.108), channel_id=1, source_target_pairs={{0,4},{4,0},{8,12},{12,8},{16,20},{20,16},{24,28},{28,24},{1,5},{5... | collective-permute-start | bytes 393224 | tf_op jit(solution)/shard_map/ppermute | solution.py:466
  81.9 8.8 %collective-permute-start.24 = (bf16[16,32,128]{2,1,0:T(8,128)(2,1)S(1)}, bf16[16,32,128]{2,1,0:T(8,128)(2,1)S(1)}, u32[]{:S(2)}, u32[]{:S(2)}) collective-permute-start(bf16[16,32,128]{2,1,0:T(8,128)(2,1)S(1)} %get-tuple-element.106), channel_id=1, source_target_pairs={{0,8},{4,12},{8,0},{12,4},{16,24},{20,28},{24,16},{28,20},{1,9},{5... | collective-permute-start | bytes 393224 | tf_op jit(solution)/shard_map/ppermute | solution.py:466
  83.9 3.9 %collective-permute-start.29 = (f32[8,128]{1,0:T(8,128)S(1)}, f32[8,128]{1,0:T(8,128)S(1)}, u32[]{:S(2)}, u32[]{:S(2)}) collective-permute-start(f32[8,128]{1,0:T(8,128)S(1)} %get-tuple-element.116.refs_9_), channel_id=1, source_target_pairs={{0,2},{1,3},{2,0},{3,1},{4,6},{5,7},{6,4},{7,5},{8,10},{9,11},{10,... | collective-permute-start | bytes 12296 | tf_op jit(solution)/shard_map/ppermute | solution.py:466
  88.0 9.9 %collective-permute-start.31 = (bf16[17,32,128]{2,1,0:T(8,128)(2,1)S(1)}, bf16[17,32,128]{2,1,0:T(8,128)(2,1)S(1)}, u32[]{:S(2)}, u32[]{:S(2)}) collective-permute-start(bf16[17,32,128]{2,1,0:T(8,128)(2,1)S(1)} %fold.13.refs_2_.refs_4_), channel_id=1, source_target_pairs={{0,16},{4,20},{8,24},{12,28},{16,0},{20,4},{24,8},{28,12},{1,17},{... | collective-permute-start | bytes 417800 | tf_op jit(solution)/shard_map/ppermute | solution.py:466
  90.7 5.0 %collective-permute-start.30 = (bf16[16,32,128]{2,1,0:T(8,128)(2,1)S(1)}, bf16[16,32,128]{2,1,0:T(8,128)(2,1)S(1)}, u32[]{:S(2)}, u32[]{:S(2)}) collective-permute-start(bf16[16,32,128]{2,1,0:T(8,128)(2,1)S(1)} %fold.14), channel_id=1, source_target_pairs={{0,4},{4,0},{8,12},{12,8},{16,20},{20,16},{24,28},{28,24},{1,5},{5... | collective-permute-start | bytes 393224 | tf_op jit(solution)/shard_map/ppermute | solution.py:466
  98.1 6.7 %collective-permute-start.35 = (bf16[16,32,128]{2,1,0:T(8,128)(2,1)S(1)}, bf16[16,32,128]{2,1,0:T(8,128)(2,1)S(1)}, u32[]{:S(2)}, u32[]{:S(2)}) collective-permute-start(bf16[16,32,128]{2,1,0:T(8,128)(2,1)S(1)} %get-tuple-element.119.panel_ref.refs_0_), channel_id=1, source_target_pairs={{0,16},{4,20},{8,24},{12,28},{16,0},{20,4},{24,8},{28,12},{1,17},{... | collective-permute-start | bytes 393224 | tf_op jit(solution)/shard_map/ppermute | solution.py:466
  98.1 9.8 %collective-permute-start.32 = (bf16[16,32,128]{2,1,0:T(8,128)(2,1)S(1)}, bf16[16,32,128]{2,1,0:T(8,128)(2,1)S(1)}, u32[]{:S(2)}, u32[]{:S(2)}) collective-permute-start(bf16[16,32,128]{2,1,0:T(8,128)(2,1)S(1)} %get-tuple-element.119.panel_ref.refs_0_), channel_id=1, source_target_pairs={{0,4},{4,0},{8,12},{12,8},{16,20},{20,16},{24,28},{28,24},{1,5},{5... | collective-permute-start | bytes 393224 | tf_op jit(solution)/shard_map/ppermute | solution.py:466
  104.8 5.0 %collective-permute-start.37 = (bf16[16,32,128]{2,1,0:T(8,128)(2,1)S(1)}, bf16[16,32,128]{2,1,0:T(8,128)(2,1)S(1)}, u32[]{:S(2)}, u32[]{:S(2)}) collective-permute-start(bf16[16,32,128]{2,1,0:T(8,128)(2,1)S(1)} %get-tuple-element.122.refs_4_), channel_id=1, source_target_pairs={{0,8},{4,12},{8,0},{12,4},{16,24},{20,28},{24,16},{28,20},{1,9},{5... | collective-permute-start | bytes 393224 | tf_op jit(solution)/shard_map/ppermute | solution.py:466
  106.2 5.0 %collective-permute-start.33 = (bf16[16,32,128]{2,1,0:T(8,128)(2,1)S(1)}, bf16[16,32,128]{2,1,0:T(8,128)(2,1)S(1)}, u32[]{:S(2)}, u32[]{:S(2)}) collective-permute-start(bf16[16,32,128]{2,1,0:T(8,128)(2,1)S(1)} %get-tuple-element.119.panel_ref.refs_0_), channel_id=1, source_target_pairs={{0,8},{4,12},{8,0},{12,4},{16,24},{20,28},{24,16},{28,20},{1,9},{5... | collective-permute-start | bytes 393224 | tf_op jit(solution)/shard_map/ppermute | solution.py:466
  106.9 6.0 %collective-permute-start.36 = (bf16[16,32,128]{2,1,0:T(8,128)(2,1)S(1)}, bf16[16,32,128]{2,1,0:T(8,128)(2,1)S(1)}, u32[]{:S(2)}, u32[]{:S(2)}) collective-permute-start(bf16[16,32,128]{2,1,0:T(8,128)(2,1)S(1)} %get-tuple-element.122.refs_4_), channel_id=1, source_target_pairs={{0,4},{4,0},{8,12},{12,8},{16,20},{20,16},{24,28},{28,24},{1,5},{5... | collective-permute-start | bytes 393224 | tf_op jit(solution)/shard_map/ppermute | solution.py:466
  107.9 5.0 %collective-permute-start.34 = (bf16[16,32,128]{2,1,0:T(8,128)(2,1)S(1)}, bf16[16,32,128]{2,1,0:T(8,128)(2,1)S(1)}, u32[]{:S(2)}, u32[]{:S(2)}) collective-permute-start(bf16[16,32,128]{2,1,0:T(8,128)(2,1)S(1)} %collective-permute-done.32.refs_1_), channel_id=1, source_target_pairs={{0,8},{4,12},{8,0},{12,4},{16,24},{20,28},{24,16},{28,20},{1,9},{5... | collective-permute-start | bytes 393224 | tf_op jit(solution)/shard_map/ppermute | solution.py:466
  109.8 5.0 %collective-permute-start.38 = (bf16[16,32,128]{2,1,0:T(8,128)(2,1)S(1)}, bf16[16,32,128]{2,1,0:T(8,128)(2,1)S(1)}, u32[]{:S(2)}, u32[]{:S(2)}) collective-permute-start(bf16[16,32,128]{2,1,0:T(8,128)(2,1)S(1)} %collective-permute-done.37.refs_6_), channel_id=1, source_target_pairs={{0,4},{4,0},{8,12},{12,8},{16,20},{20,16},{24,28},{28,24},{1,5},{5... | collective-permute-start | bytes 393224 | tf_op jit(solution)/shard_map/ppermute | solution.py:466
  110.8 1.2 collective-permute-start.39
  118.7 6.6 %collective-permute-start.42 = (bf16[17,32,128]{2,1,0:T(8,128)(2,1)S(1)}, bf16[17,32,128]{2,1,0:T(8,128)(2,1)S(1)}, u32[]{:S(2)}, u32[]{:S(2)}) collective-permute-start(bf16[17,32,128]{2,1,0:T(8,128)(2,1)S(1)} %get-tuple-element.134.refs_2_), channel_id=1, source_target_pairs={{0,4},{4,0},{8,12},{12,8},{16,20},{20,16},{24,28},{28,24},{1,5},{5... | collective-permute-start | bytes 417800 | tf_op jit(solution)/shard_map/ppermute | solution.py:466
  119.7 5.6 %collective-permute-start.43 = (bf16[16,32,128]{2,1,0:T(8,128)(2,1)S(1)}, bf16[16,32,128]{2,1,0:T(8,128)(2,1)S(1)}, u32[]{:S(2)}, u32[]{:S(2)}) collective-permute-start(bf16[16,32,128]{2,1,0:T(8,128)(2,1)S(1)} %get-tuple-element.136), channel_id=1, source_target_pairs={{0,8},{4,12},{8,0},{12,4},{16,24},{20,28},{24,16},{28,20},{1,9},{5... | collective-permute-start | bytes 393224 | tf_op jit(solution)/shard_map/ppermute | solution.py:466
  125.4 7.3 %collective-permute-start.44 = (bf16[17,32,128]{2,1,0:T(8,128)(2,1)S(1)}, bf16[17,32,128]{2,1,0:T(8,128)(2,1)S(1)}, u32[]{:S(2)}, u32[]{:S(2)}) collective-permute-start(bf16[17,32,128]{2,1,0:T(8,128)(2,1)S(1)} %get-tuple-element.139.refs_3_), channel_id=1, source_target_pairs={{0,8},{4,12},{8,0},{12,4},{16,24},{20,28},{24,16},{28,20},{1,9},{5... | collective-permute-start | bytes 417800 | tf_op jit(solution)/shard_map/ppermute | solution.py:466
  126.0 6.8 %collective-permute-start.41 = (bf16[16,32,128]{2,1,0:T(8,128)(2,1)S(1)}, bf16[16,32,128]{2,1,0:T(8,128)(2,1)S(1)}, u32[]{:S(2)}, u32[]{:S(2)}) collective-permute-start(bf16[16,32,128]{2,1,0:T(8,128)(2,1)S(1)} %get-tuple-element.132), channel_id=1, source_target_pairs={{0,4},{4,0},{8,12},{12,8},{16,20},{20,16},{24,28},{28,24},{1,5},{5... | collective-permute-start | bytes 393224 | tf_op jit(solution)/shard_map/ppermute | solution.py:466
  128.5 6.2 %collective-permute-start.40 = (bf16[16,32,128]{2,1,0:T(8,128)(2,1)S(1)}, bf16[16,32,128]{2,1,0:T(8,128)(2,1)S(1)}, u32[]{:S(2)}, u32[]{:S(2)}) collective-permute-start(bf16[16,32,128]{2,1,0:T(8,128)(2,1)S(1)} %get-tuple-element.130), channel_id=1, source_target_pairs={{0,8},{4,12},{8,0},{12,4},{16,24},{20,28},{24,16},{28,20},{1,9},{5... | collective-permute-start | bytes 393224 | tf_op jit(solution)/shard_map/ppermute | solution.py:466
  129.1 3.6 %collective-permute-start.45 = (f32[8,128]{1,0:T(8,128)S(1)}, f32[8,128]{1,0:T(8,128)S(1)}, u32[]{:S(2)}, u32[]{:S(2)}) collective-permute-start(f32[8,128]{1,0:T(8,128)S(1)} %get-tuple-element.140.refs_9_), channel_id=1, source_target_pairs={{0,2},{1,3},{2,0},{3,1},{4,6},{5,7},{6,4},{7,5},{8,10},{9,11},{10,... | collective-permute-start | bytes 12296 | tf_op jit(solution)/shard_map/ppermute | solution.py:466
  132.9 7.5 %collective-permute-start.47 = (bf16[17,32,128]{2,1,0:T(8,128)(2,1)S(1)}, bf16[17,32,128]{2,1,0:T(8,128)(2,1)S(1)}, u32[]{:S(2)}, u32[]{:S(2)}) collective-permute-start(bf16[17,32,128]{2,1,0:T(8,128)(2,1)S(1)} %fold.16.refs_2_.refs_4_), channel_id=1, source_target_pairs={{0,16},{4,20},{8,24},{12,28},{16,0},{20,4},{24,8},{28,12},{1,17},{... | collective-permute-start | bytes 417800 | tf_op jit(solution)/shard_map/ppermute | solution.py:466
  134.7 5.0 %collective-permute-start.46 = (bf16[16,32,128]{2,1,0:T(8,128)(2,1)S(1)}, bf16[16,32,128]{2,1,0:T(8,128)(2,1)S(1)}, u32[]{:S(2)}, u32[]{:S(2)}) collective-permute-start(bf16[16,32,128]{2,1,0:T(8,128)(2,1)S(1)} %fold.17), channel_id=1, source_target_pairs={{0,4},{4,0},{8,12},{12,8},{16,20},{20,16},{24,28},{28,24},{1,5},{5... | collective-permute-start | bytes 393224 | tf_op jit(solution)/shard_map/ppermute | solution.py:466

commit v12 on v11

--- a/solution.py
+++ b/solution.py
@@ -16,7 +16,7 @@
 
 MIB = 1024 * 1024
 GROUP = 8
-HEAD_GROUP = 32
+HEAD_GROUP = 64
 SMALL_VMEM = 6 * MIB
 
 
@@ -283,7 +283,7 @@
     scen_rows = flows.shape[0]
     peers = len(panels)
     node_blks = panels[0].shape[0]
-    group = HEAD_GROUP
+    group = min(HEAD_GROUP, arc_blks)
     steps = arc_blks // group
     kept = (node_blks, scen_rows, rows)
     sent = [kept] * (peers // 2)
@@ -528,8 +528,7 @@
         tops = sorted(inner(net_size), key=lambda k: (-k.bit_count(), -k))[:-1]
         groups = [(top,) for top in tops if top != 1] + [(1,)]
         loss, loss_top = sends[net_size - 1], net_size - 1
-        ahead = {k: swap(sends[k], "net", last_hop(k)) for k in (2,)}
-        after = (ahead[2], base)
+        after = (base,)
         for group in groups:
             terms = []
             for top in group:
@@ -537,7 +536,7 @@
                 terms.append(
                     (
                         kept[top],
-                        [ahead[k] if k in ahead else swap(sends[k], "net", last_hop(k)) for k in below],
+                        [swap(sends[k], "net", last_hop(k)) for k in below],
                     )
                 )
             chain = loss_top ^ last_hop(loss_top) == group[0]
@@ -557,7 +556,7 @@
                     risk_sum = risk_sum + swap(risk_sum, "scen", stride)
                 risk_sums = (risk_sum, swap(risk_sum, "scen", strides[-1]))
         below = sorted(children(0, net_size))
-        arrived = [ahead[k] if k in ahead else swap(sends[k], "net", last_hop(k)) for k in below]
+        arrived = [swap(sends[k], "net", last_hop(k)) for k in below]
         duals, half, risk, excess_now, level, risk_sum = settle(
             kept[0],
             arrived,

time: 141 us -> 138 us (0.979)
  starting transfers between devices: 50 us -> 37.3 us
  waiting for transfers between devices: 48.7 us -> 60 us
  Pallas kernels: 35.8 us -> 34.3 us
    ppermute x48, starting transfers between devices: 50 us -> 37.3 us  [swap(): return lax.ppermute(value, axis, [(i, i ^ distance) for i in range(size)])]
    ppermute x48, waiting for transfers between devices: 48.7 us -> 60 us  [swap(): return lax.ppermute(value, axis, [(i, i ^ distance) for i in range(size)])]
    pallas_call x3, Pallas kernels: 10.2 us -> 8.7 us  [head_step(): pl.pallas_call(functools.partial(head_kernel, group, steps, peers), out_s...]
  transfers between devices with their start and end apart: 48 -> 48, of which waited for: 31 -> 36; matrix products, arithmetic and copies ran while one was open for 0% -> 0% of each run, Pallas kernels for 17% -> 17%
where the time goes in v12:
time: 138 us
  waiting for transfers between devices  60 us (43%)
  starting transfers between devices  37.3 us (27%)
  Pallas kernels  34.3 us (25%)
  local copies, waits for them, and re-layouts  5.05 us (4%)
  between operations  1.6 us (1%)
    ppermute x48, waiting for transfers between devices, swap(): return lax.ppermute(value, axis, [(i, i ^ distance) for i in range(size)])  60 us
    ppermute x48, starting transfers between devices, swap(): return lax.ppermute(value, axis, [(i, i ^ distance) for i in range(size)])  37.3 us
    pallas_call x3, Pallas kernels, local_adjoint(): pl.pallas_call(functools.partial(local_adjoint_kernel, touches, group), o...  12.9 us
    pallas_call x3, Pallas kernels, local_forward(): pl.pallas_call(functools.partial(local_forward_kernel, touches, group, st...  10 us
    pallas_call x3, Pallas kernels, head_step(): pl.pallas_call(functools.partial(head_kernel, group, steps, peers), out_s...  8.7 us
    unnamed x26, local copies, waits for them, and re-layouts  5.01 us
  transfers between devices with their start and end apart: 48, of which 36 were waited for; matrix products, arithmetic and copies ran while one was open for 0% of the time, Pallas kernels for 17%

profile of v12, /device:TPU:0, one launch (start us, length us, event | category | flops | bytes accessed | tf_op | source)
XLA Modules:
  0.0 138.2 jit_solution(12103425535363739759)
XLA Ops:
  0.7 0.9 copy-done
  1.6 4.1 %collective-permute-start = (bf16[16,32,128]{2,1,0:T(8,128)(2,1)S(1)}, bf16[16,32,128]{2,1,0:T(8,128)(2,1)S(1)}, u32[]{:S(2)}, u32[]{:S(2)}) collective-permute-start(bf16[16,32,128]{2,1,0:T(8,128)(2,1)S(1)} %fusion.panel_ref.refs_0_), channel_id=1, source_target_pairs={{0,16},{4,20},{8,24},{12,28},{16,0},{20,4},{24,8},{28,12},{1,17},{... | collective-permute-start | bytes 393224 | tf_op jit(solution)/shard_map/ppermute | solution.py:466
  5.7 1.5 %collective-permute-start.1 = (bf16[16,32,128]{2,1,0:T(8,128)(2,1)S(1)}, bf16[16,32,128]{2,1,0:T(8,128)(2,1)S(1)}, u32[]{:S(2)}, u32[]{:S(2)}) collective-permute-start(bf16[16,32,128]{2,1,0:T(8,128)(2,1)S(1)} %fusion.panel_ref.refs_0_), channel_id=1, source_target_pairs={{0,4},{4,0},{8,12},{12,8},{16,20},{20,16},{24,28},{28,24},{1,5},{5... | collective-permute-start | bytes 393224 | tf_op jit(solution)/shard_map/ppermute | solution.py:466
  7.2 3.4 %copy-done.1 = bf16[64,4,128,128]{3,2,1,0:T(8,128)(2,1)S(1)} copy-done((bf16[64,4,128,128]{3,2,1,0:T(8,128)(2,1)S(1)}, bf16[64,4,128,128]{3,2,1,0:T(8,128)(2,1)}, u32[]{:S(2)}) %copy-start.1) | copy-done | bytes 8388632
  10.6 0.7 copy-done.6
  11.3 4.3 %local_adjoint.3 = (f32[32,8192]{1,0:T(8,128)S(1)}, f32[8,128]{1,0:T(8,128)S(1)}) custom-call(s32[4,64]{1,0:T(4,128)S(1)} %bitcast.29, bf16[16,32,128]{2,1,0:T(8,128)(2,1)S(1)} %fusion.panel_ref.refs_0_, bf16[64,4,128,128]{3,2,1,0:T(8,128)(2,1)S(1)} %copy-done.1), custom_call_target="tpu_custom_call" | custom-call | flops 268435456 | bytes 8388608 | tf_op jit(solution)/shard_map/local_adjoint/pallas_call | solution.py:255
  15.6 0.6 relay.3
  16.2 1.6 %collective-permute-start.5 = (bf16[16,32,128]{2,1,0:T(8,128)(2,1)S(1)}, bf16[16,32,128]{2,1,0:T(8,128)(2,1)S(1)}, u32[]{:S(2)}, u32[]{:S(2)}) collective-permute-start(bf16[16,32,128]{2,1,0:T(8,128)(2,1)S(1)} %get-tuple-element.77.refs_0_.refs_4_), channel_id=1, source_target_pairs={{0,8},{4,12},{8,0},{12,4},{16,24},{20,28},{24,16},{28,20},{1,9},{5... | collective-permute-start | bytes 393224 | tf_op jit(solution)/shard_map/ppermute | solution.py:466
  18.8 1.6 %collective-permute-start.3 = (bf16[16,32,128]{2,1,0:T(8,128)(2,1)S(1)}, bf16[16,32,128]{2,1,0:T(8,128)(2,1)S(1)}, u32[]{:S(2)}, u32[]{:S(2)}) collective-permute-start(bf16[16,32,128]{2,1,0:T(8,128)(2,1)S(1)} %collective-permute-done.1.refs_1_), channel_id=1, source_target_pairs={{0,8},{4,12},{8,0},{12,4},{16,24},{20,28},{24,16},{28,20},{1,9},{5... | collective-permute-start | bytes 393224 | tf_op jit(solution)/shard_map/ppermute | solution.py:466
  20.4 2.3 %collective-permute-done.5.refs_6_ = bf16[16,32,128]{2,1,0:T(8,128)(2,1)S(1)} collective-permute-done((bf16[16,32,128]{2,1,0:T(8,128)(2,1)S(1)}, bf16[16,32,128]{2,1,0:T(8,128)(2,1)S(1)}, u32[]{:S(2)}, u32[]{:S(2)}) %collective-permute-start.5) | collective-permute-done | bytes 131104 | tf_op jit(solution)/shard_map/ppermute | solution.py:466
  24.1 1.0 collective-permute-done.2.refs_2_
  25.2 1.3 collective-permute-done.3.refs_3_
  26.5 1.1 collective-permute-done.6.refs_7_
  27.6 2.6 %head_step.3 = (f32[32,8192]{1,0:T(8,128)S(1)}, bf16[32,8192]{1,0:T(8,128)(2,1)S(1)}, f32[8,128]{1,0:T(8,128)S(1)}, f32[16,32,128]{2,1,0:T(8,128)S(1)}, f32[16,3...) custom-call(s32[64]{0:T(128)S(1)} %bitcast.35, ...), custom_call_target="tpu_custom_call" | custom-call | flops 134217728 | bytes 7864320 | tf_op jit(solution)/shard_map/head_step/pallas_call | solution.py:292
  30.9 3.3 %local_forward.3.refs_4_.refs_5_ = f32[16,32,128]{2,1,0:T(8,128)S(1)} custom-call(s32[4,64]{1,0:T(4,128)S(1)} %bitcast.30, bf16[32,8192]{1,0:T(8,128)(2,1)S(1)} %get-tuple-element.90.bar_ref, bf16[64,4,128,128]{3,2,1,0:T(8,128)(2,1)S(1)} %bitcast.25, f32[16,32,128]{2,1,0:T(8,128)S(1)} %bitcast_bitcast_fusion.duals_ref, f32[32,2048]{1,0:T(8,128)S(1)} %copy-done.4), custom_call_target="tpu_custom_call" | custom-call | flops 268435456 | bytes 8388608 | tf_op jit(solution)/shard_map/local_forward/pallas_call | solution.py:390
  34.3 1.1 collective-permute-done.10.refs_1_
  35.5 1.6 %collective-permute-start.11 = (bf16[17,32,128]{2,1,0:T(8,128)(2,1)S(1)}, bf16[17,32,128]{2,1,0:T(8,128)(2,1)S(1)}, u32[]{:S(2)}, u32[]{:S(2)}) collective-permute-start(bf16[17,32,128]{2,1,0:T(8,128)(2,1)S(1)} %get-tuple-element.91.refs_3_), channel_id=1, source_target_pairs={{0,8},{4,12},{8,0},{12,4},{16,24},{20,28},{24,16},{28,20},{1,9},{5... | collective-permute-start | bytes 417800 | tf_op jit(solution)/shard_map/ppermute | solution.py:466
  38.1 1.5 %collective-permute-start.12 = (f32[8,128]{1,0:T(8,128)S(1)}, f32[8,128]{1,0:T(8,128)S(1)}, u32[]{:S(2)}, u32[]{:S(2)}) collective-permute-start(f32[8,128]{1,0:T(8,128)S(1)} %get-tuple-element.92.refs_9_), channel_id=1, source_target_pairs={{0,2},{1,3},{2,0},{3,1},{4,6},{5,7},{6,4},{7,5},{8,10},{9,11},{10,... | collective-permute-start | bytes 12296 | tf_op jit(solution)/shard_map/ppermute | solution.py:466
  39.6 2.9 %collective-permute-done.9.refs_1_ = bf16[16,32,128]{2,1,0:T(8,128)(2,1)S(1)} collective-permute-done((bf16[16,32,128]{2,1,0:T(8,128)(2,1)S(1)}, bf16[16,32,128]{2,1,0:T(8,128)(2,1)S(1)}, u32[]{:S(2)}, u32[]{:S(2)}) %collective-permute-start.9) | collective-permute-done | bytes 131104 | tf_op jit(solution)/shard_map/ppermute | solution.py:466
  42.7 1.0 collective-permute-start.14
  43.8 1.4 %collective-permute-done.8.refs_1_ = bf16[16,32,128]{2,1,0:T(8,128)(2,1)S(1)} collective-permute-done((bf16[16,32,128]{2,1,0:T(8,128)(2,1)S(1)}, bf16[16,32,128]{2,1,0:T(8,128)(2,1)S(1)}, u32[]{:S(2)}, u32[]{:S(2)}) %collective-permute-start.8) | collective-permute-done | bytes 131104 | tf_op jit(solution)/shard_map/ppermute | solution.py:466
  45.3 0.8 collective-permute-start.13
  46.1 2.0 %collective-permute-done.14.refs_2_ = bf16[16,32,128]{2,1,0:T(8,128)(2,1)S(1)} collective-permute-done((bf16[16,32,128]{2,1,0:T(8,128)(2,1)S(1)}, bf16[16,32,128]{2,1,0:T(8,128)(2,1)S(1)}, u32[]{:S(2)}, u32[]{:S(2)}) %collective-permute-start.14) | collective-permute-done | bytes 131104 | tf_op jit(solution)/shard_map/ppermute | solution.py:466
  48.0 3.0 %collective-permute-done.13.refs_1_ = bf16[16,32,128]{2,1,0:T(8,128)(2,1)S(1)} collective-permute-done((bf16[16,32,128]{2,1,0:T(8,128)(2,1)S(1)}, bf16[16,32,128]{2,1,0:T(8,128)(2,1)S(1)}, u32[]{:S(2)}, u32[]{:S(2)}) %collective-permute-start.13) | collective-permute-done | bytes 131104 | tf_op jit(solution)/shard_map/ppermute | solution.py:466
  51.1 1.7 %collective-permute-done.15.refs_3_ = bf16[17,32,128]{2,1,0:T(8,128)(2,1)S(1)} collective-permute-done((bf16[17,32,128]{2,1,0:T(8,128)(2,1)S(1)}, bf16[17,32,128]{2,1,0:T(8,128)(2,1)S(1)}, u32[]{:S(2)}, u32[]{:S(2)}) %collective-permute-start.15) | collective-permute-done | bytes 139296 | tf_op jit(solution)/shard_map/ppermute | solution.py:466
  53.1 0.9 collective-permute-start.16
  54.0 4.3 %local_adjoint.4 = (f32[32,8192]{1,0:T(8,128)S(1)}, f32[8,128]{1,0:T(8,128)S(1)}) custom-call(s32[4,64]{1,0:T(4,128)S(1)} %bitcast.31, bf16[16,32,128]{2,1,0:T(8,128)(2,1)S(1)} %get-tuple-element.96.panel_ref.refs_0_, bf16[64,4,128,128]{3,2,1,0:T(8,128)(2,1)S(1)} %bitcast.25), custom_call_target="tpu_custom_call" | custom-call | flops 268435456 | bytes 8388608 | tf_op jit(solution)/shard_map/local_adjoint/pallas_call | solution.py:255
  58.3 1.5 %collective-permute-done.19.arrived_ref = bf16[16,32,128]{2,1,0:T(8,128)(2,1)S(1)} collective-permute-done((bf16[16,32,128]{2,1,0:T(8,128)(2,1)S(1)}, bf16[16,32,128]{2,1,0:T(8,128)(2,1)S(1)}, u32[]{:S(2)}, u32[]{:S(2)}) %collective-permute-start.19) | collective-permute-done | bytes 131104 | tf_op jit(solution)/shard_map/ppermute | solution.py:466
  59.9 2.0 %collective-permute-start.17 = (bf16[16,32,128]{2,1,0:T(8,128)(2,1)S(1)}, bf16[16,32,128]{2,1,0:T(8,128)(2,1)S(1)}, u32[]{:S(2)}, u32[]{:S(2)}) collective-permute-start(bf16[16,32,128]{2,1,0:T(8,128)(2,1)S(1)} %get-tuple-element.96.panel_ref.refs_0_), channel_id=1, source_target_pairs={{0,8},{4,12},{8,0},{12,4},{16,24},{20,28},{24,16},{28,20},{1,9},{5... | collective-permute-start | bytes 393224 | tf_op jit(solution)/shard_map/ppermute | solution.py:466
  62.4 2.5 %collective-permute-done.21.refs_6_ = bf16[16,32,128]{2,1,0:T(8,128)(2,1)S(1)} collective-permute-done((bf16[16,32,128]{2,1,0:T(8,128)(2,1)S(1)}, bf16[16,32,128]{2,1,0:T(8,128)(2,1)S(1)}, u32[]{:S(2)}, u32[]{:S(2)}) %collective-permute-start.21) | collective-permute-done | bytes 131104 | tf_op jit(solution)/shard_map/ppermute | solution.py:466
  64.9 1.4 collective-permute-done.17.refs_2_
  66.3 1.4 %collective-permute-done.18.refs_3_ = bf16[16,32,128]{2,1,0:T(8,128)(2,1)S(1)} collective-permute-done((bf16[16,32,128]{2,1,0:T(8,128)(2,1)S(1)}, bf16[16,32,128]{2,1,0:T(8,128)(2,1)S(1)}, u32[]{:S(2)}, u32[]{:S(2)}) %collective-permute-start.18) | collective-permute-done | bytes 131104 | tf_op jit(solution)/shard_map/ppermute | solution.py:466
  67.7 2.2 %collective-permute-done.22.refs_7_ = bf16[16,32,128]{2,1,0:T(8,128)(2,1)S(1)} collective-permute-done((bf16[16,32,128]{2,1,0:T(8,128)(2,1)S(1)}, bf16[16,32,128]{2,1,0:T(8,128)(2,1)S(1)}, u32[]{:S(2)}, u32[]{:S(2)}) %collective-permute-start.22) | collective-permute-done | bytes 131104 | tf_op jit(solution)/shard_map/ppermute | solution.py:466
  69.8 2.6 %head_step.4 = (f32[32,8192]{1,0:T(8,128)S(1)}, bf16[32,8192]{1,0:T(8,128)(2,1)S(1)}, f32[8,128]{1,0:T(8,128)S(1)}, f32[16,32,128]{2,1,0:T(8,128)S(1)}, f32[16,3...) custom-call(s32[64]{0:T(128)S(1)} %bitcast.36, ...), custom_call_target="tpu_custom_call" | custom-call | flops 134217728 | bytes 7864320 | tf_op jit(solution)/shard_map/head_step/pallas_call | solution.py:292
  72.6 3.3 %local_forward.4.refs_4_.refs_5_ = f32[16,32,128]{2,1,0:T(8,128)S(1)} custom-call(s32[4,64]{1,0:T(4,128)S(1)} %bitcast.32, bf16[32,8192]{1,0:T(8,128)(2,1)S(1)} %get-tuple-element.112.bar_ref, bf16[64,4,128,128]{3,2,1,0:T(8,128)(2,1)S(1)} %bitcast.25, f32[16,32,128]{2,1,0:T(8,128)S(1)} %get-tuple-element.113.duals_ref, f32[32,2048]{1,0:T(8,128)S(1)} %copy-done.4), custom_call_target="tpu_custom_call" | custom-call | flops 268435456 | bytes 8388608 | tf_op jit(solution)/shard_map/local_forward/pallas_call | solution.py:390
  75.9 2.4 %collective-permute-done.26.refs_1_ = bf16[17,32,128]{2,1,0:T(8,128)(2,1)S(1)} collective-permute-done((bf16[17,32,128]{2,1,0:T(8,128)(2,1)S(1)}, bf16[17,32,128]{2,1,0:T(8,128)(2,1)S(1)}, u32[]{:S(2)}, u32[]{:S(2)}) %collective-permute-start.26) | collective-permute-done | bytes 139296 | tf_op jit(solution)/shard_map/ppermute | solution.py:466
  78.9 1.7 %collective-permute-start.24 = (bf16[16,32,128]{2,1,0:T(8,128)(2,1)S(1)}, bf16[16,32,128]{2,1,0:T(8,128)(2,1)S(1)}, u32[]{:S(2)}, u32[]{:S(2)}) collective-permute-start(bf16[16,32,128]{2,1,0:T(8,128)(2,1)S(1)} %get-tuple-element.106), channel_id=1, source_target_pairs={{0,8},{4,12},{8,0},{12,4},{16,24},{20,28},{24,16},{28,20},{1,9},{5... | collective-permute-start | bytes 393224 | tf_op jit(solution)/shard_map/ppermute | solution.py:466
  80.5 1.5 %collective-permute-start.28 = (f32[8,128]{1,0:T(8,128)S(1)}, f32[8,128]{1,0:T(8,128)S(1)}, u32[]{:S(2)}, u32[]{:S(2)}) collective-permute-start(f32[8,128]{1,0:T(8,128)S(1)} %get-tuple-element.115.refs_9_), channel_id=1, source_target_pairs={{0,2},{1,3},{2,0},{3,1},{4,6},{5,7},{6,4},{7,5},{8,10},{9,11},{10,... | collective-permute-start | bytes 12296 | tf_op jit(solution)/shard_map/ppermute | solution.py:466
  82.1 1.6 %collective-permute-done.25.refs_1_ = bf16[16,32,128]{2,1,0:T(8,128)(2,1)S(1)} collective-permute-done((bf16[16,32,128]{2,1,0:T(8,128)(2,1)S(1)}, bf16[16,32,128]{2,1,0:T(8,128)(2,1)S(1)}, u32[]{:S(2)}, u32[]{:S(2)}) %collective-permute-start.25) | collective-permute-done | bytes 131104 | tf_op jit(solution)/shard_map/ppermute | solution.py:466
  84.1 1.9 %collective-permute-done.27.refs_2_ = bf16[17,32,128]{2,1,0:T(8,128)(2,1)S(1)} collective-permute-done((bf16[17,32,128]{2,1,0:T(8,128)(2,1)S(1)}, bf16[17,32,128]{2,1,0:T(8,128)(2,1)S(1)}, u32[]{:S(2)}, u32[]{:S(2)}) %collective-permute-start.27) | collective-permute-done | bytes 139296 | tf_op jit(solution)/shard_map/ppermute | solution.py:466
  86.7 1.2 collective-permute-done.24.refs_1_
  87.9 0.7 collective-permute-start.29
  88.6 3.3 %collective-permute-done.30.refs_2_ = bf16[16,32,128]{2,1,0:T(8,128)(2,1)S(1)} collective-permute-done((bf16[16,32,128]{2,1,0:T(8,128)(2,1)S(1)}, bf16[16,32,128]{2,1,0:T(8,128)(2,1)S(1)}, u32[]{:S(2)}, u32[]{:S(2)}) %collective-permute-start.30) | collective-permute-done | bytes 131104 | tf_op jit(solution)/shard_map/ppermute | solution.py:466
  92.0 1.8 %collective-permute-done.29.refs_1_ = bf16[16,32,128]{2,1,0:T(8,128)(2,1)S(1)} collective-permute-done((bf16[16,32,128]{2,1,0:T(8,128)(2,1)S(1)}, bf16[16,32,128]{2,1,0:T(8,128)(2,1)S(1)}, u32[]{:S(2)}, u32[]{:S(2)}) %collective-permute-start.29) | collective-permute-done | bytes 131104 | tf_op jit(solution)/shard_map/ppermute | solution.py:466
  93.7 2.5 %collective-permute-done.31.refs_3_ = bf16[17,32,128]{2,1,0:T(8,128)(2,1)S(1)} collective-permute-done((bf16[17,32,128]{2,1,0:T(8,128)(2,1)S(1)}, bf16[17,32,128]{2,1,0:T(8,128)(2,1)S(1)}, u32[]{:S(2)}, u32[]{:S(2)}) %collective-permute-start.31) | collective-permute-done | bytes 139296 | tf_op jit(solution)/shard_map/ppermute | solution.py:466
  96.6 4.3 %local_adjoint.5 = (f32[32,8192]{1,0:T(8,128)S(1)}, f32[8,128]{1,0:T(8,128)S(1)}) custom-call(s32[4,64]{1,0:T(4,128)S(1)} %bitcast.33, bf16[16,32,128]{2,1,0:T(8,128)(2,1)S(1)} %get-tuple-element.119.panel_ref.refs_0_, bf16[64,4,128,128]{3,2,1,0:T(8,128)(2,1)S(1)} %bitcast.25), custom_call_target="tpu_custom_call" | custom-call | flops 268435456 | bytes 8388608 | tf_op jit(solution)/shard_map/local_adjoint/pallas_call | solution.py:255
  100.9 1.8 %collective-permute-done.35.arrived_ref = bf16[16,32,128]{2,1,0:T(8,128)(2,1)S(1)} collective-permute-done((bf16[16,32,128]{2,1,0:T(8,128)(2,1)S(1)}, bf16[16,32,128]{2,1,0:T(8,128)(2,1)S(1)}, u32[]{:S(2)}, u32[]{:S(2)}) %collective-permute-start.35) | collective-permute-done | bytes 131104 | tf_op jit(solution)/shard_map/ppermute | solution.py:466
  103.0 1.8 %collective-permute-start.33 = (bf16[16,32,128]{2,1,0:T(8,128)(2,1)S(1)}, bf16[16,32,128]{2,1,0:T(8,128)(2,1)S(1)}, u32[]{:S(2)}, u32[]{:S(2)}) collective-permute-start(bf16[16,32,128]{2,1,0:T(8,128)(2,1)S(1)} %get-tuple-element.119.panel_ref.refs_0_), channel_id=1, source_target_pairs={{0,8},{4,12},{8,0},{12,4},{16,24},{20,28},{24,16},{28,20},{1,9},{5... | collective-permute-start | bytes 393224 | tf_op jit(solution)/shard_map/ppermute | solution.py:466
  105.4 2.3 %collective-permute-done.37.refs_6_ = bf16[16,32,128]{2,1,0:T(8,128)(2,1)S(1)} collective-permute-done((bf16[16,32,128]{2,1,0:T(8,128)(2,1)S(1)}, bf16[16,32,128]{2,1,0:T(8,128)(2,1)S(1)}, u32[]{:S(2)}, u32[]{:S(2)}) %collective-permute-start.37) | collective-permute-done | bytes 131104 | tf_op jit(solution)/shard_map/ppermute | solution.py:466
  108.3 0.9 collective-permute-done.33.refs_2_
  109.4 1.1 collective-permute-done.34.refs_3_
  110.5 2.2 %collective-permute-done.38.refs_7_ = bf16[16,32,128]{2,1,0:T(8,128)(2,1)S(1)} collective-permute-done((bf16[16,32,128]{2,1,0:T(8,128)(2,1)S(1)}, bf16[16,32,128]{2,1,0:T(8,128)(2,1)S(1)}, u32[]{:S(2)}, u32[]{:S(2)}) %collective-permute-start.38) | collective-permute-done | bytes 131104 | tf_op jit(solution)/shard_map/ppermute | solution.py:466
  112.7 3.4 %head_step.5 = (f32[32,8192]{1,0:T(8,128)}, bf16[32,8192]{1,0:T(8,128)(2,1)S(1)}, f32[8,128]{1,0:T(8,128)S(1)}, f32[16,32,128]{2,1,0:T(8,128)S(1)}, f32[16,32,12...) custom-call(s32[64]{0:T(128)S(1)} %bitcast.37, ...), custom_call_target="tpu_custom_call" | custom-call | flops 134217728 | bytes 7864320 | tf_op jit(solution)/shard_map/head_step/pallas_call | solution.py:292
  116.7 3.3 %local_forward.5.refs_4_.refs_5_ = f32[16,32,128]{2,1,0:T(8,128)S(1)} custom-call(s32[4,64]{1,0:T(4,128)S(1)} %bitcast.34, bf16[32,8192]{1,0:T(8,128)(2,1)S(1)} %get-tuple-element.136.bar_ref, bf16[64,4,128,128]{3,2,1,0:T(8,128)(2,1)S(1)} %bitcast.25, f32[16,32,128]{2,1,0:T(8,128)S(1)} %get-tuple-element.137.duals_ref, f32[32,2048]{1,0:T(8,128)S(1)} %copy-done.4), custom_call_target="tpu_custom_call" | custom-call | flops 268435456 | bytes 8388608 | tf_op jit(solution)/shard_map/local_forward/pallas_call | solution.py:390
  120.0 1.9 %collective-permute-done.42.refs_1_ = bf16[17,32,128]{2,1,0:T(8,128)(2,1)S(1)} collective-permute-done((bf16[17,32,128]{2,1,0:T(8,128)(2,1)S(1)}, bf16[17,32,128]{2,1,0:T(8,128)(2,1)S(1)}, u32[]{:S(2)}, u32[]{:S(2)}) %collective-permute-start.42) | collective-permute-done | bytes 139296 | tf_op jit(solution)/shard_map/ppermute | solution.py:466
  122.5 1.8 %collective-permute-start.40 = (bf16[16,32,128]{2,1,0:T(8,128)(2,1)S(1)}, bf16[16,32,128]{2,1,0:T(8,128)(2,1)S(1)}, u32[]{:S(2)}, u32[]{:S(2)}) collective-permute-start(bf16[16,32,128]{2,1,0:T(8,128)(2,1)S(1)} %get-tuple-element.130), channel_id=1, source_target_pairs={{0,8},{4,12},{8,0},{12,4},{16,24},{20,28},{24,16},{28,20},{1,9},{5... | collective-permute-start | bytes 393224 | tf_op jit(solution)/shard_map/ppermute | solution.py:466
  124.3 1.5 %collective-permute-start.44 = (f32[8,128]{1,0:T(8,128)S(1)}, f32[8,128]{1,0:T(8,128)S(1)}, u32[]{:S(2)}, u32[]{:S(2)}) collective-permute-start(f32[8,128]{1,0:T(8,128)S(1)} %get-tuple-element.139.refs_9_), channel_id=1, source_target_pairs={{0,2},{1,3},{2,0},{3,1},{4,6},{5,7},{6,4},{7,5},{8,10},{9,11},{10,... | collective-permute-start | bytes 12296 | tf_op jit(solution)/shard_map/ppermute | solution.py:466
  125.8 1.3 collective-permute-done.41.refs_1_
  127.2 0.8 collective-permute-done.44.refs_4_.refs_10_
  127.9 1.5 %collective-permute-done.43.refs_2_ = bf16[17,32,128]{2,1,0:T(8,128)(2,1)S(1)} collective-permute-done((bf16[17,32,128]{2,1,0:T(8,128)(2,1)S(1)}, bf16[17,32,128]{2,1,0:T(8,128)(2,1)S(1)}, u32[]{:S(2)}, u32[]{:S(2)}) %collective-permute-start.43) | collective-permute-done | bytes 139296 | tf_op jit(solution)/shard_map/ppermute | solution.py:466
  129.5 1.5 %collective-permute-start.47 = (bf16[17,32,128]{2,1,0:T(8,128)(2,1)S(1)}, bf16[17,32,128]{2,1,0:T(8,128)(2,1)S(1)}, u32[]{:S(2)}, u32[]{:S(2)}) collective-permute-start(bf16[17,32,128]{2,1,0:T(8,128)(2,1)S(1)} %fold.16.refs_2_.refs_4_), channel_id=1, source_target_pairs={{0,16},{4,20},{8,24},{12,28},{16,0},{20,4},{24,8},{28,12},{1,17},{... | collective-permute-start | bytes 417800 | tf_op jit(solution)/shard_map/ppermute | solution.py:466
  131.5 2.3 %collective-permute-start.45 = (bf16[16,32,128]{2,1,0:T(8,128)(2,1)S(1)}, bf16[16,32,128]{2,1,0:T(8,128)(2,1)S(1)}, u32[]{:S(2)}, u32[]{:S(2)}) collective-permute-start(bf16[16,32,128]{2,1,0:T(8,128)(2,1)S(1)} %fold.17), channel_id=1, source_target_pairs={{0,4},{4,0},{8,12},{12,8},{16,20},{20,16},{24,28},{28,24},{1,5},{5... | collective-permute-start | bytes 393224 | tf_op jit(solution)/shard_map/ppermute | solution.py:466
  133.8 3.6 %collective-permute-done.46.refs_2_ = bf16[16,32,128]{2,1,0:T(8,128)(2,1)S(1)} collective-permute-done((bf16[16,32,128]{2,1,0:T(8,128)(2,1)S(1)}, bf16[16,32,128]{2,1,0:T(8,128)(2,1)S(1)}, u32[]{:S(2)}, u32[]{:S(2)}) %collective-permute-start.46) | collective-permute-done | bytes 131104 | tf_op jit(solution)/shard_map/ppermute | solution.py:466
  137.4 0.8 settle.5
  (86 shorter events, 10.1 us)
Async XLA Ops:
  0.6 1.0 copy-start
  0.6 23.2 %copy-start.10 = (s32[64]{0:T(128)S(1)}, s32[64]{0:T(128)}, u32[]{:S(2)}) copy-start(s32[64]{0:T(128)} %param.21) | copy-start | bytes 772
  0.7 23.2 %copy-start.8 = (f32[32]{0:T(128)S(1)}, f32[32]{0:T(128)}, u32[]{:S(2)}) copy-start(f32[32]{0:T(128)} %param.15) | copy-start | bytes 388
  0.7 23.2 %copy-start.9 = (f32[32]{0:T(128)S(1)}, f32[32]{0:T(128)}, u32[]{:S(2)}) copy-start(f32[32]{0:T(128)} %param.14) | copy-start | bytes 388
  0.7 26.9 %copy-start.5 = (f32[8192]{0:T(1024)S(1)}, f32[8192]{0:T(1024)}, u32[]{:S(2)}) copy-start(f32[8192]{0:T(1024)} %param.17) | copy-start | bytes 98308
  1.6 14.0 %collective-permute-start = (bf16[16,32,128]{2,1,0:T(8,128)(2,1)S(1)}, bf16[16,32,128]{2,1,0:T(8,128)(2,1)S(1)}, u32[]{:S(2)}, u32[]{:S(2)}) collective-permute-start(bf16[16,32,128]{2,1,0:T(8,128)(2,1)S(1)} %fusion.panel_ref.refs_0_), channel_id=1, source_target_pairs={{0,16},{4,20},{8,24},{12,28},{16,0},{20,4},{24,8},{28,12},{1,17},{... | collective-permute-start | bytes 393224 | tf_op jit(solution)/shard_map/ppermute | solution.py:466
  5.7 13.0 %collective-permute-start.1 = (bf16[16,32,128]{2,1,0:T(8,128)(2,1)S(1)}, bf16[16,32,128]{2,1,0:T(8,128)(2,1)S(1)}, u32[]{:S(2)}, u32[]{:S(2)}) collective-permute-start(bf16[16,32,128]{2,1,0:T(8,128)(2,1)S(1)} %fusion.panel_ref.refs_0_), channel_id=1, source_target_pairs={{0,4},{4,0},{8,12},{12,8},{16,20},{20,16},{24,28},{28,24},{1,5},{5... | collective-permute-start | bytes 393224 | tf_op jit(solution)/shard_map/ppermute | solution.py:466
  7.2 3.4 %copy-start.1 = (bf16[64,4,128,128]{3,2,1,0:T(8,128)(2,1)S(1)}, bf16[64,4,128,128]{3,2,1,0:T(8,128)(2,1)}, u32[]{:S(2)}) copy-start(bf16[64,4,128,128]{3,2,1,0:T(8,128)(2,1)} %blocks_ref.11) | copy-start | bytes 25165828
  10.6 0.7 copy-start.6
  11.3 12.6 %copy-start.2 = (bf16[64,128,128]{2,1,0:T(8,128)(2,1)S(1)}, bf16[64,128,128]{2,1,0:T(8,128)(2,1)}, u32[]{:S(2)}) copy-start(bf16[64,128,128]{2,1,0:T(8,128)(2,1)} %refs_8_.5) | copy-start | bytes 6291460
  11.3 12.6 %copy-start.3 = (f32[32,8192]{1,0:T(8,128)S(1)}, f32[32,8192]{1,0:T(8,128)}, u32[]{:S(2)}) copy-start(f32[32,8192]{1,0:T(8,128)} %refs_10_.1) | copy-start | bytes 3145732
  11.3 19.6 %slice-start = ((s8[8388608]{0:T(1024)(128)(4,1)}), s8[4194304]{0:T(1024)(128)(4,1)S(1)}, s32[]{:S(2)}) async-start(s8[8388608]{0:T(1024)(128)(4,1)} %bitcast.24), calls=%async_computation | async-start | bytes 8388608
  11.3 19.6 %copy-start.4 = (f32[32,2048]{1,0:T(8,128)S(1)}, f32[32,2048]{1,0:T(8,128)}, u32[]{:S(2)}) copy-start(f32[32,2048]{1,0:T(8,128)} %demand_ref.5) | copy-start | bytes 786436
  16.2 6.4 %collective-permute-start.5 = (bf16[16,32,128]{2,1,0:T(8,128)(2,1)S(1)}, bf16[16,32,128]{2,1,0:T(8,128)(2,1)S(1)}, u32[]{:S(2)}, u32[]{:S(2)}) collective-permute-start(bf16[16,32,128]{2,1,0:T(8,128)(2,1)S(1)} %get-tuple-element.77.refs_0_.refs_4_), channel_id=1, source_target_pairs={{0,8},{4,12},{8,0},{12,4},{16,24},{20,28},{24,16},{28,20},{1,9},{5... | collective-permute-start | bytes 393224 | tf_op jit(solution)/shard_map/ppermute | solution.py:466
  17.8 7.3 %collective-permute-start.2 = (bf16[16,32,128]{2,1,0:T(8,128)(2,1)S(1)}, bf16[16,32,128]{2,1,0:T(8,128)(2,1)S(1)}, u32[]{:S(2)}, u32[]{:S(2)}) collective-permute-start(bf16[16,32,128]{2,1,0:T(8,128)(2,1)S(1)} %fusion.panel_ref.refs_0_), channel_id=1, source_target_pairs={{0,8},{4,12},{8,0},{12,4},{16,24},{20,28},{24,16},{28,20},{1,9},{5... | collective-permute-start | bytes 393224 | tf_op jit(solution)/shard_map/ppermute | solution.py:466
  18.2 8.3 %collective-permute-start.4 = (bf16[16,32,128]{2,1,0:T(8,128)(2,1)S(1)}, bf16[16,32,128]{2,1,0:T(8,128)(2,1)S(1)}, u32[]{:S(2)}, u32[]{:S(2)}) collective-permute-start(bf16[16,32,128]{2,1,0:T(8,128)(2,1)S(1)} %get-tuple-element.77.refs_0_.refs_4_), channel_id=1, source_target_pairs={{0,4},{4,0},{8,12},{12,8},{16,20},{20,16},{24,28},{28,24},{1,5},{5... | collective-permute-start | bytes 393224 | tf_op jit(solution)/shard_map/ppermute | solution.py:466
  18.8 7.7 %collective-permute-start.3 = (bf16[16,32,128]{2,1,0:T(8,128)(2,1)S(1)}, bf16[16,32,128]{2,1,0:T(8,128)(2,1)S(1)}, u32[]{:S(2)}, u32[]{:S(2)}) collective-permute-start(bf16[16,32,128]{2,1,0:T(8,128)(2,1)S(1)} %collective-permute-done.1.refs_1_), channel_id=1, source_target_pairs={{0,8},{4,12},{8,0},{12,4},{16,24},{20,28},{24,16},{28,20},{1,9},{5... | collective-permute-start | bytes 393224 | tf_op jit(solution)/shard_map/ppermute | solution.py:466
  22.6 5.0 %collective-permute-start.6 = (bf16[16,32,128]{2,1,0:T(8,128)(2,1)S(1)}, bf16[16,32,128]{2,1,0:T(8,128)(2,1)S(1)}, u32[]{:S(2)}, u32[]{:S(2)}) collective-permute-start(bf16[16,32,128]{2,1,0:T(8,128)(2,1)S(1)} %collective-permute-done.5.refs_6_), channel_id=1, source_target_pairs={{0,4},{4,0},{8,12},{12,8},{16,20},{20,16},{24,28},{28,24},{1,5},{5... | collective-permute-start | bytes 393224 | tf_op jit(solution)/shard_map/ppermute | solution.py:466
  23.9 7.0 %slice-start.1 = ((s8[8388608]{0:T(1024)(128)(4,1)}), s8[4194304]{0:T(1024)(128)(4,1)S(1)}, s32[]{:S(2)}) async-start(s8[8388608]{0:T(1024)(128)(4,1)} %bitcast.24), calls=%async_computation.1 | async-start | bytes 8388608
  24.0 1.2 collective-permute-start.7
  27.6 26.4 %copy-start.7 = (s32[64,4]{0,1:T(4,128)S(1)}, s32[64,4]{0,1:T(4,128)}, u32[]{:S(2)}) copy-start(s32[64,4]{0,1:T(4,128)} %param.20) | copy-start | bytes 3076
  30.3 5.1 %collective-permute-start.10 = (bf16[17,32,128]{2,1,0:T(8,128)(2,1)S(1)}, bf16[17,32,128]{2,1,0:T(8,128)(2,1)S(1)}, u32[]{:S(2)}, u32[]{:S(2)}) collective-permute-start(bf16[17,32,128]{2,1,0:T(8,128)(2,1)S(1)} %get-tuple-element.88.refs_2_), channel_id=1, source_target_pairs={{0,4},{4,0},{8,12},{12,8},{16,20},{20,16},{24,28},{28,24},{1,5},{5... | collective-permute-start | bytes 417800 | tf_op jit(solution)/shard_map/ppermute | solution.py:466
  35.5 7.1 %collective-permute-start.11 = (bf16[17,32,128]{2,1,0:T(8,128)(2,1)S(1)}, bf16[17,32,128]{2,1,0:T(8,128)(2,1)S(1)}, u32[]{:S(2)}, u32[]{:S(2)}) collective-permute-start(bf16[17,32,128]{2,1,0:T(8,128)(2,1)S(1)} %get-tuple-element.91.refs_3_), channel_id=1, source_target_pairs={{0,8},{4,12},{8,0},{12,4},{16,24},{20,28},{24,16},{28,20},{1,9},{5... | collective-permute-start | bytes 417800 | tf_op jit(solution)/shard_map/ppermute | solution.py:466
  37.1 5.4 %collective-permute-start.9 = (bf16[16,32,128]{2,1,0:T(8,128)(2,1)S(1)}, bf16[16,32,128]{2,1,0:T(8,128)(2,1)S(1)}, u32[]{:S(2)}, u32[]{:S(2)}) collective-permute-start(bf16[16,32,128]{2,1,0:T(8,128)(2,1)S(1)} %get-tuple-element.86), channel_id=1, source_target_pairs={{0,4},{4,0},{8,12},{12,8},{16,20},{20,16},{24,28},{28,24},{1,5},{5... | collective-permute-start | bytes 393224 | tf_op jit(solution)/shard_map/ppermute | solution.py:466
  37.6 7.6 %collective-permute-start.8 = (bf16[16,32,128]{2,1,0:T(8,128)(2,1)S(1)}, bf16[16,32,128]{2,1,0:T(8,128)(2,1)S(1)}, u32[]{:S(2)}, u32[]{:S(2)}) collective-permute-start(bf16[16,32,128]{2,1,0:T(8,128)(2,1)S(1)} %get-tuple-element.84), channel_id=1, source_target_pairs={{0,8},{4,12},{8,0},{12,4},{16,24},{20,28},{24,16},{28,20},{1,9},{5... | collective-permute-start | bytes 393224 | tf_op jit(solution)/shard_map/ppermute | solution.py:466
  38.1 4.5 %collective-permute-start.12 = (f32[8,128]{1,0:T(8,128)S(1)}, f32[8,128]{1,0:T(8,128)S(1)}, u32[]{:S(2)}, u32[]{:S(2)}) collective-permute-start(f32[8,128]{1,0:T(8,128)S(1)} %get-tuple-element.92.refs_9_), channel_id=1, source_target_pairs={{0,2},{1,3},{2,0},{3,1},{4,6},{5,7},{6,4},{7,5},{8,10},{9,11},{10,... | collective-permute-start | bytes 12296 | tf_op jit(solution)/shard_map/ppermute | solution.py:466
  42.7 10.1 %collective-permute-start.15 = (bf16[17,32,128]{2,1,0:T(8,128)(2,1)S(1)}, bf16[17,32,128]{2,1,0:T(8,128)(2,1)S(1)}, u32[]{:S(2)}, u32[]{:S(2)}) collective-permute-start(bf16[17,32,128]{2,1,0:T(8,128)(2,1)S(1)} %fold.10.refs_2_.refs_4_), channel_id=1, source_target_pairs={{0,16},{4,20},{8,24},{12,28},{16,0},{20,4},{24,8},{28,12},{1,17},{... | collective-permute-start | bytes 417800 | tf_op jit(solution)/shard_map/ppermute | solution.py:466
  42.7 5.3 %collective-permute-start.14 = (bf16[16,32,128]{2,1,0:T(8,128)(2,1)S(1)}, bf16[16,32,128]{2,1,0:T(8,128)(2,1)S(1)}, u32[]{:S(2)}, u32[]{:S(2)}) collective-permute-start(bf16[16,32,128]{2,1,0:T(8,128)(2,1)S(1)} %get-tuple-element.93), channel_id=1, source_target_pairs={{0,8},{4,12},{8,0},{12,4},{16,24},{20,28},{24,16},{28,20},{1,9},{5... | collective-permute-start | bytes 393224 | tf_op jit(solution)/shard_map/ppermute | solution.py:466
  45.3 5.8 %collective-permute-start.13 = (bf16[16,32,128]{2,1,0:T(8,128)(2,1)S(1)}, bf16[16,32,128]{2,1,0:T(8,128)(2,1)S(1)}, u32[]{:S(2)}, u32[]{:S(2)}) collective-permute-start(bf16[16,32,128]{2,1,0:T(8,128)(2,1)S(1)} %fold.11), channel_id=1, source_target_pairs={{0,4},{4,0},{8,12},{12,8},{16,20},{20,16},{24,28},{28,24},{1,5},{5... | collective-permute-start | bytes 393224 | tf_op jit(solution)/shard_map/ppermute | solution.py:466
  53.0 6.8 %collective-permute-start.19 = (bf16[16,32,128]{2,1,0:T(8,128)(2,1)S(1)}, bf16[16,32,128]{2,1,0:T(8,128)(2,1)S(1)}, u32[]{:S(2)}, u32[]{:S(2)}) collective-permute-start(bf16[16,32,128]{2,1,0:T(8,128)(2,1)S(1)} %get-tuple-element.96.panel_ref.refs_0_), channel_id=1, source_target_pairs={{0,16},{4,20},{8,24},{12,28},{16,0},{20,4},{24,8},{28,12},{1,17},{... | collective-permute-start | bytes 393224 | tf_op jit(solution)/shard_map/ppermute | solution.py:466
  53.1 8.9 %collective-permute-start.16 = (bf16[16,32,128]{2,1,0:T(8,128)(2,1)S(1)}, bf16[16,32,128]{2,1,0:T(8,128)(2,1)S(1)}, u32[]{:S(2)}, u32[]{:S(2)}) collective-permute-start(bf16[16,32,128]{2,1,0:T(8,128)(2,1)S(1)} %get-tuple-element.96.panel_ref.refs_0_), channel_id=1, source_target_pairs={{0,4},{4,0},{8,12},{12,8},{16,20},{20,16},{24,28},{28,24},{1,5},{5... | collective-permute-start | bytes 393224 | tf_op jit(solution)/shard_map/ppermute | solution.py:466
  59.8 5.0 %collective-permute-start.21 = (bf16[16,32,128]{2,1,0:T(8,128)(2,1)S(1)}, bf16[16,32,128]{2,1,0:T(8,128)(2,1)S(1)}, u32[]{:S(2)}, u32[]{:S(2)}) collective-permute-start(bf16[16,32,128]{2,1,0:T(8,128)(2,1)S(1)} %get-tuple-element.99.refs_4_), channel_id=1, source_target_pairs={{0,8},{4,12},{8,0},{12,4},{16,24},{20,28},{24,16},{28,20},{1,9},{5... | collective-permute-start | bytes 393224 | tf_op jit(solution)/shard_map/ppermute | solution.py:466
  59.9 6.4 %collective-permute-start.17 = (bf16[16,32,128]{2,1,0:T(8,128)(2,1)S(1)}, bf16[16,32,128]{2,1,0:T(8,128)(2,1)S(1)}, u32[]{:S(2)}, u32[]{:S(2)}) collective-permute-start(bf16[16,32,128]{2,1,0:T(8,128)(2,1)S(1)} %get-tuple-element.96.panel_ref.refs_0_), channel_id=1, source_target_pairs={{0,8},{4,12},{8,0},{12,4},{16,24},{20,28},{24,16},{28,20},{1,9},{5... | collective-permute-start | bytes 393224 | tf_op jit(solution)/shard_map/ppermute | solution.py:466
  61.9 5.8 %collective-permute-start.20 = (bf16[16,32,128]{2,1,0:T(8,128)(2,1)S(1)}, bf16[16,32,128]{2,1,0:T(8,128)(2,1)S(1)}, u32[]{:S(2)}, u32[]{:S(2)}) collective-permute-start(bf16[16,32,128]{2,1,0:T(8,128)(2,1)S(1)} %get-tuple-element.99.refs_4_), channel_id=1, source_target_pairs={{0,4},{4,0},{8,12},{12,8},{16,20},{20,16},{24,28},{28,24},{1,5},{5... | collective-permute-start | bytes 393224 | tf_op jit(solution)/shard_map/ppermute | solution.py:466
  62.0 5.7 %collective-permute-start.18 = (bf16[16,32,128]{2,1,0:T(8,128)(2,1)S(1)}, bf16[16,32,128]{2,1,0:T(8,128)(2,1)S(1)}, u32[]{:S(2)}, u32[]{:S(2)}) collective-permute-start(bf16[16,32,128]{2,1,0:T(8,128)(2,1)S(1)} %collective-permute-done.16.refs_1_), channel_id=1, source_target_pairs={{0,8},{4,12},{8,0},{12,4},{16,24},{20,28},{24,16},{28,20},{1,9},{5... | collective-permute-start | bytes 393224 | tf_op jit(solution)/shard_map/ppermute | solution.py:466
  64.9 5.0 %collective-permute-start.22 = (bf16[16,32,128]{2,1,0:T(8,128)(2,1)S(1)}, bf16[16,32,128]{2,1,0:T(8,128)(2,1)S(1)}, u32[]{:S(2)}, u32[]{:S(2)}) collective-permute-start(bf16[16,32,128]{2,1,0:T(8,128)(2,1)S(1)} %collective-permute-done.21.refs_6_), channel_id=1, source_target_pairs={{0,4},{4,0},{8,12},{12,8},{16,20},{20,16},{24,28},{28,24},{1,5},{5... | collective-permute-start | bytes 393224 | tf_op jit(solution)/shard_map/ppermute | solution.py:466
  64.9 1.4 collective-permute-start.23
  72.5 5.9 %collective-permute-start.26 = (bf16[17,32,128]{2,1,0:T(8,128)(2,1)S(1)}, bf16[17,32,128]{2,1,0:T(8,128)(2,1)S(1)}, u32[]{:S(2)}, u32[]{:S(2)}) collective-permute-start(bf16[17,32,128]{2,1,0:T(8,128)(2,1)S(1)} %get-tuple-element.110.refs_2_), channel_id=1, source_target_pairs={{0,4},{4,0},{8,12},{12,8},{16,20},{20,16},{24,28},{28,24},{1,5},{5... | collective-permute-start | bytes 417800 | tf_op jit(solution)/shard_map/ppermute | solution.py:466
  78.4 7.6 %collective-permute-start.27 = (bf16[17,32,128]{2,1,0:T(8,128)(2,1)S(1)}, bf16[17,32,128]{2,1,0:T(8,128)(2,1)S(1)}, u32[]{:S(2)}, u32[]{:S(2)}) collective-permute-start(bf16[17,32,128]{2,1,0:T(8,128)(2,1)S(1)} %get-tuple-element.114.refs_3_), channel_id=1, source_target_pairs={{0,8},{4,12},{8,0},{12,4},{16,24},{20,28},{24,16},{28,20},{1,9},{5... | collective-permute-start | bytes 417800 | tf_op jit(solution)/shard_map/ppermute | solution.py:466
  78.5 5.2 %collective-permute-start.25 = (bf16[16,32,128]{2,1,0:T(8,128)(2,1)S(1)}, bf16[16,32,128]{2,1,0:T(8,128)(2,1)S(1)}, u32[]{:S(2)}, u32[]{:S(2)}) collective-permute-start(bf16[16,32,128]{2,1,0:T(8,128)(2,1)S(1)} %get-tuple-element.108), channel_id=1, source_target_pairs={{0,4},{4,0},{8,12},{12,8},{16,20},{20,16},{24,28},{28,24},{1,5},{5... | collective-permute-start | bytes 393224 | tf_op jit(solution)/shard_map/ppermute | solution.py:466
  78.9 9.0 %collective-permute-start.24 = (bf16[16,32,128]{2,1,0:T(8,128)(2,1)S(1)}, bf16[16,32,128]{2,1,0:T(8,128)(2,1)S(1)}, u32[]{:S(2)}, u32[]{:S(2)}) collective-permute-start(bf16[16,32,128]{2,1,0:T(8,128)(2,1)S(1)} %get-tuple-element.106), channel_id=1, source_target_pairs={{0,8},{4,12},{8,0},{12,4},{16,24},{20,28},{24,16},{28,20},{1,9},{5... | collective-permute-start | bytes 393224 | tf_op jit(solution)/shard_map/ppermute | solution.py:466
  80.5 3.6 %collective-permute-start.28 = (f32[8,128]{1,0:T(8,128)S(1)}, f32[8,128]{1,0:T(8,128)S(1)}, u32[]{:S(2)}, u32[]{:S(2)}) collective-permute-start(f32[8,128]{1,0:T(8,128)S(1)} %get-tuple-element.115.refs_9_), channel_id=1, source_target_pairs={{0,2},{1,3},{2,0},{3,1},{4,6},{5,7},{6,4},{7,5},{8,10},{9,11},{10,... | collective-permute-start | bytes 12296 | tf_op jit(solution)/shard_map/ppermute | solution.py:466
  86.2 10.1 %collective-permute-start.31 = (bf16[17,32,128]{2,1,0:T(8,128)(2,1)S(1)}, bf16[17,32,128]{2,1,0:T(8,128)(2,1)S(1)}, u32[]{:S(2)}, u32[]{:S(2)}) collective-permute-start(bf16[17,32,128]{2,1,0:T(8,128)(2,1)S(1)} %fold.13.refs_2_.refs_4_), channel_id=1, source_target_pairs={{0,16},{4,20},{8,24},{12,28},{16,0},{20,4},{24,8},{28,12},{1,17},{... | collective-permute-start | bytes 417800 | tf_op jit(solution)/shard_map/ppermute | solution.py:466
  86.5 5.4 %collective-permute-start.30 = (bf16[16,32,128]{2,1,0:T(8,128)(2,1)S(1)}, bf16[16,32,128]{2,1,0:T(8,128)(2,1)S(1)}, u32[]{:S(2)}, u32[]{:S(2)}) collective-permute-start(bf16[16,32,128]{2,1,0:T(8,128)(2,1)S(1)} %get-tuple-element.116), channel_id=1, source_target_pairs={{0,8},{4,12},{8,0},{12,4},{16,24},{20,28},{24,16},{28,20},{1,9},{5... | collective-permute-start | bytes 393224 | tf_op jit(solution)/shard_map/ppermute | solution.py:466
  87.9 5.8 %collective-permute-start.29 = (bf16[16,32,128]{2,1,0:T(8,128)(2,1)S(1)}, bf16[16,32,128]{2,1,0:T(8,128)(2,1)S(1)}, u32[]{:S(2)}, u32[]{:S(2)}) collective-permute-start(bf16[16,32,128]{2,1,0:T(8,128)(2,1)S(1)} %fold.14), channel_id=1, source_target_pairs={{0,4},{4,0},{8,12},{12,8},{16,20},{20,16},{24,28},{28,24},{1,5},{5... | collective-permute-start | bytes 393224 | tf_op jit(solution)/shard_map/ppermute | solution.py:466
  96.4 6.2 %collective-permute-start.35 = (bf16[16,32,128]{2,1,0:T(8,128)(2,1)S(1)}, bf16[16,32,128]{2,1,0:T(8,128)(2,1)S(1)}, u32[]{:S(2)}, u32[]{:S(2)}) collective-permute-start(bf16[16,32,128]{2,1,0:T(8,128)(2,1)S(1)} %get-tuple-element.119.panel_ref.refs_0_), channel_id=1, source_target_pairs={{0,16},{4,20},{8,24},{12,28},{16,0},{20,4},{24,8},{28,12},{1,17},{... | collective-permute-start | bytes 393224 | tf_op jit(solution)/shard_map/ppermute | solution.py:466
  96.5 8.8 %collective-permute-start.32 = (bf16[16,32,128]{2,1,0:T(8,128)(2,1)S(1)}, bf16[16,32,128]{2,1,0:T(8,128)(2,1)S(1)}, u32[]{:S(2)}, u32[]{:S(2)}) collective-permute-start(bf16[16,32,128]{2,1,0:T(8,128)(2,1)S(1)} %get-tuple-element.119.panel_ref.refs_0_), channel_id=1, source_target_pairs={{0,4},{4,0},{8,12},{12,8},{16,20},{20,16},{24,28},{28,24},{1,5},{5... | collective-permute-start | bytes 393224 | tf_op jit(solution)/shard_map/ppermute | solution.py:466
  102.7 5.0 %collective-permute-start.37 = (bf16[16,32,128]{2,1,0:T(8,128)(2,1)S(1)}, bf16[16,32,128]{2,1,0:T(8,128)(2,1)S(1)}, u32[]{:S(2)}, u32[]{:S(2)}) collective-permute-start(bf16[16,32,128]{2,1,0:T(8,128)(2,1)S(1)} %get-tuple-element.122.refs_4_), channel_id=1, source_target_pairs={{0,8},{4,12},{8,0},{12,4},{16,24},{20,28},{24,16},{28,20},{1,9},{5... | collective-permute-start | bytes 393224 | tf_op jit(solution)/shard_map/ppermute | solution.py:466
  103.0 6.1 %collective-permute-start.33 = (bf16[16,32,128]{2,1,0:T(8,128)(2,1)S(1)}, bf16[16,32,128]{2,1,0:T(8,128)(2,1)S(1)}, u32[]{:S(2)}, u32[]{:S(2)}) collective-permute-start(bf16[16,32,128]{2,1,0:T(8,128)(2,1)S(1)} %get-tuple-element.119.panel_ref.refs_0_), channel_id=1, source_target_pairs={{0,8},{4,12},{8,0},{12,4},{16,24},{20,28},{24,16},{28,20},{1,9},{5... | collective-permute-start | bytes 393224 | tf_op jit(solution)/shard_map/ppermute | solution.py:466
  104.8 5.8 %collective-permute-start.36 = (bf16[16,32,128]{2,1,0:T(8,128)(2,1)S(1)}, bf16[16,32,128]{2,1,0:T(8,128)(2,1)S(1)}, u32[]{:S(2)}, u32[]{:S(2)}) collective-permute-start(bf16[16,32,128]{2,1,0:T(8,128)(2,1)S(1)} %get-tuple-element.122.refs_4_), channel_id=1, source_target_pairs={{0,4},{4,0},{8,12},{12,8},{16,20},{20,16},{24,28},{28,24},{1,5},{5... | collective-permute-start | bytes 393224 | tf_op jit(solution)/shard_map/ppermute | solution.py:466
  105.3 5.2 %collective-permute-start.34 = (bf16[16,32,128]{2,1,0:T(8,128)(2,1)S(1)}, bf16[16,32,128]{2,1,0:T(8,128)(2,1)S(1)}, u32[]{:S(2)}, u32[]{:S(2)}) collective-permute-start(bf16[16,32,128]{2,1,0:T(8,128)(2,1)S(1)} %collective-permute-done.32.refs_1_), channel_id=1, source_target_pairs={{0,8},{4,12},{8,0},{12,4},{16,24},{20,28},{24,16},{28,20},{1,9},{5... | collective-permute-start | bytes 393224 | tf_op jit(solution)/shard_map/ppermute | solution.py:466
  107.7 5.0 %collective-permute-start.38 = (bf16[16,32,128]{2,1,0:T(8,128)(2,1)S(1)}, bf16[16,32,128]{2,1,0:T(8,128)(2,1)S(1)}, u32[]{:S(2)}, u32[]{:S(2)}) collective-permute-start(bf16[16,32,128]{2,1,0:T(8,128)(2,1)S(1)} %collective-permute-done.37.refs_6_), channel_id=1, source_target_pairs={{0,4},{4,0},{8,12},{12,8},{16,20},{20,16},{24,28},{28,24},{1,5},{5... | collective-permute-start | bytes 393224 | tf_op jit(solution)/shard_map/ppermute | solution.py:466
  108.3 1.2 collective-permute-start.39
  116.1 5.8 %collective-permute-start.42 = (bf16[17,32,128]{2,1,0:T(8,128)(2,1)S(1)}, bf16[17,32,128]{2,1,0:T(8,128)(2,1)S(1)}, u32[]{:S(2)}, u32[]{:S(2)}) collective-permute-start(bf16[17,32,128]{2,1,0:T(8,128)(2,1)S(1)} %get-tuple-element.134.refs_2_), channel_id=1, source_target_pairs={{0,4},{4,0},{8,12},{12,8},{16,20},{20,16},{24,28},{28,24},{1,5},{5... | collective-permute-start | bytes 417800 | tf_op jit(solution)/shard_map/ppermute | solution.py:466
  122.0 7.3 %collective-permute-start.43 = (bf16[17,32,128]{2,1,0:T(8,128)(2,1)S(1)}, bf16[17,32,128]{2,1,0:T(8,128)(2,1)S(1)}, u32[]{:S(2)}, u32[]{:S(2)}) collective-permute-start(bf16[17,32,128]{2,1,0:T(8,128)(2,1)S(1)} %get-tuple-element.138.refs_3_), channel_id=1, source_target_pairs={{0,8},{4,12},{8,0},{12,4},{16,24},{20,28},{24,16},{28,20},{1,9},{5... | collective-permute-start | bytes 417800 | tf_op jit(solution)/shard_map/ppermute | solution.py:466
  122.1 5.0 %collective-permute-start.41 = (bf16[16,32,128]{2,1,0:T(8,128)(2,1)S(1)}, bf16[16,32,128]{2,1,0:T(8,128)(2,1)S(1)}, u32[]{:S(2)}, u32[]{:S(2)}) collective-permute-start(bf16[16,32,128]{2,1,0:T(8,128)(2,1)S(1)} %get-tuple-element.132), channel_id=1, source_target_pairs={{0,4},{4,0},{8,12},{12,8},{16,20},{20,16},{24,28},{28,24},{1,5},{5... | collective-permute-start | bytes 393224 | tf_op jit(solution)/shard_map/ppermute | solution.py:466
  122.5 9.0 %collective-permute-start.40 = (bf16[16,32,128]{2,1,0:T(8,128)(2,1)S(1)}, bf16[16,32,128]{2,1,0:T(8,128)(2,1)S(1)}, u32[]{:S(2)}, u32[]{:S(2)}) collective-permute-start(bf16[16,32,128]{2,1,0:T(8,128)(2,1)S(1)} %get-tuple-element.130), channel_id=1, source_target_pairs={{0,8},{4,12},{8,0},{12,4},{16,24},{20,28},{24,16},{28,20},{1,9},{5... | collective-permute-start | bytes 393224 | tf_op jit(solution)/shard_map/ppermute | solution.py:466
  124.3 3.6 %collective-permute-start.44 = (f32[8,128]{1,0:T(8,128)S(1)}, f32[8,128]{1,0:T(8,128)S(1)}, u32[]{:S(2)}, u32[]{:S(2)}) collective-permute-start(f32[8,128]{1,0:T(8,128)S(1)} %get-tuple-element.139.refs_9_), channel_id=1, source_target_pairs={{0,2},{1,3},{2,0},{3,1},{4,6},{5,7},{6,4},{7,5},{8,10},{9,11},{10,... | collective-permute-start | bytes 12296 | tf_op jit(solution)/shard_map/ppermute | solution.py:466
  129.5 7.9 %collective-permute-start.47 = (bf16[17,32,128]{2,1,0:T(8,128)(2,1)S(1)}, bf16[17,32,128]{2,1,0:T(8,128)(2,1)S(1)}, u32[]{:S(2)}, u32[]{:S(2)}) collective-permute-start(bf16[17,32,128]{2,1,0:T(8,128)(2,1)S(1)} %fold.16.refs_2_.refs_4_), channel_id=1, source_target_pairs={{0,16},{4,20},{8,24},{12,28},{16,0},{20,4},{24,8},{28,12},{1,17},{... | collective-permute-start | bytes 417800 | tf_op jit(solution)/shard_map/ppermute | solution.py:466
  131.0 6.4 %collective-permute-start.46 = (bf16[16,32,128]{2,1,0:T(8,128)(2,1)S(1)}, bf16[16,32,128]{2,1,0:T(8,128)(2,1)S(1)}, u32[]{:S(2)}, u32[]{:S(2)}) collective-permute-start(bf16[16,32,128]{2,1,0:T(8,128)(2,1)S(1)} %get-tuple-element.140), channel_id=1, source_target_pairs={{0,8},{4,12},{8,0},{12,4},{16,24},{20,28},{24,16},{28,20},{1,9},{5... | collective-permute-start | bytes 393224 | tf_op jit(solution)/shard_map/ppermute | solution.py:466
  131.5 5.9 %collective-permute-start.45 = (bf16[16,32,128]{2,1,0:T(8,128)(2,1)S(1)}, bf16[16,32,128]{2,1,0:T(8,128)(2,1)S(1)}, u32[]{:S(2)}, u32[]{:S(2)}) collective-permute-start(bf16[16,32,128]{2,1,0:T(8,128)(2,1)S(1)} %fold.17), channel_id=1, source_target_pairs={{0,4},{4,0},{8,12},{12,8},{16,20},{20,16},{24,28},{28,24},{1,5},{5... | collective-permute-start | bytes 393224 | tf_op jit(solution)/shard_map/ppermute | solution.py:466

commit v13 on v12

--- a/solution.py
+++ b/solution.py
@@ -15,9 +15,10 @@
 tail_weight = 2.0
 
 MIB = 1024 * 1024
-GROUP = 8
+GROUP = 16
 HEAD_GROUP = 64
 SMALL_VMEM = 6 * MIB
+LOCAL_VMEM = 8 * MIB
 
 
 def contract_last(left, right):
@@ -114,8 +115,12 @@
     return 2 if distance == 3 else distance & -distance
 
 
+def first_hop(distance):
+    return distance & -distance
+
+
 def children(distance, peers):
-    return [k for k in range(1, peers) if k ^ last_hop(k) == distance]
+    return [k for k in range(1, peers) if k ^ first_hop(k) == distance]
 
 
 def inner(peers):
@@ -270,7 +275,7 @@
                 whole(8, rows),
             ),
         ),
-        compiler_params=params(SMALL_VMEM),
+        compiler_params=params(LOCAL_VMEM),
         cost_estimate=pl.CostEstimate(
             flops=2 * scen_rows * blocks.size, bytes_accessed=2 * blocks.size, transcendentals=0
         ),
@@ -402,7 +407,7 @@
             out_specs=whole(*duals.shape),
             scratch_shapes=[pltpu.VMEM(duals.shape, jnp.float32)],
         ),
-        compiler_params=params(SMALL_VMEM),
+        compiler_params=params(LOCAL_VMEM),
         cost_estimate=pl.CostEstimate(
             flops=2 * scen_rows * blocks.size, bytes_accessed=2 * blocks.size, transcendentals=0
         ),
@@ -526,7 +531,7 @@
         )
         base = local_forward(touched, bar, local_blocks, duals, demand)
         tops = sorted(inner(net_size), key=lambda k: (-k.bit_count(), -k))[:-1]
-        groups = [(top,) for top in tops if top != 1] + [(1,)]
+        groups = [(top,) for top in tops]
         loss, loss_top = sends[net_size - 1], net_size - 1
         after = (base,)
         for group in groups:
@@ -536,12 +541,12 @@
                 terms.append(
                     (
                         kept[top],
-                        [swap(sends[k], "net", last_hop(k)) for k in below],
+                        [swap(sends[k], "net", first_hop(k)) for k in below],
                     )
                 )
-            chain = loss_top ^ last_hop(loss_top) == group[0]
+            chain = loss_top ^ first_hop(loss_top) == group[0]
             sums = (risk_sum,) if group[0] == tops[0] else ()
-            if group == (1,):
+            if loss_top == net_size // 2:
                 after = (loss,)
             if group[0] == net_size // 2:
                 after = risk_sums[1:]
@@ -556,7 +561,7 @@
                     risk_sum = risk_sum + swap(risk_sum, "scen", stride)
                 risk_sums = (risk_sum, swap(risk_sum, "scen", strides[-1]))
         below = sorted(children(0, net_size))
-        arrived = [swap(sends[k], "net", last_hop(k)) for k in below]
+        arrived = [swap(sends[k], "net", first_hop(k)) for k in below]
         duals, half, risk, excess_now, level, risk_sum = settle(
             kept[0],
             arrived,

time: 138 us -> 139 us (level)
  waiting for transfers between devices: 60 us -> 63.7 us
  Pallas kernels: 34.3 us -> 31.4 us
    ppermute x48, waiting for transfers between devices: 60 us -> 63.7 us  [swap(): return lax.ppermute(value, axis, [(i, i ^ distance) for i in range(size)])]
    pallas_call x3, Pallas kernels: 10 us -> 8.42 us  [local_forward(): pl.pallas_call(functools.partial(local_forward_kernel, touches, group, st...]
  transfers between devices with their start and end apart: 48 -> 48, of which waited for: 36 -> 33; matrix products, arithmetic and copies ran while one was open for 0% -> 0% of each run, Pallas kernels for 17% -> 15%
where the time goes in v13:
time: 139 us
  waiting for transfers between devices  63.7 us (46%)
  starting transfers between devices  36.7 us (26%)
  Pallas kernels  31.4 us (23%)
  local copies, waits for them, and re-layouts  5.05 us (4%)
  between operations  1.68 us (1%)
    ppermute x48, waiting for transfers between devices, swap(): return lax.ppermute(value, axis, [(i, i ^ distance) for i in range(size)])  63.7 us
    ppermute x48, starting transfers between devices, swap(): return lax.ppermute(value, axis, [(i, i ^ distance) for i in range(size)])  36.7 us
    pallas_call x3, Pallas kernels, local_adjoint(): pl.pallas_call(functools.partial(local_adjoint_kernel, touches, group), o...  11.7 us
    pallas_call x3, Pallas kernels, head_step(): pl.pallas_call(functools.partial(head_kernel, group, steps, peers), out_s...  8.68 us
    pallas_call x3, Pallas kernels, local_forward(): pl.pallas_call(functools.partial(local_forward_kernel, touches, group, st...  8.42 us
    unnamed x26, local copies, waits for them, and re-layouts  5.01 us
  transfers between devices with their start and end apart: 48, of which 33 were waited for; matrix products, arithmetic and copies ran while one was open for 0% of the time, Pallas kernels for 15%

profile of v13, /device:TPU:0, one launch (start us, length us, event | category | flops | bytes accessed | tf_op | source)
XLA Modules:
  0.0 138.6 jit_solution(13409685261118242673)
XLA Ops:
  0.7 0.9 copy-done
  1.6 4.1 %collective-permute-start = (bf16[16,32,128]{2,1,0:T(8,128)(2,1)S(1)}, bf16[16,32,128]{2,1,0:T(8,128)(2,1)S(1)}, u32[]{:S(2)}, u32[]{:S(2)}) collective-permute-start(bf16[16,32,128]{2,1,0:T(8,128)(2,1)S(1)} %fusion.panel_ref.refs_0_), channel_id=1, source_target_pairs={{0,16},{4,20},{8,24},{12,28},{16,0},{20,4},{24,8},{28,12},{1,17},{... | collective-permute-start | bytes 393224 | tf_op jit(solution)/shard_map/ppermute | solution.py:471
  5.7 1.5 %collective-permute-start.1 = (bf16[16,32,128]{2,1,0:T(8,128)(2,1)S(1)}, bf16[16,32,128]{2,1,0:T(8,128)(2,1)S(1)}, u32[]{:S(2)}, u32[]{:S(2)}) collective-permute-start(bf16[16,32,128]{2,1,0:T(8,128)(2,1)S(1)} %fusion.panel_ref.refs_0_), channel_id=1, source_target_pairs={{0,4},{4,0},{8,12},{12,8},{16,20},{20,16},{24,28},{28,24},{1,5},{5... | collective-permute-start | bytes 393224 | tf_op jit(solution)/shard_map/ppermute | solution.py:471
  7.2 3.4 %copy-done.1 = bf16[64,4,128,128]{3,2,1,0:T(8,128)(2,1)S(1)} copy-done((bf16[64,4,128,128]{3,2,1,0:T(8,128)(2,1)S(1)}, bf16[64,4,128,128]{3,2,1,0:T(8,128)(2,1)}, u32[]{:S(2)}) %copy-start.1) | copy-done | bytes 8388632
  10.6 0.7 copy-done.6
  11.3 3.9 %local_adjoint.3 = (f32[32,8192]{1,0:T(8,128)S(1)}, f32[8,128]{1,0:T(8,128)S(1)}) custom-call(s32[4,64]{1,0:T(4,128)S(1)} %bitcast.29, bf16[16,32,128]{2,1,0:T(8,128)(2,1)S(1)} %fusion.panel_ref.refs_0_, bf16[64,4,128,128]{3,2,1,0:T(8,128)(2,1)S(1)} %copy-done.1), custom_call_target="tpu_custom_call" | custom-call | flops 268435456 | bytes 8388608 | tf_op jit(solution)/shard_map/local_adjoint/pallas_call | solution.py:260
  15.8 1.6 %collective-permute-start.5 = (bf16[16,32,128]{2,1,0:T(8,128)(2,1)S(1)}, bf16[16,32,128]{2,1,0:T(8,128)(2,1)S(1)}, u32[]{:S(2)}, u32[]{:S(2)}) collective-permute-start(bf16[16,32,128]{2,1,0:T(8,128)(2,1)S(1)} %get-tuple-element.77.refs_0_.refs_4_), channel_id=1, source_target_pairs={{0,8},{4,12},{8,0},{12,4},{16,24},{20,28},{24,16},{28,20},{1,9},{5... | collective-permute-start | bytes 393224 | tf_op jit(solution)/shard_map/ppermute | solution.py:471
  18.4 1.6 %collective-permute-start.3 = (bf16[16,32,128]{2,1,0:T(8,128)(2,1)S(1)}, bf16[16,32,128]{2,1,0:T(8,128)(2,1)S(1)}, u32[]{:S(2)}, u32[]{:S(2)}) collective-permute-start(bf16[16,32,128]{2,1,0:T(8,128)(2,1)S(1)} %collective-permute-done.1.refs_1_), channel_id=1, source_target_pairs={{0,8},{4,12},{8,0},{12,4},{16,24},{20,28},{24,16},{28,20},{1,9},{5... | collective-permute-start | bytes 393224 | tf_op jit(solution)/shard_map/ppermute | solution.py:471
  20.0 2.3 %collective-permute-done.5.refs_6_ = bf16[16,32,128]{2,1,0:T(8,128)(2,1)S(1)} collective-permute-done((bf16[16,32,128]{2,1,0:T(8,128)(2,1)S(1)}, bf16[16,32,128]{2,1,0:T(8,128)(2,1)S(1)}, u32[]{:S(2)}, u32[]{:S(2)}) %collective-permute-start.5) | collective-permute-done | bytes 131104 | tf_op jit(solution)/shard_map/ppermute | solution.py:471
  23.7 1.0 collective-permute-done.2.refs_2_
  24.8 1.3 collective-permute-done.3.refs_3_
  26.1 1.1 collective-permute-done.6.refs_7_
  27.2 2.6 %head_step.3 = (f32[32,8192]{1,0:T(8,128)S(1)}, bf16[32,8192]{1,0:T(8,128)(2,1)S(1)}, f32[8,128]{1,0:T(8,128)S(1)}, f32[16,32,128]{2,1,0:T(8,128)S(1)}, f32[16,3...) custom-call(s32[64]{0:T(128)S(1)} %bitcast.35, ...), custom_call_target="tpu_custom_call" | custom-call | flops 134217728 | bytes 7864320 | tf_op jit(solution)/shard_map/head_step/pallas_call | solution.py:297
  30.5 2.8 %local_forward.3.refs_4_.refs_5_ = f32[16,32,128]{2,1,0:T(8,128)S(1)} custom-call(s32[4,64]{1,0:T(4,128)S(1)} %bitcast.30, bf16[32,8192]{1,0:T(8,128)(2,1)S(1)} %get-tuple-element.91.bar_ref, bf16[64,4,128,128]{3,2,1,0:T(8,128)(2,1)S(1)} %bitcast.25, f32[16,32,128]{2,1,0:T(8,128)S(1)} %bitcast_bitcast_fusion.duals_ref, f32[32,2048]{1,0:T(8,128)S(1)} %copy-done.4), custom_call_target="tpu_custom_call" | custom-call | flops 268435456 | bytes 8388608 | tf_op jit(solution)/shard_map/local_forward/pallas_call | solution.py:395
  33.3 1.6 %collective-permute-done.11.refs_1_ = bf16[17,32,128]{2,1,0:T(8,128)(2,1)S(1)} collective-permute-done((bf16[17,32,128]{2,1,0:T(8,128)(2,1)S(1)}, bf16[17,32,128]{2,1,0:T(8,128)(2,1)S(1)}, u32[]{:S(2)}, u32[]{:S(2)}) %collective-permute-start.11) | collective-permute-done | bytes 139296 | tf_op jit(solution)/shard_map/ppermute | solution.py:471
  35.1 1.8 %collective-permute-start.12 = (bf16[17,32,128]{2,1,0:T(8,128)(2,1)S(1)}, bf16[17,32,128]{2,1,0:T(8,128)(2,1)S(1)}, u32[]{:S(2)}, u32[]{:S(2)}) collective-permute-start(bf16[17,32,128]{2,1,0:T(8,128)(2,1)S(1)} %get-tuple-element.92.refs_3_), channel_id=1, source_target_pairs={{0,8},{4,12},{8,0},{12,4},{16,24},{20,28},{24,16},{28,20},{1,9},{5... | collective-permute-start | bytes 417800 | tf_op jit(solution)/shard_map/ppermute | solution.py:471
  37.2 1.6 %collective-permute-start.9 = (bf16[16,32,128]{2,1,0:T(8,128)(2,1)S(1)}, bf16[16,32,128]{2,1,0:T(8,128)(2,1)S(1)}, u32[]{:S(2)}, u32[]{:S(2)}) collective-permute-start(bf16[16,32,128]{2,1,0:T(8,128)(2,1)S(1)} %get-tuple-element.85), channel_id=1, source_target_pairs={{0,4},{4,0},{8,12},{12,8},{16,20},{20,16},{24,28},{28,24},{1,5},{5... | collective-permute-start | bytes 393224 | tf_op jit(solution)/shard_map/ppermute | solution.py:471
  38.9 1.5 %collective-permute-start.13 = (f32[8,128]{1,0:T(8,128)S(1)}, f32[8,128]{1,0:T(8,128)S(1)}, u32[]{:S(2)}, u32[]{:S(2)}) collective-permute-start(f32[8,128]{1,0:T(8,128)S(1)} %get-tuple-element.93.refs_9_), channel_id=1, source_target_pairs={{0,2},{1,3},{2,0},{3,1},{4,6},{5,7},{6,4},{7,5},{8,10},{9,11},{10,... | collective-permute-start | bytes 12296 | tf_op jit(solution)/shard_map/ppermute | solution.py:471
  40.4 2.5 %collective-permute-done.10.refs_1_ = bf16[16,32,128]{2,1,0:T(8,128)(2,1)S(1)} collective-permute-done((bf16[16,32,128]{2,1,0:T(8,128)(2,1)S(1)}, bf16[16,32,128]{2,1,0:T(8,128)(2,1)S(1)}, u32[]{:S(2)}, u32[]{:S(2)}) %collective-permute-start.10) | collective-permute-done | bytes 131104 | tf_op jit(solution)/shard_map/ppermute | solution.py:471
  43.4 0.9 collective-permute-done.9.refs_1_
  44.3 0.6 collective-permute-start.14
  44.9 3.8 %collective-permute-done.8.refs_1_ = bf16[16,32,128]{2,1,0:T(8,128)(2,1)S(1)} collective-permute-done((bf16[16,32,128]{2,1,0:T(8,128)(2,1)S(1)}, bf16[16,32,128]{2,1,0:T(8,128)(2,1)S(1)}, u32[]{:S(2)}, u32[]{:S(2)}) %collective-permute-start.8) | collective-permute-done | bytes 131104 | tf_op jit(solution)/shard_map/ppermute | solution.py:471
  48.7 0.7 collective-permute-done.14.refs_2_
  49.4 3.9 %collective-permute-done.15.refs_3_ = bf16[17,32,128]{2,1,0:T(8,128)(2,1)S(1)} collective-permute-done((bf16[17,32,128]{2,1,0:T(8,128)(2,1)S(1)}, bf16[17,32,128]{2,1,0:T(8,128)(2,1)S(1)}, u32[]{:S(2)}, u32[]{:S(2)}) %collective-permute-start.15) | collective-permute-done | bytes 139296 | tf_op jit(solution)/shard_map/ppermute | solution.py:471
  53.7 3.9 %local_adjoint.4 = (f32[32,8192]{1,0:T(8,128)S(1)}, f32[8,128]{1,0:T(8,128)S(1)}) custom-call(s32[4,64]{1,0:T(4,128)S(1)} %bitcast.31, bf16[16,32,128]{2,1,0:T(8,128)(2,1)S(1)} %get-tuple-element.96.panel_ref.refs_0_, bf16[64,4,128,128]{3,2,1,0:T(8,128)(2,1)S(1)} %bitcast.25), custom_call_target="tpu_custom_call" | custom-call | flops 268435456 | bytes 8388608 | tf_op jit(solution)/shard_map/local_adjoint/pallas_call | solution.py:260
  57.6 1.9 %collective-permute-done.19.arrived_ref = bf16[16,32,128]{2,1,0:T(8,128)(2,1)S(1)} collective-permute-done((bf16[16,32,128]{2,1,0:T(8,128)(2,1)S(1)}, bf16[16,32,128]{2,1,0:T(8,128)(2,1)S(1)}, u32[]{:S(2)}, u32[]{:S(2)}) %collective-permute-start.19) | collective-permute-done | bytes 131104 | tf_op jit(solution)/shard_map/ppermute | solution.py:471
  59.6 2.0 %collective-permute-start.17 = (bf16[16,32,128]{2,1,0:T(8,128)(2,1)S(1)}, bf16[16,32,128]{2,1,0:T(8,128)(2,1)S(1)}, u32[]{:S(2)}, u32[]{:S(2)}) collective-permute-start(bf16[16,32,128]{2,1,0:T(8,128)(2,1)S(1)} %get-tuple-element.96.panel_ref.refs_0_), channel_id=1, source_target_pairs={{0,8},{4,12},{8,0},{12,4},{16,24},{20,28},{24,16},{28,20},{1,9},{5... | collective-permute-start | bytes 393224 | tf_op jit(solution)/shard_map/ppermute | solution.py:471
  61.6 0.6 collective-permute-start.20
  62.3 2.2 %collective-permute-done.21.refs_6_ = bf16[16,32,128]{2,1,0:T(8,128)(2,1)S(1)} collective-permute-done((bf16[16,32,128]{2,1,0:T(8,128)(2,1)S(1)}, bf16[16,32,128]{2,1,0:T(8,128)(2,1)S(1)}, u32[]{:S(2)}, u32[]{:S(2)}) %collective-permute-start.21) | collective-permute-done | bytes 131104 | tf_op jit(solution)/shard_map/ppermute | solution.py:471
  64.6 0.6 collective-permute-start.22
  65.2 0.8 collective-permute-done.17.refs_2_
  66.3 1.0 collective-permute-done.18.refs_3_
  67.4 2.2 %collective-permute-done.22.refs_7_ = bf16[16,32,128]{2,1,0:T(8,128)(2,1)S(1)} collective-permute-done((bf16[16,32,128]{2,1,0:T(8,128)(2,1)S(1)}, bf16[16,32,128]{2,1,0:T(8,128)(2,1)S(1)}, u32[]{:S(2)}, u32[]{:S(2)}) %collective-permute-start.22) | collective-permute-done | bytes 131104 | tf_op jit(solution)/shard_map/ppermute | solution.py:471
  69.5 2.6 %head_step.4 = (f32[32,8192]{1,0:T(8,128)S(1)}, bf16[32,8192]{1,0:T(8,128)(2,1)S(1)}, f32[8,128]{1,0:T(8,128)S(1)}, f32[16,32,128]{2,1,0:T(8,128)S(1)}, f32[16,3...) custom-call(s32[64]{0:T(128)S(1)} %bitcast.36, ...), custom_call_target="tpu_custom_call" | custom-call | flops 134217728 | bytes 7864320 | tf_op jit(solution)/shard_map/head_step/pallas_call | solution.py:297
  72.2 0.7 collective-permute-start.27
  72.8 2.8 %local_forward.4.refs_4_.refs_5_ = f32[16,32,128]{2,1,0:T(8,128)S(1)} custom-call(s32[4,64]{1,0:T(4,128)S(1)} %bitcast.32, bf16[32,8192]{1,0:T(8,128)(2,1)S(1)} %get-tuple-element.113.bar_ref, bf16[64,4,128,128]{3,2,1,0:T(8,128)(2,1)S(1)} %bitcast.25, f32[16,32,128]{2,1,0:T(8,128)S(1)} %get-tuple-element.114.duals_ref, f32[32,2048]{1,0:T(8,128)S(1)} %copy-done.4), custom_call_target="tpu_custom_call" | custom-call | flops 268435456 | bytes 8388608 | tf_op jit(solution)/shard_map/local_forward/pallas_call | solution.py:395
  75.7 2.8 %collective-permute-done.27.refs_1_ = bf16[17,32,128]{2,1,0:T(8,128)(2,1)S(1)} collective-permute-done((bf16[17,32,128]{2,1,0:T(8,128)(2,1)S(1)}, bf16[17,32,128]{2,1,0:T(8,128)(2,1)S(1)}, u32[]{:S(2)}, u32[]{:S(2)}) %collective-permute-start.27) | collective-permute-done | bytes 139296 | tf_op jit(solution)/shard_map/ppermute | solution.py:471
  78.7 2.0 %collective-permute-start.25 = (bf16[16,32,128]{2,1,0:T(8,128)(2,1)S(1)}, bf16[16,32,128]{2,1,0:T(8,128)(2,1)S(1)}, u32[]{:S(2)}, u32[]{:S(2)}) collective-permute-start(bf16[16,32,128]{2,1,0:T(8,128)(2,1)S(1)} %get-tuple-element.107), channel_id=1, source_target_pairs={{0,4},{4,0},{8,12},{12,8},{16,20},{20,16},{24,28},{28,24},{1,5},{5... | collective-permute-start | bytes 393224 | tf_op jit(solution)/shard_map/ppermute | solution.py:471
  80.7 1.5 %collective-permute-start.29 = (f32[8,128]{1,0:T(8,128)S(1)}, f32[8,128]{1,0:T(8,128)S(1)}, u32[]{:S(2)}, u32[]{:S(2)}) collective-permute-start(f32[8,128]{1,0:T(8,128)S(1)} %get-tuple-element.116.refs_9_), channel_id=1, source_target_pairs={{0,2},{1,3},{2,0},{3,1},{4,6},{5,7},{6,4},{7,5},{8,10},{9,11},{10,... | collective-permute-start | bytes 12296 | tf_op jit(solution)/shard_map/ppermute | solution.py:471
  82.2 2.8 %collective-permute-done.26.refs_1_ = bf16[16,32,128]{2,1,0:T(8,128)(2,1)S(1)} collective-permute-done((bf16[16,32,128]{2,1,0:T(8,128)(2,1)S(1)}, bf16[16,32,128]{2,1,0:T(8,128)(2,1)S(1)}, u32[]{:S(2)}, u32[]{:S(2)}) %collective-permute-start.26) | collective-permute-done | bytes 131104 | tf_op jit(solution)/shard_map/ppermute | solution.py:471
  85.0 0.7 collective-permute-done.28.refs_2_
  85.9 2.4 %collective-permute-start.24 = (bf16[16,32,128]{2,1,0:T(8,128)(2,1)S(1)}, bf16[16,32,128]{2,1,0:T(8,128)(2,1)S(1)}, u32[]{:S(2)}, u32[]{:S(2)}) collective-permute-start(bf16[16,32,128]{2,1,0:T(8,128)(2,1)S(1)} %get-tuple-element.105), channel_id=1, source_target_pairs={{0,4},{4,0},{8,12},{12,8},{16,20},{20,16},{24,28},{28,24},{1,5},{5... | collective-permute-start | bytes 393224 | tf_op jit(solution)/shard_map/ppermute | solution.py:471
  88.3 1.2 collective-permute-start.30
  89.5 3.0 %collective-permute-done.24.refs_1_ = bf16[16,32,128]{2,1,0:T(8,128)(2,1)S(1)} collective-permute-done((bf16[16,32,128]{2,1,0:T(8,128)(2,1)S(1)}, bf16[16,32,128]{2,1,0:T(8,128)(2,1)S(1)}, u32[]{:S(2)}, u32[]{:S(2)}) %collective-permute-start.24) | collective-permute-done | bytes 131104 | tf_op jit(solution)/shard_map/ppermute | solution.py:471
  92.5 3.6 %collective-permute-done.30.refs_2_ = bf16[16,32,128]{2,1,0:T(8,128)(2,1)S(1)} collective-permute-done((bf16[16,32,128]{2,1,0:T(8,128)(2,1)S(1)}, bf16[16,32,128]{2,1,0:T(8,128)(2,1)S(1)}, u32[]{:S(2)}, u32[]{:S(2)}) %collective-permute-start.30) | collective-permute-done | bytes 131104 | tf_op jit(solution)/shard_map/ppermute | solution.py:471
  96.5 3.9 %local_adjoint.5 = (f32[32,8192]{1,0:T(8,128)S(1)}, f32[8,128]{1,0:T(8,128)S(1)}) custom-call(s32[4,64]{1,0:T(4,128)S(1)} %bitcast.33, bf16[16,32,128]{2,1,0:T(8,128)(2,1)S(1)} %get-tuple-element.119.panel_ref.refs_0_, bf16[64,4,128,128]{3,2,1,0:T(8,128)(2,1)S(1)} %bitcast.25), custom_call_target="tpu_custom_call" | custom-call | flops 268435456 | bytes 8388608 | tf_op jit(solution)/shard_map/local_adjoint/pallas_call | solution.py:260
  100.4 2.8 %collective-permute-done.35.arrived_ref = bf16[16,32,128]{2,1,0:T(8,128)(2,1)S(1)} collective-permute-done((bf16[16,32,128]{2,1,0:T(8,128)(2,1)S(1)}, bf16[16,32,128]{2,1,0:T(8,128)(2,1)S(1)}, u32[]{:S(2)}, u32[]{:S(2)}) %collective-permute-start.35) | collective-permute-done | bytes 131104 | tf_op jit(solution)/shard_map/ppermute | solution.py:471
  103.4 2.0 %collective-permute-start.33 = (bf16[16,32,128]{2,1,0:T(8,128)(2,1)S(1)}, bf16[16,32,128]{2,1,0:T(8,128)(2,1)S(1)}, u32[]{:S(2)}, u32[]{:S(2)}) collective-permute-start(bf16[16,32,128]{2,1,0:T(8,128)(2,1)S(1)} %get-tuple-element.119.panel_ref.refs_0_), channel_id=1, source_target_pairs={{0,8},{4,12},{8,0},{12,4},{16,24},{20,28},{24,16},{28,20},{1,9},{5... | collective-permute-start | bytes 393224 | tf_op jit(solution)/shard_map/ppermute | solution.py:471
  105.3 0.7 collective-permute-start.34
  106.0 2.2 %collective-permute-done.37.refs_6_ = bf16[16,32,128]{2,1,0:T(8,128)(2,1)S(1)} collective-permute-done((bf16[16,32,128]{2,1,0:T(8,128)(2,1)S(1)}, bf16[16,32,128]{2,1,0:T(8,128)(2,1)S(1)}, u32[]{:S(2)}, u32[]{:S(2)}) %collective-permute-start.37) | collective-permute-done | bytes 131104 | tf_op jit(solution)/shard_map/ppermute | solution.py:471
  108.3 1.4 %collective-permute-done.33.refs_2_ = bf16[16,32,128]{2,1,0:T(8,128)(2,1)S(1)} collective-permute-done((bf16[16,32,128]{2,1,0:T(8,128)(2,1)S(1)}, bf16[16,32,128]{2,1,0:T(8,128)(2,1)S(1)}, u32[]{:S(2)}, u32[]{:S(2)}) %collective-permute-start.33) | collective-permute-done | bytes 131104 | tf_op jit(solution)/shard_map/ppermute | solution.py:471
  109.7 1.4 %collective-permute-done.34.refs_3_ = bf16[16,32,128]{2,1,0:T(8,128)(2,1)S(1)} collective-permute-done((bf16[16,32,128]{2,1,0:T(8,128)(2,1)S(1)}, bf16[16,32,128]{2,1,0:T(8,128)(2,1)S(1)}, u32[]{:S(2)}, u32[]{:S(2)}) %collective-permute-start.34) | collective-permute-done | bytes 131104 | tf_op jit(solution)/shard_map/ppermute | solution.py:471
  111.1 2.2 %collective-permute-done.38.refs_7_ = bf16[16,32,128]{2,1,0:T(8,128)(2,1)S(1)} collective-permute-done((bf16[16,32,128]{2,1,0:T(8,128)(2,1)S(1)}, bf16[16,32,128]{2,1,0:T(8,128)(2,1)S(1)}, u32[]{:S(2)}, u32[]{:S(2)}) %collective-permute-start.38) | collective-permute-done | bytes 131104 | tf_op jit(solution)/shard_map/ppermute | solution.py:471
  113.2 3.4 %head_step.5 = (f32[32,8192]{1,0:T(8,128)}, bf16[32,8192]{1,0:T(8,128)(2,1)S(1)}, f32[8,128]{1,0:T(8,128)S(1)}, f32[16,32,128]{2,1,0:T(8,128)S(1)}, f32[16,32,12...) custom-call(s32[64]{0:T(128)S(1)} %bitcast.37, ...), custom_call_target="tpu_custom_call" | custom-call | flops 134217728 | bytes 7864320 | tf_op jit(solution)/shard_map/head_step/pallas_call | solution.py:297
  116.7 2.8 %local_forward.5.refs_4_.refs_5_ = f32[16,32,128]{2,1,0:T(8,128)S(1)} custom-call(s32[4,64]{1,0:T(4,128)S(1)} %bitcast.34, bf16[32,8192]{1,0:T(8,128)(2,1)S(1)} %get-tuple-element.137.bar_ref, bf16[64,4,128,128]{3,2,1,0:T(8,128)(2,1)S(1)} %bitcast.25, f32[16,32,128]{2,1,0:T(8,128)S(1)} %get-tuple-element.138.duals_ref, f32[32,2048]{1,0:T(8,128)S(1)} %copy-done.4), custom_call_target="tpu_custom_call" | custom-call | flops 268435456 | bytes 8388608 | tf_op jit(solution)/shard_map/local_forward/pallas_call | solution.py:395
  119.5 3.4 %collective-permute-done.43.refs_1_ = bf16[17,32,128]{2,1,0:T(8,128)(2,1)S(1)} collective-permute-done((bf16[17,32,128]{2,1,0:T(8,128)(2,1)S(1)}, bf16[17,32,128]{2,1,0:T(8,128)(2,1)S(1)}, u32[]{:S(2)}, u32[]{:S(2)}) %collective-permute-start.43) | collective-permute-done | bytes 139296 | tf_op jit(solution)/shard_map/ppermute | solution.py:471
  123.1 2.0 %collective-permute-start.41 = (bf16[16,32,128]{2,1,0:T(8,128)(2,1)S(1)}, bf16[16,32,128]{2,1,0:T(8,128)(2,1)S(1)}, u32[]{:S(2)}, u32[]{:S(2)}) collective-permute-start(bf16[16,32,128]{2,1,0:T(8,128)(2,1)S(1)} %get-tuple-element.131), channel_id=1, source_target_pairs={{0,4},{4,0},{8,12},{12,8},{16,20},{20,16},{24,28},{28,24},{1,5},{5... | collective-permute-start | bytes 393224 | tf_op jit(solution)/shard_map/ppermute | solution.py:471
  125.2 1.5 %collective-permute-start.45 = (f32[8,128]{1,0:T(8,128)S(1)}, f32[8,128]{1,0:T(8,128)S(1)}, u32[]{:S(2)}, u32[]{:S(2)}) collective-permute-start(f32[8,128]{1,0:T(8,128)S(1)} %get-tuple-element.140.refs_9_), channel_id=1, source_target_pairs={{0,2},{1,3},{2,0},{3,1},{4,6},{5,7},{6,4},{7,5},{8,10},{9,11},{10,... | collective-permute-start | bytes 12296 | tf_op jit(solution)/shard_map/ppermute | solution.py:471
  126.7 2.2 %collective-permute-done.42.refs_1_ = bf16[16,32,128]{2,1,0:T(8,128)(2,1)S(1)} collective-permute-done((bf16[16,32,128]{2,1,0:T(8,128)(2,1)S(1)}, bf16[16,32,128]{2,1,0:T(8,128)(2,1)S(1)}, u32[]{:S(2)}, u32[]{:S(2)}) %collective-permute-start.42) | collective-permute-done | bytes 131104 | tf_op jit(solution)/shard_map/ppermute | solution.py:471
  128.9 1.9 %collective-permute-done.44.refs_2_ = bf16[17,32,128]{2,1,0:T(8,128)(2,1)S(1)} collective-permute-done((bf16[17,32,128]{2,1,0:T(8,128)(2,1)S(1)}, bf16[17,32,128]{2,1,0:T(8,128)(2,1)S(1)}, u32[]{:S(2)}, u32[]{:S(2)}) %collective-permute-start.44) | collective-permute-done | bytes 139296 | tf_op jit(solution)/shard_map/ppermute | solution.py:471
  131.1 1.1 collective-permute-start.46
  132.2 3.8 %collective-permute-done.40.refs_1_ = bf16[16,32,128]{2,1,0:T(8,128)(2,1)S(1)} collective-permute-done((bf16[16,32,128]{2,1,0:T(8,128)(2,1)S(1)}, bf16[16,32,128]{2,1,0:T(8,128)(2,1)S(1)}, u32[]{:S(2)}, u32[]{:S(2)}) %collective-permute-start.40) | collective-permute-done | bytes 131104 | tf_op jit(solution)/shard_map/ppermute | solution.py:471
  136.2 1.6 %collective-permute-done.47.refs_3_ = bf16[17,32,128]{2,1,0:T(8,128)(2,1)S(1)} collective-permute-done((bf16[17,32,128]{2,1,0:T(8,128)(2,1)S(1)}, bf16[17,32,128]{2,1,0:T(8,128)(2,1)S(1)}, u32[]{:S(2)}, u32[]{:S(2)}) %collective-permute-start.47) | collective-permute-done | bytes 139296 | tf_op jit(solution)/shard_map/ppermute | solution.py:471
  137.8 0.8 settle.5
  (86 shorter events, 6.9 us)
Async XLA Ops:
  0.6 1.0 copy-start
  0.6 22.8 %copy-start.10 = (s32[64]{0:T(128)S(1)}, s32[64]{0:T(128)}, u32[]{:S(2)}) copy-start(s32[64]{0:T(128)} %param.21) | copy-start | bytes 772
  0.7 22.8 %copy-start.8 = (f32[32]{0:T(128)S(1)}, f32[32]{0:T(128)}, u32[]{:S(2)}) copy-start(f32[32]{0:T(128)} %param.15) | copy-start | bytes 388
  0.7 22.8 %copy-start.9 = (f32[32]{0:T(128)S(1)}, f32[32]{0:T(128)}, u32[]{:S(2)}) copy-start(f32[32]{0:T(128)} %param.14) | copy-start | bytes 388
  0.7 26.5 %copy-start.5 = (f32[8192]{0:T(1024)S(1)}, f32[8192]{0:T(1024)}, u32[]{:S(2)}) copy-start(f32[8192]{0:T(1024)} %param.17) | copy-start | bytes 98308
  1.6 13.6 %collective-permute-start = (bf16[16,32,128]{2,1,0:T(8,128)(2,1)S(1)}, bf16[16,32,128]{2,1,0:T(8,128)(2,1)S(1)}, u32[]{:S(2)}, u32[]{:S(2)}) collective-permute-start(bf16[16,32,128]{2,1,0:T(8,128)(2,1)S(1)} %fusion.panel_ref.refs_0_), channel_id=1, source_target_pairs={{0,16},{4,20},{8,24},{12,28},{16,0},{20,4},{24,8},{28,12},{1,17},{... | collective-permute-start | bytes 393224 | tf_op jit(solution)/shard_map/ppermute | solution.py:471
  5.7 12.7 %collective-permute-start.1 = (bf16[16,32,128]{2,1,0:T(8,128)(2,1)S(1)}, bf16[16,32,128]{2,1,0:T(8,128)(2,1)S(1)}, u32[]{:S(2)}, u32[]{:S(2)}) collective-permute-start(bf16[16,32,128]{2,1,0:T(8,128)(2,1)S(1)} %fusion.panel_ref.refs_0_), channel_id=1, source_target_pairs={{0,4},{4,0},{8,12},{12,8},{16,20},{20,16},{24,28},{28,24},{1,5},{5... | collective-permute-start | bytes 393224 | tf_op jit(solution)/shard_map/ppermute | solution.py:471
  7.2 3.4 %copy-start.1 = (bf16[64,4,128,128]{3,2,1,0:T(8,128)(2,1)S(1)}, bf16[64,4,128,128]{3,2,1,0:T(8,128)(2,1)}, u32[]{:S(2)}) copy-start(bf16[64,4,128,128]{3,2,1,0:T(8,128)(2,1)} %blocks_ref.11) | copy-start | bytes 25165828
  10.6 0.7 copy-start.6
  11.3 12.2 %copy-start.2 = (bf16[64,128,128]{2,1,0:T(8,128)(2,1)S(1)}, bf16[64,128,128]{2,1,0:T(8,128)(2,1)}, u32[]{:S(2)}) copy-start(bf16[64,128,128]{2,1,0:T(8,128)(2,1)} %refs_8_.5) | copy-start | bytes 6291460
  11.3 12.2 %copy-start.3 = (f32[32,8192]{1,0:T(8,128)S(1)}, f32[32,8192]{1,0:T(8,128)}, u32[]{:S(2)}) copy-start(f32[32,8192]{1,0:T(8,128)} %refs_10_.1) | copy-start | bytes 3145732
  11.3 19.2 %slice-start = ((s8[8388608]{0:T(1024)(128)(4,1)}), s8[4194304]{0:T(1024)(128)(4,1)S(1)}, s32[]{:S(2)}) async-start(s8[8388608]{0:T(1024)(128)(4,1)} %bitcast.24), calls=%async_computation | async-start | bytes 8388608
  11.3 19.2 %copy-start.4 = (f32[32,2048]{1,0:T(8,128)S(1)}, f32[32,2048]{1,0:T(8,128)}, u32[]{:S(2)}) copy-start(f32[32,2048]{1,0:T(8,128)} %demand_ref.5) | copy-start | bytes 786436
  11.3 19.2 %copy-start.7 = (s32[64,4]{0,1:T(4,128)S(1)}, s32[64,4]{0,1:T(4,128)}, u32[]{:S(2)}) copy-start(s32[64,4]{0,1:T(4,128)} %param.20) | copy-start | bytes 3076
  15.8 6.4 %collective-permute-start.5 = (bf16[16,32,128]{2,1,0:T(8,128)(2,1)S(1)}, bf16[16,32,128]{2,1,0:T(8,128)(2,1)S(1)}, u32[]{:S(2)}, u32[]{:S(2)}) collective-permute-start(bf16[16,32,128]{2,1,0:T(8,128)(2,1)S(1)} %get-tuple-element.77.refs_0_.refs_4_), channel_id=1, source_target_pairs={{0,8},{4,12},{8,0},{12,4},{16,24},{20,28},{24,16},{28,20},{1,9},{5... | collective-permute-start | bytes 393224 | tf_op jit(solution)/shard_map/ppermute | solution.py:471
  17.4 7.3 %collective-permute-start.2 = (bf16[16,32,128]{2,1,0:T(8,128)(2,1)S(1)}, bf16[16,32,128]{2,1,0:T(8,128)(2,1)S(1)}, u32[]{:S(2)}, u32[]{:S(2)}) collective-permute-start(bf16[16,32,128]{2,1,0:T(8,128)(2,1)S(1)} %fusion.panel_ref.refs_0_), channel_id=1, source_target_pairs={{0,8},{4,12},{8,0},{12,4},{16,24},{20,28},{24,16},{28,20},{1,9},{5... | collective-permute-start | bytes 393224 | tf_op jit(solution)/shard_map/ppermute | solution.py:471
  17.8 8.3 %collective-permute-start.4 = (bf16[16,32,128]{2,1,0:T(8,128)(2,1)S(1)}, bf16[16,32,128]{2,1,0:T(8,128)(2,1)S(1)}, u32[]{:S(2)}, u32[]{:S(2)}) collective-permute-start(bf16[16,32,128]{2,1,0:T(8,128)(2,1)S(1)} %get-tuple-element.77.refs_0_.refs_4_), channel_id=1, source_target_pairs={{0,4},{4,0},{8,12},{12,8},{16,20},{20,16},{24,28},{28,24},{1,5},{5... | collective-permute-start | bytes 393224 | tf_op jit(solution)/shard_map/ppermute | solution.py:471
  18.4 7.7 %collective-permute-start.3 = (bf16[16,32,128]{2,1,0:T(8,128)(2,1)S(1)}, bf16[16,32,128]{2,1,0:T(8,128)(2,1)S(1)}, u32[]{:S(2)}, u32[]{:S(2)}) collective-permute-start(bf16[16,32,128]{2,1,0:T(8,128)(2,1)S(1)} %collective-permute-done.1.refs_1_), channel_id=1, source_target_pairs={{0,8},{4,12},{8,0},{12,4},{16,24},{20,28},{24,16},{28,20},{1,9},{5... | collective-permute-start | bytes 393224 | tf_op jit(solution)/shard_map/ppermute | solution.py:471
  22.2 5.0 %collective-permute-start.6 = (bf16[16,32,128]{2,1,0:T(8,128)(2,1)S(1)}, bf16[16,32,128]{2,1,0:T(8,128)(2,1)S(1)}, u32[]{:S(2)}, u32[]{:S(2)}) collective-permute-start(bf16[16,32,128]{2,1,0:T(8,128)(2,1)S(1)} %collective-permute-done.5.refs_6_), channel_id=1, source_target_pairs={{0,4},{4,0},{8,12},{12,8},{16,20},{20,16},{24,28},{28,24},{1,5},{5... | collective-permute-start | bytes 393224 | tf_op jit(solution)/shard_map/ppermute | solution.py:471
  23.5 7.0 %slice-start.1 = ((s8[8388608]{0:T(1024)(128)(4,1)}), s8[4194304]{0:T(1024)(128)(4,1)S(1)}, s32[]{:S(2)}) async-start(s8[8388608]{0:T(1024)(128)(4,1)} %bitcast.24), calls=%async_computation.1 | async-start | bytes 8388608
  23.6 1.2 collective-permute-start.7
  29.8 5.1 %collective-permute-start.11 = (bf16[17,32,128]{2,1,0:T(8,128)(2,1)S(1)}, bf16[17,32,128]{2,1,0:T(8,128)(2,1)S(1)}, u32[]{:S(2)}, u32[]{:S(2)}) collective-permute-start(bf16[17,32,128]{2,1,0:T(8,128)(2,1)S(1)} %get-tuple-element.89.refs_2_), channel_id=1, source_target_pairs={{0,4},{4,0},{8,12},{12,8},{16,20},{20,16},{24,28},{28,24},{1,5},{5... | collective-permute-start | bytes 417800 | tf_op jit(solution)/shard_map/ppermute | solution.py:471
  35.1 7.8 %collective-permute-start.12 = (bf16[17,32,128]{2,1,0:T(8,128)(2,1)S(1)}, bf16[17,32,128]{2,1,0:T(8,128)(2,1)S(1)}, u32[]{:S(2)}, u32[]{:S(2)}) collective-permute-start(bf16[17,32,128]{2,1,0:T(8,128)(2,1)S(1)} %get-tuple-element.92.refs_3_), channel_id=1, source_target_pairs={{0,8},{4,12},{8,0},{12,4},{16,24},{20,28},{24,16},{28,20},{1,9},{5... | collective-permute-start | bytes 417800 | tf_op jit(solution)/shard_map/ppermute | solution.py:471
  36.9 6.0 %collective-permute-start.10 = (bf16[16,32,128]{2,1,0:T(8,128)(2,1)S(1)}, bf16[16,32,128]{2,1,0:T(8,128)(2,1)S(1)}, u32[]{:S(2)}, u32[]{:S(2)}) collective-permute-start(bf16[16,32,128]{2,1,0:T(8,128)(2,1)S(1)} %get-tuple-element.87), channel_id=1, source_target_pairs={{0,4},{4,0},{8,12},{12,8},{16,20},{20,16},{24,28},{28,24},{1,5},{5... | collective-permute-start | bytes 393224 | tf_op jit(solution)/shard_map/ppermute | solution.py:471
  37.2 7.0 %collective-permute-start.9 = (bf16[16,32,128]{2,1,0:T(8,128)(2,1)S(1)}, bf16[16,32,128]{2,1,0:T(8,128)(2,1)S(1)}, u32[]{:S(2)}, u32[]{:S(2)}) collective-permute-start(bf16[16,32,128]{2,1,0:T(8,128)(2,1)S(1)} %get-tuple-element.85), channel_id=1, source_target_pairs={{0,4},{4,0},{8,12},{12,8},{16,20},{20,16},{24,28},{28,24},{1,5},{5... | collective-permute-start | bytes 393224 | tf_op jit(solution)/shard_map/ppermute | solution.py:471
  38.9 4.0 %collective-permute-start.13 = (f32[8,128]{1,0:T(8,128)S(1)}, f32[8,128]{1,0:T(8,128)S(1)}, u32[]{:S(2)}, u32[]{:S(2)}) collective-permute-start(f32[8,128]{1,0:T(8,128)S(1)} %get-tuple-element.93.refs_9_), channel_id=1, source_target_pairs={{0,2},{1,3},{2,0},{3,1},{4,6},{5,7},{6,4},{7,5},{8,10},{9,11},{10,... | collective-permute-start | bytes 12296 | tf_op jit(solution)/shard_map/ppermute | solution.py:471
  43.0 10.3 %collective-permute-start.15 = (bf16[17,32,128]{2,1,0:T(8,128)(2,1)S(1)}, bf16[17,32,128]{2,1,0:T(8,128)(2,1)S(1)}, u32[]{:S(2)}, u32[]{:S(2)}) collective-permute-start(bf16[17,32,128]{2,1,0:T(8,128)(2,1)S(1)} %fold.10.refs_2_.refs_4_), channel_id=1, source_target_pairs={{0,16},{4,20},{8,24},{12,28},{16,0},{20,4},{24,8},{28,12},{1,17},{... | collective-permute-start | bytes 417800 | tf_op jit(solution)/shard_map/ppermute | solution.py:471
  43.1 5.6 %collective-permute-start.8 = (bf16[16,32,128]{2,1,0:T(8,128)(2,1)S(1)}, bf16[16,32,128]{2,1,0:T(8,128)(2,1)S(1)}, u32[]{:S(2)}, u32[]{:S(2)}) collective-permute-start(bf16[16,32,128]{2,1,0:T(8,128)(2,1)S(1)} %get-tuple-element.83), channel_id=1, source_target_pairs={{0,4},{4,0},{8,12},{12,8},{16,20},{20,16},{24,28},{28,24},{1,5},{5... | collective-permute-start | bytes 393224 | tf_op jit(solution)/shard_map/ppermute | solution.py:471
  44.3 5.1 %collective-permute-start.14 = (bf16[16,32,128]{2,1,0:T(8,128)(2,1)S(1)}, bf16[16,32,128]{2,1,0:T(8,128)(2,1)S(1)}, u32[]{:S(2)}, u32[]{:S(2)}) collective-permute-start(bf16[16,32,128]{2,1,0:T(8,128)(2,1)S(1)} %fold.11), channel_id=1, source_target_pairs={{0,8},{4,12},{8,0},{12,4},{16,24},{20,28},{24,16},{28,20},{1,9},{5... | collective-permute-start | bytes 393224 | tf_op jit(solution)/shard_map/ppermute | solution.py:471
  53.5 6.0 %collective-permute-start.19 = (bf16[16,32,128]{2,1,0:T(8,128)(2,1)S(1)}, bf16[16,32,128]{2,1,0:T(8,128)(2,1)S(1)}, u32[]{:S(2)}, u32[]{:S(2)}) collective-permute-start(bf16[16,32,128]{2,1,0:T(8,128)(2,1)S(1)} %get-tuple-element.96.panel_ref.refs_0_), channel_id=1, source_target_pairs={{0,16},{4,20},{8,24},{12,28},{16,0},{20,4},{24,8},{28,12},{1,17},{... | collective-permute-start | bytes 393224 | tf_op jit(solution)/shard_map/ppermute | solution.py:471
  53.5 8.7 %collective-permute-start.16 = (bf16[16,32,128]{2,1,0:T(8,128)(2,1)S(1)}, bf16[16,32,128]{2,1,0:T(8,128)(2,1)S(1)}, u32[]{:S(2)}, u32[]{:S(2)}) collective-permute-start(bf16[16,32,128]{2,1,0:T(8,128)(2,1)S(1)} %get-tuple-element.96.panel_ref.refs_0_), channel_id=1, source_target_pairs={{0,4},{4,0},{8,12},{12,8},{16,20},{20,16},{24,28},{28,24},{1,5},{5... | collective-permute-start | bytes 393224 | tf_op jit(solution)/shard_map/ppermute | solution.py:471
  59.5 5.0 %collective-permute-start.21 = (bf16[16,32,128]{2,1,0:T(8,128)(2,1)S(1)}, bf16[16,32,128]{2,1,0:T(8,128)(2,1)S(1)}, u32[]{:S(2)}, u32[]{:S(2)}) collective-permute-start(bf16[16,32,128]{2,1,0:T(8,128)(2,1)S(1)} %get-tuple-element.99.refs_4_), channel_id=1, source_target_pairs={{0,8},{4,12},{8,0},{12,4},{16,24},{20,28},{24,16},{28,20},{1,9},{5... | collective-permute-start | bytes 393224 | tf_op jit(solution)/shard_map/ppermute | solution.py:471
  59.6 6.4 %collective-permute-start.17 = (bf16[16,32,128]{2,1,0:T(8,128)(2,1)S(1)}, bf16[16,32,128]{2,1,0:T(8,128)(2,1)S(1)}, u32[]{:S(2)}, u32[]{:S(2)}) collective-permute-start(bf16[16,32,128]{2,1,0:T(8,128)(2,1)S(1)} %get-tuple-element.96.panel_ref.refs_0_), channel_id=1, source_target_pairs={{0,8},{4,12},{8,0},{12,4},{16,24},{20,28},{24,16},{28,20},{1,9},{5... | collective-permute-start | bytes 393224 | tf_op jit(solution)/shard_map/ppermute | solution.py:471
  61.6 5.8 %collective-permute-start.20 = (bf16[16,32,128]{2,1,0:T(8,128)(2,1)S(1)}, bf16[16,32,128]{2,1,0:T(8,128)(2,1)S(1)}, u32[]{:S(2)}, u32[]{:S(2)}) collective-permute-start(bf16[16,32,128]{2,1,0:T(8,128)(2,1)S(1)} %get-tuple-element.99.refs_4_), channel_id=1, source_target_pairs={{0,4},{4,0},{8,12},{12,8},{16,20},{20,16},{24,28},{28,24},{1,5},{5... | collective-permute-start | bytes 393224 | tf_op jit(solution)/shard_map/ppermute | solution.py:471
  62.2 5.1 %collective-permute-start.18 = (bf16[16,32,128]{2,1,0:T(8,128)(2,1)S(1)}, bf16[16,32,128]{2,1,0:T(8,128)(2,1)S(1)}, u32[]{:S(2)}, u32[]{:S(2)}) collective-permute-start(bf16[16,32,128]{2,1,0:T(8,128)(2,1)S(1)} %collective-permute-done.16.refs_1_), channel_id=1, source_target_pairs={{0,8},{4,12},{8,0},{12,4},{16,24},{20,28},{24,16},{28,20},{1,9},{5... | collective-permute-start | bytes 393224 | tf_op jit(solution)/shard_map/ppermute | solution.py:471
  64.6 5.0 %collective-permute-start.22 = (bf16[16,32,128]{2,1,0:T(8,128)(2,1)S(1)}, bf16[16,32,128]{2,1,0:T(8,128)(2,1)S(1)}, u32[]{:S(2)}, u32[]{:S(2)}) collective-permute-start(bf16[16,32,128]{2,1,0:T(8,128)(2,1)S(1)} %collective-permute-done.21.refs_6_), channel_id=1, source_target_pairs={{0,4},{4,0},{8,12},{12,8},{16,20},{20,16},{24,28},{28,24},{1,5},{5... | collective-permute-start | bytes 393224 | tf_op jit(solution)/shard_map/ppermute | solution.py:471
  65.2 1.2 collective-permute-start.23
  72.2 6.3 %collective-permute-start.27 = (bf16[17,32,128]{2,1,0:T(8,128)(2,1)S(1)}, bf16[17,32,128]{2,1,0:T(8,128)(2,1)S(1)}, u32[]{:S(2)}, u32[]{:S(2)}) collective-permute-start(bf16[17,32,128]{2,1,0:T(8,128)(2,1)S(1)} %get-tuple-element.111.refs_2_), channel_id=1, source_target_pairs={{0,4},{4,0},{8,12},{12,8},{16,20},{20,16},{24,28},{28,24},{1,5},{5... | collective-permute-start | bytes 417800 | tf_op jit(solution)/shard_map/ppermute | solution.py:471
  78.5 7.2 %collective-permute-start.28 = (bf16[17,32,128]{2,1,0:T(8,128)(2,1)S(1)}, bf16[17,32,128]{2,1,0:T(8,128)(2,1)S(1)}, u32[]{:S(2)}, u32[]{:S(2)}) collective-permute-start(bf16[17,32,128]{2,1,0:T(8,128)(2,1)S(1)} %get-tuple-element.115.refs_3_), channel_id=1, source_target_pairs={{0,8},{4,12},{8,0},{12,4},{16,24},{20,28},{24,16},{28,20},{1,9},{5... | collective-permute-start | bytes 417800 | tf_op jit(solution)/shard_map/ppermute | solution.py:471
  78.6 6.4 %collective-permute-start.26 = (bf16[16,32,128]{2,1,0:T(8,128)(2,1)S(1)}, bf16[16,32,128]{2,1,0:T(8,128)(2,1)S(1)}, u32[]{:S(2)}, u32[]{:S(2)}) collective-permute-start(bf16[16,32,128]{2,1,0:T(8,128)(2,1)S(1)} %get-tuple-element.109), channel_id=1, source_target_pairs={{0,4},{4,0},{8,12},{12,8},{16,20},{20,16},{24,28},{28,24},{1,5},{5... | collective-permute-start | bytes 393224 | tf_op jit(solution)/shard_map/ppermute | solution.py:471
  78.7 9.6 %collective-permute-start.25 = (bf16[16,32,128]{2,1,0:T(8,128)(2,1)S(1)}, bf16[16,32,128]{2,1,0:T(8,128)(2,1)S(1)}, u32[]{:S(2)}, u32[]{:S(2)}) collective-permute-start(bf16[16,32,128]{2,1,0:T(8,128)(2,1)S(1)} %get-tuple-element.107), channel_id=1, source_target_pairs={{0,4},{4,0},{8,12},{12,8},{16,20},{20,16},{24,28},{28,24},{1,5},{5... | collective-permute-start | bytes 393224 | tf_op jit(solution)/shard_map/ppermute | solution.py:471
  80.7 4.3 %collective-permute-start.29 = (f32[8,128]{1,0:T(8,128)S(1)}, f32[8,128]{1,0:T(8,128)S(1)}, u32[]{:S(2)}, u32[]{:S(2)}) collective-permute-start(f32[8,128]{1,0:T(8,128)S(1)} %get-tuple-element.116.refs_9_), channel_id=1, source_target_pairs={{0,2},{1,3},{2,0},{3,1},{4,6},{5,7},{6,4},{7,5},{8,10},{9,11},{10,... | collective-permute-start | bytes 12296 | tf_op jit(solution)/shard_map/ppermute | solution.py:471
  85.8 10.3 %collective-permute-start.31 = (bf16[17,32,128]{2,1,0:T(8,128)(2,1)S(1)}, bf16[17,32,128]{2,1,0:T(8,128)(2,1)S(1)}, u32[]{:S(2)}, u32[]{:S(2)}) collective-permute-start(bf16[17,32,128]{2,1,0:T(8,128)(2,1)S(1)} %fold.13.refs_2_.refs_4_), channel_id=1, source_target_pairs={{0,16},{4,20},{8,24},{12,28},{16,0},{20,4},{24,8},{28,12},{1,17},{... | collective-permute-start | bytes 417800 | tf_op jit(solution)/shard_map/ppermute | solution.py:471
  85.9 6.6 %collective-permute-start.24 = (bf16[16,32,128]{2,1,0:T(8,128)(2,1)S(1)}, bf16[16,32,128]{2,1,0:T(8,128)(2,1)S(1)}, u32[]{:S(2)}, u32[]{:S(2)}) collective-permute-start(bf16[16,32,128]{2,1,0:T(8,128)(2,1)S(1)} %get-tuple-element.105), channel_id=1, source_target_pairs={{0,4},{4,0},{8,12},{12,8},{16,20},{20,16},{24,28},{28,24},{1,5},{5... | collective-permute-start | bytes 393224 | tf_op jit(solution)/shard_map/ppermute | solution.py:471
  88.3 7.8 %collective-permute-start.30 = (bf16[16,32,128]{2,1,0:T(8,128)(2,1)S(1)}, bf16[16,32,128]{2,1,0:T(8,128)(2,1)S(1)}, u32[]{:S(2)}, u32[]{:S(2)}) collective-permute-start(bf16[16,32,128]{2,1,0:T(8,128)(2,1)S(1)} %fold.14), channel_id=1, source_target_pairs={{0,8},{4,12},{8,0},{12,4},{16,24},{20,28},{24,16},{28,20},{1,9},{5... | collective-permute-start | bytes 393224 | tf_op jit(solution)/shard_map/ppermute | solution.py:471
  96.3 6.9 %collective-permute-start.35 = (bf16[16,32,128]{2,1,0:T(8,128)(2,1)S(1)}, bf16[16,32,128]{2,1,0:T(8,128)(2,1)S(1)}, u32[]{:S(2)}, u32[]{:S(2)}) collective-permute-start(bf16[16,32,128]{2,1,0:T(8,128)(2,1)S(1)} %get-tuple-element.119.panel_ref.refs_0_), channel_id=1, source_target_pairs={{0,16},{4,20},{8,24},{12,28},{16,0},{20,4},{24,8},{28,12},{1,17},{... | collective-permute-start | bytes 393224 | tf_op jit(solution)/shard_map/ppermute | solution.py:471
  96.4 8.9 %collective-permute-start.32 = (bf16[16,32,128]{2,1,0:T(8,128)(2,1)S(1)}, bf16[16,32,128]{2,1,0:T(8,128)(2,1)S(1)}, u32[]{:S(2)}, u32[]{:S(2)}) collective-permute-start(bf16[16,32,128]{2,1,0:T(8,128)(2,1)S(1)} %get-tuple-element.119.panel_ref.refs_0_), channel_id=1, source_target_pairs={{0,4},{4,0},{8,12},{12,8},{16,20},{20,16},{24,28},{28,24},{1,5},{5... | collective-permute-start | bytes 393224 | tf_op jit(solution)/shard_map/ppermute | solution.py:471
  103.2 5.0 %collective-permute-start.37 = (bf16[16,32,128]{2,1,0:T(8,128)(2,1)S(1)}, bf16[16,32,128]{2,1,0:T(8,128)(2,1)S(1)}, u32[]{:S(2)}, u32[]{:S(2)}) collective-permute-start(bf16[16,32,128]{2,1,0:T(8,128)(2,1)S(1)} %get-tuple-element.122.refs_4_), channel_id=1, source_target_pairs={{0,8},{4,12},{8,0},{12,4},{16,24},{20,28},{24,16},{28,20},{1,9},{5... | collective-permute-start | bytes 393224 | tf_op jit(solution)/shard_map/ppermute | solution.py:471
  103.4 6.3 %collective-permute-start.33 = (bf16[16,32,128]{2,1,0:T(8,128)(2,1)S(1)}, bf16[16,32,128]{2,1,0:T(8,128)(2,1)S(1)}, u32[]{:S(2)}, u32[]{:S(2)}) collective-permute-start(bf16[16,32,128]{2,1,0:T(8,128)(2,1)S(1)} %get-tuple-element.119.panel_ref.refs_0_), channel_id=1, source_target_pairs={{0,8},{4,12},{8,0},{12,4},{16,24},{20,28},{24,16},{28,20},{1,9},{5... | collective-permute-start | bytes 393224 | tf_op jit(solution)/shard_map/ppermute | solution.py:471
  105.3 5.8 %collective-permute-start.36 = (bf16[16,32,128]{2,1,0:T(8,128)(2,1)S(1)}, bf16[16,32,128]{2,1,0:T(8,128)(2,1)S(1)}, u32[]{:S(2)}, u32[]{:S(2)}) collective-permute-start(bf16[16,32,128]{2,1,0:T(8,128)(2,1)S(1)} %get-tuple-element.122.refs_4_), channel_id=1, source_target_pairs={{0,4},{4,0},{8,12},{12,8},{16,20},{20,16},{24,28},{28,24},{1,5},{5... | collective-permute-start | bytes 393224 | tf_op jit(solution)/shard_map/ppermute | solution.py:471
  105.3 5.7 %collective-permute-start.34 = (bf16[16,32,128]{2,1,0:T(8,128)(2,1)S(1)}, bf16[16,32,128]{2,1,0:T(8,128)(2,1)S(1)}, u32[]{:S(2)}, u32[]{:S(2)}) collective-permute-start(bf16[16,32,128]{2,1,0:T(8,128)(2,1)S(1)} %collective-permute-done.32.refs_1_), channel_id=1, source_target_pairs={{0,8},{4,12},{8,0},{12,4},{16,24},{20,28},{24,16},{28,20},{1,9},{5... | collective-permute-start | bytes 393224 | tf_op jit(solution)/shard_map/ppermute | solution.py:471
  108.3 5.0 %collective-permute-start.38 = (bf16[16,32,128]{2,1,0:T(8,128)(2,1)S(1)}, bf16[16,32,128]{2,1,0:T(8,128)(2,1)S(1)}, u32[]{:S(2)}, u32[]{:S(2)}) collective-permute-start(bf16[16,32,128]{2,1,0:T(8,128)(2,1)S(1)} %collective-permute-done.37.refs_6_), channel_id=1, source_target_pairs={{0,4},{4,0},{8,12},{12,8},{16,20},{20,16},{24,28},{28,24},{1,5},{5... | collective-permute-start | bytes 393224 | tf_op jit(solution)/shard_map/ppermute | solution.py:471
  108.3 1.4 %collective-permute-start.39 = (f32[8,128]{1,0:T(8,128)S(1)}, f32[8,128]{1,0:T(8,128)S(1)}, u32[]{:S(2)}, u32[]{:S(2)}) collective-permute-start(f32[8,128]{1,0:T(8,128)S(1)} %get-tuple-element.126.refs_13_), channel_id=1, source_target_pairs={{0,1},{1,0},{2,3},{3,2},{4,5},{5,4},{6,7},{7,6},{8,9},{9,8},{10,11... | collective-permute-start | bytes 12296 | tf_op jit(solution)/shard_map/ppermute | solution.py:471
  116.7 6.2 %collective-permute-start.43 = (bf16[17,32,128]{2,1,0:T(8,128)(2,1)S(1)}, bf16[17,32,128]{2,1,0:T(8,128)(2,1)S(1)}, u32[]{:S(2)}, u32[]{:S(2)}) collective-permute-start(bf16[17,32,128]{2,1,0:T(8,128)(2,1)S(1)} %get-tuple-element.135.refs_2_), channel_id=1, source_target_pairs={{0,4},{4,0},{8,12},{12,8},{16,20},{20,16},{24,28},{28,24},{1,5},{5... | collective-permute-start | bytes 417800 | tf_op jit(solution)/shard_map/ppermute | solution.py:471
  123.0 7.7 %collective-permute-start.44 = (bf16[17,32,128]{2,1,0:T(8,128)(2,1)S(1)}, bf16[17,32,128]{2,1,0:T(8,128)(2,1)S(1)}, u32[]{:S(2)}, u32[]{:S(2)}) collective-permute-start(bf16[17,32,128]{2,1,0:T(8,128)(2,1)S(1)} %get-tuple-element.139.refs_3_), channel_id=1, source_target_pairs={{0,8},{4,12},{8,0},{12,4},{16,24},{20,28},{24,16},{28,20},{1,9},{5... | collective-permute-start | bytes 417800 | tf_op jit(solution)/shard_map/ppermute | solution.py:471
  123.1 5.8 %collective-permute-start.42 = (bf16[16,32,128]{2,1,0:T(8,128)(2,1)S(1)}, bf16[16,32,128]{2,1,0:T(8,128)(2,1)S(1)}, u32[]{:S(2)}, u32[]{:S(2)}) collective-permute-start(bf16[16,32,128]{2,1,0:T(8,128)(2,1)S(1)} %get-tuple-element.133), channel_id=1, source_target_pairs={{0,4},{4,0},{8,12},{12,8},{16,20},{20,16},{24,28},{28,24},{1,5},{5... | collective-permute-start | bytes 393224 | tf_op jit(solution)/shard_map/ppermute | solution.py:471
  123.1 7.9 %collective-permute-start.41 = (bf16[16,32,128]{2,1,0:T(8,128)(2,1)S(1)}, bf16[16,32,128]{2,1,0:T(8,128)(2,1)S(1)}, u32[]{:S(2)}, u32[]{:S(2)}) collective-permute-start(bf16[16,32,128]{2,1,0:T(8,128)(2,1)S(1)} %get-tuple-element.131), channel_id=1, source_target_pairs={{0,4},{4,0},{8,12},{12,8},{16,20},{20,16},{24,28},{28,24},{1,5},{5... | collective-permute-start | bytes 393224 | tf_op jit(solution)/shard_map/ppermute | solution.py:471
  125.2 3.7 %collective-permute-start.45 = (f32[8,128]{1,0:T(8,128)S(1)}, f32[8,128]{1,0:T(8,128)S(1)}, u32[]{:S(2)}, u32[]{:S(2)}) collective-permute-start(f32[8,128]{1,0:T(8,128)S(1)} %get-tuple-element.140.refs_9_), channel_id=1, source_target_pairs={{0,2},{1,3},{2,0},{3,1},{4,6},{5,7},{6,4},{7,5},{8,10},{9,11},{10,... | collective-permute-start | bytes 12296 | tf_op jit(solution)/shard_map/ppermute | solution.py:471
  130.9 6.9 %collective-permute-start.47 = (bf16[17,32,128]{2,1,0:T(8,128)(2,1)S(1)}, bf16[17,32,128]{2,1,0:T(8,128)(2,1)S(1)}, u32[]{:S(2)}, u32[]{:S(2)}) collective-permute-start(bf16[17,32,128]{2,1,0:T(8,128)(2,1)S(1)} %fold.16.refs_2_.refs_4_), channel_id=1, source_target_pairs={{0,16},{4,20},{8,24},{12,28},{16,0},{20,4},{24,8},{28,12},{1,17},{... | collective-permute-start | bytes 417800 | tf_op jit(solution)/shard_map/ppermute | solution.py:471
  130.9 5.0 %collective-permute-start.40 = (bf16[16,32,128]{2,1,0:T(8,128)(2,1)S(1)}, bf16[16,32,128]{2,1,0:T(8,128)(2,1)S(1)}, u32[]{:S(2)}, u32[]{:S(2)}) collective-permute-start(bf16[16,32,128]{2,1,0:T(8,128)(2,1)S(1)} %get-tuple-element.129), channel_id=1, source_target_pairs={{0,4},{4,0},{8,12},{12,8},{16,20},{20,16},{24,28},{28,24},{1,5},{5... | collective-permute-start | bytes 393224 | tf_op jit(solution)/shard_map/ppermute | solution.py:471
  131.1 5.1 %collective-permute-start.46 = (bf16[16,32,128]{2,1,0:T(8,128)(2,1)S(1)}, bf16[16,32,128]{2,1,0:T(8,128)(2,1)S(1)}, u32[]{:S(2)}, u32[]{:S(2)}) collective-permute-start(bf16[16,32,128]{2,1,0:T(8,128)(2,1)S(1)} %fold.17), channel_id=1, source_target_pairs={{0,8},{4,12},{8,0},{12,4},{16,24},{20,28},{24,16},{28,20},{1,9},{5... | collective-permute-start | bytes 393224 | tf_op jit(solution)/shard_map/ppermute | solution.py:471

commit v14 on v12

--- a/solution.py
+++ b/solution.py
@@ -15,9 +15,10 @@
 tail_weight = 2.0
 
 MIB = 1024 * 1024
-GROUP = 8
+GROUP = 32
 HEAD_GROUP = 64
 SMALL_VMEM = 6 * MIB
+LOCAL_VMEM = 14 * MIB
 
 
 def contract_last(left, right):
@@ -251,7 +252,7 @@
 def local_adjoint(index, panel, blocks):
     arc_blks, touches, rows, _ = blocks.shape
     scen_rows = panel.shape[1]
-    group = GROUP
+    group = min(GROUP, arc_blks)
     return pl.pallas_call(
         functools.partial(local_adjoint_kernel, touches, group),
         out_shape=(
@@ -270,7 +271,7 @@
                 whole(8, rows),
             ),
         ),
-        compiler_params=params(SMALL_VMEM),
+        compiler_params=params(LOCAL_VMEM),
         cost_estimate=pl.CostEstimate(
             flops=2 * scen_rows * blocks.size, bytes_accessed=2 * blocks.size, transcendentals=0
         ),
@@ -385,7 +386,7 @@
 def local_forward(index, bar, blocks, duals, demand):
     arc_blks, touches, rows, _ = blocks.shape
     scen_rows = bar.shape[0]
-    group = GROUP
+    group = min(GROUP, arc_blks)
     steps = arc_blks // group
     return pl.pallas_call(
         functools.partial(local_forward_kernel, touches, group, steps),
@@ -402,7 +403,7 @@
             out_specs=whole(*duals.shape),
             scratch_shapes=[pltpu.VMEM(duals.shape, jnp.float32)],
         ),
-        compiler_params=params(SMALL_VMEM),
+        compiler_params=params(LOCAL_VMEM),
         cost_estimate=pl.CostEstimate(
             flops=2 * scen_rows * blocks.size, bytes_accessed=2 * blocks.size, transcendentals=0
         ),

time: 138 us -> 138 us (level)
  Pallas kernels: 34.3 us -> 29.9 us
  waiting for transfers between devices: 60 us -> 63.4 us
    ppermute x48, waiting for transfers between devices: 60 us -> 63.4 us  [swap(): return lax.ppermute(value, axis, [(i, i ^ distance) for i in range(size)])]
    pallas_call x3, Pallas kernels: 10 us -> 7.56 us  [local_forward(): pl.pallas_call(functools.partial(local_forward_kernel, touches, group, st...]
    pallas_call x3, Pallas kernels: 12.9 us -> 11.1 us  [local_adjoint(): pl.pallas_call(functools.partial(local_adjoint_kernel, touches, group), o...]
    unnamed x26 -> x24, local copies, waits for them, and re-layouts: 5.01 us -> 5.01 us
  transfers between devices with their start and end apart: 48 -> 48, of which waited for: 36 -> 37; matrix products, arithmetic and copies ran while one was open for 0% -> 0% of each run, Pallas kernels for 17% -> 14%
where the time goes in v14:
time: 138 us
  waiting for transfers between devices  63.4 us (46%)
  starting transfers between devices  37.6 us (27%)
  Pallas kernels  29.9 us (22%)
  local copies, waits for them, and re-layouts  5.05 us (4%)
  between operations  1.65 us (1%)
    ppermute x48, waiting for transfers between devices, swap(): return lax.ppermute(value, axis, [(i, i ^ distance) for i in range(size)])  63.4 us
    ppermute x48, starting transfers between devices, swap(): return lax.ppermute(value, axis, [(i, i ^ distance) for i in range(size)])  37.6 us
    pallas_call x3, Pallas kernels, local_adjoint(): pl.pallas_call(functools.partial(local_adjoint_kernel, touches, group), o...  11.1 us
    pallas_call x3, Pallas kernels, head_step(): pl.pallas_call(functools.partial(head_kernel, group, steps, peers), out_s...  8.59 us
    pallas_call x3, Pallas kernels, local_forward(): pl.pallas_call(functools.partial(local_forward_kernel, touches, group, st...  7.56 us
    unnamed x24, local copies, waits for them, and re-layouts  5.01 us
  transfers between devices with their start and end apart: 48, of which 37 were waited for; matrix products, arithmetic and copies ran while one was open for 0% of the time, Pallas kernels for 14%

profile of v14, /device:TPU:0, one launch (start us, length us, event | category | flops | bytes accessed | tf_op | source)
XLA Modules:
  0.0 137.7 jit_solution(13684391693340019504)
XLA Ops:
  0.7 0.9 copy-done
  1.6 4.1 %collective-permute-start = (bf16[16,32,128]{2,1,0:T(8,128)(2,1)S(1)}, bf16[16,32,128]{2,1,0:T(8,128)(2,1)S(1)}, u32[]{:S(2)}, u32[]{:S(2)}) collective-permute-start(bf16[16,32,128]{2,1,0:T(8,128)(2,1)S(1)} %fusion.panel_ref.refs_0_), channel_id=1, source_target_pairs={{0,16},{4,20},{8,24},{12,28},{16,0},{20,4},{24,8},{28,12},{1,17},{... | collective-permute-start | bytes 393224 | tf_op jit(solution)/shard_map/ppermute | solution.py:467
  5.7 1.5 %collective-permute-start.1 = (bf16[16,32,128]{2,1,0:T(8,128)(2,1)S(1)}, bf16[16,32,128]{2,1,0:T(8,128)(2,1)S(1)}, u32[]{:S(2)}, u32[]{:S(2)}) collective-permute-start(bf16[16,32,128]{2,1,0:T(8,128)(2,1)S(1)} %fusion.panel_ref.refs_0_), channel_id=1, source_target_pairs={{0,4},{4,0},{8,12},{12,8},{16,20},{20,16},{24,28},{28,24},{1,5},{5... | collective-permute-start | bytes 393224 | tf_op jit(solution)/shard_map/ppermute | solution.py:467
  7.2 3.4 %copy-done.1 = bf16[64,4,128,128]{3,2,1,0:T(8,128)(2,1)S(1)} copy-done((bf16[64,4,128,128]{3,2,1,0:T(8,128)(2,1)S(1)}, bf16[64,4,128,128]{3,2,1,0:T(8,128)(2,1)}, u32[]{:S(2)}) %copy-start.1) | copy-done | bytes 8388632
  11.3 3.6 %local_adjoint.3 = (f32[32,8192]{1,0:T(8,128)S(1)}, f32[8,128]{1,0:T(8,128)S(1)}) custom-call(s32[4,64]{1,0:T(4,128)S(1)} %bitcast.29, bf16[16,32,128]{2,1,0:T(8,128)(2,1)S(1)} %fusion.panel_ref.refs_0_, bf16[64,4,128,128]{3,2,1,0:T(8,128)(2,1)S(1)} %copy-done.1), custom_call_target="tpu_custom_call" | custom-call | flops 268435456 | bytes 8388608 | tf_op jit(solution)/shard_map/local_adjoint/pallas_call | solution.py:256
  15.5 1.6 %collective-permute-start.5 = (bf16[16,32,128]{2,1,0:T(8,128)(2,1)S(1)}, bf16[16,32,128]{2,1,0:T(8,128)(2,1)S(1)}, u32[]{:S(2)}, u32[]{:S(2)}) collective-permute-start(bf16[16,32,128]{2,1,0:T(8,128)(2,1)S(1)} %get-tuple-element.77.refs_0_.refs_4_), channel_id=1, source_target_pairs={{0,8},{4,12},{8,0},{12,4},{16,24},{20,28},{24,16},{28,20},{1,9},{5... | collective-permute-start | bytes 393224 | tf_op jit(solution)/shard_map/ppermute | solution.py:467
  18.1 1.6 %collective-permute-start.3 = (bf16[16,32,128]{2,1,0:T(8,128)(2,1)S(1)}, bf16[16,32,128]{2,1,0:T(8,128)(2,1)S(1)}, u32[]{:S(2)}, u32[]{:S(2)}) collective-permute-start(bf16[16,32,128]{2,1,0:T(8,128)(2,1)S(1)} %collective-permute-done.1.refs_1_), channel_id=1, source_target_pairs={{0,8},{4,12},{8,0},{12,4},{16,24},{20,28},{24,16},{28,20},{1,9},{5... | collective-permute-start | bytes 393224 | tf_op jit(solution)/shard_map/ppermute | solution.py:467
  19.7 2.3 %collective-permute-done.5.refs_6_ = bf16[16,32,128]{2,1,0:T(8,128)(2,1)S(1)} collective-permute-done((bf16[16,32,128]{2,1,0:T(8,128)(2,1)S(1)}, bf16[16,32,128]{2,1,0:T(8,128)(2,1)S(1)}, u32[]{:S(2)}, u32[]{:S(2)}) %collective-permute-start.5) | collective-permute-done | bytes 131104 | tf_op jit(solution)/shard_map/ppermute | solution.py:467
  23.4 1.0 collective-permute-done.2.refs_2_
  24.6 1.3 collective-permute-done.3.refs_3_
  25.8 1.1 collective-permute-done.6.refs_7_
  27.0 2.6 %head_step.3 = (f32[32,8192]{1,0:T(8,128)S(1)}, bf16[32,8192]{1,0:T(8,128)(2,1)S(1)}, f32[8,128]{1,0:T(8,128)S(1)}, f32[16,32,128]{2,1,0:T(8,128)S(1)}, f32[16,3...) custom-call(s32[64]{0:T(128)S(1)} %bitcast.35, ...), custom_call_target="tpu_custom_call" | custom-call | flops 134217728 | bytes 7864320 | tf_op jit(solution)/shard_map/head_step/pallas_call | solution.py:293
  30.2 2.5 %local_forward.3.refs_4_.refs_5_ = f32[16,32,128]{2,1,0:T(8,128)S(1)} custom-call(s32[4,64]{1,0:T(4,128)S(1)} %bitcast.30, bf16[32,8192]{1,0:T(8,128)(2,1)S(1)} %get-tuple-element.90.bar_ref, bf16[64,4,128,128]{3,2,1,0:T(8,128)(2,1)S(1)} %bitcast.25, f32[16,32,128]{2,1,0:T(8,128)S(1)} %bitcast_bitcast_fusion.duals_ref, f32[32,2048]{1,0:T(8,128)S(1)} %copy-done.4), custom_call_target="tpu_custom_call" | custom-call | flops 268435456 | bytes 8388608 | tf_op jit(solution)/shard_map/local_forward/pallas_call | solution.py:391
  32.7 1.9 %collective-permute-done.10.refs_1_ = bf16[17,32,128]{2,1,0:T(8,128)(2,1)S(1)} collective-permute-done((bf16[17,32,128]{2,1,0:T(8,128)(2,1)S(1)}, bf16[17,32,128]{2,1,0:T(8,128)(2,1)S(1)}, u32[]{:S(2)}, u32[]{:S(2)}) %collective-permute-start.10) | collective-permute-done | bytes 139296 | tf_op jit(solution)/shard_map/ppermute | solution.py:467
  34.8 2.0 %collective-permute-start.11 = (bf16[17,32,128]{2,1,0:T(8,128)(2,1)S(1)}, bf16[17,32,128]{2,1,0:T(8,128)(2,1)S(1)}, u32[]{:S(2)}, u32[]{:S(2)}) collective-permute-start(bf16[17,32,128]{2,1,0:T(8,128)(2,1)S(1)} %get-tuple-element.91.refs_3_), channel_id=1, source_target_pairs={{0,8},{4,12},{8,0},{12,4},{16,24},{20,28},{24,16},{28,20},{1,9},{5... | collective-permute-start | bytes 417800 | tf_op jit(solution)/shard_map/ppermute | solution.py:467
  37.4 1.5 %collective-permute-start.12 = (f32[8,128]{1,0:T(8,128)S(1)}, f32[8,128]{1,0:T(8,128)S(1)}, u32[]{:S(2)}, u32[]{:S(2)}) collective-permute-start(f32[8,128]{1,0:T(8,128)S(1)} %get-tuple-element.92.refs_9_), channel_id=1, source_target_pairs={{0,2},{1,3},{2,0},{3,1},{4,6},{5,7},{6,4},{7,5},{8,10},{9,11},{10,... | collective-permute-start | bytes 12296 | tf_op jit(solution)/shard_map/ppermute | solution.py:467
  38.9 3.5 %collective-permute-done.9.refs_1_ = bf16[16,32,128]{2,1,0:T(8,128)(2,1)S(1)} collective-permute-done((bf16[16,32,128]{2,1,0:T(8,128)(2,1)S(1)}, bf16[16,32,128]{2,1,0:T(8,128)(2,1)S(1)}, u32[]{:S(2)}, u32[]{:S(2)}) %collective-permute-start.9) | collective-permute-done | bytes 131104 | tf_op jit(solution)/shard_map/ppermute | solution.py:467
  42.6 1.0 collective-permute-start.14
  44.2 1.4 %collective-permute-start.13 = (bf16[16,32,128]{2,1,0:T(8,128)(2,1)S(1)}, bf16[16,32,128]{2,1,0:T(8,128)(2,1)S(1)}, u32[]{:S(2)}, u32[]{:S(2)}) collective-permute-start(bf16[16,32,128]{2,1,0:T(8,128)(2,1)S(1)} %fold.11), channel_id=1, source_target_pairs={{0,4},{4,0},{8,12},{12,8},{16,20},{20,16},{24,28},{28,24},{1,5},{5... | collective-permute-start | bytes 393224 | tf_op jit(solution)/shard_map/ppermute | solution.py:467
  45.6 2.5 %collective-permute-done.14.refs_2_ = bf16[16,32,128]{2,1,0:T(8,128)(2,1)S(1)} collective-permute-done((bf16[16,32,128]{2,1,0:T(8,128)(2,1)S(1)}, bf16[16,32,128]{2,1,0:T(8,128)(2,1)S(1)}, u32[]{:S(2)}, u32[]{:S(2)}) %collective-permute-start.14) | collective-permute-done | bytes 131104 | tf_op jit(solution)/shard_map/ppermute | solution.py:467
  48.1 2.4 %collective-permute-done.13.refs_1_ = bf16[16,32,128]{2,1,0:T(8,128)(2,1)S(1)} collective-permute-done((bf16[16,32,128]{2,1,0:T(8,128)(2,1)S(1)}, bf16[16,32,128]{2,1,0:T(8,128)(2,1)S(1)}, u32[]{:S(2)}, u32[]{:S(2)}) %collective-permute-start.13) | collective-permute-done | bytes 131104 | tf_op jit(solution)/shard_map/ppermute | solution.py:467
  50.5 2.0 %collective-permute-done.15.refs_3_ = bf16[17,32,128]{2,1,0:T(8,128)(2,1)S(1)} collective-permute-done((bf16[17,32,128]{2,1,0:T(8,128)(2,1)S(1)}, bf16[17,32,128]{2,1,0:T(8,128)(2,1)S(1)}, u32[]{:S(2)}, u32[]{:S(2)}) %collective-permute-start.15) | collective-permute-done | bytes 139296 | tf_op jit(solution)/shard_map/ppermute | solution.py:467
  52.8 0.9 collective-permute-start.16
  53.7 3.6 %local_adjoint.4 = (f32[32,8192]{1,0:T(8,128)S(1)}, f32[8,128]{1,0:T(8,128)S(1)}) custom-call(s32[4,64]{1,0:T(4,128)S(1)} %bitcast.31, bf16[16,32,128]{2,1,0:T(8,128)(2,1)S(1)} %get-tuple-element.96.panel_ref.refs_0_, bf16[64,4,128,128]{3,2,1,0:T(8,128)(2,1)S(1)} %bitcast.25), custom_call_target="tpu_custom_call" | custom-call | flops 268435456 | bytes 8388608 | tf_op jit(solution)/shard_map/local_adjoint/pallas_call | solution.py:256
  57.3 2.1 %collective-permute-done.19.arrived_ref = bf16[16,32,128]{2,1,0:T(8,128)(2,1)S(1)} collective-permute-done((bf16[16,32,128]{2,1,0:T(8,128)(2,1)S(1)}, bf16[16,32,128]{2,1,0:T(8,128)(2,1)S(1)}, u32[]{:S(2)}, u32[]{:S(2)}) %collective-permute-start.19) | collective-permute-done | bytes 131104 | tf_op jit(solution)/shard_map/ppermute | solution.py:467
  59.5 2.0 %collective-permute-start.17 = (bf16[16,32,128]{2,1,0:T(8,128)(2,1)S(1)}, bf16[16,32,128]{2,1,0:T(8,128)(2,1)S(1)}, u32[]{:S(2)}, u32[]{:S(2)}) collective-permute-start(bf16[16,32,128]{2,1,0:T(8,128)(2,1)S(1)} %get-tuple-element.96.panel_ref.refs_0_), channel_id=1, source_target_pairs={{0,8},{4,12},{8,0},{12,4},{16,24},{20,28},{24,16},{28,20},{1,9},{5... | collective-permute-start | bytes 393224 | tf_op jit(solution)/shard_map/ppermute | solution.py:467
  61.9 2.6 %collective-permute-done.21.refs_6_ = bf16[16,32,128]{2,1,0:T(8,128)(2,1)S(1)} collective-permute-done((bf16[16,32,128]{2,1,0:T(8,128)(2,1)S(1)}, bf16[16,32,128]{2,1,0:T(8,128)(2,1)S(1)}, u32[]{:S(2)}, u32[]{:S(2)}) %collective-permute-start.21) | collective-permute-done | bytes 131104 | tf_op jit(solution)/shard_map/ppermute | solution.py:467
  64.5 1.4 %collective-permute-done.17.refs_2_ = bf16[16,32,128]{2,1,0:T(8,128)(2,1)S(1)} collective-permute-done((bf16[16,32,128]{2,1,0:T(8,128)(2,1)S(1)}, bf16[16,32,128]{2,1,0:T(8,128)(2,1)S(1)}, u32[]{:S(2)}, u32[]{:S(2)}) %collective-permute-start.17) | collective-permute-done | bytes 131104 | tf_op jit(solution)/shard_map/ppermute | solution.py:467
  65.9 1.4 %collective-permute-done.18.refs_3_ = bf16[16,32,128]{2,1,0:T(8,128)(2,1)S(1)} collective-permute-done((bf16[16,32,128]{2,1,0:T(8,128)(2,1)S(1)}, bf16[16,32,128]{2,1,0:T(8,128)(2,1)S(1)}, u32[]{:S(2)}, u32[]{:S(2)}) %collective-permute-start.18) | collective-permute-done | bytes 131104 | tf_op jit(solution)/shard_map/ppermute | solution.py:467
  67.3 2.2 %collective-permute-done.22.refs_7_ = bf16[16,32,128]{2,1,0:T(8,128)(2,1)S(1)} collective-permute-done((bf16[16,32,128]{2,1,0:T(8,128)(2,1)S(1)}, bf16[16,32,128]{2,1,0:T(8,128)(2,1)S(1)}, u32[]{:S(2)}, u32[]{:S(2)}) %collective-permute-start.22) | collective-permute-done | bytes 131104 | tf_op jit(solution)/shard_map/ppermute | solution.py:467
  69.4 2.6 %head_step.4 = (f32[32,8192]{1,0:T(8,128)S(1)}, bf16[32,8192]{1,0:T(8,128)(2,1)S(1)}, f32[8,128]{1,0:T(8,128)S(1)}, f32[16,32,128]{2,1,0:T(8,128)S(1)}, f32[16,3...) custom-call(s32[64]{0:T(128)S(1)} %bitcast.36, ...), custom_call_target="tpu_custom_call" | custom-call | flops 134217728 | bytes 7864320 | tf_op jit(solution)/shard_map/head_step/pallas_call | solution.py:293
  72.1 2.5 %local_forward.4.refs_4_.refs_5_ = f32[16,32,128]{2,1,0:T(8,128)S(1)} custom-call(s32[4,64]{1,0:T(4,128)S(1)} %bitcast.32, bf16[32,8192]{1,0:T(8,128)(2,1)S(1)} %get-tuple-element.112.bar_ref, bf16[64,4,128,128]{3,2,1,0:T(8,128)(2,1)S(1)} %bitcast.25, f32[16,32,128]{2,1,0:T(8,128)S(1)} %get-tuple-element.113.duals_ref, f32[32,2048]{1,0:T(8,128)S(1)} %copy-done.4), custom_call_target="tpu_custom_call" | custom-call | flops 268435456 | bytes 8388608 | tf_op jit(solution)/shard_map/local_forward/pallas_call | solution.py:391
  74.6 3.7 %collective-permute-done.26.refs_1_ = bf16[17,32,128]{2,1,0:T(8,128)(2,1)S(1)} collective-permute-done((bf16[17,32,128]{2,1,0:T(8,128)(2,1)S(1)}, bf16[17,32,128]{2,1,0:T(8,128)(2,1)S(1)}, u32[]{:S(2)}, u32[]{:S(2)}) %collective-permute-start.26) | collective-permute-done | bytes 139296 | tf_op jit(solution)/shard_map/ppermute | solution.py:467
  78.6 2.0 %collective-permute-start.24 = (bf16[16,32,128]{2,1,0:T(8,128)(2,1)S(1)}, bf16[16,32,128]{2,1,0:T(8,128)(2,1)S(1)}, u32[]{:S(2)}, u32[]{:S(2)}) collective-permute-start(bf16[16,32,128]{2,1,0:T(8,128)(2,1)S(1)} %get-tuple-element.106), channel_id=1, source_target_pairs={{0,8},{4,12},{8,0},{12,4},{16,24},{20,28},{24,16},{28,20},{1,9},{5... | collective-permute-start | bytes 393224 | tf_op jit(solution)/shard_map/ppermute | solution.py:467
  80.5 1.5 %collective-permute-start.28 = (f32[8,128]{1,0:T(8,128)S(1)}, f32[8,128]{1,0:T(8,128)S(1)}, u32[]{:S(2)}, u32[]{:S(2)}) collective-permute-start(f32[8,128]{1,0:T(8,128)S(1)} %get-tuple-element.115.refs_9_), channel_id=1, source_target_pairs={{0,2},{1,3},{2,0},{3,1},{4,6},{5,7},{6,4},{7,5},{8,10},{9,11},{10,... | collective-permute-start | bytes 12296 | tf_op jit(solution)/shard_map/ppermute | solution.py:467
  82.0 2.6 %collective-permute-done.25.refs_1_ = bf16[16,32,128]{2,1,0:T(8,128)(2,1)S(1)} collective-permute-done((bf16[16,32,128]{2,1,0:T(8,128)(2,1)S(1)}, bf16[16,32,128]{2,1,0:T(8,128)(2,1)S(1)}, u32[]{:S(2)}, u32[]{:S(2)}) %collective-permute-start.25) | collective-permute-done | bytes 131104 | tf_op jit(solution)/shard_map/ppermute | solution.py:467
  84.6 1.2 collective-permute-done.27.refs_2_
  86.4 0.9 collective-permute-done.24.refs_1_
  87.7 4.0 %collective-permute-done.30.refs_2_ = bf16[16,32,128]{2,1,0:T(8,128)(2,1)S(1)} collective-permute-done((bf16[16,32,128]{2,1,0:T(8,128)(2,1)S(1)}, bf16[16,32,128]{2,1,0:T(8,128)(2,1)S(1)}, u32[]{:S(2)}, u32[]{:S(2)}) %collective-permute-start.30) | collective-permute-done | bytes 131104 | tf_op jit(solution)/shard_map/ppermute | solution.py:467
  91.7 1.2 collective-permute-done.29.refs_1_
  92.9 1.9 %collective-permute-done.31.refs_3_ = bf16[17,32,128]{2,1,0:T(8,128)(2,1)S(1)} collective-permute-done((bf16[17,32,128]{2,1,0:T(8,128)(2,1)S(1)}, bf16[17,32,128]{2,1,0:T(8,128)(2,1)S(1)}, u32[]{:S(2)}, u32[]{:S(2)}) %collective-permute-start.31) | collective-permute-done | bytes 139296 | tf_op jit(solution)/shard_map/ppermute | solution.py:467
  95.3 0.9 collective-permute-start.32
  96.3 3.8 %local_adjoint.5 = (f32[32,8192]{1,0:T(8,128)S(1)}, f32[8,128]{1,0:T(8,128)S(1)}) custom-call(s32[4,64]{1,0:T(4,128)S(1)} %bitcast.33, bf16[16,32,128]{2,1,0:T(8,128)(2,1)S(1)} %get-tuple-element.119.panel_ref.refs_0_, bf16[64,4,128,128]{3,2,1,0:T(8,128)(2,1)S(1)} %bitcast.25), custom_call_target="tpu_custom_call" | custom-call | flops 268435456 | bytes 8388608 | tf_op jit(solution)/shard_map/local_adjoint/pallas_call | solution.py:256
  100.1 1.6 %collective-permute-done.35.arrived_ref = bf16[16,32,128]{2,1,0:T(8,128)(2,1)S(1)} collective-permute-done((bf16[16,32,128]{2,1,0:T(8,128)(2,1)S(1)}, bf16[16,32,128]{2,1,0:T(8,128)(2,1)S(1)}, u32[]{:S(2)}, u32[]{:S(2)}) %collective-permute-start.35) | collective-permute-done | bytes 131104 | tf_op jit(solution)/shard_map/ppermute | solution.py:467
  101.8 2.0 %collective-permute-start.33 = (bf16[16,32,128]{2,1,0:T(8,128)(2,1)S(1)}, bf16[16,32,128]{2,1,0:T(8,128)(2,1)S(1)}, u32[]{:S(2)}, u32[]{:S(2)}) collective-permute-start(bf16[16,32,128]{2,1,0:T(8,128)(2,1)S(1)} %get-tuple-element.119.panel_ref.refs_0_), channel_id=1, source_target_pairs={{0,8},{4,12},{8,0},{12,4},{16,24},{20,28},{24,16},{28,20},{1,9},{5... | collective-permute-start | bytes 393224 | tf_op jit(solution)/shard_map/ppermute | solution.py:467
  103.8 0.9 collective-permute-start.36
  104.8 2.0 %collective-permute-done.37.refs_6_ = bf16[16,32,128]{2,1,0:T(8,128)(2,1)S(1)} collective-permute-done((bf16[16,32,128]{2,1,0:T(8,128)(2,1)S(1)}, bf16[16,32,128]{2,1,0:T(8,128)(2,1)S(1)}, u32[]{:S(2)}, u32[]{:S(2)}) %collective-permute-start.37) | collective-permute-done | bytes 131104 | tf_op jit(solution)/shard_map/ppermute | solution.py:467
  106.8 0.9 collective-permute-start.38
  108.8 0.9 collective-permute-done.34.refs_3_
  109.7 2.0 %collective-permute-done.38.refs_7_ = bf16[16,32,128]{2,1,0:T(8,128)(2,1)S(1)} collective-permute-done((bf16[16,32,128]{2,1,0:T(8,128)(2,1)S(1)}, bf16[16,32,128]{2,1,0:T(8,128)(2,1)S(1)}, u32[]{:S(2)}, u32[]{:S(2)}) %collective-permute-start.38) | collective-permute-done | bytes 131104 | tf_op jit(solution)/shard_map/ppermute | solution.py:467
  111.7 3.4 %head_step.5 = (f32[32,8192]{1,0:T(8,128)}, bf16[32,8192]{1,0:T(8,128)(2,1)S(1)}, f32[8,128]{1,0:T(8,128)S(1)}, f32[16,32,128]{2,1,0:T(8,128)S(1)}, f32[16,32,12...) custom-call(s32[64]{0:T(128)S(1)} %bitcast.37, ...), custom_call_target="tpu_custom_call" | custom-call | flops 134217728 | bytes 7864320 | tf_op jit(solution)/shard_map/head_step/pallas_call | solution.py:293
  115.1 0.9 collective-permute-start.42
  116.1 2.5 %local_forward.5.refs_4_.refs_5_ = f32[16,32,128]{2,1,0:T(8,128)S(1)} custom-call(s32[4,64]{1,0:T(4,128)S(1)} %bitcast.34, bf16[32,8192]{1,0:T(8,128)(2,1)S(1)} %get-tuple-element.136.bar_ref, bf16[64,4,128,128]{3,2,1,0:T(8,128)(2,1)S(1)} %bitcast.25, f32[16,32,128]{2,1,0:T(8,128)S(1)} %get-tuple-element.137.duals_ref, f32[32,2048]{1,0:T(8,128)S(1)} %copy-done.4), custom_call_target="tpu_custom_call" | custom-call | flops 268435456 | bytes 8388608 | tf_op jit(solution)/shard_map/local_forward/pallas_call | solution.py:391
  118.6 2.7 %collective-permute-done.42.refs_1_ = bf16[17,32,128]{2,1,0:T(8,128)(2,1)S(1)} collective-permute-done((bf16[17,32,128]{2,1,0:T(8,128)(2,1)S(1)}, bf16[17,32,128]{2,1,0:T(8,128)(2,1)S(1)}, u32[]{:S(2)}, u32[]{:S(2)}) %collective-permute-start.42) | collective-permute-done | bytes 139296 | tf_op jit(solution)/shard_map/ppermute | solution.py:467
  121.5 0.7 collective-permute-start.41
  122.2 1.9 %collective-permute-start.40 = (bf16[16,32,128]{2,1,0:T(8,128)(2,1)S(1)}, bf16[16,32,128]{2,1,0:T(8,128)(2,1)S(1)}, u32[]{:S(2)}, u32[]{:S(2)}) collective-permute-start(bf16[16,32,128]{2,1,0:T(8,128)(2,1)S(1)} %get-tuple-element.130), channel_id=1, source_target_pairs={{0,8},{4,12},{8,0},{12,4},{16,24},{20,28},{24,16},{28,20},{1,9},{5... | collective-permute-start | bytes 393224 | tf_op jit(solution)/shard_map/ppermute | solution.py:467
  124.1 1.9 %collective-permute-start.44 = (f32[8,128]{1,0:T(8,128)S(1)}, f32[8,128]{1,0:T(8,128)S(1)}, u32[]{:S(2)}, u32[]{:S(2)}) collective-permute-start(f32[8,128]{1,0:T(8,128)S(1)} %get-tuple-element.139.refs_9_), channel_id=1, source_target_pairs={{0,2},{1,3},{2,0},{3,1},{4,6},{5,7},{6,4},{7,5},{8,10},{9,11},{10,... | collective-permute-start | bytes 12296 | tf_op jit(solution)/shard_map/ppermute | solution.py:467
  126.1 1.3 collective-permute-done.41.refs_1_
  127.8 1.6 %collective-permute-done.43.refs_2_ = bf16[17,32,128]{2,1,0:T(8,128)(2,1)S(1)} collective-permute-done((bf16[17,32,128]{2,1,0:T(8,128)(2,1)S(1)}, bf16[17,32,128]{2,1,0:T(8,128)(2,1)S(1)}, u32[]{:S(2)}, u32[]{:S(2)}) %collective-permute-start.43) | collective-permute-done | bytes 139296 | tf_op jit(solution)/shard_map/ppermute | solution.py:467
  130.8 0.7 collective-permute-start.45
  131.6 3.1 %collective-permute-done.46.refs_2_ = bf16[16,32,128]{2,1,0:T(8,128)(2,1)S(1)} collective-permute-done((bf16[16,32,128]{2,1,0:T(8,128)(2,1)S(1)}, bf16[16,32,128]{2,1,0:T(8,128)(2,1)S(1)}, u32[]{:S(2)}, u32[]{:S(2)}) %collective-permute-start.46) | collective-permute-done | bytes 131104 | tf_op jit(solution)/shard_map/ppermute | solution.py:467
  134.6 1.3 collective-permute-done.45.refs_1_
  135.9 1.0 collective-permute-done.47.refs_3_
  136.9 0.8 settle.5
  (84 shorter events, 11.2 us)
Async XLA Ops:
  0.6 1.0 copy-start
  0.6 22.5 %copy-start.9 = (s32[64]{0:T(128)S(1)}, s32[64]{0:T(128)}, u32[]{:S(2)}) copy-start(s32[64]{0:T(128)} %param.21) | copy-start | bytes 772
  0.7 22.5 %copy-start.7 = (f32[32]{0:T(128)S(1)}, f32[32]{0:T(128)}, u32[]{:S(2)}) copy-start(f32[32]{0:T(128)} %param.15) | copy-start | bytes 388
  0.7 22.5 %copy-start.8 = (f32[32]{0:T(128)S(1)}, f32[32]{0:T(128)}, u32[]{:S(2)}) copy-start(f32[32]{0:T(128)} %param.14) | copy-start | bytes 388
  0.7 26.3 %copy-start.5 = (f32[8192]{0:T(1024)S(1)}, f32[8192]{0:T(1024)}, u32[]{:S(2)}) copy-start(f32[8192]{0:T(1024)} %param.17) | copy-start | bytes 98308
  1.6 13.3 %collective-permute-start = (bf16[16,32,128]{2,1,0:T(8,128)(2,1)S(1)}, bf16[16,32,128]{2,1,0:T(8,128)(2,1)S(1)}, u32[]{:S(2)}, u32[]{:S(2)}) collective-permute-start(bf16[16,32,128]{2,1,0:T(8,128)(2,1)S(1)} %fusion.panel_ref.refs_0_), channel_id=1, source_target_pairs={{0,16},{4,20},{8,24},{12,28},{16,0},{20,4},{24,8},{28,12},{1,17},{... | collective-permute-start | bytes 393224 | tf_op jit(solution)/shard_map/ppermute | solution.py:467
  5.7 12.4 %collective-permute-start.1 = (bf16[16,32,128]{2,1,0:T(8,128)(2,1)S(1)}, bf16[16,32,128]{2,1,0:T(8,128)(2,1)S(1)}, u32[]{:S(2)}, u32[]{:S(2)}) collective-permute-start(bf16[16,32,128]{2,1,0:T(8,128)(2,1)S(1)} %fusion.panel_ref.refs_0_), channel_id=1, source_target_pairs={{0,4},{4,0},{8,12},{12,8},{16,20},{20,16},{24,28},{28,24},{1,5},{5... | collective-permute-start | bytes 393224 | tf_op jit(solution)/shard_map/ppermute | solution.py:467
  7.2 3.4 %copy-start.1 = (bf16[64,4,128,128]{3,2,1,0:T(8,128)(2,1)S(1)}, bf16[64,4,128,128]{3,2,1,0:T(8,128)(2,1)}, u32[]{:S(2)}) copy-start(bf16[64,4,128,128]{3,2,1,0:T(8,128)(2,1)} %blocks_ref.11) | copy-start | bytes 25165828
  10.6 0.7 copy-start.6
  11.3 11.9 %copy-start.2 = (bf16[64,128,128]{2,1,0:T(8,128)(2,1)S(1)}, bf16[64,128,128]{2,1,0:T(8,128)(2,1)}, u32[]{:S(2)}) copy-start(bf16[64,128,128]{2,1,0:T(8,128)(2,1)} %refs_8_.5) | copy-start | bytes 6291460
  11.3 11.9 %copy-start.3 = (f32[32,8192]{1,0:T(8,128)S(1)}, f32[32,8192]{1,0:T(8,128)}, u32[]{:S(2)}) copy-start(f32[32,8192]{1,0:T(8,128)} %refs_10_.1) | copy-start | bytes 3145732
  11.3 18.9 %slice-start = ((s8[8388608]{0:T(1024)(128)(4,1)}), s8[4194304]{0:T(1024)(128)(4,1)S(1)}, s32[]{:S(2)}) async-start(s8[8388608]{0:T(1024)(128)(4,1)} %bitcast.24), calls=%async_computation | async-start | bytes 8388608
  11.3 18.9 %copy-start.4 = (f32[32,2048]{1,0:T(8,128)S(1)}, f32[32,2048]{1,0:T(8,128)}, u32[]{:S(2)}) copy-start(f32[32,2048]{1,0:T(8,128)} %demand_ref.5) | copy-start | bytes 786436
  15.5 6.4 %collective-permute-start.5 = (bf16[16,32,128]{2,1,0:T(8,128)(2,1)S(1)}, bf16[16,32,128]{2,1,0:T(8,128)(2,1)S(1)}, u32[]{:S(2)}, u32[]{:S(2)}) collective-permute-start(bf16[16,32,128]{2,1,0:T(8,128)(2,1)S(1)} %get-tuple-element.77.refs_0_.refs_4_), channel_id=1, source_target_pairs={{0,8},{4,12},{8,0},{12,4},{16,24},{20,28},{24,16},{28,20},{1,9},{5... | collective-permute-start | bytes 393224 | tf_op jit(solution)/shard_map/ppermute | solution.py:467
  17.1 7.3 %collective-permute-start.2 = (bf16[16,32,128]{2,1,0:T(8,128)(2,1)S(1)}, bf16[16,32,128]{2,1,0:T(8,128)(2,1)S(1)}, u32[]{:S(2)}, u32[]{:S(2)}) collective-permute-start(bf16[16,32,128]{2,1,0:T(8,128)(2,1)S(1)} %fusion.panel_ref.refs_0_), channel_id=1, source_target_pairs={{0,8},{4,12},{8,0},{12,4},{16,24},{20,28},{24,16},{28,20},{1,9},{5... | collective-permute-start | bytes 393224 | tf_op jit(solution)/shard_map/ppermute | solution.py:467
  17.6 8.3 %collective-permute-start.4 = (bf16[16,32,128]{2,1,0:T(8,128)(2,1)S(1)}, bf16[16,32,128]{2,1,0:T(8,128)(2,1)S(1)}, u32[]{:S(2)}, u32[]{:S(2)}) collective-permute-start(bf16[16,32,128]{2,1,0:T(8,128)(2,1)S(1)} %get-tuple-element.77.refs_0_.refs_4_), channel_id=1, source_target_pairs={{0,4},{4,0},{8,12},{12,8},{16,20},{20,16},{24,28},{28,24},{1,5},{5... | collective-permute-start | bytes 393224 | tf_op jit(solution)/shard_map/ppermute | solution.py:467
  18.1 7.7 %collective-permute-start.3 = (bf16[16,32,128]{2,1,0:T(8,128)(2,1)S(1)}, bf16[16,32,128]{2,1,0:T(8,128)(2,1)S(1)}, u32[]{:S(2)}, u32[]{:S(2)}) collective-permute-start(bf16[16,32,128]{2,1,0:T(8,128)(2,1)S(1)} %collective-permute-done.1.refs_1_), channel_id=1, source_target_pairs={{0,8},{4,12},{8,0},{12,4},{16,24},{20,28},{24,16},{28,20},{1,9},{5... | collective-permute-start | bytes 393224 | tf_op jit(solution)/shard_map/ppermute | solution.py:467
  22.0 5.0 %collective-permute-start.6 = (bf16[16,32,128]{2,1,0:T(8,128)(2,1)S(1)}, bf16[16,32,128]{2,1,0:T(8,128)(2,1)S(1)}, u32[]{:S(2)}, u32[]{:S(2)}) collective-permute-start(bf16[16,32,128]{2,1,0:T(8,128)(2,1)S(1)} %collective-permute-done.5.refs_6_), channel_id=1, source_target_pairs={{0,4},{4,0},{8,12},{12,8},{16,20},{20,16},{24,28},{28,24},{1,5},{5... | collective-permute-start | bytes 393224 | tf_op jit(solution)/shard_map/ppermute | solution.py:467
  23.2 7.0 %slice-start.1 = ((s8[8388608]{0:T(1024)(128)(4,1)}), s8[4194304]{0:T(1024)(128)(4,1)S(1)}, s32[]{:S(2)}) async-start(s8[8388608]{0:T(1024)(128)(4,1)} %bitcast.24), calls=%async_computation.1 | async-start | bytes 8388608
  23.3 1.2 collective-permute-start.7
  29.5 5.1 %collective-permute-start.10 = (bf16[17,32,128]{2,1,0:T(8,128)(2,1)S(1)}, bf16[17,32,128]{2,1,0:T(8,128)(2,1)S(1)}, u32[]{:S(2)}, u32[]{:S(2)}) collective-permute-start(bf16[17,32,128]{2,1,0:T(8,128)(2,1)S(1)} %get-tuple-element.88.refs_2_), channel_id=1, source_target_pairs={{0,4},{4,0},{8,12},{12,8},{16,20},{20,16},{24,28},{28,24},{1,5},{5... | collective-permute-start | bytes 417800 | tf_op jit(solution)/shard_map/ppermute | solution.py:467
  34.8 7.6 %collective-permute-start.11 = (bf16[17,32,128]{2,1,0:T(8,128)(2,1)S(1)}, bf16[17,32,128]{2,1,0:T(8,128)(2,1)S(1)}, u32[]{:S(2)}, u32[]{:S(2)}) collective-permute-start(bf16[17,32,128]{2,1,0:T(8,128)(2,1)S(1)} %get-tuple-element.91.refs_3_), channel_id=1, source_target_pairs={{0,8},{4,12},{8,0},{12,4},{16,24},{20,28},{24,16},{28,20},{1,9},{5... | collective-permute-start | bytes 417800 | tf_op jit(solution)/shard_map/ppermute | solution.py:467
  36.8 5.6 %collective-permute-start.9 = (bf16[16,32,128]{2,1,0:T(8,128)(2,1)S(1)}, bf16[16,32,128]{2,1,0:T(8,128)(2,1)S(1)}, u32[]{:S(2)}, u32[]{:S(2)}) collective-permute-start(bf16[16,32,128]{2,1,0:T(8,128)(2,1)S(1)} %get-tuple-element.86), channel_id=1, source_target_pairs={{0,4},{4,0},{8,12},{12,8},{16,20},{20,16},{24,28},{28,24},{1,5},{5... | collective-permute-start | bytes 393224 | tf_op jit(solution)/shard_map/ppermute | solution.py:467
  37.0 7.2 %collective-permute-start.8 = (bf16[16,32,128]{2,1,0:T(8,128)(2,1)S(1)}, bf16[16,32,128]{2,1,0:T(8,128)(2,1)S(1)}, u32[]{:S(2)}, u32[]{:S(2)}) collective-permute-start(bf16[16,32,128]{2,1,0:T(8,128)(2,1)S(1)} %get-tuple-element.84), channel_id=1, source_target_pairs={{0,8},{4,12},{8,0},{12,4},{16,24},{20,28},{24,16},{28,20},{1,9},{5... | collective-permute-start | bytes 393224 | tf_op jit(solution)/shard_map/ppermute | solution.py:467
  37.4 5.0 %collective-permute-start.12 = (f32[8,128]{1,0:T(8,128)S(1)}, f32[8,128]{1,0:T(8,128)S(1)}, u32[]{:S(2)}, u32[]{:S(2)}) collective-permute-start(f32[8,128]{1,0:T(8,128)S(1)} %get-tuple-element.92.refs_9_), channel_id=1, source_target_pairs={{0,2},{1,3},{2,0},{3,1},{4,6},{5,7},{6,4},{7,5},{8,10},{9,11},{10,... | collective-permute-start | bytes 12296 | tf_op jit(solution)/shard_map/ppermute | solution.py:467
  42.5 10.0 %collective-permute-start.15 = (bf16[17,32,128]{2,1,0:T(8,128)(2,1)S(1)}, bf16[17,32,128]{2,1,0:T(8,128)(2,1)S(1)}, u32[]{:S(2)}, u32[]{:S(2)}) collective-permute-start(bf16[17,32,128]{2,1,0:T(8,128)(2,1)S(1)} %fold.10.refs_2_.refs_4_), channel_id=1, source_target_pairs={{0,16},{4,20},{8,24},{12,28},{16,0},{20,4},{24,8},{28,12},{1,17},{... | collective-permute-start | bytes 417800 | tf_op jit(solution)/shard_map/ppermute | solution.py:467
  42.6 5.5 %collective-permute-start.14 = (bf16[16,32,128]{2,1,0:T(8,128)(2,1)S(1)}, bf16[16,32,128]{2,1,0:T(8,128)(2,1)S(1)}, u32[]{:S(2)}, u32[]{:S(2)}) collective-permute-start(bf16[16,32,128]{2,1,0:T(8,128)(2,1)S(1)} %get-tuple-element.93), channel_id=1, source_target_pairs={{0,8},{4,12},{8,0},{12,4},{16,24},{20,28},{24,16},{28,20},{1,9},{5... | collective-permute-start | bytes 393224 | tf_op jit(solution)/shard_map/ppermute | solution.py:467
  44.2 6.2 %collective-permute-start.13 = (bf16[16,32,128]{2,1,0:T(8,128)(2,1)S(1)}, bf16[16,32,128]{2,1,0:T(8,128)(2,1)S(1)}, u32[]{:S(2)}, u32[]{:S(2)}) collective-permute-start(bf16[16,32,128]{2,1,0:T(8,128)(2,1)S(1)} %fold.11), channel_id=1, source_target_pairs={{0,4},{4,0},{8,12},{12,8},{16,20},{20,16},{24,28},{28,24},{1,5},{5... | collective-permute-start | bytes 393224 | tf_op jit(solution)/shard_map/ppermute | solution.py:467
  52.7 6.7 %collective-permute-start.19 = (bf16[16,32,128]{2,1,0:T(8,128)(2,1)S(1)}, bf16[16,32,128]{2,1,0:T(8,128)(2,1)S(1)}, u32[]{:S(2)}, u32[]{:S(2)}) collective-permute-start(bf16[16,32,128]{2,1,0:T(8,128)(2,1)S(1)} %get-tuple-element.96.panel_ref.refs_0_), channel_id=1, source_target_pairs={{0,16},{4,20},{8,24},{12,28},{16,0},{20,4},{24,8},{28,12},{1,17},{... | collective-permute-start | bytes 393224 | tf_op jit(solution)/shard_map/ppermute | solution.py:467
  52.8 8.8 %collective-permute-start.16 = (bf16[16,32,128]{2,1,0:T(8,128)(2,1)S(1)}, bf16[16,32,128]{2,1,0:T(8,128)(2,1)S(1)}, u32[]{:S(2)}, u32[]{:S(2)}) collective-permute-start(bf16[16,32,128]{2,1,0:T(8,128)(2,1)S(1)} %get-tuple-element.96.panel_ref.refs_0_), channel_id=1, source_target_pairs={{0,4},{4,0},{8,12},{12,8},{16,20},{20,16},{24,28},{28,24},{1,5},{5... | collective-permute-start | bytes 393224 | tf_op jit(solution)/shard_map/ppermute | solution.py:467
  59.4 5.0 %collective-permute-start.21 = (bf16[16,32,128]{2,1,0:T(8,128)(2,1)S(1)}, bf16[16,32,128]{2,1,0:T(8,128)(2,1)S(1)}, u32[]{:S(2)}, u32[]{:S(2)}) collective-permute-start(bf16[16,32,128]{2,1,0:T(8,128)(2,1)S(1)} %get-tuple-element.99.refs_4_), channel_id=1, source_target_pairs={{0,8},{4,12},{8,0},{12,4},{16,24},{20,28},{24,16},{28,20},{1,9},{5... | collective-permute-start | bytes 393224 | tf_op jit(solution)/shard_map/ppermute | solution.py:467
  59.5 6.4 %collective-permute-start.17 = (bf16[16,32,128]{2,1,0:T(8,128)(2,1)S(1)}, bf16[16,32,128]{2,1,0:T(8,128)(2,1)S(1)}, u32[]{:S(2)}, u32[]{:S(2)}) collective-permute-start(bf16[16,32,128]{2,1,0:T(8,128)(2,1)S(1)} %get-tuple-element.96.panel_ref.refs_0_), channel_id=1, source_target_pairs={{0,8},{4,12},{8,0},{12,4},{16,24},{20,28},{24,16},{28,20},{1,9},{5... | collective-permute-start | bytes 393224 | tf_op jit(solution)/shard_map/ppermute | solution.py:467
  61.5 5.8 %collective-permute-start.20 = (bf16[16,32,128]{2,1,0:T(8,128)(2,1)S(1)}, bf16[16,32,128]{2,1,0:T(8,128)(2,1)S(1)}, u32[]{:S(2)}, u32[]{:S(2)}) collective-permute-start(bf16[16,32,128]{2,1,0:T(8,128)(2,1)S(1)} %get-tuple-element.99.refs_4_), channel_id=1, source_target_pairs={{0,4},{4,0},{8,12},{12,8},{16,20},{20,16},{24,28},{28,24},{1,5},{5... | collective-permute-start | bytes 393224 | tf_op jit(solution)/shard_map/ppermute | solution.py:467
  61.5 5.7 %collective-permute-start.18 = (bf16[16,32,128]{2,1,0:T(8,128)(2,1)S(1)}, bf16[16,32,128]{2,1,0:T(8,128)(2,1)S(1)}, u32[]{:S(2)}, u32[]{:S(2)}) collective-permute-start(bf16[16,32,128]{2,1,0:T(8,128)(2,1)S(1)} %collective-permute-done.16.refs_1_), channel_id=1, source_target_pairs={{0,8},{4,12},{8,0},{12,4},{16,24},{20,28},{24,16},{28,20},{1,9},{5... | collective-permute-start | bytes 393224 | tf_op jit(solution)/shard_map/ppermute | solution.py:467
  64.5 5.0 %collective-permute-start.22 = (bf16[16,32,128]{2,1,0:T(8,128)(2,1)S(1)}, bf16[16,32,128]{2,1,0:T(8,128)(2,1)S(1)}, u32[]{:S(2)}, u32[]{:S(2)}) collective-permute-start(bf16[16,32,128]{2,1,0:T(8,128)(2,1)S(1)} %collective-permute-done.21.refs_6_), channel_id=1, source_target_pairs={{0,4},{4,0},{8,12},{12,8},{16,20},{20,16},{24,28},{28,24},{1,5},{5... | collective-permute-start | bytes 393224 | tf_op jit(solution)/shard_map/ppermute | solution.py:467
  64.5 1.4 %collective-permute-start.23 = (f32[8,128]{1,0:T(8,128)S(1)}, f32[8,128]{1,0:T(8,128)S(1)}, u32[]{:S(2)}, u32[]{:S(2)}) collective-permute-start(f32[8,128]{1,0:T(8,128)S(1)} %get-tuple-element.103.refs_13_), channel_id=1, source_target_pairs={{0,1},{1,0},{2,3},{3,2},{4,5},{5,4},{6,7},{7,6},{8,9},{9,8},{10,11... | collective-permute-start | bytes 12296 | tf_op jit(solution)/shard_map/ppermute | solution.py:467
  72.0 6.3 %collective-permute-start.26 = (bf16[17,32,128]{2,1,0:T(8,128)(2,1)S(1)}, bf16[17,32,128]{2,1,0:T(8,128)(2,1)S(1)}, u32[]{:S(2)}, u32[]{:S(2)}) collective-permute-start(bf16[17,32,128]{2,1,0:T(8,128)(2,1)S(1)} %get-tuple-element.110.refs_2_), channel_id=1, source_target_pairs={{0,4},{4,0},{8,12},{12,8},{16,20},{20,16},{24,28},{28,24},{1,5},{5... | collective-permute-start | bytes 417800 | tf_op jit(solution)/shard_map/ppermute | solution.py:467
  78.4 7.4 %collective-permute-start.27 = (bf16[17,32,128]{2,1,0:T(8,128)(2,1)S(1)}, bf16[17,32,128]{2,1,0:T(8,128)(2,1)S(1)}, u32[]{:S(2)}, u32[]{:S(2)}) collective-permute-start(bf16[17,32,128]{2,1,0:T(8,128)(2,1)S(1)} %get-tuple-element.114.refs_3_), channel_id=1, source_target_pairs={{0,8},{4,12},{8,0},{12,4},{16,24},{20,28},{24,16},{28,20},{1,9},{5... | collective-permute-start | bytes 417800 | tf_op jit(solution)/shard_map/ppermute | solution.py:467
  78.5 6.1 %collective-permute-start.25 = (bf16[16,32,128]{2,1,0:T(8,128)(2,1)S(1)}, bf16[16,32,128]{2,1,0:T(8,128)(2,1)S(1)}, u32[]{:S(2)}, u32[]{:S(2)}) collective-permute-start(bf16[16,32,128]{2,1,0:T(8,128)(2,1)S(1)} %get-tuple-element.108), channel_id=1, source_target_pairs={{0,4},{4,0},{8,12},{12,8},{16,20},{20,16},{24,28},{28,24},{1,5},{5... | collective-permute-start | bytes 393224 | tf_op jit(solution)/shard_map/ppermute | solution.py:467
  78.6 8.7 %collective-permute-start.24 = (bf16[16,32,128]{2,1,0:T(8,128)(2,1)S(1)}, bf16[16,32,128]{2,1,0:T(8,128)(2,1)S(1)}, u32[]{:S(2)}, u32[]{:S(2)}) collective-permute-start(bf16[16,32,128]{2,1,0:T(8,128)(2,1)S(1)} %get-tuple-element.106), channel_id=1, source_target_pairs={{0,8},{4,12},{8,0},{12,4},{16,24},{20,28},{24,16},{28,20},{1,9},{5... | collective-permute-start | bytes 393224 | tf_op jit(solution)/shard_map/ppermute | solution.py:467
  80.5 4.1 %collective-permute-start.28 = (f32[8,128]{1,0:T(8,128)S(1)}, f32[8,128]{1,0:T(8,128)S(1)}, u32[]{:S(2)}, u32[]{:S(2)}) collective-permute-start(f32[8,128]{1,0:T(8,128)S(1)} %get-tuple-element.115.refs_9_), channel_id=1, source_target_pairs={{0,2},{1,3},{2,0},{3,1},{4,6},{5,7},{6,4},{7,5},{8,10},{9,11},{10,... | collective-permute-start | bytes 12296 | tf_op jit(solution)/shard_map/ppermute | solution.py:467
  85.9 8.9 %collective-permute-start.31 = (bf16[17,32,128]{2,1,0:T(8,128)(2,1)S(1)}, bf16[17,32,128]{2,1,0:T(8,128)(2,1)S(1)}, u32[]{:S(2)}, u32[]{:S(2)}) collective-permute-start(bf16[17,32,128]{2,1,0:T(8,128)(2,1)S(1)} %fold.13.refs_2_.refs_4_), channel_id=1, source_target_pairs={{0,16},{4,20},{8,24},{12,28},{16,0},{20,4},{24,8},{28,12},{1,17},{... | collective-permute-start | bytes 417800 | tf_op jit(solution)/shard_map/ppermute | solution.py:467
  86.0 5.7 %collective-permute-start.30 = (bf16[16,32,128]{2,1,0:T(8,128)(2,1)S(1)}, bf16[16,32,128]{2,1,0:T(8,128)(2,1)S(1)}, u32[]{:S(2)}, u32[]{:S(2)}) collective-permute-start(bf16[16,32,128]{2,1,0:T(8,128)(2,1)S(1)} %get-tuple-element.116), channel_id=1, source_target_pairs={{0,8},{4,12},{8,0},{12,4},{16,24},{20,28},{24,16},{28,20},{1,9},{5... | collective-permute-start | bytes 393224 | tf_op jit(solution)/shard_map/ppermute | solution.py:467
  87.3 5.7 %collective-permute-start.29 = (bf16[16,32,128]{2,1,0:T(8,128)(2,1)S(1)}, bf16[16,32,128]{2,1,0:T(8,128)(2,1)S(1)}, u32[]{:S(2)}, u32[]{:S(2)}) collective-permute-start(bf16[16,32,128]{2,1,0:T(8,128)(2,1)S(1)} %fold.14), channel_id=1, source_target_pairs={{0,4},{4,0},{8,12},{12,8},{16,20},{20,16},{24,28},{28,24},{1,5},{5... | collective-permute-start | bytes 393224 | tf_op jit(solution)/shard_map/ppermute | solution.py:467
  95.0 6.7 %collective-permute-start.35 = (bf16[16,32,128]{2,1,0:T(8,128)(2,1)S(1)}, bf16[16,32,128]{2,1,0:T(8,128)(2,1)S(1)}, u32[]{:S(2)}, u32[]{:S(2)}) collective-permute-start(bf16[16,32,128]{2,1,0:T(8,128)(2,1)S(1)} %get-tuple-element.119.panel_ref.refs_0_), channel_id=1, source_target_pairs={{0,16},{4,20},{8,24},{12,28},{16,0},{20,4},{24,8},{28,12},{1,17},{... | collective-permute-start | bytes 393224 | tf_op jit(solution)/shard_map/ppermute | solution.py:467
  95.3 9.4 %collective-permute-start.32 = (bf16[16,32,128]{2,1,0:T(8,128)(2,1)S(1)}, bf16[16,32,128]{2,1,0:T(8,128)(2,1)S(1)}, u32[]{:S(2)}, u32[]{:S(2)}) collective-permute-start(bf16[16,32,128]{2,1,0:T(8,128)(2,1)S(1)} %get-tuple-element.119.panel_ref.refs_0_), channel_id=1, source_target_pairs={{0,4},{4,0},{8,12},{12,8},{16,20},{20,16},{24,28},{28,24},{1,5},{5... | collective-permute-start | bytes 393224 | tf_op jit(solution)/shard_map/ppermute | solution.py:467
  101.7 5.0 %collective-permute-start.37 = (bf16[16,32,128]{2,1,0:T(8,128)(2,1)S(1)}, bf16[16,32,128]{2,1,0:T(8,128)(2,1)S(1)}, u32[]{:S(2)}, u32[]{:S(2)}) collective-permute-start(bf16[16,32,128]{2,1,0:T(8,128)(2,1)S(1)} %get-tuple-element.122.refs_4_), channel_id=1, source_target_pairs={{0,8},{4,12},{8,0},{12,4},{16,24},{20,28},{24,16},{28,20},{1,9},{5... | collective-permute-start | bytes 393224 | tf_op jit(solution)/shard_map/ppermute | solution.py:467
  101.8 6.4 %collective-permute-start.33 = (bf16[16,32,128]{2,1,0:T(8,128)(2,1)S(1)}, bf16[16,32,128]{2,1,0:T(8,128)(2,1)S(1)}, u32[]{:S(2)}, u32[]{:S(2)}) collective-permute-start(bf16[16,32,128]{2,1,0:T(8,128)(2,1)S(1)} %get-tuple-element.119.panel_ref.refs_0_), channel_id=1, source_target_pairs={{0,8},{4,12},{8,0},{12,4},{16,24},{20,28},{24,16},{28,20},{1,9},{5... | collective-permute-start | bytes 393224 | tf_op jit(solution)/shard_map/ppermute | solution.py:467
  103.8 5.9 %collective-permute-start.36 = (bf16[16,32,128]{2,1,0:T(8,128)(2,1)S(1)}, bf16[16,32,128]{2,1,0:T(8,128)(2,1)S(1)}, u32[]{:S(2)}, u32[]{:S(2)}) collective-permute-start(bf16[16,32,128]{2,1,0:T(8,128)(2,1)S(1)} %get-tuple-element.122.refs_4_), channel_id=1, source_target_pairs={{0,4},{4,0},{8,12},{12,8},{16,20},{20,16},{24,28},{28,24},{1,5},{5... | collective-permute-start | bytes 393224 | tf_op jit(solution)/shard_map/ppermute | solution.py:467
  104.7 5.0 %collective-permute-start.34 = (bf16[16,32,128]{2,1,0:T(8,128)(2,1)S(1)}, bf16[16,32,128]{2,1,0:T(8,128)(2,1)S(1)}, u32[]{:S(2)}, u32[]{:S(2)}) collective-permute-start(bf16[16,32,128]{2,1,0:T(8,128)(2,1)S(1)} %collective-permute-done.32.refs_1_), channel_id=1, source_target_pairs={{0,8},{4,12},{8,0},{12,4},{16,24},{20,28},{24,16},{28,20},{1,9},{5... | collective-permute-start | bytes 393224 | tf_op jit(solution)/shard_map/ppermute | solution.py:467
  106.8 5.0 %collective-permute-start.38 = (bf16[16,32,128]{2,1,0:T(8,128)(2,1)S(1)}, bf16[16,32,128]{2,1,0:T(8,128)(2,1)S(1)}, u32[]{:S(2)}, u32[]{:S(2)}) collective-permute-start(bf16[16,32,128]{2,1,0:T(8,128)(2,1)S(1)} %collective-permute-done.37.refs_6_), channel_id=1, source_target_pairs={{0,4},{4,0},{8,12},{12,8},{16,20},{20,16},{24,28},{28,24},{1,5},{5... | collective-permute-start | bytes 393224 | tf_op jit(solution)/shard_map/ppermute | solution.py:467
  107.7 1.2 collective-permute-start.39
  115.1 6.1 %collective-permute-start.42 = (bf16[17,32,128]{2,1,0:T(8,128)(2,1)S(1)}, bf16[17,32,128]{2,1,0:T(8,128)(2,1)S(1)}, u32[]{:S(2)}, u32[]{:S(2)}) collective-permute-start(bf16[17,32,128]{2,1,0:T(8,128)(2,1)S(1)} %get-tuple-element.134.refs_2_), channel_id=1, source_target_pairs={{0,4},{4,0},{8,12},{12,8},{16,20},{20,16},{24,28},{28,24},{1,5},{5... | collective-permute-start | bytes 417800 | tf_op jit(solution)/shard_map/ppermute | solution.py:467
  121.4 8.0 %collective-permute-start.43 = (bf16[17,32,128]{2,1,0:T(8,128)(2,1)S(1)}, bf16[17,32,128]{2,1,0:T(8,128)(2,1)S(1)}, u32[]{:S(2)}, u32[]{:S(2)}) collective-permute-start(bf16[17,32,128]{2,1,0:T(8,128)(2,1)S(1)} %get-tuple-element.138.refs_3_), channel_id=1, source_target_pairs={{0,8},{4,12},{8,0},{12,4},{16,24},{20,28},{24,16},{28,20},{1,9},{5... | collective-permute-start | bytes 417800 | tf_op jit(solution)/shard_map/ppermute | solution.py:467
  121.5 6.0 %collective-permute-start.41 = (bf16[16,32,128]{2,1,0:T(8,128)(2,1)S(1)}, bf16[16,32,128]{2,1,0:T(8,128)(2,1)S(1)}, u32[]{:S(2)}, u32[]{:S(2)}) collective-permute-start(bf16[16,32,128]{2,1,0:T(8,128)(2,1)S(1)} %get-tuple-element.132), channel_id=1, source_target_pairs={{0,4},{4,0},{8,12},{12,8},{16,20},{20,16},{24,28},{28,24},{1,5},{5... | collective-permute-start | bytes 393224 | tf_op jit(solution)/shard_map/ppermute | solution.py:467
  122.2 8.6 %collective-permute-start.40 = (bf16[16,32,128]{2,1,0:T(8,128)(2,1)S(1)}, bf16[16,32,128]{2,1,0:T(8,128)(2,1)S(1)}, u32[]{:S(2)}, u32[]{:S(2)}) collective-permute-start(bf16[16,32,128]{2,1,0:T(8,128)(2,1)S(1)} %get-tuple-element.130), channel_id=1, source_target_pairs={{0,8},{4,12},{8,0},{12,4},{16,24},{20,28},{24,16},{28,20},{1,9},{5... | collective-permute-start | bytes 393224 | tf_op jit(solution)/shard_map/ppermute | solution.py:467
  124.1 3.6 %collective-permute-start.44 = (f32[8,128]{1,0:T(8,128)S(1)}, f32[8,128]{1,0:T(8,128)S(1)}, u32[]{:S(2)}, u32[]{:S(2)}) collective-permute-start(f32[8,128]{1,0:T(8,128)S(1)} %get-tuple-element.139.refs_9_), channel_id=1, source_target_pairs={{0,2},{1,3},{2,0},{3,1},{4,6},{5,7},{6,4},{7,5},{8,10},{9,11},{10,... | collective-permute-start | bytes 12296 | tf_op jit(solution)/shard_map/ppermute | solution.py:467
  129.5 7.4 %collective-permute-start.47 = (bf16[17,32,128]{2,1,0:T(8,128)(2,1)S(1)}, bf16[17,32,128]{2,1,0:T(8,128)(2,1)S(1)}, u32[]{:S(2)}, u32[]{:S(2)}) collective-permute-start(bf16[17,32,128]{2,1,0:T(8,128)(2,1)S(1)} %fold.16.refs_2_.refs_4_), channel_id=1, source_target_pairs={{0,16},{4,20},{8,24},{12,28},{16,0},{20,4},{24,8},{28,12},{1,17},{... | collective-permute-start | bytes 417800 | tf_op jit(solution)/shard_map/ppermute | solution.py:467
  129.5 5.1 %collective-permute-start.46 = (bf16[16,32,128]{2,1,0:T(8,128)(2,1)S(1)}, bf16[16,32,128]{2,1,0:T(8,128)(2,1)S(1)}, u32[]{:S(2)}, u32[]{:S(2)}) collective-permute-start(bf16[16,32,128]{2,1,0:T(8,128)(2,1)S(1)} %get-tuple-element.140), channel_id=1, source_target_pairs={{0,8},{4,12},{8,0},{12,4},{16,24},{20,28},{24,16},{28,20},{1,9},{5... | collective-permute-start | bytes 393224 | tf_op jit(solution)/shard_map/ppermute | solution.py:467
  130.8 5.0 %collective-permute-start.45 = (bf16[16,32,128]{2,1,0:T(8,128)(2,1)S(1)}, bf16[16,32,128]{2,1,0:T(8,128)(2,1)S(1)}, u32[]{:S(2)}, u32[]{:S(2)}) collective-permute-start(bf16[16,32,128]{2,1,0:T(8,128)(2,1)S(1)} %fold.17), channel_id=1, source_target_pairs={{0,4},{4,0},{8,12},{12,8},{16,20},{20,16},{24,28},{28,24},{1,5},{5... | collective-permute-start | bytes 393224 | tf_op jit(solution)/shard_map/ppermute | solution.py:467
